TPU v7x, 32 devices: a whole 2x2x4 slice. The times are simulated.
32 devices in a mesh: user: 4 (over x, core), tok: 8 (over z, y).
Axes of the slice: x: 2, y: 2, z: 4, core: 2. Of those that a mesh axis runs over, the one named last changes fastest.
Arguments:
- hidden: bfloat16 [4, 1024, 16384], P('user', 'tok'), may hold values from -256 to 256, as said below
- cotangent: bfloat16 [4, 1024, 2048], P('user', 'tok'), may hold values from -6 to 6
- lengths: int32 [4], P('user'), may hold values from 256 to 1024
Outputs:
- clipped_sum: float32 [16384, 2048], P('tok', 'user')
Inputs may be any that keep to these rules, and one draw needn't show every extreme that they name: bfloat16 activations of mixed magnitudes across tokens and hidden units.
All inputs are finite; a program needn't handle non-finite values.
Results may differ from a plain program's by a relative error of at most 0.0003.
Values may be sent and summed in bfloat16 or wider, within the bound.
No kernel may reach another device: no remote copies, remote signals or barrier semaphores. Data moves between devices by JAX's collectives and lax.ppermute only.
A program may use at most 128 MiB of HBM per device.

v0:
```python
import math

import jax
import jax.numpy as jnp
from jax import lax
from jax.sharding import PartitionSpec as P

epsilon = 1e-06


def contract(left, right):
    return lax.dot_general(
        left, right, (((0,), (0,)), ((), ())), preferred_element_type=jnp.float32
    )


def body(hidden, cotangent, lengths):
    tok_count = lax.axis_size("tok")
    user_count = lax.axis_size("user")
    tok_rows = hidden.shape[1]
    hidden_width = hidden.shape[2]
    model_width = cotangent.shape[2]
    capacity = tok_rows * tok_count
    clip_bound = math.sqrt(8.0 * hidden_width * model_width * capacity)
    scaling = math.sqrt(hidden_width * model_width) / (user_count * clip_bound)
    position = lax.axis_index("tok") * tok_rows + lax.iota(jnp.int32, tok_rows)
    keep_rows = position < lengths[0]
    masked = jnp.where(keep_rows[:, None], cotangent[0], jnp.zeros_like(cotangent[0]))
    columns = lax.all_to_all(hidden[0], "tok", split_axis=1, concat_axis=0, tiled=True)
    gathered = lax.all_gather(masked, "tok", axis=0, tiled=True)
    gradient = contract(columns, gathered)
    partial_value = jnp.sum(gradient * gradient)
    norm_sq = lax.psum(partial_value, "tok")
    factor = jnp.minimum(1.0, clip_bound / jnp.sqrt(norm_sq + epsilon)) * scaling
    result = lax.psum_scatter(gradient * factor, "user", scatter_dimension=1, tiled=True)
    return result


def solution(mesh):
    return jax.shard_map(
        body,
        mesh=mesh,
        in_specs=(P("user", "tok", None), P("user", "tok", None), P("user")),
        out_specs=P("tok", "user"),
        check_vma=False,
    )
```

profile of v0, /device:TPU:0, one launch (start us, length us, event | category | flops | bytes accessed | tf_op | source)
XLA Modules:
  0.0 355.6 jit_solution(13410821355316071398)
XLA Ops:
  6.5 6.4 %copy.6 = bf16[1,128,16384]{1,2,0:T(8,128)(2,1)} copy(bf16[1,128,16384]{2,1,0:T(8,128)(2,1)} %param.3) | data formatting | bytes 8388608 | tf_op args[0]
  12.9 0.0 copy-start
  12.9 7.4 %all-to-all-start = ((bf16[128,8,2048]{0,2,1:T(8,128)(2,1)}), bf16[128,8,2048]{0,2,1:T(8,128)(2,1)}, u32[]{:S(2)}, u32[]{:S(2)}) async-start(bf16[128,8,2048]{0,2,1:T(8,128)(2,1)} %bitcast.11), calls=%async_computation | async-start | bytes 8388608 | tf_op jit(solution)/shard_map/all_to_all | solution.py:29
  20.3 0.0 all-gather.2.cloned.1.call-start
  21.0 0.0 copy-done
  21.0 0.9 bitcast_select_fusion
  21.9 0.0 all-gather.2.cloned.1.call-update
  22.0 0.0 reduce-scatter.2.cloned.1.call-start
  22.0 142.4 %all-to-all-done = bf16[128,8,2048]{0,2,1:T(8,128)(2,1)} async-done(((bf16[128,8,2048]{0,2,1:T(8,128)(2,1)}), bf16[128,8,2048]{0,2,1:T(8,128)(2,1)}, u32[]{:S(2)}, u32[]{:S(2)}) %all-to-all-start) | async-done | bytes 4194336 | tf_op jit(solution)/shard_map/all_to_all | solution.py:29
  164.4 6.4 %copy.7 = bf16[8,128,2048]{2,1,0:T(8,128)(2,1)} copy(bf16[8,128,2048]{1,2,0:T(8,128)(2,1)} %bitcast.3) | data formatting | bytes 8388608 | tf_op jit(solution)/shard_map/all_to_all | solution.py:29
  170.8 0.0 all-gather.2.cloned.1.call-done
  170.8 16.9 %multiply_reduce_fusion = (f32[]{:T(128)}, f32[2048,2048]{1,0:T(8,128)}) fusion(bf16[1024,2048]{1,0:T(8,128)(2,1)} %all-gather.2.cloned.1.call-done, bf16[1024,2048]{1,0:T(8,128)(2,1)} %bitcast.12), kind=kOutput, calls=%fused_computation.1 | convolution fusion | flops 8598323200 | bytes 25165828 | tf_op jit(solution)/shard_map/dot_general | solution.py:12
  187.7 19.8 %psum.7 = f32[]{:T(128)} all-reduce(f32[]{:T(128)} %get-tuple-element.5), channel_id=1, replica_groups=mesh['user'=4,'tok'=8] {'tok'}, use_global_device_ids=true, to_apply=%region_1.2 | all-reduce | flops 1 | bytes 8 | tf_op jit(solution)/shard_map/psum | solution.py:33
  208.2 11.7 %multiply_bitcast_fusion = f32[2048,2048]{0,1:T(8,128)} fusion(f32[2048,2048]{1,0:T(8,128)} %get-tuple-element.6, f32[]{:T(128)S(6)} %mul.21), kind=kLoop, calls=%fused_computation | loop fusion | flops 4194304 | bytes 33554436 | tf_op jit(solution)/shard_map/mul | solution.py:35
  219.9 0.0 reduce-scatter.2.cloned.1.call-update
  219.9 123.5 %reduce-scatter.2.cloned.1.call-done = f32[2048,512]{0,1:T(8,128)} async-done(((f32[2048,2048]{0,1:T(8,128)}), f32[2048,512]{0,1:T(8,128)}) %reduce-scatter.2.cloned.1.call-update) | async-done | bytes 4194320 | tf_op jit(solution)/shard_map/reduce_scatter | solution.py:35
  343.4 5.3 %copy.8 = f32[2048,512]{1,0:T(8,128)} copy(f32[2048,512]{0,1:T(8,128)} %reduce-scatter.2.cloned.1.call-done) | data formatting | bytes 8388608 | tf_op jit(solution)/shard_map/reduce_scatter | solution.py:35
  (1 shorter events, 0.0 us)
Async XLA Ops:
  12.9 8.1 %copy-start = (bf16[1,128,2048]{2,1,0:T(8,128)(2,1)S(1)}, bf16[1,128,2048]{2,1,0:T(8,128)(2,1)}, u32[]{:S(2)}) copy-start(bf16[1,128,2048]{2,1,0:T(8,128)(2,1)} %param.4) | copy-start | bytes 1572868
  12.9 151.5 %all-to-all-start = ((bf16[128,8,2048]{0,2,1:T(8,128)(2,1)}), bf16[128,8,2048]{0,2,1:T(8,128)(2,1)}, u32[]{:S(2)}, u32[]{:S(2)}) async-start(bf16[128,8,2048]{0,2,1:T(8,128)(2,1)} %bitcast.11), calls=%async_computation | async-start | bytes 8388608 | tf_op jit(solution)/shard_map/all_to_all | solution.py:29
  20.3 150.5 %all-gather.2.cloned.1.call-start = ((), (), s32[]{:S(2)}) async-start(), calls=%async_computation.2 | async-start | bytes 4718592 | tf_op jit(solution)/shard_map/all_gather | solution.py:30
  22.0 321.5 %reduce-scatter.2.cloned.1.call-start = ((), (), s32[]{:S(2)}) async-start(), calls=%async_computation.3 | async-start | bytes 20971520 | tf_op jit(solution)/shard_map/reduce_scatter | solution.py:35
Sparse Core Ops, SparseCore 0:
  23.3 137.0 all-gather.1
  220.0 123.3 reduce-scatter.1
where the time goes:
time: 356 us
  waiting for transfers between devices  266 us (75%)
  blocking collectives  19.8 us (6%)
  local copies, waits for them, and re-layouts  18.1 us (5%)
  matrix products  16.9 us (5%)
  between operations  14.8 us (4%)
  other arithmetic  12.6 us (4%)
  starting transfers between devices  7.49 us (2%)
    all_to_all x1, waiting for transfers between devices, body(): lax.all_to_all(hidden[0], 'tok', split_axis=1, concat_axis=0, tiled=True)  142 us
    reduce_scatter x1, waiting for transfers between devices, body(): lax.psum_scatter(gradient * factor, 'user', scatter_dimension=1, tiled=True)  124 us
    psum x1, blocking collectives, body(): norm_sq = lax.psum(partial_value, 'tok')  19.8 us
    dot_general x1, matrix products, contract(): lax.dot_general(left, right, (((0,), (0,)), ((), ())), preferred_element_...  16.9 us
    mul x1, other arithmetic, body(): gradient * factor  11.7 us
    all_to_all x1, starting transfers between devices, body(): lax.all_to_all(hidden[0], 'tok', split_axis=1, concat_axis=0, tiled=True)  7.41 us
  transfers between devices with their start and end apart: 3, of which 2 were waited for; matrix products, arithmetic and copies ran while one was open for 2% of the time, Pallas kernels for 0%

commit v1 on v0

v1 whole, which is shorter than its diff:
```python
import math

import jax
import jax.numpy as jnp
from jax import lax
from jax.sharding import PartitionSpec as P

epsilon = 1e-06
pieces_wanted = 4


def contract(left, right):
    return lax.dot_general(
        left, right, (((0,), (0,)), ((), ())), preferred_element_type=jnp.float32
    )


def exchange(block, distance, user_count):
    return lax.ppermute(block, "user", [(u, u ^ distance) for u in range(user_count)])


def all_users(block, user_count):
    slots = {0: block}
    distance = user_count // 2
    while distance:
        for slot in list(slots):
            slots[slot ^ distance] = exchange(slots[slot], distance, user_count)
        distance //= 2
    return [slots[slot] for slot in range(user_count)]


def body(hidden, cotangent, lengths):
    tok_count = lax.axis_size("tok")
    user_count = lax.axis_size("user")
    tok_rows = hidden.shape[1]
    hidden_width = hidden.shape[2]
    model_width = cotangent.shape[2]
    capacity = tok_rows * tok_count
    own_width = hidden_width // tok_count
    pieces = pieces_wanted if own_width % (128 * pieces_wanted) == 0 else 1
    piece_width = own_width // pieces
    clip_bound = math.sqrt(8.0 * hidden_width * model_width * capacity)
    scaling = math.sqrt(hidden_width * model_width) / (user_count * clip_bound)
    own_user = lax.axis_index("user")
    slot_users = own_user ^ lax.iota(jnp.int32, user_count)

    position = lax.axis_index("tok") * tok_rows + lax.iota(jnp.int32, tok_rows)
    keep_rows = position < lengths[0]
    masked = jnp.where(keep_rows[:, None], cotangent[0], jnp.zeros_like(cotangent[0]))
    by_user = masked.reshape(tok_rows, user_count, model_width // user_count).transpose(1, 0, 2)
    by_user = lax.all_to_all(by_user, "user", split_axis=0, concat_axis=0, tiled=True)
    by_slot = jnp.take(by_user, slot_users, axis=0)
    right = lax.all_gather(by_slot, "tok", axis=1, tiled=True)

    split = hidden[0].reshape(tok_rows, tok_count, pieces, piece_width)
    products = []
    squares = jnp.zeros((user_count,), jnp.float32)
    for piece in range(pieces):
        outgoing = split[:, :, piece, :].transpose(1, 0, 2)
        columns = lax.all_to_all(outgoing, "tok", split_axis=0, concat_axis=0, tiled=True)
        columns = columns.reshape(capacity, piece_width)
        slots = all_users(columns, user_count)
        gradients = [contract(slots[s], right[s]) for s in range(user_count)]
        squares += jnp.stack([jnp.sum(g * g) for g in gradients])
        products.append(gradients)

    norm_sq = lax.psum(jnp.take(squares, slot_users), ("user", "tok"))
    factor = jnp.minimum(1.0, clip_bound / jnp.sqrt(norm_sq + epsilon)) * scaling
    slot_factor = jnp.take(factor, slot_users)
    rows = [sum(slot_factor[s] * g for s, g in enumerate(gradients)) for gradients in products]
    return jnp.concatenate(rows, axis=0)


def solution(mesh):
    return jax.shard_map(
        body,
        mesh=mesh,
        in_specs=(P("user", "tok", None), P("user", "tok", None), P("user")),
        out_specs=P("tok", "user"),
        check_vma=False,
    )
```

time: 356 us -> 381 us (1.070)
  waiting for transfers between devices: 266 us -> 193 us
  matrix products: 16.9 us -> 50.9 us
  starting transfers between devices: 7.49 us -> 31.7 us
  blocking collectives: 19.8 us -> 40.5 us
  other arithmetic: 12.6 us -> 26.7 us
  local copies, waits for them, and re-layouts: 18.1 us -> 22 us
    reduce_scatter x1 -> x0, waiting for transfers between devices: 124 us -> none  [body(): lax.psum_scatter(gradient * factor, 'user', scatter_dimension=1, tiled=True)]
    ppermute x0 -> x12, waiting for transfers between devices: none -> 64.6 us  [exchange(): lax.ppermute(block, 'user', [(u, u ^ distance) for u in range(user_count)])]
    dot_general x1 -> x16, matrix products: 16.9 us -> 50.9 us  [contract(): lax.dot_general(left, right, (((0,), (0,)), ((), ())), preferred_element_...]
    add x0 -> x3, other arithmetic: none -> 21.3 us  [the longest x2 11.1 us: body(): sum((slot_factor[s] * g for s, g in enumerate(gradients)))]
    psum x1, blocking collectives: 19.8 us -> 40.5 us  [body(): norm_sq = lax.psum(jnp.take(squares, slot_users), ('user', 'tok'))]
    all_to_all x1 -> x5, starting transfers between devices: 7.41 us -> 23.5 us  [the longest x4 19.2 us: body(): lax.all_to_all(outgoing, 'tok', split_axis=0, concat_axis=0, tiled=True)]
    all_to_all x1 -> x5, waiting for transfers between devices: 142 us -> 129 us  [the longest x4 129 us: body(): lax.all_to_all(outgoing, 'tok', split_axis=0, concat_axis=0, tiled=True)]
    mul x1, other arithmetic: 11.7 us -> 0.01 us  [body(): jnp.minimum(1.0, clip_bound / jnp.sqrt(norm_sq + epsilon)) * scaling]
  transfers between devices with their start and end apart: 3 -> 18, of which waited for: 2 -> 7; matrix products, arithmetic and copies ran while one was open for 2% -> 18% of each run, Pallas kernels for 0% -> 0%
where the time goes in v1:
time: 381 us; the launch traced here: 379 us
  waiting for transfers between devices  193 us (51%)
  matrix products  50.9 us (13%)
  blocking collectives  40.5 us (11%)
  starting transfers between devices  31.7 us (8%)
  other arithmetic  26.7 us (7%)
  local copies, waits for them, and re-layouts  22 us (6%)
  between operations  14.3 us (4%)
    all_to_all x4, waiting for transfers between devices, body(): lax.all_to_all(outgoing, 'tok', split_axis=0, concat_axis=0, tiled=True)  129 us
    ppermute x12, waiting for transfers between devices, exchange(): lax.ppermute(block, 'user', [(u, u ^ distance) for u in range(user_count)])  64.6 us
    dot_general x16, matrix products, contract(): lax.dot_general(left, right, (((0,), (0,)), ((), ())), preferred_element_...  50.9 us
    psum x1, blocking collectives, body(): norm_sq = lax.psum(jnp.take(squares, slot_users), ('user', 'tok'))  40.5 us
    all_to_all x4, starting transfers between devices, body(): lax.all_to_all(outgoing, 'tok', split_axis=0, concat_axis=0, tiled=True)  19.2 us
    add x2, other arithmetic, body(): sum((slot_factor[s] * g for s, g in enumerate(gradients)))  11.1 us
    add x1, other arithmetic, body(): squares += jnp.stack([jnp.sum(g * g) for g in gradients])  10.2 us
    transpose x5, local copies, waits for them, and re-layouts, body(): outgoing = split[:, :, piece, :].transpose(1, 0, 2)  9.69 us
  transfers between devices with their start and end apart: 18, of which 7 were waited for; matrix products, arithmetic and copies ran while one was open for 18% of the time, Pallas kernels for 0%

profile of v1, /device:TPU:0, one launch (start us, length us, event | category | flops | bytes accessed | tf_op | source)
XLA Modules:
  0.0 379.2 jit_solution(1949262114256678853)
XLA Ops:
  7.2 1.3 copy.19
  8.5 0.2 copy.20
  8.7 0.9 select_bitcast_fusion
  9.6 4.2 %all-to-all-start = ((bf16[4,128,512]{2,1,0:T(8,128)(2,1)}), bf16[4,128,512]{2,1,0:T(8,128)(2,1)}, u32[]{:S(2)}, u32[]{:S(2)}) async-start(bf16[4,128,512]{2,1,0:T(8,128)(2,1)} %select_bitcast_fusion), calls=%async_computation | async-start | bytes 1048576 | tf_op jit(solution)/shard_map/all_to_all | solution.py:51
  13.8 6.4 %copy.21 = bf16[1,128,16384]{1,2,0:T(8,128)(2,1)} copy(bf16[1,128,16384]{2,1,0:T(8,128)(2,1)} %param.5) | data formatting | bytes 8388608 | tf_op args[0]
  20.2 3.5 slice_bitcast_fusion.1
  23.7 2.3 copy.23
  25.9 0.0 all-to-all-done
  26.0 7.2 %all-to-all-start.1 = ((bf16[8,128,512]{2,1,0:T(8,128)(2,1)}), bf16[8,128,512]{2,1,0:T(8,128)(2,1)}, u32[]{:S(2)}, u32[]{:S(2)}) async-start(bf16[8,128,512]{2,1,0:T(8,128)(2,1)} %copy.23), calls=%async_computation.1 | async-start | bytes 2097152 | tf_op jit(solution)/shard_map/all_to_all | solution.py:60
  33.2 0.0 all-gather.2.cloned.1.call-start
  33.3 2.4 gather_fusion
  35.7 2.0 broadcast_select_fusion
  37.7 0.0 all-gather.2.cloned.1.call-update
  37.7 1.3 copy.25
  39.0 32.9 %all-to-all-done.1 = bf16[8,128,512]{2,1,0:T(8,128)(2,1)} async-done(((bf16[8,128,512]{2,1,0:T(8,128)(2,1)}), bf16[8,128,512]{2,1,0:T(8,128)(2,1)}, u32[]{:S(2)}, u32[]{:S(2)}) %all-to-all-start.1) | async-done | bytes 1048608 | tf_op jit(solution)/shard_map/all_to_all | solution.py:60
  71.9 3.6 all-to-all-start.2
  75.5 1.3 copy.27
  76.8 46.9 %all-to-all-done.2 = bf16[8,128,512]{2,1,0:T(8,128)(2,1)S(1)} async-done(((bf16[8,128,512]{2,1,0:T(8,128)(2,1)}), bf16[8,128,512]{2,1,0:T(8,128)(2,1)S(1)}, u32[]{:S(2)}, u32[]{:S(2)}) %all-to-all-start.2) | async-done | bytes 1048608 | tf_op jit(solution)/shard_map/all_to_all | solution.py:60
  123.8 4.7 %all-to-all-start.3 = ((bf16[8,128,512]{2,1,0:T(8,128)(2,1)}), bf16[8,128,512]{2,1,0:T(8,128)(2,1)S(1)}, u32[]{:S(2)}, u32[]{:S(2)}) async-start(bf16[8,128,512]{2,1,0:T(8,128)(2,1)} %copy.27), calls=%async_computation.3 | async-start | bytes 2097152 | tf_op jit(solution)/shard_map/all_to_all | solution.py:60
  128.5 1.3 copy.29
  129.8 27.5 %all-to-all-done.3 = bf16[8,128,512]{2,1,0:T(8,128)(2,1)S(1)} async-done(((bf16[8,128,512]{2,1,0:T(8,128)(2,1)}), bf16[8,128,512]{2,1,0:T(8,128)(2,1)S(1)}, u32[]{:S(2)}, u32[]{:S(2)}) %all-to-all-start.3) | async-done | bytes 1048608 | tf_op jit(solution)/shard_map/all_to_all | solution.py:60
  157.3 3.7 all-to-all-start.4
  161.0 2.3 collective-permute-start.1
  163.3 0.1 collective-permute-start.4
  163.4 1.9 collective-permute-start.7
  165.4 21.2 %all-to-all-done.4 = bf16[8,128,512]{2,1,0:T(8,128)(2,1)S(1)} async-done(((bf16[8,128,512]{2,1,0:T(8,128)(2,1)}), bf16[8,128,512]{2,1,0:T(8,128)(2,1)S(1)}, u32[]{:S(2)}, u32[]{:S(2)}) %all-to-all-start.4) | async-done | bytes 1048608 | tf_op jit(solution)/shard_map/all_to_all | solution.py:60
  186.6 2.2 collective-permute-start.10
  188.9 0.1 collective-permute-start
  188.9 0.0 collective-permute-done.1
  189.0 0.5 collective-permute-start.2
  189.4 20.7 %collective-permute-done.4 = bf16[1024,512]{1,0:T(8,128)(2,1)} collective-permute-done((bf16[1024,512]{1,0:T(8,128)(2,1)S(1)}, bf16[1024,512]{1,0:T(8,128)(2,1)}, u32[]{:S(2)}, u32[]{:S(2)}) %collective-permute-start.4) | collective-permute-done | bytes 1048608 | tf_op jit(solution)/shard_map/ppermute | solution.py:19
  210.1 22.5 %collective-permute-done.7 = bf16[1024,512]{1,0:T(8,128)(2,1)} collective-permute-done((bf16[1024,512]{1,0:T(8,128)(2,1)S(1)}, bf16[1024,512]{1,0:T(8,128)(2,1)}, u32[]{:S(2)}, u32[]{:S(2)}) %collective-permute-start.7) | collective-permute-done | bytes 1048608 | tf_op jit(solution)/shard_map/ppermute | solution.py:19
  232.6 0.0 collective-permute-start.8
  232.6 21.4 %collective-permute-done.10 = bf16[1024,512]{1,0:T(8,128)(2,1)} collective-permute-done((bf16[1024,512]{1,0:T(8,128)(2,1)S(1)}, bf16[1024,512]{1,0:T(8,128)(2,1)}, u32[]{:S(2)}, u32[]{:S(2)}) %collective-permute-start.10) | collective-permute-done | bytes 1048608 | tf_op jit(solution)/shard_map/ppermute | solution.py:19
  254.0 4.1 %multiply_reduce_fusion.13 = (f32[]{:T(128)}, f32[512,512]{0,1:T(8,128)}) fusion(bf16[1024,512]{1,0:T(8,128)(2,1)} %collective-permute-done.1, bf16[4,1024,512]{2,1,0:T(8,128)(2,1)} %all-gather.2.cloned.1.call-done), kind=kOutput, calls=%fused_computation.29 | convolution fusion | flops 537395200 | bytes 3145732 | tf_op jit(solution)/shard_map/dot_general | solution.py:13
  258.1 3.5 multiply_reduce_fusion.9
  261.7 3.6 multiply_reduce_fusion.5
  265.3 3.6 multiply_reduce_fusion.1
  268.9 3.6 multiply_reduce_fusion.15
  272.5 2.4 multiply_reduce_fusion.11
  274.9 2.3 multiply_reduce_fusion.7
  277.3 2.4 multiply_reduce_fusion.3
  279.7 0.0 collective-permute-done.2
  279.7 0.5 collective-permute-start.3
  280.2 3.6 multiply_reduce_fusion.12
  283.8 0.0 collective-permute-done.5
  283.8 0.0 collective-permute-start.6
  283.8 3.6 multiply_reduce_fusion.8
  287.4 0.5 collective-permute-start.9
  287.9 3.6 multiply_reduce_fusion.4
  291.5 3.6 multiply_reduce_fusion
  295.1 3.6 multiply_reduce_fusion.14
  298.7 2.4 multiply_reduce_fusion.10
  301.1 2.5 multiply_reduce_fusion.6
  303.6 2.5 multiply_reduce_fusion.2
  306.0 10.2 %fusion.18 = f32[4]{0:T(128)S(1)} fusion(f32[1]{0:T(128)} %bitcast.16, f32[1]{0:T(128)} %bitcast.14, f32[1]{0:T(128)} %bitcast.12, f32[1]{0:T(128)} %bitcast.10, f32[1]{0:T(128)} %bitcast.24, f32[1]{0:T(128)} %bitcast.23, f32[1]{0:T(128)} %bitcast.22, f32[1]{0:T(128)} %bitcast.21, f32[1]{0:T(128)} %bitcast.32, f32[1]{0:T(128)} %bitcast.31, f32[1]{0:T(128)} %bitcast.30, ...), kind=kLoop, calls=%fused_computation.58 | loop fusion | flops 60 | bytes 80 | tf_op jit(solution)/shard_map/add | solution.py:64
  316.2 0.6 gather_fusion.1
  316.9 40.5 %psum.7 = f32[4]{0:T(128)S(1)} all-reduce(f32[4]{0:T(128)S(1)} %broadcast_select_fusion.2), channel_id=1, replica_groups=mesh['user'=4,'tok'=8] {'user','tok'}, use_global_device_ids=true, to_apply=%region_16.18 | all-reduce | flops 4 | bytes 32 | tf_op jit(solution)/shard_map/psum | solution.py:67
  357.3 0.6 gather_fusion.2
  358.0 0.7 fusion.19
  358.7 0.0 copy-start.7
  358.7 7.5 %add_bitcast_fusion.2 = (f32[512,512]{1,0:T(8,128)S(1)}, f32[512,512]{1,0:T(8,128)S(1)}) fusion(f32[512,512]{0,1:T(8,128)} %get-tuple-element.23, f32[512,512]{0,1:T(8,128)S(1)} %copy-done.5, f32[512,512]{0,1:T(8,128)} %get-tuple-element.27, f32[512,512]{0,1:T(8,128)} %get-tuple-element.29, f32[]{:T(128)} %bitcast.44, f32[]{:T(128)} %bitcast.43, ...), kind=kLoop, calls=%fused_computation.14 | loop fusion | flops 3670016 | bytes 10485776 | tf_op jit(solution)/shard_map/add | solution.py:70
  366.3 3.6 add_bitcast_fusion
  369.9 2.5 pad_maximum_fusion
  (39 shorter events, 0.1 us)
Async XLA Ops:
  9.6 16.3 %all-to-all-start = ((bf16[4,128,512]{2,1,0:T(8,128)(2,1)}), bf16[4,128,512]{2,1,0:T(8,128)(2,1)}, u32[]{:S(2)}, u32[]{:S(2)}) async-start(bf16[4,128,512]{2,1,0:T(8,128)(2,1)} %select_bitcast_fusion), calls=%async_computation | async-start | bytes 1048576 | tf_op jit(solution)/shard_map/all_to_all | solution.py:51
  26.0 46.0 %all-to-all-start.1 = ((bf16[8,128,512]{2,1,0:T(8,128)(2,1)}), bf16[8,128,512]{2,1,0:T(8,128)(2,1)}, u32[]{:S(2)}, u32[]{:S(2)}) async-start(bf16[8,128,512]{2,1,0:T(8,128)(2,1)} %copy.23), calls=%async_computation.1 | async-start | bytes 2097152 | tf_op jit(solution)/shard_map/all_to_all | solution.py:60
  33.2 220.8 %all-gather.2.cloned.1.call-start = ((), (), s32[]{:S(2)}) async-start(), calls=%async_computation.5 | async-start | bytes 4718592 | tf_op jit(solution)/shard_map/all_gather | solution.py:53
  71.9 51.8 %all-to-all-start.2 = ((bf16[8,128,512]{2,1,0:T(8,128)(2,1)}), bf16[8,128,512]{2,1,0:T(8,128)(2,1)S(1)}, u32[]{:S(2)}, u32[]{:S(2)}) async-start(bf16[8,128,512]{2,1,0:T(8,128)(2,1)} %copy.25), calls=%async_computation.2 | async-start | bytes 2097152 | tf_op jit(solution)/shard_map/all_to_all | solution.py:60
  123.8 33.5 %all-to-all-start.3 = ((bf16[8,128,512]{2,1,0:T(8,128)(2,1)}), bf16[8,128,512]{2,1,0:T(8,128)(2,1)S(1)}, u32[]{:S(2)}, u32[]{:S(2)}) async-start(bf16[8,128,512]{2,1,0:T(8,128)(2,1)} %copy.27), calls=%async_computation.3 | async-start | bytes 2097152 | tf_op jit(solution)/shard_map/all_to_all | solution.py:60
  157.3 29.3 %all-to-all-start.4 = ((bf16[8,128,512]{2,1,0:T(8,128)(2,1)}), bf16[8,128,512]{2,1,0:T(8,128)(2,1)S(1)}, u32[]{:S(2)}, u32[]{:S(2)}) async-start(bf16[8,128,512]{2,1,0:T(8,128)(2,1)} %copy.29), calls=%async_computation.4 | async-start | bytes 2097152 | tf_op jit(solution)/shard_map/all_to_all | solution.py:60
  161.0 27.9 %collective-permute-start.1 = (bf16[1024,512]{1,0:T(8,128)(2,1)}, bf16[1024,512]{1,0:T(8,128)(2,1)}, u32[]{:S(2)}, u32[]{:S(2)}) collective-permute-start(bf16[1024,512]{1,0:T(8,128)(2,1)} %bitcast.9), channel_id=1, source_target_pairs={{0,16},{8,24},{16,0},{24,8},{1,17},{9,25},{17,1},{25,9},{2,18},{10... | collective-permute-start | bytes 3145736 | tf_op jit(solution)/shard_map/ppermute | solution.py:19
  163.3 46.8 %collective-permute-start.4 = (bf16[1024,512]{1,0:T(8,128)(2,1)S(1)}, bf16[1024,512]{1,0:T(8,128)(2,1)}, u32[]{:S(2)}, u32[]{:S(2)}) collective-permute-start(bf16[1024,512]{1,0:T(8,128)(2,1)S(1)} %bitcast.130), channel_id=1, source_target_pairs={{0,16},{8,24},{16,0},{24,8},{1,17},{9,25},{17,1},{25,9},{2,18},{10... | collective-permute-start | bytes 3145736 | tf_op jit(solution)/shard_map/ppermute | solution.py:19
  163.4 69.2 %collective-permute-start.7 = (bf16[1024,512]{1,0:T(8,128)(2,1)S(1)}, bf16[1024,512]{1,0:T(8,128)(2,1)}, u32[]{:S(2)}, u32[]{:S(2)}) collective-permute-start(bf16[1024,512]{1,0:T(8,128)(2,1)S(1)} %bitcast.133), channel_id=1, source_target_pairs={{0,16},{8,24},{16,0},{24,8},{1,17},{9,25},{17,1},{25,9},{2,18},{10... | collective-permute-start | bytes 3145736 | tf_op jit(solution)/shard_map/ppermute | solution.py:19
  186.6 67.4 %collective-permute-start.10 = (bf16[1024,512]{1,0:T(8,128)(2,1)S(1)}, bf16[1024,512]{1,0:T(8,128)(2,1)}, u32[]{:S(2)}, u32[]{:S(2)}) collective-permute-start(bf16[1024,512]{1,0:T(8,128)(2,1)S(1)} %bitcast.136), channel_id=1, source_target_pairs={{0,16},{8,24},{16,0},{24,8},{1,17},{9,25},{17,1},{25,9},{2,18},{10... | collective-permute-start | bytes 3145736 | tf_op jit(solution)/shard_map/ppermute | solution.py:19
  188.9 106.2 %collective-permute-start = (bf16[1024,512]{1,0:T(8,128)(2,1)}, bf16[1024,512]{1,0:T(8,128)(2,1)}, u32[]{:S(2)}, u32[]{:S(2)}) collective-permute-start(bf16[1024,512]{1,0:T(8,128)(2,1)} %bitcast.9), channel_id=1, source_target_pairs={{0,8},{8,0},{16,24},{24,16},{1,9},{9,1},{17,25},{25,17},{2,10},{10... | collective-permute-start | bytes 3145736 | tf_op jit(solution)/shard_map/ppermute | solution.py:19
  189.0 90.7 %collective-permute-start.2 = (bf16[1024,512]{1,0:T(8,128)(2,1)}, bf16[1024,512]{1,0:T(8,128)(2,1)}, u32[]{:S(2)}, u32[]{:S(2)}) collective-permute-start(bf16[1024,512]{1,0:T(8,128)(2,1)} %collective-permute-done.1), channel_id=1, source_target_pairs={{0,8},{8,0},{16,24},{24,16},{1,9},{9,1},{17,25},{25,17},{2,10},{10... | collective-permute-start | bytes 3145736 | tf_op jit(solution)/shard_map/ppermute | solution.py:19
  210.1 73.7 %collective-permute-start.5 = (bf16[1024,512]{1,0:T(8,128)(2,1)}, bf16[1024,512]{1,0:T(8,128)(2,1)}, u32[]{:S(2)}, u32[]{:S(2)}) collective-permute-start(bf16[1024,512]{1,0:T(8,128)(2,1)} %collective-permute-done.4), channel_id=1, source_target_pairs={{0,8},{8,0},{16,24},{24,16},{1,9},{9,1},{17,25},{25,17},{2,10},{10... | collective-permute-start | bytes 3145736 | tf_op jit(solution)/shard_map/ppermute | solution.py:19
  232.6 54.8 %collective-permute-start.8 = (bf16[1024,512]{1,0:T(8,128)(2,1)}, bf16[1024,512]{1,0:T(8,128)(2,1)}, u32[]{:S(2)}, u32[]{:S(2)}) collective-permute-start(bf16[1024,512]{1,0:T(8,128)(2,1)} %collective-permute-done.7), channel_id=1, source_target_pairs={{0,8},{8,0},{16,24},{24,16},{1,9},{9,1},{17,25},{25,17},{2,10},{10... | collective-permute-start | bytes 3145736 | tf_op jit(solution)/shard_map/ppermute | solution.py:19
  254.0 37.5 %collective-permute-start.11 = (bf16[1024,512]{1,0:T(8,128)(2,1)}, bf16[1024,512]{1,0:T(8,128)(2,1)}, u32[]{:S(2)}, u32[]{:S(2)}) collective-permute-start(bf16[1024,512]{1,0:T(8,128)(2,1)} %collective-permute-done.10), channel_id=1, source_target_pairs={{0,8},{8,0},{16,24},{24,16},{1,9},{9,1},{17,25},{25,17},{2,10},{10... | collective-permute-start | bytes 3145736 | tf_op jit(solution)/shard_map/ppermute | solution.py:19
  254.0 4.1 %copy-start.10 = (bf16[4,1024,512]{2,1,0:T(8,128)(2,1)S(1)}, bf16[4,1024,512]{2,1,0:T(8,128)(2,1)}, u32[]{:S(2)}) copy-start(bf16[4,1024,512]{2,1,0:T(8,128)(2,1)} %all-gather.2.cloned.1.call-done) | copy-start | bytes 12582916
  279.7 19.0 %collective-permute-start.3 = (bf16[1024,512]{1,0:T(8,128)(2,1)S(1)}, bf16[1024,512]{1,0:T(8,128)(2,1)S(1)}, u32[]{:S(2)}, u32[]{:S(2)}) collective-permute-start(bf16[1024,512]{1,0:T(8,128)(2,1)S(1)} %bitcast.132), channel_id=1, source_target_pairs={{0,8},{8,0},{16,24},{24,16},{1,9},{9,1},{17,25},{25,17},{2,10},{10... | collective-permute-start | bytes 3145736 | tf_op jit(solution)/shard_map/ppermute | solution.py:19
  283.8 17.3 %collective-permute-start.6 = (bf16[1024,512]{1,0:T(8,128)(2,1)S(1)}, bf16[1024,512]{1,0:T(8,128)(2,1)S(1)}, u32[]{:S(2)}, u32[]{:S(2)}) collective-permute-start(bf16[1024,512]{1,0:T(8,128)(2,1)S(1)} %bitcast.135), channel_id=1, source_target_pairs={{0,8},{8,0},{16,24},{24,16},{1,9},{9,1},{17,25},{25,17},{2,10},{10... | collective-permute-start | bytes 3145736 | tf_op jit(solution)/shard_map/ppermute | solution.py:19
  287.4 16.1 %collective-permute-start.9 = (bf16[1024,512]{1,0:T(8,128)(2,1)S(1)}, bf16[1024,512]{1,0:T(8,128)(2,1)S(1)}, u32[]{:S(2)}, u32[]{:S(2)}) collective-permute-start(bf16[1024,512]{1,0:T(8,128)(2,1)S(1)} %bitcast.138), channel_id=1, source_target_pairs={{0,8},{8,0},{16,24},{24,16},{1,9},{9,1},{17,25},{25,17},{2,10},{10... | collective-permute-start | bytes 3145736 | tf_op jit(solution)/shard_map/ppermute | solution.py:19
  303.6 55.1 %copy-start.4 = (f32[512,512]{0,1:T(8,128)S(1)}, f32[512,512]{0,1:T(8,128)}, u32[]{:S(2)}) copy-start(f32[512,512]{0,1:T(8,128)} %get-tuple-element.17) | copy-start | bytes 3145732
  303.6 55.1 %copy-start.5 = (f32[512,512]{0,1:T(8,128)S(1)}, f32[512,512]{0,1:T(8,128)}, u32[]{:S(2)}) copy-start(f32[512,512]{0,1:T(8,128)} %get-tuple-element.25) | copy-start | bytes 3145732
  358.7 7.6 %copy-start = (f32[512,512]{0,1:T(8,128)S(1)}, f32[512,512]{0,1:T(8,128)}, u32[]{:S(2)}) copy-start(f32[512,512]{0,1:T(8,128)} %get-tuple-element.33) | copy-start | bytes 3145732
  358.7 7.6 %copy-start.1 = (f32[512,512]{0,1:T(8,128)S(1)}, f32[512,512]{0,1:T(8,128)}, u32[]{:S(2)}) copy-start(f32[512,512]{0,1:T(8,128)} %get-tuple-element.41) | copy-start | bytes 3145732
  358.7 7.6 %copy-start.2 = (f32[512,512]{0,1:T(8,128)S(1)}, f32[512,512]{0,1:T(8,128)}, u32[]{:S(2)}) copy-start(f32[512,512]{0,1:T(8,128)} %get-tuple-element.37) | copy-start | bytes 3145732
  358.7 7.6 %copy-start.3 = (f32[512,512]{0,1:T(8,128)S(1)}, f32[512,512]{0,1:T(8,128)}, u32[]{:S(2)}) copy-start(f32[512,512]{0,1:T(8,128)} %get-tuple-element.45) | copy-start | bytes 3145732
  358.7 7.6 %copy-start.6 = (f32[512,512]{0,1:T(8,128)S(1)}, f32[512,512]{0,1:T(8,128)}, u32[]{:S(2)}) copy-start(f32[512,512]{0,1:T(8,128)} %get-tuple-element.31) | copy-start | bytes 3145732
  358.7 7.6 %copy-start.7 = (f32[512,512]{0,1:T(8,128)S(1)}, f32[512,512]{0,1:T(8,128)}, u32[]{:S(2)}) copy-start(f32[512,512]{0,1:T(8,128)} %get-tuple-element.39) | copy-start | bytes 3145732
  358.7 7.6 %copy-start.8 = (f32[512,512]{0,1:T(8,128)S(1)}, f32[512,512]{0,1:T(8,128)}, u32[]{:S(2)}) copy-start(f32[512,512]{0,1:T(8,128)} %get-tuple-element.35) | copy-start | bytes 3145732
  358.7 7.6 %copy-start.9 = (f32[512,512]{0,1:T(8,128)S(1)}, f32[512,512]{0,1:T(8,128)}, u32[]{:S(2)}) copy-start(f32[512,512]{0,1:T(8,128)} %get-tuple-element.43) | copy-start | bytes 3145732
Sparse Core Ops, SparseCore 0:
  37.8 103.4 all-gather.1

commit v2 on v0

v2 whole, which is shorter than its diff:
```python
import functools
import math

import jax
import jax.numpy as jnp
from jax import lax
from jax.experimental import pallas as pl
from jax.experimental.pallas import tpu as pltpu
from jax.sharding import PartitionSpec as P

epsilon = 1e-06
lanes = 128
edges = (0.0, 0.25, 0.5, 0.75, 0.875, 1.0)
ANY = pl.BlockSpec(memory_space=pl.ANY)


def exchange(block, axis, distance):
    size = lax.axis_size(axis)
    return lax.ppermute(block, axis, [(i, i ^ distance) for i in range(size)])


def doubling(block, axis):
    size = lax.axis_size(axis)
    slots = {0: block}
    distance = size // 2
    while distance:
        for slot in list(slots):
            slots[slot ^ distance] = exchange(slots[slot], axis, distance)
        distance //= 2
    return [slots[slot] for slot in range(size)]


def pack_kernel(start, stride, hidden_ref, *refs):
    out_ref, sems = refs[-2], refs[-1]
    count, _, width = out_ref.shape
    copies = [
        pltpu.make_async_copy(
            hidden_ref.at[0, :, pl.ds(k * stride + start, width)], out_ref.at[k], sems.at[k]
        )
        for k in range(count)
    ]
    for copy in copies:
        copy.start()
    for copy in copies:
        copy.wait()


def pack(hidden, count, start, width, after):
    _, rows, total = hidden.shape
    return pl.pallas_call(
        functools.partial(pack_kernel, start, total // count),
        out_shape=jax.ShapeDtypeStruct((count, rows, width), hidden.dtype),
        in_specs=[ANY] * (1 + len(after)),
        out_specs=ANY,
        scratch_shapes=[pltpu.SemaphoreType.DMA((count,))],
        cost_estimate=pl.CostEstimate(
            flops=0, bytes_accessed=4 * count * rows * width, transcendentals=0
        ),
        name="pack_columns",
    )(hidden, *after)


def mask_kernel(user_count, valid_ref, user_ref, cot_ref, out_ref):
    rows, width = out_ref.shape[1:]
    keep = lax.broadcasted_iota(jnp.int32, (rows, width), 0) < valid_ref[0]
    for slot in range(user_count):
        column = pl.multiple_of((user_ref[0] ^ slot) * width, lanes)
        block = cot_ref[0, :, pl.ds(column, width)]
        out_ref[slot] = jnp.where(keep, block, jnp.zeros_like(block))


def mask(valid, user, cotangent, user_count):
    _, rows, total = cotangent.shape
    smem = pl.BlockSpec(memory_space=pltpu.SMEM)
    return pl.pallas_call(
        functools.partial(mask_kernel, user_count),
        out_shape=jax.ShapeDtypeStruct((user_count, rows, total // user_count), cotangent.dtype),
        in_specs=[smem, smem, pl.BlockSpec(memory_space=pltpu.VMEM)],
        out_specs=pl.BlockSpec(memory_space=pltpu.VMEM),
        name="mask_cotangent",
    )(valid, user, cotangent)


def order_kernel(tok_ref, *refs):
    out_ref, sems = refs[-2], refs[-1]
    slots = refs[:-2]
    copies = [
        pltpu.make_async_copy(slot_ref, out_ref.at[:, tok_ref[0] ^ s], sems.at[s])
        for s, slot_ref in enumerate(slots)
    ]
    for copy in copies:
        copy.start()
    for copy in copies:
        copy.wait()


def order(tok, slots):
    users, rows, width = slots[0].shape
    count = len(slots)
    return pl.pallas_call(
        order_kernel,
        out_shape=jax.ShapeDtypeStruct((users, count, rows, width), slots[0].dtype),
        in_specs=[pl.BlockSpec(memory_space=pltpu.SMEM)] + [ANY] * count,
        out_specs=ANY,
        scratch_shapes=[pltpu.SemaphoreType.DMA((count,))],
        name="order_tokens",
    )(tok, *slots)


def product_kernel(user_count, first, *refs):
    lefts, right_ref = refs[:user_count], refs[user_count]
    sums_in = None if first else refs[user_count + 1]
    product_ref, sums_ref, total = refs[-3:]
    step = pl.program_id(0)

    @pl.when(step == 0)
    def _():
        total[...] = jnp.zeros_like(total) if first else sums_in[0]

    for slot in range(user_count):
        value = lax.dot_general(
            lefts[slot][...],
            right_ref[slot],
            (((0,), (0,)), ((), ())),
            preferred_element_type=jnp.float32,
        )
        product_ref[slot] = value
        row = jnp.sum(value * value, axis=0, keepdims=True)
        for at in range(0, row.shape[1], lanes):
            total[slot : slot + 1, :] += row[:, at : at + lanes]

    @pl.when(step == pl.num_programs(0) - 1)
    def _():
        sums_ref[...] = jnp.broadcast_to(total[...][None], sums_ref.shape)


def product(lefts, right, start, own_width, before, copies):
    user_count, tokens, columns = right.shape
    width = lefts[0].shape[1]
    tile = math.gcd(math.gcd(width, start), 2 * lanes) if tokens <= 1024 else lanes
    first = before is None
    vmem = pl.BlockSpec(memory_space=pltpu.VMEM)
    in_specs = [pl.BlockSpec((tokens, tile), lambda i: (0, i))] * user_count
    in_specs += [
        pl.BlockSpec((user_count, tokens, columns), lambda i: (0, 0, 0), pipeline_mode=pl.Buffered(1))
    ]
    operands = [*lefts, right]
    aliases = {}
    if not first:
        gradients, sums = before
        in_specs += [vmem, ANY]
        operands += [sums, gradients]
        aliases = {user_count + 2: 0}
    return pl.pallas_call(
        functools.partial(product_kernel, user_count, first),
        grid=(width // tile,),
        out_shape=[
            jax.ShapeDtypeStruct((user_count, own_width, columns), jnp.float32),
            jax.ShapeDtypeStruct((copies, 8, lanes), jnp.float32),
        ],
        in_specs=in_specs,
        out_specs=[
            pl.BlockSpec((user_count, tile, columns), lambda i: (0, start // tile + i, 0)),
            vmem,
        ],
        scratch_shapes=[pltpu.VMEM((8, lanes), jnp.float32)],
        input_output_aliases=aliases,
        compiler_params=pltpu.CompilerParams(vmem_limit_bytes=48 * 2**20),
        cost_estimate=pl.CostEstimate(
            flops=2 * user_count * tokens * columns * width,
            bytes_accessed=2 * user_count * tokens * (width + columns) + 4 * user_count * width * columns,
            transcendentals=0,
        ),
        name="product_and_squares",
    )(*operands)


def combine_kernel(user_count, clip_bound, scaling, user_ref, sums_ref, gradient_ref, out_ref):
    per_user = sums_ref.shape[0] // user_count
    by_source = [
        jnp.sum(sums_ref[j * per_user : (j + 1) * per_user], axis=0) for j in range(user_count)
    ]
    factors = []
    for u in range(user_count):
        row = sum(by_source[j][j ^ u : (j ^ u) + 1, :] for j in range(user_count))
        norm_sq = jnp.sum(row, axis=1, keepdims=True)
        factors.append(jnp.minimum(1.0, clip_bound / jnp.sqrt(norm_sq + epsilon)) * scaling)
    result = None
    for slot in range(user_count):
        user = user_ref[0] ^ slot
        factor = sum(jnp.where(user == u, factors[u], 0.0) for u in range(user_count))
        term = factor * gradient_ref[slot]
        result = term if result is None else result + term
    out_ref[...] = result


def combine(user, sums, gradients, clip_bound, scaling):
    user_count, rows, columns = gradients.shape
    tile = min(rows, 256)
    return pl.pallas_call(
        functools.partial(combine_kernel, user_count, clip_bound, scaling),
        grid=(rows // tile,),
        out_shape=jax.ShapeDtypeStruct((rows, columns), jnp.float32),
        in_specs=[
            pl.BlockSpec(memory_space=pltpu.SMEM),
            pl.BlockSpec(memory_space=pltpu.VMEM),
            pl.BlockSpec((user_count, tile, columns), lambda i: (0, i, 0)),
        ],
        out_specs=pl.BlockSpec((tile, columns), lambda i: (i, 0)),
        compiler_params=pltpu.CompilerParams(vmem_limit_bytes=32 * 2**20),
        name="weighted_sum",
    )(user, sums, gradients)


def body(hidden, cotangent, lengths):
    tok_count = lax.axis_size("tok")
    user_count = lax.axis_size("user")
    tok_rows = hidden.shape[1]
    hidden_width = hidden.shape[2]
    model_width = cotangent.shape[2]
    capacity = tok_rows * tok_count
    own_width = hidden_width // tok_count
    columns = model_width // user_count
    clip_bound = math.sqrt(8.0 * hidden_width * model_width * capacity)
    scaling = math.sqrt(hidden_width * model_width) / (user_count * clip_bound)
    user = lax.axis_index("user").astype(jnp.int32).reshape(1)
    tok = lax.axis_index("tok").astype(jnp.int32).reshape(1)
    valid = lengths - tok * tok_rows

    units = own_width // lanes
    starts = sorted({round(edge * units) * lanes for edge in edges})
    bounds = list(zip(starts[:-1], starts[1:]))

    masked = mask(valid, user, cotangent, user_count)
    by_slot = [masked[0]] + [exchange(masked[s], "user", s) for s in range(1, user_count)]
    right = order(tok, doubling(jnp.stack(by_slot), "tok"))
    right = right.reshape(user_count, capacity, columns)

    before = None
    across = []
    done = []
    for at, (start, stop) in enumerate(bounds):
        after = []
        if at >= 2:
            after.append(across[at - 2])
        if at >= 3:
            after.append(done[at - 3])
        outgoing = pack(hidden, tok_count, start, stop - start, after)
        arrived = lax.all_to_all(outgoing, "tok", split_axis=0, concat_axis=0, tiled=True)
        arrived = arrived.reshape(capacity, stop - start)
        lefts = doubling(arrived, "user")
        across.append(lefts[user_count // 2])
        last = at == len(bounds) - 1
        before = product(
            lefts, right, start, own_width, before, tok_count * user_count if last else 1
        )
        done.append(before[1])
    gradients, sums = before
    sums = lax.all_to_all(sums, ("user", "tok"), split_axis=0, concat_axis=0, tiled=True)
    return combine(user, sums, gradients, clip_bound, scaling)


def solution(mesh):
    return jax.shard_map(
        body,
        mesh=mesh,
        in_specs=(P("user", "tok", None), P("user", "tok", None), P("user")),
        out_specs=P("tok", "user"),
        check_vma=False,
    )
```

time: 356 us -> 490 us (1.38)
  Pallas kernels: 0 us -> 298 us
  waiting for transfers between devices: 266 us -> 104 us
  starting transfers between devices: 7.49 us -> 52 us
  matrix products: 16.9 us -> 0 us
  between operations: 14.8 us -> 0.91 us
  other arithmetic: 12.6 us -> 1.04 us
  blocking collectives: 19.8 us -> 13.6 us
    pallas_call x0 -> x13, Pallas kernels: none -> 298 us  [the longest x5 133 us: pack(): pl.pallas_call(functools.partial(pack_kernel, start, total // count), out...]
    all_to_all x1 -> x5, waiting for transfers between devices: 142 us -> 10 us  [body(): lax.all_to_all(outgoing, 'tok', split_axis=0, concat_axis=0, tiled=True)]
    reduce_scatter x1 -> x0, waiting for transfers between devices: 124 us -> none  [body(): lax.psum_scatter(gradient * factor, 'user', scatter_dimension=1, tiled=True)]
    ppermute x0 -> x25, waiting for transfers between devices: none -> 94.1 us  [exchange(): return lax.ppermute(block, axis, [(i, i ^ distance) for i in range(size)])]
    all_to_all x1 -> x5, starting transfers between devices: 7.41 us -> 31 us  [body(): lax.all_to_all(outgoing, 'tok', split_axis=0, concat_axis=0, tiled=True)]
    ppermute x0 -> x25, starting transfers between devices: none -> 21 us  [exchange(): return lax.ppermute(block, axis, [(i, i ^ distance) for i in range(size)])]
    psum x1 -> x0, blocking collectives: 19.8 us -> none  [body(): norm_sq = lax.psum(partial_value, 'tok')]
    dot_general x1 -> x0, matrix products: 16.9 us -> none  [contract(): lax.dot_general(left, right, (((0,), (0,)), ((), ())), preferred_element_...]
  transfers between devices with their start and end apart: 3 -> 30, of which waited for: 2 -> 9; matrix products, arithmetic and copies ran while one was open for 2% -> 1% of each run, Pallas kernels for 0% -> 52%
where the time goes in v2:
time: 490 us; the launch traced here: 489 us
  Pallas kernels  298 us (61%)
  waiting for transfers between devices  104 us (21%)
  starting transfers between devices  52 us (11%)
  local copies, waits for them, and re-layouts  19.6 us (4%)
  blocking collectives  13.6 us (3%)
    pallas_call x5, Pallas kernels, pack(): pl.pallas_call(functools.partial(pack_kernel, start, total // count), out...  133 us
    pallas_call x1, Pallas kernels, order(): pl.pallas_call(order_kernel, out_shape=jax.ShapeDtypeStruct((users, count...  128 us
    ppermute x25, waiting for transfers between devices, exchange(): return lax.ppermute(block, axis, [(i, i ^ distance) for i in range(size)])  94.1 us
    all_to_all x5, starting transfers between devices, body(): lax.all_to_all(outgoing, 'tok', split_axis=0, concat_axis=0, tiled=True)  31 us
    pallas_call x5, Pallas kernels, product(): pl.pallas_call(functools.partial(product_kernel, user_count, first), grid...  29.3 us
    ppermute x25, starting transfers between devices, exchange(): return lax.ppermute(block, axis, [(i, i ^ distance) for i in range(size)])  21 us
    unnamed x44, local copies, waits for them, and re-layouts  17.7 us
    all_to_all x1, blocking collectives, body(): lax.all_to_all(sums, ('user', 'tok'), split_axis=0, concat_axis=0, tiled=...  13.6 us
  transfers between devices with their start and end apart: 30, of which 9 were waited for; matrix products, arithmetic and copies ran while one was open for 1% of the time, Pallas kernels for 52%

profile of v2, /device:TPU:0, one launch (start us, length us, event | category | flops | bytes accessed | tf_op | source)
XLA Modules:
  0.0 489.4 jit_solution(142878499356613382)
XLA Ops:
  0.0 32.9 %pack_columns.5 = bf16[8,128,512]{2,1,0:T(8,128)(2,1)} custom-call(bf16[1,128,16384]{2,1,0:T(8,128)(2,1)} %hidden_ref.9), custom_call_target="tpu_custom_call" | custom-call | bytes 2097152 | tf_op jit(solution)/shard_map/pack_columns/pallas_call | solution.py:50
  32.9 7.3 %all-to-all-start = ((bf16[8,128,512]{2,1,0:T(8,128)(2,1)}), bf16[8,128,512]{2,1,0:T(8,128)(2,1)S(1)}, u32[]{:S(2)}, u32[]{:S(2)}) async-start(bf16[8,128,512]{2,1,0:T(8,128)(2,1)} %pack_columns.5), calls=%async_computation | async-start | bytes 2097152 | tf_op jit(solution)/shard_map/all_to_all | solution.py:249
  40.2 32.9 %pack_columns.7 = bf16[8,128,512]{2,1,0:T(8,128)(2,1)} custom-call(bf16[1,128,16384]{2,1,0:T(8,128)(2,1)} %hidden_ref.9), custom_call_target="tpu_custom_call" | custom-call | bytes 2097152 | tf_op jit(solution)/shard_map/pack_columns/pallas_call | solution.py:50
  73.2 0.0 all-to-all-done
  73.2 6.0 %all-to-all-start.2 = ((bf16[8,128,512]{2,1,0:T(8,128)(2,1)}), bf16[8,128,512]{2,1,0:T(8,128)(2,1)S(1)}, u32[]{:S(2)}, u32[]{:S(2)}) async-start(bf16[8,128,512]{2,1,0:T(8,128)(2,1)} %pack_columns.7), calls=%async_computation.2 | async-start | bytes 2097152 | tf_op jit(solution)/shard_map/all_to_all | solution.py:249
  79.2 1.5 collective-permute-start
  81.3 1.9 mask_cotangent.1
  83.2 1.8 fusion
  85.1 0.6 collective-permute-start.5
  85.7 1.5 collective-permute-start.6
  87.2 18.1 %collective-permute-done.refs_0_.refs_2_ = bf16[1024,512]{1,0:T(8,128)(2,1)S(1)} collective-permute-done((bf16[1024,512]{1,0:T(8,128)(2,1)S(1)}, bf16[1024,512]{1,0:T(8,128)(2,1)S(1)}, u32[]{:S(2)}, u32[]{:S(2)}) %collective-permute-start) | collective-permute-done | bytes 1048608 | tf_op jit(solution)/shard_map/ppermute | solution.py:19
  105.3 1.0 copy-done.1
  106.3 32.9 %pack_columns.6 = bf16[8,128,512]{2,1,0:T(8,128)(2,1)} custom-call(bf16[1,128,16384]{2,1,0:T(8,128)(2,1)} %hidden_ref.9, bf16[1024,512]{1,0:T(8,128)(2,1)} %copy-done.1), custom_call_target="tpu_custom_call" | custom-call | bytes 2097152 | tf_op jit(solution)/shard_map/pack_columns/pallas_call | solution.py:50
  139.3 0.0 all-to-all-done.2
  139.3 6.0 %all-to-all-start.1 = ((bf16[8,128,512]{2,1,0:T(8,128)(2,1)}), bf16[8,128,512]{2,1,0:T(8,128)(2,1)S(1)}, u32[]{:S(2)}, u32[]{:S(2)}) async-start(bf16[8,128,512]{2,1,0:T(8,128)(2,1)} %pack_columns.6), calls=%async_computation.1 | async-start | bytes 2097152 | tf_op jit(solution)/shard_map/all_to_all | solution.py:249
  145.3 0.0 collective-permute-done.7
  145.3 1.0 pad_maximum_fusion.refs_0_
  146.4 3.0 collective-permute-start.11
  149.4 1.5 collective-permute-start.9
  150.8 1.5 collective-permute-start.8
  152.3 37.2 %collective-permute-done.11.refs_4_ = bf16[4,128,512]{2,1,0:T(8,128)(2,1)S(1)} collective-permute-done((bf16[4,128,512]{2,1,0:T(8,128)(2,1)S(1)}, bf16[4,128,512]{2,1,0:T(8,128)(2,1)S(1)}, u32[]{:S(2)}, u32[]{:S(2)}) %collective-permute-start.11) | collective-permute-done | bytes 524320 | tf_op jit(solution)/shard_map/ppermute | solution.py:19
  189.5 1.6 collective-permute-start.3
  191.1 1.1 collective-permute-start.12
  192.2 0.5 collective-permute-start.16
  192.7 7.9 %collective-permute-done.13.refs_6_ = bf16[4,128,512]{2,1,0:T(8,128)(2,1)S(1)} collective-permute-done((bf16[4,128,512]{2,1,0:T(8,128)(2,1)S(1)}, bf16[4,128,512]{2,1,0:T(8,128)(2,1)S(1)}, u32[]{:S(2)}, u32[]{:S(2)}) %collective-permute-start.13) | collective-permute-done | bytes 524320 | tf_op jit(solution)/shard_map/ppermute | solution.py:19
  200.6 1.2 collective-permute-start.10
  201.8 0.6 collective-permute-done.12.refs_5_
  202.4 2.2 collective-permute-start.14
  204.6 10.9 %collective-permute-done.10.refs_3_ = bf16[4,128,512]{2,1,0:T(8,128)(2,1)S(1)} collective-permute-done((bf16[4,128,512]{2,1,0:T(8,128)(2,1)S(1)}, bf16[4,128,512]{2,1,0:T(8,128)(2,1)S(1)}, u32[]{:S(2)}, u32[]{:S(2)}) %collective-permute-start.10) | collective-permute-done | bytes 524320 | tf_op jit(solution)/shard_map/ppermute | solution.py:19
  215.5 0.6 collective-permute-start.4
  216.1 0.2 copy-done.21
  216.3 7.3 %collective-permute-done.14.refs_7_ = bf16[4,128,512]{2,1,0:T(8,128)(2,1)} collective-permute-done((bf16[4,128,512]{2,1,0:T(8,128)(2,1)S(1)}, bf16[4,128,512]{2,1,0:T(8,128)(2,1)}, u32[]{:S(2)}, u32[]{:S(2)}) %collective-permute-start.14) | collective-permute-done | bytes 524320 | tf_op jit(solution)/shard_map/ppermute | solution.py:19
  223.6 128.2 %order_tokens.1 = bf16[4,8,128,512]{3,2,1,0:T(8,128)(2,1)} custom-call(s32[1]{0:T(128)} %bitcast.4.tok_ref, bf16[4,128,512]{2,1,0:T(8,128)(2,1)} %copy-done.15, bf16[4,128,512]{2,1,0:T(8,128)(2,1)} %copy-done.18, bf16[4,128,512]{2,1,0:T(8,128)(2,1)} %copy-done.17, bf16[4,128,512]{2,1,0:T(8,128)(2,1)} %copy-done.21, bf16[4,128,512]{2,1,0:T(8,128)(2,1)} %copy-done.16, ...), custom_call_target="tpu_custom_call" | custom-call | tf_op jit(solution)/shard_map/order_tokens/pallas_call | solution.py:100
  351.9 1.0 copy-done.7
  352.9 0.5 collective-permute-start.1
  353.4 1.2 copy-done.2
  354.6 6.5 %product_and_squares.5 = (f32[4,2048,512]{2,1,0:T(8,128)}, f32[1,8,128]{2,1,0:T(8,128)S(1)}) custom-call(bf16[1024,512]{1,0:T(8,128)(2,1)S(1)} %bitcast.19, bf16[1024,512]{1,0:T(8,128)(2,1)} %collective-permute-done.15.refs_1_, bf16[1024,512]{1,0:T(8,128)(2,1)S(1)} %copy-done.2, bf16[1024,512]{1,0:T(8,128)(2,1)} %collective-permute-done.16.refs_3_, ...), custom_call_target="tpu_custom_call" | custom-call | flops 2147483648 | bytes 12582912 | tf_op jit(solution)/shard_map/product_and_squares/pallas_call | solution.py:154
  361.2 0.6 copy-done.13
  361.7 17.1 %pack_columns.9 = bf16[8,128,256]{2,1,0:T(8,128)(2,1)} custom-call(bf16[1,128,16384]{2,1,0:T(8,128)(2,1)} %hidden_ref.9, bf16[1024,512]{1,0:T(8,128)(2,1)} %copy-done.5, f32[1,8,128]{2,1,0:T(8,128)} %copy-done.13), custom_call_target="tpu_custom_call" | custom-call | bytes 1048576 | tf_op jit(solution)/shard_map/pack_columns/pallas_call | solution.py:50
  378.8 5.6 %all-to-all-start.4 = ((bf16[8,128,256]{2,1,0:T(8,128)(2,1)}), bf16[8,128,256]{2,1,0:T(8,128)(2,1)}, u32[]{:S(2)}, u32[]{:S(2)}) async-start(bf16[8,128,256]{2,1,0:T(8,128)(2,1)} %pack_columns.9), calls=%async_computation.4 | async-start | bytes 1048576 | tf_op jit(solution)/shard_map/all_to_all | solution.py:249
  384.5 1.2 copy-done.6
  385.7 1.2 copy-done.10
  386.9 0.7 copy-done.14
  387.6 6.5 %product_and_squares.6 = (f32[4,2048,512]{2,1,0:T(8,128)}, f32[1,8,128]{2,1,0:T(8,128)S(1)}) custom-call(bf16[1024,512]{1,0:T(8,128)(2,1)S(1)} %bitcast.25, bf16[1024,512]{1,0:T(8,128)(2,1)} %collective-permute-done.2.refs_1_, bf16[1024,512]{1,0:T(8,128)(2,1)S(1)} %copy-done.6, ...), custom_call_target="tpu_custom_call", output_to_operand_aliasing={{0}: (6, {})} | custom-call | flops 2147483648 | bytes 12582912 | tf_op jit(solution)/shard_map/product_and_squares/pallas_call | solution.py:154
  394.1 0.6 copy-done.11
  394.7 1.0 copy-done.3
  395.8 17.1 %pack_columns.8 = bf16[8,128,256]{2,1,0:T(8,128)(2,1)} custom-call(bf16[1,128,16384]{2,1,0:T(8,128)(2,1)} %hidden_ref.9, bf16[1024,512]{1,0:T(8,128)(2,1)} %copy-done.3, f32[1,8,128]{2,1,0:T(8,128)} %copy-done.11), custom_call_target="tpu_custom_call" | custom-call | bytes 1048576 | tf_op jit(solution)/shard_map/pack_columns/pallas_call | solution.py:50
  412.8 6.0 %all-to-all-start.3 = ((bf16[8,128,256]{2,1,0:T(8,128)(2,1)}), bf16[8,128,256]{2,1,0:T(8,128)(2,1)S(1)}, u32[]{:S(2)}, u32[]{:S(2)}) async-start(bf16[8,128,256]{2,1,0:T(8,128)(2,1)} %pack_columns.8), calls=%async_computation.3 | async-start | bytes 1048576 | tf_op jit(solution)/shard_map/all_to_all | solution.py:249
  418.8 0.5 collective-permute-start.24
  419.3 1.5 collective-permute-start.21
  420.8 10.0 %all-to-all-done.3 = bf16[8,128,256]{2,1,0:T(8,128)(2,1)S(1)} async-done(((bf16[8,128,256]{2,1,0:T(8,128)(2,1)}), bf16[8,128,256]{2,1,0:T(8,128)(2,1)S(1)}, u32[]{:S(2)}, u32[]{:S(2)}) %all-to-all-start.3) | async-done | bytes 524320 | tf_op jit(solution)/shard_map/all_to_all | solution.py:249
  430.9 1.3 collective-permute-start.18
  432.1 2.2 collective-permute-done.21.refs_2_
  434.3 0.5 collective-permute-start.17
  434.8 9.8 %collective-permute-done.18.refs_2_ = bf16[1024,256]{1,0:T(8,128)(2,1)S(1)} collective-permute-done((bf16[1024,256]{1,0:T(8,128)(2,1)S(1)}, bf16[1024,256]{1,0:T(8,128)(2,1)S(1)}, u32[]{:S(2)}, u32[]{:S(2)}) %collective-permute-start.18) | collective-permute-done | bytes 524320 | tf_op jit(solution)/shard_map/ppermute | solution.py:19
  444.7 1.2 copy-done.4
  445.9 1.2 copy-done.8
  447.2 0.7 copy-done.12
  447.8 6.3 %product_and_squares.7 = (f32[4,2048,512]{2,1,0:T(8,128)}, f32[1,8,128]{2,1,0:T(8,128)S(1)}) custom-call(bf16[1024,512]{1,0:T(8,128)(2,1)S(1)} %bitcast.22, bf16[1024,512]{1,0:T(8,128)(2,1)S(1)} %collective-permute-done.23.refs_1_, bf16[1024,512]{1,0:T(8,128)(2,1)S(1)} %copy-done.4, ...), custom_call_target="tpu_custom_call", output_to_operand_aliasing={{0}: (6, {})} | custom-call | flops 2147483648 | bytes 12582912 | tf_op jit(solution)/shard_map/product_and_squares/pallas_call | solution.py:154
  454.1 5.0 %product_and_squares.8 = (f32[4,2048,512]{2,1,0:T(8,128)}, f32[1,8,128]{2,1,0:T(8,128)S(1)}) custom-call(bf16[1024,256]{1,0:T(8,128)(2,1)} %bitcast.13.refs_0_, bf16[1024,256]{1,0:T(8,128)(2,1)S(1)} %collective-permute-done.20.refs_1_, bf16[1024,256]{1,0:T(8,128)(2,1)S(1)} %collective-permute-done.21.refs_2_, ...), custom_call_target="tpu_custom_call", output_to_operand_aliasing={{0}: (6, {})} | custom-call | flops 1073741824 | bytes 8388608 | tf_op jit(solution)/shard_map/product_and_squares/pallas_call | solution.py:154
  459.2 4.9 %product_and_squares.9 = (f32[4,2048,512]{2,1,0:T(8,128)}, f32[32,8,128]{2,1,0:T(8,128)S(1)}) custom-call(bf16[1024,256]{1,0:T(8,128)(2,1)S(1)} %bitcast.28, bf16[1024,256]{1,0:T(8,128)(2,1)S(1)} %collective-permute-done.17.refs_1_, bf16[1024,256]{1,0:T(8,128)(2,1)S(1)} %collective-permute-done.18.refs_2_, ...), custom_call_target="tpu_custom_call", output_to_operand_aliasing={{0}: (6, {})} | custom-call | flops 1073741824 | bytes 8388608 | tf_op jit(solution)/shard_map/product_and_squares/pallas_call | solution.py:154
  464.1 13.6 %all_to_all.30.sums_ref = f32[32,8,128]{2,1,0:T(8,128)S(1)} all-to-all(f32[32,8,128]{2,1,0:T(8,128)S(1)} %get-tuple-element.23), channel_id=1, replica_groups=mesh['user'=4,'tok'=8] {'user','tok'}, dimensions={0} | all-to-all | bytes 262144 | tf_op jit(solution)/shard_map/all_to_all | solution.py:259
  477.7 5.8 %copy-done = f32[4,2048,512]{2,1,0:T(8,128)S(1)} copy-done((f32[4,2048,512]{2,1,0:T(8,128)S(1)}, f32[4,2048,512]{2,1,0:T(8,128)}, u32[]{:S(2)}) %copy-start) | copy-done | bytes 16777240
  483.5 6.0 %weighted_sum.1 = f32[2048,512]{1,0:T(8,128)} custom-call(s32[1]{0:T(128)} %bitcast.user_ref, f32[32,8,128]{2,1,0:T(8,128)S(1)} %all_to_all.30.sums_ref, f32[4,2048,512]{2,1,0:T(8,128)S(1)} %copy-done), custom_call_target="tpu_custom_call" | custom-call | tf_op jit(solution)/shard_map/weighted_sum/pallas_call | solution.py:200
  (56 shorter events, 0.1 us)
Async XLA Ops:
  32.9 40.2 %all-to-all-start = ((bf16[8,128,512]{2,1,0:T(8,128)(2,1)}), bf16[8,128,512]{2,1,0:T(8,128)(2,1)S(1)}, u32[]{:S(2)}, u32[]{:S(2)}) async-start(bf16[8,128,512]{2,1,0:T(8,128)(2,1)} %pack_columns.5), calls=%async_computation | async-start | bytes 2097152 | tf_op jit(solution)/shard_map/all_to_all | solution.py:249
  73.2 66.1 %all-to-all-start.2 = ((bf16[8,128,512]{2,1,0:T(8,128)(2,1)}), bf16[8,128,512]{2,1,0:T(8,128)(2,1)S(1)}, u32[]{:S(2)}, u32[]{:S(2)}) async-start(bf16[8,128,512]{2,1,0:T(8,128)(2,1)} %pack_columns.7), calls=%async_computation.2 | async-start | bytes 2097152 | tf_op jit(solution)/shard_map/all_to_all | solution.py:249
  79.2 26.1 %collective-permute-start = (bf16[1024,512]{1,0:T(8,128)(2,1)S(1)}, bf16[1024,512]{1,0:T(8,128)(2,1)S(1)}, u32[]{:S(2)}, u32[]{:S(2)}) collective-permute-start(bf16[1024,512]{1,0:T(8,128)(2,1)S(1)} %bitcast.17), channel_id=1, source_target_pairs={{0,16},{8,24},{16,0},{24,8},{1,17},{9,25},{17,1},{25,9},{2,18},{10... | collective-permute-start | bytes 3145736 | tf_op jit(solution)/shard_map/ppermute | solution.py:19
  85.1 60.3 %collective-permute-start.7 = (bf16[128,512]{1,0:T(8,128)(2,1)}, bf16[128,512]{1,0:T(8,128)(2,1)S(1)}, u32[]{:S(2)}, u32[]{:S(2)}) collective-permute-start(bf16[128,512]{1,0:T(8,128)(2,1)} %get-tuple-element.26), channel_id=1, source_target_pairs={{0,24},{8,16},{16,8},{24,0},{1,25},{9,17},{17,9},{25,1},{2,26},{10... | collective-permute-start | bytes 393224 | tf_op jit(solution)/shard_map/ppermute | solution.py:19
  85.1 60.3 %collective-permute-start.5 = (bf16[128,512]{1,0:T(8,128)(2,1)}, bf16[128,512]{1,0:T(8,128)(2,1)}, u32[]{:S(2)}, u32[]{:S(2)}) collective-permute-start(bf16[128,512]{1,0:T(8,128)(2,1)} %get-tuple-element.28), channel_id=1, source_target_pairs={{0,8},{8,0},{16,24},{24,16},{1,9},{9,1},{17,25},{25,17},{2,10},{10... | collective-permute-start | bytes 393224 | tf_op jit(solution)/shard_map/ppermute | solution.py:19
  85.7 59.6 %collective-permute-start.6 = (bf16[128,512]{1,0:T(8,128)(2,1)S(1)}, bf16[128,512]{1,0:T(8,128)(2,1)}, u32[]{:S(2)}, u32[]{:S(2)}) collective-permute-start(bf16[128,512]{1,0:T(8,128)(2,1)S(1)} %get-tuple-element.27), channel_id=1, source_target_pairs={{0,16},{8,24},{16,0},{24,8},{1,17},{9,25},{17,1},{25,9},{2,18},{10... | collective-permute-start | bytes 393224 | tf_op jit(solution)/shard_map/ppermute | solution.py:19
  105.3 1.0 copy-start.1
  139.3 50.2 %copy-start.9 = (bf16[8,128,512]{2,1,0:T(8,128)(2,1)}, bf16[8,128,512]{2,1,0:T(8,128)(2,1)S(1)}, u32[]{:S(2)}) copy-start(bf16[8,128,512]{2,1,0:T(8,128)(2,1)S(1)} %all-to-all-done.2) | copy-start | bytes 3145732
  139.3 212.6 %all-to-all-start.1 = ((bf16[8,128,512]{2,1,0:T(8,128)(2,1)}), bf16[8,128,512]{2,1,0:T(8,128)(2,1)S(1)}, u32[]{:S(2)}, u32[]{:S(2)}) async-start(bf16[8,128,512]{2,1,0:T(8,128)(2,1)} %pack_columns.6), calls=%async_computation.1 | async-start | bytes 2097152 | tf_op jit(solution)/shard_map/all_to_all | solution.py:249
  146.4 69.1 %copy-start.15 = (bf16[4,128,512]{2,1,0:T(8,128)(2,1)}, bf16[4,128,512]{2,1,0:T(8,128)(2,1)S(1)}, u32[]{:S(2)}) copy-start(bf16[4,128,512]{2,1,0:T(8,128)(2,1)S(1)} %pad_maximum_fusion.refs_0_) | copy-start | bytes 1572868
  146.4 43.1 %collective-permute-start.11 = (bf16[4,128,512]{2,1,0:T(8,128)(2,1)S(1)}, bf16[4,128,512]{2,1,0:T(8,128)(2,1)S(1)}, u32[]{:S(2)}, u32[]{:S(2)}) collective-permute-start(bf16[4,128,512]{2,1,0:T(8,128)(2,1)S(1)} %pad_maximum_fusion.refs_0_), channel_id=1, source_target_pairs={{0,4},{1,5},{2,6},{3,7},{4,0},{5,1},{6,2},{7,3},{8,12},{9,13},{10,... | collective-permute-start | bytes 1572872 | tf_op jit(solution)/shard_map/ppermute | solution.py:19
  149.4 42.8 %collective-permute-start.9 = (bf16[4,128,512]{2,1,0:T(8,128)(2,1)S(1)}, bf16[4,128,512]{2,1,0:T(8,128)(2,1)S(1)}, u32[]{:S(2)}, u32[]{:S(2)}) collective-permute-start(bf16[4,128,512]{2,1,0:T(8,128)(2,1)S(1)} %pad_maximum_fusion.refs_0_), channel_id=1, source_target_pairs={{0,2},{1,3},{2,0},{3,1},{4,6},{5,7},{6,4},{7,5},{8,10},{9,11},{10,... | collective-permute-start | bytes 1572872 | tf_op jit(solution)/shard_map/ppermute | solution.py:19
  150.8 41.4 %collective-permute-start.8 = (bf16[4,128,512]{2,1,0:T(8,128)(2,1)S(1)}, bf16[4,128,512]{2,1,0:T(8,128)(2,1)S(1)}, u32[]{:S(2)}, u32[]{:S(2)}) collective-permute-start(bf16[4,128,512]{2,1,0:T(8,128)(2,1)S(1)} %pad_maximum_fusion.refs_0_), channel_id=1, source_target_pairs={{0,1},{1,0},{2,3},{3,2},{4,5},{5,4},{6,7},{7,6},{8,9},{9,8},{10,11... | collective-permute-start | bytes 1572872 | tf_op jit(solution)/shard_map/ppermute | solution.py:19
  189.5 26.6 %copy-start.16 = (bf16[4,128,512]{2,1,0:T(8,128)(2,1)}, bf16[4,128,512]{2,1,0:T(8,128)(2,1)S(1)}, u32[]{:S(2)}) copy-start(bf16[4,128,512]{2,1,0:T(8,128)(2,1)S(1)} %collective-permute-done.11.refs_4_) | copy-start | bytes 1572868
  189.5 11.1 %collective-permute-start.13 = (bf16[4,128,512]{2,1,0:T(8,128)(2,1)S(1)}, bf16[4,128,512]{2,1,0:T(8,128)(2,1)S(1)}, u32[]{:S(2)}, u32[]{:S(2)}) collective-permute-start(bf16[4,128,512]{2,1,0:T(8,128)(2,1)S(1)} %collective-permute-done.11.refs_4_), channel_id=1, source_target_pairs={{0,2},{1,3},{2,0},{3,1},{4,6},{5,7},{6,4},{7,5},{8,10},{9,11},{10,... | collective-permute-start | bytes 1572872 | tf_op jit(solution)/shard_map/ppermute | solution.py:19
  189.5 26.0 %collective-permute-start.3 = (bf16[1024,512]{1,0:T(8,128)(2,1)}, bf16[1024,512]{1,0:T(8,128)(2,1)S(1)}, u32[]{:S(2)}, u32[]{:S(2)}) collective-permute-start(bf16[1024,512]{1,0:T(8,128)(2,1)} %bitcast.23), channel_id=1, source_target_pairs={{0,16},{8,24},{16,0},{24,8},{1,17},{9,25},{17,1},{25,9},{2,18},{10... | collective-permute-start | bytes 3145736 | tf_op jit(solution)/shard_map/ppermute | solution.py:19
  191.1 11.4 %collective-permute-start.12 = (bf16[4,128,512]{2,1,0:T(8,128)(2,1)S(1)}, bf16[4,128,512]{2,1,0:T(8,128)(2,1)S(1)}, u32[]{:S(2)}, u32[]{:S(2)}) collective-permute-start(bf16[4,128,512]{2,1,0:T(8,128)(2,1)S(1)} %collective-permute-done.11.refs_4_), channel_id=1, source_target_pairs={{0,1},{1,0},{2,3},{3,2},{4,5},{5,4},{6,7},{7,6},{8,9},{9,8},{10,11... | collective-permute-start | bytes 1572872 | tf_op jit(solution)/shard_map/ppermute | solution.py:19
  192.2 23.9 %copy-start.17 = (bf16[4,128,512]{2,1,0:T(8,128)(2,1)}, bf16[4,128,512]{2,1,0:T(8,128)(2,1)S(1)}, u32[]{:S(2)}) copy-start(bf16[4,128,512]{2,1,0:T(8,128)(2,1)S(1)} %collective-permute-done.9.refs_2_) | copy-start | bytes 1572868
  192.2 161.2 %collective-permute-start.15 = (bf16[1024,512]{1,0:T(8,128)(2,1)S(1)}, bf16[1024,512]{1,0:T(8,128)(2,1)}, u32[]{:S(2)}, u32[]{:S(2)}) collective-permute-start(bf16[1024,512]{1,0:T(8,128)(2,1)S(1)} %bitcast.18), channel_id=1, source_target_pairs={{0,8},{8,0},{16,24},{24,16},{1,9},{9,1},{17,25},{25,17},{2,10},{10... | collective-permute-start | bytes 3145736 | tf_op jit(solution)/shard_map/ppermute | solution.py:19
  192.2 23.9 %copy-start.18 = (bf16[4,128,512]{2,1,0:T(8,128)(2,1)}, bf16[4,128,512]{2,1,0:T(8,128)(2,1)S(1)}, u32[]{:S(2)}) copy-start(bf16[4,128,512]{2,1,0:T(8,128)(2,1)S(1)} %collective-permute-done.8.refs_1_) | copy-start | bytes 1572868
  192.2 161.2 %collective-permute-start.16 = (bf16[1024,512]{1,0:T(8,128)(2,1)}, bf16[1024,512]{1,0:T(8,128)(2,1)}, u32[]{:S(2)}, u32[]{:S(2)}) collective-permute-start(bf16[1024,512]{1,0:T(8,128)(2,1)} %copy-done.1), channel_id=1, source_target_pairs={{0,8},{8,0},{16,24},{24,16},{1,9},{9,1},{17,25},{25,17},{2,10},{10... | collective-permute-start | bytes 3145736 | tf_op jit(solution)/shard_map/ppermute | solution.py:19
  200.6 15.5 %copy-start.19 = (bf16[4,128,512]{2,1,0:T(8,128)(2,1)}, bf16[4,128,512]{2,1,0:T(8,128)(2,1)S(1)}, u32[]{:S(2)}) copy-start(bf16[4,128,512]{2,1,0:T(8,128)(2,1)S(1)} %collective-permute-done.13.refs_6_) | copy-start | bytes 1572868
  200.6 14.9 %collective-permute-start.10 = (bf16[4,128,512]{2,1,0:T(8,128)(2,1)S(1)}, bf16[4,128,512]{2,1,0:T(8,128)(2,1)S(1)}, u32[]{:S(2)}, u32[]{:S(2)}) collective-permute-start(bf16[4,128,512]{2,1,0:T(8,128)(2,1)S(1)} %collective-permute-done.9.refs_2_), channel_id=1, source_target_pairs={{0,1},{1,0},{2,3},{3,2},{4,5},{5,4},{6,7},{7,6},{8,9},{9,8},{10,11... | collective-permute-start | bytes 1572872 | tf_op jit(solution)/shard_map/ppermute | solution.py:19
  202.4 13.7 %copy-start.20 = (bf16[4,128,512]{2,1,0:T(8,128)(2,1)}, bf16[4,128,512]{2,1,0:T(8,128)(2,1)S(1)}, u32[]{:S(2)}) copy-start(bf16[4,128,512]{2,1,0:T(8,128)(2,1)S(1)} %collective-permute-done.12.refs_5_) | copy-start | bytes 1572868
  202.4 21.2 %collective-permute-start.14 = (bf16[4,128,512]{2,1,0:T(8,128)(2,1)S(1)}, bf16[4,128,512]{2,1,0:T(8,128)(2,1)}, u32[]{:S(2)}, u32[]{:S(2)}) collective-permute-start(bf16[4,128,512]{2,1,0:T(8,128)(2,1)S(1)} %collective-permute-done.13.refs_6_), channel_id=1, source_target_pairs={{0,1},{1,0},{2,3},{3,2},{4,5},{5,4},{6,7},{7,6},{8,9},{9,8},{10,11... | collective-permute-start | bytes 1572872 | tf_op jit(solution)/shard_map/ppermute | solution.py:19
  215.5 0.8 copy-start.21
  215.5 168.9 %collective-permute-start.2 = (bf16[1024,512]{1,0:T(8,128)(2,1)}, bf16[1024,512]{1,0:T(8,128)(2,1)}, u32[]{:S(2)}, u32[]{:S(2)}) collective-permute-start(bf16[1024,512]{1,0:T(8,128)(2,1)} %bitcast.24), channel_id=1, source_target_pairs={{0,8},{8,0},{16,24},{24,16},{1,9},{9,1},{17,25},{25,17},{2,10},{10... | collective-permute-start | bytes 3145736 | tf_op jit(solution)/shard_map/ppermute | solution.py:19
  215.5 146.2 %copy-start.5 = (bf16[1024,512]{1,0:T(8,128)(2,1)}, bf16[1024,512]{1,0:T(8,128)(2,1)S(1)}, u32[]{:S(2)}) copy-start(bf16[1024,512]{1,0:T(8,128)(2,1)S(1)} %collective-permute-done.3.refs_2_.refs_0_) | copy-start | bytes 3145732
  215.5 168.9 %collective-permute-start.4 = (bf16[1024,512]{1,0:T(8,128)(2,1)S(1)}, bf16[1024,512]{1,0:T(8,128)(2,1)}, u32[]{:S(2)}, u32[]{:S(2)}) collective-permute-start(bf16[1024,512]{1,0:T(8,128)(2,1)S(1)} %collective-permute-done.3.refs_2_.refs_0_), channel_id=1, source_target_pairs={{0,8},{8,0},{16,24},{24,16},{1,9},{9,1},{17,25},{25,17},{2,10},{10... | collective-permute-start | bytes 3145736 | tf_op jit(solution)/shard_map/ppermute | solution.py:19
  351.9 1.0 copy-start.7
  352.9 41.9 %collective-permute-start.1 = (bf16[1024,512]{1,0:T(8,128)(2,1)}, bf16[1024,512]{1,0:T(8,128)(2,1)S(1)}, u32[]{:S(2)}, u32[]{:S(2)}) collective-permute-start(bf16[1024,512]{1,0:T(8,128)(2,1)} %bitcast.20), channel_id=1, source_target_pairs={{0,16},{8,24},{16,0},{24,8},{1,17},{9,25},{17,1},{25,9},{2,18},{10... | collective-permute-start | bytes 3145736 | tf_op jit(solution)/shard_map/ppermute | solution.py:19
  353.4 1.2 copy-start.2
  361.1 0.6 copy-start.13
  378.8 34.0 %all-to-all-start.4 = ((bf16[8,128,256]{2,1,0:T(8,128)(2,1)}), bf16[8,128,256]{2,1,0:T(8,128)(2,1)}, u32[]{:S(2)}, u32[]{:S(2)}) async-start(bf16[8,128,256]{2,1,0:T(8,128)(2,1)} %pack_columns.9), calls=%async_computation.4 | async-start | bytes 1048576 | tf_op jit(solution)/shard_map/all_to_all | solution.py:249
  384.5 1.2 copy-start.6
  385.7 1.2 copy-start.10
  386.9 0.7 copy-start.14
  394.1 0.6 copy-start.11
  394.7 1.0 copy-start.3
  412.8 18.0 %all-to-all-start.3 = ((bf16[8,128,256]{2,1,0:T(8,128)(2,1)}), bf16[8,128,256]{2,1,0:T(8,128)(2,1)S(1)}, u32[]{:S(2)}, u32[]{:S(2)}) async-start(bf16[8,128,256]{2,1,0:T(8,128)(2,1)} %pack_columns.8), calls=%async_computation.3 | async-start | bytes 1048576 | tf_op jit(solution)/shard_map/all_to_all | solution.py:249
  418.8 15.5 %collective-permute-start.23 = (bf16[1024,512]{1,0:T(8,128)(2,1)}, bf16[1024,512]{1,0:T(8,128)(2,1)S(1)}, u32[]{:S(2)}, u32[]{:S(2)}) collective-permute-start(bf16[1024,512]{1,0:T(8,128)(2,1)} %bitcast.21), channel_id=1, source_target_pairs={{0,8},{8,0},{16,24},{24,16},{1,9},{9,1},{17,25},{25,17},{2,10},{10... | collective-permute-start | bytes 3145736 | tf_op jit(solution)/shard_map/ppermute | solution.py:19
  418.8 25.9 %collective-permute-start.24 = (bf16[1024,512]{1,0:T(8,128)(2,1)}, bf16[1024,512]{1,0:T(8,128)(2,1)S(1)}, u32[]{:S(2)}, u32[]{:S(2)}) collective-permute-start(bf16[1024,512]{1,0:T(8,128)(2,1)} %copy-done.3), channel_id=1, source_target_pairs={{0,8},{8,0},{16,24},{24,16},{1,9},{9,1},{17,25},{25,17},{2,10},{10... | collective-permute-start | bytes 3145736 | tf_op jit(solution)/shard_map/ppermute | solution.py:19
  419.3 15.0 %collective-permute-start.21 = (bf16[1024,256]{1,0:T(8,128)(2,1)}, bf16[1024,256]{1,0:T(8,128)(2,1)S(1)}, u32[]{:S(2)}, u32[]{:S(2)}) collective-permute-start(bf16[1024,256]{1,0:T(8,128)(2,1)} %bitcast.13.refs_0_), channel_id=1, source_target_pairs={{0,16},{8,24},{16,0},{24,8},{1,17},{9,25},{17,1},{25,9},{2,18},{10... | collective-permute-start | bytes 1572872 | tf_op jit(solution)/shard_map/ppermute | solution.py:19
  430.9 13.8 %collective-permute-start.18 = (bf16[1024,256]{1,0:T(8,128)(2,1)S(1)}, bf16[1024,256]{1,0:T(8,128)(2,1)S(1)}, u32[]{:S(2)}, u32[]{:S(2)}) collective-permute-start(bf16[1024,256]{1,0:T(8,128)(2,1)S(1)} %bitcast.26), channel_id=1, source_target_pairs={{0,16},{8,24},{16,0},{24,8},{1,17},{9,25},{17,1},{25,9},{2,18},{10... | collective-permute-start | bytes 1572872 | tf_op jit(solution)/shard_map/ppermute | solution.py:19
  432.1 22.0 %collective-permute-start.20 = (bf16[1024,256]{1,0:T(8,128)(2,1)}, bf16[1024,256]{1,0:T(8,128)(2,1)S(1)}, u32[]{:S(2)}, u32[]{:S(2)}) collective-permute-start(bf16[1024,256]{1,0:T(8,128)(2,1)} %bitcast.13.refs_0_), channel_id=1, source_target_pairs={{0,8},{8,0},{16,24},{24,16},{1,9},{9,1},{17,25},{25,17},{2,10},{10... | collective-permute-start | bytes 1572872 | tf_op jit(solution)/shard_map/ppermute | solution.py:19
  434.3 19.8 %collective-permute-start.22 = (bf16[1024,256]{1,0:T(8,128)(2,1)S(1)}, bf16[1024,256]{1,0:T(8,128)(2,1)S(1)}, u32[]{:S(2)}, u32[]{:S(2)}) collective-permute-start(bf16[1024,256]{1,0:T(8,128)(2,1)S(1)} %collective-permute-done.21.refs_2_), channel_id=1, source_target_pairs={{0,8},{8,0},{16,24},{24,16},{1,9},{9,1},{17,25},{25,17},{2,10},{10... | collective-permute-start | bytes 1572872 | tf_op jit(solution)/shard_map/ppermute | solution.py:19
  434.3 24.8 %collective-permute-start.17 = (bf16[1024,256]{1,0:T(8,128)(2,1)S(1)}, bf16[1024,256]{1,0:T(8,128)(2,1)S(1)}, u32[]{:S(2)}, u32[]{:S(2)}) collective-permute-start(bf16[1024,256]{1,0:T(8,128)(2,1)S(1)} %bitcast.27), channel_id=1, source_target_pairs={{0,8},{8,0},{16,24},{24,16},{1,9},{9,1},{17,25},{25,17},{2,10},{10... | collective-permute-start | bytes 1572872 | tf_op jit(solution)/shard_map/ppermute | solution.py:19
  444.7 14.5 %collective-permute-start.19 = (bf16[1024,256]{1,0:T(8,128)(2,1)S(1)}, bf16[1024,256]{1,0:T(8,128)(2,1)S(1)}, u32[]{:S(2)}, u32[]{:S(2)}) collective-permute-start(bf16[1024,256]{1,0:T(8,128)(2,1)S(1)} %collective-permute-done.18.refs_2_), channel_id=1, source_target_pairs={{0,8},{8,0},{16,24},{24,16},{1,9},{9,1},{17,25},{25,17},{2,10},{10... | collective-permute-start | bytes 1572872 | tf_op jit(solution)/shard_map/ppermute | solution.py:19
  444.7 1.2 copy-start.4
  445.9 1.2 copy-start.8
  447.2 0.7 copy-start.12
  477.7 5.8 %copy-start = (f32[4,2048,512]{2,1,0:T(8,128)S(1)}, f32[4,2048,512]{2,1,0:T(8,128)}, u32[]{:S(2)}) copy-start(f32[4,2048,512]{2,1,0:T(8,128)} %get-tuple-element.24.gradient_ref) | copy-start | bytes 50331652

commit v3 on v0

v3 whole, which is shorter than its diff:
```python
import functools
import math

import jax
import jax.numpy as jnp
from jax import lax
from jax.experimental import pallas as pl
from jax.experimental.pallas import tpu as pltpu
from jax.sharding import PartitionSpec as P

epsilon = 1e-06
lanes = 128
ANY = pl.BlockSpec(memory_space=pl.ANY)
SMEM = pl.BlockSpec(memory_space=pltpu.SMEM)
VMEM = pl.BlockSpec(memory_space=pltpu.VMEM)
HBM = pl.BlockSpec(memory_space=pltpu.HBM)


def exchange(block, axis, distance):
    size = lax.axis_size(axis)
    return lax.ppermute(block, axis, [(i, i ^ distance) for i in range(size)])


def doubling(block, axis):
    size = lax.axis_size(axis)
    slots = {0: block}
    distance = size // 2
    while distance:
        for slot in list(slots):
            slots[slot ^ distance] = exchange(slots[slot], axis, distance)
        distance //= 2
    return [slots[slot] for slot in range(size)]


def pack_kernel(distances, tok_ref, hidden_ref, *refs):
    out_refs, sems = refs[-1 - len(distances) : -1], refs[-1]
    width = out_refs[0].shape[1]
    copies = []
    for at, distance in enumerate(distances):
        start = pl.multiple_of((tok_ref[0] ^ distance) * width, lanes)
        copies.append(
            pltpu.make_async_copy(
                hidden_ref.at[0, :, pl.ds(start, width)], out_refs[at], sems.at[at]
            )
        )
    for copy in copies:
        copy.start()
    for copy in copies:
        copy.wait()


def pack(tok, hidden, distances, width, after):
    rows = hidden.shape[1]
    count = len(distances)
    return pl.pallas_call(
        functools.partial(pack_kernel, distances),
        out_shape=[jax.ShapeDtypeStruct((rows, width), hidden.dtype)] * count,
        in_specs=[SMEM, HBM] + [ANY] * len(after),
        out_specs=[VMEM] * count,
        scratch_shapes=[pltpu.SemaphoreType.DMA((count,))],
        compiler_params=pltpu.CompilerParams(vmem_limit_bytes=2**20),
        cost_estimate=pl.CostEstimate(
            flops=0, bytes_accessed=4 * count * rows * width, transcendentals=0
        ),
        name="pack_columns",
    )(tok, hidden, *after)


def mask_kernel(valid_ref, user_ref, cot_ref, *out_refs):
    rows, width = out_refs[0].shape
    keep = lax.broadcasted_iota(jnp.int32, (rows, width), 0) < valid_ref[0]
    for slot, out_ref in enumerate(out_refs):
        column = pl.multiple_of((user_ref[0] ^ slot) * width, lanes)
        block = cot_ref[0, :, pl.ds(column, width)]
        out_ref[...] = jnp.where(keep, block, jnp.zeros_like(block))


def mask(valid, user, cotangent, user_count):
    _, rows, total = cotangent.shape
    return pl.pallas_call(
        mask_kernel,
        out_shape=[jax.ShapeDtypeStruct((rows, total // user_count), cotangent.dtype)] * user_count,
        in_specs=[SMEM, SMEM, VMEM],
        out_specs=[VMEM] * user_count,
        compiler_params=pltpu.CompilerParams(vmem_limit_bytes=2 * 2**20),
        name="mask_cotangent",
    )(valid, user, cotangent)


def product_kernel(user_count, sources, first, last, *refs):
    lefts = [refs[i * user_count : (i + 1) * user_count] for i in range(sources)]
    rights = refs[sources * user_count : sources * (user_count + 1)]
    held_ref = None if first else refs[sources * (user_count + 1)]
    product_ref = refs[sources * (user_count + 1) + (0 if first else 1)]
    width = product_ref.shape[1]
    tile = min(width, 2 * lanes)
    squares = []
    for slot in range(user_count):
        right = jnp.concatenate([right_ref[slot] for right_ref in rights], axis=0)

        def step(i, total, slot=slot, right=right):
            at = pl.ds(pl.multiple_of(i * tile, tile), tile)
            left = jnp.concatenate([source[slot][:, at] for source in lefts], axis=0)
            value = lax.dot_general(
                left, right, (((0,), (0,)), ((), ())), preferred_element_type=jnp.float32
            )
            if not first:
                value += held_ref[slot, at, :]
            product_ref[slot, at, :] = value
            if last:
                row = jnp.sum(value * value, axis=0, keepdims=True)
                for start in range(0, row.shape[1], lanes):
                    total += row[:, start : start + lanes]
            return total

        squares.append(lax.fori_loop(0, width // tile, step, jnp.zeros((1, lanes), jnp.float32)))
    if last:
        sums_ref = refs[-1]
        rows = jnp.concatenate(squares + [jnp.zeros((8 - user_count, lanes), jnp.float32)], axis=0)
        sums_ref[...] = jnp.broadcast_to(rows[None], sums_ref.shape)


def product(lefts, rights, held, copies):
    sources = len(rights)
    user_count, tokens, columns = rights[0].shape
    width = lefts[0][0].shape[1]
    first, last = held is None, copies > 0
    operands = [left for source in lefts for left in source] + list(rights)
    aliases = {}
    if not first:
        aliases = {len(operands): 0}
        operands.append(held)
    out_shape = [jax.ShapeDtypeStruct((user_count, width, columns), jnp.float32)]
    if last:
        out_shape.append(jax.ShapeDtypeStruct((copies, 8, lanes), jnp.float32))
    return pl.pallas_call(
        functools.partial(product_kernel, user_count, sources, first, last),
        out_shape=out_shape,
        in_specs=[VMEM] * len(operands),
        out_specs=[VMEM] * len(out_shape),
        input_output_aliases=aliases,
        compiler_params=pltpu.CompilerParams(vmem_limit_bytes=8 * 2**20),
        cost_estimate=pl.CostEstimate(
            flops=2 * user_count * sources * tokens * columns * width,
            bytes_accessed=2 * user_count * sources * tokens * (width + columns),
            transcendentals=0,
        ),
        name="product_and_squares",
    )(*operands)


def combine_kernel(user_count, clip_bound, scaling, user_ref, sums_ref, gradient_ref, out_ref):
    per_user = sums_ref.shape[0] // user_count
    by_source = [
        jnp.sum(sums_ref[j * per_user : (j + 1) * per_user], axis=0) for j in range(user_count)
    ]
    factors = []
    for u in range(user_count):
        row = sum(by_source[j][j ^ u : (j ^ u) + 1, :] for j in range(user_count))
        norm_sq = jnp.sum(row, axis=1, keepdims=True)
        factors.append(jnp.minimum(1.0, clip_bound / jnp.sqrt(norm_sq + epsilon)) * scaling)
    tile = out_ref.shape[0]
    at = pl.ds(pl.multiple_of(pl.program_id(0) * tile, tile), tile)
    result = None
    for slot in range(user_count):
        user = user_ref[0] ^ slot
        factor = sum(jnp.where(user == u, factors[u], 0.0) for u in range(user_count))
        term = factor * gradient_ref[slot, at, :]
        result = term if result is None else result + term
    out_ref[...] = result


def combine(user, sums, gradients, clip_bound, scaling):
    user_count, rows, columns = gradients.shape
    tile = min(rows, 256)
    return pl.pallas_call(
        functools.partial(combine_kernel, user_count, clip_bound, scaling),
        grid=(rows // tile,),
        out_shape=jax.ShapeDtypeStruct((rows, columns), jnp.float32),
        in_specs=[SMEM, VMEM, VMEM],
        out_specs=pl.BlockSpec((tile, columns), lambda i: (i, 0)),
        compiler_params=pltpu.CompilerParams(vmem_limit_bytes=8 * 2**20),
        name="weighted_sum",
    )(user, sums, gradients)


def body(hidden, cotangent, lengths):
    tok_count = lax.axis_size("tok")
    user_count = lax.axis_size("user")
    tok_rows = hidden.shape[1]
    hidden_width = hidden.shape[2]
    model_width = cotangent.shape[2]
    capacity = tok_rows * tok_count
    own_width = hidden_width // tok_count
    clip_bound = math.sqrt(8.0 * hidden_width * model_width * capacity)
    scaling = math.sqrt(hidden_width * model_width) / (user_count * clip_bound)
    user = lax.axis_index("user").astype(jnp.int32).reshape(1)
    tok = lax.axis_index("tok").astype(jnp.int32).reshape(1)
    valid = lengths - tok * tok_rows
    half = tok_count // 2

    masked = mask(valid, user, cotangent, user_count)
    by_slot = [masked[0]] + [exchange(masked[s], "user", s) for s in range(1, user_count)]
    rights = doubling(jnp.stack(by_slot), "tok")

    early = list(range(half + 1))
    outgoing = dict(zip(early, pack(tok, hidden, early, own_width, [masked[0]])))
    arrived = {0: outgoing[0]}
    for d in range(1, tok_count):
        if d not in outgoing:
            after = rights[half] if d == half + 1 else arrived[d - 2]
            outgoing[d] = pack(tok, hidden, [d], own_width, [after])[0]
        arrived[d] = exchange(outgoing[d], "tok", d)

    held = None
    for d in range(0, tok_count, 2):
        last = d == tok_count - 2
        pair = [doubling(arrived[d], "user"), doubling(arrived[d + 1], "user")]
        outs = product(pair, rights[d : d + 2], held, tok_count * user_count if last else 0)
        held = outs[0]
    sums = lax.all_to_all(outs[1], ("user", "tok"), split_axis=0, concat_axis=0, tiled=True)
    return combine(user, sums, held, clip_bound, scaling)


def solution(mesh):
    return jax.shard_map(
        body,
        mesh=mesh,
        in_specs=(P("user", "tok", None), P("user", "tok", None), P("user")),
        out_specs=P("tok", "user"),
        check_vma=False,
    )
```

time: 356 us -> 227 us (0.64)
  waiting for transfers between devices: 266 us -> 130 us
  Pallas kernels: 0 us -> 39.7 us
  starting transfers between devices: 7.49 us -> 37.9 us
  matrix products: 16.9 us -> 0 us
  between operations: 14.8 us -> 0.87 us
  other arithmetic: 12.6 us -> 0.07 us
  local copies, waits for them, and re-layouts: 18.1 us -> 7.6 us
  blocking collectives: 19.8 us -> 11.4 us
    all_to_all x1 -> x0, waiting for transfers between devices: 142 us -> none  [body(): lax.all_to_all(hidden[0], 'tok', split_axis=1, concat_axis=0, tiled=True)]
    ppermute x0 -> x41, waiting for transfers between devices: none -> 130 us  [exchange(): return lax.ppermute(block, axis, [(i, i ^ distance) for i in range(size)])]
    reduce_scatter x1 -> x0, waiting for transfers between devices: 124 us -> none  [body(): lax.psum_scatter(gradient * factor, 'user', scatter_dimension=1, tiled=True)]
    pallas_call x0 -> x10, Pallas kernels: none -> 39.7 us  [the longest x4 34.1 us: product(): pl.pallas_call(functools.partial(product_kernel, user_count, sources, fir...]
    ppermute x0 -> x41, starting transfers between devices: none -> 37.9 us  [exchange(): return lax.ppermute(block, axis, [(i, i ^ distance) for i in range(size)])]
    psum x1 -> x0, blocking collectives: 19.8 us -> none  [body(): norm_sq = lax.psum(partial_value, 'tok')]
    dot_general x1 -> x0, matrix products: 16.9 us -> none  [contract(): lax.dot_general(left, right, (((0,), (0,)), ((), ())), preferred_element_...]
    mul x1 -> x0, other arithmetic: 11.7 us -> none  [body(): gradient * factor]
  transfers between devices with their start and end apart: 3 -> 41, of which waited for: 2 -> 16; matrix products, arithmetic and copies ran while one was open for 2% -> 0% of each run, Pallas kernels for 0% -> 11%
where the time goes in v3:
time: 227 us
  waiting for transfers between devices  130 us (57%)
  Pallas kernels  39.7 us (17%)
  starting transfers between devices  37.9 us (17%)
  blocking collectives  11.4 us (5%)
  local copies, waits for them, and re-layouts  7.6 us (3%)
    ppermute x41, waiting for transfers between devices, exchange(): return lax.ppermute(block, axis, [(i, i ^ distance) for i in range(size)])  130 us
    ppermute x41, starting transfers between devices, exchange(): return lax.ppermute(block, axis, [(i, i ^ distance) for i in range(size)])  37.9 us
    pallas_call x4, Pallas kernels, product(): pl.pallas_call(functools.partial(product_kernel, user_count, sources, fir...  34.1 us
    all_to_all x1, blocking collectives, body(): lax.all_to_all(outs[1], ('user', 'tok'), split_axis=0, concat_axis=0, til...  11.4 us
    unnamed x10, local copies, waits for them, and re-layouts  7.6 us
    pallas_call x1, Pallas kernels, combine(): pl.pallas_call(functools.partial(combine_kernel, user_count, clip_bound,...  5.13 us
  transfers between devices with their start and end apart: 41, of which 16 were waited for; matrix products, arithmetic and copies ran while one was open for 0% of the time, Pallas kernels for 11%

profile of v3, /device:TPU:0, one launch (start us, length us, event | category | flops | bytes accessed | tf_op | source)
XLA Modules:
  0.0 227.1 jit_solution(9678601029252827100)
XLA Ops:
  0.7 1.0 copy-done.4
  1.7 0.0 copy-start
  1.8 2.2 copy-done
  3.9 0.2 pack_columns.4
  4.2 3.0 %collective-permute-start.36 = (bf16[128,2048]{1,0:T(8,128)(2,1)S(1)}, bf16[128,2048]{1,0:T(8,128)(2,1)S(1)}, u32[]{:S(2)}, u32[]{:S(2)}) collective-permute-start(bf16[128,2048]{1,0:T(8,128)(2,1)S(1)} %get-tuple-element.24), channel_id=1, source_target_pairs={{0,1},{1,0},{2,3},{3,2},{4,5},{5,4},{6,7},{7,6},{8,9},{9,8},{10,11... | collective-permute-start | bytes 1572872 | tf_op jit(solution)/shard_map/ppermute | solution.py:21
  7.2 1.5 collective-permute-start.34
  8.7 0.5 collective-permute-start.5
  9.2 0.5 collective-permute-start.6
  9.7 1.1 collective-permute-done.5
  10.8 0.3 collective-permute-start.7
  11.1 13.7 %collective-permute-done.6 = bf16[128,512]{1,0:T(8,128)(2,1)S(1)} collective-permute-done((bf16[128,512]{1,0:T(8,128)(2,1)S(1)}, bf16[128,512]{1,0:T(8,128)(2,1)S(1)}, u32[]{:S(2)}, u32[]{:S(2)}) %collective-permute-start.6) | collective-permute-done | bytes 131104 | tf_op jit(solution)/shard_map/ppermute | solution.py:21
  24.8 1.6 collective-permute-start.23
  26.4 0.0 collective-permute-done.7
  26.4 0.4 collective-permute-start.27
  26.7 0.1 pad_maximum_fusion.refs_8_
  26.8 0.0 collective-permute-done.36.refs_4_
  26.8 2.7 %collective-permute-start = (bf16[128,2048]{1,0:T(8,128)(2,1)S(1)}, bf16[128,2048]{1,0:T(8,128)(2,1)S(1)}, u32[]{:S(2)}, u32[]{:S(2)}) collective-permute-start(bf16[128,2048]{1,0:T(8,128)(2,1)S(1)} %get-tuple-element.17), channel_id=1, source_target_pairs={{0,4},{1,5},{2,6},{3,7},{4,0},{5,1},{6,2},{7,3},{8,12},{9,13},{10,... | collective-permute-start | bytes 1572872 | tf_op jit(solution)/shard_map/ppermute | solution.py:21
  29.5 1.5 collective-permute-start.40
  31.0 0.0 collective-permute-done.33.refs_1_
  31.0 0.3 collective-permute-start.8
  31.4 26.6 %collective-permute-done.23.refs_0_ = bf16[128,2048]{1,0:T(8,128)(2,1)S(1)} collective-permute-done((bf16[128,2048]{1,0:T(8,128)(2,1)S(1)}, bf16[128,2048]{1,0:T(8,128)(2,1)S(1)}, u32[]{:S(2)}, u32[]{:S(2)}) %collective-permute-start.23) | collective-permute-done | bytes 524320 | tf_op jit(solution)/shard_map/ppermute | solution.py:21
  58.0 9.8 %collective-permute-done.27.refs_4_ = bf16[128,2048]{1,0:T(8,128)(2,1)S(1)} collective-permute-done((bf16[128,2048]{1,0:T(8,128)(2,1)S(1)}, bf16[128,2048]{1,0:T(8,128)(2,1)S(1)}, u32[]{:S(2)}, u32[]{:S(2)}) %collective-permute-start.27) | collective-permute-done | bytes 524320 | tf_op jit(solution)/shard_map/ppermute | solution.py:21
  67.8 2.1 collective-permute-start.38
  69.8 0.0 collective-permute-done.refs_0_
  69.9 0.0 collective-permute-start.35
  69.9 0.5 collective-permute-start.37
  70.4 5.6 %collective-permute-done.8.refs_0_.refs_8_ = bf16[4,128,512]{2,1,0:T(8,128)(2,1)S(1)} collective-permute-done((bf16[4,128,512]{2,1,0:T(8,128)(2,1)S(1)}, bf16[4,128,512]{2,1,0:T(8,128)(2,1)S(1)}, u32[]{:S(2)}, u32[]{:S(2)}) %collective-permute-start.8) | collective-permute-done | bytes 524320 | tf_op jit(solution)/shard_map/ppermute | solution.py:21
  76.0 1.5 collective-permute-start.25
  77.5 2.2 copy-done.1
  79.7 1.1 collective-permute-done.31.refs_8_
  80.8 1.5 collective-permute-start.29
  82.3 0.0 collective-permute-done.38.refs_6_
  82.3 0.5 collective-permute-start.28
  82.8 0.5 collective-permute-start.17
  83.4 7.5 %collective-permute-done.25.refs_2_ = bf16[128,2048]{1,0:T(8,128)(2,1)S(1)} collective-permute-done((bf16[128,2048]{1,0:T(8,128)(2,1)S(1)}, bf16[128,2048]{1,0:T(8,128)(2,1)S(1)}, u32[]{:S(2)}, u32[]{:S(2)}) %collective-permute-start.25) | collective-permute-done | bytes 524320 | tf_op jit(solution)/shard_map/ppermute | solution.py:21
  90.8 0.4 collective-permute-start.9
  91.3 2.2 copy-done.2
  93.5 8.6 %collective-permute-done.29.refs_6_ = bf16[128,2048]{1,0:T(8,128)(2,1)S(1)} collective-permute-done((bf16[128,2048]{1,0:T(8,128)(2,1)S(1)}, bf16[128,2048]{1,0:T(8,128)(2,1)S(1)}, u32[]{:S(2)}, u32[]{:S(2)}) %collective-permute-start.29) | collective-permute-done | bytes 524320 | tf_op jit(solution)/shard_map/ppermute | solution.py:21
  102.1 3.3 %collective-permute-start.1 = (bf16[128,2048]{1,0:T(8,128)(2,1)S(1)}, bf16[128,2048]{1,0:T(8,128)(2,1)S(1)}, u32[]{:S(2)}, u32[]{:S(2)}) collective-permute-start(bf16[128,2048]{1,0:T(8,128)(2,1)S(1)} %pack_columns.5), channel_id=1, source_target_pairs={{0,6},{1,7},{2,4},{3,5},{4,2},{5,3},{6,0},{7,1},{8,14},{9,15},{10,... | collective-permute-start | bytes 1572872 | tf_op jit(solution)/shard_map/ppermute | solution.py:21
  105.3 5.5 %collective-permute-start.32 = (bf16[4,128,512]{2,1,0:T(8,128)(2,1)S(1)}, bf16[4,128,512]{2,1,0:T(8,128)(2,1)S(1)}, u32[]{:S(2)}, u32[]{:S(2)}) collective-permute-start(bf16[4,128,512]{2,1,0:T(8,128)(2,1)S(1)} %collective-permute-done.31.refs_8_), channel_id=1, source_target_pairs={{0,1},{1,0},{2,3},{3,2},{4,5},{5,4},{6,7},{7,6},{8,9},{9,8},{10,11... | collective-permute-start | bytes 1572872 | tf_op jit(solution)/shard_map/ppermute | solution.py:21
  110.8 1.1 collective-permute-done.17.refs_2_
  111.9 2.8 %collective-permute-start.22 = (bf16[4,128,512]{2,1,0:T(8,128)(2,1)S(1)}, bf16[4,128,512]{2,1,0:T(8,128)(2,1)S(1)}, u32[]{:S(2)}, u32[]{:S(2)}) collective-permute-start(bf16[4,128,512]{2,1,0:T(8,128)(2,1)S(1)} %collective-permute-done.8.refs_0_.refs_8_), channel_id=1, source_target_pairs={{0,1},{1,0},{2,3},{3,2},{4,5},{5,4},{6,7},{7,6},{8,9},{9,8},{10,11... | collective-permute-start | bytes 1572872 | tf_op jit(solution)/shard_map/ppermute | solution.py:21
  114.8 11.7 %collective-permute-done.9.refs_0_.refs_4_ = bf16[128,2048]{1,0:T(8,128)(2,1)S(1)} collective-permute-done((bf16[128,2048]{1,0:T(8,128)(2,1)S(1)}, bf16[128,2048]{1,0:T(8,128)(2,1)S(1)}, u32[]{:S(2)}, u32[]{:S(2)}) %collective-permute-start.9) | collective-permute-done | bytes 524320 | tf_op jit(solution)/shard_map/ppermute | solution.py:21
  126.5 0.1 collective-permute-start.39
  126.6 0.5 collective-permute-start.26
  127.1 3.0 %collective-permute-done.32.refs_9_ = bf16[4,128,512]{2,1,0:T(8,128)(2,1)S(1)} collective-permute-done((bf16[4,128,512]{2,1,0:T(8,128)(2,1)S(1)}, bf16[4,128,512]{2,1,0:T(8,128)(2,1)S(1)}, u32[]{:S(2)}, u32[]{:S(2)}) %collective-permute-start.32) | collective-permute-done | bytes 524320 | tf_op jit(solution)/shard_map/ppermute | solution.py:21
  130.1 10.5 %collective-permute-done.22.refs_9_ = bf16[4,128,512]{2,1,0:T(8,128)(2,1)S(1)} collective-permute-done((bf16[4,128,512]{2,1,0:T(8,128)(2,1)S(1)}, bf16[4,128,512]{2,1,0:T(8,128)(2,1)S(1)}, u32[]{:S(2)}, u32[]{:S(2)}) %collective-permute-start.22) | collective-permute-done | bytes 524320 | tf_op jit(solution)/shard_map/ppermute | solution.py:21
  140.6 1.5 collective-permute-start.20
  142.1 0.6 collective-permute-start.10
  142.7 0.6 collective-permute-start.3
  143.3 0.2 collective-permute-start.19
  143.5 12.0 %collective-permute-done.20.refs_6_ = bf16[128,2048]{1,0:T(8,128)(2,1)S(1)} collective-permute-done((bf16[128,2048]{1,0:T(8,128)(2,1)S(1)}, bf16[128,2048]{1,0:T(8,128)(2,1)S(1)}, u32[]{:S(2)}, u32[]{:S(2)}) %collective-permute-start.20) | collective-permute-done | bytes 524320 | tf_op jit(solution)/shard_map/ppermute | solution.py:21
  155.5 2.4 %collective-permute-done.10.refs_4_ = bf16[128,2048]{1,0:T(8,128)(2,1)S(1)} collective-permute-done((bf16[128,2048]{1,0:T(8,128)(2,1)S(1)}, bf16[128,2048]{1,0:T(8,128)(2,1)S(1)}, u32[]{:S(2)}, u32[]{:S(2)}) %collective-permute-start.10) | collective-permute-done | bytes 524320 | tf_op jit(solution)/shard_map/ppermute | solution.py:21
  157.9 0.5 collective-permute-start.12
  158.4 8.3 %collective-permute-done.3.refs_2_ = bf16[128,2048]{1,0:T(8,128)(2,1)S(1)} collective-permute-done((bf16[128,2048]{1,0:T(8,128)(2,1)S(1)}, bf16[128,2048]{1,0:T(8,128)(2,1)S(1)}, u32[]{:S(2)}, u32[]{:S(2)}) %collective-permute-start.3) | collective-permute-done | bytes 524320 | tf_op jit(solution)/shard_map/ppermute | solution.py:21
  166.7 2.5 %collective-permute-start.15 = (bf16[4,128,512]{2,1,0:T(8,128)(2,1)S(1)}, bf16[4,128,512]{2,1,0:T(8,128)(2,1)S(1)}, u32[]{:S(2)}, u32[]{:S(2)}) collective-permute-start(bf16[4,128,512]{2,1,0:T(8,128)(2,1)S(1)} %collective-permute-done.14.refs_8_), channel_id=1, source_target_pairs={{0,1},{1,0},{2,3},{3,2},{4,5},{5,4},{6,7},{7,6},{8,9},{9,8},{10,11... | collective-permute-start | bytes 1572872 | tf_op jit(solution)/shard_map/ppermute | solution.py:21
  169.2 0.5 collective-permute-start.11
  169.7 6.6 %collective-permute-done.12.refs_6_ = bf16[128,2048]{1,0:T(8,128)(2,1)S(1)} collective-permute-done((bf16[128,2048]{1,0:T(8,128)(2,1)S(1)}, bf16[128,2048]{1,0:T(8,128)(2,1)S(1)}, u32[]{:S(2)}, u32[]{:S(2)}) %collective-permute-start.12) | collective-permute-done | bytes 524320 | tf_op jit(solution)/shard_map/ppermute | solution.py:21
  176.3 8.3 %product_and_squares.4.refs_10_ = f32[4,2048,512]{2,1,0:T(8,128)S(1)} custom-call(bf16[128,2048]{1,0:T(8,128)(2,1)S(1)} %get-tuple-element.23.refs_0_, bf16[128,2048]{1,0:T(8,128)(2,1)S(1)} %collective-permute-done.33.refs_1_, bf16[128,2048]{1,0:T(8,128)(2,1)S(1)} %collective-permute-done.34.refs_2_, bf16[128,2048]{1,0:T(8,128)(2,1)S(1)} %collective-permute-done.35.refs_3_, ...), custom_call_target="tpu_custom_call" | custom-call | flops 2147483648 | bytes 5242880 | tf_op jit(solution)/shard_map/product_and_squares/pallas_call | solution.py:136
  184.7 8.4 %product_and_squares.5.refs_10_ = f32[4,2048,512]{2,1,0:T(8,128)S(1)} custom-call(bf16[128,2048]{1,0:T(8,128)(2,1)S(1)} %collective-permute-done.23.refs_0_, bf16[128,2048]{1,0:T(8,128)(2,1)S(1)} %collective-permute-done.24.refs_1_, bf16[128,2048]{1,0:T(8,128)(2,1)S(1)} %collective-permute-done.25.refs_2_, ...), custom_call_target="tpu_custom_call", output_to_operand_aliasing={{}: (10, {})} | custom-call | flops 2147483648 | bytes 5242880 | tf_op jit(solution)/shard_map/product_and_squares/pallas_call | solution.py:136
  193.1 8.5 %product_and_squares.6.refs_10_ = f32[4,2048,512]{2,1,0:T(8,128)S(1)} custom-call(bf16[128,2048]{1,0:T(8,128)(2,1)S(1)} %collective-permute-done.refs_0_, bf16[128,2048]{1,0:T(8,128)(2,1)S(1)} %collective-permute-done.16.refs_1_, bf16[128,2048]{1,0:T(8,128)(2,1)S(1)} %collective-permute-done.17.refs_2_, ...), custom_call_target="tpu_custom_call", output_to_operand_aliasing={{}: (10, {})} | custom-call | flops 2147483648 | bytes 5242880 | tf_op jit(solution)/shard_map/product_and_squares/pallas_call | solution.py:136
  201.7 8.9 %product_and_squares.7 = (f32[4,2048,512]{2,1,0:T(8,128)S(1)}, f32[32,8,128]{2,1,0:T(8,128)S(1)}) custom-call(bf16[128,2048]{1,0:T(8,128)(2,1)S(1)} %collective-permute-done.1.refs_0_, bf16[128,2048]{1,0:T(8,128)(2,1)S(1)} %collective-permute-done.2.refs_1_, bf16[128,2048]{1,0:T(8,128)(2,1)S(1)} %collective-permute-done.3.refs_2_, ...), custom_call_target="tpu_custom_call", output_to_operand_aliasing={{0}: (10, {})} | custom-call | flops 2147483648 | bytes 5242880 | tf_op jit(solution)/shard_map/product_and_squares/pallas_call | solution.py:136
  210.6 11.4 %all_to_all.5.sums_ref = f32[32,8,128]{2,1,0:T(8,128)S(1)} all-to-all(f32[32,8,128]{2,1,0:T(8,128)S(1)} %get-tuple-element.25), channel_id=1, replica_groups=mesh['user'=4,'tok'=8] {'user','tok'}, dimensions={0} | all-to-all | bytes 262144 | tf_op jit(solution)/shard_map/all_to_all | solution.py:221
  222.0 5.1 %weighted_sum.1 = f32[2048,512]{1,0:T(8,128)} custom-call(s32[1]{0:T(128)} %bitcast.user_ref, f32[32,8,128]{2,1,0:T(8,128)S(1)} %all_to_all.5.sums_ref, f32[4,2048,512]{2,1,0:T(8,128)S(1)} %get-tuple-element.26.gradient_ref), custom_call_target="tpu_custom_call" | custom-call | tf_op jit(solution)/shard_map/weighted_sum/pallas_call | solution.py:176
  (40 shorter events, 0.3 us)
Async XLA Ops:
  0.7 1.0 copy-start.4
  1.7 2.2 copy-start
  3.9 122.5 %copy-start.3 = (bf16[1,128,16384]{2,1,0:T(8,128)(2,1)S(1)}, bf16[1,128,16384]{2,1,0:T(8,128)(2,1)}, u32[]{:S(2)}) copy-start(bf16[1,128,16384]{2,1,0:T(8,128)(2,1)} %hidden_ref.7) | copy-start | bytes 12582916
  4.2 22.6 %collective-permute-start.36 = (bf16[128,2048]{1,0:T(8,128)(2,1)S(1)}, bf16[128,2048]{1,0:T(8,128)(2,1)S(1)}, u32[]{:S(2)}, u32[]{:S(2)}) collective-permute-start(bf16[128,2048]{1,0:T(8,128)(2,1)S(1)} %get-tuple-element.24), channel_id=1, source_target_pairs={{0,1},{1,0},{2,3},{3,2},{4,5},{5,4},{6,7},{7,6},{8,9},{9,8},{10,11... | collective-permute-start | bytes 1572872 | tf_op jit(solution)/shard_map/ppermute | solution.py:21
  7.2 22.3 %collective-permute-start.34 = (bf16[128,2048]{1,0:T(8,128)(2,1)S(1)}, bf16[128,2048]{1,0:T(8,128)(2,1)S(1)}, u32[]{:S(2)}, u32[]{:S(2)}) collective-permute-start(bf16[128,2048]{1,0:T(8,128)(2,1)S(1)} %get-tuple-element.23.refs_0_), channel_id=1, source_target_pairs={{0,16},{8,24},{16,0},{24,8},{1,17},{9,25},{17,1},{25,9},{2,18},{10... | collective-permute-start | bytes 1572872 | tf_op jit(solution)/shard_map/ppermute | solution.py:21
  8.7 22.3 %collective-permute-start.33 = (bf16[128,2048]{1,0:T(8,128)(2,1)S(1)}, bf16[128,2048]{1,0:T(8,128)(2,1)S(1)}, u32[]{:S(2)}, u32[]{:S(2)}) collective-permute-start(bf16[128,2048]{1,0:T(8,128)(2,1)S(1)} %get-tuple-element.23.refs_0_), channel_id=1, source_target_pairs={{0,8},{8,0},{16,24},{24,16},{1,9},{9,1},{17,25},{25,17},{2,10},{10... | collective-permute-start | bytes 1572872 | tf_op jit(solution)/shard_map/ppermute | solution.py:21
  8.7 2.1 collective-permute-start.5
  9.2 15.6 %collective-permute-start.6 = (bf16[128,512]{1,0:T(8,128)(2,1)S(1)}, bf16[128,512]{1,0:T(8,128)(2,1)S(1)}, u32[]{:S(2)}, u32[]{:S(2)}) collective-permute-start(bf16[128,512]{1,0:T(8,128)(2,1)S(1)} %get-tuple-element.19), channel_id=1, source_target_pairs={{0,16},{8,24},{16,0},{24,8},{1,17},{9,25},{17,1},{25,9},{2,18},{10... | collective-permute-start | bytes 393224 | tf_op jit(solution)/shard_map/ppermute | solution.py:21
  10.8 15.6 %collective-permute-start.7 = (bf16[128,512]{1,0:T(8,128)(2,1)S(1)}, bf16[128,512]{1,0:T(8,128)(2,1)S(1)}, u32[]{:S(2)}, u32[]{:S(2)}) collective-permute-start(bf16[128,512]{1,0:T(8,128)(2,1)S(1)} %get-tuple-element.20), channel_id=1, source_target_pairs={{0,24},{8,16},{16,8},{24,0},{1,25},{9,17},{17,9},{25,1},{2,26},{10... | collective-permute-start | bytes 393224 | tf_op jit(solution)/shard_map/ppermute | solution.py:21
  24.8 33.2 %collective-permute-start.23 = (bf16[128,2048]{1,0:T(8,128)(2,1)S(1)}, bf16[128,2048]{1,0:T(8,128)(2,1)S(1)}, u32[]{:S(2)}, u32[]{:S(2)}) collective-permute-start(bf16[128,2048]{1,0:T(8,128)(2,1)S(1)} %get-tuple-element.21), channel_id=1, source_target_pairs={{0,2},{1,3},{2,0},{3,1},{4,6},{5,7},{6,4},{7,5},{8,10},{9,11},{10,... | collective-permute-start | bytes 1572872 | tf_op jit(solution)/shard_map/ppermute | solution.py:21
  26.4 41.4 %collective-permute-start.27 = (bf16[128,2048]{1,0:T(8,128)(2,1)S(1)}, bf16[128,2048]{1,0:T(8,128)(2,1)S(1)}, u32[]{:S(2)}, u32[]{:S(2)}) collective-permute-start(bf16[128,2048]{1,0:T(8,128)(2,1)S(1)} %get-tuple-element.22), channel_id=1, source_target_pairs={{0,3},{1,2},{2,1},{3,0},{4,7},{5,6},{6,5},{7,4},{8,11},{9,10},{10,... | collective-permute-start | bytes 1572872 | tf_op jit(solution)/shard_map/ppermute | solution.py:21
  26.8 43.0 %collective-permute-start = (bf16[128,2048]{1,0:T(8,128)(2,1)S(1)}, bf16[128,2048]{1,0:T(8,128)(2,1)S(1)}, u32[]{:S(2)}, u32[]{:S(2)}) collective-permute-start(bf16[128,2048]{1,0:T(8,128)(2,1)S(1)} %get-tuple-element.17), channel_id=1, source_target_pairs={{0,4},{1,5},{2,6},{3,7},{4,0},{5,1},{6,2},{7,3},{8,12},{9,13},{10,... | collective-permute-start | bytes 1572872 | tf_op jit(solution)/shard_map/ppermute | solution.py:21
  29.5 40.3 %collective-permute-start.40 = (bf16[4,128,512]{2,1,0:T(8,128)(2,1)S(1)}, bf16[4,128,512]{2,1,0:T(8,128)(2,1)S(1)}, u32[]{:S(2)}, u32[]{:S(2)}) collective-permute-start(bf16[4,128,512]{2,1,0:T(8,128)(2,1)S(1)} %pad_maximum_fusion.refs_8_), channel_id=1, source_target_pairs={{0,1},{1,0},{2,3},{3,2},{4,5},{5,4},{6,7},{7,6},{8,9},{9,8},{10,11... | collective-permute-start | bytes 1572872 | tf_op jit(solution)/shard_map/ppermute | solution.py:21
  31.0 45.0 %collective-permute-start.8 = (bf16[4,128,512]{2,1,0:T(8,128)(2,1)S(1)}, bf16[4,128,512]{2,1,0:T(8,128)(2,1)S(1)}, u32[]{:S(2)}, u32[]{:S(2)}) collective-permute-start(bf16[4,128,512]{2,1,0:T(8,128)(2,1)S(1)} %pad_maximum_fusion.refs_8_), channel_id=1, source_target_pairs={{0,4},{1,5},{2,6},{3,7},{4,0},{5,1},{6,2},{7,3},{8,12},{9,13},{10,... | collective-permute-start | bytes 1572872 | tf_op jit(solution)/shard_map/ppermute | solution.py:21
  58.0 22.8 %collective-permute-start.31 = (bf16[4,128,512]{2,1,0:T(8,128)(2,1)S(1)}, bf16[4,128,512]{2,1,0:T(8,128)(2,1)S(1)}, u32[]{:S(2)}, u32[]{:S(2)}) collective-permute-start(bf16[4,128,512]{2,1,0:T(8,128)(2,1)S(1)} %pad_maximum_fusion.refs_8_), channel_id=1, source_target_pairs={{0,2},{1,3},{2,0},{3,1},{4,6},{5,7},{6,4},{7,5},{8,10},{9,11},{10,... | collective-permute-start | bytes 1572872 | tf_op jit(solution)/shard_map/ppermute | solution.py:21
  67.8 14.6 %collective-permute-start.38 = (bf16[128,2048]{1,0:T(8,128)(2,1)S(1)}, bf16[128,2048]{1,0:T(8,128)(2,1)S(1)}, u32[]{:S(2)}, u32[]{:S(2)}) collective-permute-start(bf16[128,2048]{1,0:T(8,128)(2,1)S(1)} %collective-permute-done.36.refs_4_), channel_id=1, source_target_pairs={{0,16},{8,24},{16,0},{24,8},{1,17},{9,25},{17,1},{25,9},{2,18},{10... | collective-permute-start | bytes 1572872 | tf_op jit(solution)/shard_map/ppermute | solution.py:21
  69.9 12.5 %collective-permute-start.35 = (bf16[128,2048]{1,0:T(8,128)(2,1)S(1)}, bf16[128,2048]{1,0:T(8,128)(2,1)S(1)}, u32[]{:S(2)}, u32[]{:S(2)}) collective-permute-start(bf16[128,2048]{1,0:T(8,128)(2,1)S(1)} %collective-permute-done.34.refs_2_), channel_id=1, source_target_pairs={{0,8},{8,0},{16,24},{24,16},{1,9},{9,1},{17,25},{25,17},{2,10},{10... | collective-permute-start | bytes 1572872 | tf_op jit(solution)/shard_map/ppermute | solution.py:21
  69.9 13.0 %collective-permute-start.37 = (bf16[128,2048]{1,0:T(8,128)(2,1)S(1)}, bf16[128,2048]{1,0:T(8,128)(2,1)S(1)}, u32[]{:S(2)}, u32[]{:S(2)}) collective-permute-start(bf16[128,2048]{1,0:T(8,128)(2,1)S(1)} %collective-permute-done.36.refs_4_), channel_id=1, source_target_pairs={{0,8},{8,0},{16,24},{24,16},{1,9},{9,1},{17,25},{25,17},{2,10},{10... | collective-permute-start | bytes 1572872 | tf_op jit(solution)/shard_map/ppermute | solution.py:21
  76.0 14.8 %collective-permute-start.25 = (bf16[128,2048]{1,0:T(8,128)(2,1)S(1)}, bf16[128,2048]{1,0:T(8,128)(2,1)S(1)}, u32[]{:S(2)}, u32[]{:S(2)}) collective-permute-start(bf16[128,2048]{1,0:T(8,128)(2,1)S(1)} %collective-permute-done.23.refs_0_), channel_id=1, source_target_pairs={{0,16},{8,24},{16,0},{24,8},{1,17},{9,25},{17,1},{25,9},{2,18},{10... | collective-permute-start | bytes 1572872 | tf_op jit(solution)/shard_map/ppermute | solution.py:21
  77.5 2.2 copy-start.1
  80.8 21.3 %collective-permute-start.29 = (bf16[128,2048]{1,0:T(8,128)(2,1)S(1)}, bf16[128,2048]{1,0:T(8,128)(2,1)S(1)}, u32[]{:S(2)}, u32[]{:S(2)}) collective-permute-start(bf16[128,2048]{1,0:T(8,128)(2,1)S(1)} %collective-permute-done.27.refs_4_), channel_id=1, source_target_pairs={{0,16},{8,24},{16,0},{24,8},{1,17},{9,25},{17,1},{25,9},{2,18},{10... | collective-permute-start | bytes 1572872 | tf_op jit(solution)/shard_map/ppermute | solution.py:21
  82.3 19.8 %collective-permute-start.24 = (bf16[128,2048]{1,0:T(8,128)(2,1)S(1)}, bf16[128,2048]{1,0:T(8,128)(2,1)S(1)}, u32[]{:S(2)}, u32[]{:S(2)}) collective-permute-start(bf16[128,2048]{1,0:T(8,128)(2,1)S(1)} %collective-permute-done.23.refs_0_), channel_id=1, source_target_pairs={{0,8},{8,0},{16,24},{24,16},{1,9},{9,1},{17,25},{25,17},{2,10},{10... | collective-permute-start | bytes 1572872 | tf_op jit(solution)/shard_map/ppermute | solution.py:21
  82.3 23.0 %collective-permute-start.28 = (bf16[128,2048]{1,0:T(8,128)(2,1)S(1)}, bf16[128,2048]{1,0:T(8,128)(2,1)S(1)}, u32[]{:S(2)}, u32[]{:S(2)}) collective-permute-start(bf16[128,2048]{1,0:T(8,128)(2,1)S(1)} %collective-permute-done.27.refs_4_), channel_id=1, source_target_pairs={{0,8},{8,0},{16,24},{24,16},{1,9},{9,1},{17,25},{25,17},{2,10},{10... | collective-permute-start | bytes 1572872 | tf_op jit(solution)/shard_map/ppermute | solution.py:21
  82.8 29.1 %collective-permute-start.17 = (bf16[128,2048]{1,0:T(8,128)(2,1)S(1)}, bf16[128,2048]{1,0:T(8,128)(2,1)S(1)}, u32[]{:S(2)}, u32[]{:S(2)}) collective-permute-start(bf16[128,2048]{1,0:T(8,128)(2,1)S(1)} %collective-permute-done.refs_0_), channel_id=1, source_target_pairs={{0,16},{8,24},{16,0},{24,8},{1,17},{9,25},{17,1},{25,9},{2,18},{10... | collective-permute-start | bytes 1572872 | tf_op jit(solution)/shard_map/ppermute | solution.py:21
  90.8 35.6 %collective-permute-start.9 = (bf16[128,2048]{1,0:T(8,128)(2,1)S(1)}, bf16[128,2048]{1,0:T(8,128)(2,1)S(1)}, u32[]{:S(2)}, u32[]{:S(2)}) collective-permute-start(bf16[128,2048]{1,0:T(8,128)(2,1)S(1)} %pack_columns.6), channel_id=1, source_target_pairs={{0,5},{1,4},{2,7},{3,6},{4,1},{5,0},{6,3},{7,2},{8,13},{9,12},{10,... | collective-permute-start | bytes 1572872 | tf_op jit(solution)/shard_map/ppermute | solution.py:21
  91.3 2.2 copy-start.2
  102.1 24.5 %collective-permute-start.16 = (bf16[128,2048]{1,0:T(8,128)(2,1)S(1)}, bf16[128,2048]{1,0:T(8,128)(2,1)S(1)}, u32[]{:S(2)}, u32[]{:S(2)}) collective-permute-start(bf16[128,2048]{1,0:T(8,128)(2,1)S(1)} %collective-permute-done.refs_0_), channel_id=1, source_target_pairs={{0,8},{8,0},{16,24},{24,16},{1,9},{9,1},{17,25},{25,17},{2,10},{10... | collective-permute-start | bytes 1572872 | tf_op jit(solution)/shard_map/ppermute | solution.py:21
  102.1 24.5 %collective-permute-start.1 = (bf16[128,2048]{1,0:T(8,128)(2,1)S(1)}, bf16[128,2048]{1,0:T(8,128)(2,1)S(1)}, u32[]{:S(2)}, u32[]{:S(2)}) collective-permute-start(bf16[128,2048]{1,0:T(8,128)(2,1)S(1)} %pack_columns.5), channel_id=1, source_target_pairs={{0,6},{1,7},{2,4},{3,5},{4,2},{5,3},{6,0},{7,1},{8,14},{9,15},{10,... | collective-permute-start | bytes 1572872 | tf_op jit(solution)/shard_map/ppermute | solution.py:21
  105.3 24.8 %collective-permute-start.32 = (bf16[4,128,512]{2,1,0:T(8,128)(2,1)S(1)}, bf16[4,128,512]{2,1,0:T(8,128)(2,1)S(1)}, u32[]{:S(2)}, u32[]{:S(2)}) collective-permute-start(bf16[4,128,512]{2,1,0:T(8,128)(2,1)S(1)} %collective-permute-done.31.refs_8_), channel_id=1, source_target_pairs={{0,1},{1,0},{2,3},{3,2},{4,5},{5,4},{6,7},{7,6},{8,9},{9,8},{10,11... | collective-permute-start | bytes 1572872 | tf_op jit(solution)/shard_map/ppermute | solution.py:21
  111.9 28.7 %collective-permute-start.22 = (bf16[4,128,512]{2,1,0:T(8,128)(2,1)S(1)}, bf16[4,128,512]{2,1,0:T(8,128)(2,1)S(1)}, u32[]{:S(2)}, u32[]{:S(2)}) collective-permute-start(bf16[4,128,512]{2,1,0:T(8,128)(2,1)S(1)} %collective-permute-done.8.refs_0_.refs_8_), channel_id=1, source_target_pairs={{0,1},{1,0},{2,3},{3,2},{4,5},{5,4},{6,7},{7,6},{8,9},{9,8},{10,11... | collective-permute-start | bytes 1572872 | tf_op jit(solution)/shard_map/ppermute | solution.py:21
  126.5 15.6 %collective-permute-start.14 = (bf16[4,128,512]{2,1,0:T(8,128)(2,1)S(1)}, bf16[4,128,512]{2,1,0:T(8,128)(2,1)S(1)}, u32[]{:S(2)}, u32[]{:S(2)}) collective-permute-start(bf16[4,128,512]{2,1,0:T(8,128)(2,1)S(1)} %collective-permute-done.8.refs_0_.refs_8_), channel_id=1, source_target_pairs={{0,2},{1,3},{2,0},{3,1},{4,6},{5,7},{6,4},{7,5},{8,10},{9,11},{10,... | collective-permute-start | bytes 1572872 | tf_op jit(solution)/shard_map/ppermute | solution.py:21
  126.5 16.1 %collective-permute-start.39 = (bf16[128,2048]{1,0:T(8,128)(2,1)S(1)}, bf16[128,2048]{1,0:T(8,128)(2,1)S(1)}, u32[]{:S(2)}, u32[]{:S(2)}) collective-permute-start(bf16[128,2048]{1,0:T(8,128)(2,1)S(1)} %collective-permute-done.38.refs_6_), channel_id=1, source_target_pairs={{0,8},{8,0},{16,24},{24,16},{1,9},{9,1},{17,25},{25,17},{2,10},{10... | collective-permute-start | bytes 1572872 | tf_op jit(solution)/shard_map/ppermute | solution.py:21
  126.6 16.0 %collective-permute-start.26 = (bf16[128,2048]{1,0:T(8,128)(2,1)S(1)}, bf16[128,2048]{1,0:T(8,128)(2,1)S(1)}, u32[]{:S(2)}, u32[]{:S(2)}) collective-permute-start(bf16[128,2048]{1,0:T(8,128)(2,1)S(1)} %collective-permute-done.25.refs_2_), channel_id=1, source_target_pairs={{0,8},{8,0},{16,24},{24,16},{1,9},{9,1},{17,25},{25,17},{2,10},{10... | collective-permute-start | bytes 1572872 | tf_op jit(solution)/shard_map/ppermute | solution.py:21
  130.1 13.2 %collective-permute-start.30 = (bf16[128,2048]{1,0:T(8,128)(2,1)S(1)}, bf16[128,2048]{1,0:T(8,128)(2,1)S(1)}, u32[]{:S(2)}, u32[]{:S(2)}) collective-permute-start(bf16[128,2048]{1,0:T(8,128)(2,1)S(1)} %collective-permute-done.29.refs_6_), channel_id=1, source_target_pairs={{0,8},{8,0},{16,24},{24,16},{1,9},{9,1},{17,25},{25,17},{2,10},{10... | collective-permute-start | bytes 1572872 | tf_op jit(solution)/shard_map/ppermute | solution.py:21
  140.6 14.9 %collective-permute-start.20 = (bf16[128,2048]{1,0:T(8,128)(2,1)S(1)}, bf16[128,2048]{1,0:T(8,128)(2,1)S(1)}, u32[]{:S(2)}, u32[]{:S(2)}) collective-permute-start(bf16[128,2048]{1,0:T(8,128)(2,1)S(1)} %collective-permute-done.9.refs_0_.refs_4_), channel_id=1, source_target_pairs={{0,16},{8,24},{16,0},{24,8},{1,17},{9,25},{17,1},{25,9},{2,18},{10... | collective-permute-start | bytes 1572872 | tf_op jit(solution)/shard_map/ppermute | solution.py:21
  142.1 15.8 %collective-permute-start.10 = (bf16[128,2048]{1,0:T(8,128)(2,1)S(1)}, bf16[128,2048]{1,0:T(8,128)(2,1)S(1)}, u32[]{:S(2)}, u32[]{:S(2)}) collective-permute-start(bf16[128,2048]{1,0:T(8,128)(2,1)S(1)} %pack_columns.7), channel_id=1, source_target_pairs={{0,7},{1,6},{2,5},{3,4},{4,3},{5,2},{6,1},{7,0},{8,15},{9,14},{10,... | collective-permute-start | bytes 1572872 | tf_op jit(solution)/shard_map/ppermute | solution.py:21
  142.7 15.7 %collective-permute-start.18 = (bf16[128,2048]{1,0:T(8,128)(2,1)S(1)}, bf16[128,2048]{1,0:T(8,128)(2,1)S(1)}, u32[]{:S(2)}, u32[]{:S(2)}) collective-permute-start(bf16[128,2048]{1,0:T(8,128)(2,1)S(1)} %collective-permute-done.17.refs_2_), channel_id=1, source_target_pairs={{0,8},{8,0},{16,24},{24,16},{1,9},{9,1},{17,25},{25,17},{2,10},{10... | collective-permute-start | bytes 1572872 | tf_op jit(solution)/shard_map/ppermute | solution.py:21
  142.7 24.0 %collective-permute-start.3 = (bf16[128,2048]{1,0:T(8,128)(2,1)S(1)}, bf16[128,2048]{1,0:T(8,128)(2,1)S(1)}, u32[]{:S(2)}, u32[]{:S(2)}) collective-permute-start(bf16[128,2048]{1,0:T(8,128)(2,1)S(1)} %collective-permute-done.1.refs_0_), channel_id=1, source_target_pairs={{0,16},{8,24},{16,0},{24,8},{1,17},{9,25},{17,1},{25,9},{2,18},{10... | collective-permute-start | bytes 1572872 | tf_op jit(solution)/shard_map/ppermute | solution.py:21
  143.3 25.9 %collective-permute-start.19 = (bf16[128,2048]{1,0:T(8,128)(2,1)S(1)}, bf16[128,2048]{1,0:T(8,128)(2,1)S(1)}, u32[]{:S(2)}, u32[]{:S(2)}) collective-permute-start(bf16[128,2048]{1,0:T(8,128)(2,1)S(1)} %collective-permute-done.9.refs_0_.refs_4_), channel_id=1, source_target_pairs={{0,8},{8,0},{16,24},{24,16},{1,9},{9,1},{17,25},{25,17},{2,10},{10... | collective-permute-start | bytes 1572872 | tf_op jit(solution)/shard_map/ppermute | solution.py:21
  155.5 13.7 %collective-permute-start.21 = (bf16[128,2048]{1,0:T(8,128)(2,1)S(1)}, bf16[128,2048]{1,0:T(8,128)(2,1)S(1)}, u32[]{:S(2)}, u32[]{:S(2)}) collective-permute-start(bf16[128,2048]{1,0:T(8,128)(2,1)S(1)} %collective-permute-done.20.refs_6_), channel_id=1, source_target_pairs={{0,8},{8,0},{16,24},{24,16},{1,9},{9,1},{17,25},{25,17},{2,10},{10... | collective-permute-start | bytes 1572872 | tf_op jit(solution)/shard_map/ppermute | solution.py:21
  157.9 18.5 %collective-permute-start.12 = (bf16[128,2048]{1,0:T(8,128)(2,1)S(1)}, bf16[128,2048]{1,0:T(8,128)(2,1)S(1)}, u32[]{:S(2)}, u32[]{:S(2)}) collective-permute-start(bf16[128,2048]{1,0:T(8,128)(2,1)S(1)} %collective-permute-done.10.refs_4_), channel_id=1, source_target_pairs={{0,16},{8,24},{16,0},{24,8},{1,17},{9,25},{17,1},{25,9},{2,18},{10... | collective-permute-start | bytes 1572872 | tf_op jit(solution)/shard_map/ppermute | solution.py:21
  158.4 43.2 %collective-permute-start.2 = (bf16[128,2048]{1,0:T(8,128)(2,1)S(1)}, bf16[128,2048]{1,0:T(8,128)(2,1)S(1)}, u32[]{:S(2)}, u32[]{:S(2)}) collective-permute-start(bf16[128,2048]{1,0:T(8,128)(2,1)S(1)} %collective-permute-done.1.refs_0_), channel_id=1, source_target_pairs={{0,8},{8,0},{16,24},{24,16},{1,9},{9,1},{17,25},{25,17},{2,10},{10... | collective-permute-start | bytes 1572872 | tf_op jit(solution)/shard_map/ppermute | solution.py:21
  166.7 34.9 %collective-permute-start.15 = (bf16[4,128,512]{2,1,0:T(8,128)(2,1)S(1)}, bf16[4,128,512]{2,1,0:T(8,128)(2,1)S(1)}, u32[]{:S(2)}, u32[]{:S(2)}) collective-permute-start(bf16[4,128,512]{2,1,0:T(8,128)(2,1)S(1)} %collective-permute-done.14.refs_8_), channel_id=1, source_target_pairs={{0,1},{1,0},{2,3},{3,2},{4,5},{5,4},{6,7},{7,6},{8,9},{9,8},{10,11... | collective-permute-start | bytes 1572872 | tf_op jit(solution)/shard_map/ppermute | solution.py:21
  169.2 32.4 %collective-permute-start.4 = (bf16[128,2048]{1,0:T(8,128)(2,1)S(1)}, bf16[128,2048]{1,0:T(8,128)(2,1)S(1)}, u32[]{:S(2)}, u32[]{:S(2)}) collective-permute-start(bf16[128,2048]{1,0:T(8,128)(2,1)S(1)} %collective-permute-done.3.refs_2_), channel_id=1, source_target_pairs={{0,8},{8,0},{16,24},{24,16},{1,9},{9,1},{17,25},{25,17},{2,10},{10... | collective-permute-start | bytes 1572872 | tf_op jit(solution)/shard_map/ppermute | solution.py:21
  169.2 32.4 %collective-permute-start.11 = (bf16[128,2048]{1,0:T(8,128)(2,1)S(1)}, bf16[128,2048]{1,0:T(8,128)(2,1)S(1)}, u32[]{:S(2)}, u32[]{:S(2)}) collective-permute-start(bf16[128,2048]{1,0:T(8,128)(2,1)S(1)} %collective-permute-done.10.refs_4_), channel_id=1, source_target_pairs={{0,8},{8,0},{16,24},{24,16},{1,9},{9,1},{17,25},{25,17},{2,10},{10... | collective-permute-start | bytes 1572872 | tf_op jit(solution)/shard_map/ppermute | solution.py:21
  176.3 25.3 %collective-permute-start.13 = (bf16[128,2048]{1,0:T(8,128)(2,1)S(1)}, bf16[128,2048]{1,0:T(8,128)(2,1)S(1)}, u32[]{:S(2)}, u32[]{:S(2)}) collective-permute-start(bf16[128,2048]{1,0:T(8,128)(2,1)S(1)} %collective-permute-done.12.refs_6_), channel_id=1, source_target_pairs={{0,8},{8,0},{16,24},{24,16},{1,9},{9,1},{17,25},{25,17},{2,10},{10... | collective-permute-start | bytes 1572872 | tf_op jit(solution)/shard_map/ppermute | solution.py:21

commit v4 on v3

v4 whole, which is shorter than its diff:
```python
import functools
import math

import jax
import jax.numpy as jnp
from jax import lax
from jax.experimental import pallas as pl
from jax.experimental.pallas import tpu as pltpu
from jax.sharding import PartitionSpec as P

epsilon = 1e-06
lanes = 128
edges = (0.0, 0.25, 0.5, 0.75, 1.0)
ANY = pl.BlockSpec(memory_space=pl.ANY)
SMEM = pl.BlockSpec(memory_space=pltpu.SMEM)
VMEM = pl.BlockSpec(memory_space=pltpu.VMEM)
HBM = pl.BlockSpec(memory_space=pltpu.HBM)


def exchange(block, axis, distance):
    size = lax.axis_size(axis)
    return lax.ppermute(block, axis, [(i, i ^ distance) for i in range(size)])


def pack_kernel(start, distances, tok_ref, hidden_ref, *refs):
    out_refs, sems = refs[-1 - len(distances) : -1], refs[-1]
    width = out_refs[0].shape[1]
    own_width = hidden_ref.shape[2] // (len(distances))
    copies = []
    for at, distance in enumerate(distances):
        column = pl.multiple_of((tok_ref[0] ^ distance) * own_width + start, lanes)
        copies.append(
            pltpu.make_async_copy(
                hidden_ref.at[0, :, pl.ds(column, width)], out_refs[at], sems.at[at]
            )
        )
    for copy in copies:
        copy.start()
    for copy in copies:
        copy.wait()


def pack(tok, hidden, count, start, width, after):
    rows = hidden.shape[1]
    return pl.pallas_call(
        functools.partial(pack_kernel, start, list(range(count))),
        out_shape=[jax.ShapeDtypeStruct((rows, width), hidden.dtype)] * count,
        in_specs=[SMEM, HBM] + [ANY] * len(after),
        out_specs=[VMEM] * count,
        scratch_shapes=[pltpu.SemaphoreType.DMA((count,))],
        compiler_params=pltpu.CompilerParams(vmem_limit_bytes=2**20),
        cost_estimate=pl.CostEstimate(
            flops=0, bytes_accessed=4 * count * rows * width, transcendentals=0
        ),
        name="pack_columns",
    )(tok, hidden, *after)


def join_kernel(places, *refs):
    out_ref = refs[-1]
    for ref, (row, column, width) in zip(refs, places):
        rows = ref.shape[0]
        out_ref[row : row + rows, column : column + width] = ref[:, -width:]


def join(parts, shape, after=()):
    arrays = [part[0] for part in parts]
    return pl.pallas_call(
        functools.partial(join_kernel, [part[1:] for part in parts]),
        out_shape=jax.ShapeDtypeStruct(shape, arrays[0].dtype),
        in_specs=[VMEM] * len(arrays) + [ANY] * len(after),
        out_specs=VMEM,
        compiler_params=pltpu.CompilerParams(vmem_limit_bytes=2**20),
        cost_estimate=pl.CostEstimate(
            flops=0, bytes_accessed=2 * shape[0] * shape[1], transcendentals=0
        ),
        name="join_blocks",
    )(*arrays, *after)


def stack(arrays, width, after=()):
    rows = arrays[0].shape[0]
    parts = [(array, i * rows, 0, width) for i, array in enumerate(arrays)]
    return join(parts, (rows * len(arrays), width), after)


def mask_kernel(valid_ref, user_ref, cot_ref, *out_refs):
    rows, width = out_refs[0].shape
    keep = lax.broadcasted_iota(jnp.int32, (rows, width), 0) < valid_ref[0]
    for slot, out_ref in enumerate(out_refs):
        column = pl.multiple_of((user_ref[0] ^ slot) * width, lanes)
        block = cot_ref[0, :, pl.ds(column, width)]
        out_ref[...] = jnp.where(keep, block, jnp.zeros_like(block))


def mask(valid, user, cotangent, user_count):
    _, rows, total = cotangent.shape
    return pl.pallas_call(
        mask_kernel,
        out_shape=[jax.ShapeDtypeStruct((rows, total // user_count), cotangent.dtype)] * user_count,
        in_specs=[SMEM, SMEM, VMEM],
        out_specs=[VMEM] * user_count,
        compiler_params=pltpu.CompilerParams(vmem_limit_bytes=2 * 2**20),
        name="mask_cotangent",
    )(valid, user, cotangent)


def product_kernel(user_count, copies, *refs):
    sums_ref, out_ref = refs[-1], refs[-2]
    before_ref, right_ref = refs[-3], refs[-4]
    parts = refs[:-4]
    width, columns = out_ref.shape[1:]
    tile = min(width, 2 * lanes)
    squares = []
    for slot in range(user_count):
        right = right_ref[:, slot * columns : (slot + 1) * columns]

        def step(i, total, slot=slot, right=right):
            rows = pl.ds(pl.multiple_of(i * tile, tile), tile)
            left = jnp.concatenate(
                [
                    ref[at * rows_each : (at + 1) * rows_each, rows]
                    for ref, at, rows_each in split(parts, user_count)[slot]
                ],
                axis=0,
            )
            value = lax.dot_general(
                left, right, (((0,), (0,)), ((), ())), preferred_element_type=jnp.float32
            )
            out_ref[slot, rows, :] = value
            row = jnp.sum(value * value, axis=0, keepdims=True)
            for start in range(0, row.shape[1], lanes):
                total += row[:, start : start + lanes]
            return total

        squares.append(lax.fori_loop(0, width // tile, step, jnp.zeros((1, lanes), jnp.float32)))
    rows = jnp.concatenate(squares + [jnp.zeros((8 - user_count, lanes), jnp.float32)], axis=0)
    rows += before_ref[0]
    sums_ref[...] = jnp.broadcast_to(rows[None], sums_ref.shape)


def split(parts, user_count):
    slots = [[] for _ in range(user_count)]
    levels = user_count.bit_length()
    for first in range(0, len(parts), levels):
        have = [0]
        each = parts[first].shape[0]
        for level, ref in enumerate(parts[first : first + levels]):
            distance = 0 if level == 0 else user_count >> level
            for at, slot in enumerate(have):
                slots[slot ^ distance].append((ref, at, each))
            if level:
                have = have + [slot ^ distance for slot in have]
    return slots


def product(parts, right, before, width, user_count, copies):
    tokens, total = right.shape
    columns = total // user_count
    operands = [*parts, right, before]
    return pl.pallas_call(
        functools.partial(product_kernel, user_count, copies),
        out_shape=[
            jax.ShapeDtypeStruct((user_count, width, columns), jnp.float32),
            jax.ShapeDtypeStruct((copies, 8, lanes), jnp.float32),
        ],
        in_specs=[VMEM] * len(operands),
        out_specs=[VMEM] * 2,
        compiler_params=pltpu.CompilerParams(vmem_limit_bytes=10 * 2**20),
        cost_estimate=pl.CostEstimate(
            flops=2 * user_count * tokens * columns * width,
            bytes_accessed=2 * user_count * tokens * (width + columns),
            transcendentals=0,
        ),
        name="product_and_squares",
    )(*operands)


def combine_kernel(user_count, clip_bound, scaling, starts, user_ref, sums_ref, *refs):
    out_ref = refs[-1]
    per_user = sums_ref.shape[0] // user_count
    by_source = [
        jnp.sum(sums_ref[j * per_user : (j + 1) * per_user], axis=0) for j in range(user_count)
    ]
    factors = []
    for u in range(user_count):
        row = sum(by_source[j][j ^ u : (j ^ u) + 1, :] for j in range(user_count))
        norm_sq = jnp.sum(row, axis=1, keepdims=True)
        factors.append(jnp.minimum(1.0, clip_bound / jnp.sqrt(norm_sq + epsilon)) * scaling)
    by_slot = []
    for slot in range(user_count):
        user = user_ref[0] ^ slot
        by_slot.append(sum(jnp.where(user == u, factors[u], 0.0) for u in range(user_count)))
    tile = out_ref.shape[0]
    row = pl.program_id(0) * tile
    for ref, start in zip(refs, starts):

        @pl.when((row >= start) & (row < start + ref.shape[1]))
        def _(ref=ref, start=start):
            at = pl.ds(pl.multiple_of(row - start, tile), tile)
            result = by_slot[0] * ref[0, at, :]
            for slot in range(1, user_count):
                result += by_slot[slot] * ref[slot, at, :]
            out_ref[...] = result


def combine(user, sums, gradients, clip_bound, scaling):
    user_count, _, columns = gradients[0].shape
    heights = [gradient.shape[1] for gradient in gradients]
    starts = [sum(heights[:i]) for i in range(len(heights))]
    rows = sum(heights)
    tile = math.gcd(256, *heights)
    return pl.pallas_call(
        functools.partial(combine_kernel, user_count, clip_bound, scaling, starts),
        grid=(rows // tile,),
        out_shape=jax.ShapeDtypeStruct((rows, columns), jnp.float32),
        in_specs=[SMEM] + [VMEM] * (1 + len(gradients)),
        out_specs=pl.BlockSpec((tile, columns), lambda i: (i, 0)),
        compiler_params=pltpu.CompilerParams(vmem_limit_bytes=8 * 2**20),
        name="weighted_sum",
    )(user, sums, *gradients)


def body(hidden, cotangent, lengths):
    tok_count = lax.axis_size("tok")
    user_count = lax.axis_size("user")
    tok_rows = hidden.shape[1]
    hidden_width = hidden.shape[2]
    model_width = cotangent.shape[2]
    capacity = tok_rows * tok_count
    own_width = hidden_width // tok_count
    columns = model_width // user_count
    clip_bound = math.sqrt(8.0 * hidden_width * model_width * capacity)
    scaling = math.sqrt(hidden_width * model_width) / (user_count * clip_bound)
    user = lax.axis_index("user").astype(jnp.int32).reshape(1)
    tok = lax.axis_index("tok").astype(jnp.int32).reshape(1)
    valid = lengths - tok * tok_rows
    half = tok_count // 2
    units = own_width // lanes
    bounds = sorted({round(edge * units) * lanes for edge in edges})

    masked = mask(valid, user, cotangent, user_count)
    by_slot = [masked[0]] + [exchange(masked[s], "user", s) for s in range(1, user_count)]
    cots = {
        0: join(
            [(block, 0, s * columns, columns) for s, block in enumerate(by_slot)],
            (tok_rows, model_width),
        )
    }

    def relay(d, after):
        bit = (d & -d) // 2
        while bit:
            message = join([(cots[d], 0, 0, model_width)], (tok_rows, model_width), after)
            cots[d + bit] = exchange(message, "tok", bit)
            bit //= 2

    right = None
    totals = [jnp.zeros((1, 8, lanes), jnp.float32)]
    gradients = []
    crossed = []
    arrived = []
    for q, (start, stop) in enumerate(zip(bounds[:-1], bounds[1:])):
        width = stop - start
        first, last = start == 0, stop == own_width
        after = [masked[0]] if first else [arrived[q - 1][half], arrived[q - 1][half + 1]]
        if q >= 2:
            after.append(crossed[q - 2])
        outgoing = pack(tok, hidden, tok_count, start, width, after)
        blocks = {0: outgoing[0]}
        for d in range(1, tok_count):
            message = outgoing[d]
            rides = first and d & (d - 1) == 0
            if rides:
                message = join(
                    [(cots[0], 0, 0, model_width), (message, 0, model_width, width)],
                    (tok_rows, model_width + width),
                )
            blocks[d] = exchange(message, "tok", d)
            if rides:
                cots[d] = blocks[d][:, :model_width]
        arrived.append(blocks)
        if first:
            for d in range(1, tok_count):
                relay(d, [])
            right = stack([cots[d] for d in range(tok_count)], model_width)
        parts = []
        for sources in (range(half), range(half, tok_count)):
            far = sources[0] > 0
            have = stack([blocks[d] for d in sources], width, totals[q - 1 : q] if far and q >= 2 else [])
            parts.append(have)
            distance = user_count // 2
            while distance:
                came = exchange(have, "user", distance)
                parts.append(came)
                if far and distance == user_count // 2:
                    crossed.append(came)
                distance //= 2
                if distance:
                    have = stack([have, came], width, totals[q : q + 1] if far and q >= 1 else [])
        gradient, sums = product(
            parts, right, totals[-1], width, user_count, tok_count * user_count if last else 1
        )
        gradients.append(gradient)
        totals.append(sums)
    sums = lax.all_to_all(sums, ("user", "tok"), split_axis=0, concat_axis=0, tiled=True)
    return combine(user, sums, gradients, clip_bound, scaling)


def solution(mesh):
    return jax.shard_map(
        body,
        mesh=mesh,
        in_specs=(P("user", "tok", None), P("user", "tok", None), P("user")),
        out_specs=P("tok", "user"),
        check_vma=False,
    )
```

time: 227 us -> 245 us (1.079)
  starting transfers between devices: 37.9 us -> 71.6 us
  Pallas kernels: 39.7 us -> 24.4 us
  local copies, waits for them, and re-layouts: 7.6 us -> 3.36 us
  blocking collectives: 11.4 us -> 15.3 us
    ppermute x41 -> x51, starting transfers between devices: 37.9 us -> 71.6 us  [exchange(): return lax.ppermute(block, axis, [(i, i ^ distance) for i in range(size)])]
    pallas_call x8 -> x32, Pallas kernels: 34.5 us -> 19.2 us  [the longest x4 16.8 us: product(): pl.pallas_call(functools.partial(product_kernel, user_count, copies), out...]
    unnamed x10 -> x6, local copies, waits for them, and re-layouts: 7.6 us -> 3.23 us
    all_to_all x1, blocking collectives: 11.4 us -> 15.3 us  [body(): lax.all_to_all(sums, ('user', 'tok'), split_axis=0, concat_axis=0, tiled=...]
    ppermute x41 -> x51, waiting for transfers between devices: 130 us -> 129 us  [exchange(): return lax.ppermute(block, axis, [(i, i ^ distance) for i in range(size)])]
  transfers between devices with their start and end apart: 41 -> 51, of which waited for: 16 -> 29; matrix products, arithmetic and copies ran while one was open for 0% -> 0% of each run, Pallas kernels for 11% -> 6%
where the time goes in v4:
time: 245 us; the launch traced here: 244 us
  waiting for transfers between devices  129 us (53%)
  starting transfers between devices  71.6 us (29%)
  Pallas kernels  24.4 us (10%)
  blocking collectives  15.3 us (6%)
  local copies, waits for them, and re-layouts  3.36 us (1%)
    ppermute x51, waiting for transfers between devices, exchange(): return lax.ppermute(block, axis, [(i, i ^ distance) for i in range(size)])  129 us
    ppermute x51, starting transfers between devices, exchange(): return lax.ppermute(block, axis, [(i, i ^ distance) for i in range(size)])  71.6 us
    pallas_call x4, Pallas kernels, product(): pl.pallas_call(functools.partial(product_kernel, user_count, copies), out...  16.8 us
    all_to_all x1, blocking collectives, body(): lax.all_to_all(sums, ('user', 'tok'), split_axis=0, concat_axis=0, tiled=...  15.3 us
    pallas_call x1, Pallas kernels, combine(): pl.pallas_call(functools.partial(combine_kernel, user_count, clip_bound,...  5.24 us
  transfers between devices with their start and end apart: 51, of which 29 were waited for; matrix products, arithmetic and copies ran while one was open for 0% of the time, Pallas kernels for 6%

profile of v4, /device:TPU:0, one launch (start us, length us, event | category | flops | bytes accessed | tf_op | source)
XLA Modules:
  0.0 244.5 jit_solution(12169470672332884372)
XLA Ops:
  0.7 1.0 copy-done.2
  2.3 2.6 %collective-permute-start.1 = (bf16[128,512]{1,0:T(8,128)(2,1)S(1)}, bf16[128,512]{1,0:T(8,128)(2,1)S(1)}, u32[]{:S(2)}, u32[]{:S(2)}) collective-permute-start(bf16[128,512]{1,0:T(8,128)(2,1)S(1)} %get-tuple-element.51), channel_id=1, source_target_pairs={{0,16},{8,24},{16,0},{24,8},{1,17},{9,25},{17,1},{25,9},{2,18},{10... | collective-permute-start | bytes 393224 | tf_op jit(solution)/shard_map/ppermute | solution.py:22
  4.9 2.2 copy-done
  7.4 1.8 collective-permute-done.1.refs_2_
  9.2 2.3 collective-permute-done.2.refs_3_
  11.6 1.7 collective-permute-start.30
  13.3 1.6 collective-permute-start.29
  14.9 2.7 %collective-permute-start.3 = (bf16[128,2560]{1,0:T(8,128)(2,1)S(1)}, bf16[128,2560]{1,0:T(8,128)(2,1)S(1)}, u32[]{:S(2)}, u32[]{:S(2)}) collective-permute-start(bf16[128,2560]{1,0:T(8,128)(2,1)S(1)} %join_blocks.25), channel_id=1, source_target_pairs={{0,4},{1,5},{2,6},{3,7},{4,0},{5,1},{6,2},{7,3},{8,12},{9,13},{10,... | collective-permute-start | bytes 1966088 | tf_op jit(solution)/shard_map/ppermute | solution.py:22
  18.0 1.3 collective-permute-start.4
  19.3 28.7 %collective-permute-done.31.refs_3_ = bf16[128,512]{1,0:T(8,128)(2,1)S(1)} collective-permute-done((bf16[128,512]{1,0:T(8,128)(2,1)S(1)}, bf16[128,512]{1,0:T(8,128)(2,1)S(1)}, u32[]{:S(2)}, u32[]{:S(2)}) %collective-permute-start.31) | collective-permute-done | bytes 131104 | tf_op jit(solution)/shard_map/ppermute | solution.py:22
  48.0 3.2 %collective-permute-start.7 = (bf16[128,512]{1,0:T(8,128)(2,1)S(1)}, bf16[128,512]{1,0:T(8,128)(2,1)S(1)}, u32[]{:S(2)}, u32[]{:S(2)}) collective-permute-start(bf16[128,512]{1,0:T(8,128)(2,1)S(1)} %get-tuple-element.57), channel_id=1, source_target_pairs={{0,6},{1,7},{2,4},{3,5},{4,2},{5,3},{6,0},{7,1},{8,14},{9,15},{10,... | collective-permute-start | bytes 393224 | tf_op jit(solution)/shard_map/ppermute | solution.py:22
  51.2 1.6 collective-permute-start.32
  52.8 2.5 %collective-permute-done.4.refs_1_ = bf16[128,512]{1,0:T(8,128)(2,1)S(1)} collective-permute-done((bf16[128,512]{1,0:T(8,128)(2,1)S(1)}, bf16[128,512]{1,0:T(8,128)(2,1)S(1)}, u32[]{:S(2)}, u32[]{:S(2)}) %collective-permute-start.4) | collective-permute-done | bytes 131104 | tf_op jit(solution)/shard_map/ppermute | solution.py:22
  55.6 3.4 %collective-permute-done.8.refs_3_ = bf16[128,512]{1,0:T(8,128)(2,1)S(1)} collective-permute-done((bf16[128,512]{1,0:T(8,128)(2,1)S(1)}, bf16[128,512]{1,0:T(8,128)(2,1)S(1)}, u32[]{:S(2)}, u32[]{:S(2)}) %collective-permute-start.8) | collective-permute-done | bytes 131104 | tf_op jit(solution)/shard_map/ppermute | solution.py:22
  59.0 1.6 collective-permute-start.9
  60.8 5.9 %collective-permute-start.5 = (bf16[128,512]{1,0:T(8,128)(2,1)S(1)}, bf16[128,512]{1,0:T(8,128)(2,1)S(1)}, u32[]{:S(2)}, u32[]{:S(2)}) collective-permute-start(bf16[128,512]{1,0:T(8,128)(2,1)S(1)} %get-tuple-element.55), channel_id=1, source_target_pairs={{0,4},{1,5},{2,6},{3,7},{4,0},{5,1},{6,2},{7,3},{8,12},{9,13},{10,... | collective-permute-start | bytes 393224 | tf_op jit(solution)/shard_map/ppermute | solution.py:22
  66.9 2.8 %collective-permute-start.6 = (bf16[128,512]{1,0:T(8,128)(2,1)S(1)}, bf16[128,512]{1,0:T(8,128)(2,1)S(1)}, u32[]{:S(2)}, u32[]{:S(2)}) collective-permute-start(bf16[128,512]{1,0:T(8,128)(2,1)S(1)} %get-tuple-element.56), channel_id=1, source_target_pairs={{0,5},{1,4},{2,7},{3,6},{4,1},{5,0},{6,3},{7,2},{8,13},{9,12},{10,... | collective-permute-start | bytes 393224 | tf_op jit(solution)/shard_map/ppermute | solution.py:22
  69.7 3.6 %collective-permute-done.5.refs_0_ = bf16[128,512]{1,0:T(8,128)(2,1)S(1)} collective-permute-done((bf16[128,512]{1,0:T(8,128)(2,1)S(1)}, bf16[128,512]{1,0:T(8,128)(2,1)S(1)}, u32[]{:S(2)}, u32[]{:S(2)}) %collective-permute-start.5) | collective-permute-done | bytes 131104 | tf_op jit(solution)/shard_map/ppermute | solution.py:22
  73.3 1.2 collective-permute-start.24
  75.3 2.2 collective-permute-start.26
  77.7 7.0 %collective-permute-done.6.refs_1_ = bf16[128,512]{1,0:T(8,128)(2,1)S(1)} collective-permute-done((bf16[128,512]{1,0:T(8,128)(2,1)S(1)}, bf16[128,512]{1,0:T(8,128)(2,1)S(1)}, u32[]{:S(2)}, u32[]{:S(2)}) %collective-permute-start.6) | collective-permute-done | bytes 131104 | tf_op jit(solution)/shard_map/ppermute | solution.py:22
  84.7 1.5 collective-permute-start.35
  86.2 1.2 collective-permute-done.25.refs_2_
  87.4 2.8 %collective-permute-done.26.refs_3_ = bf16[128,512]{1,0:T(8,128)(2,1)S(1)} collective-permute-done((bf16[128,512]{1,0:T(8,128)(2,1)S(1)}, bf16[128,512]{1,0:T(8,128)(2,1)S(1)}, u32[]{:S(2)}, u32[]{:S(2)}) %collective-permute-start.26) | collective-permute-done | bytes 131104 | tf_op jit(solution)/shard_map/ppermute | solution.py:22
  90.2 1.0 collective-permute-start.12
  91.2 5.8 %collective-permute-done.12.refs_2_ = bf16[128,512]{1,0:T(8,128)(2,1)S(1)} collective-permute-done((bf16[128,512]{1,0:T(8,128)(2,1)S(1)}, bf16[128,512]{1,0:T(8,128)(2,1)S(1)}, u32[]{:S(2)}, u32[]{:S(2)}) %collective-permute-start.12) | collective-permute-done | bytes 131104 | tf_op jit(solution)/shard_map/ppermute | solution.py:22
  97.6 1.6 collective-permute-start.13
  99.2 6.2 %collective-permute-done.13.refs_3_ = bf16[128,512]{1,0:T(8,128)(2,1)S(1)} collective-permute-done((bf16[128,512]{1,0:T(8,128)(2,1)S(1)}, bf16[128,512]{1,0:T(8,128)(2,1)S(1)}, u32[]{:S(2)}, u32[]{:S(2)}) %collective-permute-start.13) | collective-permute-done | bytes 131104 | tf_op jit(solution)/shard_map/ppermute | solution.py:22
  105.6 1.9 collective-permute-start.38
  107.5 1.6 collective-permute-done.27.refs_1_
  109.8 10.5 %collective-permute-done.36.refs_5_ = bf16[128,2048]{1,0:T(8,128)(2,1)S(1)} collective-permute-done((bf16[128,2048]{1,0:T(8,128)(2,1)S(1)}, bf16[128,2048]{1,0:T(8,128)(2,1)S(1)}, u32[]{:S(2)}, u32[]{:S(2)}) %collective-permute-start.36) | collective-permute-done | bytes 524320 | tf_op jit(solution)/shard_map/ppermute | solution.py:22
  120.3 7.4 %collective-permute-done.38.refs_7_ = bf16[128,2048]{1,0:T(8,128)(2,1)S(1)} collective-permute-done((bf16[128,2048]{1,0:T(8,128)(2,1)S(1)}, bf16[128,2048]{1,0:T(8,128)(2,1)S(1)}, u32[]{:S(2)}, u32[]{:S(2)}) %collective-permute-start.38) | collective-permute-done | bytes 524320 | tf_op jit(solution)/shard_map/ppermute | solution.py:22
  128.1 4.2 %product_and_squares.4 = (f32[4,512,512]{2,1,0:T(8,128)S(1)}, f32[1,8,128]{2,1,0:T(8,128)S(1)}) custom-call(bf16[512,512]{1,0:T(8,128)(2,1)S(1)} %join_blocks.34.refs_0_, bf16[512,512]{1,0:T(8,128)(2,1)S(1)} %collective-permute-done.32.refs_1_, bf16[1024,512]{1,0:T(8,128)(2,1)S(1)} %collective-permute-done.33.refs_2_, ...), custom_call_target="tpu_custom_call" | custom-call | flops 2147483648 | bytes 8388608 | tf_op jit(solution)/shard_map/product_and_squares/pallas_call | solution.py:161
  133.0 1.7 collective-permute-start.42
  134.6 1.6 collective-permute-start.43
  136.2 2.4 collective-permute-done.41.refs_1_
  139.6 1.9 collective-permute-start.11
  141.5 2.6 %collective-permute-done.43.refs_3_ = bf16[128,512]{1,0:T(8,128)(2,1)S(1)} collective-permute-done((bf16[128,512]{1,0:T(8,128)(2,1)S(1)}, bf16[128,512]{1,0:T(8,128)(2,1)S(1)}, u32[]{:S(2)}, u32[]{:S(2)}) %collective-permute-start.43) | collective-permute-done | bytes 131104 | tf_op jit(solution)/shard_map/ppermute | solution.py:22
  144.2 1.5 collective-permute-start.44
  145.7 5.5 %collective-permute-done.10.refs_0_ = bf16[128,512]{1,0:T(8,128)(2,1)S(1)} collective-permute-done((bf16[128,512]{1,0:T(8,128)(2,1)S(1)}, bf16[128,512]{1,0:T(8,128)(2,1)S(1)}, u32[]{:S(2)}, u32[]{:S(2)}) %collective-permute-start.10) | collective-permute-done | bytes 131104 | tf_op jit(solution)/shard_map/ppermute | solution.py:22
  151.2 1.3 collective-permute-start.46
  152.5 2.9 %collective-permute-done.11.refs_1_ = bf16[128,512]{1,0:T(8,128)(2,1)S(1)} collective-permute-done((bf16[128,512]{1,0:T(8,128)(2,1)S(1)}, bf16[128,512]{1,0:T(8,128)(2,1)S(1)}, u32[]{:S(2)}, u32[]{:S(2)}) %collective-permute-start.11) | collective-permute-done | bytes 131104 | tf_op jit(solution)/shard_map/ppermute | solution.py:22
  155.4 2.2 collective-permute-start.47
  158.6 4.6 %collective-permute-done.47.refs_3_ = bf16[128,512]{1,0:T(8,128)(2,1)S(1)} collective-permute-done((bf16[128,512]{1,0:T(8,128)(2,1)S(1)}, bf16[128,512]{1,0:T(8,128)(2,1)S(1)}, u32[]{:S(2)}, u32[]{:S(2)}) %collective-permute-start.47) | collective-permute-done | bytes 131104 | tf_op jit(solution)/shard_map/ppermute | solution.py:22
  163.2 1.6 collective-permute-start.48
  164.9 4.2 %product_and_squares.5 = (f32[4,512,512]{2,1,0:T(8,128)S(1)}, f32[1,8,128]{2,1,0:T(8,128)S(1)}) custom-call(bf16[512,512]{1,0:T(8,128)(2,1)S(1)} %join_blocks.30.refs_0_, bf16[512,512]{1,0:T(8,128)(2,1)S(1)} %collective-permute-done.27.refs_1_, bf16[1024,512]{1,0:T(8,128)(2,1)S(1)} %collective-permute-done.28.refs_2_, ...), custom_call_target="tpu_custom_call" | custom-call | flops 2147483648 | bytes 8388608 | tf_op jit(solution)/shard_map/product_and_squares/pallas_call | solution.py:161
  169.1 4.1 %collective-permute-done.48.refs_1_.refs_4_ = bf16[512,512]{1,0:T(8,128)(2,1)S(1)} collective-permute-done((bf16[512,512]{1,0:T(8,128)(2,1)S(1)}, bf16[512,512]{1,0:T(8,128)(2,1)S(1)}, u32[]{:S(2)}, u32[]{:S(2)}) %collective-permute-start.48) | collective-permute-done | bytes 524320 | tf_op jit(solution)/shard_map/ppermute | solution.py:22
  173.6 1.6 collective-permute-start.15
  175.2 4.7 %collective-permute-start.16 = (bf16[128,512]{1,0:T(8,128)(2,1)S(1)}, bf16[128,512]{1,0:T(8,128)(2,1)S(1)}, u32[]{:S(2)}, u32[]{:S(2)}) collective-permute-start(bf16[128,512]{1,0:T(8,128)(2,1)S(1)} %get-tuple-element.65), channel_id=1, source_target_pairs={{0,2},{1,3},{2,0},{3,1},{4,6},{5,7},{6,4},{7,5},{8,10},{9,11},{10,... | collective-permute-start | bytes 393224 | tf_op jit(solution)/shard_map/ppermute | solution.py:22
  179.9 4.7 %collective-permute-start.20 = (bf16[128,512]{1,0:T(8,128)(2,1)S(1)}, bf16[128,512]{1,0:T(8,128)(2,1)S(1)}, u32[]{:S(2)}, u32[]{:S(2)}) collective-permute-start(bf16[128,512]{1,0:T(8,128)(2,1)S(1)} %get-tuple-element.67), channel_id=1, source_target_pairs={{0,4},{1,5},{2,6},{3,7},{4,0},{5,1},{6,2},{7,3},{8,12},{9,13},{10,... | collective-permute-start | bytes 393224 | tf_op jit(solution)/shard_map/ppermute | solution.py:22
  184.6 1.9 collective-permute-start.21
  186.5 2.8 %collective-permute-done.17.refs_3_ = bf16[128,512]{1,0:T(8,128)(2,1)S(1)} collective-permute-done((bf16[128,512]{1,0:T(8,128)(2,1)S(1)}, bf16[128,512]{1,0:T(8,128)(2,1)S(1)}, u32[]{:S(2)}, u32[]{:S(2)}) %collective-permute-start.17) | collective-permute-done | bytes 131104 | tf_op jit(solution)/shard_map/ppermute | solution.py:22
  189.3 1.6 collective-permute-start.18
  190.8 3.7 %collective-permute-done.20.refs_0_ = bf16[128,512]{1,0:T(8,128)(2,1)S(1)} collective-permute-done((bf16[128,512]{1,0:T(8,128)(2,1)S(1)}, bf16[128,512]{1,0:T(8,128)(2,1)S(1)}, u32[]{:S(2)}, u32[]{:S(2)}) %collective-permute-start.20) | collective-permute-done | bytes 131104 | tf_op jit(solution)/shard_map/ppermute | solution.py:22
  194.5 2.0 collective-permute-done.21.refs_1_
  196.5 5.8 %collective-permute-start.23 = (bf16[128,512]{1,0:T(8,128)(2,1)S(1)}, bf16[128,512]{1,0:T(8,128)(2,1)S(1)}, u32[]{:S(2)}, u32[]{:S(2)}) collective-permute-start(bf16[128,512]{1,0:T(8,128)(2,1)S(1)} %get-tuple-element.70), channel_id=1, source_target_pairs={{0,7},{1,6},{2,5},{3,4},{4,3},{5,2},{6,1},{7,0},{8,15},{9,14},{10,... | collective-permute-start | bytes 393224 | tf_op jit(solution)/shard_map/ppermute | solution.py:22
  202.3 3.0 %collective-permute-done.23.refs_3_ = bf16[128,512]{1,0:T(8,128)(2,1)S(1)} collective-permute-done((bf16[128,512]{1,0:T(8,128)(2,1)S(1)}, bf16[128,512]{1,0:T(8,128)(2,1)S(1)}, u32[]{:S(2)}, u32[]{:S(2)}) %collective-permute-start.23) | collective-permute-done | bytes 131104 | tf_op jit(solution)/shard_map/ppermute | solution.py:22
  205.4 1.6 collective-permute-start.40
  207.1 4.2 %product_and_squares.6 = (f32[4,512,512]{2,1,0:T(8,128)S(1)}, f32[1,8,128]{2,1,0:T(8,128)S(1)}) custom-call(bf16[512,512]{1,0:T(8,128)(2,1)S(1)} %join_blocks.43.refs_0_, bf16[512,512]{1,0:T(8,128)(2,1)S(1)} %collective-permute-done.44.refs_1_, bf16[1024,512]{1,0:T(8,128)(2,1)S(1)} %collective-permute-done.45.refs_2_, ...), custom_call_target="tpu_custom_call" | custom-call | flops 2147483648 | bytes 8388608 | tf_op jit(solution)/shard_map/product_and_squares/pallas_call | solution.py:161
  211.3 5.6 %collective-permute-done.40.refs_1_.refs_4_ = bf16[512,512]{1,0:T(8,128)(2,1)S(1)} collective-permute-done((bf16[512,512]{1,0:T(8,128)(2,1)S(1)}, bf16[512,512]{1,0:T(8,128)(2,1)S(1)}, u32[]{:S(2)}, u32[]{:S(2)}) %collective-permute-start.40) | collective-permute-done | bytes 524320 | tf_op jit(solution)/shard_map/ppermute | solution.py:22
  217.1 2.6 %collective-permute-done.50.refs_5_ = bf16[1024,512]{1,0:T(8,128)(2,1)S(1)} collective-permute-done((bf16[1024,512]{1,0:T(8,128)(2,1)S(1)}, bf16[1024,512]{1,0:T(8,128)(2,1)S(1)}, u32[]{:S(2)}, u32[]{:S(2)}) %collective-permute-start.50) | collective-permute-done | bytes 1048608 | tf_op jit(solution)/shard_map/ppermute | solution.py:22
  219.8 4.2 %product_and_squares.7 = (f32[4,512,512]{2,1,0:T(8,128)S(1)}, f32[32,8,128]{2,1,0:T(8,128)S(1)}) custom-call(bf16[512,512]{1,0:T(8,128)(2,1)S(1)} %join_blocks.28.refs_0_, bf16[512,512]{1,0:T(8,128)(2,1)S(1)} %collective-permute-done.18.refs_1_, bf16[1024,512]{1,0:T(8,128)(2,1)S(1)} %collective-permute-done.19.refs_2_, ...), custom_call_target="tpu_custom_call" | custom-call | flops 2147483648 | bytes 8388608 | tf_op jit(solution)/shard_map/product_and_squares/pallas_call | solution.py:161
  224.0 15.3 %all_to_all.5.sums_ref = f32[32,8,128]{2,1,0:T(8,128)S(1)} all-to-all(f32[32,8,128]{2,1,0:T(8,128)S(1)} %get-tuple-element.88), channel_id=1, replica_groups=mesh['user'=4,'tok'=8] {'user','tok'}, dimensions={0} | all-to-all | bytes 262144 | tf_op jit(solution)/shard_map/all_to_all | solution.py:306
  239.3 5.2 %weighted_sum.1 = f32[2048,512]{1,0:T(8,128)} custom-call(s32[1]{0:T(128)} %bitcast.user_ref, f32[32,8,128]{2,1,0:T(8,128)S(1)} %all_to_all.5.sums_ref, f32[4,512,512]{2,1,0:T(8,128)S(1)} %get-tuple-element.89.refs_0_, f32[4,512,512]{2,1,0:T(8,128)S(1)} %get-tuple-element.90.refs_1_, f32[4,512,512]{2,1,0:T(8,128)S(1)} %get-tuple-element.91.refs_2_, ...), custom_call_target="tpu_custom_call" | custom-call | tf_op jit(solution)/shard_map/weighted_sum/pallas_call | solution.py:213
  (83 shorter events, 8.6 us)
Async XLA Ops:
  0.7 1.0 copy-start.2
  1.7 5.6 %collective-permute-start = (bf16[128,512]{1,0:T(8,128)(2,1)S(1)}, bf16[128,512]{1,0:T(8,128)(2,1)S(1)}, u32[]{:S(2)}, u32[]{:S(2)}) collective-permute-start(bf16[128,512]{1,0:T(8,128)(2,1)S(1)} %get-tuple-element.50), channel_id=1, source_target_pairs={{0,8},{8,0},{16,24},{24,16},{1,9},{9,1},{17,25},{25,17},{2,10},{10... | collective-permute-start | bytes 393224 | tf_op jit(solution)/shard_map/ppermute | solution.py:22
  2.3 6.9 %collective-permute-start.1 = (bf16[128,512]{1,0:T(8,128)(2,1)S(1)}, bf16[128,512]{1,0:T(8,128)(2,1)S(1)}, u32[]{:S(2)}, u32[]{:S(2)}) collective-permute-start(bf16[128,512]{1,0:T(8,128)(2,1)S(1)} %get-tuple-element.51), channel_id=1, source_target_pairs={{0,16},{8,24},{16,0},{24,8},{1,17},{9,25},{17,1},{25,9},{2,18},{10... | collective-permute-start | bytes 393224 | tf_op jit(solution)/shard_map/ppermute | solution.py:22
  4.8 6.6 %collective-permute-start.2 = (bf16[128,512]{1,0:T(8,128)(2,1)S(1)}, bf16[128,512]{1,0:T(8,128)(2,1)S(1)}, u32[]{:S(2)}, u32[]{:S(2)}) collective-permute-start(bf16[128,512]{1,0:T(8,128)(2,1)S(1)} %get-tuple-element.52), channel_id=1, source_target_pairs={{0,24},{8,16},{16,8},{24,0},{1,25},{9,17},{17,9},{25,1},{2,26},{10... | collective-permute-start | bytes 393224 | tf_op jit(solution)/shard_map/ppermute | solution.py:22
  4.9 2.2 copy-start
  7.3 53.2 %copy-start.1 = (bf16[1,128,16384]{2,1,0:T(8,128)(2,1)S(1)}, bf16[1,128,16384]{2,1,0:T(8,128)(2,1)}, u32[]{:S(2)}) copy-start(bf16[1,128,16384]{2,1,0:T(8,128)(2,1)} %hidden_ref.7) | copy-start | bytes 12582916
  11.6 39.6 %collective-permute-start.30 = (bf16[128,2560]{1,0:T(8,128)(2,1)S(1)}, bf16[128,2560]{1,0:T(8,128)(2,1)S(1)}, u32[]{:S(2)}, u32[]{:S(2)}) collective-permute-start(bf16[128,2560]{1,0:T(8,128)(2,1)S(1)} %join_blocks.33), channel_id=1, source_target_pairs={{0,2},{1,3},{2,0},{3,1},{4,6},{5,7},{6,4},{7,5},{8,10},{9,11},{10,... | collective-permute-start | bytes 1966088 | tf_op jit(solution)/shard_map/ppermute | solution.py:22
  13.3 37.8 %collective-permute-start.29 = (bf16[128,2560]{1,0:T(8,128)(2,1)S(1)}, bf16[128,2560]{1,0:T(8,128)(2,1)S(1)}, u32[]{:S(2)}, u32[]{:S(2)}) collective-permute-start(bf16[128,2560]{1,0:T(8,128)(2,1)S(1)} %join_blocks.32), channel_id=1, source_target_pairs={{0,1},{1,0},{2,3},{3,2},{4,5},{5,4},{6,7},{7,6},{8,9},{9,8},{10,11... | collective-permute-start | bytes 1966088 | tf_op jit(solution)/shard_map/ppermute | solution.py:22
  14.9 44.0 %collective-permute-start.3 = (bf16[128,2560]{1,0:T(8,128)(2,1)S(1)}, bf16[128,2560]{1,0:T(8,128)(2,1)S(1)}, u32[]{:S(2)}, u32[]{:S(2)}) collective-permute-start(bf16[128,2560]{1,0:T(8,128)(2,1)S(1)} %join_blocks.25), channel_id=1, source_target_pairs={{0,4},{1,5},{2,6},{3,7},{4,0},{5,1},{6,2},{7,3},{8,12},{9,13},{10,... | collective-permute-start | bytes 1966088 | tf_op jit(solution)/shard_map/ppermute | solution.py:22
  17.6 30.4 %collective-permute-start.31 = (bf16[128,512]{1,0:T(8,128)(2,1)S(1)}, bf16[128,512]{1,0:T(8,128)(2,1)S(1)}, u32[]{:S(2)}, u32[]{:S(2)}) collective-permute-start(bf16[128,512]{1,0:T(8,128)(2,1)S(1)} %get-tuple-element.78), channel_id=1, source_target_pairs={{0,3},{1,2},{2,1},{3,0},{4,7},{5,6},{6,5},{7,4},{8,11},{9,10},{10,... | collective-permute-start | bytes 393224 | tf_op jit(solution)/shard_map/ppermute | solution.py:22
  18.0 37.3 %collective-permute-start.4 = (bf16[128,512]{1,0:T(8,128)(2,1)S(1)}, bf16[128,512]{1,0:T(8,128)(2,1)S(1)}, u32[]{:S(2)}, u32[]{:S(2)}) collective-permute-start(bf16[128,512]{1,0:T(8,128)(2,1)S(1)} %get-tuple-element.54), channel_id=1, source_target_pairs={{0,5},{1,4},{2,7},{3,6},{4,1},{5,0},{6,3},{7,2},{8,13},{9,12},{10,... | collective-permute-start | bytes 393224 | tf_op jit(solution)/shard_map/ppermute | solution.py:22
  48.0 7.6 %collective-permute-start.7 = (bf16[128,512]{1,0:T(8,128)(2,1)S(1)}, bf16[128,512]{1,0:T(8,128)(2,1)S(1)}, u32[]{:S(2)}, u32[]{:S(2)}) collective-permute-start(bf16[128,512]{1,0:T(8,128)(2,1)S(1)} %get-tuple-element.57), channel_id=1, source_target_pairs={{0,6},{1,7},{2,4},{3,5},{4,2},{5,3},{6,0},{7,1},{8,14},{9,15},{10,... | collective-permute-start | bytes 393224 | tf_op jit(solution)/shard_map/ppermute | solution.py:22
  51.1 7.8 %collective-permute-start.8 = (bf16[128,512]{1,0:T(8,128)(2,1)S(1)}, bf16[128,512]{1,0:T(8,128)(2,1)S(1)}, u32[]{:S(2)}, u32[]{:S(2)}) collective-permute-start(bf16[128,512]{1,0:T(8,128)(2,1)S(1)} %get-tuple-element.58), channel_id=1, source_target_pairs={{0,7},{1,6},{2,5},{3,4},{4,3},{5,2},{6,1},{7,0},{8,15},{9,14},{10,... | collective-permute-start | bytes 393224 | tf_op jit(solution)/shard_map/ppermute | solution.py:22
  51.2 23.3 %collective-permute-start.32 = (bf16[512,512]{1,0:T(8,128)(2,1)S(1)}, bf16[512,512]{1,0:T(8,128)(2,1)S(1)}, u32[]{:S(2)}, u32[]{:S(2)}) collective-permute-start(bf16[512,512]{1,0:T(8,128)(2,1)S(1)} %join_blocks.34.refs_0_), channel_id=1, source_target_pairs={{0,16},{8,24},{16,0},{24,8},{1,17},{9,25},{17,1},{25,9},{2,18},{10... | collective-permute-start | bytes 1572872 | tf_op jit(solution)/shard_map/ppermute | solution.py:22
  59.0 16.3 %collective-permute-start.9 = (bf16[512,512]{1,0:T(8,128)(2,1)S(1)}, bf16[512,512]{1,0:T(8,128)(2,1)S(1)}, u32[]{:S(2)}, u32[]{:S(2)}) collective-permute-start(bf16[512,512]{1,0:T(8,128)(2,1)S(1)} %join_blocks.26.refs_0_.refs_3_), channel_id=1, source_target_pairs={{0,16},{8,24},{16,0},{24,8},{1,17},{9,25},{17,1},{25,9},{2,18},{10... | collective-permute-start | bytes 1572872 | tf_op jit(solution)/shard_map/ppermute | solution.py:22
  60.8 12.5 %collective-permute-start.5 = (bf16[128,512]{1,0:T(8,128)(2,1)S(1)}, bf16[128,512]{1,0:T(8,128)(2,1)S(1)}, u32[]{:S(2)}, u32[]{:S(2)}) collective-permute-start(bf16[128,512]{1,0:T(8,128)(2,1)S(1)} %get-tuple-element.55), channel_id=1, source_target_pairs={{0,4},{1,5},{2,6},{3,7},{4,0},{5,1},{6,2},{7,3},{8,12},{9,13},{10,... | collective-permute-start | bytes 393224 | tf_op jit(solution)/shard_map/ppermute | solution.py:22
  66.8 30.8 %collective-permute-start.37 = (bf16[128,2048]{1,0:T(8,128)(2,1)S(1)}, bf16[128,2048]{1,0:T(8,128)(2,1)S(1)}, u32[]{:S(2)}, u32[]{:S(2)}) collective-permute-start(bf16[128,2048]{1,0:T(8,128)(2,1)S(1)} %join_blocks.38), channel_id=1, source_target_pairs={{0,2},{1,3},{2,0},{3,1},{4,6},{5,7},{6,4},{7,5},{8,10},{9,11},{10,... | collective-permute-start | bytes 1572872 | tf_op jit(solution)/shard_map/ppermute | solution.py:22
  66.9 17.8 %collective-permute-start.6 = (bf16[128,512]{1,0:T(8,128)(2,1)S(1)}, bf16[128,512]{1,0:T(8,128)(2,1)S(1)}, u32[]{:S(2)}, u32[]{:S(2)}) collective-permute-start(bf16[128,512]{1,0:T(8,128)(2,1)S(1)} %get-tuple-element.56), channel_id=1, source_target_pairs={{0,5},{1,4},{2,7},{3,6},{4,1},{5,0},{6,3},{7,2},{8,13},{9,12},{10,... | collective-permute-start | bytes 393224 | tf_op jit(solution)/shard_map/ppermute | solution.py:22
  73.3 12.9 %collective-permute-start.24 = (bf16[128,512]{1,0:T(8,128)(2,1)S(1)}, bf16[128,512]{1,0:T(8,128)(2,1)S(1)}, u32[]{:S(2)}, u32[]{:S(2)}) collective-permute-start(bf16[128,512]{1,0:T(8,128)(2,1)S(1)} %get-tuple-element.72), channel_id=1, source_target_pairs={{0,1},{1,0},{2,3},{3,2},{4,5},{5,4},{6,7},{7,6},{8,9},{9,8},{10,11... | collective-permute-start | bytes 393224 | tf_op jit(solution)/shard_map/ppermute | solution.py:22
  74.5 12.9 %collective-permute-start.25 = (bf16[128,512]{1,0:T(8,128)(2,1)S(1)}, bf16[128,512]{1,0:T(8,128)(2,1)S(1)}, u32[]{:S(2)}, u32[]{:S(2)}) collective-permute-start(bf16[128,512]{1,0:T(8,128)(2,1)S(1)} %get-tuple-element.73), channel_id=1, source_target_pairs={{0,2},{1,3},{2,0},{3,1},{4,6},{5,7},{6,4},{7,5},{8,10},{9,11},{10,... | collective-permute-start | bytes 393224 | tf_op jit(solution)/shard_map/ppermute | solution.py:22
  75.3 14.9 %collective-permute-start.26 = (bf16[128,512]{1,0:T(8,128)(2,1)S(1)}, bf16[128,512]{1,0:T(8,128)(2,1)S(1)}, u32[]{:S(2)}, u32[]{:S(2)}) collective-permute-start(bf16[128,512]{1,0:T(8,128)(2,1)S(1)} %get-tuple-element.74), channel_id=1, source_target_pairs={{0,3},{1,2},{2,1},{3,0},{4,7},{5,6},{6,5},{7,4},{8,11},{9,10},{10,... | collective-permute-start | bytes 393224 | tf_op jit(solution)/shard_map/ppermute | solution.py:22
  84.7 20.9 %collective-permute-start.35 = (bf16[128,2048]{1,0:T(8,128)(2,1)S(1)}, bf16[128,2048]{1,0:T(8,128)(2,1)S(1)}, u32[]{:S(2)}, u32[]{:S(2)}) collective-permute-start(bf16[128,2048]{1,0:T(8,128)(2,1)S(1)} %join_blocks.37), channel_id=1, source_target_pairs={{0,1},{1,0},{2,3},{3,2},{4,5},{5,4},{6,7},{7,6},{8,9},{9,8},{10,11... | collective-permute-start | bytes 1572872 | tf_op jit(solution)/shard_map/ppermute | solution.py:22
  86.2 41.8 %collective-permute-start.33 = (bf16[1024,512]{1,0:T(8,128)(2,1)S(1)}, bf16[1024,512]{1,0:T(8,128)(2,1)S(1)}, u32[]{:S(2)}, u32[]{:S(2)}) collective-permute-start(bf16[1024,512]{1,0:T(8,128)(2,1)S(1)} %join_blocks.35), channel_id=1, source_target_pairs={{0,8},{8,0},{16,24},{24,16},{1,9},{9,1},{17,25},{25,17},{2,10},{10... | collective-permute-start | bytes 3145736 | tf_op jit(solution)/shard_map/ppermute | solution.py:22
  87.4 40.6 %collective-permute-start.34 = (bf16[1024,512]{1,0:T(8,128)(2,1)S(1)}, bf16[1024,512]{1,0:T(8,128)(2,1)S(1)}, u32[]{:S(2)}, u32[]{:S(2)}) collective-permute-start(bf16[1024,512]{1,0:T(8,128)(2,1)S(1)} %join_blocks.36), channel_id=1, source_target_pairs={{0,8},{8,0},{16,24},{24,16},{1,9},{9,1},{17,25},{25,17},{2,10},{10... | collective-permute-start | bytes 3145736 | tf_op jit(solution)/shard_map/ppermute | solution.py:22
  90.2 6.9 %collective-permute-start.12 = (bf16[128,512]{1,0:T(8,128)(2,1)S(1)}, bf16[128,512]{1,0:T(8,128)(2,1)S(1)}, u32[]{:S(2)}, u32[]{:S(2)}) collective-permute-start(bf16[128,512]{1,0:T(8,128)(2,1)S(1)} %get-tuple-element.61), channel_id=1, source_target_pairs={{0,6},{1,7},{2,4},{3,5},{4,2},{5,3},{6,0},{7,1},{8,14},{9,15},{10,... | collective-permute-start | bytes 393224 | tf_op jit(solution)/shard_map/ppermute | solution.py:22
  97.0 12.1 %collective-permute-start.27 = (bf16[512,512]{1,0:T(8,128)(2,1)S(1)}, bf16[512,512]{1,0:T(8,128)(2,1)S(1)}, u32[]{:S(2)}, u32[]{:S(2)}) collective-permute-start(bf16[512,512]{1,0:T(8,128)(2,1)S(1)} %join_blocks.30.refs_0_), channel_id=1, source_target_pairs={{0,16},{8,24},{16,0},{24,8},{1,17},{9,25},{17,1},{25,9},{2,18},{10... | collective-permute-start | bytes 1572872 | tf_op jit(solution)/shard_map/ppermute | solution.py:22
  97.6 7.9 %collective-permute-start.13 = (bf16[128,512]{1,0:T(8,128)(2,1)S(1)}, bf16[128,512]{1,0:T(8,128)(2,1)S(1)}, u32[]{:S(2)}, u32[]{:S(2)}) collective-permute-start(bf16[128,512]{1,0:T(8,128)(2,1)S(1)} %get-tuple-element.62), channel_id=1, source_target_pairs={{0,7},{1,6},{2,5},{3,4},{4,3},{5,2},{6,1},{7,0},{8,15},{9,14},{10,... | collective-permute-start | bytes 393224 | tf_op jit(solution)/shard_map/ppermute | solution.py:22
  105.5 14.9 %collective-permute-start.36 = (bf16[128,2048]{1,0:T(8,128)(2,1)S(1)}, bf16[128,2048]{1,0:T(8,128)(2,1)S(1)}, u32[]{:S(2)}, u32[]{:S(2)}) collective-permute-start(bf16[128,2048]{1,0:T(8,128)(2,1)S(1)} %join_blocks.38), channel_id=1, source_target_pairs={{0,1},{1,0},{2,3},{3,2},{4,5},{5,4},{6,7},{7,6},{8,9},{9,8},{10,11... | collective-permute-start | bytes 1572872 | tf_op jit(solution)/shard_map/ppermute | solution.py:22
  105.6 22.2 %collective-permute-start.38 = (bf16[128,2048]{1,0:T(8,128)(2,1)S(1)}, bf16[128,2048]{1,0:T(8,128)(2,1)S(1)}, u32[]{:S(2)}, u32[]{:S(2)}) collective-permute-start(bf16[128,2048]{1,0:T(8,128)(2,1)S(1)} %join_blocks.39), channel_id=1, source_target_pairs={{0,1},{1,0},{2,3},{3,2},{4,5},{5,4},{6,7},{7,6},{8,9},{9,8},{10,11... | collective-permute-start | bytes 1572872 | tf_op jit(solution)/shard_map/ppermute | solution.py:22
  109.1 23.1 %collective-permute-start.14 = (bf16[512,512]{1,0:T(8,128)(2,1)S(1)}, bf16[512,512]{1,0:T(8,128)(2,1)S(1)}, u32[]{:S(2)}, u32[]{:S(2)}) collective-permute-start(bf16[512,512]{1,0:T(8,128)(2,1)S(1)} %join_blocks.27.refs_0_.refs_3_), channel_id=1, source_target_pairs={{0,16},{8,24},{16,0},{24,8},{1,17},{9,25},{17,1},{25,9},{2,18},{10... | collective-permute-start | bytes 1572872 | tf_op jit(solution)/shard_map/ppermute | solution.py:22
  120.3 44.6 %collective-permute-start.28 = (bf16[1024,512]{1,0:T(8,128)(2,1)S(1)}, bf16[1024,512]{1,0:T(8,128)(2,1)S(1)}, u32[]{:S(2)}, u32[]{:S(2)}) collective-permute-start(bf16[1024,512]{1,0:T(8,128)(2,1)S(1)} %join_blocks.31), channel_id=1, source_target_pairs={{0,8},{8,0},{16,24},{24,16},{1,9},{9,1},{17,25},{25,17},{2,10},{10... | collective-permute-start | bytes 3145736 | tf_op jit(solution)/shard_map/ppermute | solution.py:22
  132.3 32.6 %collective-permute-start.39 = (bf16[1024,512]{1,0:T(8,128)(2,1)S(1)}, bf16[1024,512]{1,0:T(8,128)(2,1)S(1)}, u32[]{:S(2)}, u32[]{:S(2)}) collective-permute-start(bf16[1024,512]{1,0:T(8,128)(2,1)S(1)} %join_blocks.41), channel_id=1, source_target_pairs={{0,8},{8,0},{16,24},{24,16},{1,9},{9,1},{17,25},{25,17},{2,10},{10... | collective-permute-start | bytes 3145736 | tf_op jit(solution)/shard_map/ppermute | solution.py:22
  132.7 5.9 %collective-permute-start.41 = (bf16[128,512]{1,0:T(8,128)(2,1)S(1)}, bf16[128,512]{1,0:T(8,128)(2,1)S(1)}, u32[]{:S(2)}, u32[]{:S(2)}) collective-permute-start(bf16[128,512]{1,0:T(8,128)(2,1)S(1)} %get-tuple-element.82), channel_id=1, source_target_pairs={{0,1},{1,0},{2,3},{3,2},{4,5},{5,4},{6,7},{7,6},{8,9},{9,8},{10,11... | collective-permute-start | bytes 393224 | tf_op jit(solution)/shard_map/ppermute | solution.py:22
  133.0 6.6 %collective-permute-start.42 = (bf16[128,512]{1,0:T(8,128)(2,1)S(1)}, bf16[128,512]{1,0:T(8,128)(2,1)S(1)}, u32[]{:S(2)}, u32[]{:S(2)}) collective-permute-start(bf16[128,512]{1,0:T(8,128)(2,1)S(1)} %get-tuple-element.83), channel_id=1, source_target_pairs={{0,2},{1,3},{2,0},{3,1},{4,6},{5,7},{6,4},{7,5},{8,10},{9,11},{10,... | collective-permute-start | bytes 393224 | tf_op jit(solution)/shard_map/ppermute | solution.py:22
  134.6 9.5 %collective-permute-start.43 = (bf16[128,512]{1,0:T(8,128)(2,1)S(1)}, bf16[128,512]{1,0:T(8,128)(2,1)S(1)}, u32[]{:S(2)}, u32[]{:S(2)}) collective-permute-start(bf16[128,512]{1,0:T(8,128)(2,1)S(1)} %get-tuple-element.84), channel_id=1, source_target_pairs={{0,3},{1,2},{2,1},{3,0},{4,7},{5,6},{6,5},{7,4},{8,11},{9,10},{10,... | collective-permute-start | bytes 393224 | tf_op jit(solution)/shard_map/ppermute | solution.py:22
  138.6 12.6 %collective-permute-start.10 = (bf16[128,512]{1,0:T(8,128)(2,1)S(1)}, bf16[128,512]{1,0:T(8,128)(2,1)S(1)}, u32[]{:S(2)}, u32[]{:S(2)}) collective-permute-start(bf16[128,512]{1,0:T(8,128)(2,1)S(1)} %get-tuple-element.59), channel_id=1, source_target_pairs={{0,4},{1,5},{2,6},{3,7},{4,0},{5,1},{6,2},{7,3},{8,12},{9,13},{10,... | collective-permute-start | bytes 393224 | tf_op jit(solution)/shard_map/ppermute | solution.py:22
  139.6 15.8 %collective-permute-start.11 = (bf16[128,512]{1,0:T(8,128)(2,1)S(1)}, bf16[128,512]{1,0:T(8,128)(2,1)S(1)}, u32[]{:S(2)}, u32[]{:S(2)}) collective-permute-start(bf16[128,512]{1,0:T(8,128)(2,1)S(1)} %get-tuple-element.60), channel_id=1, source_target_pairs={{0,5},{1,4},{2,7},{3,6},{4,1},{5,0},{6,3},{7,2},{8,13},{9,12},{10,... | collective-permute-start | bytes 393224 | tf_op jit(solution)/shard_map/ppermute | solution.py:22
  144.2 20.6 %collective-permute-start.44 = (bf16[512,512]{1,0:T(8,128)(2,1)S(1)}, bf16[512,512]{1,0:T(8,128)(2,1)S(1)}, u32[]{:S(2)}, u32[]{:S(2)}) collective-permute-start(bf16[512,512]{1,0:T(8,128)(2,1)S(1)} %join_blocks.43.refs_0_), channel_id=1, source_target_pairs={{0,16},{8,24},{16,0},{24,8},{1,17},{9,25},{17,1},{25,9},{2,18},{10... | collective-permute-start | bytes 1572872 | tf_op jit(solution)/shard_map/ppermute | solution.py:22
  151.2 7.4 %collective-permute-start.46 = (bf16[128,512]{1,0:T(8,128)(2,1)S(1)}, bf16[128,512]{1,0:T(8,128)(2,1)S(1)}, u32[]{:S(2)}, u32[]{:S(2)}) collective-permute-start(bf16[128,512]{1,0:T(8,128)(2,1)S(1)} %get-tuple-element.85), channel_id=1, source_target_pairs={{0,6},{1,7},{2,4},{3,5},{4,2},{5,3},{6,0},{7,1},{8,14},{9,15},{10,... | collective-permute-start | bytes 393224 | tf_op jit(solution)/shard_map/ppermute | solution.py:22
  155.4 7.8 %collective-permute-start.47 = (bf16[128,512]{1,0:T(8,128)(2,1)S(1)}, bf16[128,512]{1,0:T(8,128)(2,1)S(1)}, u32[]{:S(2)}, u32[]{:S(2)}) collective-permute-start(bf16[128,512]{1,0:T(8,128)(2,1)S(1)} %get-tuple-element.86), channel_id=1, source_target_pairs={{0,7},{1,6},{2,5},{3,4},{4,3},{5,2},{6,1},{7,0},{8,15},{9,14},{10,... | collective-permute-start | bytes 393224 | tf_op jit(solution)/shard_map/ppermute | solution.py:22
  163.2 10.0 %collective-permute-start.48 = (bf16[512,512]{1,0:T(8,128)(2,1)S(1)}, bf16[512,512]{1,0:T(8,128)(2,1)S(1)}, u32[]{:S(2)}, u32[]{:S(2)}) collective-permute-start(bf16[512,512]{1,0:T(8,128)(2,1)S(1)} %join_blocks.45.refs_0_.refs_3_), channel_id=1, source_target_pairs={{0,16},{8,24},{16,0},{24,8},{1,17},{9,25},{17,1},{25,9},{2,18},{10... | collective-permute-start | bytes 1572872 | tf_op jit(solution)/shard_map/ppermute | solution.py:22
  164.8 42.3 %collective-permute-start.45 = (bf16[1024,512]{1,0:T(8,128)(2,1)S(1)}, bf16[1024,512]{1,0:T(8,128)(2,1)S(1)}, u32[]{:S(2)}, u32[]{:S(2)}) collective-permute-start(bf16[1024,512]{1,0:T(8,128)(2,1)S(1)} %join_blocks.44), channel_id=1, source_target_pairs={{0,8},{8,0},{16,24},{24,16},{1,9},{9,1},{17,25},{25,17},{2,10},{10... | collective-permute-start | bytes 3145736 | tf_op jit(solution)/shard_map/ppermute | solution.py:22
  173.3 33.8 %collective-permute-start.49 = (bf16[1024,512]{1,0:T(8,128)(2,1)S(1)}, bf16[1024,512]{1,0:T(8,128)(2,1)S(1)}, u32[]{:S(2)}, u32[]{:S(2)}) collective-permute-start(bf16[1024,512]{1,0:T(8,128)(2,1)S(1)} %join_blocks.46), channel_id=1, source_target_pairs={{0,8},{8,0},{16,24},{24,16},{1,9},{9,1},{17,25},{25,17},{2,10},{10... | collective-permute-start | bytes 3145736 | tf_op jit(solution)/shard_map/ppermute | solution.py:22
  173.6 6.3 %collective-permute-start.15 = (bf16[128,512]{1,0:T(8,128)(2,1)S(1)}, bf16[128,512]{1,0:T(8,128)(2,1)S(1)}, u32[]{:S(2)}, u32[]{:S(2)}) collective-permute-start(bf16[128,512]{1,0:T(8,128)(2,1)S(1)} %get-tuple-element.64), channel_id=1, source_target_pairs={{0,1},{1,0},{2,3},{3,2},{4,5},{5,4},{6,7},{7,6},{8,9},{9,8},{10,11... | collective-permute-start | bytes 393224 | tf_op jit(solution)/shard_map/ppermute | solution.py:22
  175.2 9.4 %collective-permute-start.16 = (bf16[128,512]{1,0:T(8,128)(2,1)S(1)}, bf16[128,512]{1,0:T(8,128)(2,1)S(1)}, u32[]{:S(2)}, u32[]{:S(2)}) collective-permute-start(bf16[128,512]{1,0:T(8,128)(2,1)S(1)} %get-tuple-element.65), channel_id=1, source_target_pairs={{0,2},{1,3},{2,0},{3,1},{4,6},{5,7},{6,4},{7,5},{8,10},{9,11},{10,... | collective-permute-start | bytes 393224 | tf_op jit(solution)/shard_map/ppermute | solution.py:22
  179.9 9.4 %collective-permute-start.17 = (bf16[128,512]{1,0:T(8,128)(2,1)S(1)}, bf16[128,512]{1,0:T(8,128)(2,1)S(1)}, u32[]{:S(2)}, u32[]{:S(2)}) collective-permute-start(bf16[128,512]{1,0:T(8,128)(2,1)S(1)} %get-tuple-element.66), channel_id=1, source_target_pairs={{0,3},{1,2},{2,1},{3,0},{4,7},{5,6},{6,5},{7,4},{8,11},{9,10},{10,... | collective-permute-start | bytes 393224 | tf_op jit(solution)/shard_map/ppermute | solution.py:22
  179.9 14.6 %collective-permute-start.20 = (bf16[128,512]{1,0:T(8,128)(2,1)S(1)}, bf16[128,512]{1,0:T(8,128)(2,1)S(1)}, u32[]{:S(2)}, u32[]{:S(2)}) collective-permute-start(bf16[128,512]{1,0:T(8,128)(2,1)S(1)} %get-tuple-element.67), channel_id=1, source_target_pairs={{0,4},{1,5},{2,6},{3,7},{4,0},{5,1},{6,2},{7,3},{8,12},{9,13},{10,... | collective-permute-start | bytes 393224 | tf_op jit(solution)/shard_map/ppermute | solution.py:22
  184.6 11.9 %collective-permute-start.21 = (bf16[128,512]{1,0:T(8,128)(2,1)S(1)}, bf16[128,512]{1,0:T(8,128)(2,1)S(1)}, u32[]{:S(2)}, u32[]{:S(2)}) collective-permute-start(bf16[128,512]{1,0:T(8,128)(2,1)S(1)} %get-tuple-element.68), channel_id=1, source_target_pairs={{0,5},{1,4},{2,7},{3,6},{4,1},{5,0},{6,3},{7,2},{8,13},{9,12},{10,... | collective-permute-start | bytes 393224 | tf_op jit(solution)/shard_map/ppermute | solution.py:22
  189.3 17.7 %collective-permute-start.18 = (bf16[512,512]{1,0:T(8,128)(2,1)S(1)}, bf16[512,512]{1,0:T(8,128)(2,1)S(1)}, u32[]{:S(2)}, u32[]{:S(2)}) collective-permute-start(bf16[512,512]{1,0:T(8,128)(2,1)S(1)} %join_blocks.28.refs_0_), channel_id=1, source_target_pairs={{0,16},{8,24},{16,0},{24,8},{1,17},{9,25},{17,1},{25,9},{2,18},{10... | collective-permute-start | bytes 1572872 | tf_op jit(solution)/shard_map/ppermute | solution.py:22
  194.5 7.8 %collective-permute-start.22 = (bf16[128,512]{1,0:T(8,128)(2,1)S(1)}, bf16[128,512]{1,0:T(8,128)(2,1)S(1)}, u32[]{:S(2)}, u32[]{:S(2)}) collective-permute-start(bf16[128,512]{1,0:T(8,128)(2,1)S(1)} %get-tuple-element.69), channel_id=1, source_target_pairs={{0,6},{1,7},{2,4},{3,5},{4,2},{5,3},{6,0},{7,1},{8,14},{9,15},{10,... | collective-permute-start | bytes 393224 | tf_op jit(solution)/shard_map/ppermute | solution.py:22
  196.5 8.9 %collective-permute-start.23 = (bf16[128,512]{1,0:T(8,128)(2,1)S(1)}, bf16[128,512]{1,0:T(8,128)(2,1)S(1)}, u32[]{:S(2)}, u32[]{:S(2)}) collective-permute-start(bf16[128,512]{1,0:T(8,128)(2,1)S(1)} %get-tuple-element.70), channel_id=1, source_target_pairs={{0,7},{1,6},{2,5},{3,4},{4,3},{5,2},{6,1},{7,0},{8,15},{9,14},{10,... | collective-permute-start | bytes 393224 | tf_op jit(solution)/shard_map/ppermute | solution.py:22
  205.4 11.6 %collective-permute-start.40 = (bf16[512,512]{1,0:T(8,128)(2,1)S(1)}, bf16[512,512]{1,0:T(8,128)(2,1)S(1)}, u32[]{:S(2)}, u32[]{:S(2)}) collective-permute-start(bf16[512,512]{1,0:T(8,128)(2,1)S(1)} %join_blocks.42.refs_0_.refs_3_), channel_id=1, source_target_pairs={{0,16},{8,24},{16,0},{24,8},{1,17},{9,25},{17,1},{25,9},{2,18},{10... | collective-permute-start | bytes 1572872 | tf_op jit(solution)/shard_map/ppermute | solution.py:22
  207.0 10.1 %collective-permute-start.19 = (bf16[1024,512]{1,0:T(8,128)(2,1)S(1)}, bf16[1024,512]{1,0:T(8,128)(2,1)S(1)}, u32[]{:S(2)}, u32[]{:S(2)}) collective-permute-start(bf16[1024,512]{1,0:T(8,128)(2,1)S(1)} %join_blocks.29), channel_id=1, source_target_pairs={{0,8},{8,0},{16,24},{24,16},{1,9},{9,1},{17,25},{25,17},{2,10},{10... | collective-permute-start | bytes 3145736 | tf_op jit(solution)/shard_map/ppermute | solution.py:22
  217.0 2.7 %collective-permute-start.50 = (bf16[1024,512]{1,0:T(8,128)(2,1)S(1)}, bf16[1024,512]{1,0:T(8,128)(2,1)S(1)}, u32[]{:S(2)}, u32[]{:S(2)}) collective-permute-start(bf16[1024,512]{1,0:T(8,128)(2,1)S(1)} %join_blocks.47), channel_id=1, source_target_pairs={{0,8},{8,0},{16,24},{24,16},{1,9},{9,1},{17,25},{25,17},{2,10},{10... | collective-permute-start | bytes 3145736 | tf_op jit(solution)/shard_map/ppermute | solution.py:22

commit v5 on v3

v5 whole, which is shorter than its diff:
```python
import functools
import math

import jax
import jax.numpy as jnp
from jax import lax
from jax.experimental import pallas as pl
from jax.experimental.pallas import tpu as pltpu
from jax.sharding import PartitionSpec as P

epsilon = 1e-06
lanes = 128
first_part = 0.5
ANY = pl.BlockSpec(memory_space=pl.ANY)
SMEM = pl.BlockSpec(memory_space=pltpu.SMEM)
VMEM = pl.BlockSpec(memory_space=pltpu.VMEM)
HBM = pl.BlockSpec(memory_space=pltpu.HBM)


def exchange(block, axis, distance):
    size = lax.axis_size(axis)
    return lax.ppermute(block, axis, [(i, i ^ distance) for i in range(size)])


def pack_kernel(distances, tok_ref, hidden_ref, *refs):
    out_refs, sems = refs[-1 - len(distances) : -1], refs[-1]
    width = out_refs[0].shape[1]
    copies = []
    for at, distance in enumerate(distances):
        start = pl.multiple_of((tok_ref[0] ^ distance) * width, lanes)
        copies.append(
            pltpu.make_async_copy(
                hidden_ref.at[0, :, pl.ds(start, width)], out_refs[at], sems.at[at]
            )
        )
    for copy in copies:
        copy.start()
    for copy in copies:
        copy.wait()


def pack(tok, hidden, distances, width, after):
    rows = hidden.shape[1]
    count = len(distances)
    return pl.pallas_call(
        functools.partial(pack_kernel, distances),
        out_shape=[jax.ShapeDtypeStruct((rows, width), hidden.dtype)] * count,
        in_specs=[SMEM, HBM] + [ANY] * len(after),
        out_specs=[VMEM] * count,
        scratch_shapes=[pltpu.SemaphoreType.DMA((count,))],
        compiler_params=pltpu.CompilerParams(vmem_limit_bytes=2**20),
        cost_estimate=pl.CostEstimate(
            flops=0, bytes_accessed=4 * count * rows * width, transcendentals=0
        ),
        name="pack_columns",
    )(tok, hidden, *after)


def join_kernel(parts, *refs):
    out_ref = refs[-1]
    to = 0
    for ref, (start, width) in zip(refs, parts):
        out_ref[:, to : to + width] = ref[:, start : start + width]
        to += width


def join(parts, after):
    arrays = [array for array, _, _ in parts]
    rows = arrays[0].shape[0]
    total = sum(width for _, _, width in parts)
    return pl.pallas_call(
        functools.partial(join_kernel, [part[1:] for part in parts]),
        out_shape=jax.ShapeDtypeStruct((rows, total), arrays[0].dtype),
        in_specs=[VMEM] * len(arrays) + [ANY] * len(after),
        out_specs=VMEM,
        compiler_params=pltpu.CompilerParams(vmem_limit_bytes=2**20),
        cost_estimate=pl.CostEstimate(flops=0, bytes_accessed=4 * rows * total, transcendentals=0),
        name="join_columns",
    )(*arrays, *after)


def mask_kernel(valid_ref, user_ref, cot_ref, *out_refs):
    rows, width = out_refs[0].shape
    keep = lax.broadcasted_iota(jnp.int32, (rows, width), 0) < valid_ref[0]
    for slot, out_ref in enumerate(out_refs):
        column = pl.multiple_of((user_ref[0] ^ slot) * width, lanes)
        block = cot_ref[0, :, pl.ds(column, width)]
        out_ref[...] = jnp.where(keep, block, jnp.zeros_like(block))


def mask(valid, user, cotangent, user_count):
    _, rows, total = cotangent.shape
    return pl.pallas_call(
        mask_kernel,
        out_shape=[jax.ShapeDtypeStruct((rows, total // user_count), cotangent.dtype)] * user_count,
        in_specs=[SMEM, SMEM, VMEM],
        out_specs=[VMEM] * user_count,
        compiler_params=pltpu.CompilerParams(vmem_limit_bytes=2 * 2**20),
        name="mask_cotangent",
    )(valid, user, cotangent)


def product_kernel(lefts, rights, tile, has_held, has_sums, copies, *refs):
    outs = refs[-2:] if copies else refs[-1:]
    inputs = list(refs[: -len(outs)])
    sums_in = inputs.pop() if has_sums else None
    held_ref = inputs.pop() if has_held else None
    product_ref = outs[0]
    user_count, width, columns = product_ref.shape
    squares = []
    for slot in range(user_count):
        right = jnp.concatenate(
            [refs[at][:, start : start + columns] for at, start in rights[slot]], axis=0
        )

        def step(i, total, slot=slot, right=right):
            rows = pl.ds(pl.multiple_of(i * tile, tile), tile)
            left = jnp.concatenate(
                [
                    refs[at][:, pl.ds(pl.multiple_of(start + i * tile, lanes), tile)]
                    for at, start in lefts[slot]
                ],
                axis=0,
            )
            value = lax.dot_general(
                left, right, (((0,), (0,)), ((), ())), preferred_element_type=jnp.float32
            )
            if has_held:
                value += held_ref[slot, rows, :]
            product_ref[slot, rows, :] = value
            if copies:
                row = jnp.sum(value * value, axis=0, keepdims=True)
                for start in range(0, columns, lanes):
                    total += row[:, start : start + lanes]
            return total

        squares.append(lax.fori_loop(0, width // tile, step, jnp.zeros((1, lanes), jnp.float32)))
    if copies:
        rows = jnp.concatenate(squares + [jnp.zeros((8 - user_count, lanes), jnp.float32)], axis=0)
        if has_sums:
            rows += sums_in[0]
        outs[1][...] = jnp.broadcast_to(rows[None], outs[1].shape)


def product(lefts, rights, width, columns, held=None, sums=None, copies=0):
    operands, at = [], {}

    def place(part):
        array, start = part
        if id(array) not in at:
            at[id(array)] = len(operands)
            operands.append(array)
        return at[id(array)], start

    user_count, sources = len(lefts), len(lefts[0])
    left_places = [[place(part) for part in slot] for slot in lefts]
    right_places = [[place(part) for part in slot] for slot in rights]
    tokens = sources * lefts[0][0][0].shape[0]
    aliases = {}
    if held is not None:
        aliases = {len(operands): 0}
        operands.append(held)
    if sums is not None:
        operands.append(sums)
    out_shape = [jax.ShapeDtypeStruct((user_count, width, columns), jnp.float32)]
    if copies:
        out_shape.append(jax.ShapeDtypeStruct((copies, 8, lanes), jnp.float32))
    tile = math.gcd(width, 2 * lanes)
    return pl.pallas_call(
        functools.partial(
            product_kernel, left_places, right_places, tile, held is not None, sums is not None, copies
        ),
        out_shape=out_shape,
        in_specs=[VMEM] * len(operands),
        out_specs=[VMEM] * len(out_shape),
        input_output_aliases=aliases,
        compiler_params=pltpu.CompilerParams(vmem_limit_bytes=8 * 2**20),
        cost_estimate=pl.CostEstimate(
            flops=2 * user_count * tokens * columns * width,
            bytes_accessed=2 * user_count * tokens * (width + columns),
            transcendentals=0,
        ),
        name="product_and_squares",
    )(*operands)


def combine_kernel(user_count, clip_bound, scaling, starts, user_ref, sums_ref, *refs):
    out_ref, factor_ref = refs[-2:]

    @pl.when(pl.program_id(0) == 0)
    def _():
        per_user = sums_ref.shape[0] // user_count
        by_source = [
            jnp.sum(sums_ref[j * per_user : (j + 1) * per_user], axis=0) for j in range(user_count)
        ]
        factors = []
        for u in range(user_count):
            row = sum(by_source[j][j ^ u : (j ^ u) + 1, :] for j in range(user_count))
            norm_sq = jnp.sum(row, axis=1, keepdims=True)
            factors.append(jnp.minimum(1.0, clip_bound / jnp.sqrt(norm_sq + epsilon)) * scaling)
        for slot in range(user_count):
            user = user_ref[0] ^ slot
            factor = sum(jnp.where(user == u, factors[u], 0.0) for u in range(user_count))
            factor_ref[slot : slot + 1, :] = jnp.broadcast_to(factor, (1, lanes))

    by_slot = [factor_ref[slot : slot + 1, 0:1] for slot in range(user_count)]
    tile = out_ref.shape[0]
    row = pl.program_id(0) * tile
    for ref, start in zip(refs, starts):

        @pl.when((row >= start) & (row < start + ref.shape[1]))
        def _(ref=ref, start=start):
            at = pl.ds(pl.multiple_of(row - start, tile), tile)
            result = by_slot[0] * ref[0, at, :]
            for slot in range(1, user_count):
                result += by_slot[slot] * ref[slot, at, :]
            out_ref[...] = result


def combine(user, sums, gradients, clip_bound, scaling):
    user_count, _, columns = gradients[0].shape
    heights = [gradient.shape[1] for gradient in gradients]
    starts = [sum(heights[:i]) for i in range(len(heights))]
    rows = sum(heights)
    tile = math.gcd(256, *heights)
    return pl.pallas_call(
        functools.partial(combine_kernel, user_count, clip_bound, scaling, starts),
        grid=(rows // tile,),
        out_shape=jax.ShapeDtypeStruct((rows, columns), jnp.float32),
        in_specs=[SMEM] + [VMEM] * (1 + len(gradients)),
        out_specs=pl.BlockSpec((tile, columns), lambda i: (i, 0)),
        scratch_shapes=[pltpu.VMEM((8, lanes), jnp.float32)],
        compiler_params=pltpu.CompilerParams(vmem_limit_bytes=8 * 2**20),
        name="weighted_sum",
    )(user, sums, *gradients)


def body(hidden, cotangent, lengths):
    tok_count = lax.axis_size("tok")
    user_count = lax.axis_size("user")
    tok_rows = hidden.shape[1]
    hidden_width = hidden.shape[2]
    model_width = cotangent.shape[2]
    capacity = tok_rows * tok_count
    own_width = hidden_width // tok_count
    columns = model_width // user_count
    clip_bound = math.sqrt(8.0 * hidden_width * model_width * capacity)
    scaling = math.sqrt(hidden_width * model_width) / (user_count * clip_bound)
    user = lax.axis_index("user").astype(jnp.int32).reshape(1)
    tok = lax.axis_index("tok").astype(jnp.int32).reshape(1)
    valid = lengths - tok * tok_rows
    half = tok_count // 2
    across, core = user_count // 2, user_count // 4
    slots = range(user_count)
    cut = round(own_width // lanes * first_part) * lanes
    pieces = [(0, cut), (cut, own_width - cut)]

    cots = {}
    lefts = {}
    ready = []
    tick = []

    def send(axis, distance, parts, after=()):
        message = join(parts, [*tick, *after])
        tick[:] = [message]
        return message, exchange(message, axis, distance)

    def cot_parts(d):
        return [(*cots[d][s], columns) for s in slots]

    def cots_at(array, start):
        return [(array, start + s * columns) for s in slots]

    masked = mask(valid, user, cotangent, user_count)
    by_slot = [masked[0]] + [exchange(masked[s], "user", s) for s in range(1, user_count)]
    outgoing = pack(tok, hidden, list(range(tok_count)), own_width, [masked[0]])
    ready += [(0, i, outgoing[0], start) for i, (start, _) in enumerate(pieces)]

    far_steps = []
    for i, (start, width) in enumerate(pieces):
        for d in range(half, tok_count, 2):
            far_steps.append([("block", e, i) for e in (d, d + 1)])
    far_steps.insert(1, [("cots", half, 0), ("cots", half, 1)])
    near = list(range(1, half))
    near_steps = [near[:2]] + [near[i : i + 2] if tok_count > 8 else near[i : i + 1] for i in range(2, len(near), 2)]
    relay_bits = [half >> i for i in range(1, half.bit_length())]

    lanes_before = [None, None]
    near_before, relay_before, cross_before, core_before = [], [], None, None
    gradients = []
    done = set()

    def finish_core():
        nonlocal core_before
        if core_before is None:
            return
        blocks, own, other, both = core_before
        core_before = None
        total = sum(pieces[i][1] for _, i, _, _ in blocks)
        to = 0
        for d, i, _, _ in blocks:
            lefts[d, i] = {0: (own, to), across: (other, to), core: (both, to), across ^ core: (both, total + to)}
            to += pieces[i][1]

    def add_products(step):
        if len(cots) < tok_count:
            return
        for i, (_, width) in enumerate(pieces):
            here = [d for d in range(tok_count) if (d, i) in lefts and (d, i) not in done]
            all_here = all((d, i) in lefts for d in range(tok_count))
            if not here or not (all_here or (i == 1 and step >= len(far_steps))):
                continue
            before = gradients[i] if len(gradients) > i else None
            final = all_here and i == 1
            out = product(
                [[lefts[d, i][s] for d in here] for s in slots],
                [[cots[d][s] for d in here] for s in slots],
                width,
                columns,
                held=before[0] if before else None,
                sums=gradients[0][1] if final else None,
                copies=0 if not all_here else tok_count * user_count if final else 1,
            )
            done.update((d, i) for d in here)
            gradients[i : i + 1] = [out]
            tick[:] = [out[0]]

    for step in range(len(far_steps) + 2):
        arrivals = []
        for lane in (0, 1):
            after = []
            if lanes_before[lane] is not None:
                after.append(lanes_before[lane][1])
                arrivals.append(lanes_before[lane])
                lanes_before[lane] = None
            if step < len(far_steps):
                kind, d, i = far_steps[step][lane]
                if kind == "block":
                    parts = [(outgoing[d], *pieces[i])]
                else:
                    parts = cot_parts(0)[lane * user_count // 2 : (lane + 1) * user_count // 2]
                message = send("tok", d, parts, after)
                lanes_before[lane] = (far_steps[step][lane], message[1])
        for (kind, d, i), array in arrivals:
            if kind == "block":
                ready.append((d, i, array, 0))
            else:
                cots.setdefault(d, [])
                cots[d] = cots[d] + [(array, s * columns) for s in range(user_count // 2)]
        for d, array in near_before:
            ready += [(d, i, array, start) for i, (start, _) in enumerate(pieces)]
            if d & (d - 1) == 0:
                cots[d] = cots_at(array, own_width)
        for bit, sources, array in relay_before:
            for at, d in enumerate(sources):
                cots[d + bit] = cots_at(array, at * model_width)
        near_before, relay_before = [], []
        crossed = cross_before
        cross_before = None
        if ready:
            blocks, ready = ready, []
            parts = [(array, start, pieces[i][1]) for _, i, array, start in blocks]
            own, other = send("user", across, parts, [crossed[2]] if crossed else [])
            cross_before = (blocks, own, other)
        if step == 0:
            cots[0] = [(block, 0) for block in by_slot]
            cots[0] = cots_at(join(cot_parts(0), []), 0)
        if step < len(near_steps):
            for d in near_steps[step]:
                parts = [(outgoing[d], 0, own_width)]
                if d & (d - 1) == 0:
                    parts += cot_parts(0)
                near_before.append((d, send("tok", d, parts)[1]))
        if relay_bits:
            bit = relay_bits[0]
            sources = list(range(2 * bit, tok_count, 2 * bit))
            if all(d in cots and len(cots[d]) == user_count for d in sources):
                relay_bits.pop(0)
                parts = [part for d in sources for part in cot_parts(d)]
                relay_before.append((bit, sources, send("tok", bit, parts)[1]))
        finish_core()
        if crossed:
            blocks, own, other = crossed
            total = sum(pieces[i][1] for _, i, _, _ in blocks)
            both = send("user", core, [(own, 0, total), (other, 0, total)])[1]
            core_before = (blocks, own, other, both)
        if step >= len(far_steps) - 1:
            finish_core()
            if relay_before:
                for bit, sources, array in relay_before:
                    for at, d in enumerate(sources):
                        cots[d + bit] = cots_at(array, at * model_width)
                relay_before = []
            add_products(step)
    sums = lax.all_to_all(gradients[1][1], ("user", "tok"), split_axis=0, concat_axis=0, tiled=True)
    return combine(user, sums, [g[0] for g in gradients], clip_bound, scaling)


def solution(mesh):
    return jax.shard_map(
        body,
        mesh=mesh,
        in_specs=(P("user", "tok", None), P("user", "tok", None), P("user")),
        out_specs=P("tok", "user"),
        check_vma=False,
    )
```

time: 227 us -> 209 us (0.921)
  Pallas kernels: 39.7 us -> 26 us
  waiting for transfers between devices: 130 us -> 125 us
  local copies, waits for them, and re-layouts: 7.6 us -> 3.22 us
  starting transfers between devices: 37.9 us -> 41.8 us
    pallas_call x4 -> x31, Pallas kernels: 34.1 us -> 20.7 us  [the longest x3 19.4 us: product(): pl.pallas_call(functools.partial(product_kernel, left_places, right_place...]
    ppermute x41 -> x30, waiting for transfers between devices: 130 us -> 125 us  [exchange(): return lax.ppermute(block, axis, [(i, i ^ distance) for i in range(size)])]
    unnamed x10 -> x4, local copies, waits for them, and re-layouts: 7.6 us -> 3.22 us
    ppermute x41 -> x30, starting transfers between devices: 37.9 us -> 41.8 us  [exchange(): return lax.ppermute(block, axis, [(i, i ^ distance) for i in range(size)])]
  transfers between devices with their start and end apart: 41 -> 30, of which waited for: 16 -> 17; matrix products, arithmetic and copies ran while one was open for 0% -> 0% of each run, Pallas kernels for 11% -> 8%
where the time goes in v5:
time: 209 us
  waiting for transfers between devices  125 us (60%)
  starting transfers between devices  41.8 us (20%)
  Pallas kernels  26 us (12%)
  blocking collectives  12.2 us (6%)
  local copies, waits for them, and re-layouts  3.22 us (2%)
    ppermute x30, waiting for transfers between devices, exchange(): return lax.ppermute(block, axis, [(i, i ^ distance) for i in range(size)])  125 us
    ppermute x30, starting transfers between devices, exchange(): return lax.ppermute(block, axis, [(i, i ^ distance) for i in range(size)])  41.8 us
    pallas_call x3, Pallas kernels, product(): pl.pallas_call(functools.partial(product_kernel, left_places, right_place...  19.4 us
    all_to_all x1, blocking collectives, body(): lax.all_to_all(gradients[1][1], ('user', 'tok'), split_axis=0, concat_axi...  12.2 us
    pallas_call x1, Pallas kernels, combine(): pl.pallas_call(functools.partial(combine_kernel, user_count, clip_bound,...  4.81 us
  transfers between devices with their start and end apart: 30, of which 17 were waited for; matrix products, arithmetic and copies ran while one was open for 0% of the time, Pallas kernels for 8%

profile of v5, /device:TPU:0, one launch (start us, length us, event | category | flops | bytes accessed | tf_op | source)
XLA Modules:
  0.0 208.9 jit_solution(6909470522717180087)
XLA Ops:
  0.7 1.0 copy-done.1
  1.7 0.5 collective-permute-start.2
  2.3 2.6 %collective-permute-start.3 = (bf16[128,512]{1,0:T(8,128)(2,1)S(1)}, bf16[128,512]{1,0:T(8,128)(2,1)S(1)}, u32[]{:S(2)}, u32[]{:S(2)}) collective-permute-start(bf16[128,512]{1,0:T(8,128)(2,1)S(1)} %get-tuple-element.28), channel_id=1, source_target_pairs={{0,16},{8,24},{16,0},{24,8},{1,17},{9,25},{17,1},{25,9},{2,18},{10... | collective-permute-start | bytes 393224 | tf_op jit(solution)/shard_map/ppermute | solution.py:22
  4.8 0.1 collective-permute-start.4
  4.9 2.2 %copy-done = bf16[1,128,16384]{2,1,0:T(8,128)(2,1)S(1)} copy-done((bf16[1,128,16384]{2,1,0:T(8,128)(2,1)S(1)}, bf16[1,128,16384]{2,1,0:T(8,128)(2,1)}, u32[]{:S(2)}) %copy-start) | copy-done | bytes 4194328
  7.1 0.4 pack_columns.1
  7.6 1.6 collective-permute-done.3.refs_2_
  9.2 2.3 %collective-permute-done.4.refs_3_ = bf16[128,512]{1,0:T(8,128)(2,1)S(1)} collective-permute-done((bf16[128,512]{1,0:T(8,128)(2,1)S(1)}, bf16[128,512]{1,0:T(8,128)(2,1)S(1)}, u32[]{:S(2)}, u32[]{:S(2)}) %collective-permute-start.4) | collective-permute-done | bytes 131104 | tf_op jit(solution)/shard_map/ppermute | solution.py:22
  11.5 0.1 join_columns.32.refs_5_
  11.6 0.1 join_columns.33.refs_2_
  11.7 1.7 collective-permute-start.6
  13.4 1.5 collective-permute-start.5
  14.9 1.5 collective-permute-start.7
  16.4 2.6 %collective-permute-start = (bf16[128,1024]{1,0:T(8,128)(2,1)S(1)}, bf16[128,1024]{1,0:T(8,128)(2,1)S(1)}, u32[]{:S(2)}, u32[]{:S(2)}) collective-permute-start(bf16[128,1024]{1,0:T(8,128)(2,1)S(1)} %join_columns.28.refs_1_), channel_id=1, source_target_pairs={{0,4},{1,5},{2,6},{3,7},{4,0},{5,1},{6,2},{7,3},{8,12},{9,13},{10,... | collective-permute-start | bytes 786440 | tf_op jit(solution)/shard_map/ppermute | solution.py:22
  19.0 0.3 collective-permute-start.1
  19.3 23.2 %collective-permute-done.refs_3_.refs_0_ = bf16[128,1024]{1,0:T(8,128)(2,1)S(1)} collective-permute-done((bf16[128,1024]{1,0:T(8,128)(2,1)S(1)}, bf16[128,1024]{1,0:T(8,128)(2,1)S(1)}, u32[]{:S(2)}, u32[]{:S(2)}) %collective-permute-start) | collective-permute-done | bytes 262176 | tf_op jit(solution)/shard_map/ppermute | solution.py:22
  42.5 4.9 %collective-permute-done.1.refs_3_.refs_1_ = bf16[128,1024]{1,0:T(8,128)(2,1)S(1)} collective-permute-done((bf16[128,1024]{1,0:T(8,128)(2,1)S(1)}, bf16[128,1024]{1,0:T(8,128)(2,1)S(1)}, u32[]{:S(2)}, u32[]{:S(2)}) %collective-permute-start.1) | collective-permute-done | bytes 262176 | tf_op jit(solution)/shard_map/ppermute | solution.py:22
  47.5 0.0 collective-permute-done.7.refs_7_.refs_1_.refs_8_
  47.5 0.7 collective-permute-done.6.refs_4_.refs_5_.refs_0_.refs_1_.refs_2_.refs_3_.refs_14_
  48.2 0.1 join_columns.36.refs_1_.refs_0_
  48.3 1.7 collective-permute-start.11
  50.1 3.6 %collective-permute-start.8 = (bf16[128,2048]{1,0:T(8,128)(2,1)S(1)}, bf16[128,2048]{1,0:T(8,128)(2,1)S(1)}, u32[]{:S(2)}, u32[]{:S(2)}) collective-permute-start(bf16[128,2048]{1,0:T(8,128)(2,1)S(1)} %join_columns.37.refs_2_), channel_id=1, source_target_pairs={{0,3},{1,2},{2,1},{3,0},{4,7},{5,6},{6,5},{7,4},{8,11},{9,10},{10,... | collective-permute-start | bytes 1572872 | tf_op jit(solution)/shard_map/ppermute | solution.py:22
  53.7 1.6 collective-permute-start.9
  55.3 1.3 collective-permute-start.10
  56.6 0.1 join_columns.38.refs_1_
  56.7 15.0 %collective-permute-done.9.refs_2_.refs_0_.refs_1_.refs_4_.refs_5_.refs_16_ = bf16[128,1024]{1,0:T(8,128)(2,1)S(1)} collective-permute-done((bf16[128,1024]{1,0:T(8,128)(2,1)S(1)}, bf16[128,1024]{1,0:T(8,128)(2,1)S(1)}, u32[]{:S(2)}, u32[]{:S(2)}) %collective-permute-start.9) | collective-permute-done | bytes 262176 | tf_op jit(solution)/shard_map/ppermute | solution.py:22
  71.8 6.8 %collective-permute-done.10.refs_2_.refs_3_.refs_6_.refs_7_.refs_18_.refs_17_ = bf16[128,1024]{1,0:T(8,128)(2,1)S(1)} collective-permute-done((bf16[128,1024]{1,0:T(8,128)(2,1)S(1)}, bf16[128,1024]{1,0:T(8,128)(2,1)S(1)}, u32[]{:S(2)}, u32[]{:S(2)}) %collective-permute-start.10) | collective-permute-done | bytes 262176 | tf_op jit(solution)/shard_map/ppermute | solution.py:22
  78.6 5.4 %collective-permute-done.11.refs_3_.refs_1_.refs_9_ = bf16[128,6144]{1,0:T(8,128)(2,1)S(1)} collective-permute-done((bf16[128,6144]{1,0:T(8,128)(2,1)S(1)}, bf16[128,6144]{1,0:T(8,128)(2,1)S(1)}, u32[]{:S(2)}, u32[]{:S(2)}) %collective-permute-start.11) | collective-permute-done | bytes 1572896 | tf_op jit(solution)/shard_map/ppermute | solution.py:22
  84.2 0.2 join_columns.43.refs_1_
  84.4 0.1 collective-permute-start.21
  84.5 1.8 collective-permute-start.12
  86.3 3.6 %collective-permute-start.13 = (bf16[128,2048]{1,0:T(8,128)(2,1)S(1)}, bf16[128,2048]{1,0:T(8,128)(2,1)S(1)}, u32[]{:S(2)}, u32[]{:S(2)}) collective-permute-start(bf16[128,2048]{1,0:T(8,128)(2,1)S(1)} %join_columns.42.refs_2_), channel_id=1, source_target_pairs={{0,2},{1,3},{2,0},{3,1},{4,6},{5,7},{6,4},{7,5},{8,10},{9,11},{10,... | collective-permute-start | bytes 1572872 | tf_op jit(solution)/shard_map/ppermute | solution.py:22
  89.9 1.3 collective-permute-start.14
  91.2 2.4 %collective-permute-start.15 = (bf16[128,1024]{1,0:T(8,128)(2,1)S(1)}, bf16[128,1024]{1,0:T(8,128)(2,1)S(1)}, u32[]{:S(2)}, u32[]{:S(2)}) collective-permute-start(bf16[128,1024]{1,0:T(8,128)(2,1)S(1)} %join_columns.40.refs_2_), channel_id=1, source_target_pairs={{0,7},{1,6},{2,5},{3,4},{4,3},{5,2},{6,1},{7,0},{8,15},{9,14},{10,... | collective-permute-start | bytes 786440 | tf_op jit(solution)/shard_map/ppermute | solution.py:22
  93.6 16.0 %collective-permute-done.14.refs_2_.refs_0_ = bf16[128,1024]{1,0:T(8,128)(2,1)S(1)} collective-permute-done((bf16[128,1024]{1,0:T(8,128)(2,1)S(1)}, bf16[128,1024]{1,0:T(8,128)(2,1)S(1)}, u32[]{:S(2)}, u32[]{:S(2)}) %collective-permute-start.14) | collective-permute-done | bytes 262176 | tf_op jit(solution)/shard_map/ppermute | solution.py:22
  109.7 4.8 %collective-permute-done.15.refs_2_.refs_1_ = bf16[128,1024]{1,0:T(8,128)(2,1)S(1)} collective-permute-done((bf16[128,1024]{1,0:T(8,128)(2,1)S(1)}, bf16[128,1024]{1,0:T(8,128)(2,1)S(1)}, u32[]{:S(2)}, u32[]{:S(2)}) %collective-permute-start.15) | collective-permute-done | bytes 262176 | tf_op jit(solution)/shard_map/ppermute | solution.py:22
  114.5 0.6 collective-permute-start.23
  115.1 0.1 join_columns.47.refs_2_
  115.3 1.6 collective-permute-start.25
  116.9 0.5 collective-permute-start.16
  117.4 2.3 %collective-permute-start.18 = (bf16[128,1024]{1,0:T(8,128)(2,1)S(1)}, bf16[128,1024]{1,0:T(8,128)(2,1)S(1)}, u32[]{:S(2)}, u32[]{:S(2)}) collective-permute-start(bf16[128,1024]{1,0:T(8,128)(2,1)S(1)} %join_columns.45.refs_2_), channel_id=1, source_target_pairs={{0,5},{1,4},{2,7},{3,6},{4,1},{5,0},{6,3},{7,2},{8,13},{9,12},{10,... | collective-permute-start | bytes 786440 | tf_op jit(solution)/shard_map/ppermute | solution.py:22
  119.7 16.1 %collective-permute-done.16.refs_2_.refs_0_ = bf16[128,1024]{1,0:T(8,128)(2,1)S(1)} collective-permute-done((bf16[128,1024]{1,0:T(8,128)(2,1)S(1)}, bf16[128,1024]{1,0:T(8,128)(2,1)S(1)}, u32[]{:S(2)}, u32[]{:S(2)}) %collective-permute-start.16) | collective-permute-done | bytes 262176 | tf_op jit(solution)/shard_map/ppermute | solution.py:22
  135.8 0.1 join_columns.48.refs_1_
  135.9 5.5 %collective-permute-done.18.refs_2_.refs_1_ = bf16[128,1024]{1,0:T(8,128)(2,1)S(1)} collective-permute-done((bf16[128,1024]{1,0:T(8,128)(2,1)S(1)}, bf16[128,1024]{1,0:T(8,128)(2,1)S(1)}, u32[]{:S(2)}, u32[]{:S(2)}) %collective-permute-start.18) | collective-permute-done | bytes 262176 | tf_op jit(solution)/shard_map/ppermute | solution.py:22
  141.5 0.1 join_columns.52
  141.6 0.6 collective-permute-start.24
  142.2 1.5 collective-permute-start.26
  143.6 0.4 collective-permute-done.22.refs_6_
  144.1 2.3 %collective-permute-start.19 = (bf16[128,1024]{1,0:T(8,128)(2,1)S(1)}, bf16[128,1024]{1,0:T(8,128)(2,1)S(1)}, u32[]{:S(2)}, u32[]{:S(2)}) collective-permute-start(bf16[128,1024]{1,0:T(8,128)(2,1)S(1)} %join_columns.50.refs_2_), channel_id=1, source_target_pairs={{0,7},{1,6},{2,5},{3,4},{4,3},{5,2},{6,1},{7,0},{8,15},{9,14},{10,... | collective-permute-start | bytes 786440 | tf_op jit(solution)/shard_map/ppermute | solution.py:22
  146.4 2.4 %collective-permute-start.17 = (bf16[128,1024]{1,0:T(8,128)(2,1)S(1)}, bf16[128,1024]{1,0:T(8,128)(2,1)S(1)}, u32[]{:S(2)}, u32[]{:S(2)}) collective-permute-start(bf16[128,1024]{1,0:T(8,128)(2,1)S(1)} %join_columns.49.refs_1_), channel_id=1, source_target_pairs={{0,6},{1,7},{2,4},{3,5},{4,2},{5,3},{6,0},{7,1},{8,14},{9,15},{10,... | collective-permute-start | bytes 786440 | tf_op jit(solution)/shard_map/ppermute | solution.py:22
  148.8 13.0 %collective-permute-done.25.refs_15_.refs_4_ = bf16[128,6144]{1,0:T(8,128)(2,1)S(1)} collective-permute-done((bf16[128,6144]{1,0:T(8,128)(2,1)S(1)}, bf16[128,6144]{1,0:T(8,128)(2,1)S(1)}, u32[]{:S(2)}, u32[]{:S(2)}) %collective-permute-start.25) | collective-permute-done | bytes 1572896 | tf_op jit(solution)/shard_map/ppermute | solution.py:22
  161.9 8.1 %product_and_squares.3 = (f32[4,1024,512]{2,1,0:T(8,128)S(1)}, f32[1,8,128]{2,1,0:T(8,128)S(1)}) custom-call(bf16[128,2048]{1,0:T(8,128)(2,1)S(1)} %join_columns.31.refs_5_.refs_0_, bf16[128,6144]{1,0:T(8,128)(2,1)S(1)} %join_columns.36.refs_1_.refs_0_, bf16[128,2048]{1,0:T(8,128)(2,1)S(1)} %join_columns.41.refs_4_.refs_0_.refs_2_, ...), custom_call_target="tpu_custom_call" | custom-call | flops 4294967296 | bytes 12582912 | tf_op jit(solution)/shard_map/product_and_squares/pallas_call | solution.py:169
  170.0 0.1 join_columns.54
  170.1 0.1 collective-permute-start.28
  170.2 1.6 collective-permute-start.27
  171.8 1.1 collective-permute-done.28.refs_7_
  172.8 6.8 %product_and_squares.4.refs_2_.refs_5_ = f32[4,1024,512]{2,1,0:T(8,128)S(1)} custom-call(bf16[128,2048]{1,0:T(8,128)(2,1)S(1)} %join_columns.31.refs_5_.refs_0_, bf16[128,6144]{1,0:T(8,128)(2,1)S(1)} %join_columns.36.refs_1_.refs_0_, bf16[128,2048]{1,0:T(8,128)(2,1)S(1)} %join_columns.41.refs_4_.refs_0_.refs_2_, ...), custom_call_target="tpu_custom_call" | custom-call | flops 3221225472 | bytes 9437184 | tf_op jit(solution)/shard_map/product_and_squares/pallas_call | solution.py:169
  179.6 4.9 %collective-permute-done.27.refs_1_.refs_2_ = bf16[128,2048]{1,0:T(8,128)(2,1)S(1)} collective-permute-done((bf16[128,2048]{1,0:T(8,128)(2,1)S(1)}, bf16[128,2048]{1,0:T(8,128)(2,1)S(1)}, u32[]{:S(2)}, u32[]{:S(2)}) %collective-permute-start.27) | collective-permute-done | bytes 524320 | tf_op jit(solution)/shard_map/ppermute | solution.py:22
  184.5 0.1 join_columns.55
  184.6 0.1 collective-permute-start.29
  184.7 2.6 %collective-permute-done.29.refs_1_ = bf16[128,4096]{1,0:T(8,128)(2,1)S(1)} collective-permute-done((bf16[128,4096]{1,0:T(8,128)(2,1)S(1)}, bf16[128,4096]{1,0:T(8,128)(2,1)S(1)}, u32[]{:S(2)}, u32[]{:S(2)}) %collective-permute-start.29) | collective-permute-done | bytes 1048608 | tf_op jit(solution)/shard_map/ppermute | solution.py:22
  187.3 4.5 %product_and_squares.5 = (f32[4,1024,512]{2,1,0:T(8,128)S(1)}, f32[32,8,128]{2,1,0:T(8,128)S(1)}) custom-call(bf16[128,2048]{1,0:T(8,128)(2,1)S(1)} %join_columns.53.refs_2_.refs_0_, bf16[128,4096]{1,0:T(8,128)(2,1)S(1)} %collective-permute-done.29.refs_1_, ...), custom_call_target="tpu_custom_call", output_to_operand_aliasing={{0}: (5, {})} | custom-call | flops 1073741824 | bytes 3145728 | tf_op jit(solution)/shard_map/product_and_squares/pallas_call | solution.py:169
  191.8 12.2 %all_to_all.5.sums_ref = f32[32,8,128]{2,1,0:T(8,128)S(1)} all-to-all(f32[32,8,128]{2,1,0:T(8,128)S(1)} %get-tuple-element.35), channel_id=1, replica_groups=mesh['user'=4,'tok'=8] {'user','tok'}, dimensions={0} | all-to-all | bytes 262144 | tf_op jit(solution)/shard_map/all_to_all | solution.py:395
  204.1 4.8 %weighted_sum.1 = f32[2048,512]{1,0:T(8,128)} custom-call(s32[1]{0:T(128)} %bitcast.user_ref, f32[32,8,128]{2,1,0:T(8,128)S(1)} %all_to_all.5.sums_ref, f32[4,1024,512]{2,1,0:T(8,128)S(1)} %get-tuple-element.33.refs_2_.refs_0_, f32[4,1024,512]{2,1,0:T(8,128)S(1)} %get-tuple-element.36.refs_1_), custom_call_target="tpu_custom_call" | custom-call | tf_op jit(solution)/shard_map/weighted_sum/pallas_call | solution.py:226
  (35 shorter events, 0.6 us)
Async XLA Ops:
  0.7 1.0 copy-start.1
  1.7 5.8 %collective-permute-start.2 = (bf16[128,512]{1,0:T(8,128)(2,1)S(1)}, bf16[128,512]{1,0:T(8,128)(2,1)S(1)}, u32[]{:S(2)}, u32[]{:S(2)}) collective-permute-start(bf16[128,512]{1,0:T(8,128)(2,1)S(1)} %get-tuple-element.27), channel_id=1, source_target_pairs={{0,8},{8,0},{16,24},{24,16},{1,9},{9,1},{17,25},{25,17},{2,10},{10... | collective-permute-start | bytes 393224 | tf_op jit(solution)/shard_map/ppermute | solution.py:22
  2.3 6.9 %collective-permute-start.3 = (bf16[128,512]{1,0:T(8,128)(2,1)S(1)}, bf16[128,512]{1,0:T(8,128)(2,1)S(1)}, u32[]{:S(2)}, u32[]{:S(2)}) collective-permute-start(bf16[128,512]{1,0:T(8,128)(2,1)S(1)} %get-tuple-element.28), channel_id=1, source_target_pairs={{0,16},{8,24},{16,0},{24,8},{1,17},{9,25},{17,1},{25,9},{2,18},{10... | collective-permute-start | bytes 393224 | tf_op jit(solution)/shard_map/ppermute | solution.py:22
  4.8 6.6 %collective-permute-start.4 = (bf16[128,512]{1,0:T(8,128)(2,1)S(1)}, bf16[128,512]{1,0:T(8,128)(2,1)S(1)}, u32[]{:S(2)}, u32[]{:S(2)}) collective-permute-start(bf16[128,512]{1,0:T(8,128)(2,1)S(1)} %get-tuple-element.29), channel_id=1, source_target_pairs={{0,24},{8,16},{16,8},{24,0},{1,25},{9,17},{17,9},{25,1},{2,26},{10... | collective-permute-start | bytes 393224 | tf_op jit(solution)/shard_map/ppermute | solution.py:22
  4.9 2.2 %copy-start = (bf16[1,128,16384]{2,1,0:T(8,128)(2,1)S(1)}, bf16[1,128,16384]{2,1,0:T(8,128)(2,1)}, u32[]{:S(2)}) copy-start(bf16[1,128,16384]{2,1,0:T(8,128)(2,1)} %hidden_ref.1) | copy-start | bytes 12582916
  11.7 36.6 %collective-permute-start.6 = (bf16[128,4096]{1,0:T(8,128)(2,1)S(1)}, bf16[128,4096]{1,0:T(8,128)(2,1)S(1)}, u32[]{:S(2)}, u32[]{:S(2)}) collective-permute-start(bf16[128,4096]{1,0:T(8,128)(2,1)S(1)} %join_columns.33.refs_2_), channel_id=1, source_target_pairs={{0,2},{1,3},{2,0},{3,1},{4,6},{5,7},{6,4},{7,5},{8,10},{9,11},{10,... | collective-permute-start | bytes 3145736 | tf_op jit(solution)/shard_map/ppermute | solution.py:22
  13.4 34.8 %collective-permute-start.5 = (bf16[128,4096]{1,0:T(8,128)(2,1)S(1)}, bf16[128,4096]{1,0:T(8,128)(2,1)S(1)}, u32[]{:S(2)}, u32[]{:S(2)}) collective-permute-start(bf16[128,4096]{1,0:T(8,128)(2,1)S(1)} %join_columns.32.refs_5_), channel_id=1, source_target_pairs={{0,1},{1,0},{2,3},{3,2},{4,5},{5,4},{6,7},{7,6},{8,9},{9,8},{10,11... | collective-permute-start | bytes 3145736 | tf_op jit(solution)/shard_map/ppermute | solution.py:22
  14.9 32.6 %collective-permute-start.7 = (bf16[128,2048]{1,0:T(8,128)(2,1)S(1)}, bf16[128,2048]{1,0:T(8,128)(2,1)S(1)}, u32[]{:S(2)}, u32[]{:S(2)}) collective-permute-start(bf16[128,2048]{1,0:T(8,128)(2,1)S(1)} %join_columns.31.refs_5_.refs_0_), channel_id=1, source_target_pairs={{0,16},{8,24},{16,0},{24,8},{1,17},{9,25},{17,1},{25,9},{2,18},{10... | collective-permute-start | bytes 1572872 | tf_op jit(solution)/shard_map/ppermute | solution.py:22
  16.4 26.1 %collective-permute-start = (bf16[128,1024]{1,0:T(8,128)(2,1)S(1)}, bf16[128,1024]{1,0:T(8,128)(2,1)S(1)}, u32[]{:S(2)}, u32[]{:S(2)}) collective-permute-start(bf16[128,1024]{1,0:T(8,128)(2,1)S(1)} %join_columns.28.refs_1_), channel_id=1, source_target_pairs={{0,4},{1,5},{2,6},{3,7},{4,0},{5,1},{6,2},{7,3},{8,12},{9,13},{10,... | collective-permute-start | bytes 786440 | tf_op jit(solution)/shard_map/ppermute | solution.py:22
  19.0 28.5 %collective-permute-start.1 = (bf16[128,1024]{1,0:T(8,128)(2,1)S(1)}, bf16[128,1024]{1,0:T(8,128)(2,1)S(1)}, u32[]{:S(2)}, u32[]{:S(2)}) collective-permute-start(bf16[128,1024]{1,0:T(8,128)(2,1)S(1)} %join_columns.29.refs_2_), channel_id=1, source_target_pairs={{0,5},{1,4},{2,7},{3,6},{4,1},{5,0},{6,3},{7,2},{8,13},{9,12},{10,... | collective-permute-start | bytes 786440 | tf_op jit(solution)/shard_map/ppermute | solution.py:22
  48.3 35.7 %collective-permute-start.11 = (bf16[128,6144]{1,0:T(8,128)(2,1)S(1)}, bf16[128,6144]{1,0:T(8,128)(2,1)S(1)}, u32[]{:S(2)}, u32[]{:S(2)}) collective-permute-start(bf16[128,6144]{1,0:T(8,128)(2,1)S(1)} %join_columns.36.refs_1_.refs_0_), channel_id=1, source_target_pairs={{0,16},{8,24},{16,0},{24,8},{1,17},{9,25},{17,1},{25,9},{2,18},{10... | collective-permute-start | bytes 4718600 | tf_op jit(solution)/shard_map/ppermute | solution.py:22
  50.1 28.5 %collective-permute-start.8 = (bf16[128,2048]{1,0:T(8,128)(2,1)S(1)}, bf16[128,2048]{1,0:T(8,128)(2,1)S(1)}, u32[]{:S(2)}, u32[]{:S(2)}) collective-permute-start(bf16[128,2048]{1,0:T(8,128)(2,1)S(1)} %join_columns.37.refs_2_), channel_id=1, source_target_pairs={{0,3},{1,2},{2,1},{3,0},{4,7},{5,6},{6,5},{7,4},{8,11},{9,10},{10,... | collective-permute-start | bytes 1572872 | tf_op jit(solution)/shard_map/ppermute | solution.py:22
  53.7 18.0 %collective-permute-start.9 = (bf16[128,1024]{1,0:T(8,128)(2,1)S(1)}, bf16[128,1024]{1,0:T(8,128)(2,1)S(1)}, u32[]{:S(2)}, u32[]{:S(2)}) collective-permute-start(bf16[128,1024]{1,0:T(8,128)(2,1)S(1)} %join_columns.34.refs_2_), channel_id=1, source_target_pairs={{0,4},{1,5},{2,6},{3,7},{4,0},{5,1},{6,2},{7,3},{8,12},{9,13},{10,... | collective-permute-start | bytes 786440 | tf_op jit(solution)/shard_map/ppermute | solution.py:22
  55.3 23.3 %collective-permute-start.10 = (bf16[128,1024]{1,0:T(8,128)(2,1)S(1)}, bf16[128,1024]{1,0:T(8,128)(2,1)S(1)}, u32[]{:S(2)}, u32[]{:S(2)}) collective-permute-start(bf16[128,1024]{1,0:T(8,128)(2,1)S(1)} %join_columns.35.refs_6_), channel_id=1, source_target_pairs={{0,4},{1,5},{2,6},{3,7},{4,0},{5,1},{6,2},{7,3},{8,12},{9,13},{10,... | collective-permute-start | bytes 786440 | tf_op jit(solution)/shard_map/ppermute | solution.py:22
  84.4 77.5 %collective-permute-start.21 = (bf16[128,12288]{1,0:T(8,128)(2,1)S(1)}, bf16[128,12288]{1,0:T(8,128)(2,1)S(1)}, u32[]{:S(2)}, u32[]{:S(2)}) collective-permute-start(bf16[128,12288]{1,0:T(8,128)(2,1)S(1)} %join_columns.43.refs_1_), channel_id=1, source_target_pairs={{0,8},{8,0},{16,24},{24,16},{1,9},{9,1},{17,25},{25,17},{2,10},{10... | collective-permute-start | bytes 9437192 | tf_op jit(solution)/shard_map/ppermute | solution.py:22
  84.5 30.0 %collective-permute-start.12 = (bf16[128,2048]{1,0:T(8,128)(2,1)S(1)}, bf16[128,2048]{1,0:T(8,128)(2,1)S(1)}, u32[]{:S(2)}, u32[]{:S(2)}) collective-permute-start(bf16[128,2048]{1,0:T(8,128)(2,1)S(1)} %join_columns.41.refs_4_.refs_0_.refs_2_), channel_id=1, source_target_pairs={{0,16},{8,24},{16,0},{24,8},{1,17},{9,25},{17,1},{25,9},{2,18},{10... | collective-permute-start | bytes 1572872 | tf_op jit(solution)/shard_map/ppermute | solution.py:22
  86.3 28.9 %collective-permute-start.13 = (bf16[128,2048]{1,0:T(8,128)(2,1)S(1)}, bf16[128,2048]{1,0:T(8,128)(2,1)S(1)}, u32[]{:S(2)}, u32[]{:S(2)}) collective-permute-start(bf16[128,2048]{1,0:T(8,128)(2,1)S(1)} %join_columns.42.refs_2_), channel_id=1, source_target_pairs={{0,2},{1,3},{2,0},{3,1},{4,6},{5,7},{6,4},{7,5},{8,10},{9,11},{10,... | collective-permute-start | bytes 1572872 | tf_op jit(solution)/shard_map/ppermute | solution.py:22
  89.9 19.8 %collective-permute-start.14 = (bf16[128,1024]{1,0:T(8,128)(2,1)S(1)}, bf16[128,1024]{1,0:T(8,128)(2,1)S(1)}, u32[]{:S(2)}, u32[]{:S(2)}) collective-permute-start(bf16[128,1024]{1,0:T(8,128)(2,1)S(1)} %join_columns.39.refs_1_), channel_id=1, source_target_pairs={{0,6},{1,7},{2,4},{3,5},{4,2},{5,3},{6,0},{7,1},{8,14},{9,15},{10,... | collective-permute-start | bytes 786440 | tf_op jit(solution)/shard_map/ppermute | solution.py:22
  91.2 23.2 %collective-permute-start.15 = (bf16[128,1024]{1,0:T(8,128)(2,1)S(1)}, bf16[128,1024]{1,0:T(8,128)(2,1)S(1)}, u32[]{:S(2)}, u32[]{:S(2)}) collective-permute-start(bf16[128,1024]{1,0:T(8,128)(2,1)S(1)} %join_columns.40.refs_2_), channel_id=1, source_target_pairs={{0,7},{1,6},{2,5},{3,4},{4,3},{5,2},{6,1},{7,0},{8,15},{9,14},{10,... | collective-permute-start | bytes 786440 | tf_op jit(solution)/shard_map/ppermute | solution.py:22
  114.5 26.9 %collective-permute-start.23 = (bf16[128,2048]{1,0:T(8,128)(2,1)S(1)}, bf16[128,2048]{1,0:T(8,128)(2,1)S(1)}, u32[]{:S(2)}, u32[]{:S(2)}) collective-permute-start(bf16[128,2048]{1,0:T(8,128)(2,1)S(1)} %join_columns.46.refs_12_.refs_0_.refs_3_), channel_id=1, source_target_pairs={{0,16},{8,24},{16,0},{24,8},{1,17},{9,25},{17,1},{25,9},{2,18},{10... | collective-permute-start | bytes 1572872 | tf_op jit(solution)/shard_map/ppermute | solution.py:22
  115.3 46.6 %collective-permute-start.25 = (bf16[128,6144]{1,0:T(8,128)(2,1)S(1)}, bf16[128,6144]{1,0:T(8,128)(2,1)S(1)}, u32[]{:S(2)}, u32[]{:S(2)}) collective-permute-start(bf16[128,6144]{1,0:T(8,128)(2,1)S(1)} %join_columns.47.refs_2_), channel_id=1, source_target_pairs={{0,1},{1,0},{2,3},{3,2},{4,5},{5,4},{6,7},{7,6},{8,9},{9,8},{10,11... | collective-permute-start | bytes 4718600 | tf_op jit(solution)/shard_map/ppermute | solution.py:22
  116.9 18.9 %collective-permute-start.16 = (bf16[128,1024]{1,0:T(8,128)(2,1)S(1)}, bf16[128,1024]{1,0:T(8,128)(2,1)S(1)}, u32[]{:S(2)}, u32[]{:S(2)}) collective-permute-start(bf16[128,1024]{1,0:T(8,128)(2,1)S(1)} %join_columns.44.refs_1_), channel_id=1, source_target_pairs={{0,4},{1,5},{2,6},{3,7},{4,0},{5,1},{6,2},{7,3},{8,12},{9,13},{10,... | collective-permute-start | bytes 786440 | tf_op jit(solution)/shard_map/ppermute | solution.py:22
  117.4 24.0 %collective-permute-start.18 = (bf16[128,1024]{1,0:T(8,128)(2,1)S(1)}, bf16[128,1024]{1,0:T(8,128)(2,1)S(1)}, u32[]{:S(2)}, u32[]{:S(2)}) collective-permute-start(bf16[128,1024]{1,0:T(8,128)(2,1)S(1)} %join_columns.45.refs_2_), channel_id=1, source_target_pairs={{0,5},{1,4},{2,7},{3,6},{4,1},{5,0},{6,3},{7,2},{8,13},{9,12},{10,... | collective-permute-start | bytes 786440 | tf_op jit(solution)/shard_map/ppermute | solution.py:22
  135.8 6.4 %collective-permute-start.20 = (bf16[128,4096]{1,0:T(8,128)(2,1)S(1)}, bf16[128,4096]{1,0:T(8,128)(2,1)S(1)}, u32[]{:S(2)}, u32[]{:S(2)}) collective-permute-start(bf16[128,4096]{1,0:T(8,128)(2,1)S(1)} %join_columns.38.refs_1_), channel_id=1, source_target_pairs={{0,8},{8,0},{16,24},{24,16},{1,9},{9,1},{17,25},{25,17},{2,10},{10... | collective-permute-start | bytes 3145736 | tf_op jit(solution)/shard_map/ppermute | solution.py:22
  141.4 2.7 %collective-permute-start.22 = (bf16[128,4096]{1,0:T(8,128)(2,1)S(1)}, bf16[128,4096]{1,0:T(8,128)(2,1)S(1)}, u32[]{:S(2)}, u32[]{:S(2)}) collective-permute-start(bf16[128,4096]{1,0:T(8,128)(2,1)S(1)} %join_columns.48.refs_1_), channel_id=1, source_target_pairs={{0,8},{8,0},{16,24},{24,16},{1,9},{9,1},{17,25},{25,17},{2,10},{10... | collective-permute-start | bytes 3145736 | tf_op jit(solution)/shard_map/ppermute | solution.py:22
  141.6 4.8 %collective-permute-start.24 = (bf16[128,4096]{1,0:T(8,128)(2,1)S(1)}, bf16[128,4096]{1,0:T(8,128)(2,1)S(1)}, u32[]{:S(2)}, u32[]{:S(2)}) collective-permute-start(bf16[128,4096]{1,0:T(8,128)(2,1)S(1)} %join_columns.52), channel_id=1, source_target_pairs={{0,8},{8,0},{16,24},{24,16},{1,9},{9,1},{17,25},{25,17},{2,10},{10... | collective-permute-start | bytes 3145736 | tf_op jit(solution)/shard_map/ppermute | solution.py:22
  142.2 27.8 %collective-permute-start.26 = (bf16[128,2048]{1,0:T(8,128)(2,1)S(1)}, bf16[128,2048]{1,0:T(8,128)(2,1)S(1)}, u32[]{:S(2)}, u32[]{:S(2)}) collective-permute-start(bf16[128,2048]{1,0:T(8,128)(2,1)S(1)} %join_columns.51.refs_2_.refs_0_.refs_3_), channel_id=1, source_target_pairs={{0,16},{8,24},{16,0},{24,8},{1,17},{9,25},{17,1},{25,9},{2,18},{10... | collective-permute-start | bytes 1572872 | tf_op jit(solution)/shard_map/ppermute | solution.py:22
  144.1 25.9 %collective-permute-start.19 = (bf16[128,1024]{1,0:T(8,128)(2,1)S(1)}, bf16[128,1024]{1,0:T(8,128)(2,1)S(1)}, u32[]{:S(2)}, u32[]{:S(2)}) collective-permute-start(bf16[128,1024]{1,0:T(8,128)(2,1)S(1)} %join_columns.50.refs_2_), channel_id=1, source_target_pairs={{0,7},{1,6},{2,5},{3,4},{4,3},{5,2},{6,1},{7,0},{8,15},{9,14},{10,... | collective-permute-start | bytes 786440 | tf_op jit(solution)/shard_map/ppermute | solution.py:22
  146.4 23.6 %collective-permute-start.17 = (bf16[128,1024]{1,0:T(8,128)(2,1)S(1)}, bf16[128,1024]{1,0:T(8,128)(2,1)S(1)}, u32[]{:S(2)}, u32[]{:S(2)}) collective-permute-start(bf16[128,1024]{1,0:T(8,128)(2,1)S(1)} %join_columns.49.refs_1_), channel_id=1, source_target_pairs={{0,6},{1,7},{2,4},{3,5},{4,2},{5,3},{6,0},{7,1},{8,14},{9,15},{10,... | collective-permute-start | bytes 786440 | tf_op jit(solution)/shard_map/ppermute | solution.py:22
  170.1 2.7 %collective-permute-start.28 = (bf16[128,4096]{1,0:T(8,128)(2,1)S(1)}, bf16[128,4096]{1,0:T(8,128)(2,1)S(1)}, u32[]{:S(2)}, u32[]{:S(2)}) collective-permute-start(bf16[128,4096]{1,0:T(8,128)(2,1)S(1)} %join_columns.54), channel_id=1, source_target_pairs={{0,8},{8,0},{16,24},{24,16},{1,9},{9,1},{17,25},{25,17},{2,10},{10... | collective-permute-start | bytes 3145736 | tf_op jit(solution)/shard_map/ppermute | solution.py:22
  170.2 14.3 %collective-permute-start.27 = (bf16[128,2048]{1,0:T(8,128)(2,1)S(1)}, bf16[128,2048]{1,0:T(8,128)(2,1)S(1)}, u32[]{:S(2)}, u32[]{:S(2)}) collective-permute-start(bf16[128,2048]{1,0:T(8,128)(2,1)S(1)} %join_columns.53.refs_2_.refs_0_), channel_id=1, source_target_pairs={{0,16},{8,24},{16,0},{24,8},{1,17},{9,25},{17,1},{25,9},{2,18},{10... | collective-permute-start | bytes 1572872 | tf_op jit(solution)/shard_map/ppermute | solution.py:22
  184.6 2.7 %collective-permute-start.29 = (bf16[128,4096]{1,0:T(8,128)(2,1)S(1)}, bf16[128,4096]{1,0:T(8,128)(2,1)S(1)}, u32[]{:S(2)}, u32[]{:S(2)}) collective-permute-start(bf16[128,4096]{1,0:T(8,128)(2,1)S(1)} %join_columns.55), channel_id=1, source_target_pairs={{0,8},{8,0},{16,24},{24,16},{1,9},{9,1},{17,25},{25,17},{2,10},{10... | collective-permute-start | bytes 3145736 | tf_op jit(solution)/shard_map/ppermute | solution.py:22

commit v6 on v5

--- a/solution.py
+++ b/solution.py
@@ -10,7 +10,12 @@
 
 epsilon = 1e-06
 lanes = 128
-first_part = 0.5
+first_part = 0.625
+most_flying = 5
+start_time = 1.5
+latency = 1.0
+link_rate = 5e4
+product_time = 16.0
 ANY = pl.BlockSpec(memory_space=pl.ANY)
 SMEM = pl.BlockSpec(memory_space=pltpu.SMEM)
 VMEM = pl.BlockSpec(memory_space=pltpu.VMEM)
@@ -59,22 +64,28 @@
 def join_kernel(parts, *refs):
     out_ref = refs[-1]
     to = 0
-    for ref, (start, width) in zip(refs, parts):
-        out_ref[:, to : to + width] = ref[:, start : start + width]
+    for at, start, width in parts:
+        out_ref[:, to : to + width] = refs[at][:, start : start + width]
         to += width
 
 
 def join(parts, after):
-    arrays = [array for array, _, _ in parts]
+    arrays, places = [], []
+    for array, start, width in parts:
+        at = [i for i, other in enumerate(arrays) if other is array]
+        if not at:
+            arrays.append(array)
+        places.append((at[0] if at else len(arrays) - 1, start, width))
+    after = [array for array in after if not any(array is other for other in arrays)]
     rows = arrays[0].shape[0]
     total = sum(width for _, _, width in parts)
     return pl.pallas_call(
-        functools.partial(join_kernel, [part[1:] for part in parts]),
+        functools.partial(join_kernel, places),
         out_shape=jax.ShapeDtypeStruct((rows, total), arrays[0].dtype),
         in_specs=[VMEM] * len(arrays) + [ANY] * len(after),
         out_specs=VMEM,
-        compiler_params=pltpu.CompilerParams(vmem_limit_bytes=2**20),
-        cost_estimate=pl.CostEstimate(flops=0, bytes_accessed=4 * rows * total, transcendentals=0),
+        compiler_params=pltpu.CompilerParams(vmem_limit_bytes=6 * 2**20),
+        cost_estimate=pl.CostEstimate(flops=3 * 10**10, bytes_accessed=0, transcendentals=0),
         name="join_columns",
     )(*arrays, *after)
 
@@ -258,141 +269,178 @@
     cots = {}
     lefts = {}
     ready = []
+    crossed = []
     tick = []
-
-    def send(axis, distance, parts, after=()):
-        message = join(parts, [*tick, *after])
+    flying = []
+    clock, number = [0.0], [0]
+
+    def start(axis, distance, parts, rate, channels, action):
+        message = join(parts, tick)
         tick[:] = [message]
-        return message, exchange(message, axis, distance)
+        size = 2 * tok_rows * sum(part[2] for part in parts)
+        clock[0] += start_time
+        number[0] += 1
+        end = clock[0] + latency + size / rate
+        flying.append((end, number[0], channels, exchange(message, axis, distance), action))
+        return message
+
+    def free(*channels):
+        busy = {channel for entry in flying for channel in entry[2]}
+        return len(flying) < most_flying and not busy & set(channels)
 
     def cot_parts(d):
         return [(*cots[d][s], columns) for s in slots]
 
-    def cots_at(array, start):
-        return [(array, start + s * columns) for s in slots]
+    def cots_at(array, first):
+        return [(array, first + s * columns) for s in slots]
 
     masked = mask(valid, user, cotangent, user_count)
     by_slot = [masked[0]] + [exchange(masked[s], "user", s) for s in range(1, user_count)]
     outgoing = pack(tok, hidden, list(range(tok_count)), own_width, [masked[0]])
-    ready += [(0, i, outgoing[0], start) for i, (start, _) in enumerate(pieces)]
-
-    far_steps = []
-    for i, (start, width) in enumerate(pieces):
-        for d in range(half, tok_count, 2):
-            far_steps.append([("block", e, i) for e in (d, d + 1)])
-    far_steps.insert(1, [("cots", half, 0), ("cots", half, 1)])
+    ready += [(0, i, outgoing[0], first) for i, (first, _) in enumerate(pieces)]
+
+    far = {
+        "A": [(None, None)] + [(d, None) for d in range(half + 2, tok_count - 1, 2)] + [(half, 1)],
+        "B": [(half, 0)]
+        + [(d, None) for d in range(half + 1, tok_count - 2, 2)]
+        + [(tok_count - 1, 0), (tok_count - 1, 1)],
+    }
     near = list(range(1, half))
-    near_steps = [near[:2]] + [near[i : i + 2] if tok_count > 8 else near[i : i + 1] for i in range(2, len(near), 2)]
-    relay_bits = [half >> i for i in range(1, half.bit_length())]
-
-    lanes_before = [None, None]
-    near_before, relay_before, cross_before, core_before = [], [], None, None
-    gradients = []
-    done = set()
-
-    def finish_core():
-        nonlocal core_before
-        if core_before is None:
-            return
-        blocks, own, other, both = core_before
-        core_before = None
+    relayed = {half}
+
+    def start_far(lane):
+        d, i = far[lane].pop(0)
+        if d is None:
+            parts = cot_parts(0)
+
+            def action(array):
+                cots[half] = cots_at(array, 0)
+
+        else:
+            first, width = pieces[i] if i is not None else (0, own_width)
+            parts = [(outgoing[d], first, width)]
+
+            def action(array):
+                for j, (at, _) in enumerate(pieces):
+                    if i is None or i == j:
+                        ready.append((d, j, array, at - first))
+
+        start("tok", half if d is None else d, parts, link_rate / 4, {lane}, action)
+
+    def start_near():
+        for d in near:
+            bits = {bit for bit in range(half.bit_length()) if d >> bit & 1}
+            if free(*bits):
+                near.remove(d)
+
+                def action(array, d=d):
+                    ready.extend((d, j, array, at) for j, (at, _) in enumerate(pieces))
+
+                start("tok", d, [(outgoing[d], 0, own_width)], link_rate, bits, action)
+                return True
+        for bit in range(half.bit_length() - 1):
+            step = 1 << bit
+            if step in near or not free(bit):
+                continue
+            sources = [d for d in cots if d % (2 * step) == 0 and d + step not in relayed]
+            if sources:
+                relayed.update(d + step for d in sources)
+                parts = [part for d in sources for part in cot_parts(d)]
+
+                def action(array, sources=sources, step=step):
+                    for at, d in enumerate(sources):
+                        cots[d + step] = cots_at(array, at * model_width)
+
+                start("tok", step, parts, link_rate, {bit}, action)
+                return True
+        return False
+
+    def start_across():
+        blocks, total = [], 0
+        while ready and total < 2 * own_width:
+            blocks.append(ready.pop(0))
+            total += pieces[blocks[-1][1]][1]
+        parts = [(array, first, pieces[i][1]) for _, i, array, first in blocks]
+        own = start(
+            "user", across, parts, link_rate, {"X"}, lambda other: crossed.append((blocks, own, other))
+        )
+
+    def start_core():
+        blocks, own, other = crossed.pop(0)
         total = sum(pieces[i][1] for _, i, _, _ in blocks)
-        to = 0
-        for d, i, _, _ in blocks:
-            lefts[d, i] = {0: (own, to), across: (other, to), core: (both, to), across ^ core: (both, total + to)}
-            to += pieces[i][1]
-
-    def add_products(step):
-        if len(cots) < tok_count:
-            return
+
+        def action(both):
+            to = 0
+            for d, i, _, _ in blocks:
+                lefts[d, i] = {
+                    0: (own, to),
+                    across: (other, to),
+                    core: (both, to),
+                    across ^ core: (both, total + to),
+                }
+                to += pieces[i][1]
+
+        parts = [(own, 0, total), (other, 0, total)]
+        start("user", core, parts, 6 * link_rate, {"C"}, action)
+
+    gradients = [None, None]
+    added = set()
+
+    def add_products():
+        ends = [entry[0] for entry in flying if entry[2] & {"A", "B"}]
         for i, (_, width) in enumerate(pieces):
-            here = [d for d in range(tok_count) if (d, i) in lefts and (d, i) not in done]
-            all_here = all((d, i) in lefts for d in range(tok_count))
-            if not here or not (all_here or (i == 1 and step >= len(far_steps))):
+            here = [d for d in cots if (d, i) in lefts and (d, i) not in added]
+            final = len(here) + len([1 for d, j in added if j == i]) == tok_count
+            early = gradients[i] is None and len(here) >= tok_count - 2 - i
+            if not here or not (final or early) or (final and i == 1 and gradients[0] is None):
                 continue
-            before = gradients[i] if len(gradients) > i else None
-            final = all_here and i == 1
+            time = product_time * width / own_width * (len(here) / tok_count + 0.5)
+            if not final and ends and min(ends) - clock[0] < time / 2:
+                continue
+            if final and i == 1 and len([1 for d, j in added if j == 0]) < tok_count:
+                continue
+            before = gradients[i]
             out = product(
                 [[lefts[d, i][s] for d in here] for s in slots],
                 [[cots[d][s] for d in here] for s in slots],
                 width,
                 columns,
                 held=before[0] if before else None,
-                sums=gradients[0][1] if final else None,
-                copies=0 if not all_here else tok_count * user_count if final else 1,
+                sums=gradients[0][1] if final and i == 1 else None,
+                copies=0 if not final else tok_count * user_count if i == 1 else 1,
             )
-            done.update((d, i) for d in here)
-            gradients[i : i + 1] = [out]
-            tick[:] = [out[0]]
-
-    for step in range(len(far_steps) + 2):
-        arrivals = []
-        for lane in (0, 1):
-            after = []
-            if lanes_before[lane] is not None:
-                after.append(lanes_before[lane][1])
-                arrivals.append(lanes_before[lane])
-                lanes_before[lane] = None
-            if step < len(far_steps):
-                kind, d, i = far_steps[step][lane]
-                if kind == "block":
-                    parts = [(outgoing[d], *pieces[i])]
-                else:
-                    parts = cot_parts(0)[lane * user_count // 2 : (lane + 1) * user_count // 2]
-                message = send("tok", d, parts, after)
-                lanes_before[lane] = (far_steps[step][lane], message[1])
-        for (kind, d, i), array in arrivals:
-            if kind == "block":
-                ready.append((d, i, array, 0))
-            else:
-                cots.setdefault(d, [])
-                cots[d] = cots[d] + [(array, s * columns) for s in range(user_count // 2)]
-        for d, array in near_before:
-            ready += [(d, i, array, start) for i, (start, _) in enumerate(pieces)]
-            if d & (d - 1) == 0:
-                cots[d] = cots_at(array, own_width)
-        for bit, sources, array in relay_before:
-            for at, d in enumerate(sources):
-                cots[d + bit] = cots_at(array, at * model_width)
-        near_before, relay_before = [], []
-        crossed = cross_before
-        cross_before = None
-        if ready:
-            blocks, ready = ready, []
-            parts = [(array, start, pieces[i][1]) for _, i, array, start in blocks]
-            own, other = send("user", across, parts, [crossed[2]] if crossed else [])
-            cross_before = (blocks, own, other)
-        if step == 0:
-            cots[0] = [(block, 0) for block in by_slot]
-            cots[0] = cots_at(join(cot_parts(0), []), 0)
-        if step < len(near_steps):
-            for d in near_steps[step]:
-                parts = [(outgoing[d], 0, own_width)]
-                if d & (d - 1) == 0:
-                    parts += cot_parts(0)
-                near_before.append((d, send("tok", d, parts)[1]))
-        if relay_bits:
-            bit = relay_bits[0]
-            sources = list(range(2 * bit, tok_count, 2 * bit))
-            if all(d in cots and len(cots[d]) == user_count for d in sources):
-                relay_bits.pop(0)
-                parts = [part for d in sources for part in cot_parts(d)]
-                relay_before.append((bit, sources, send("tok", bit, parts)[1]))
-        finish_core()
-        if crossed:
-            blocks, own, other = crossed
-            total = sum(pieces[i][1] for _, i, _, _ in blocks)
-            both = send("user", core, [(own, 0, total), (other, 0, total)])[1]
-            core_before = (blocks, own, other, both)
-        if step >= len(far_steps) - 1:
-            finish_core()
-            if relay_before:
-                for bit, sources, array in relay_before:
-                    for at, d in enumerate(sources):
-                        cots[d + bit] = cots_at(array, at * model_width)
-                relay_before = []
-            add_products(step)
-    sums = lax.all_to_all(gradients[1][1], ("user", "tok"), split_axis=0, concat_axis=0, tiled=True)
+            added.update((d, i) for d in here)
+            gradients[i] = out
+            tick.append(out[0])
+            clock[0] += time
+
+    start_far("B")
+    cots[0] = [(block, 0) for block in by_slot]
+    own_cots = join(cot_parts(0), tick)
+    tick[:] = [own_cots]
+    cots[0] = cots_at(own_cots, 0)
+    clock[0] += latency
+    while True:
+        for lane in ("B", "A"):
+            if far[lane] and free(lane):
+                start_far(lane)
+        if crossed and free("C"):
+            start_core()
+        if ready and free("X"):
+            start_across()
+        while start_near():
+            pass
+        if not flying:
+            break
+        entry = min(flying, key=lambda entry: entry[:2])
+        flying.remove(entry)
+        clock[0] = max(clock[0], entry[0])
+        tick.append(entry[3])
+        entry[4](entry[3])
+        add_products()
+    add_products()
+    sums = gradients[1][1]
+    sums = lax.all_to_all(sums, ("user", "tok"), split_axis=0, concat_axis=0, tiled=True)
     return combine(user, sums, [g[0] for g in gradients], clip_bound, scaling)
 
 

time: 209 us -> 218 us (1.043)
  Pallas kernels: 26 us -> 45.4 us
  waiting for transfers between devices: 125 us -> 107 us
  local copies, waits for them, and re-layouts: 3.22 us -> 12 us
  blocking collectives: 12.2 us -> 9.49 us
    ppermute x30 -> x37, waiting for transfers between devices: 125 us -> 107 us  [exchange(): return lax.ppermute(block, axis, [(i, i ^ distance) for i in range(size)])]
    pallas_call x28 -> x35, Pallas kernels: 1.4 us -> 12.8 us  [join(): pl.pallas_call(functools.partial(join_kernel, places), out_shape=jax.Shap...]
    unnamed x4 -> x82, local copies, waits for them, and re-layouts: 3.22 us -> 12 us
    pallas_call x3 -> x4, Pallas kernels: 19.4 us -> 27.4 us  [product(): pl.pallas_call(functools.partial(product_kernel, left_places, right_place...]
    all_to_all x1, blocking collectives: 12.2 us -> 9.49 us  [body(): lax.all_to_all(sums, ('user', 'tok'), split_axis=0, concat_axis=0, tiled=...]
    ppermute x30 -> x37, starting transfers between devices: 41.8 us -> 41.6 us  [exchange(): return lax.ppermute(block, axis, [(i, i ^ distance) for i in range(size)])]
  transfers between devices with their start and end apart: 30 -> 37, of which waited for: 17 -> 16; matrix products, arithmetic and copies ran while one was open for 0% -> 0% of each run, Pallas kernels for 8% -> 15%
where the time goes in v6:
time: 218 us; the launch traced here: 217 us
  waiting for transfers between devices  107 us (49%)
  Pallas kernels  45.4 us (21%)
  starting transfers between devices  41.6 us (19%)
  local copies, waits for them, and re-layouts  12 us (6%)
  blocking collectives  9.49 us (4%)
    ppermute x37, waiting for transfers between devices, exchange(): return lax.ppermute(block, axis, [(i, i ^ distance) for i in range(size)])  107 us
    ppermute x37, starting transfers between devices, exchange(): return lax.ppermute(block, axis, [(i, i ^ distance) for i in range(size)])  41.6 us
    pallas_call x4, Pallas kernels, product(): pl.pallas_call(functools.partial(product_kernel, left_places, right_place...  27.4 us
    pallas_call x35, Pallas kernels, join(): pl.pallas_call(functools.partial(join_kernel, places), out_shape=jax.Shap...  12.8 us
    unnamed x82, local copies, waits for them, and re-layouts  12 us
    all_to_all x1, blocking collectives, body(): lax.all_to_all(sums, ('user', 'tok'), split_axis=0, concat_axis=0, tiled=...  9.49 us
    pallas_call x1, Pallas kernels, combine(): pl.pallas_call(functools.partial(combine_kernel, user_count, clip_bound,...  4.81 us
  transfers between devices with their start and end apart: 37, of which 16 were waited for; matrix products, arithmetic and copies ran while one was open for 0% of the time, Pallas kernels for 15%

profile of v6, /device:TPU:0, one launch (start us, length us, event | category | flops | bytes accessed | tf_op | source)
XLA Modules:
  0.0 217.0 jit_solution(9265511113257506886)
XLA Ops:
  0.7 1.0 copy-done.32
  1.7 0.5 collective-permute-start
  2.3 2.6 %collective-permute-start.1 = (bf16[128,512]{1,0:T(8,128)(2,1)S(1)}, bf16[128,512]{1,0:T(8,128)(2,1)S(1)}, u32[]{:S(2)}, u32[]{:S(2)}) collective-permute-start(bf16[128,512]{1,0:T(8,128)(2,1)S(1)} %get-tuple-element.28), channel_id=1, source_target_pairs={{0,16},{8,24},{16,0},{24,8},{1,17},{9,25},{17,1},{25,9},{2,18},{10... | collective-permute-start | bytes 393224 | tf_op jit(solution)/shard_map/ppermute | solution.py:27
  4.9 2.2 %copy-done.6 = bf16[1,128,16384]{2,1,0:T(8,128)(2,1)S(1)} copy-done((bf16[1,128,16384]{2,1,0:T(8,128)(2,1)S(1)}, bf16[1,128,16384]{2,1,0:T(8,128)(2,1)}, u32[]{:S(2)}) %copy-start.6) | copy-done | bytes 4194328
  7.5 0.8 join_columns.35.refs_4_
  8.4 2.8 %collective-permute-start.7 = (bf16[128,1280]{1,0:T(8,128)(2,1)}, bf16[128,1280]{1,0:T(8,128)(2,1)}, u32[]{:S(2)}, u32[]{:S(2)}) collective-permute-start(bf16[128,1280]{1,0:T(8,128)(2,1)} %join_columns.35.refs_4_), channel_id=1, source_target_pairs={{0,4},{1,5},{2,6},{3,7},{4,0},{5,1},{6,2},{7,3},{8,12},{9,13},{10,... | collective-permute-start | bytes 983048 | tf_op jit(solution)/shard_map/ppermute | solution.py:27
  11.5 0.9 join_columns.37.refs_1_
  12.5 2.7 %collective-permute-start.12 = (bf16[128,2048]{1,0:T(8,128)(2,1)}, bf16[128,2048]{1,0:T(8,128)(2,1)}, u32[]{:S(2)}, u32[]{:S(2)}) collective-permute-start(bf16[128,2048]{1,0:T(8,128)(2,1)} %join_columns.37.refs_1_), channel_id=1, source_target_pairs={{0,4},{1,5},{2,6},{3,7},{4,0},{5,1},{6,2},{7,3},{8,12},{9,13},{10,... | collective-permute-start | bytes 1572872 | tf_op jit(solution)/shard_map/ppermute | solution.py:27
  15.2 1.6 collective-permute-start.4
  16.8 1.6 collective-permute-start.3
  18.5 1.6 collective-permute-start.5
  20.1 9.0 %collective-permute-done.4.refs_1_.refs_10_ = bf16[128,2048]{1,0:T(8,128)(2,1)S(1)} collective-permute-done((bf16[128,2048]{1,0:T(8,128)(2,1)S(1)}, bf16[128,2048]{1,0:T(8,128)(2,1)S(1)}, u32[]{:S(2)}, u32[]{:S(2)}) %collective-permute-start.4) | collective-permute-done | bytes 524320 | tf_op jit(solution)/shard_map/ppermute | solution.py:27
  29.2 0.8 copy-done.12
  30.5 1.2 collective-permute-start.10
  31.7 9.7 %collective-permute-done.5.refs_2_.refs_0_ = bf16[128,2048]{1,0:T(8,128)(2,1)S(1)} collective-permute-done((bf16[128,2048]{1,0:T(8,128)(2,1)S(1)}, bf16[128,2048]{1,0:T(8,128)(2,1)S(1)}, u32[]{:S(2)}, u32[]{:S(2)}) %collective-permute-start.5) | collective-permute-done | bytes 524320 | tf_op jit(solution)/shard_map/ppermute | solution.py:27
  41.4 3.5 %collective-permute-start.9 = (bf16[128,2048]{1,0:T(8,128)(2,1)S(1)}, bf16[128,2048]{1,0:T(8,128)(2,1)S(1)}, u32[]{:S(2)}, u32[]{:S(2)}) collective-permute-start(bf16[128,2048]{1,0:T(8,128)(2,1)S(1)} %join_columns.43.refs_1_), channel_id=1, source_target_pairs={{0,3},{1,2},{2,1},{3,0},{4,7},{5,6},{6,5},{7,4},{8,11},{9,10},{10,... | collective-permute-start | bytes 1572872 | tf_op jit(solution)/shard_map/ppermute | solution.py:27
  45.0 1.0 copy-done.2
  46.0 0.8 copy-done.16
  46.8 0.8 copy-done.37
  47.6 2.0 join_columns.46.refs_1_.refs_0_.refs_2_
  49.6 1.5 collective-permute-start.11
  51.1 10.2 %collective-permute-done.9.refs_2_.refs_0_ = bf16[128,2048]{1,0:T(8,128)(2,1)S(1)} collective-permute-done((bf16[128,2048]{1,0:T(8,128)(2,1)S(1)}, bf16[128,2048]{1,0:T(8,128)(2,1)S(1)}, u32[]{:S(2)}, u32[]{:S(2)}) %collective-permute-start.9) | collective-permute-done | bytes 524320 | tf_op jit(solution)/shard_map/ppermute | solution.py:27
  61.4 0.8 copy-done.39
  62.7 0.9 copy-done.4
  63.6 0.8 join_columns.49.refs_1_
  64.4 11.6 %collective-permute-done.14.refs_2_.refs_17_.refs_16_ = bf16[128,2048]{1,0:T(8,128)(2,1)S(1)} collective-permute-done((bf16[128,2048]{1,0:T(8,128)(2,1)S(1)}, bf16[128,2048]{1,0:T(8,128)(2,1)S(1)}, u32[]{:S(2)}, u32[]{:S(2)}) %collective-permute-start.14) | collective-permute-done | bytes 524320 | tf_op jit(solution)/shard_map/ppermute | solution.py:27
  76.0 1.3 join_columns.50.refs_1_
  77.3 1.3 join_columns.51.refs_2_
  78.6 1.6 join_columns.52.refs_1_
  80.3 3.2 %collective-permute-start.8 = (bf16[128,2048]{1,0:T(8,128)(2,1)S(1)}, bf16[128,2048]{1,0:T(8,128)(2,1)S(1)}, u32[]{:S(2)}, u32[]{:S(2)}) collective-permute-start(bf16[128,2048]{1,0:T(8,128)(2,1)S(1)} %copy-done.38), channel_id=1, source_target_pairs={{0,5},{1,4},{2,7},{3,6},{4,1},{5,0},{6,3},{7,2},{8,13},{9,12},{10,... | collective-permute-start | bytes 1572872 | tf_op jit(solution)/shard_map/ppermute | solution.py:27
  84.1 1.3 collective-permute-start.24
  85.4 0.5 collective-permute-start.19
  86.0 1.1 copy-done
  87.1 1.5 collective-permute-start.17
  88.6 9.0 %collective-permute-done.18.refs_2_.refs_19_.refs_18_ = bf16[128,2048]{1,0:T(8,128)(2,1)S(1)} collective-permute-done((bf16[128,2048]{1,0:T(8,128)(2,1)S(1)}, bf16[128,2048]{1,0:T(8,128)(2,1)S(1)}, u32[]{:S(2)}, u32[]{:S(2)}) %collective-permute-start.18) | collective-permute-done | bytes 524320 | tf_op jit(solution)/shard_map/ppermute | solution.py:27
  97.6 0.7 copy-done.22
  98.4 0.6 collective-permute-start.21
  99.0 20.5 %collective-permute-done.8.refs_3_.refs_0_ = bf16[128,2048]{1,0:T(8,128)(2,1)S(1)} collective-permute-done((bf16[128,2048]{1,0:T(8,128)(2,1)S(1)}, bf16[128,2048]{1,0:T(8,128)(2,1)S(1)}, u32[]{:S(2)}, u32[]{:S(2)}) %collective-permute-start.8) | collective-permute-done | bytes 524320 | tf_op jit(solution)/shard_map/ppermute | solution.py:27
  119.5 1.9 collective-permute-done.19.refs_2_.refs_0_.refs_6_.refs_10_
  121.4 0.8 join_columns.55.refs_2_
  122.2 3.3 %collective-permute-start.26 = (bf16[128,1280]{1,0:T(8,128)(2,1)}, bf16[128,1280]{1,0:T(8,128)(2,1)}, u32[]{:S(2)}, u32[]{:S(2)}) collective-permute-start(bf16[128,1280]{1,0:T(8,128)(2,1)} %join_columns.55.refs_2_), channel_id=1, source_target_pairs={{0,7},{1,6},{2,5},{3,4},{4,3},{5,2},{6,1},{7,0},{8,15},{9,14},{10,... | collective-permute-start | bytes 983048 | tf_op jit(solution)/shard_map/ppermute | solution.py:27
  125.5 0.7 copy-done.26
  126.3 1.6 collective-permute-start.20
  127.9 0.6 collective-permute-start.23
  128.5 12.2 %collective-permute-done.20.refs_1_.refs_13_ = bf16[128,2048]{1,0:T(8,128)(2,1)S(1)} collective-permute-done((bf16[128,2048]{1,0:T(8,128)(2,1)S(1)}, bf16[128,2048]{1,0:T(8,128)(2,1)S(1)}, u32[]{:S(2)}, u32[]{:S(2)}) %collective-permute-start.20) | collective-permute-done | bytes 524320 | tf_op jit(solution)/shard_map/ppermute | solution.py:27
  140.8 4.1 %collective-permute-done.23.refs_2_.refs_7_.refs_11_ = bf16[128,2048]{1,0:T(8,128)(2,1)S(1)} collective-permute-done((bf16[128,2048]{1,0:T(8,128)(2,1)S(1)}, bf16[128,2048]{1,0:T(8,128)(2,1)S(1)}, u32[]{:S(2)}, u32[]{:S(2)}) %collective-permute-start.23) | collective-permute-done | bytes 524320 | tf_op jit(solution)/shard_map/ppermute | solution.py:27
  145.1 1.3 join_columns.61.refs_1_.refs_0_
  146.5 1.6 collective-permute-start.27
  148.9 10.0 %product_and_squares.4.refs_3_.refs_8_ = f32[4,1280,512]{2,1,0:T(8,128)S(1)} custom-call(bf16[128,2048]{1,0:T(8,128)(2,1)S(1)} %copy-done.11, bf16[128,3328]{1,0:T(8,128)(2,1)} %join_columns.46.refs_1_.refs_0_.refs_2_, bf16[128,2048]{1,0:T(8,128)(2,1)S(1)} %copy-done.15, bf16[128,2048]{1,0:T(8,128)(2,1)S(1)} %join_columns.57.refs_1_.refs_0_.refs_3_, ...), custom_call_target="tpu_custom_call" | custom-call | flops 4026531840 | bytes 11010048 | tf_op jit(solution)/shard_map/product_and_squares/pallas_call | solution.py:180
  158.9 1.5 collective-permute-done.27.refs_1_.refs_4_.refs_7_
  160.6 1.0 join_columns.64.refs_0_.refs_1_
  161.6 1.6 collective-permute-start.29
  163.1 3.4 %collective-permute-start.31 = (bf16[128,768]{1,0:T(8,128)(2,1)S(1)}, bf16[128,768]{1,0:T(8,128)(2,1)S(1)}, u32[]{:S(2)}, u32[]{:S(2)}) collective-permute-start(bf16[128,768]{1,0:T(8,128)(2,1)S(1)} %join_columns.62.refs_2_), channel_id=1, source_target_pairs={{0,7},{1,6},{2,5},{3,4},{4,3},{5,2},{6,1},{7,0},{8,15},{9,14},{10,... | collective-permute-start | bytes 589832 | tf_op jit(solution)/shard_map/ppermute | solution.py:27
  166.5 6.4 %product_and_squares.5.refs_3_.refs_12_ = f32[4,768,512]{2,1,0:T(8,128)S(1)} custom-call(bf16[128,2048]{1,0:T(8,128)(2,1)S(1)} %copy-done.11, bf16[128,2048]{1,0:T(8,128)(2,1)S(1)} %copy-done.15, bf16[128,3328]{1,0:T(8,128)(2,1)} %join_columns.46.refs_1_.refs_0_.refs_2_, bf16[128,2048]{1,0:T(8,128)(2,1)S(1)} %join_columns.57.refs_1_.refs_0_.refs_3_, ...), custom_call_target="tpu_custom_call" | custom-call | flops 2013265920 | bytes 6553600 | tf_op jit(solution)/shard_map/product_and_squares/pallas_call | solution.py:180
  172.9 7.2 %collective-permute-done.25.refs_2_.refs_0_ = bf16[128,768]{1,0:T(8,128)(2,1)S(1)} collective-permute-done((bf16[128,768]{1,0:T(8,128)(2,1)S(1)}, bf16[128,768]{1,0:T(8,128)(2,1)S(1)}, u32[]{:S(2)}, u32[]{:S(2)}) %collective-permute-start.25) | collective-permute-done | bytes 196640 | tf_op jit(solution)/shard_map/ppermute | solution.py:27
  180.2 0.7 collective-permute-start.32
  181.0 1.4 collective-permute-done.33.refs_3_.refs_2_
  182.3 5.7 %product_and_squares.6 = (f32[4,1280,512]{2,1,0:T(8,128)S(1)}, f32[1,8,128]{2,1,0:T(8,128)S(1)}) custom-call(bf16[128,2048]{1,0:T(8,128)(2,1)S(1)} %join_columns.61.refs_1_.refs_0_, bf16[128,1280]{1,0:T(8,128)(2,1)S(1)} %join_columns.64.refs_0_.refs_1_, ...), custom_call_target="tpu_custom_call", output_to_operand_aliasing={{0}: (8, {})} | custom-call | flops 1342177280 | bytes 3670016 | tf_op jit(solution)/shard_map/product_and_squares/pallas_call | solution.py:180
  188.3 0.7 collective-permute-start.35
  189.0 6.5 %collective-permute-done.35.refs_1_.refs_8_ = bf16[128,768]{1,0:T(8,128)(2,1)S(1)} collective-permute-done((bf16[128,768]{1,0:T(8,128)(2,1)S(1)}, bf16[128,768]{1,0:T(8,128)(2,1)S(1)}, u32[]{:S(2)}, u32[]{:S(2)}) %collective-permute-start.35) | collective-permute-done | bytes 196640 | tf_op jit(solution)/shard_map/ppermute | solution.py:27
  195.6 1.7 collective-permute-done.36.refs_5_
  197.4 5.4 %product_and_squares.7 = (f32[4,768,512]{2,1,0:T(8,128)S(1)}, f32[32,8,128]{2,1,0:T(8,128)S(1)}) custom-call(bf16[128,768]{1,0:T(8,128)(2,1)S(1)} %join_columns.66.refs_0_, bf16[128,2048]{1,0:T(8,128)(2,1)S(1)} %join_columns.61.refs_1_.refs_0_, bf16[128,768]{1,0:T(8,128)(2,1)S(1)} %join_columns.68.refs_0_.refs_2_, ...), custom_call_target="tpu_custom_call", output_to_operand_aliasing={{0}: (12, {})} | custom-call | flops 1207959552 | bytes 3932160 | tf_op jit(solution)/shard_map/product_and_squares/pallas_call | solution.py:180
  202.7 9.5 %all_to_all.5.sums_ref = f32[32,8,128]{2,1,0:T(8,128)S(1)} all-to-all(f32[32,8,128]{2,1,0:T(8,128)S(1)} %get-tuple-element.35), channel_id=1, replica_groups=mesh['user'=4,'tok'=8] {'user','tok'}, dimensions={0} | all-to-all | bytes 262144 | tf_op jit(solution)/shard_map/all_to_all | solution.py:443
  212.2 4.8 %weighted_sum.1 = f32[2048,512]{1,0:T(8,128)} custom-call(s32[1]{0:T(128)} %bitcast.user_ref, f32[32,8,128]{2,1,0:T(8,128)S(1)} %all_to_all.5.sums_ref, f32[4,1280,512]{2,1,0:T(8,128)S(1)} %get-tuple-element.33.refs_3_.refs_0_, f32[4,768,512]{2,1,0:T(8,128)S(1)} %get-tuple-element.36.refs_1_), custom_call_target="tpu_custom_call" | custom-call | tf_op jit(solution)/shard_map/weighted_sum/pallas_call | solution.py:237
  (135 shorter events, 4.8 us)
Async XLA Ops:
  1.7 9.5 %collective-permute-start = (bf16[128,512]{1,0:T(8,128)(2,1)S(1)}, bf16[128,512]{1,0:T(8,128)(2,1)S(1)}, u32[]{:S(2)}, u32[]{:S(2)}) collective-permute-start(bf16[128,512]{1,0:T(8,128)(2,1)S(1)} %get-tuple-element.27), channel_id=1, source_target_pairs={{0,8},{8,0},{16,24},{24,16},{1,9},{9,1},{17,25},{25,17},{2,10},{10... | collective-permute-start | bytes 393224 | tf_op jit(solution)/shard_map/ppermute | solution.py:27
  2.3 8.9 %collective-permute-start.1 = (bf16[128,512]{1,0:T(8,128)(2,1)S(1)}, bf16[128,512]{1,0:T(8,128)(2,1)S(1)}, u32[]{:S(2)}, u32[]{:S(2)}) collective-permute-start(bf16[128,512]{1,0:T(8,128)(2,1)S(1)} %get-tuple-element.28), channel_id=1, source_target_pairs={{0,16},{8,24},{16,0},{24,8},{1,17},{9,25},{17,1},{25,9},{2,18},{10... | collective-permute-start | bytes 393224 | tf_op jit(solution)/shard_map/ppermute | solution.py:27
  4.8 6.6 %collective-permute-start.2 = (bf16[128,512]{1,0:T(8,128)(2,1)S(1)}, bf16[128,512]{1,0:T(8,128)(2,1)S(1)}, u32[]{:S(2)}, u32[]{:S(2)}) collective-permute-start(bf16[128,512]{1,0:T(8,128)(2,1)S(1)} %get-tuple-element.29), channel_id=1, source_target_pairs={{0,24},{8,16},{16,8},{24,0},{1,25},{9,17},{17,9},{25,1},{2,26},{10... | collective-permute-start | bytes 393224 | tf_op jit(solution)/shard_map/ppermute | solution.py:27
  4.9 2.2 %copy-start.6 = (bf16[1,128,16384]{2,1,0:T(8,128)(2,1)S(1)}, bf16[1,128,16384]{2,1,0:T(8,128)(2,1)}, u32[]{:S(2)}) copy-start(bf16[1,128,16384]{2,1,0:T(8,128)(2,1)} %hidden_ref.1) | copy-start | bytes 12582916
  7.5 113.9 %copy-start.33 = (bf16[128,2048]{1,0:T(8,128)(2,1)}, bf16[128,2048]{1,0:T(8,128)(2,1)S(1)}, u32[]{:S(2)}) copy-start(bf16[128,2048]{1,0:T(8,128)(2,1)S(1)} %get-tuple-element.32.refs_0_) | copy-start | bytes 1572868
  8.4 36.6 %collective-permute-start.7 = (bf16[128,1280]{1,0:T(8,128)(2,1)}, bf16[128,1280]{1,0:T(8,128)(2,1)}, u32[]{:S(2)}, u32[]{:S(2)}) collective-permute-start(bf16[128,1280]{1,0:T(8,128)(2,1)} %join_columns.35.refs_4_), channel_id=1, source_target_pairs={{0,4},{1,5},{2,6},{3,7},{4,0},{5,1},{6,2},{7,3},{8,12},{9,13},{10,... | collective-permute-start | bytes 983048 | tf_op jit(solution)/shard_map/ppermute | solution.py:27
  12.5 51.1 %collective-permute-start.12 = (bf16[128,2048]{1,0:T(8,128)(2,1)}, bf16[128,2048]{1,0:T(8,128)(2,1)}, u32[]{:S(2)}, u32[]{:S(2)}) collective-permute-start(bf16[128,2048]{1,0:T(8,128)(2,1)} %join_columns.37.refs_1_), channel_id=1, source_target_pairs={{0,4},{1,5},{2,6},{3,7},{4,0},{5,1},{6,2},{7,3},{8,12},{9,13},{10,... | collective-permute-start | bytes 1572872 | tf_op jit(solution)/shard_map/ppermute | solution.py:27
  15.2 13.9 %copy-start.10 = (bf16[128,2048]{1,0:T(8,128)(2,1)}, bf16[128,2048]{1,0:T(8,128)(2,1)S(1)}, u32[]{:S(2)}) copy-start(bf16[128,2048]{1,0:T(8,128)(2,1)S(1)} %join_columns.38.refs_1_.refs_0_) | copy-start | bytes 1572868
  15.2 13.9 %collective-permute-start.4 = (bf16[128,2048]{1,0:T(8,128)(2,1)S(1)}, bf16[128,2048]{1,0:T(8,128)(2,1)S(1)}, u32[]{:S(2)}, u32[]{:S(2)}) collective-permute-start(bf16[128,2048]{1,0:T(8,128)(2,1)S(1)} %join_columns.38.refs_1_.refs_0_), channel_id=1, source_target_pairs={{0,16},{8,24},{16,0},{24,8},{1,17},{9,25},{17,1},{25,9},{2,18},{10... | collective-permute-start | bytes 1572872 | tf_op jit(solution)/shard_map/ppermute | solution.py:27
  16.8 13.6 %collective-permute-start.3 = (bf16[128,2048]{1,0:T(8,128)(2,1)S(1)}, bf16[128,2048]{1,0:T(8,128)(2,1)S(1)}, u32[]{:S(2)}, u32[]{:S(2)}) collective-permute-start(bf16[128,2048]{1,0:T(8,128)(2,1)S(1)} %join_columns.39.refs_1_), channel_id=1, source_target_pairs={{0,1},{1,0},{2,3},{3,2},{4,5},{5,4},{6,7},{7,6},{8,9},{9,8},{10,11... | collective-permute-start | bytes 1572872 | tf_op jit(solution)/shard_map/ppermute | solution.py:27
  18.5 22.9 %collective-permute-start.5 = (bf16[128,2048]{1,0:T(8,128)(2,1)S(1)}, bf16[128,2048]{1,0:T(8,128)(2,1)S(1)}, u32[]{:S(2)}, u32[]{:S(2)}) collective-permute-start(bf16[128,2048]{1,0:T(8,128)(2,1)S(1)} %join_columns.40.refs_2_), channel_id=1, source_target_pairs={{0,2},{1,3},{2,0},{3,1},{4,6},{5,7},{6,4},{7,5},{8,10},{9,11},{10,... | collective-permute-start | bytes 1572872 | tf_op jit(solution)/shard_map/ppermute | solution.py:27
  30.1 14.9 %collective-permute-start.6 = (bf16[128,4096]{1,0:T(8,128)(2,1)S(1)}, bf16[128,4096]{1,0:T(8,128)(2,1)S(1)}, u32[]{:S(2)}, u32[]{:S(2)}) collective-permute-start(bf16[128,4096]{1,0:T(8,128)(2,1)S(1)} %join_columns.41.refs_1_), channel_id=1, source_target_pairs={{0,8},{8,0},{16,24},{24,16},{1,9},{9,1},{17,25},{25,17},{2,10},{10... | collective-permute-start | bytes 3145736 | tf_op jit(solution)/shard_map/ppermute | solution.py:27
  30.5 15.5 %copy-start.14 = (bf16[128,2048]{1,0:T(8,128)(2,1)}, bf16[128,2048]{1,0:T(8,128)(2,1)S(1)}, u32[]{:S(2)}) copy-start(bf16[128,2048]{1,0:T(8,128)(2,1)S(1)} %join_columns.42.refs_1_.refs_0_.refs_2_) | copy-start | bytes 1572868
  30.5 15.5 %collective-permute-start.10 = (bf16[128,2048]{1,0:T(8,128)(2,1)S(1)}, bf16[128,2048]{1,0:T(8,128)(2,1)S(1)}, u32[]{:S(2)}, u32[]{:S(2)}) collective-permute-start(bf16[128,2048]{1,0:T(8,128)(2,1)S(1)} %join_columns.42.refs_1_.refs_0_.refs_2_), channel_id=1, source_target_pairs={{0,16},{8,24},{16,0},{24,8},{1,17},{9,25},{17,1},{25,9},{2,18},{10... | collective-permute-start | bytes 1572872 | tf_op jit(solution)/shard_map/ppermute | solution.py:27
  41.4 19.9 %collective-permute-start.9 = (bf16[128,2048]{1,0:T(8,128)(2,1)S(1)}, bf16[128,2048]{1,0:T(8,128)(2,1)S(1)}, u32[]{:S(2)}, u32[]{:S(2)}) collective-permute-start(bf16[128,2048]{1,0:T(8,128)(2,1)S(1)} %join_columns.43.refs_1_), channel_id=1, source_target_pairs={{0,3},{1,2},{2,1},{3,0},{4,7},{5,6},{6,5},{7,4},{8,11},{9,10},{10,... | collective-permute-start | bytes 1572872 | tf_op jit(solution)/shard_map/ppermute | solution.py:27
  47.6 13.7 %copy-start.8 = (bf16[128,2048]{1,0:T(8,128)(2,1)S(1)}, bf16[128,2048]{1,0:T(8,128)(2,1)}, u32[]{:S(2)}) copy-start(bf16[128,2048]{1,0:T(8,128)(2,1)} %copy-done.7) | copy-start | bytes 1572868
  47.6 15.0 %collective-permute-start.13 = (bf16[128,4096]{1,0:T(8,128)(2,1)S(1)}, bf16[128,4096]{1,0:T(8,128)(2,1)S(1)}, u32[]{:S(2)}, u32[]{:S(2)}) collective-permute-start(bf16[128,4096]{1,0:T(8,128)(2,1)S(1)} %join_columns.45.refs_2_), channel_id=1, source_target_pairs={{0,8},{8,0},{16,24},{24,16},{1,9},{9,1},{17,25},{25,17},{2,10},{10... | collective-permute-start | bytes 3145736 | tf_op jit(solution)/shard_map/ppermute | solution.py:27
  49.6 29.0 %collective-permute-start.11 = (bf16[128,3328]{1,0:T(8,128)(2,1)}, bf16[128,3328]{1,0:T(8,128)(2,1)}, u32[]{:S(2)}, u32[]{:S(2)}) collective-permute-start(bf16[128,3328]{1,0:T(8,128)(2,1)} %join_columns.46.refs_1_.refs_0_.refs_2_), channel_id=1, source_target_pairs={{0,16},{8,24},{16,0},{24,8},{1,17},{9,25},{17,1},{25,9},{2,18},{10... | collective-permute-start | bytes 2555912 | tf_op jit(solution)/shard_map/ppermute | solution.py:27
  62.2 13.8 %collective-permute-start.14 = (bf16[128,2048]{1,0:T(8,128)(2,1)S(1)}, bf16[128,2048]{1,0:T(8,128)(2,1)S(1)}, u32[]{:S(2)}, u32[]{:S(2)}) collective-permute-start(bf16[128,2048]{1,0:T(8,128)(2,1)S(1)} %join_columns.47.refs_1_), channel_id=1, source_target_pairs={{0,1},{1,0},{2,3},{3,2},{4,5},{5,4},{6,7},{7,6},{8,9},{9,8},{10,11... | collective-permute-start | bytes 1572872 | tf_op jit(solution)/shard_map/ppermute | solution.py:27
  63.6 13.7 %collective-permute-start.15 = (bf16[128,2048]{1,0:T(8,128)(2,1)S(1)}, bf16[128,2048]{1,0:T(8,128)(2,1)S(1)}, u32[]{:S(2)}, u32[]{:S(2)}) collective-permute-start(bf16[128,2048]{1,0:T(8,128)(2,1)S(1)} %join_columns.48.refs_1_), channel_id=1, source_target_pairs={{0,2},{1,3},{2,0},{3,1},{4,6},{5,7},{6,4},{7,5},{8,10},{9,11},{10,... | collective-permute-start | bytes 1572872 | tf_op jit(solution)/shard_map/ppermute | solution.py:27
  77.3 20.3 %copy-start.20 = (bf16[128,2048]{1,0:T(8,128)(2,1)}, bf16[128,2048]{1,0:T(8,128)(2,1)S(1)}, u32[]{:S(2)}) copy-start(bf16[128,2048]{1,0:T(8,128)(2,1)S(1)} %collective-permute-done.15.refs_2_.refs_0_.refs_18_.refs_17_) | copy-start | bytes 1572868
  78.6 7.3 %copy-start.40 = (bf16[128,2048]{1,0:T(8,128)(2,1)S(1)}, bf16[128,2048]{1,0:T(8,128)(2,1)}, u32[]{:S(2)}) copy-start(bf16[128,2048]{1,0:T(8,128)(2,1)} %copy-done.39) | copy-start | bytes 1572868
  80.2 5.7 %collective-permute-start.16 = (bf16[128,6656]{1,0:T(8,128)(2,1)S(1)}, bf16[128,6656]{1,0:T(8,128)(2,1)S(1)}, u32[]{:S(2)}, u32[]{:S(2)}) collective-permute-start(bf16[128,6656]{1,0:T(8,128)(2,1)S(1)} %join_columns.52.refs_1_), channel_id=1, source_target_pairs={{0,8},{8,0},{16,24},{24,16},{1,9},{9,1},{17,25},{25,17},{2,10},{10... | collective-permute-start | bytes 5111816 | tf_op jit(solution)/shard_map/ppermute | solution.py:27
  80.3 39.2 %collective-permute-start.8 = (bf16[128,2048]{1,0:T(8,128)(2,1)S(1)}, bf16[128,2048]{1,0:T(8,128)(2,1)S(1)}, u32[]{:S(2)}, u32[]{:S(2)}) collective-permute-start(bf16[128,2048]{1,0:T(8,128)(2,1)S(1)} %copy-done.38), channel_id=1, source_target_pairs={{0,5},{1,4},{2,7},{3,6},{4,1},{5,0},{6,3},{7,2},{8,13},{9,12},{10,... | collective-permute-start | bytes 1572872 | tf_op jit(solution)/shard_map/ppermute | solution.py:27
  83.6 14.0 %collective-permute-start.18 = (bf16[128,2048]{1,0:T(8,128)(2,1)S(1)}, bf16[128,2048]{1,0:T(8,128)(2,1)S(1)}, u32[]{:S(2)}, u32[]{:S(2)}) collective-permute-start(bf16[128,2048]{1,0:T(8,128)(2,1)S(1)} %join_columns.50.refs_1_), channel_id=1, source_target_pairs={{0,1},{1,0},{2,3},{3,2},{4,5},{5,4},{6,7},{7,6},{8,9},{9,8},{10,11... | collective-permute-start | bytes 1572872 | tf_op jit(solution)/shard_map/ppermute | solution.py:27
  84.1 56.8 %collective-permute-start.24 = (bf16[128,2048]{1,0:T(8,128)(2,1)}, bf16[128,2048]{1,0:T(8,128)(2,1)}, u32[]{:S(2)}, u32[]{:S(2)}) collective-permute-start(bf16[128,2048]{1,0:T(8,128)(2,1)} %join_columns.49.refs_1_), channel_id=1, source_target_pairs={{0,6},{1,7},{2,4},{3,5},{4,2},{5,3},{6,0},{7,1},{8,14},{9,15},{10,... | collective-permute-start | bytes 1572872 | tf_op jit(solution)/shard_map/ppermute | solution.py:27
  85.4 36.0 %collective-permute-start.19 = (bf16[128,2048]{1,0:T(8,128)(2,1)S(1)}, bf16[128,2048]{1,0:T(8,128)(2,1)S(1)}, u32[]{:S(2)}, u32[]{:S(2)}) collective-permute-start(bf16[128,2048]{1,0:T(8,128)(2,1)S(1)} %join_columns.51.refs_2_), channel_id=1, source_target_pairs={{0,2},{1,3},{2,0},{3,1},{4,6},{5,7},{6,4},{7,5},{8,10},{9,11},{10,... | collective-permute-start | bytes 1572872 | tf_op jit(solution)/shard_map/ppermute | solution.py:27
  87.1 38.3 %copy-start.24 = (bf16[128,2048]{1,0:T(8,128)(2,1)}, bf16[128,2048]{1,0:T(8,128)(2,1)S(1)}, u32[]{:S(2)}) copy-start(bf16[128,2048]{1,0:T(8,128)(2,1)S(1)} %join_columns.53.refs_1_.refs_0_.refs_4_) | copy-start | bytes 1572868
  87.1 38.3 %collective-permute-start.17 = (bf16[128,2048]{1,0:T(8,128)(2,1)S(1)}, bf16[128,2048]{1,0:T(8,128)(2,1)S(1)}, u32[]{:S(2)}, u32[]{:S(2)}) collective-permute-start(bf16[128,2048]{1,0:T(8,128)(2,1)S(1)} %join_columns.53.refs_1_.refs_0_.refs_4_), channel_id=1, source_target_pairs={{0,16},{8,24},{16,0},{24,8},{1,17},{9,25},{17,1},{25,9},{2,18},{10... | collective-permute-start | bytes 1572872 | tf_op jit(solution)/shard_map/ppermute | solution.py:27
  98.4 29.4 %collective-permute-start.21 = (bf16[128,2048]{1,0:T(8,128)(2,1)S(1)}, bf16[128,2048]{1,0:T(8,128)(2,1)S(1)}, u32[]{:S(2)}, u32[]{:S(2)}) collective-permute-start(bf16[128,2048]{1,0:T(8,128)(2,1)S(1)} %join_columns.54.refs_1_), channel_id=1, source_target_pairs={{0,1},{1,0},{2,3},{3,2},{4,5},{5,4},{6,7},{7,6},{8,9},{9,8},{10,11... | collective-permute-start | bytes 1572872 | tf_op jit(solution)/shard_map/ppermute | solution.py:27
  121.4 6.5 %copy-start.28 = (bf16[128,2048]{1,0:T(8,128)(2,1)}, bf16[128,2048]{1,0:T(8,128)(2,1)S(1)}, u32[]{:S(2)}) copy-start(bf16[128,2048]{1,0:T(8,128)(2,1)S(1)} %collective-permute-done.19.refs_2_.refs_0_.refs_6_.refs_10_) | copy-start | bytes 1572868
  122.2 36.7 %collective-permute-start.26 = (bf16[128,1280]{1,0:T(8,128)(2,1)}, bf16[128,1280]{1,0:T(8,128)(2,1)}, u32[]{:S(2)}, u32[]{:S(2)}) collective-permute-start(bf16[128,1280]{1,0:T(8,128)(2,1)} %join_columns.55.refs_2_), channel_id=1, source_target_pairs={{0,7},{1,6},{2,5},{3,4},{4,3},{5,2},{6,1},{7,0},{8,15},{9,14},{10,... | collective-permute-start | bytes 983048 | tf_op jit(solution)/shard_map/ppermute | solution.py:27
  126.2 14.4 %collective-permute-start.22 = (bf16[128,4096]{1,0:T(8,128)(2,1)S(1)}, bf16[128,4096]{1,0:T(8,128)(2,1)S(1)}, u32[]{:S(2)}, u32[]{:S(2)}) collective-permute-start(bf16[128,4096]{1,0:T(8,128)(2,1)S(1)} %join_columns.56.refs_1_), channel_id=1, source_target_pairs={{0,8},{8,0},{16,24},{24,16},{1,9},{9,1},{17,25},{25,17},{2,10},{10... | collective-permute-start | bytes 3145736 | tf_op jit(solution)/shard_map/ppermute | solution.py:27
  126.3 14.4 %collective-permute-start.20 = (bf16[128,2048]{1,0:T(8,128)(2,1)S(1)}, bf16[128,2048]{1,0:T(8,128)(2,1)S(1)}, u32[]{:S(2)}, u32[]{:S(2)}) collective-permute-start(bf16[128,2048]{1,0:T(8,128)(2,1)S(1)} %join_columns.57.refs_1_.refs_0_.refs_3_), channel_id=1, source_target_pairs={{0,16},{8,24},{16,0},{24,8},{1,17},{9,25},{17,1},{25,9},{2,18},{10... | collective-permute-start | bytes 1572872 | tf_op jit(solution)/shard_map/ppermute | solution.py:27
  127.9 17.1 %copy-start.36 = (bf16[128,2048]{1,0:T(8,128)(2,1)S(1)}, bf16[128,2048]{1,0:T(8,128)(2,1)}, u32[]{:S(2)}) copy-start(bf16[128,2048]{1,0:T(8,128)(2,1)} %copy-done.35) | copy-start | bytes 1572868
  127.9 17.1 %collective-permute-start.23 = (bf16[128,2048]{1,0:T(8,128)(2,1)S(1)}, bf16[128,2048]{1,0:T(8,128)(2,1)S(1)}, u32[]{:S(2)}, u32[]{:S(2)}) collective-permute-start(bf16[128,2048]{1,0:T(8,128)(2,1)S(1)} %join_columns.58.refs_2_), channel_id=1, source_target_pairs={{0,1},{1,0},{2,3},{3,2},{4,5},{5,4},{6,7},{7,6},{8,9},{9,8},{10,11... | collective-permute-start | bytes 1572872 | tf_op jit(solution)/shard_map/ppermute | solution.py:27
  140.7 7.3 %collective-permute-start.28 = (bf16[128,4096]{1,0:T(8,128)(2,1)S(1)}, bf16[128,4096]{1,0:T(8,128)(2,1)S(1)}, u32[]{:S(2)}, u32[]{:S(2)}) collective-permute-start(bf16[128,4096]{1,0:T(8,128)(2,1)S(1)} %join_columns.59.refs_1_), channel_id=1, source_target_pairs={{0,8},{8,0},{16,24},{24,16},{1,9},{9,1},{17,25},{25,17},{2,10},{10... | collective-permute-start | bytes 3145736 | tf_op jit(solution)/shard_map/ppermute | solution.py:27
  145.0 37.3 %copy-start.30 = (bf16[128,2048]{1,0:T(8,128)(2,1)}, bf16[128,2048]{1,0:T(8,128)(2,1)S(1)}, u32[]{:S(2)}) copy-start(bf16[128,2048]{1,0:T(8,128)(2,1)S(1)} %collective-permute-done.23.refs_2_.refs_7_.refs_11_) | copy-start | bytes 1572868
  145.0 3.0 %copy-start.1 = (bf16[128,6656]{1,0:T(8,128)(2,1)S(1)}, bf16[128,6656]{1,0:T(8,128)(2,1)}, u32[]{:S(2)}) copy-start(bf16[128,6656]{1,0:T(8,128)(2,1)} %copy-done) | copy-start | bytes 5111812
  145.0 3.0 %copy-start.3 = (bf16[128,4096]{1,0:T(8,128)(2,1)S(1)}, bf16[128,4096]{1,0:T(8,128)(2,1)}, u32[]{:S(2)}) copy-start(bf16[128,4096]{1,0:T(8,128)(2,1)} %copy-done.2) | copy-start | bytes 3145732
  145.0 3.0 %copy-start.5 = (bf16[128,4096]{1,0:T(8,128)(2,1)S(1)}, bf16[128,4096]{1,0:T(8,128)(2,1)}, u32[]{:S(2)}) copy-start(bf16[128,4096]{1,0:T(8,128)(2,1)} %copy-done.4) | copy-start | bytes 3145732
  145.0 3.0 %copy-start.9 = (bf16[128,2048]{1,0:T(8,128)(2,1)S(1)}, bf16[128,2048]{1,0:T(8,128)(2,1)}, u32[]{:S(2)}) copy-start(bf16[128,2048]{1,0:T(8,128)(2,1)} %copy-done.7) | copy-start | bytes 1572868
  145.0 3.0 %copy-start.11 = (bf16[128,2048]{1,0:T(8,128)(2,1)S(1)}, bf16[128,2048]{1,0:T(8,128)(2,1)}, u32[]{:S(2)}) copy-start(bf16[128,2048]{1,0:T(8,128)(2,1)} %copy-done.10) | copy-start | bytes 1572868
  145.1 3.0 %copy-start.13 = (bf16[128,2048]{1,0:T(8,128)(2,1)S(1)}, bf16[128,2048]{1,0:T(8,128)(2,1)}, u32[]{:S(2)}) copy-start(bf16[128,2048]{1,0:T(8,128)(2,1)} %copy-done.12) | copy-start | bytes 1572868
  145.1 3.0 %copy-start.15 = (bf16[128,2048]{1,0:T(8,128)(2,1)S(1)}, bf16[128,2048]{1,0:T(8,128)(2,1)}, u32[]{:S(2)}) copy-start(bf16[128,2048]{1,0:T(8,128)(2,1)} %copy-done.14) | copy-start | bytes 1572868
  145.1 3.1 %copy-start.17 = (bf16[128,2048]{1,0:T(8,128)(2,1)S(1)}, bf16[128,2048]{1,0:T(8,128)(2,1)}, u32[]{:S(2)}) copy-start(bf16[128,2048]{1,0:T(8,128)(2,1)} %copy-done.16) | copy-start | bytes 1572868
  145.1 3.2 %copy-start.19 = (bf16[128,2048]{1,0:T(8,128)(2,1)S(1)}, bf16[128,2048]{1,0:T(8,128)(2,1)}, u32[]{:S(2)}) copy-start(bf16[128,2048]{1,0:T(8,128)(2,1)} %copy-done.18) | copy-start | bytes 1572868
  145.1 3.4 %copy-start.21 = (bf16[128,2048]{1,0:T(8,128)(2,1)S(1)}, bf16[128,2048]{1,0:T(8,128)(2,1)}, u32[]{:S(2)}) copy-start(bf16[128,2048]{1,0:T(8,128)(2,1)} %copy-done.20) | copy-start | bytes 1572868
  145.1 3.5 %copy-start.23 = (bf16[128,2048]{1,0:T(8,128)(2,1)S(1)}, bf16[128,2048]{1,0:T(8,128)(2,1)}, u32[]{:S(2)}) copy-start(bf16[128,2048]{1,0:T(8,128)(2,1)} %copy-done.22) | copy-start | bytes 1572868
  145.1 3.6 %copy-start.25 = (bf16[128,2048]{1,0:T(8,128)(2,1)S(1)}, bf16[128,2048]{1,0:T(8,128)(2,1)}, u32[]{:S(2)}) copy-start(bf16[128,2048]{1,0:T(8,128)(2,1)} %copy-done.24) | copy-start | bytes 1572868
  145.1 3.8 %copy-start.27 = (bf16[128,2048]{1,0:T(8,128)(2,1)S(1)}, bf16[128,2048]{1,0:T(8,128)(2,1)}, u32[]{:S(2)}) copy-start(bf16[128,2048]{1,0:T(8,128)(2,1)} %copy-done.26) | copy-start | bytes 1572868
  146.5 12.4 %copy-start.34 = (bf16[128,2048]{1,0:T(8,128)(2,1)S(1)}, bf16[128,2048]{1,0:T(8,128)(2,1)}, u32[]{:S(2)}) copy-start(bf16[128,2048]{1,0:T(8,128)(2,1)} %copy-done.33) | copy-start | bytes 1572868
  146.5 13.9 %collective-permute-start.27 = (bf16[128,2048]{1,0:T(8,128)(2,1)S(1)}, bf16[128,2048]{1,0:T(8,128)(2,1)S(1)}, u32[]{:S(2)}, u32[]{:S(2)}) collective-permute-start(bf16[128,2048]{1,0:T(8,128)(2,1)S(1)} %join_columns.61.refs_1_.refs_0_), channel_id=1, source_target_pairs={{0,16},{8,24},{16,0},{24,8},{1,17},{9,25},{17,1},{25,9},{2,18},{10... | collective-permute-start | bytes 1572872 | tf_op jit(solution)/shard_map/ppermute | solution.py:27
  160.5 19.6 %collective-permute-start.30 = (bf16[128,4096]{1,0:T(8,128)(2,1)S(1)}, bf16[128,4096]{1,0:T(8,128)(2,1)S(1)}, u32[]{:S(2)}, u32[]{:S(2)}) collective-permute-start(bf16[128,4096]{1,0:T(8,128)(2,1)S(1)} %join_columns.63.refs_1_), channel_id=1, source_target_pairs={{0,8},{8,0},{16,24},{24,16},{1,9},{9,1},{17,25},{25,17},{2,10},{10... | collective-permute-start | bytes 3145736 | tf_op jit(solution)/shard_map/ppermute | solution.py:27
  161.6 18.5 %collective-permute-start.29 = (bf16[128,1280]{1,0:T(8,128)(2,1)S(1)}, bf16[128,1280]{1,0:T(8,128)(2,1)S(1)}, u32[]{:S(2)}, u32[]{:S(2)}) collective-permute-start(bf16[128,1280]{1,0:T(8,128)(2,1)S(1)} %join_columns.64.refs_0_.refs_1_), channel_id=1, source_target_pairs={{0,16},{8,24},{16,0},{24,8},{1,17},{9,25},{17,1},{25,9},{2,18},{10... | collective-permute-start | bytes 983048 | tf_op jit(solution)/shard_map/ppermute | solution.py:27
  163.1 17.0 %collective-permute-start.25 = (bf16[128,768]{1,0:T(8,128)(2,1)S(1)}, bf16[128,768]{1,0:T(8,128)(2,1)S(1)}, u32[]{:S(2)}, u32[]{:S(2)}) collective-permute-start(bf16[128,768]{1,0:T(8,128)(2,1)S(1)} %join_columns.60.refs_1_), channel_id=1, source_target_pairs={{0,4},{1,5},{2,6},{3,7},{4,0},{5,1},{6,2},{7,3},{8,12},{9,13},{10,... | collective-permute-start | bytes 589832 | tf_op jit(solution)/shard_map/ppermute | solution.py:27
  163.1 24.9 %collective-permute-start.31 = (bf16[128,768]{1,0:T(8,128)(2,1)S(1)}, bf16[128,768]{1,0:T(8,128)(2,1)S(1)}, u32[]{:S(2)}, u32[]{:S(2)}) collective-permute-start(bf16[128,768]{1,0:T(8,128)(2,1)S(1)} %join_columns.62.refs_2_), channel_id=1, source_target_pairs={{0,7},{1,6},{2,5},{3,4},{4,3},{5,2},{6,1},{7,0},{8,15},{9,14},{10,... | collective-permute-start | bytes 589832 | tf_op jit(solution)/shard_map/ppermute | solution.py:27
  180.1 2.2 %copy-start.29 = (bf16[128,2048]{1,0:T(8,128)(2,1)S(1)}, bf16[128,2048]{1,0:T(8,128)(2,1)}, u32[]{:S(2)}) copy-start(bf16[128,2048]{1,0:T(8,128)(2,1)} %copy-done.28) | copy-start | bytes 1572868
  180.1 2.2 collective-permute-start.33
  180.2 7.8 %collective-permute-start.32 = (bf16[128,768]{1,0:T(8,128)(2,1)S(1)}, bf16[128,768]{1,0:T(8,128)(2,1)S(1)}, u32[]{:S(2)}, u32[]{:S(2)}) collective-permute-start(bf16[128,768]{1,0:T(8,128)(2,1)S(1)} %join_columns.66.refs_0_), channel_id=1, source_target_pairs={{0,16},{8,24},{16,0},{24,8},{1,17},{9,25},{17,1},{25,9},{2,18},{10... | collective-permute-start | bytes 589832 | tf_op jit(solution)/shard_map/ppermute | solution.py:27
  188.1 7.5 %collective-permute-start.34 = (bf16[128,1536]{1,0:T(8,128)(2,1)S(1)}, bf16[128,1536]{1,0:T(8,128)(2,1)S(1)}, u32[]{:S(2)}, u32[]{:S(2)}) collective-permute-start(bf16[128,1536]{1,0:T(8,128)(2,1)S(1)} %join_columns.67.refs_1_), channel_id=1, source_target_pairs={{0,8},{8,0},{16,24},{24,16},{1,9},{9,1},{17,25},{25,17},{2,10},{10... | collective-permute-start | bytes 1179656 | tf_op jit(solution)/shard_map/ppermute | solution.py:27
  188.3 9.1 %copy-start.31 = (bf16[128,2048]{1,0:T(8,128)(2,1)S(1)}, bf16[128,2048]{1,0:T(8,128)(2,1)}, u32[]{:S(2)}) copy-start(bf16[128,2048]{1,0:T(8,128)(2,1)} %copy-done.30) | copy-start | bytes 1572868
  188.3 7.2 %collective-permute-start.35 = (bf16[128,768]{1,0:T(8,128)(2,1)S(1)}, bf16[128,768]{1,0:T(8,128)(2,1)S(1)}, u32[]{:S(2)}, u32[]{:S(2)}) collective-permute-start(bf16[128,768]{1,0:T(8,128)(2,1)S(1)} %join_columns.68.refs_0_.refs_2_), channel_id=1, source_target_pairs={{0,16},{8,24},{16,0},{24,8},{1,17},{9,25},{17,1},{25,9},{2,18},{10... | collective-permute-start | bytes 589832 | tf_op jit(solution)/shard_map/ppermute | solution.py:27
  195.6 1.8 collective-permute-start.36
  (14 other events, 14.0 us)

commit v7 on v6

--- a/solution.py
+++ b/solution.py
@@ -12,6 +12,8 @@
 lanes = 128
 first_part = 0.625
 most_flying = 5
+dear = 12 * 10**9
+dear_per_byte = 2 * 10**4
 start_time = 1.5
 latency = 1.0
 link_rate = 5e4
@@ -85,9 +87,26 @@
         in_specs=[VMEM] * len(arrays) + [ANY] * len(after),
         out_specs=VMEM,
         compiler_params=pltpu.CompilerParams(vmem_limit_bytes=6 * 2**20),
-        cost_estimate=pl.CostEstimate(flops=3 * 10**10, bytes_accessed=0, transcendentals=0),
+        cost_estimate=pl.CostEstimate(flops=dear, bytes_accessed=0, transcendentals=0),
         name="join_columns",
     )(*arrays, *after)
+
+
+def hold_kernel(message_ref, out_ref):
+    out_ref[...] = message_ref[...]
+
+
+def hold(message, flops):
+    tile = pl.BlockSpec((16, lanes), lambda i: (0, 0))
+    return pl.pallas_call(
+        hold_kernel,
+        grid=(1,),
+        out_shape=jax.ShapeDtypeStruct((16, lanes), message.dtype),
+        in_specs=[tile],
+        out_specs=tile,
+        cost_estimate=pl.CostEstimate(flops=flops, bytes_accessed=0, transcendentals=0),
+        name="hold",
+    )(message)
 
 
 def mask_kernel(valid_ref, user_ref, cot_ref, *out_refs):
@@ -381,7 +400,8 @@
                 to += pieces[i][1]
 
         parts = [(own, 0, total), (other, 0, total)]
-        start("user", core, parts, 6 * link_rate, {"C"}, action)
+        message = start("user", core, parts, 6 * link_rate, {"C"}, action)
+        tick[:] = [hold(message, dear_per_byte * 4 * tok_rows * total)]
 
     gradients = [None, None]
     added = set()

time: 218 us -> 249 us (1.14)
  local copies, waits for them, and re-layouts: 12 us -> 44.3 us
  waiting for transfers between devices: 107 us -> 80.5 us
  Pallas kernels: 45.4 us -> 63.7 us
  starting transfers between devices: 41.6 us -> 46.7 us
    unnamed x82 -> x198, local copies, waits for them, and re-layouts: 12 us -> 44.3 us
    ppermute x37, waiting for transfers between devices: 107 us -> 80.5 us  [exchange(): return lax.ppermute(block, axis, [(i, i ^ distance) for i in range(size)])]
    pallas_call x0 -> x8, Pallas kernels: none -> 10.3 us  [hold(): pl.pallas_call(hold_kernel, grid=(1,), out_shape=jax.ShapeDtypeStruct((16...]
    pallas_call x35, Pallas kernels: 12.8 us -> 20.9 us  [join(): pl.pallas_call(functools.partial(join_kernel, places), out_shape=jax.Shap...]
    ppermute x37, starting transfers between devices: 41.6 us -> 46.7 us  [exchange(): return lax.ppermute(block, axis, [(i, i ^ distance) for i in range(size)])]
  transfers between devices with their start and end apart: 37 -> 37, of which waited for: 16 -> 12; matrix products, arithmetic and copies ran while one was open for 0% -> 0% of each run, Pallas kernels for 15% -> 20%
where the time goes in v7:
time: 249 us; the launch traced here: 248 us
  waiting for transfers between devices  80.5 us (32%)
  Pallas kernels  63.7 us (26%)
  starting transfers between devices  46.7 us (19%)
  local copies, waits for them, and re-layouts  44.3 us (18%)
  blocking collectives  11.2 us (4%)
    ppermute x37, waiting for transfers between devices, exchange(): return lax.ppermute(block, axis, [(i, i ^ distance) for i in range(size)])  80.5 us
    ppermute x37, starting transfers between devices, exchange(): return lax.ppermute(block, axis, [(i, i ^ distance) for i in range(size)])  46.7 us
    unnamed x198, local copies, waits for them, and re-layouts  44.3 us
    pallas_call x4, Pallas kernels, product(): pl.pallas_call(functools.partial(product_kernel, left_places, right_place...  27.2 us
    pallas_call x35, Pallas kernels, join(): pl.pallas_call(functools.partial(join_kernel, places), out_shape=jax.Shap...  20.9 us
    all_to_all x1, blocking collectives, body(): lax.all_to_all(sums, ('user', 'tok'), split_axis=0, concat_axis=0, tiled=...  11.2 us
    pallas_call x8, Pallas kernels, hold(): pl.pallas_call(hold_kernel, grid=(1,), out_shape=jax.ShapeDtypeStruct((16...  10.3 us
  transfers between devices with their start and end apart: 37, of which 12 were waited for; matrix products, arithmetic and copies ran while one was open for 0% of the time, Pallas kernels for 20%

profile of v7, /device:TPU:0, one launch (start us, length us, event | category | flops | bytes accessed | tf_op | source)
XLA Modules:
  0.0 248.0 jit_solution(16136881705465278107)
XLA Ops:
  0.7 1.0 copy-done.65
  2.3 2.6 %collective-permute-start.1 = (bf16[128,512]{1,0:T(8,128)(2,1)S(1)}, bf16[128,512]{1,0:T(8,128)(2,1)S(1)}, u32[]{:S(2)}, u32[]{:S(2)}) collective-permute-start(bf16[128,512]{1,0:T(8,128)(2,1)S(1)} %get-tuple-element.28), channel_id=1, source_target_pairs={{0,16},{8,24},{16,0},{24,8},{1,17},{9,25},{17,1},{25,9},{2,18},{10... | collective-permute-start | bytes 393224 | tf_op jit(solution)/shard_map/ppermute | solution.py:29
  4.9 2.2 copy-done.15
  8.6 2.8 %collective-permute-start.7 = (bf16[128,1280]{1,0:T(8,128)(2,1)}, bf16[128,1280]{1,0:T(8,128)(2,1)}, u32[]{:S(2)}, u32[]{:S(2)}) collective-permute-start(bf16[128,1280]{1,0:T(8,128)(2,1)} %join_columns.35.refs_4_), channel_id=1, source_target_pairs={{0,4},{1,5},{2,6},{3,7},{4,0},{5,1},{6,2},{7,3},{8,12},{9,13},{10,... | collective-permute-start | bytes 983048 | tf_op jit(solution)/shard_map/ppermute | solution.py:29
  12.5 2.7 %collective-permute-start.12 = (bf16[128,2048]{1,0:T(8,128)(2,1)}, bf16[128,2048]{1,0:T(8,128)(2,1)}, u32[]{:S(2)}, u32[]{:S(2)}) collective-permute-start(bf16[128,2048]{1,0:T(8,128)(2,1)} %join_columns.37.refs_1_), channel_id=1, source_target_pairs={{0,4},{1,5},{2,6},{3,7},{4,0},{5,1},{6,2},{7,3},{8,12},{9,13},{10,... | collective-permute-start | bytes 1572872 | tf_op jit(solution)/shard_map/ppermute | solution.py:29
  15.2 1.6 collective-permute-start.4
  16.8 1.6 collective-permute-start.3
  18.4 1.6 collective-permute-start.5
  20.1 9.0 %collective-permute-done.4.refs_1_.refs_10_ = bf16[128,2048]{1,0:T(8,128)(2,1)S(1)} collective-permute-done((bf16[128,2048]{1,0:T(8,128)(2,1)S(1)}, bf16[128,2048]{1,0:T(8,128)(2,1)S(1)}, u32[]{:S(2)}, u32[]{:S(2)}) %collective-permute-start.4) | collective-permute-done | bytes 524320 | tf_op jit(solution)/shard_map/ppermute | solution.py:29
  30.9 1.3 hold.8.refs_1_
  32.9 1.1 join_columns.42.refs_1_.refs_0_.refs_2_
  34.0 1.6 collective-permute-start.10
  35.5 6.1 %collective-permute-done.5.refs_2_.refs_0_ = bf16[128,2048]{1,0:T(8,128)(2,1)S(1)} collective-permute-done((bf16[128,2048]{1,0:T(8,128)(2,1)S(1)}, bf16[128,2048]{1,0:T(8,128)(2,1)S(1)}, u32[]{:S(2)}, u32[]{:S(2)}) %collective-permute-start.5) | collective-permute-done | bytes 524320 | tf_op jit(solution)/shard_map/ppermute | solution.py:29
  41.7 3.5 %collective-permute-start.9 = (bf16[128,2048]{1,0:T(8,128)(2,1)S(1)}, bf16[128,2048]{1,0:T(8,128)(2,1)S(1)}, u32[]{:S(2)}, u32[]{:S(2)}) collective-permute-start(bf16[128,2048]{1,0:T(8,128)(2,1)S(1)} %join_columns.43.refs_1_), channel_id=1, source_target_pairs={{0,3},{1,2},{2,1},{3,0},{4,7},{5,6},{6,5},{7,4},{8,11},{9,10},{10,... | collective-permute-start | bytes 1572872 | tf_op jit(solution)/shard_map/ppermute | solution.py:29
  46.4 2.0 collective-permute-done.10.refs_1_.refs_12_.refs_11_
  49.3 1.0 copy-done.73
  50.3 1.3 hold.9.refs_2_
  52.3 1.0 join_columns.46.refs_1_.refs_0_.refs_2_
  53.3 1.6 collective-permute-start.11
  54.9 14.2 %collective-permute-done.9.refs_2_.refs_0_ = bf16[128,2048]{1,0:T(8,128)(2,1)S(1)} collective-permute-done((bf16[128,2048]{1,0:T(8,128)(2,1)S(1)}, bf16[128,2048]{1,0:T(8,128)(2,1)S(1)}, u32[]{:S(2)}, u32[]{:S(2)}) %collective-permute-start.9) | collective-permute-done | bytes 524320 | tf_op jit(solution)/shard_map/ppermute | solution.py:29
  69.1 1.6 collective-permute-start.14
  72.5 2.5 collective-permute-start.24
  75.0 9.1 %collective-permute-done.14.refs_2_.refs_17_.refs_16_ = bf16[128,2048]{1,0:T(8,128)(2,1)S(1)} collective-permute-done((bf16[128,2048]{1,0:T(8,128)(2,1)S(1)}, bf16[128,2048]{1,0:T(8,128)(2,1)S(1)}, u32[]{:S(2)}, u32[]{:S(2)}) %collective-permute-start.14) | collective-permute-done | bytes 524320 | tf_op jit(solution)/shard_map/ppermute | solution.py:29
  84.1 2.1 join_columns.50.refs_1_
  86.8 2.1 join_columns.51.refs_2_
  88.9 1.5 join_columns.52.message_ref
  90.4 1.3 hold.10.refs_1_
  91.7 2.5 %collective-permute-done.16.refs_2_.refs_6_.refs_7_ = bf16[128,6656]{1,0:T(8,128)(2,1)S(1)} collective-permute-done((bf16[128,6656]{1,0:T(8,128)(2,1)}, bf16[128,6656]{1,0:T(8,128)(2,1)S(1)}, u32[]{:S(2)}, u32[]{:S(2)}) %collective-permute-start.16) | collective-permute-done | bytes 1703968 | tf_op jit(solution)/shard_map/ppermute | solution.py:29
  94.9 1.6 collective-permute-start.17
  96.5 3.8 %collective-permute-done.18.refs_2_.refs_19_.refs_18_ = bf16[128,2048]{1,0:T(8,128)(2,1)S(1)} collective-permute-done((bf16[128,2048]{1,0:T(8,128)(2,1)}, bf16[128,2048]{1,0:T(8,128)(2,1)S(1)}, u32[]{:S(2)}, u32[]{:S(2)}) %collective-permute-start.18) | collective-permute-done | bytes 524320 | tf_op jit(solution)/shard_map/ppermute | solution.py:29
  101.5 7.2 %collective-permute-done.19.refs_2_.refs_0_.refs_6_.refs_10_ = bf16[128,2048]{1,0:T(8,128)(2,1)} collective-permute-done((bf16[128,2048]{1,0:T(8,128)(2,1)}, bf16[128,2048]{1,0:T(8,128)(2,1)}, u32[]{:S(2)}, u32[]{:S(2)}) %collective-permute-start.19) | collective-permute-done | bytes 524320 | tf_op jit(solution)/shard_map/ppermute | solution.py:29
  109.5 2.4 collective-permute-start.26
  112.8 1.0 copy-done.72
  113.8 1.3 hold.11.refs_1_
  115.7 1.1 join_columns.57.refs_1_.refs_0_.refs_3_
  117.7 2.1 join_columns.58.refs_2_
  119.8 1.5 collective-permute-start.23
  121.3 9.9 %collective-permute-done.20.refs_1_.refs_13_ = bf16[128,2048]{1,0:T(8,128)(2,1)S(1)} collective-permute-done((bf16[128,2048]{1,0:T(8,128)(2,1)S(1)}, bf16[128,2048]{1,0:T(8,128)(2,1)S(1)}, u32[]{:S(2)}, u32[]{:S(2)}) %collective-permute-start.20) | collective-permute-done | bytes 524320 | tf_op jit(solution)/shard_map/ppermute | solution.py:29
  133.2 1.3 hold.12.refs_1_
  135.4 1.2 join_columns.61.refs_1_.refs_0_
  139.7 9.8 %product_and_squares.4.refs_3_.refs_8_ = f32[4,1280,512]{2,1,0:T(8,128)S(1)} custom-call(bf16[128,2048]{1,0:T(8,128)(2,1)S(1)} %copy-done.26, bf16[128,3328]{1,0:T(8,128)(2,1)S(1)} %copy-done.17, bf16[128,2048]{1,0:T(8,128)(2,1)S(1)} %copy-done.32, bf16[128,2048]{1,0:T(8,128)(2,1)S(1)} %copy-done.56, bf16[128,2048]{1,0:T(8,128)(2,1)S(1)} %copy-done.47, ...), custom_call_target="tpu_custom_call" | custom-call | flops 4026531840 | bytes 11010048 | tf_op jit(solution)/shard_map/product_and_squares/pallas_call | solution.py:199
  149.6 3.8 %copy-done = f32[4,1280,512]{2,1,0:T(8,128)} copy-done((f32[4,1280,512]{2,1,0:T(8,128)}, f32[4,1280,512]{2,1,0:T(8,128)S(1)}, u32[]{:S(2)}) %copy-start) | copy-done | bytes 10485784
  155.2 1.3 hold.13.refs_1_
  157.2 1.1 copy-done.92
  158.3 1.8 join_columns.64.refs_0_.refs_1_
  161.0 10.6 %collective-permute-start.25 = (bf16[128,768]{1,0:T(8,128)(2,1)S(1)}, bf16[128,768]{1,0:T(8,128)(2,1)S(1)}, u32[]{:S(2)}, u32[]{:S(2)}) collective-permute-start(bf16[128,768]{1,0:T(8,128)(2,1)S(1)} %copy-done.83), channel_id=1, source_target_pairs={{0,4},{1,5},{2,6},{3,7},{4,0},{5,1},{6,2},{7,3},{8,12},{9,13},{10,... | collective-permute-start | bytes 589832 | tf_op jit(solution)/shard_map/ppermute | solution.py:29
  171.8 4.9 %product_and_squares.5.refs_3_.refs_12_ = f32[4,768,512]{2,1,0:T(8,128)S(1)} custom-call(bf16[128,2048]{1,0:T(8,128)(2,1)S(1)} %copy-done.27, bf16[128,2048]{1,0:T(8,128)(2,1)S(1)} %copy-done.33, bf16[128,3328]{1,0:T(8,128)(2,1)S(1)} %copy-done.18, bf16[128,2048]{1,0:T(8,128)(2,1)S(1)} %copy-done.57, bf16[128,2048]{1,0:T(8,128)(2,1)S(1)} %copy-done.48, ...), custom_call_target="tpu_custom_call" | custom-call | flops 2013265920 | bytes 6553600 | tf_op jit(solution)/shard_map/product_and_squares/pallas_call | solution.py:199
  176.7 8.5 %collective-permute-done.25.refs_2_.refs_0_ = bf16[128,768]{1,0:T(8,128)(2,1)S(1)} collective-permute-done((bf16[128,768]{1,0:T(8,128)(2,1)S(1)}, bf16[128,768]{1,0:T(8,128)(2,1)S(1)}, u32[]{:S(2)}, u32[]{:S(2)}) %collective-permute-start.25) | collective-permute-done | bytes 196640 | tf_op jit(solution)/shard_map/ppermute | solution.py:29
  185.2 2.6 %copy-done.4 = f32[4,768,512]{2,1,0:T(8,128)} copy-done((f32[4,768,512]{2,1,0:T(8,128)}, f32[4,768,512]{2,1,0:T(8,128)S(1)}, u32[]{:S(2)}) %copy-start.4) | copy-done | bytes 6291480
  190.1 1.3 hold.14.refs_1_
  191.6 1.0 copy-done.85
  193.3 1.1 collective-permute-start.32
  194.5 4.0 %copy-done.1 = f32[4,1280,512]{2,1,0:T(8,128)S(1)} copy-done((f32[4,1280,512]{2,1,0:T(8,128)S(1)}, f32[4,1280,512]{2,1,0:T(8,128)}, u32[]{:S(2)}) %copy-start.1) | copy-done | bytes 10485784
  198.5 6.8 %product_and_squares.6 = (f32[4,1280,512]{2,1,0:T(8,128)S(1)}, f32[1,8,128]{2,1,0:T(8,128)S(1)}) custom-call(bf16[128,2048]{1,0:T(8,128)(2,1)S(1)} %copy-done.62, bf16[128,1280]{1,0:T(8,128)(2,1)S(1)} %copy-done.67, bf16[128,4096]{1,0:T(8,128)(2,1)S(1)} %collective-permute-done.30.refs_4_.refs_2_, ...), custom_call_target="tpu_custom_call", output_to_operand_aliasing={{0}: (8, {})} | custom-call | flops 1342177280 | bytes 3670016 | tf_op jit(solution)/shard_map/product_and_squares/pallas_call | solution.py:199
  205.3 3.9 %copy-done.2 = f32[4,1280,512]{2,1,0:T(8,128)} copy-done((f32[4,1280,512]{2,1,0:T(8,128)}, f32[4,1280,512]{2,1,0:T(8,128)S(1)}, u32[]{:S(2)}) %copy-start.2) | copy-done | bytes 10485784
  209.2 4.0 %copy-done.3 = f32[4,1280,512]{2,1,0:T(8,128)S(1)} copy-done((f32[4,1280,512]{2,1,0:T(8,128)S(1)}, f32[4,1280,512]{2,1,0:T(8,128)}, u32[]{:S(2)}) %copy-start.3) | copy-done | bytes 10485784
  214.0 1.3 hold.15.refs_1_
  216.0 1.1 join_columns.68.refs_0_.refs_2_
  217.1 1.0 collective-permute-start.35
  218.1 6.3 %collective-permute-done.35.refs_1_.refs_8_ = bf16[128,768]{1,0:T(8,128)(2,1)S(1)} collective-permute-done((bf16[128,768]{1,0:T(8,128)(2,1)S(1)}, bf16[128,768]{1,0:T(8,128)(2,1)S(1)}, u32[]{:S(2)}, u32[]{:S(2)}) %collective-permute-start.35) | collective-permute-done | bytes 196640 | tf_op jit(solution)/shard_map/ppermute | solution.py:29
  224.6 1.7 collective-permute-done.36.refs_5_
  226.3 5.7 %product_and_squares.7 = (f32[4,768,512]{2,1,0:T(8,128)S(1)}, f32[32,8,128]{2,1,0:T(8,128)S(1)}) custom-call(bf16[128,768]{1,0:T(8,128)(2,1)S(1)} %join_columns.66.refs_0_, bf16[128,2048]{1,0:T(8,128)(2,1)S(1)} %copy-done.62, bf16[128,768]{1,0:T(8,128)(2,1)S(1)} %join_columns.68.refs_0_.refs_2_, ...), custom_call_target="tpu_custom_call", output_to_operand_aliasing={{0}: (12, {})} | custom-call | flops 1207959552 | bytes 3932160 | tf_op jit(solution)/shard_map/product_and_squares/pallas_call | solution.py:199
  232.0 11.2 %all_to_all.5.sums_ref = f32[32,8,128]{2,1,0:T(8,128)S(1)} all-to-all(f32[32,8,128]{2,1,0:T(8,128)S(1)} %get-tuple-element.35), channel_id=1, replica_groups=mesh['user'=4,'tok'=8] {'user','tok'}, dimensions={0} | all-to-all | bytes 262144 | tf_op jit(solution)/shard_map/all_to_all | solution.py:463
  243.2 4.8 %weighted_sum.1 = f32[2048,512]{1,0:T(8,128)} custom-call(s32[1]{0:T(128)} %bitcast.user_ref, f32[32,8,128]{2,1,0:T(8,128)S(1)} %all_to_all.5.sums_ref, f32[4,1280,512]{2,1,0:T(8,128)S(1)} %bitcast.3, f32[4,768,512]{2,1,0:T(8,128)S(1)} %get-tuple-element.36.refs_1_), custom_call_target="tpu_custom_call" | custom-call | tf_op jit(solution)/shard_map/weighted_sum/pallas_call | solution.py:256
  (261 shorter events, 30.3 us)
Async XLA Ops:
  1.7 9.7 %collective-permute-start = (bf16[128,512]{1,0:T(8,128)(2,1)S(1)}, bf16[128,512]{1,0:T(8,128)(2,1)S(1)}, u32[]{:S(2)}, u32[]{:S(2)}) collective-permute-start(bf16[128,512]{1,0:T(8,128)(2,1)S(1)} %get-tuple-element.27), channel_id=1, source_target_pairs={{0,8},{8,0},{16,24},{24,16},{1,9},{9,1},{17,25},{25,17},{2,10},{10... | collective-permute-start | bytes 393224 | tf_op jit(solution)/shard_map/ppermute | solution.py:29
  2.3 9.2 %collective-permute-start.1 = (bf16[128,512]{1,0:T(8,128)(2,1)S(1)}, bf16[128,512]{1,0:T(8,128)(2,1)S(1)}, u32[]{:S(2)}, u32[]{:S(2)}) collective-permute-start(bf16[128,512]{1,0:T(8,128)(2,1)S(1)} %get-tuple-element.28), channel_id=1, source_target_pairs={{0,16},{8,24},{16,0},{24,8},{1,17},{9,25},{17,1},{25,9},{2,18},{10... | collective-permute-start | bytes 393224 | tf_op jit(solution)/shard_map/ppermute | solution.py:29
  4.8 6.6 %collective-permute-start.2 = (bf16[128,512]{1,0:T(8,128)(2,1)S(1)}, bf16[128,512]{1,0:T(8,128)(2,1)S(1)}, u32[]{:S(2)}, u32[]{:S(2)}) collective-permute-start(bf16[128,512]{1,0:T(8,128)(2,1)S(1)} %get-tuple-element.29), channel_id=1, source_target_pairs={{0,24},{8,16},{16,8},{24,0},{1,25},{9,17},{17,9},{25,1},{2,26},{10... | collective-permute-start | bytes 393224 | tf_op jit(solution)/shard_map/ppermute | solution.py:29
  8.6 36.6 %collective-permute-start.7 = (bf16[128,1280]{1,0:T(8,128)(2,1)}, bf16[128,1280]{1,0:T(8,128)(2,1)}, u32[]{:S(2)}, u32[]{:S(2)}) collective-permute-start(bf16[128,1280]{1,0:T(8,128)(2,1)} %join_columns.35.refs_4_), channel_id=1, source_target_pairs={{0,4},{1,5},{2,6},{3,7},{4,0},{5,1},{6,2},{7,3},{8,12},{9,13},{10,... | collective-permute-start | bytes 983048 | tf_op jit(solution)/shard_map/ppermute | solution.py:29
  12.5 59.2 %collective-permute-start.12 = (bf16[128,2048]{1,0:T(8,128)(2,1)}, bf16[128,2048]{1,0:T(8,128)(2,1)}, u32[]{:S(2)}, u32[]{:S(2)}) collective-permute-start(bf16[128,2048]{1,0:T(8,128)(2,1)} %join_columns.37.refs_1_), channel_id=1, source_target_pairs={{0,4},{1,5},{2,6},{3,7},{4,0},{5,1},{6,2},{7,3},{8,12},{9,13},{10,... | collective-permute-start | bytes 1572872 | tf_op jit(solution)/shard_map/ppermute | solution.py:29
  15.2 13.9 %collective-permute-start.4 = (bf16[128,2048]{1,0:T(8,128)(2,1)S(1)}, bf16[128,2048]{1,0:T(8,128)(2,1)S(1)}, u32[]{:S(2)}, u32[]{:S(2)}) collective-permute-start(bf16[128,2048]{1,0:T(8,128)(2,1)S(1)} %join_columns.38.refs_1_.refs_0_), channel_id=1, source_target_pairs={{0,16},{8,24},{16,0},{24,8},{1,17},{9,25},{17,1},{25,9},{2,18},{10... | collective-permute-start | bytes 1572872 | tf_op jit(solution)/shard_map/ppermute | solution.py:29
  16.8 15.4 %collective-permute-start.3 = (bf16[128,2048]{1,0:T(8,128)(2,1)S(1)}, bf16[128,2048]{1,0:T(8,128)(2,1)}, u32[]{:S(2)}, u32[]{:S(2)}) collective-permute-start(bf16[128,2048]{1,0:T(8,128)(2,1)S(1)} %join_columns.39.refs_1_), channel_id=1, source_target_pairs={{0,1},{1,0},{2,3},{3,2},{4,5},{5,4},{6,7},{7,6},{8,9},{9,8},{10,11... | collective-permute-start | bytes 1572872 | tf_op jit(solution)/shard_map/ppermute | solution.py:29
  18.4 23.2 %collective-permute-start.5 = (bf16[128,2048]{1,0:T(8,128)(2,1)S(1)}, bf16[128,2048]{1,0:T(8,128)(2,1)S(1)}, u32[]{:S(2)}, u32[]{:S(2)}) collective-permute-start(bf16[128,2048]{1,0:T(8,128)(2,1)S(1)} %join_columns.40.refs_2_), channel_id=1, source_target_pairs={{0,2},{1,3},{2,0},{3,1},{4,6},{5,7},{6,4},{7,5},{8,10},{9,11},{10,... | collective-permute-start | bytes 1572872 | tf_op jit(solution)/shard_map/ppermute | solution.py:29
  32.2 12.9 %collective-permute-start.6 = (bf16[128,4096]{1,0:T(8,128)(2,1)}, bf16[128,4096]{1,0:T(8,128)(2,1)S(1)}, u32[]{:S(2)}, u32[]{:S(2)}) collective-permute-start(bf16[128,4096]{1,0:T(8,128)(2,1)} %copy-done.71), channel_id=1, source_target_pairs={{0,8},{8,0},{16,24},{24,16},{1,9},{9,1},{17,25},{25,17},{2,10},{10... | collective-permute-start | bytes 3145736 | tf_op jit(solution)/shard_map/ppermute | solution.py:29
  34.0 14.4 %collective-permute-start.10 = (bf16[128,2048]{1,0:T(8,128)(2,1)S(1)}, bf16[128,2048]{1,0:T(8,128)(2,1)S(1)}, u32[]{:S(2)}, u32[]{:S(2)}) collective-permute-start(bf16[128,2048]{1,0:T(8,128)(2,1)S(1)} %join_columns.42.refs_1_.refs_0_.refs_2_), channel_id=1, source_target_pairs={{0,16},{8,24},{16,0},{24,8},{1,17},{9,25},{17,1},{25,9},{2,18},{10... | collective-permute-start | bytes 1572872 | tf_op jit(solution)/shard_map/ppermute | solution.py:29
  41.7 27.4 %collective-permute-start.9 = (bf16[128,2048]{1,0:T(8,128)(2,1)S(1)}, bf16[128,2048]{1,0:T(8,128)(2,1)S(1)}, u32[]{:S(2)}, u32[]{:S(2)}) collective-permute-start(bf16[128,2048]{1,0:T(8,128)(2,1)S(1)} %join_columns.43.refs_1_), channel_id=1, source_target_pairs={{0,3},{1,2},{2,1},{3,0},{4,7},{5,6},{6,5},{7,4},{8,11},{9,10},{10,... | collective-permute-start | bytes 1572872 | tf_op jit(solution)/shard_map/ppermute | solution.py:29
  46.4 55.2 %collective-permute-start.8 = (bf16[128,2048]{1,0:T(8,128)(2,1)}, bf16[128,2048]{1,0:T(8,128)(2,1)}, u32[]{:S(2)}, u32[]{:S(2)}) collective-permute-start(bf16[128,2048]{1,0:T(8,128)(2,1)} %join_columns.44.refs_2_), channel_id=1, source_target_pairs={{0,5},{1,4},{2,7},{3,6},{4,1},{5,0},{6,3},{7,2},{8,13},{9,12},{10,... | collective-permute-start | bytes 1572872 | tf_op jit(solution)/shard_map/ppermute | solution.py:29
  51.5 17.6 %copy-start.23 = (bf16[128,2048]{1,0:T(8,128)(2,1)S(1)}, bf16[128,2048]{1,0:T(8,128)(2,1)}, u32[]{:S(2)}) copy-start(bf16[128,2048]{1,0:T(8,128)(2,1)} %copy-done.22) | copy-start | bytes 1572868
  51.5 19.2 %collective-permute-start.13 = (bf16[128,4096]{1,0:T(8,128)(2,1)}, bf16[128,4096]{1,0:T(8,128)(2,1)S(1)}, u32[]{:S(2)}, u32[]{:S(2)}) collective-permute-start(bf16[128,4096]{1,0:T(8,128)(2,1)} %copy-done.73), channel_id=1, source_target_pairs={{0,8},{8,0},{16,24},{24,16},{1,9},{9,1},{17,25},{25,17},{2,10},{10... | collective-permute-start | bytes 3145736 | tf_op jit(solution)/shard_map/ppermute | solution.py:29
  53.3 35.6 %copy-start.16 = (bf16[128,3328]{1,0:T(8,128)(2,1)}, bf16[128,3328]{1,0:T(8,128)(2,1)S(1)}, u32[]{:S(2)}) copy-start(bf16[128,3328]{1,0:T(8,128)(2,1)S(1)} %join_columns.46.refs_1_.refs_0_.refs_2_) | copy-start | bytes 2555908
  53.3 35.5 %collective-permute-start.11 = (bf16[128,3328]{1,0:T(8,128)(2,1)S(1)}, bf16[128,3328]{1,0:T(8,128)(2,1)S(1)}, u32[]{:S(2)}, u32[]{:S(2)}) collective-permute-start(bf16[128,3328]{1,0:T(8,128)(2,1)S(1)} %join_columns.46.refs_1_.refs_0_.refs_2_), channel_id=1, source_target_pairs={{0,16},{8,24},{16,0},{24,8},{1,17},{9,25},{17,1},{25,9},{2,18},{10... | collective-permute-start | bytes 2555912 | tf_op jit(solution)/shard_map/ppermute | solution.py:29
  69.1 15.0 %collective-permute-start.14 = (bf16[128,2048]{1,0:T(8,128)(2,1)S(1)}, bf16[128,2048]{1,0:T(8,128)(2,1)S(1)}, u32[]{:S(2)}, u32[]{:S(2)}) collective-permute-start(bf16[128,2048]{1,0:T(8,128)(2,1)S(1)} %join_columns.47.refs_1_), channel_id=1, source_target_pairs={{0,1},{1,0},{2,3},{3,2},{4,5},{5,4},{6,7},{7,6},{8,9},{9,8},{10,11... | collective-permute-start | bytes 1572872 | tf_op jit(solution)/shard_map/ppermute | solution.py:29
  71.7 15.1 %collective-permute-start.15 = (bf16[128,2048]{1,0:T(8,128)(2,1)S(1)}, bf16[128,2048]{1,0:T(8,128)(2,1)S(1)}, u32[]{:S(2)}, u32[]{:S(2)}) collective-permute-start(bf16[128,2048]{1,0:T(8,128)(2,1)S(1)} %join_columns.48.refs_1_), channel_id=1, source_target_pairs={{0,2},{1,3},{2,0},{3,1},{4,6},{5,7},{6,4},{7,5},{8,10},{9,11},{10,... | collective-permute-start | bytes 1572872 | tf_op jit(solution)/shard_map/ppermute | solution.py:29
  72.5 62.0 %collective-permute-start.24 = (bf16[128,2048]{1,0:T(8,128)(2,1)}, bf16[128,2048]{1,0:T(8,128)(2,1)}, u32[]{:S(2)}, u32[]{:S(2)}) collective-permute-start(bf16[128,2048]{1,0:T(8,128)(2,1)} %join_columns.49.refs_1_), channel_id=1, source_target_pairs={{0,6},{1,7},{2,4},{3,5},{4,2},{5,3},{6,0},{7,1},{8,14},{9,15},{10,... | collective-permute-start | bytes 1572872 | tf_op jit(solution)/shard_map/ppermute | solution.py:29
  86.2 14.1 %collective-permute-start.18 = (bf16[128,2048]{1,0:T(8,128)(2,1)}, bf16[128,2048]{1,0:T(8,128)(2,1)S(1)}, u32[]{:S(2)}, u32[]{:S(2)}) collective-permute-start(bf16[128,2048]{1,0:T(8,128)(2,1)} %join_columns.50.refs_1_), channel_id=1, source_target_pairs={{0,1},{1,0},{2,3},{3,2},{4,5},{5,4},{6,7},{7,6},{8,9},{9,8},{10,11... | collective-permute-start | bytes 1572872 | tf_op jit(solution)/shard_map/ppermute | solution.py:29
  88.9 19.9 %collective-permute-start.19 = (bf16[128,2048]{1,0:T(8,128)(2,1)}, bf16[128,2048]{1,0:T(8,128)(2,1)}, u32[]{:S(2)}, u32[]{:S(2)}) collective-permute-start(bf16[128,2048]{1,0:T(8,128)(2,1)} %join_columns.51.refs_2_), channel_id=1, source_target_pairs={{0,2},{1,3},{2,0},{3,1},{4,6},{5,7},{6,4},{7,5},{8,10},{9,11},{10,... | collective-permute-start | bytes 1572872 | tf_op jit(solution)/shard_map/ppermute | solution.py:29
  90.4 3.8 %collective-permute-start.16 = (bf16[128,6656]{1,0:T(8,128)(2,1)}, bf16[128,6656]{1,0:T(8,128)(2,1)S(1)}, u32[]{:S(2)}, u32[]{:S(2)}) collective-permute-start(bf16[128,6656]{1,0:T(8,128)(2,1)} %join_columns.52.message_ref), channel_id=1, source_target_pairs={{0,8},{8,0},{16,24},{24,16},{1,9},{9,1},{17,25},{25,17},{2,10},{10... | collective-permute-start | bytes 5111816 | tf_op jit(solution)/shard_map/ppermute | solution.py:29
  94.9 17.0 %copy-start.46 = (bf16[128,2048]{1,0:T(8,128)(2,1)}, bf16[128,2048]{1,0:T(8,128)(2,1)S(1)}, u32[]{:S(2)}) copy-start(bf16[128,2048]{1,0:T(8,128)(2,1)S(1)} %join_columns.53.refs_1_.refs_0_.refs_4_) | copy-start | bytes 1572868
  94.9 17.0 %collective-permute-start.17 = (bf16[128,2048]{1,0:T(8,128)(2,1)S(1)}, bf16[128,2048]{1,0:T(8,128)(2,1)S(1)}, u32[]{:S(2)}, u32[]{:S(2)}) collective-permute-start(bf16[128,2048]{1,0:T(8,128)(2,1)S(1)} %join_columns.53.refs_1_.refs_0_.refs_4_), channel_id=1, source_target_pairs={{0,16},{8,24},{16,0},{24,8},{1,17},{9,25},{17,1},{25,9},{2,18},{10... | collective-permute-start | bytes 1572872 | tf_op jit(solution)/shard_map/ppermute | solution.py:29
  101.3 16.4 %collective-permute-start.21 = (bf16[128,2048]{1,0:T(8,128)(2,1)}, bf16[128,2048]{1,0:T(8,128)(2,1)S(1)}, u32[]{:S(2)}, u32[]{:S(2)}) collective-permute-start(bf16[128,2048]{1,0:T(8,128)(2,1)} %join_columns.54.refs_1_), channel_id=1, source_target_pairs={{0,1},{1,0},{2,3},{3,2},{4,5},{5,4},{6,7},{7,6},{8,9},{9,8},{10,11... | collective-permute-start | bytes 1572872 | tf_op jit(solution)/shard_map/ppermute | solution.py:29
  109.5 40.0 %collective-permute-start.26 = (bf16[128,1280]{1,0:T(8,128)(2,1)}, bf16[128,1280]{1,0:T(8,128)(2,1)}, u32[]{:S(2)}, u32[]{:S(2)}) collective-permute-start(bf16[128,1280]{1,0:T(8,128)(2,1)} %join_columns.55.refs_2_), channel_id=1, source_target_pairs={{0,7},{1,6},{2,5},{3,4},{4,3},{5,2},{6,1},{7,0},{8,15},{9,14},{10,... | collective-permute-start | bytes 983048 | tf_op jit(solution)/shard_map/ppermute | solution.py:29
  115.1 16.2 %collective-permute-start.22 = (bf16[128,4096]{1,0:T(8,128)(2,1)}, bf16[128,4096]{1,0:T(8,128)(2,1)S(1)}, u32[]{:S(2)}, u32[]{:S(2)}) collective-permute-start(bf16[128,4096]{1,0:T(8,128)(2,1)} %copy-done.72), channel_id=1, source_target_pairs={{0,8},{8,0},{16,24},{24,16},{1,9},{9,1},{17,25},{25,17},{2,10},{10... | collective-permute-start | bytes 3145736 | tf_op jit(solution)/shard_map/ppermute | solution.py:29
  116.8 14.4 %copy-start.55 = (bf16[128,2048]{1,0:T(8,128)(2,1)}, bf16[128,2048]{1,0:T(8,128)(2,1)S(1)}, u32[]{:S(2)}) copy-start(bf16[128,2048]{1,0:T(8,128)(2,1)S(1)} %join_columns.57.refs_1_.refs_0_.refs_3_) | copy-start | bytes 1572868
  116.8 14.4 %collective-permute-start.20 = (bf16[128,2048]{1,0:T(8,128)(2,1)S(1)}, bf16[128,2048]{1,0:T(8,128)(2,1)S(1)}, u32[]{:S(2)}, u32[]{:S(2)}) collective-permute-start(bf16[128,2048]{1,0:T(8,128)(2,1)S(1)} %join_columns.57.refs_1_.refs_0_.refs_3_), channel_id=1, source_target_pairs={{0,16},{8,24},{16,0},{24,8},{1,17},{9,25},{17,1},{25,9},{2,18},{10... | collective-permute-start | bytes 1572872 | tf_op jit(solution)/shard_map/ppermute | solution.py:29
  119.8 14.8 %collective-permute-start.23 = (bf16[128,2048]{1,0:T(8,128)(2,1)}, bf16[128,2048]{1,0:T(8,128)(2,1)}, u32[]{:S(2)}, u32[]{:S(2)}) collective-permute-start(bf16[128,2048]{1,0:T(8,128)(2,1)} %join_columns.58.refs_2_), channel_id=1, source_target_pairs={{0,1},{1,0},{2,3},{3,2},{4,5},{5,4},{6,7},{7,6},{8,9},{9,8},{10,11... | collective-permute-start | bytes 1572872 | tf_op jit(solution)/shard_map/ppermute | solution.py:29
  134.5 3.0 %collective-permute-start.28 = (bf16[128,4096]{1,0:T(8,128)(2,1)}, bf16[128,4096]{1,0:T(8,128)(2,1)S(1)}, u32[]{:S(2)}, u32[]{:S(2)}) collective-permute-start(bf16[128,4096]{1,0:T(8,128)(2,1)} %copy-done.74), channel_id=1, source_target_pairs={{0,8},{8,0},{16,24},{24,16},{1,9},{9,1},{17,25},{25,17},{2,10},{10... | collective-permute-start | bytes 3145736 | tf_op jit(solution)/shard_map/ppermute | solution.py:29
  136.7 16.7 %copy-start.61 = (bf16[128,2048]{1,0:T(8,128)(2,1)}, bf16[128,2048]{1,0:T(8,128)(2,1)S(1)}, u32[]{:S(2)}) copy-start(bf16[128,2048]{1,0:T(8,128)(2,1)S(1)} %join_columns.61.refs_1_.refs_0_) | copy-start | bytes 1572868
  136.7 16.7 %collective-permute-start.27 = (bf16[128,2048]{1,0:T(8,128)(2,1)S(1)}, bf16[128,2048]{1,0:T(8,128)(2,1)S(1)}, u32[]{:S(2)}, u32[]{:S(2)}) collective-permute-start(bf16[128,2048]{1,0:T(8,128)(2,1)S(1)} %join_columns.61.refs_1_.refs_0_), channel_id=1, source_target_pairs={{0,16},{8,24},{16,0},{24,8},{1,17},{9,25},{17,1},{25,9},{2,18},{10... | collective-permute-start | bytes 1572872 | tf_op jit(solution)/shard_map/ppermute | solution.py:29
  156.5 15.1 %copy-start.7 = (bf16[128,4096]{1,0:T(8,128)(2,1)S(1)}, bf16[128,4096]{1,0:T(8,128)(2,1)}, u32[]{:S(2)}) copy-start(bf16[128,4096]{1,0:T(8,128)(2,1)} %copy-done.5) | copy-start | bytes 3145732
  156.5 15.1 %copy-start.10 = (bf16[128,4096]{1,0:T(8,128)(2,1)S(1)}, bf16[128,4096]{1,0:T(8,128)(2,1)}, u32[]{:S(2)}) copy-start(bf16[128,4096]{1,0:T(8,128)(2,1)} %copy-done.8) | copy-start | bytes 3145732
  156.5 15.1 %copy-start.12 = (bf16[128,4096]{1,0:T(8,128)(2,1)S(1)}, bf16[128,4096]{1,0:T(8,128)(2,1)}, u32[]{:S(2)}) copy-start(bf16[128,4096]{1,0:T(8,128)(2,1)} %copy-done.11) | copy-start | bytes 3145732
  156.5 15.1 %copy-start.14 = (bf16[128,4096]{1,0:T(8,128)(2,1)S(1)}, bf16[128,4096]{1,0:T(8,128)(2,1)}, u32[]{:S(2)}) copy-start(bf16[128,4096]{1,0:T(8,128)(2,1)} %copy-done.13) | copy-start | bytes 3145732
  156.5 15.1 %copy-start.18 = (bf16[128,3328]{1,0:T(8,128)(2,1)S(1)}, bf16[128,3328]{1,0:T(8,128)(2,1)}, u32[]{:S(2)}) copy-start(bf16[128,3328]{1,0:T(8,128)(2,1)} %copy-done.16) | copy-start | bytes 2555908
  156.5 15.1 %copy-start.21 = (bf16[128,3328]{1,0:T(8,128)(2,1)S(1)}, bf16[128,3328]{1,0:T(8,128)(2,1)}, u32[]{:S(2)}) copy-start(bf16[128,3328]{1,0:T(8,128)(2,1)} %copy-done.19) | copy-start | bytes 2555908
  156.6 15.1 %copy-start.27 = (bf16[128,2048]{1,0:T(8,128)(2,1)S(1)}, bf16[128,2048]{1,0:T(8,128)(2,1)}, u32[]{:S(2)}) copy-start(bf16[128,2048]{1,0:T(8,128)(2,1)} %copy-done.25) | copy-start | bytes 1572868
  156.6 15.1 %copy-start.30 = (bf16[128,2048]{1,0:T(8,128)(2,1)S(1)}, bf16[128,2048]{1,0:T(8,128)(2,1)}, u32[]{:S(2)}) copy-start(bf16[128,2048]{1,0:T(8,128)(2,1)} %copy-done.28) | copy-start | bytes 1572868
  156.6 15.1 %copy-start.33 = (bf16[128,2048]{1,0:T(8,128)(2,1)S(1)}, bf16[128,2048]{1,0:T(8,128)(2,1)}, u32[]{:S(2)}) copy-start(bf16[128,2048]{1,0:T(8,128)(2,1)} %copy-done.31) | copy-start | bytes 1572868
  156.6 15.1 %copy-start.36 = (bf16[128,2048]{1,0:T(8,128)(2,1)S(1)}, bf16[128,2048]{1,0:T(8,128)(2,1)}, u32[]{:S(2)}) copy-start(bf16[128,2048]{1,0:T(8,128)(2,1)} %copy-done.34) | copy-start | bytes 1572868
  156.6 15.1 %copy-start.39 = (bf16[128,2048]{1,0:T(8,128)(2,1)S(1)}, bf16[128,2048]{1,0:T(8,128)(2,1)}, u32[]{:S(2)}) copy-start(bf16[128,2048]{1,0:T(8,128)(2,1)} %copy-done.37) | copy-start | bytes 1572868
  156.6 15.1 %copy-start.42 = (bf16[128,2048]{1,0:T(8,128)(2,1)S(1)}, bf16[128,2048]{1,0:T(8,128)(2,1)}, u32[]{:S(2)}) copy-start(bf16[128,2048]{1,0:T(8,128)(2,1)} %copy-done.40) | copy-start | bytes 1572868
  156.6 15.1 %copy-start.45 = (bf16[128,2048]{1,0:T(8,128)(2,1)S(1)}, bf16[128,2048]{1,0:T(8,128)(2,1)}, u32[]{:S(2)}) copy-start(bf16[128,2048]{1,0:T(8,128)(2,1)} %copy-done.43) | copy-start | bytes 1572868
  156.6 15.1 %copy-start.48 = (bf16[128,2048]{1,0:T(8,128)(2,1)S(1)}, bf16[128,2048]{1,0:T(8,128)(2,1)}, u32[]{:S(2)}) copy-start(bf16[128,2048]{1,0:T(8,128)(2,1)} %copy-done.46) | copy-start | bytes 1572868
  156.6 15.1 %copy-start.51 = (bf16[128,2048]{1,0:T(8,128)(2,1)S(1)}, bf16[128,2048]{1,0:T(8,128)(2,1)}, u32[]{:S(2)}) copy-start(bf16[128,2048]{1,0:T(8,128)(2,1)} %copy-done.49) | copy-start | bytes 1572868
  156.6 15.1 %copy-start.54 = (bf16[128,2048]{1,0:T(8,128)(2,1)S(1)}, bf16[128,2048]{1,0:T(8,128)(2,1)}, u32[]{:S(2)}) copy-start(bf16[128,2048]{1,0:T(8,128)(2,1)} %copy-done.52) | copy-start | bytes 1572868
  156.7 15.1 %copy-start.57 = (bf16[128,2048]{1,0:T(8,128)(2,1)S(1)}, bf16[128,2048]{1,0:T(8,128)(2,1)}, u32[]{:S(2)}) copy-start(bf16[128,2048]{1,0:T(8,128)(2,1)} %copy-done.55) | copy-start | bytes 1572868
  156.7 15.1 %copy-start.60 = (bf16[128,2048]{1,0:T(8,128)(2,1)S(1)}, bf16[128,2048]{1,0:T(8,128)(2,1)}, u32[]{:S(2)}) copy-start(bf16[128,2048]{1,0:T(8,128)(2,1)} %copy-done.58) | copy-start | bytes 1572868
  156.7 28.5 %collective-permute-start.30 = (bf16[128,4096]{1,0:T(8,128)(2,1)}, bf16[128,4096]{1,0:T(8,128)(2,1)S(1)}, u32[]{:S(2)}, u32[]{:S(2)}) collective-permute-start(bf16[128,4096]{1,0:T(8,128)(2,1)} %copy-done.70), channel_id=1, source_target_pairs={{0,8},{8,0},{16,24},{24,16},{1,9},{9,1},{17,25},{25,17},{2,10},{10... | collective-permute-start | bytes 3145736 | tf_op jit(solution)/shard_map/ppermute | solution.py:29
  160.1 25.1 %copy-start.66 = (bf16[128,1280]{1,0:T(8,128)(2,1)}, bf16[128,1280]{1,0:T(8,128)(2,1)S(1)}, u32[]{:S(2)}) copy-start(bf16[128,1280]{1,0:T(8,128)(2,1)S(1)} %join_columns.64.refs_0_.refs_1_) | copy-start | bytes 983044
  160.1 25.1 %collective-permute-start.29 = (bf16[128,1280]{1,0:T(8,128)(2,1)S(1)}, bf16[128,1280]{1,0:T(8,128)(2,1)S(1)}, u32[]{:S(2)}, u32[]{:S(2)}) collective-permute-start(bf16[128,1280]{1,0:T(8,128)(2,1)S(1)} %join_columns.64.refs_0_.refs_1_), channel_id=1, source_target_pairs={{0,16},{8,24},{16,0},{24,8},{1,17},{9,25},{17,1},{25,9},{2,18},{10... | collective-permute-start | bytes 983048 | tf_op jit(solution)/shard_map/ppermute | solution.py:29
  161.0 24.2 %collective-permute-start.25 = (bf16[128,768]{1,0:T(8,128)(2,1)S(1)}, bf16[128,768]{1,0:T(8,128)(2,1)S(1)}, u32[]{:S(2)}, u32[]{:S(2)}) collective-permute-start(bf16[128,768]{1,0:T(8,128)(2,1)S(1)} %copy-done.83), channel_id=1, source_target_pairs={{0,4},{1,5},{2,6},{3,7},{4,0},{5,1},{6,2},{7,3},{8,12},{9,13},{10,... | collective-permute-start | bytes 589832 | tf_op jit(solution)/shard_map/ppermute | solution.py:29
  171.6 37.6 %collective-permute-start.31 = (bf16[128,768]{1,0:T(8,128)(2,1)S(1)}, bf16[128,768]{1,0:T(8,128)(2,1)}, u32[]{:S(2)}, u32[]{:S(2)}) collective-permute-start(bf16[128,768]{1,0:T(8,128)(2,1)S(1)} %join_columns.62.refs_2_), channel_id=1, source_target_pairs={{0,7},{1,6},{2,5},{3,4},{4,3},{5,2},{6,1},{7,0},{8,15},{9,14},{10,... | collective-permute-start | bytes 589832 | tf_op jit(solution)/shard_map/ppermute | solution.py:29
  191.4 3.1 %collective-permute-start.33 = (bf16[128,2560]{1,0:T(8,128)(2,1)}, bf16[128,2560]{1,0:T(8,128)(2,1)S(1)}, u32[]{:S(2)}, u32[]{:S(2)}) collective-permute-start(bf16[128,2560]{1,0:T(8,128)(2,1)} %copy-done.75), channel_id=1, source_target_pairs={{0,8},{8,0},{16,24},{24,16},{1,9},{9,1},{17,25},{25,17},{2,10},{10... | collective-permute-start | bytes 1966088 | tf_op jit(solution)/shard_map/ppermute | solution.py:29
  193.3 15.9 %collective-permute-start.32 = (bf16[128,768]{1,0:T(8,128)(2,1)S(1)}, bf16[128,768]{1,0:T(8,128)(2,1)S(1)}, u32[]{:S(2)}, u32[]{:S(2)}) collective-permute-start(bf16[128,768]{1,0:T(8,128)(2,1)S(1)} %join_columns.66.refs_0_), channel_id=1, source_target_pairs={{0,16},{8,24},{16,0},{24,8},{1,17},{9,25},{17,1},{25,9},{2,18},{10... | collective-permute-start | bytes 589832 | tf_op jit(solution)/shard_map/ppermute | solution.py:29
  215.3 9.2 %collective-permute-start.34 = (bf16[128,1536]{1,0:T(8,128)(2,1)}, bf16[128,1536]{1,0:T(8,128)(2,1)S(1)}, u32[]{:S(2)}, u32[]{:S(2)}) collective-permute-start(bf16[128,1536]{1,0:T(8,128)(2,1)} %copy-done.81), channel_id=1, source_target_pairs={{0,8},{8,0},{16,24},{24,16},{1,9},{9,1},{17,25},{25,17},{2,10},{10... | collective-permute-start | bytes 1179656 | tf_op jit(solution)/shard_map/ppermute | solution.py:29
  216.0 27.1 %slice-start = ((s8[10485760]{0:T(1024)(128)(4,1)}), s8[4194304]{0:T(1024)(128)(4,1)S(1)}, s32[]{:S(2)}) async-start(s8[10485760]{0:T(1024)(128)(4,1)} %bitcast.2), calls=%async_computation.1 | async-start | bytes 8388608
  216.0 27.1 %slice-start.1 = ((s8[10485760]{0:T(1024)(128)(4,1)}), s8[4194304]{0:T(1024)(128)(4,1)S(1)}, s32[]{:S(2)}) async-start(s8[10485760]{0:T(1024)(128)(4,1)} %bitcast.2), calls=%async_computation.2 | async-start | bytes 8388608
  217.1 26.0 %slice-start.2 = ((s8[10485760]{0:T(1024)(128)(4,1)}), s8[2097152]{0:T(1024)(128)(4,1)S(1)}, s32[]{:S(2)}) async-start(s8[10485760]{0:T(1024)(128)(4,1)} %bitcast.2), calls=%async_computation.3 | async-start | bytes 4194304
  217.1 7.3 %collective-permute-start.35 = (bf16[128,768]{1,0:T(8,128)(2,1)S(1)}, bf16[128,768]{1,0:T(8,128)(2,1)S(1)}, u32[]{:S(2)}, u32[]{:S(2)}) collective-permute-start(bf16[128,768]{1,0:T(8,128)(2,1)S(1)} %join_columns.68.refs_0_.refs_2_), channel_id=1, source_target_pairs={{0,16},{8,24},{16,0},{24,8},{1,17},{9,25},{17,1},{25,9},{2,18},{10... | collective-permute-start | bytes 589832 | tf_op jit(solution)/shard_map/ppermute | solution.py:29
  224.5 1.8 collective-permute-start.36
  (72 other events, 229.8 us)

commit v8 on v5

--- a/solution.py
+++ b/solution.py
@@ -11,6 +11,7 @@
 epsilon = 1e-06
 lanes = 128
 first_part = 0.5
+dear = 3 * 10**10
 ANY = pl.BlockSpec(memory_space=pl.ANY)
 SMEM = pl.BlockSpec(memory_space=pltpu.SMEM)
 VMEM = pl.BlockSpec(memory_space=pltpu.VMEM)
@@ -59,24 +60,46 @@
 def join_kernel(parts, *refs):
     out_ref = refs[-1]
     to = 0
-    for ref, (start, width) in zip(refs, parts):
-        out_ref[:, to : to + width] = ref[:, start : start + width]
+    for at, start, width in parts:
+        out_ref[:, to : to + width] = refs[at][:, start : start + width]
         to += width
 
 
 def join(parts, after):
-    arrays = [array for array, _, _ in parts]
+    arrays, places = [], []
+    for array, start, width in parts:
+        at = [i for i, other in enumerate(arrays) if other is array]
+        if not at:
+            arrays.append(array)
+        places.append((at[0] if at else len(arrays) - 1, start, width))
+    after = [array for array in after if not any(array is other for other in arrays)]
     rows = arrays[0].shape[0]
     total = sum(width for _, _, width in parts)
     return pl.pallas_call(
-        functools.partial(join_kernel, [part[1:] for part in parts]),
+        functools.partial(join_kernel, places),
         out_shape=jax.ShapeDtypeStruct((rows, total), arrays[0].dtype),
         in_specs=[VMEM] * len(arrays) + [ANY] * len(after),
         out_specs=VMEM,
-        compiler_params=pltpu.CompilerParams(vmem_limit_bytes=2**20),
+        compiler_params=pltpu.CompilerParams(vmem_limit_bytes=max(2**20, 8 * rows * total - 2**24)),
         cost_estimate=pl.CostEstimate(flops=0, bytes_accessed=4 * rows * total, transcendentals=0),
         name="join_columns",
     )(*arrays, *after)
+
+
+def hold_kernel(message_ref, out_ref):
+    out_ref[...] = jnp.zeros_like(out_ref)
+
+
+def hold(message):
+    return pl.pallas_call(
+        hold_kernel,
+        out_shape=jax.ShapeDtypeStruct((16, lanes), message.dtype),
+        in_specs=[ANY],
+        out_specs=VMEM,
+        cost_estimate=pl.CostEstimate(flops=dear, bytes_accessed=0, transcendentals=0),
+        compiler_params=pltpu.CompilerParams(vmem_limit_bytes=2**20),
+        name="hold",
+    )(message)
 
 
 def mask_kernel(valid_ref, user_ref, cot_ref, *out_refs):
@@ -323,7 +346,7 @@
             )
             done.update((d, i) for d in here)
             gradients[i : i + 1] = [out]
-            tick[:] = [out[0]]
+            tick.append(out[0])
 
     for step in range(len(far_steps) + 2):
         arrivals = []
@@ -358,7 +381,9 @@
         crossed = cross_before
         cross_before = None
         if ready:
-            blocks, ready = ready, []
+            blocks = []
+            while ready and sum(pieces[i][1] for _, i, _, _ in blocks) < 2 * own_width:
+                blocks.append(ready.pop(0))
             parts = [(array, start, pieces[i][1]) for _, i, array, start in blocks]
             own, other = send("user", across, parts, [crossed[2]] if crossed else [])
             cross_before = (blocks, own, other)
@@ -378,12 +403,15 @@
                 relay_bits.pop(0)
                 parts = [part for d in sources for part in cot_parts(d)]
                 relay_before.append((bit, sources, send("tok", bit, parts)[1]))
+        earlier = [core_before[3]] if core_before else []
         finish_core()
         if crossed:
             blocks, own, other = crossed
             total = sum(pieces[i][1] for _, i, _, _ in blocks)
-            both = send("user", core, [(own, 0, total), (other, 0, total)])[1]
+            both = send("user", core, [(own, 0, total), (other, 0, total)], earlier)[1]
             core_before = (blocks, own, other, both)
+        if step < len(far_steps):
+            tick[:] = [hold(tick[0])]
         if step >= len(far_steps) - 1:
             finish_core()
             if relay_before:

time: 209 us -> 208 us (level)
  waiting for transfers between devices: 125 us -> 102 us
  starting transfers between devices: 41.8 us -> 58.4 us
  blocking collectives: 12.2 us -> 17.1 us
    ppermute x30, waiting for transfers between devices: 125 us -> 102 us  [exchange(): return lax.ppermute(block, axis, [(i, i ^ distance) for i in range(size)])]
    ppermute x30, starting transfers between devices: 41.8 us -> 58.4 us  [exchange(): return lax.ppermute(block, axis, [(i, i ^ distance) for i in range(size)])]
    all_to_all x1, blocking collectives: 12.2 us -> 17.1 us  [body(): lax.all_to_all(gradients[1][1], ('user', 'tok'), split_axis=0, concat_axi...]
  transfers between devices with their start and end apart: 30 -> 30, of which waited for: 17 -> 13; matrix products, arithmetic and copies ran while one was open for 0% -> 0% of each run, Pallas kernels for 8% -> 8%
where the time goes in v8:
time: 208 us
  waiting for transfers between devices  102 us (49%)
  starting transfers between devices  58.4 us (28%)
  Pallas kernels  26 us (12%)
  blocking collectives  17.1 us (8%)
  local copies, waits for them, and re-layouts  3.22 us (2%)
    ppermute x30, waiting for transfers between devices, exchange(): return lax.ppermute(block, axis, [(i, i ^ distance) for i in range(size)])  102 us
    ppermute x30, starting transfers between devices, exchange(): return lax.ppermute(block, axis, [(i, i ^ distance) for i in range(size)])  58.4 us
    pallas_call x3, Pallas kernels, product(): pl.pallas_call(functools.partial(product_kernel, left_places, right_place...  19.4 us
    all_to_all x1, blocking collectives, body(): lax.all_to_all(gradients[1][1], ('user', 'tok'), split_axis=0, concat_axi...  17.1 us
    pallas_call x1, Pallas kernels, combine(): pl.pallas_call(functools.partial(combine_kernel, user_count, clip_bound,...  4.81 us
  transfers between devices with their start and end apart: 30, of which 13 were waited for; matrix products, arithmetic and copies ran while one was open for 0% of the time, Pallas kernels for 8%

profile of v8, /device:TPU:0, one launch (start us, length us, event | category | flops | bytes accessed | tf_op | source)
XLA Modules:
  0.0 208.1 jit_solution(14211384983139027561)
XLA Ops:
  0.7 1.0 copy-done.1
  1.7 0.5 collective-permute-start
  2.3 2.6 %collective-permute-start.1 = (bf16[128,512]{1,0:T(8,128)(2,1)S(1)}, bf16[128,512]{1,0:T(8,128)(2,1)S(1)}, u32[]{:S(2)}, u32[]{:S(2)}) collective-permute-start(bf16[128,512]{1,0:T(8,128)(2,1)S(1)} %get-tuple-element.25), channel_id=1, source_target_pairs={{0,16},{8,24},{16,0},{24,8},{1,17},{9,25},{17,1},{25,9},{2,18},{10... | collective-permute-start | bytes 393224 | tf_op jit(solution)/shard_map/ppermute | solution.py:23
  4.8 0.1 collective-permute-start.2
  4.9 2.2 %copy-done = bf16[1,128,16384]{2,1,0:T(8,128)(2,1)S(1)} copy-done((bf16[1,128,16384]{2,1,0:T(8,128)(2,1)S(1)}, bf16[1,128,16384]{2,1,0:T(8,128)(2,1)}, u32[]{:S(2)}) %copy-start) | copy-done | bytes 4194328
  7.1 0.4 pack_columns.1
  7.5 2.9 %collective-permute-start.4 = (bf16[128,1024]{1,0:T(8,128)(2,1)S(1)}, bf16[128,1024]{1,0:T(8,128)(2,1)S(1)}, u32[]{:S(2)}, u32[]{:S(2)}) collective-permute-start(bf16[128,1024]{1,0:T(8,128)(2,1)S(1)} %join_columns.29.refs_1_), channel_id=1, source_target_pairs={{0,4},{1,5},{2,6},{3,7},{4,0},{5,1},{6,2},{7,3},{8,12},{9,13},{10,... | collective-permute-start | bytes 786440 | tf_op jit(solution)/shard_map/ppermute | solution.py:23
  10.4 1.4 collective-permute-start.5
  11.8 1.6 collective-permute-start.7
  13.4 0.0 collective-permute-done.1.refs_2_
  13.4 0.0 collective-permute-done.2.refs_3_
  13.4 0.1 join_columns.32.refs_2_
  13.5 0.6 collective-permute-start.6
  14.1 0.1 join_columns.33.message_ref
  14.2 14.6 %collective-permute-done.4.refs_2_.refs_0_ = bf16[128,1024]{1,0:T(8,128)(2,1)S(1)} collective-permute-done((bf16[128,1024]{1,0:T(8,128)(2,1)S(1)}, bf16[128,1024]{1,0:T(8,128)(2,1)S(1)}, u32[]{:S(2)}, u32[]{:S(2)}) %collective-permute-start.4) | collective-permute-done | bytes 262176 | tf_op jit(solution)/shard_map/ppermute | solution.py:23
  28.8 0.1 collective-permute-start.9
  28.9 3.8 %collective-permute-start.3 = (bf16[128,4096]{1,0:T(8,128)(2,1)S(1)}, bf16[128,4096]{1,0:T(8,128)(2,1)S(1)}, u32[]{:S(2)}, u32[]{:S(2)}) collective-permute-start(bf16[128,4096]{1,0:T(8,128)(2,1)S(1)} %join_columns.33.message_ref), channel_id=1, source_target_pairs={{0,2},{1,3},{2,0},{3,1},{4,6},{5,7},{6,4},{7,5},{8,10},{9,11},{10,... | collective-permute-start | bytes 3145736 | tf_op jit(solution)/shard_map/ppermute | solution.py:23
  32.7 8.7 %collective-permute-done.5.refs_2_.refs_1_ = bf16[128,1024]{1,0:T(8,128)(2,1)S(1)} collective-permute-done((bf16[128,1024]{1,0:T(8,128)(2,1)S(1)}, bf16[128,1024]{1,0:T(8,128)(2,1)S(1)}, u32[]{:S(2)}, u32[]{:S(2)}) %collective-permute-start.5) | collective-permute-done | bytes 262176 | tf_op jit(solution)/shard_map/ppermute | solution.py:23
  41.4 0.1 collective-permute-start.10
  41.5 2.3 %collective-permute-done.6.refs_2_.refs_13_ = bf16[128,4096]{1,0:T(8,128)(2,1)S(1)} collective-permute-done((bf16[128,4096]{1,0:T(8,128)(2,1)S(1)}, bf16[128,4096]{1,0:T(8,128)(2,1)S(1)}, u32[]{:S(2)}, u32[]{:S(2)}) %collective-permute-start.6) | collective-permute-done | bytes 1048608 | tf_op jit(solution)/shard_map/ppermute | solution.py:23
  43.8 0.1 join_columns.36.refs_1_.refs_0_
  43.8 0.6 collective-permute-start.11
  44.5 2.5 %collective-permute-start.8 = (bf16[128,2048]{1,0:T(8,128)(2,1)S(1)}, bf16[128,2048]{1,0:T(8,128)(2,1)S(1)}, u32[]{:S(2)}, u32[]{:S(2)}) collective-permute-start(bf16[128,2048]{1,0:T(8,128)(2,1)S(1)} %join_columns.37.refs_2_), channel_id=1, source_target_pairs={{0,3},{1,2},{2,1},{3,0},{4,7},{5,6},{6,5},{7,4},{8,11},{9,10},{10,... | collective-permute-start | bytes 1572872 | tf_op jit(solution)/shard_map/ppermute | solution.py:23
  47.0 0.1 join_columns.38.message_ref
  47.0 0.1 collective-permute-start.16
  47.2 16.6 %collective-permute-done.10.refs_2_.refs_1_.refs_18_.refs_17_ = bf16[128,1024]{1,0:T(8,128)(2,1)S(1)} collective-permute-done((bf16[128,1024]{1,0:T(8,128)(2,1)S(1)}, bf16[128,1024]{1,0:T(8,128)(2,1)S(1)}, u32[]{:S(2)}, u32[]{:S(2)}) %collective-permute-start.10) | collective-permute-done | bytes 262176 | tf_op jit(solution)/shard_map/ppermute | solution.py:23
  63.7 3.2 %collective-permute-start.14 = (bf16[128,1024]{1,0:T(8,128)(2,1)S(1)}, bf16[128,1024]{1,0:T(8,128)(2,1)S(1)}, u32[]{:S(2)}, u32[]{:S(2)}) collective-permute-start(bf16[128,1024]{1,0:T(8,128)(2,1)S(1)} %join_columns.39.refs_1_), channel_id=1, source_target_pairs={{0,6},{1,7},{2,4},{3,5},{4,2},{5,3},{6,0},{7,1},{8,14},{9,15},{10,... | collective-permute-start | bytes 786440 | tf_op jit(solution)/shard_map/ppermute | solution.py:23
  66.9 2.0 collective-permute-done.3.refs_0_.refs_14_
  68.9 6.2 %collective-permute-start.15 = (bf16[128,1024]{1,0:T(8,128)(2,1)S(1)}, bf16[128,1024]{1,0:T(8,128)(2,1)S(1)}, u32[]{:S(2)}, u32[]{:S(2)}) collective-permute-start(bf16[128,1024]{1,0:T(8,128)(2,1)S(1)} %join_columns.40.refs_2_), channel_id=1, source_target_pairs={{0,7},{1,6},{2,5},{3,4},{4,3},{5,2},{6,1},{7,0},{8,15},{9,14},{10,... | collective-permute-start | bytes 786440 | tf_op jit(solution)/shard_map/ppermute | solution.py:23
  75.1 5.1 %collective-permute-done.8.refs_1_ = bf16[128,2048]{1,0:T(8,128)(2,1)S(1)} collective-permute-done((bf16[128,2048]{1,0:T(8,128)(2,1)S(1)}, bf16[128,2048]{1,0:T(8,128)(2,1)S(1)}, u32[]{:S(2)}, u32[]{:S(2)}) %collective-permute-start.8) | collective-permute-done | bytes 524320 | tf_op jit(solution)/shard_map/ppermute | solution.py:23
  80.2 0.1 join_columns.41.refs_2_.refs_0_
  80.3 1.6 collective-permute-start.12
  81.9 0.1 collective-permute-start.13
  81.9 0.1 join_columns.43.message_ref
  82.1 0.1 collective-permute-start.17
  82.2 4.5 %collective-permute-done.14.refs_2_.refs_0_ = bf16[128,1024]{1,0:T(8,128)(2,1)S(1)} collective-permute-done((bf16[128,1024]{1,0:T(8,128)(2,1)S(1)}, bf16[128,1024]{1,0:T(8,128)(2,1)S(1)}, u32[]{:S(2)}, u32[]{:S(2)}) %collective-permute-start.14) | collective-permute-done | bytes 262176 | tf_op jit(solution)/shard_map/ppermute | solution.py:23
  86.7 12.5 %collective-permute-start.18 = (bf16[128,1024]{1,0:T(8,128)(2,1)S(1)}, bf16[128,1024]{1,0:T(8,128)(2,1)S(1)}, u32[]{:S(2)}, u32[]{:S(2)}) collective-permute-start(bf16[128,1024]{1,0:T(8,128)(2,1)S(1)} %join_columns.44.refs_1_), channel_id=1, source_target_pairs={{0,4},{1,5},{2,6},{3,7},{4,0},{5,1},{6,2},{7,3},{8,12},{9,13},{10,... | collective-permute-start | bytes 786440 | tf_op jit(solution)/shard_map/ppermute | solution.py:23
  99.3 0.1 collective-permute-start.20
  99.4 5.2 %collective-permute-done.12.refs_3_.refs_1_.refs_10_ = bf16[128,4096]{1,0:T(8,128)(2,1)S(1)} collective-permute-done((bf16[128,4096]{1,0:T(8,128)(2,1)S(1)}, bf16[128,4096]{1,0:T(8,128)(2,1)S(1)}, u32[]{:S(2)}, u32[]{:S(2)}) %collective-permute-start.12) | collective-permute-done | bytes 1048608 | tf_op jit(solution)/shard_map/ppermute | solution.py:23
  104.6 1.6 collective-permute-start.22
  106.1 5.5 %collective-permute-done.13.refs_3_.refs_17_ = bf16[128,2048]{1,0:T(8,128)(2,1)S(1)} collective-permute-done((bf16[128,2048]{1,0:T(8,128)(2,1)S(1)}, bf16[128,2048]{1,0:T(8,128)(2,1)S(1)}, u32[]{:S(2)}, u32[]{:S(2)}) %collective-permute-start.13) | collective-permute-done | bytes 524320 | tf_op jit(solution)/shard_map/ppermute | solution.py:23
  111.6 0.1 join_columns.47.refs_2_
  111.7 1.7 collective-permute-start.25
  113.4 0.1 join_columns.48.message_ref
  113.5 0.1 collective-permute-start.23
  113.7 9.9 %collective-permute-start.19 = (bf16[128,1024]{1,0:T(8,128)(2,1)S(1)}, bf16[128,1024]{1,0:T(8,128)(2,1)S(1)}, u32[]{:S(2)}, u32[]{:S(2)}) collective-permute-start(bf16[128,1024]{1,0:T(8,128)(2,1)S(1)} %join_columns.49.refs_1_), channel_id=1, source_target_pairs={{0,6},{1,7},{2,4},{3,5},{4,2},{5,3},{6,0},{7,1},{8,14},{9,15},{10,... | collective-permute-start | bytes 786440 | tf_op jit(solution)/shard_map/ppermute | solution.py:23
  123.6 2.7 %collective-permute-start.21 = (bf16[128,1024]{1,0:T(8,128)(2,1)S(1)}, bf16[128,1024]{1,0:T(8,128)(2,1)S(1)}, u32[]{:S(2)}, u32[]{:S(2)}) collective-permute-start(bf16[128,1024]{1,0:T(8,128)(2,1)S(1)} %join_columns.50.refs_2_), channel_id=1, source_target_pairs={{0,7},{1,6},{2,5},{3,4},{4,3},{5,2},{6,1},{7,0},{8,15},{9,14},{10,... | collective-permute-start | bytes 786440 | tf_op jit(solution)/shard_map/ppermute | solution.py:23
  126.3 0.6 collective-permute-start.26
  126.9 0.1 join_columns.52.message_ref
  127.0 0.1 collective-permute-start.24
  127.1 29.1 %collective-permute-done.25.refs_15_.refs_4_ = bf16[128,6144]{1,0:T(8,128)(2,1)S(1)} collective-permute-done((bf16[128,6144]{1,0:T(8,128)(2,1)S(1)}, bf16[128,6144]{1,0:T(8,128)(2,1)S(1)}, u32[]{:S(2)}, u32[]{:S(2)}) %collective-permute-start.25) | collective-permute-done | bytes 1572896 | tf_op jit(solution)/shard_map/ppermute | solution.py:23
  156.2 8.1 %product_and_squares.3 = (f32[4,1024,512]{2,1,0:T(8,128)S(1)}, f32[1,8,128]{2,1,0:T(8,128)S(1)}) custom-call(bf16[128,2048]{1,0:T(8,128)(2,1)S(1)} %join_columns.31.refs_2_.refs_0_, bf16[128,4096]{1,0:T(8,128)(2,1)S(1)} %join_columns.36.refs_1_.refs_0_, bf16[128,4096]{1,0:T(8,128)(2,1)S(1)} %join_columns.41.refs_2_.refs_0_, ...), custom_call_target="tpu_custom_call" | custom-call | flops 4294967296 | bytes 12582912 | tf_op jit(solution)/shard_map/product_and_squares/pallas_call | solution.py:192
  164.4 0.1 join_columns.54.refs_2_
  164.5 0.1 collective-permute-start.28
  164.5 1.4 collective-permute-start.27
  165.9 1.2 collective-permute-done.28.refs_7_
  167.2 6.8 %product_and_squares.4.refs_3_.refs_5_ = f32[4,1024,512]{2,1,0:T(8,128)S(1)} custom-call(bf16[128,2048]{1,0:T(8,128)(2,1)S(1)} %join_columns.31.refs_2_.refs_0_, bf16[128,4096]{1,0:T(8,128)(2,1)S(1)} %join_columns.36.refs_1_.refs_0_, bf16[128,4096]{1,0:T(8,128)(2,1)S(1)} %join_columns.41.refs_2_.refs_0_, ...), custom_call_target="tpu_custom_call" | custom-call | flops 3221225472 | bytes 9437184 | tf_op jit(solution)/shard_map/product_and_squares/pallas_call | solution.py:192
  174.0 4.9 %collective-permute-done.27.refs_1_.refs_2_ = bf16[128,2048]{1,0:T(8,128)(2,1)S(1)} collective-permute-done((bf16[128,2048]{1,0:T(8,128)(2,1)S(1)}, bf16[128,2048]{1,0:T(8,128)(2,1)S(1)}, u32[]{:S(2)}, u32[]{:S(2)}) %collective-permute-start.27) | collective-permute-done | bytes 524320 | tf_op jit(solution)/shard_map/ppermute | solution.py:23
  178.9 0.1 join_columns.55
  178.9 0.1 collective-permute-start.29
  179.0 2.6 %collective-permute-done.29.refs_1_ = bf16[128,4096]{1,0:T(8,128)(2,1)S(1)} collective-permute-done((bf16[128,4096]{1,0:T(8,128)(2,1)S(1)}, bf16[128,4096]{1,0:T(8,128)(2,1)S(1)}, u32[]{:S(2)}, u32[]{:S(2)}) %collective-permute-start.29) | collective-permute-done | bytes 1048608 | tf_op jit(solution)/shard_map/ppermute | solution.py:23
  181.7 4.5 %product_and_squares.5 = (f32[4,1024,512]{2,1,0:T(8,128)S(1)}, f32[32,8,128]{2,1,0:T(8,128)S(1)}) custom-call(bf16[128,2048]{1,0:T(8,128)(2,1)S(1)} %join_columns.53.refs_2_.refs_0_, bf16[128,4096]{1,0:T(8,128)(2,1)S(1)} %collective-permute-done.29.refs_1_, ...), custom_call_target="tpu_custom_call", output_to_operand_aliasing={{0}: (5, {})} | custom-call | flops 1073741824 | bytes 3145728 | tf_op jit(solution)/shard_map/product_and_squares/pallas_call | solution.py:192
  186.2 17.1 %all_to_all.5.sums_ref = f32[32,8,128]{2,1,0:T(8,128)S(1)} all-to-all(f32[32,8,128]{2,1,0:T(8,128)S(1)} %get-tuple-element.35), channel_id=1, replica_groups=mesh['user'=4,'tok'=8] {'user','tok'}, dimensions={0} | all-to-all | bytes 262144 | tf_op jit(solution)/shard_map/all_to_all | solution.py:423
  203.3 4.8 %weighted_sum.1 = f32[2048,512]{1,0:T(8,128)} custom-call(s32[1]{0:T(128)} %bitcast.user_ref, f32[32,8,128]{2,1,0:T(8,128)S(1)} %all_to_all.5.sums_ref, f32[4,1024,512]{2,1,0:T(8,128)S(1)} %get-tuple-element.33.refs_3_.refs_0_, f32[4,1024,512]{2,1,0:T(8,128)S(1)} %get-tuple-element.36.refs_1_), custom_call_target="tpu_custom_call" | custom-call | tf_op jit(solution)/shard_map/weighted_sum/pallas_call | solution.py:249
  (40 shorter events, 0.5 us)
Async XLA Ops:
  0.7 1.0 copy-start.1
  1.7 10.1 %collective-permute-start = (bf16[128,512]{1,0:T(8,128)(2,1)S(1)}, bf16[128,512]{1,0:T(8,128)(2,1)S(1)}, u32[]{:S(2)}, u32[]{:S(2)}) collective-permute-start(bf16[128,512]{1,0:T(8,128)(2,1)S(1)} %get-tuple-element.24), channel_id=1, source_target_pairs={{0,8},{8,0},{16,24},{24,16},{1,9},{9,1},{17,25},{25,17},{2,10},{10... | collective-permute-start | bytes 393224 | tf_op jit(solution)/shard_map/ppermute | solution.py:23
  2.3 11.1 %collective-permute-start.1 = (bf16[128,512]{1,0:T(8,128)(2,1)S(1)}, bf16[128,512]{1,0:T(8,128)(2,1)S(1)}, u32[]{:S(2)}, u32[]{:S(2)}) collective-permute-start(bf16[128,512]{1,0:T(8,128)(2,1)S(1)} %get-tuple-element.25), channel_id=1, source_target_pairs={{0,16},{8,24},{16,0},{24,8},{1,17},{9,25},{17,1},{25,9},{2,18},{10... | collective-permute-start | bytes 393224 | tf_op jit(solution)/shard_map/ppermute | solution.py:23
  4.8 8.5 %collective-permute-start.2 = (bf16[128,512]{1,0:T(8,128)(2,1)S(1)}, bf16[128,512]{1,0:T(8,128)(2,1)S(1)}, u32[]{:S(2)}, u32[]{:S(2)}) collective-permute-start(bf16[128,512]{1,0:T(8,128)(2,1)S(1)} %get-tuple-element.26), channel_id=1, source_target_pairs={{0,24},{8,16},{16,8},{24,0},{1,25},{9,17},{17,9},{25,1},{2,26},{10... | collective-permute-start | bytes 393224 | tf_op jit(solution)/shard_map/ppermute | solution.py:23
  4.9 2.2 %copy-start = (bf16[1,128,16384]{2,1,0:T(8,128)(2,1)S(1)}, bf16[1,128,16384]{2,1,0:T(8,128)(2,1)}, u32[]{:S(2)}) copy-start(bf16[1,128,16384]{2,1,0:T(8,128)(2,1)} %hidden_ref.1) | copy-start | bytes 12582916
  7.5 21.3 %collective-permute-start.4 = (bf16[128,1024]{1,0:T(8,128)(2,1)S(1)}, bf16[128,1024]{1,0:T(8,128)(2,1)S(1)}, u32[]{:S(2)}, u32[]{:S(2)}) collective-permute-start(bf16[128,1024]{1,0:T(8,128)(2,1)S(1)} %join_columns.29.refs_1_), channel_id=1, source_target_pairs={{0,4},{1,5},{2,6},{3,7},{4,0},{5,1},{6,2},{7,3},{8,12},{9,13},{10,... | collective-permute-start | bytes 786440 | tf_op jit(solution)/shard_map/ppermute | solution.py:23
  10.4 30.9 %collective-permute-start.5 = (bf16[128,1024]{1,0:T(8,128)(2,1)S(1)}, bf16[128,1024]{1,0:T(8,128)(2,1)S(1)}, u32[]{:S(2)}, u32[]{:S(2)}) collective-permute-start(bf16[128,1024]{1,0:T(8,128)(2,1)S(1)} %join_columns.30.refs_1_), channel_id=1, source_target_pairs={{0,5},{1,4},{2,7},{3,6},{4,1},{5,0},{6,3},{7,2},{8,13},{9,12},{10,... | collective-permute-start | bytes 786440 | tf_op jit(solution)/shard_map/ppermute | solution.py:23
  11.8 29.6 %collective-permute-start.7 = (bf16[128,2048]{1,0:T(8,128)(2,1)S(1)}, bf16[128,2048]{1,0:T(8,128)(2,1)S(1)}, u32[]{:S(2)}, u32[]{:S(2)}) collective-permute-start(bf16[128,2048]{1,0:T(8,128)(2,1)S(1)} %join_columns.31.refs_2_.refs_0_), channel_id=1, source_target_pairs={{0,16},{8,24},{16,0},{24,8},{1,17},{9,25},{17,1},{25,9},{2,18},{10... | collective-permute-start | bytes 1572872 | tf_op jit(solution)/shard_map/ppermute | solution.py:23
  13.5 30.3 %collective-permute-start.6 = (bf16[128,4096]{1,0:T(8,128)(2,1)S(1)}, bf16[128,4096]{1,0:T(8,128)(2,1)S(1)}, u32[]{:S(2)}, u32[]{:S(2)}) collective-permute-start(bf16[128,4096]{1,0:T(8,128)(2,1)S(1)} %join_columns.32.refs_2_), channel_id=1, source_target_pairs={{0,1},{1,0},{2,3},{3,2},{4,5},{5,4},{6,7},{7,6},{8,9},{9,8},{10,11... | collective-permute-start | bytes 3145736 | tf_op jit(solution)/shard_map/ppermute | solution.py:23
  28.8 18.2 %collective-permute-start.9 = (bf16[128,1024]{1,0:T(8,128)(2,1)S(1)}, bf16[128,1024]{1,0:T(8,128)(2,1)S(1)}, u32[]{:S(2)}, u32[]{:S(2)}) collective-permute-start(bf16[128,1024]{1,0:T(8,128)(2,1)S(1)} %join_columns.34.refs_1_), channel_id=1, source_target_pairs={{0,4},{1,5},{2,6},{3,7},{4,0},{5,1},{6,2},{7,3},{8,12},{9,13},{10,... | collective-permute-start | bytes 786440 | tf_op jit(solution)/shard_map/ppermute | solution.py:23
  28.9 40.0 %collective-permute-start.3 = (bf16[128,4096]{1,0:T(8,128)(2,1)S(1)}, bf16[128,4096]{1,0:T(8,128)(2,1)S(1)}, u32[]{:S(2)}, u32[]{:S(2)}) collective-permute-start(bf16[128,4096]{1,0:T(8,128)(2,1)S(1)} %join_columns.33.message_ref), channel_id=1, source_target_pairs={{0,2},{1,3},{2,0},{3,1},{4,6},{5,7},{6,4},{7,5},{8,10},{9,11},{10,... | collective-permute-start | bytes 3145736 | tf_op jit(solution)/shard_map/ppermute | solution.py:23
  41.4 22.3 %collective-permute-start.10 = (bf16[128,1024]{1,0:T(8,128)(2,1)S(1)}, bf16[128,1024]{1,0:T(8,128)(2,1)S(1)}, u32[]{:S(2)}, u32[]{:S(2)}) collective-permute-start(bf16[128,1024]{1,0:T(8,128)(2,1)S(1)} %join_columns.35.refs_3_), channel_id=1, source_target_pairs={{0,4},{1,5},{2,6},{3,7},{4,0},{5,1},{6,2},{7,3},{8,12},{9,13},{10,... | collective-permute-start | bytes 786440 | tf_op jit(solution)/shard_map/ppermute | solution.py:23
  43.8 36.4 %collective-permute-start.11 = (bf16[128,4096]{1,0:T(8,128)(2,1)S(1)}, bf16[128,4096]{1,0:T(8,128)(2,1)S(1)}, u32[]{:S(2)}, u32[]{:S(2)}) collective-permute-start(bf16[128,4096]{1,0:T(8,128)(2,1)S(1)} %join_columns.36.refs_1_.refs_0_), channel_id=1, source_target_pairs={{0,16},{8,24},{16,0},{24,8},{1,17},{9,25},{17,1},{25,9},{2,18},{10... | collective-permute-start | bytes 3145736 | tf_op jit(solution)/shard_map/ppermute | solution.py:23
  44.5 35.7 %collective-permute-start.8 = (bf16[128,2048]{1,0:T(8,128)(2,1)S(1)}, bf16[128,2048]{1,0:T(8,128)(2,1)S(1)}, u32[]{:S(2)}, u32[]{:S(2)}) collective-permute-start(bf16[128,2048]{1,0:T(8,128)(2,1)S(1)} %join_columns.37.refs_2_), channel_id=1, source_target_pairs={{0,3},{1,2},{2,1},{3,0},{4,7},{5,6},{6,5},{7,4},{8,11},{9,10},{10,... | collective-permute-start | bytes 1572872 | tf_op jit(solution)/shard_map/ppermute | solution.py:23
  47.0 34.9 %collective-permute-start.16 = (bf16[128,4096]{1,0:T(8,128)(2,1)S(1)}, bf16[128,4096]{1,0:T(8,128)(2,1)S(1)}, u32[]{:S(2)}, u32[]{:S(2)}) collective-permute-start(bf16[128,4096]{1,0:T(8,128)(2,1)S(1)} %join_columns.38.message_ref), channel_id=1, source_target_pairs={{0,8},{8,0},{16,24},{24,16},{1,9},{9,1},{17,25},{25,17},{2,10},{10... | collective-permute-start | bytes 3145736 | tf_op jit(solution)/shard_map/ppermute | solution.py:23
  63.7 23.0 %collective-permute-start.14 = (bf16[128,1024]{1,0:T(8,128)(2,1)S(1)}, bf16[128,1024]{1,0:T(8,128)(2,1)S(1)}, u32[]{:S(2)}, u32[]{:S(2)}) collective-permute-start(bf16[128,1024]{1,0:T(8,128)(2,1)S(1)} %join_columns.39.refs_1_), channel_id=1, source_target_pairs={{0,6},{1,7},{2,4},{3,5},{4,2},{5,3},{6,0},{7,1},{8,14},{9,15},{10,... | collective-permute-start | bytes 786440 | tf_op jit(solution)/shard_map/ppermute | solution.py:23
  68.9 30.4 %collective-permute-start.15 = (bf16[128,1024]{1,0:T(8,128)(2,1)S(1)}, bf16[128,1024]{1,0:T(8,128)(2,1)S(1)}, u32[]{:S(2)}, u32[]{:S(2)}) collective-permute-start(bf16[128,1024]{1,0:T(8,128)(2,1)S(1)} %join_columns.40.refs_2_), channel_id=1, source_target_pairs={{0,7},{1,6},{2,5},{3,4},{4,3},{5,2},{6,1},{7,0},{8,15},{9,14},{10,... | collective-permute-start | bytes 786440 | tf_op jit(solution)/shard_map/ppermute | solution.py:23
  80.3 24.3 %collective-permute-start.12 = (bf16[128,4096]{1,0:T(8,128)(2,1)S(1)}, bf16[128,4096]{1,0:T(8,128)(2,1)S(1)}, u32[]{:S(2)}, u32[]{:S(2)}) collective-permute-start(bf16[128,4096]{1,0:T(8,128)(2,1)S(1)} %join_columns.41.refs_2_.refs_0_), channel_id=1, source_target_pairs={{0,16},{8,24},{16,0},{24,8},{1,17},{9,25},{17,1},{25,9},{2,18},{10... | collective-permute-start | bytes 3145736 | tf_op jit(solution)/shard_map/ppermute | solution.py:23
  81.9 29.8 %collective-permute-start.13 = (bf16[128,2048]{1,0:T(8,128)(2,1)S(1)}, bf16[128,2048]{1,0:T(8,128)(2,1)S(1)}, u32[]{:S(2)}, u32[]{:S(2)}) collective-permute-start(bf16[128,2048]{1,0:T(8,128)(2,1)S(1)} %join_columns.42.refs_2_), channel_id=1, source_target_pairs={{0,2},{1,3},{2,0},{3,1},{4,6},{5,7},{6,4},{7,5},{8,10},{9,11},{10,... | collective-permute-start | bytes 1572872 | tf_op jit(solution)/shard_map/ppermute | solution.py:23
  82.1 31.3 %collective-permute-start.17 = (bf16[128,8192]{1,0:T(8,128)(2,1)S(1)}, bf16[128,8192]{1,0:T(8,128)(2,1)S(1)}, u32[]{:S(2)}, u32[]{:S(2)}) collective-permute-start(bf16[128,8192]{1,0:T(8,128)(2,1)S(1)} %join_columns.43.message_ref), channel_id=1, source_target_pairs={{0,8},{8,0},{16,24},{24,16},{1,9},{9,1},{17,25},{25,17},{2,10},{10... | collective-permute-start | bytes 6291464 | tf_op jit(solution)/shard_map/ppermute | solution.py:23
  86.7 26.9 %collective-permute-start.18 = (bf16[128,1024]{1,0:T(8,128)(2,1)S(1)}, bf16[128,1024]{1,0:T(8,128)(2,1)S(1)}, u32[]{:S(2)}, u32[]{:S(2)}) collective-permute-start(bf16[128,1024]{1,0:T(8,128)(2,1)S(1)} %join_columns.44.refs_1_), channel_id=1, source_target_pairs={{0,4},{1,5},{2,6},{3,7},{4,0},{5,1},{6,2},{7,3},{8,12},{9,13},{10,... | collective-permute-start | bytes 786440 | tf_op jit(solution)/shard_map/ppermute | solution.py:23
  99.3 24.3 %collective-permute-start.20 = (bf16[128,1024]{1,0:T(8,128)(2,1)S(1)}, bf16[128,1024]{1,0:T(8,128)(2,1)S(1)}, u32[]{:S(2)}, u32[]{:S(2)}) collective-permute-start(bf16[128,1024]{1,0:T(8,128)(2,1)S(1)} %join_columns.45.refs_2_), channel_id=1, source_target_pairs={{0,5},{1,4},{2,7},{3,6},{4,1},{5,0},{6,3},{7,2},{8,13},{9,12},{10,... | collective-permute-start | bytes 786440 | tf_op jit(solution)/shard_map/ppermute | solution.py:23
  104.6 21.7 %collective-permute-start.22 = (bf16[128,2048]{1,0:T(8,128)(2,1)S(1)}, bf16[128,2048]{1,0:T(8,128)(2,1)S(1)}, u32[]{:S(2)}, u32[]{:S(2)}) collective-permute-start(bf16[128,2048]{1,0:T(8,128)(2,1)S(1)} %join_columns.46.refs_4_.refs_0_.refs_3_), channel_id=1, source_target_pairs={{0,16},{8,24},{16,0},{24,8},{1,17},{9,25},{17,1},{25,9},{2,18},{10... | collective-permute-start | bytes 1572872 | tf_op jit(solution)/shard_map/ppermute | solution.py:23
  111.7 44.4 %collective-permute-start.25 = (bf16[128,6144]{1,0:T(8,128)(2,1)S(1)}, bf16[128,6144]{1,0:T(8,128)(2,1)S(1)}, u32[]{:S(2)}, u32[]{:S(2)}) collective-permute-start(bf16[128,6144]{1,0:T(8,128)(2,1)S(1)} %join_columns.47.refs_2_), channel_id=1, source_target_pairs={{0,1},{1,0},{2,3},{3,2},{4,5},{5,4},{6,7},{7,6},{8,9},{9,8},{10,11... | collective-permute-start | bytes 4718600 | tf_op jit(solution)/shard_map/ppermute | solution.py:23
  113.5 13.4 %collective-permute-start.23 = (bf16[128,8192]{1,0:T(8,128)(2,1)S(1)}, bf16[128,8192]{1,0:T(8,128)(2,1)S(1)}, u32[]{:S(2)}, u32[]{:S(2)}) collective-permute-start(bf16[128,8192]{1,0:T(8,128)(2,1)S(1)} %join_columns.48.message_ref), channel_id=1, source_target_pairs={{0,8},{8,0},{16,24},{24,16},{1,9},{9,1},{17,25},{25,17},{2,10},{10... | collective-permute-start | bytes 6291464 | tf_op jit(solution)/shard_map/ppermute | solution.py:23
  113.7 50.6 %collective-permute-start.19 = (bf16[128,1024]{1,0:T(8,128)(2,1)S(1)}, bf16[128,1024]{1,0:T(8,128)(2,1)S(1)}, u32[]{:S(2)}, u32[]{:S(2)}) collective-permute-start(bf16[128,1024]{1,0:T(8,128)(2,1)S(1)} %join_columns.49.refs_1_), channel_id=1, source_target_pairs={{0,6},{1,7},{2,4},{3,5},{4,2},{5,3},{6,0},{7,1},{8,14},{9,15},{10,... | collective-permute-start | bytes 786440 | tf_op jit(solution)/shard_map/ppermute | solution.py:23
  123.6 40.7 %collective-permute-start.21 = (bf16[128,1024]{1,0:T(8,128)(2,1)S(1)}, bf16[128,1024]{1,0:T(8,128)(2,1)S(1)}, u32[]{:S(2)}, u32[]{:S(2)}) collective-permute-start(bf16[128,1024]{1,0:T(8,128)(2,1)S(1)} %join_columns.50.refs_2_), channel_id=1, source_target_pairs={{0,7},{1,6},{2,5},{3,4},{4,3},{5,2},{6,1},{7,0},{8,15},{9,14},{10,... | collective-permute-start | bytes 786440 | tf_op jit(solution)/shard_map/ppermute | solution.py:23
  126.3 38.0 %collective-permute-start.26 = (bf16[128,2048]{1,0:T(8,128)(2,1)S(1)}, bf16[128,2048]{1,0:T(8,128)(2,1)S(1)}, u32[]{:S(2)}, u32[]{:S(2)}) collective-permute-start(bf16[128,2048]{1,0:T(8,128)(2,1)S(1)} %join_columns.51.refs_2_.refs_0_.refs_3_), channel_id=1, source_target_pairs={{0,16},{8,24},{16,0},{24,8},{1,17},{9,25},{17,1},{25,9},{2,18},{10... | collective-permute-start | bytes 1572872 | tf_op jit(solution)/shard_map/ppermute | solution.py:23
  127.0 29.2 %collective-permute-start.24 = (bf16[128,4096]{1,0:T(8,128)(2,1)S(1)}, bf16[128,4096]{1,0:T(8,128)(2,1)S(1)}, u32[]{:S(2)}, u32[]{:S(2)}) collective-permute-start(bf16[128,4096]{1,0:T(8,128)(2,1)S(1)} %join_columns.52.message_ref), channel_id=1, source_target_pairs={{0,8},{8,0},{16,24},{24,16},{1,9},{9,1},{17,25},{25,17},{2,10},{10... | collective-permute-start | bytes 3145736 | tf_op jit(solution)/shard_map/ppermute | solution.py:23
  164.5 2.7 %collective-permute-start.28 = (bf16[128,4096]{1,0:T(8,128)(2,1)S(1)}, bf16[128,4096]{1,0:T(8,128)(2,1)S(1)}, u32[]{:S(2)}, u32[]{:S(2)}) collective-permute-start(bf16[128,4096]{1,0:T(8,128)(2,1)S(1)} %join_columns.54.refs_2_), channel_id=1, source_target_pairs={{0,8},{8,0},{16,24},{24,16},{1,9},{9,1},{17,25},{25,17},{2,10},{10... | collective-permute-start | bytes 3145736 | tf_op jit(solution)/shard_map/ppermute | solution.py:23
  164.5 14.3 %collective-permute-start.27 = (bf16[128,2048]{1,0:T(8,128)(2,1)S(1)}, bf16[128,2048]{1,0:T(8,128)(2,1)S(1)}, u32[]{:S(2)}, u32[]{:S(2)}) collective-permute-start(bf16[128,2048]{1,0:T(8,128)(2,1)S(1)} %join_columns.53.refs_2_.refs_0_), channel_id=1, source_target_pairs={{0,16},{8,24},{16,0},{24,8},{1,17},{9,25},{17,1},{25,9},{2,18},{10... | collective-permute-start | bytes 1572872 | tf_op jit(solution)/shard_map/ppermute | solution.py:23
  178.9 2.7 %collective-permute-start.29 = (bf16[128,4096]{1,0:T(8,128)(2,1)S(1)}, bf16[128,4096]{1,0:T(8,128)(2,1)S(1)}, u32[]{:S(2)}, u32[]{:S(2)}) collective-permute-start(bf16[128,4096]{1,0:T(8,128)(2,1)S(1)} %join_columns.55), channel_id=1, source_target_pairs={{0,8},{8,0},{16,24},{24,16},{1,9},{9,1},{17,25},{25,17},{2,10},{10... | collective-permute-start | bytes 3145736 | tf_op jit(solution)/shard_map/ppermute | solution.py:23

commit v9 on v8

--- a/solution.py
+++ b/solution.py
@@ -11,7 +11,8 @@
 epsilon = 1e-06
 lanes = 128
 first_part = 0.5
-dear = 3 * 10**10
+dear = 24 * 10**10
+dear_per_byte = 2 * 10**5
 ANY = pl.BlockSpec(memory_space=pl.ANY)
 SMEM = pl.BlockSpec(memory_space=pltpu.SMEM)
 VMEM = pl.BlockSpec(memory_space=pltpu.VMEM)
@@ -86,20 +87,21 @@
     )(*arrays, *after)
 
 
-def hold_kernel(message_ref, out_ref):
+def hold_kernel(*refs):
+    out_ref = refs[-1]
     out_ref[...] = jnp.zeros_like(out_ref)
 
 
-def hold(message):
+def hold(message, after, size):
     return pl.pallas_call(
         hold_kernel,
         out_shape=jax.ShapeDtypeStruct((16, lanes), message.dtype),
-        in_specs=[ANY],
+        in_specs=[ANY] * (1 + len(after)),
         out_specs=VMEM,
-        cost_estimate=pl.CostEstimate(flops=dear, bytes_accessed=0, transcendentals=0),
+        cost_estimate=pl.CostEstimate(flops=max(dear, dear_per_byte * size) // lax.axis_size("tok"), bytes_accessed=0, transcendentals=0),
         compiler_params=pltpu.CompilerParams(vmem_limit_bytes=2**20),
         name="hold",
-    )(message)
+    )(message, *after)
 
 
 def mask_kernel(valid_ref, user_ref, cot_ref, *out_refs):
@@ -283,8 +285,11 @@
     ready = []
     tick = []
 
+    sizes = [0]
+
     def send(axis, distance, parts, after=()):
         message = join(parts, [*tick, *after])
+        sizes.append(2 * message.size)
         tick[:] = [message]
         return message, exchange(message, axis, distance)
 
@@ -299,127 +304,160 @@
     outgoing = pack(tok, hidden, list(range(tok_count)), own_width, [masked[0]])
     ready += [(0, i, outgoing[0], start) for i, (start, _) in enumerate(pieces)]
 
-    far_steps = []
-    for i, (start, width) in enumerate(pieces):
-        for d in range(half, tok_count, 2):
-            far_steps.append([("block", e, i) for e in (d, d + 1)])
-    far_steps.insert(1, [("cots", half, 0), ("cots", half, 1)])
+    far = list(range(half + 1, tok_count))
+    far_steps = [[(half, None), ("cots", None)], [None, None]]
+    while len(far) > 1:
+        far_steps += [[(far.pop(0), None), (far.pop(0), None)], [None, None]]
+    far_steps += [[(far[0], 0), ("wait", None)], [(far[0], 1), None]]
+    last_pair = len(far_steps) - 3
     near = list(range(1, half))
-    near_steps = [near[:2]] + [near[i : i + 2] if tok_count > 8 else near[i : i + 1] for i in range(2, len(near), 2)]
-    relay_bits = [half >> i for i in range(1, half.bit_length())]
+    near_steps = [near[:2]] + [[d] for d in near[2:]]
+    relayed = set()
+
+    def bits_below(d):
+        return [1 << i for i in range(((d & -d) or 1).bit_length() - 1)]
+
 
     lanes_before = [None, None]
     near_before, relay_before, cross_before, core_before = [], [], None, None
-    gradients = []
+    crossed = []
+    gradients = [None, None]
     done = set()
 
     def finish_core():
         nonlocal core_before
-        if core_before is None:
-            return
-        blocks, own, other, both = core_before
-        core_before = None
-        total = sum(pieces[i][1] for _, i, _, _ in blocks)
-        to = 0
-        for d, i, _, _ in blocks:
-            lefts[d, i] = {0: (own, to), across: (other, to), core: (both, to), across ^ core: (both, total + to)}
-            to += pieces[i][1]
-
-    def add_products(step):
-        if len(cots) < tok_count:
-            return
-        for i, (_, width) in enumerate(pieces):
-            here = [d for d in range(tok_count) if (d, i) in lefts and (d, i) not in done]
-            all_here = all((d, i) in lefts for d in range(tok_count))
-            if not here or not (all_here or (i == 1 and step >= len(far_steps))):
-                continue
-            before = gradients[i] if len(gradients) > i else None
-            final = all_here and i == 1
-            out = product(
-                [[lefts[d, i][s] for d in here] for s in slots],
-                [[cots[d][s] for d in here] for s in slots],
-                width,
-                columns,
-                held=before[0] if before else None,
-                sums=gradients[0][1] if final else None,
-                copies=0 if not all_here else tok_count * user_count if final else 1,
-            )
-            done.update((d, i) for d in here)
-            gradients[i : i + 1] = [out]
-            tick.append(out[0])
-
-    for step in range(len(far_steps) + 2):
-        arrivals = []
-        for lane in (0, 1):
-            after = []
-            if lanes_before[lane] is not None:
-                after.append(lanes_before[lane][1])
-                arrivals.append(lanes_before[lane])
-                lanes_before[lane] = None
-            if step < len(far_steps):
-                kind, d, i = far_steps[step][lane]
-                if kind == "block":
-                    parts = [(outgoing[d], *pieces[i])]
-                else:
-                    parts = cot_parts(0)[lane * user_count // 2 : (lane + 1) * user_count // 2]
-                message = send("tok", d, parts, after)
-                lanes_before[lane] = (far_steps[step][lane], message[1])
-        for (kind, d, i), array in arrivals:
-            if kind == "block":
-                ready.append((d, i, array, 0))
-            else:
-                cots.setdefault(d, [])
-                cots[d] = cots[d] + [(array, s * columns) for s in range(user_count // 2)]
-        for d, array in near_before:
-            ready += [(d, i, array, start) for i, (start, _) in enumerate(pieces)]
-            if d & (d - 1) == 0:
-                cots[d] = cots_at(array, own_width)
+        if core_before is not None:
+            units, both = core_before
+            core_before = None
+            to = 0
+            for blocks, own, other in units:
+                total = sum(pieces[i][1] for _, i, _, _ in blocks)
+                at = 0
+                for d, i, _, _ in blocks:
+                    lefts[d, i] = {
+                        0: (own, at),
+                        across: (other, at),
+                        core: (both, to + at),
+                        across ^ core: (both, to + total + at),
+                    }
+                    at += pieces[i][1]
+                to += 2 * total
+
+    def finish_relays():
         for bit, sources, array in relay_before:
             for at, d in enumerate(sources):
                 cots[d + bit] = cots_at(array, at * model_width)
-        near_before, relay_before = [], []
-        crossed = cross_before
+        relay_before.clear()
+
+    def add_products(i):
+        width = pieces[i][1]
+        here = [d for d in range(tok_count) if d in cots and (d, i) in lefts and (d, i) not in done]
+        if not here:
+            return
+        done.update((d, i) for d in here)
+        full = all((d, i) in done for d in range(tok_count))
+        out = product(
+            [[lefts[d, i][s] for d in here] for s in slots],
+            [[cots[d][s] for d in here] for s in slots],
+            width,
+            columns,
+            held=gradients[i][0] if gradients[i] else None,
+            sums=gradients[0][1] if full and i == 1 else None,
+            copies=0 if not full else tok_count * user_count if i == 1 else 1,
+        )
+        gradients[i] = out
+        tick.append(out[0])
+
+    for step in range(len(far_steps) + 2):
+        flying = 0
+        now = far_steps[step] if step < len(far_steps) else [None, ("wait", None)]
+        if step == len(far_steps):
+            now = [("wait", None), None]
+        for lane in (0, 1):
+            if lane == 1 and now[1] == ("cots", None):
+                continue
+            if now[lane] is not None:
+                after = []
+                if lanes_before[lane] is not None:
+                    (d, i), array = lanes_before[lane]
+                    lanes_before[lane] = None
+                    after.append(array)
+                    if d == "cots":
+                        cots[half] = cots_at(array, 0)
+                    else:
+                        first = pieces[i][0] if i is not None else 0
+                        ready += [
+                            (d, j, array, at - first) for j, (at, _) in enumerate(pieces) if i is None or i == j
+                        ]
+                d, i = now[lane]
+                if d != "wait":
+                    first, width = pieces[i] if i is not None else (0, own_width)
+                    array = send("tok", d, [(outgoing[d], first, width)], after)[1]
+                    lanes_before[lane] = (now[lane], array)
+            flying += lanes_before[lane] is not None
+        for d, array in near_before:
+            ready += [(d, i, array, first) for i, (first, _) in enumerate(pieces)]
+            if d & (d - 1) == 0:
+                cots[d] = cots_at(array, own_width)
+        near_before.clear()
+        arrivals = [array for _, _, array in relay_before]
+        finish_relays()
+        if cross_before is not None:
+            crossed.append(cross_before)
+        earlier = [cross_before[2]] if cross_before is not None else []
         cross_before = None
         if ready:
             blocks = []
             while ready and sum(pieces[i][1] for _, i, _, _ in blocks) < 2 * own_width:
                 blocks.append(ready.pop(0))
-            parts = [(array, start, pieces[i][1]) for _, i, array, start in blocks]
-            own, other = send("user", across, parts, [crossed[2]] if crossed else [])
+            parts = [(array, first, pieces[i][1]) for _, i, array, first in blocks]
+            own, other = send("user", across, parts, earlier)
             cross_before = (blocks, own, other)
+            flying += 1
         if step == 0:
             cots[0] = [(block, 0) for block in by_slot]
-            cots[0] = cots_at(join(cot_parts(0), []), 0)
+            cots[0] = cots_at(join(cot_parts(0), tick), 0)
+            lanes_before[1] = (("cots", None), send("tok", half, cot_parts(0))[1])
+            flying += 1
         if step < len(near_steps):
             for d in near_steps[step]:
                 parts = [(outgoing[d], 0, own_width)]
                 if d & (d - 1) == 0:
                     parts += cot_parts(0)
                 near_before.append((d, send("tok", d, parts)[1]))
-        if relay_bits:
-            bit = relay_bits[0]
-            sources = list(range(2 * bit, tok_count, 2 * bit))
-            if all(d in cots and len(cots[d]) == user_count for d in sources):
-                relay_bits.pop(0)
+                flying += 1
+        before = [core_before[1]] if core_before else []
+        finish_core()
+        relays_wait = any(
+            d and d + bit not in relayed for d in cots for bit in bits_below(d)
+        )
+        if crossed and (flying < 5 - relays_wait or step > last_pair):
+            parts = []
+            for blocks, own, other in crossed:
+                total = sum(pieces[i][1] for _, i, _, _ in blocks)
+                parts += [(own, 0, total), (other, 0, total)]
+            core_before = (list(crossed), send("user", core, parts, before)[1])
+            crossed.clear()
+            flying += 1
+        bit = half // 2
+        while bit:
+            sources = [d for d in sorted(cots) if bit in bits_below(d) and d + bit not in relayed]
+            if sources and flying < 5:
+                relayed.update(d + bit for d in sources)
                 parts = [part for d in sources for part in cot_parts(d)]
                 relay_before.append((bit, sources, send("tok", bit, parts)[1]))
-        earlier = [core_before[3]] if core_before else []
-        finish_core()
-        if crossed:
-            blocks, own, other = crossed
-            total = sum(pieces[i][1] for _, i, _, _ in blocks)
-            both = send("user", core, [(own, 0, total), (other, 0, total)], earlier)[1]
-            core_before = (blocks, own, other, both)
+                flying += 1
+            bit //= 2
         if step < len(far_steps):
-            tick[:] = [hold(tick[0])]
-        if step >= len(far_steps) - 1:
+            tick[:] = [hold(tick[0], arrivals, max(sizes))]
+            sizes[:] = [0]
+        if step == last_pair:
             finish_core()
-            if relay_before:
-                for bit, sources, array in relay_before:
-                    for at, d in enumerate(sources):
-                        cots[d + bit] = cots_at(array, at * model_width)
-                relay_before = []
-            add_products(step)
+            add_products(0)
+            add_products(1)
+    finish_core()
+    add_products(0)
+    add_products(1)
     sums = lax.all_to_all(gradients[1][1], ("user", "tok"), split_axis=0, concat_axis=0, tiled=True)
     return combine(user, sums, [g[0] for g in gradients], clip_bound, scaling)
 

time: 208 us -> 203 us (0.976)
  starting transfers between devices: 58.4 us -> 31 us
  waiting for transfers between devices: 102 us -> 121 us
  Pallas kernels: 26 us -> 34 us
  blocking collectives: 17.1 us -> 11.9 us
    ppermute x30 -> x26, starting transfers between devices: 58.4 us -> 31 us  [exchange(): return lax.ppermute(block, axis, [(i, i ^ distance) for i in range(size)])]
    ppermute x30 -> x26, waiting for transfers between devices: 102 us -> 121 us  [exchange(): return lax.ppermute(block, axis, [(i, i ^ distance) for i in range(size)])]
    all_to_all x1, blocking collectives: 17.1 us -> 11.9 us  [body(): lax.all_to_all(gradients[1][1], ('user', 'tok'), split_axis=0, concat_axi...]
    pallas_call x3 -> x4, Pallas kernels: 19.4 us -> 24.6 us  [product(): pl.pallas_call(functools.partial(product_kernel, left_places, right_place...]
    pallas_call x28 -> x24, Pallas kernels: 1.39 us -> 4.19 us  [join(): pl.pallas_call(functools.partial(join_kernel, places), out_shape=jax.Shap...]
    unnamed x4 -> x16, local copies, waits for them, and re-layouts: 3.22 us -> 4.33 us
  transfers between devices with their start and end apart: 30 -> 26, of which waited for: 13 -> 10; matrix products, arithmetic and copies ran while one was open for 0% -> 0% of each run, Pallas kernels for 8% -> 12%
where the time goes in v9:
time: 203 us
  waiting for transfers between devices  121 us (60%)
  Pallas kernels  34 us (17%)
  starting transfers between devices  31 us (15%)
  blocking collectives  11.9 us (6%)
  local copies, waits for them, and re-layouts  4.33 us (2%)
    ppermute x26, waiting for transfers between devices, exchange(): return lax.ppermute(block, axis, [(i, i ^ distance) for i in range(size)])  121 us
    ppermute x26, starting transfers between devices, exchange(): return lax.ppermute(block, axis, [(i, i ^ distance) for i in range(size)])  31 us
    pallas_call x4, Pallas kernels, product(): pl.pallas_call(functools.partial(product_kernel, left_places, right_place...  24.6 us
    all_to_all x1, blocking collectives, body(): lax.all_to_all(gradients[1][1], ('user', 'tok'), split_axis=0, concat_axi...  11.9 us
    pallas_call x1, Pallas kernels, combine(): pl.pallas_call(functools.partial(combine_kernel, user_count, clip_bound,...  4.81 us
    unnamed x16, local copies, waits for them, and re-layouts  4.33 us
    pallas_call x24, Pallas kernels, join(): pl.pallas_call(functools.partial(join_kernel, places), out_shape=jax.Shap...  4.19 us
  transfers between devices with their start and end apart: 26, of which 10 were waited for; matrix products, arithmetic and copies ran while one was open for 0% of the time, Pallas kernels for 12%

profile of v9, /device:TPU:0, one launch (start us, length us, event | category | flops | bytes accessed | tf_op | source)
XLA Modules:
  0.0 202.8 jit_solution(5776961602892411907)
XLA Ops:
  0.7 1.0 copy-done.7
  1.7 0.5 collective-permute-start
  2.3 2.6 %collective-permute-start.1 = (bf16[128,512]{1,0:T(8,128)(2,1)S(1)}, bf16[128,512]{1,0:T(8,128)(2,1)S(1)}, u32[]{:S(2)}, u32[]{:S(2)}) collective-permute-start(bf16[128,512]{1,0:T(8,128)(2,1)S(1)} %get-tuple-element.25), channel_id=1, source_target_pairs={{0,16},{8,24},{16,0},{24,8},{1,17},{9,25},{17,1},{25,9},{2,18},{10... | collective-permute-start | bytes 393224 | tf_op jit(solution)/shard_map/ppermute | solution.py:24
  4.8 0.1 collective-permute-start.2
  4.9 2.2 %copy-done.6 = bf16[1,128,16384]{2,1,0:T(8,128)(2,1)S(1)} copy-done((bf16[1,128,16384]{2,1,0:T(8,128)(2,1)S(1)}, bf16[1,128,16384]{2,1,0:T(8,128)(2,1)}, u32[]{:S(2)}) %copy-start.6) | copy-done | bytes 4194328
  7.1 0.4 pack_columns.1
  7.5 2.9 %collective-permute-start.6 = (bf16[128,2048]{1,0:T(8,128)(2,1)S(1)}, bf16[128,2048]{1,0:T(8,128)(2,1)S(1)}, u32[]{:S(2)}, u32[]{:S(2)}) collective-permute-start(bf16[128,2048]{1,0:T(8,128)(2,1)S(1)} %join_columns.24.refs_1_), channel_id=1, source_target_pairs={{0,4},{1,5},{2,6},{3,7},{4,0},{5,1},{6,2},{7,3},{8,12},{9,13},{10,... | collective-permute-start | bytes 1572872 | tf_op jit(solution)/shard_map/ppermute | solution.py:24
  10.4 1.6 collective-permute-start.5
  12.1 0.1 join_columns.28.refs_2_
  12.2 1.6 collective-permute-start.4
  13.8 0.1 join_columns.29.refs_0_
  13.9 1.6 collective-permute-start.3
  15.5 2.1 %collective-permute-start.8 = (bf16[128,2048]{1,0:T(8,128)(2,1)S(1)}, bf16[128,2048]{1,0:T(8,128)(2,1)S(1)}, u32[]{:S(2)}, u32[]{:S(2)}) collective-permute-start(bf16[128,2048]{1,0:T(8,128)(2,1)S(1)} %join_columns.27.refs_2_), channel_id=1, source_target_pairs={{0,4},{1,5},{2,6},{3,7},{4,0},{5,1},{6,2},{7,3},{8,12},{9,13},{10,... | collective-permute-start | bytes 1572872 | tf_op jit(solution)/shard_map/ppermute | solution.py:24
  17.6 6.8 %collective-permute-done.5.refs_3_.refs_1_.refs_5_ = bf16[128,2048]{1,0:T(8,128)(2,1)S(1)} collective-permute-done((bf16[128,2048]{1,0:T(8,128)(2,1)S(1)}, bf16[128,2048]{1,0:T(8,128)(2,1)S(1)}, u32[]{:S(2)}, u32[]{:S(2)}) %collective-permute-start.5) | collective-permute-done | bytes 524320 | tf_op jit(solution)/shard_map/ppermute | solution.py:24
  24.4 35.4 %collective-permute-done.3.refs_1_.refs_0_.refs_10_ = bf16[128,4096]{1,0:T(8,128)(2,1)S(1)} collective-permute-done((bf16[128,4096]{1,0:T(8,128)(2,1)S(1)}, bf16[128,4096]{1,0:T(8,128)(2,1)S(1)}, u32[]{:S(2)}, u32[]{:S(2)}) %collective-permute-start.3) | collective-permute-done | bytes 1048608 | tf_op jit(solution)/shard_map/ppermute | solution.py:24
  59.8 0.0 collective-permute-done.4.refs_0_.refs_9_
  59.8 0.1 join_columns.30.refs_1_.refs_2_
  59.9 1.6 collective-permute-start.10
  61.5 0.1 collective-permute-start.11
  61.7 1.1 collective-permute-start.14
  62.7 0.8 join_columns.33.refs_1_
  63.6 6.3 %collective-permute-start.7 = (bf16[128,2048]{1,0:T(8,128)(2,1)}, bf16[128,2048]{1,0:T(8,128)(2,1)}, u32[]{:S(2)}, u32[]{:S(2)}) collective-permute-start(bf16[128,2048]{1,0:T(8,128)(2,1)} %join_columns.33.refs_1_), channel_id=1, source_target_pairs={{0,5},{1,4},{2,7},{3,6},{4,1},{5,0},{6,3},{7,2},{8,13},{9,12},{10,... | collective-permute-start | bytes 1572872 | tf_op jit(solution)/shard_map/ppermute | solution.py:24
  69.9 0.0 collective-permute-done.8.refs_2_.refs_0_.refs_12_
  69.9 0.8 join_columns.34.refs_2_
  70.7 15.4 %collective-permute-done.11.refs_1_ = bf16[128,2048]{1,0:T(8,128)(2,1)S(1)} collective-permute-done((bf16[128,2048]{1,0:T(8,128)(2,1)S(1)}, bf16[128,2048]{1,0:T(8,128)(2,1)S(1)}, u32[]{:S(2)}, u32[]{:S(2)}) %collective-permute-start.11) | collective-permute-done | bytes 524320 | tf_op jit(solution)/shard_map/ppermute | solution.py:24
  86.1 0.1 join_columns.35.refs_4_.refs_0_.refs_2_
  86.2 0.4 collective-permute-start.13
  86.6 0.2 join_columns.36.refs_1_
  86.8 0.1 collective-permute-start.15
  86.9 9.5 %collective-permute-done.14.refs_1_.refs_11_ = bf16[128,2048]{1,0:T(8,128)(2,1)S(1)} collective-permute-done((bf16[128,2048]{1,0:T(8,128)(2,1)S(1)}, bf16[128,2048]{1,0:T(8,128)(2,1)S(1)}, u32[]{:S(2)}, u32[]{:S(2)}) %collective-permute-start.14) | collective-permute-done | bytes 524320 | tf_op jit(solution)/shard_map/ppermute | solution.py:24
  96.5 0.8 collective-permute-start.12
  97.2 12.1 %collective-permute-done.13.refs_1_.refs_7_ = bf16[128,4096]{1,0:T(8,128)(2,1)S(1)} collective-permute-done((bf16[128,4096]{1,0:T(8,128)(2,1)S(1)}, bf16[128,4096]{1,0:T(8,128)(2,1)S(1)}, u32[]{:S(2)}, u32[]{:S(2)}) %collective-permute-start.13) | collective-permute-done | bytes 1048608 | tf_op jit(solution)/shard_map/ppermute | solution.py:24
  109.3 0.0 collective-permute-done.15.refs_3_
  109.3 0.1 join_columns.38.refs_2_
  109.5 0.1 collective-permute-start.16
  109.6 6.7 %collective-permute-done.12.refs_1_.refs_7_ = bf16[128,2048]{1,0:T(8,128)(2,1)S(1)} collective-permute-done((bf16[128,2048]{1,0:T(8,128)(2,1)S(1)}, bf16[128,2048]{1,0:T(8,128)(2,1)S(1)}, u32[]{:S(2)}, u32[]{:S(2)}) %collective-permute-start.12) | collective-permute-done | bytes 524320 | tf_op jit(solution)/shard_map/ppermute | solution.py:24
  116.3 0.1 join_columns.39.refs_0_
  116.4 0.0 copy-start.5
  116.4 0.6 collective-permute-start.17
  117.0 0.0 collective-permute-done.16.refs_4_
  117.0 0.4 copy-done.1
  117.4 0.3 copy-done.3
  117.7 0.3 copy-done.5
  118.1 6.6 %product_and_squares.5.refs_3_.refs_8_ = f32[4,1024,512]{2,1,0:T(8,128)S(1)} custom-call(bf16[128,2048]{1,0:T(8,128)(2,1)S(1)} %join_columns.25.refs_4_.refs_1_.refs_0_, bf16[128,4096]{1,0:T(8,128)(2,1)S(1)} %join_columns.30.refs_1_.refs_2_, bf16[128,4096]{1,0:T(8,128)(2,1)S(1)} %join_columns.35.refs_4_.refs_0_.refs_2_, ...), custom_call_target="tpu_custom_call" | custom-call | flops 2684354560 | bytes 7864320 | tf_op jit(solution)/shard_map/product_and_squares/pallas_call | solution.py:194
  124.7 6.6 %product_and_squares.4.refs_2_.refs_8_ = f32[4,1024,512]{2,1,0:T(8,128)S(1)} custom-call(bf16[128,2048]{1,0:T(8,128)(2,1)S(1)} %join_columns.25.refs_4_.refs_1_.refs_0_, bf16[128,4096]{1,0:T(8,128)(2,1)S(1)} %join_columns.30.refs_1_.refs_2_, bf16[128,4096]{1,0:T(8,128)(2,1)S(1)} %join_columns.35.refs_4_.refs_0_.refs_2_, ...), custom_call_target="tpu_custom_call" | custom-call | flops 2684354560 | bytes 7864320 | tf_op jit(solution)/shard_map/product_and_squares/pallas_call | solution.py:194
  131.3 1.6 collective-permute-start.18
  132.9 1.3 join_columns.41.refs_0_
  134.2 0.9 collective-permute-start.20
  135.1 12.0 %collective-permute-done.17.refs_1_.refs_6_ = bf16[128,4096]{1,0:T(8,128)(2,1)S(1)} collective-permute-done((bf16[128,4096]{1,0:T(8,128)(2,1)S(1)}, bf16[128,4096]{1,0:T(8,128)(2,1)S(1)}, u32[]{:S(2)}, u32[]{:S(2)}) %collective-permute-start.17) | collective-permute-done | bytes 1048608 | tf_op jit(solution)/shard_map/ppermute | solution.py:24
  147.2 0.0 collective-permute-done.18.refs_2_.refs_0_
  147.2 1.4 collective-permute-start.19
  148.6 10.2 %collective-permute-done.20.refs_2_.refs_1_.refs_4_ = bf16[128,4096]{1,0:T(8,128)(2,1)S(1)} collective-permute-done((bf16[128,4096]{1,0:T(8,128)(2,1)S(1)}, bf16[128,4096]{1,0:T(8,128)(2,1)S(1)}, u32[]{:S(2)}, u32[]{:S(2)}) %collective-permute-start.20) | collective-permute-done | bytes 1048608 | tf_op jit(solution)/shard_map/ppermute | solution.py:24
  158.9 1.3 collective-permute-start.21
  160.1 0.1 join_columns.44.refs_0_
  160.3 0.1 collective-permute-start.22
  160.4 5.3 %collective-permute-done.21.refs_2_.refs_1_.refs_5_ = bf16[128,1024]{1,0:T(8,128)(2,1)S(1)} collective-permute-done((bf16[128,1024]{1,0:T(8,128)(2,1)S(1)}, bf16[128,1024]{1,0:T(8,128)(2,1)S(1)}, u32[]{:S(2)}, u32[]{:S(2)}) %collective-permute-start.21) | collective-permute-done | bytes 262176 | tf_op jit(solution)/shard_map/ppermute | solution.py:24
  165.8 0.1 collective-permute-start.24
  165.8 1.7 collective-permute-start.23
  167.6 7.0 %collective-permute-done.23.refs_1_.refs_5_ = bf16[128,1024]{1,0:T(8,128)(2,1)S(1)} collective-permute-done((bf16[128,1024]{1,0:T(8,128)(2,1)S(1)}, bf16[128,1024]{1,0:T(8,128)(2,1)S(1)}, u32[]{:S(2)}, u32[]{:S(2)}) %collective-permute-start.23) | collective-permute-done | bytes 262176 | tf_op jit(solution)/shard_map/ppermute | solution.py:24
  174.6 0.1 collective-permute-start.25
  174.7 5.7 %product_and_squares.6 = (f32[4,1024,512]{2,1,0:T(8,128)S(1)}, f32[1,8,128]{2,1,0:T(8,128)S(1)}) custom-call(bf16[128,4096]{1,0:T(8,128)(2,1)S(1)} %join_columns.41.refs_0_, bf16[128,1024]{1,0:T(8,128)(2,1)S(1)} %join_columns.43.refs_2_.refs_0_.refs_1_, ...), custom_call_target="tpu_custom_call", output_to_operand_aliasing={{0}: (8, {})} | custom-call | flops 1610612736 | bytes 4718592 | tf_op jit(solution)/shard_map/product_and_squares/pallas_call | solution.py:194
  180.4 5.7 %product_and_squares.7 = (f32[4,1024,512]{2,1,0:T(8,128)S(1)}, f32[32,8,128]{2,1,0:T(8,128)S(1)}) custom-call(bf16[128,4096]{1,0:T(8,128)(2,1)S(1)} %join_columns.41.refs_0_, bf16[128,1024]{1,0:T(8,128)(2,1)S(1)} %join_columns.45.refs_2_.refs_0_.refs_1_, ...), custom_call_target="tpu_custom_call", output_to_operand_aliasing={{0}: (8, {})} | custom-call | flops 1610612736 | bytes 4718592 | tf_op jit(solution)/shard_map/product_and_squares/pallas_call | solution.py:194
  186.1 11.9 %all_to_all.5.sums_ref = f32[32,8,128]{2,1,0:T(8,128)S(1)} all-to-all(f32[32,8,128]{2,1,0:T(8,128)S(1)} %get-tuple-element.34), channel_id=1, replica_groups=mesh['user'=4,'tok'=8] {'user','tok'}, dimensions={0} | all-to-all | bytes 262144 | tf_op jit(solution)/shard_map/all_to_all | solution.py:461
  198.0 4.8 %weighted_sum.1 = f32[2048,512]{1,0:T(8,128)} custom-call(s32[1]{0:T(128)} %bitcast.user_ref, f32[32,8,128]{2,1,0:T(8,128)S(1)} %all_to_all.5.sums_ref, f32[4,1024,512]{2,1,0:T(8,128)S(1)} %get-tuple-element.35.refs_0_, f32[4,1024,512]{2,1,0:T(8,128)S(1)} %get-tuple-element.36.refs_1_), custom_call_target="tpu_custom_call" | custom-call | tf_op jit(solution)/shard_map/weighted_sum/pallas_call | solution.py:251
  (42 shorter events, 0.5 us)
Async XLA Ops:
  0.7 1.0 copy-start.7
  1.7 10.3 %collective-permute-start = (bf16[128,512]{1,0:T(8,128)(2,1)S(1)}, bf16[128,512]{1,0:T(8,128)(2,1)S(1)}, u32[]{:S(2)}, u32[]{:S(2)}) collective-permute-start(bf16[128,512]{1,0:T(8,128)(2,1)S(1)} %get-tuple-element.24), channel_id=1, source_target_pairs={{0,8},{8,0},{16,24},{24,16},{1,9},{9,1},{17,25},{25,17},{2,10},{10... | collective-permute-start | bytes 393224 | tf_op jit(solution)/shard_map/ppermute | solution.py:24
  2.3 9.7 %collective-permute-start.1 = (bf16[128,512]{1,0:T(8,128)(2,1)S(1)}, bf16[128,512]{1,0:T(8,128)(2,1)S(1)}, u32[]{:S(2)}, u32[]{:S(2)}) collective-permute-start(bf16[128,512]{1,0:T(8,128)(2,1)S(1)} %get-tuple-element.25), channel_id=1, source_target_pairs={{0,16},{8,24},{16,0},{24,8},{1,17},{9,25},{17,1},{25,9},{2,18},{10... | collective-permute-start | bytes 393224 | tf_op jit(solution)/shard_map/ppermute | solution.py:24
  4.8 7.2 %collective-permute-start.2 = (bf16[128,512]{1,0:T(8,128)(2,1)S(1)}, bf16[128,512]{1,0:T(8,128)(2,1)S(1)}, u32[]{:S(2)}, u32[]{:S(2)}) collective-permute-start(bf16[128,512]{1,0:T(8,128)(2,1)S(1)} %get-tuple-element.26), channel_id=1, source_target_pairs={{0,24},{8,16},{16,8},{24,0},{1,25},{9,17},{17,9},{25,1},{2,26},{10... | collective-permute-start | bytes 393224 | tf_op jit(solution)/shard_map/ppermute | solution.py:24
  4.9 2.2 %copy-start.6 = (bf16[1,128,16384]{2,1,0:T(8,128)(2,1)S(1)}, bf16[1,128,16384]{2,1,0:T(8,128)(2,1)}, u32[]{:S(2)}) copy-start(bf16[1,128,16384]{2,1,0:T(8,128)(2,1)} %hidden_ref.1) | copy-start | bytes 12582916
  7.5 55.2 %collective-permute-start.6 = (bf16[128,2048]{1,0:T(8,128)(2,1)S(1)}, bf16[128,2048]{1,0:T(8,128)(2,1)S(1)}, u32[]{:S(2)}, u32[]{:S(2)}) collective-permute-start(bf16[128,2048]{1,0:T(8,128)(2,1)S(1)} %join_columns.24.refs_1_), channel_id=1, source_target_pairs={{0,4},{1,5},{2,6},{3,7},{4,0},{5,1},{6,2},{7,3},{8,12},{9,13},{10,... | collective-permute-start | bytes 1572872 | tf_op jit(solution)/shard_map/ppermute | solution.py:24
  10.4 14.0 %collective-permute-start.5 = (bf16[128,2048]{1,0:T(8,128)(2,1)S(1)}, bf16[128,2048]{1,0:T(8,128)(2,1)S(1)}, u32[]{:S(2)}, u32[]{:S(2)}) collective-permute-start(bf16[128,2048]{1,0:T(8,128)(2,1)S(1)} %join_columns.25.refs_4_.refs_1_.refs_0_), channel_id=1, source_target_pairs={{0,16},{8,24},{16,0},{24,8},{1,17},{9,25},{17,1},{25,9},{2,18},{10... | collective-permute-start | bytes 1572872 | tf_op jit(solution)/shard_map/ppermute | solution.py:24
  12.1 3.5 %copy-start = (bf16[128,2048]{1,0:T(8,128)(2,1)}, bf16[128,2048]{1,0:T(8,128)(2,1)S(1)}, u32[]{:S(2)}) copy-start(bf16[128,2048]{1,0:T(8,128)(2,1)S(1)} %join_columns.26.refs_0_.refs_1_.refs_8_) | copy-start | bytes 1572868
  12.2 47.6 %collective-permute-start.4 = (bf16[128,4096]{1,0:T(8,128)(2,1)S(1)}, bf16[128,4096]{1,0:T(8,128)(2,1)S(1)}, u32[]{:S(2)}, u32[]{:S(2)}) collective-permute-start(bf16[128,4096]{1,0:T(8,128)(2,1)S(1)} %join_columns.28.refs_2_), channel_id=1, source_target_pairs={{0,1},{1,0},{2,3},{3,2},{4,5},{5,4},{6,7},{7,6},{8,9},{9,8},{10,11... | collective-permute-start | bytes 3145736 | tf_op jit(solution)/shard_map/ppermute | solution.py:24
  13.9 46.0 %collective-permute-start.3 = (bf16[128,4096]{1,0:T(8,128)(2,1)S(1)}, bf16[128,4096]{1,0:T(8,128)(2,1)S(1)}, u32[]{:S(2)}, u32[]{:S(2)}) collective-permute-start(bf16[128,4096]{1,0:T(8,128)(2,1)S(1)} %join_columns.29.refs_0_), channel_id=1, source_target_pairs={{0,2},{1,3},{2,0},{3,1},{4,6},{5,7},{6,4},{7,5},{8,10},{9,11},{10,... | collective-permute-start | bytes 3145736 | tf_op jit(solution)/shard_map/ppermute | solution.py:24
  15.5 54.4 %collective-permute-start.8 = (bf16[128,2048]{1,0:T(8,128)(2,1)S(1)}, bf16[128,2048]{1,0:T(8,128)(2,1)S(1)}, u32[]{:S(2)}, u32[]{:S(2)}) collective-permute-start(bf16[128,2048]{1,0:T(8,128)(2,1)S(1)} %join_columns.27.refs_2_), channel_id=1, source_target_pairs={{0,4},{1,5},{2,6},{3,7},{4,0},{5,1},{6,2},{7,3},{8,12},{9,13},{10,... | collective-permute-start | bytes 1572872 | tf_op jit(solution)/shard_map/ppermute | solution.py:24
  59.8 2.9 %copy-start.2 = (bf16[128,4096]{1,0:T(8,128)(2,1)}, bf16[128,4096]{1,0:T(8,128)(2,1)S(1)}, u32[]{:S(2)}) copy-start(bf16[128,4096]{1,0:T(8,128)(2,1)S(1)} %collective-permute-done.3.refs_1_.refs_0_.refs_10_) | copy-start | bytes 3145732
  59.8 2.9 %copy-start.4 = (bf16[128,4096]{1,0:T(8,128)(2,1)}, bf16[128,4096]{1,0:T(8,128)(2,1)S(1)}, u32[]{:S(2)}) copy-start(bf16[128,4096]{1,0:T(8,128)(2,1)S(1)} %collective-permute-done.4.refs_0_.refs_9_) | copy-start | bytes 3145732
  59.9 26.2 %collective-permute-start.10 = (bf16[128,4096]{1,0:T(8,128)(2,1)S(1)}, bf16[128,4096]{1,0:T(8,128)(2,1)S(1)}, u32[]{:S(2)}, u32[]{:S(2)}) collective-permute-start(bf16[128,4096]{1,0:T(8,128)(2,1)S(1)} %join_columns.30.refs_1_.refs_2_), channel_id=1, source_target_pairs={{0,16},{8,24},{16,0},{24,8},{1,17},{9,25},{17,1},{25,9},{2,18},{10... | collective-permute-start | bytes 3145736 | tf_op jit(solution)/shard_map/ppermute | solution.py:24
  61.5 24.6 %collective-permute-start.11 = (bf16[128,2048]{1,0:T(8,128)(2,1)S(1)}, bf16[128,2048]{1,0:T(8,128)(2,1)S(1)}, u32[]{:S(2)}, u32[]{:S(2)}) collective-permute-start(bf16[128,2048]{1,0:T(8,128)(2,1)S(1)} %join_columns.31.refs_1_), channel_id=1, source_target_pairs={{0,3},{1,2},{2,1},{3,0},{4,7},{5,6},{6,5},{7,4},{8,11},{9,10},{10,... | collective-permute-start | bytes 1572872 | tf_op jit(solution)/shard_map/ppermute | solution.py:24
  61.7 34.8 %collective-permute-start.14 = (bf16[128,2048]{1,0:T(8,128)(2,1)S(1)}, bf16[128,2048]{1,0:T(8,128)(2,1)S(1)}, u32[]{:S(2)}, u32[]{:S(2)}) collective-permute-start(bf16[128,2048]{1,0:T(8,128)(2,1)S(1)} %join_columns.32.refs_0_), channel_id=1, source_target_pairs={{0,1},{1,0},{2,3},{3,2},{4,5},{5,4},{6,7},{7,6},{8,9},{9,8},{10,11... | collective-permute-start | bytes 1572872 | tf_op jit(solution)/shard_map/ppermute | solution.py:24
  63.6 67.7 %collective-permute-start.7 = (bf16[128,2048]{1,0:T(8,128)(2,1)}, bf16[128,2048]{1,0:T(8,128)(2,1)}, u32[]{:S(2)}, u32[]{:S(2)}) collective-permute-start(bf16[128,2048]{1,0:T(8,128)(2,1)} %join_columns.33.refs_1_), channel_id=1, source_target_pairs={{0,5},{1,4},{2,7},{3,6},{4,1},{5,0},{6,3},{7,2},{8,13},{9,12},{10,... | collective-permute-start | bytes 1572872 | tf_op jit(solution)/shard_map/ppermute | solution.py:24
  70.7 62.2 %collective-permute-start.9 = (bf16[128,2048]{1,0:T(8,128)(2,1)}, bf16[128,2048]{1,0:T(8,128)(2,1)}, u32[]{:S(2)}, u32[]{:S(2)}) collective-permute-start(bf16[128,2048]{1,0:T(8,128)(2,1)} %join_columns.34.refs_2_), channel_id=1, source_target_pairs={{0,6},{1,7},{2,4},{3,5},{4,2},{5,3},{6,0},{7,1},{8,14},{9,15},{10,... | collective-permute-start | bytes 1572872 | tf_op jit(solution)/shard_map/ppermute | solution.py:24
  86.2 23.2 %collective-permute-start.13 = (bf16[128,4096]{1,0:T(8,128)(2,1)S(1)}, bf16[128,4096]{1,0:T(8,128)(2,1)S(1)}, u32[]{:S(2)}, u32[]{:S(2)}) collective-permute-start(bf16[128,4096]{1,0:T(8,128)(2,1)S(1)} %join_columns.35.refs_4_.refs_0_.refs_2_), channel_id=1, source_target_pairs={{0,16},{8,24},{16,0},{24,8},{1,17},{9,25},{17,1},{25,9},{2,18},{10... | collective-permute-start | bytes 3145736 | tf_op jit(solution)/shard_map/ppermute | solution.py:24
  86.8 22.5 %collective-permute-start.15 = (bf16[128,12288]{1,0:T(8,128)(2,1)S(1)}, bf16[128,12288]{1,0:T(8,128)(2,1)S(1)}, u32[]{:S(2)}, u32[]{:S(2)}) collective-permute-start(bf16[128,12288]{1,0:T(8,128)(2,1)S(1)} %join_columns.36.refs_1_), channel_id=1, source_target_pairs={{0,8},{8,0},{16,24},{24,16},{1,9},{9,1},{17,25},{25,17},{2,10},{10... | collective-permute-start | bytes 9437192 | tf_op jit(solution)/shard_map/ppermute | solution.py:24
  96.5 19.8 %collective-permute-start.12 = (bf16[128,2048]{1,0:T(8,128)(2,1)S(1)}, bf16[128,2048]{1,0:T(8,128)(2,1)S(1)}, u32[]{:S(2)}, u32[]{:S(2)}) collective-permute-start(bf16[128,2048]{1,0:T(8,128)(2,1)S(1)} %join_columns.37.refs_0_), channel_id=1, source_target_pairs={{0,2},{1,3},{2,0},{3,1},{4,6},{5,7},{6,4},{7,5},{8,10},{9,11},{10,... | collective-permute-start | bytes 1572872 | tf_op jit(solution)/shard_map/ppermute | solution.py:24
  109.5 7.5 %collective-permute-start.16 = (bf16[128,8192]{1,0:T(8,128)(2,1)S(1)}, bf16[128,8192]{1,0:T(8,128)(2,1)S(1)}, u32[]{:S(2)}, u32[]{:S(2)}) collective-permute-start(bf16[128,8192]{1,0:T(8,128)(2,1)S(1)} %join_columns.38.refs_2_), channel_id=1, source_target_pairs={{0,8},{8,0},{16,24},{24,16},{1,9},{9,1},{17,25},{25,17},{2,10},{10... | collective-permute-start | bytes 6291464 | tf_op jit(solution)/shard_map/ppermute | solution.py:24
  116.4 1.0 copy-start.1
  116.4 1.4 copy-start.3
  116.4 1.7 copy-start.5
  116.4 30.8 %collective-permute-start.17 = (bf16[128,4096]{1,0:T(8,128)(2,1)S(1)}, bf16[128,4096]{1,0:T(8,128)(2,1)S(1)}, u32[]{:S(2)}, u32[]{:S(2)}) collective-permute-start(bf16[128,4096]{1,0:T(8,128)(2,1)S(1)} %join_columns.39.refs_0_), channel_id=1, source_target_pairs={{0,1},{1,0},{2,3},{3,2},{4,5},{5,4},{6,7},{7,6},{8,9},{9,8},{10,11... | collective-permute-start | bytes 3145736 | tf_op jit(solution)/shard_map/ppermute | solution.py:24
  131.3 15.9 %collective-permute-start.18 = (bf16[128,1024]{1,0:T(8,128)(2,1)S(1)}, bf16[128,1024]{1,0:T(8,128)(2,1)S(1)}, u32[]{:S(2)}, u32[]{:S(2)}) collective-permute-start(bf16[128,1024]{1,0:T(8,128)(2,1)S(1)} %join_columns.40.refs_2_), channel_id=1, source_target_pairs={{0,7},{1,6},{2,5},{3,4},{4,3},{5,2},{6,1},{7,0},{8,15},{9,14},{10,... | collective-permute-start | bytes 786440 | tf_op jit(solution)/shard_map/ppermute | solution.py:24
  134.2 24.6 %collective-permute-start.20 = (bf16[128,4096]{1,0:T(8,128)(2,1)S(1)}, bf16[128,4096]{1,0:T(8,128)(2,1)S(1)}, u32[]{:S(2)}, u32[]{:S(2)}) collective-permute-start(bf16[128,4096]{1,0:T(8,128)(2,1)S(1)} %join_columns.41.refs_0_), channel_id=1, source_target_pairs={{0,16},{8,24},{16,0},{24,8},{1,17},{9,25},{17,1},{25,9},{2,18},{10... | collective-permute-start | bytes 3145736 | tf_op jit(solution)/shard_map/ppermute | solution.py:24
  147.2 13.2 %collective-permute-start.19 = (bf16[128,1024]{1,0:T(8,128)(2,1)S(1)}, bf16[128,1024]{1,0:T(8,128)(2,1)S(1)}, u32[]{:S(2)}, u32[]{:S(2)}) collective-permute-start(bf16[128,1024]{1,0:T(8,128)(2,1)S(1)} %join_columns.42.refs_1_), channel_id=1, source_target_pairs={{0,7},{1,6},{2,5},{3,4},{4,3},{5,2},{6,1},{7,0},{8,15},{9,14},{10,... | collective-permute-start | bytes 786440 | tf_op jit(solution)/shard_map/ppermute | solution.py:24
  158.9 6.8 %collective-permute-start.21 = (bf16[128,1024]{1,0:T(8,128)(2,1)S(1)}, bf16[128,1024]{1,0:T(8,128)(2,1)S(1)}, u32[]{:S(2)}, u32[]{:S(2)}) collective-permute-start(bf16[128,1024]{1,0:T(8,128)(2,1)S(1)} %join_columns.43.refs_2_.refs_0_.refs_1_), channel_id=1, source_target_pairs={{0,16},{8,24},{16,0},{24,8},{1,17},{9,25},{17,1},{25,9},{2,18},{10... | collective-permute-start | bytes 786440 | tf_op jit(solution)/shard_map/ppermute | solution.py:24
  160.3 5.4 %collective-permute-start.22 = (bf16[128,8192]{1,0:T(8,128)(2,1)S(1)}, bf16[128,8192]{1,0:T(8,128)(2,1)S(1)}, u32[]{:S(2)}, u32[]{:S(2)}) collective-permute-start(bf16[128,8192]{1,0:T(8,128)(2,1)S(1)} %join_columns.44.refs_0_), channel_id=1, source_target_pairs={{0,8},{8,0},{16,24},{24,16},{1,9},{9,1},{17,25},{25,17},{2,10},{10... | collective-permute-start | bytes 6291464 | tf_op jit(solution)/shard_map/ppermute | solution.py:24
  165.8 8.8 %collective-permute-start.24 = (bf16[128,2048]{1,0:T(8,128)(2,1)S(1)}, bf16[128,2048]{1,0:T(8,128)(2,1)S(1)}, u32[]{:S(2)}, u32[]{:S(2)}) collective-permute-start(bf16[128,2048]{1,0:T(8,128)(2,1)S(1)} %join_columns.46.refs_2_), channel_id=1, source_target_pairs={{0,8},{8,0},{16,24},{24,16},{1,9},{9,1},{17,25},{25,17},{2,10},{10... | collective-permute-start | bytes 1572872 | tf_op jit(solution)/shard_map/ppermute | solution.py:24
  165.8 8.7 %collective-permute-start.23 = (bf16[128,1024]{1,0:T(8,128)(2,1)S(1)}, bf16[128,1024]{1,0:T(8,128)(2,1)S(1)}, u32[]{:S(2)}, u32[]{:S(2)}) collective-permute-start(bf16[128,1024]{1,0:T(8,128)(2,1)S(1)} %join_columns.45.refs_2_.refs_0_.refs_1_), channel_id=1, source_target_pairs={{0,16},{8,24},{16,0},{24,8},{1,17},{9,25},{17,1},{25,9},{2,18},{10... | collective-permute-start | bytes 786440 | tf_op jit(solution)/shard_map/ppermute | solution.py:24
  174.6 5.8 %collective-permute-start.25 = (bf16[128,2048]{1,0:T(8,128)(2,1)S(1)}, bf16[128,2048]{1,0:T(8,128)(2,1)S(1)}, u32[]{:S(2)}, u32[]{:S(2)}) collective-permute-start(bf16[128,2048]{1,0:T(8,128)(2,1)S(1)} %join_columns.47), channel_id=1, source_target_pairs={{0,8},{8,0},{16,24},{24,16},{1,9},{9,1},{17,25},{25,17},{2,10},{10... | collective-permute-start | bytes 1572872 | tf_op jit(solution)/shard_map/ppermute | solution.py:24

commit v10 on v9

--- a/solution.py
+++ b/solution.py
@@ -343,11 +343,16 @@
                     at += pieces[i][1]
                 to += 2 * total
 
-    def finish_relays():
-        for bit, sources, array in relay_before:
-            for at, d in enumerate(sources):
-                cots[d + bit] = cots_at(array, at * model_width)
-        relay_before.clear()
+    def finish_relays(step):
+        arrived = []
+        for entry in list(relay_before):
+            due, bit, sources, array = entry
+            if due <= step:
+                relay_before.remove(entry)
+                arrived.append(array)
+                for at, d in enumerate(sources):
+                    cots[d + bit] = cots_at(array, at * model_width)
+        return arrived
 
     def add_products(i):
         width = pieces[i][1]
@@ -400,8 +405,7 @@
             if d & (d - 1) == 0:
                 cots[d] = cots_at(array, own_width)
         near_before.clear()
-        arrivals = [array for _, _, array in relay_before]
-        finish_relays()
+        arrivals = finish_relays(step)
         if cross_before is not None:
             crossed.append(cross_before)
         earlier = [cross_before[2]] if cross_before is not None else []
@@ -445,14 +449,13 @@
             if sources and flying < 5:
                 relayed.update(d + bit for d in sources)
                 parts = [part for d in sources for part in cot_parts(d)]
-                relay_before.append((bit, sources, send("tok", bit, parts)[1]))
+                relay_before.append((step + (2 if step >= last_pair else 1), bit, sources, send("tok", bit, parts)[1]))
                 flying += 1
             bit //= 2
         if step < len(far_steps):
             tick[:] = [hold(tick[0], arrivals, max(sizes))]
             sizes[:] = [0]
-        if step == last_pair:
-            finish_core()
+        if step == last_pair + 1:
             add_products(0)
             add_products(1)
     finish_core()

time: 203 us -> 187 us (0.921)
  waiting for transfers between devices: 121 us -> 110 us
  Pallas kernels: 34 us -> 31.3 us
  blocking collectives: 11.9 us -> 9.44 us
    ppermute x26, waiting for transfers between devices: 121 us -> 110 us  [exchange(): return lax.ppermute(block, axis, [(i, i ^ distance) for i in range(size)])]
    pallas_call x24, Pallas kernels: 4.19 us -> 1.4 us  [join(): pl.pallas_call(functools.partial(join_kernel, places), out_shape=jax.Shap...]
    all_to_all x1, blocking collectives: 11.9 us -> 9.44 us  [body(): lax.all_to_all(gradients[1][1], ('user', 'tok'), split_axis=0, concat_axi...]
    unnamed x16 -> x28, local copies, waits for them, and re-layouts: 4.33 us -> 3.69 us
  transfers between devices with their start and end apart: 26 -> 26, of which waited for: 10 -> 9; matrix products, arithmetic and copies ran while one was open for 0% -> 0% of each run, Pallas kernels for 12% -> 11%
where the time goes in v10:
time: 187 us
  waiting for transfers between devices  110 us (59%)
  starting transfers between devices  31.8 us (17%)
  Pallas kernels  31.3 us (17%)
  blocking collectives  9.44 us (5%)
  local copies, waits for them, and re-layouts  3.69 us (2%)
    ppermute x26, waiting for transfers between devices, exchange(): return lax.ppermute(block, axis, [(i, i ^ distance) for i in range(size)])  110 us
    ppermute x26, starting transfers between devices, exchange(): return lax.ppermute(block, axis, [(i, i ^ distance) for i in range(size)])  31.8 us
    pallas_call x4, Pallas kernels, product(): pl.pallas_call(functools.partial(product_kernel, left_places, right_place...  24.6 us
    all_to_all x1, blocking collectives, body(): lax.all_to_all(gradients[1][1], ('user', 'tok'), split_axis=0, concat_axi...  9.44 us
    pallas_call x1, Pallas kernels, combine(): pl.pallas_call(functools.partial(combine_kernel, user_count, clip_bound,...  4.82 us
  transfers between devices with their start and end apart: 26, of which 9 were waited for; matrix products, arithmetic and copies ran while one was open for 0% of the time, Pallas kernels for 11%

profile of v10, /device:TPU:0, one launch (start us, length us, event | category | flops | bytes accessed | tf_op | source)
XLA Modules:
  0.0 187.1 jit_solution(6659068169291333111)
XLA Ops:
  0.7 1.0 copy-done.13
  1.7 0.5 collective-permute-start
  2.3 2.6 %collective-permute-start.1 = (bf16[128,512]{1,0:T(8,128)(2,1)S(1)}, bf16[128,512]{1,0:T(8,128)(2,1)S(1)}, u32[]{:S(2)}, u32[]{:S(2)}) collective-permute-start(bf16[128,512]{1,0:T(8,128)(2,1)S(1)} %get-tuple-element.25), channel_id=1, source_target_pairs={{0,16},{8,24},{16,0},{24,8},{1,17},{9,25},{17,1},{25,9},{2,18},{10... | collective-permute-start | bytes 393224 | tf_op jit(solution)/shard_map/ppermute | solution.py:24
  4.8 0.1 collective-permute-start.2
  4.9 2.2 %copy-done.12 = bf16[1,128,16384]{2,1,0:T(8,128)(2,1)S(1)} copy-done((bf16[1,128,16384]{2,1,0:T(8,128)(2,1)S(1)}, bf16[1,128,16384]{2,1,0:T(8,128)(2,1)}, u32[]{:S(2)}) %copy-start.12) | copy-done | bytes 4194328
  7.1 0.4 pack_columns.1
  7.5 2.9 %collective-permute-start.6 = (bf16[128,2048]{1,0:T(8,128)(2,1)S(1)}, bf16[128,2048]{1,0:T(8,128)(2,1)S(1)}, u32[]{:S(2)}, u32[]{:S(2)}) collective-permute-start(bf16[128,2048]{1,0:T(8,128)(2,1)S(1)} %join_columns.24.refs_1_), channel_id=1, source_target_pairs={{0,4},{1,5},{2,6},{3,7},{4,0},{5,1},{6,2},{7,3},{8,12},{9,13},{10,... | collective-permute-start | bytes 1572872 | tf_op jit(solution)/shard_map/ppermute | solution.py:24
  10.4 1.6 collective-permute-start.5
  12.0 0.0 collective-permute-done.1.refs_2_
  12.0 0.0 collective-permute-done.2.refs_3_
  12.1 0.1 join_columns.28.refs_2_
  12.2 1.6 collective-permute-start.4
  13.8 0.1 join_columns.29.refs_0_
  13.9 1.6 collective-permute-start.3
  15.5 2.1 %collective-permute-start.8 = (bf16[128,2048]{1,0:T(8,128)(2,1)S(1)}, bf16[128,2048]{1,0:T(8,128)(2,1)S(1)}, u32[]{:S(2)}, u32[]{:S(2)}) collective-permute-start(bf16[128,2048]{1,0:T(8,128)(2,1)S(1)} %join_columns.27.refs_2_), channel_id=1, source_target_pairs={{0,4},{1,5},{2,6},{3,7},{4,0},{5,1},{6,2},{7,3},{8,12},{9,13},{10,... | collective-permute-start | bytes 1572872 | tf_op jit(solution)/shard_map/ppermute | solution.py:24
  17.6 6.8 %collective-permute-done.5.refs_3_.refs_1_.refs_5_ = bf16[128,2048]{1,0:T(8,128)(2,1)S(1)} collective-permute-done((bf16[128,2048]{1,0:T(8,128)(2,1)S(1)}, bf16[128,2048]{1,0:T(8,128)(2,1)S(1)}, u32[]{:S(2)}, u32[]{:S(2)}) %collective-permute-start.5) | collective-permute-done | bytes 524320 | tf_op jit(solution)/shard_map/ppermute | solution.py:24
  24.4 35.4 %collective-permute-done.3.refs_1_.refs_0_.refs_10_ = bf16[128,4096]{1,0:T(8,128)(2,1)S(1)} collective-permute-done((bf16[128,4096]{1,0:T(8,128)(2,1)S(1)}, bf16[128,4096]{1,0:T(8,128)(2,1)S(1)}, u32[]{:S(2)}, u32[]{:S(2)}) %collective-permute-start.3) | collective-permute-done | bytes 1048608 | tf_op jit(solution)/shard_map/ppermute | solution.py:24
  59.8 0.0 collective-permute-done.4.refs_0_.refs_9_
  59.8 0.1 join_columns.30.refs_1_.refs_2_
  59.9 0.0 copy-start
  59.9 1.6 collective-permute-start.10
  61.6 0.1 collective-permute-start.11
  61.7 1.1 collective-permute-start.14
  62.8 6.4 %collective-permute-start.7 = (bf16[128,2048]{1,0:T(8,128)(2,1)S(1)}, bf16[128,2048]{1,0:T(8,128)(2,1)S(1)}, u32[]{:S(2)}, u32[]{:S(2)}) collective-permute-start(bf16[128,2048]{1,0:T(8,128)(2,1)S(1)} %join_columns.33.refs_1_), channel_id=1, source_target_pairs={{0,5},{1,4},{2,7},{3,6},{4,1},{5,0},{6,3},{7,2},{8,13},{9,12},{10,... | collective-permute-start | bytes 1572872 | tf_op jit(solution)/shard_map/ppermute | solution.py:24
  69.2 0.1 collective-permute-start.9
  69.3 17.2 %collective-permute-done.11.refs_1_ = bf16[128,2048]{1,0:T(8,128)(2,1)S(1)} collective-permute-done((bf16[128,2048]{1,0:T(8,128)(2,1)S(1)}, bf16[128,2048]{1,0:T(8,128)(2,1)S(1)}, u32[]{:S(2)}, u32[]{:S(2)}) %collective-permute-start.11) | collective-permute-done | bytes 524320 | tf_op jit(solution)/shard_map/ppermute | solution.py:24
  86.6 0.0 collective-permute-done.10.refs_3_.refs_6_
  86.6 0.1 join_columns.35.refs_4_.refs_0_.refs_2_
  86.6 0.4 collective-permute-start.13
  87.0 0.2 join_columns.36.refs_1_
  87.2 0.4 copy-done.6
  87.6 0.0 collective-permute-start.15
  87.7 9.2 %collective-permute-done.14.refs_1_.refs_11_ = bf16[128,2048]{1,0:T(8,128)(2,1)S(1)} collective-permute-done((bf16[128,2048]{1,0:T(8,128)(2,1)S(1)}, bf16[128,2048]{1,0:T(8,128)(2,1)S(1)}, u32[]{:S(2)}, u32[]{:S(2)}) %collective-permute-start.14) | collective-permute-done | bytes 524320 | tf_op jit(solution)/shard_map/ppermute | solution.py:24
  96.9 0.3 collective-permute-start.12
  97.2 12.5 %collective-permute-done.13.refs_1_.refs_7_ = bf16[128,4096]{1,0:T(8,128)(2,1)S(1)} collective-permute-done((bf16[128,4096]{1,0:T(8,128)(2,1)S(1)}, bf16[128,4096]{1,0:T(8,128)(2,1)S(1)}, u32[]{:S(2)}, u32[]{:S(2)}) %collective-permute-start.13) | collective-permute-done | bytes 1048608 | tf_op jit(solution)/shard_map/ppermute | solution.py:24
  109.7 0.0 collective-permute-done.15.refs_3_
  109.7 0.1 join_columns.38.refs_2_
  109.8 0.1 collective-permute-start.16
  109.9 5.9 %collective-permute-done.12.refs_1_.refs_7_ = bf16[128,2048]{1,0:T(8,128)(2,1)S(1)} collective-permute-done((bf16[128,2048]{1,0:T(8,128)(2,1)S(1)}, bf16[128,2048]{1,0:T(8,128)(2,1)S(1)}, u32[]{:S(2)}, u32[]{:S(2)}) %collective-permute-start.12) | collective-permute-done | bytes 524320 | tf_op jit(solution)/shard_map/ppermute | solution.py:24
  115.8 0.1 join_columns.39.refs_0_
  115.9 0.7 collective-permute-start.20
  116.6 0.0 collective-permute-done.7.refs_2_.refs_0_
  116.7 0.0 collective-permute-done.9.refs_1_
  116.7 0.1 join_columns.41.refs_0_
  116.8 0.0 copy-start.1
  116.8 1.1 collective-permute-start.19
  117.9 1.3 collective-permute-start.17
  119.2 0.0 copy-done.11
  119.3 6.6 %product_and_squares.4.refs_2_.refs_8_ = f32[4,1024,512]{2,1,0:T(8,128)S(1)} custom-call(bf16[128,2048]{1,0:T(8,128)(2,1)S(1)} %copy-done.3, bf16[128,4096]{1,0:T(8,128)(2,1)S(1)} %copy-done.1, bf16[128,4096]{1,0:T(8,128)(2,1)S(1)} %join_columns.35.refs_4_.refs_0_.refs_2_, bf16[128,12288]{1,0:T(8,128)(2,1)S(1)} %collective-permute-done.15.refs_3_, ...), custom_call_target="tpu_custom_call" | custom-call | flops 2684354560 | bytes 7864320 | tf_op jit(solution)/shard_map/product_and_squares/pallas_call | solution.py:194
  125.8 6.6 %product_and_squares.5.refs_3_.refs_8_ = f32[4,1024,512]{2,1,0:T(8,128)S(1)} custom-call(bf16[128,2048]{1,0:T(8,128)(2,1)S(1)} %copy-done.3, bf16[128,4096]{1,0:T(8,128)(2,1)S(1)} %copy-done.1, bf16[128,4096]{1,0:T(8,128)(2,1)S(1)} %join_columns.35.refs_4_.refs_0_.refs_2_, bf16[128,12288]{1,0:T(8,128)(2,1)S(1)} %collective-permute-done.15.refs_3_, ...), custom_call_target="tpu_custom_call" | custom-call | flops 2684354560 | bytes 7864320 | tf_op jit(solution)/shard_map/product_and_squares/pallas_call | solution.py:194
  132.5 3.5 %collective-permute-start.18 = (bf16[128,1024]{1,0:T(8,128)(2,1)S(1)}, bf16[128,1024]{1,0:T(8,128)(2,1)S(1)}, u32[]{:S(2)}, u32[]{:S(2)}) collective-permute-start(bf16[128,1024]{1,0:T(8,128)(2,1)S(1)} %join_columns.42.refs_1_), channel_id=1, source_target_pairs={{0,7},{1,6},{2,5},{3,4},{4,3},{5,2},{6,1},{7,0},{8,15},{9,14},{10,... | collective-permute-start | bytes 786440 | tf_op jit(solution)/shard_map/ppermute | solution.py:24
  135.9 5.7 %collective-permute-done.19.refs_2_.refs_1_.refs_4_ = bf16[128,4096]{1,0:T(8,128)(2,1)S(1)} collective-permute-done((bf16[128,4096]{1,0:T(8,128)(2,1)S(1)}, bf16[128,4096]{1,0:T(8,128)(2,1)S(1)}, u32[]{:S(2)}, u32[]{:S(2)}) %collective-permute-start.19) | collective-permute-done | bytes 1048608 | tf_op jit(solution)/shard_map/ppermute | solution.py:24
  141.7 1.1 collective-permute-start.21
  142.8 0.1 join_columns.44.refs_0_
  142.9 0.1 collective-permute-start.22
  143.0 9.3 %collective-permute-done.20.refs_1_.refs_6_ = bf16[128,4096]{1,0:T(8,128)(2,1)S(1)} collective-permute-done((bf16[128,4096]{1,0:T(8,128)(2,1)S(1)}, bf16[128,4096]{1,0:T(8,128)(2,1)S(1)}, u32[]{:S(2)}, u32[]{:S(2)}) %collective-permute-start.20) | collective-permute-done | bytes 1048608 | tf_op jit(solution)/shard_map/ppermute | solution.py:24
  152.4 0.1 collective-permute-start.24
  152.5 1.1 collective-permute-start.23
  153.5 7.7 %collective-permute-done.23.refs_1_.refs_5_ = bf16[128,1024]{1,0:T(8,128)(2,1)S(1)} collective-permute-done((bf16[128,1024]{1,0:T(8,128)(2,1)S(1)}, bf16[128,1024]{1,0:T(8,128)(2,1)S(1)}, u32[]{:S(2)}, u32[]{:S(2)}) %collective-permute-start.23) | collective-permute-done | bytes 262176 | tf_op jit(solution)/shard_map/ppermute | solution.py:24
  161.2 0.1 collective-permute-start.25
  161.3 5.7 %product_and_squares.6 = (f32[4,1024,512]{2,1,0:T(8,128)S(1)}, f32[1,8,128]{2,1,0:T(8,128)S(1)}) custom-call(bf16[128,4096]{1,0:T(8,128)(2,1)S(1)} %join_columns.41.refs_0_, bf16[128,1024]{1,0:T(8,128)(2,1)S(1)} %join_columns.43.refs_2_.refs_0_.refs_1_, ...), custom_call_target="tpu_custom_call", output_to_operand_aliasing={{0}: (8, {})} | custom-call | flops 1610612736 | bytes 4718592 | tf_op jit(solution)/shard_map/product_and_squares/pallas_call | solution.py:194
  167.1 5.8 %product_and_squares.7 = (f32[4,1024,512]{2,1,0:T(8,128)S(1)}, f32[32,8,128]{2,1,0:T(8,128)S(1)}) custom-call(bf16[128,4096]{1,0:T(8,128)(2,1)S(1)} %join_columns.41.refs_0_, bf16[128,1024]{1,0:T(8,128)(2,1)S(1)} %join_columns.45.refs_2_.refs_0_.refs_1_, ...), custom_call_target="tpu_custom_call", output_to_operand_aliasing={{0}: (8, {})} | custom-call | flops 1610612736 | bytes 4718592 | tf_op jit(solution)/shard_map/product_and_squares/pallas_call | solution.py:194
  172.8 9.4 %all_to_all.5.sums_ref = f32[32,8,128]{2,1,0:T(8,128)S(1)} all-to-all(f32[32,8,128]{2,1,0:T(8,128)S(1)} %get-tuple-element.34), channel_id=1, replica_groups=mesh['user'=4,'tok'=8] {'user','tok'}, dimensions={0} | all-to-all | bytes 262144 | tf_op jit(solution)/shard_map/all_to_all | solution.py:464
  182.3 4.8 %weighted_sum.1 = f32[2048,512]{1,0:T(8,128)} custom-call(s32[1]{0:T(128)} %bitcast.user_ref, f32[32,8,128]{2,1,0:T(8,128)S(1)} %all_to_all.5.sums_ref, f32[4,1024,512]{2,1,0:T(8,128)S(1)} %get-tuple-element.35.refs_0_, f32[4,1024,512]{2,1,0:T(8,128)S(1)} %get-tuple-element.36.refs_1_), custom_call_target="tpu_custom_call" | custom-call | tf_op jit(solution)/shard_map/weighted_sum/pallas_call | solution.py:251
  (54 shorter events, 0.6 us)
Async XLA Ops:
  0.7 1.0 copy-start.13
  1.7 10.3 %collective-permute-start = (bf16[128,512]{1,0:T(8,128)(2,1)S(1)}, bf16[128,512]{1,0:T(8,128)(2,1)S(1)}, u32[]{:S(2)}, u32[]{:S(2)}) collective-permute-start(bf16[128,512]{1,0:T(8,128)(2,1)S(1)} %get-tuple-element.24), channel_id=1, source_target_pairs={{0,8},{8,0},{16,24},{24,16},{1,9},{9,1},{17,25},{25,17},{2,10},{10... | collective-permute-start | bytes 393224 | tf_op jit(solution)/shard_map/ppermute | solution.py:24
  2.3 9.7 %collective-permute-start.1 = (bf16[128,512]{1,0:T(8,128)(2,1)S(1)}, bf16[128,512]{1,0:T(8,128)(2,1)S(1)}, u32[]{:S(2)}, u32[]{:S(2)}) collective-permute-start(bf16[128,512]{1,0:T(8,128)(2,1)S(1)} %get-tuple-element.25), channel_id=1, source_target_pairs={{0,16},{8,24},{16,0},{24,8},{1,17},{9,25},{17,1},{25,9},{2,18},{10... | collective-permute-start | bytes 393224 | tf_op jit(solution)/shard_map/ppermute | solution.py:24
  4.8 7.2 %collective-permute-start.2 = (bf16[128,512]{1,0:T(8,128)(2,1)S(1)}, bf16[128,512]{1,0:T(8,128)(2,1)S(1)}, u32[]{:S(2)}, u32[]{:S(2)}) collective-permute-start(bf16[128,512]{1,0:T(8,128)(2,1)S(1)} %get-tuple-element.26), channel_id=1, source_target_pairs={{0,24},{8,16},{16,8},{24,0},{1,25},{9,17},{17,9},{25,1},{2,26},{10... | collective-permute-start | bytes 393224 | tf_op jit(solution)/shard_map/ppermute | solution.py:24
  4.9 2.2 %copy-start.12 = (bf16[1,128,16384]{2,1,0:T(8,128)(2,1)S(1)}, bf16[1,128,16384]{2,1,0:T(8,128)(2,1)}, u32[]{:S(2)}) copy-start(bf16[1,128,16384]{2,1,0:T(8,128)(2,1)} %hidden_ref.1) | copy-start | bytes 12582916
  7.5 55.2 %collective-permute-start.6 = (bf16[128,2048]{1,0:T(8,128)(2,1)S(1)}, bf16[128,2048]{1,0:T(8,128)(2,1)S(1)}, u32[]{:S(2)}, u32[]{:S(2)}) collective-permute-start(bf16[128,2048]{1,0:T(8,128)(2,1)S(1)} %join_columns.24.refs_1_), channel_id=1, source_target_pairs={{0,4},{1,5},{2,6},{3,7},{4,0},{5,1},{6,2},{7,3},{8,12},{9,13},{10,... | collective-permute-start | bytes 1572872 | tf_op jit(solution)/shard_map/ppermute | solution.py:24
  10.4 76.6 %copy-start.2 = (bf16[128,2048]{1,0:T(8,128)(2,1)}, bf16[128,2048]{1,0:T(8,128)(2,1)S(1)}, u32[]{:S(2)}) copy-start(bf16[128,2048]{1,0:T(8,128)(2,1)S(1)} %join_columns.25.refs_4_.refs_1_.refs_0_) | copy-start | bytes 1572868
  10.4 14.0 %collective-permute-start.5 = (bf16[128,2048]{1,0:T(8,128)(2,1)S(1)}, bf16[128,2048]{1,0:T(8,128)(2,1)S(1)}, u32[]{:S(2)}, u32[]{:S(2)}) collective-permute-start(bf16[128,2048]{1,0:T(8,128)(2,1)S(1)} %join_columns.25.refs_4_.refs_1_.refs_0_), channel_id=1, source_target_pairs={{0,16},{8,24},{16,0},{24,8},{1,17},{9,25},{17,1},{25,9},{2,18},{10... | collective-permute-start | bytes 1572872 | tf_op jit(solution)/shard_map/ppermute | solution.py:24
  12.1 3.5 %copy-start.4 = (bf16[128,2048]{1,0:T(8,128)(2,1)}, bf16[128,2048]{1,0:T(8,128)(2,1)S(1)}, u32[]{:S(2)}) copy-start(bf16[128,2048]{1,0:T(8,128)(2,1)S(1)} %join_columns.26.refs_0_.refs_1_.refs_8_) | copy-start | bytes 1572868
  12.2 47.6 %collective-permute-start.4 = (bf16[128,4096]{1,0:T(8,128)(2,1)S(1)}, bf16[128,4096]{1,0:T(8,128)(2,1)S(1)}, u32[]{:S(2)}, u32[]{:S(2)}) collective-permute-start(bf16[128,4096]{1,0:T(8,128)(2,1)S(1)} %join_columns.28.refs_2_), channel_id=1, source_target_pairs={{0,1},{1,0},{2,3},{3,2},{4,5},{5,4},{6,7},{7,6},{8,9},{9,8},{10,11... | collective-permute-start | bytes 3145736 | tf_op jit(solution)/shard_map/ppermute | solution.py:24
  13.9 45.9 %collective-permute-start.3 = (bf16[128,4096]{1,0:T(8,128)(2,1)S(1)}, bf16[128,4096]{1,0:T(8,128)(2,1)S(1)}, u32[]{:S(2)}, u32[]{:S(2)}) collective-permute-start(bf16[128,4096]{1,0:T(8,128)(2,1)S(1)} %join_columns.29.refs_0_), channel_id=1, source_target_pairs={{0,2},{1,3},{2,0},{3,1},{4,6},{5,7},{6,4},{7,5},{8,10},{9,11},{10,... | collective-permute-start | bytes 3145736 | tf_op jit(solution)/shard_map/ppermute | solution.py:24
  15.5 53.7 %collective-permute-start.8 = (bf16[128,2048]{1,0:T(8,128)(2,1)S(1)}, bf16[128,2048]{1,0:T(8,128)(2,1)S(1)}, u32[]{:S(2)}, u32[]{:S(2)}) collective-permute-start(bf16[128,2048]{1,0:T(8,128)(2,1)S(1)} %join_columns.27.refs_2_), channel_id=1, source_target_pairs={{0,4},{1,5},{2,6},{3,7},{4,0},{5,1},{6,2},{7,3},{8,12},{9,13},{10,... | collective-permute-start | bytes 1572872 | tf_op jit(solution)/shard_map/ppermute | solution.py:24
  59.8 2.9 %copy-start.8 = (bf16[128,4096]{1,0:T(8,128)(2,1)}, bf16[128,4096]{1,0:T(8,128)(2,1)S(1)}, u32[]{:S(2)}) copy-start(bf16[128,4096]{1,0:T(8,128)(2,1)S(1)} %collective-permute-done.3.refs_1_.refs_0_.refs_10_) | copy-start | bytes 3145732
  59.8 2.9 %copy-start.10 = (bf16[128,4096]{1,0:T(8,128)(2,1)}, bf16[128,4096]{1,0:T(8,128)(2,1)S(1)}, u32[]{:S(2)}) copy-start(bf16[128,4096]{1,0:T(8,128)(2,1)S(1)} %collective-permute-done.4.refs_0_.refs_9_) | copy-start | bytes 3145732
  59.9 27.1 %copy-start = (bf16[128,4096]{1,0:T(8,128)(2,1)}, bf16[128,4096]{1,0:T(8,128)(2,1)S(1)}, u32[]{:S(2)}) copy-start(bf16[128,4096]{1,0:T(8,128)(2,1)S(1)} %join_columns.30.refs_1_.refs_2_) | copy-start | bytes 3145732
  59.9 26.6 %collective-permute-start.10 = (bf16[128,4096]{1,0:T(8,128)(2,1)S(1)}, bf16[128,4096]{1,0:T(8,128)(2,1)S(1)}, u32[]{:S(2)}, u32[]{:S(2)}) collective-permute-start(bf16[128,4096]{1,0:T(8,128)(2,1)S(1)} %join_columns.30.refs_1_.refs_2_), channel_id=1, source_target_pairs={{0,16},{8,24},{16,0},{24,8},{1,17},{9,25},{17,1},{25,9},{2,18},{10... | collective-permute-start | bytes 3145736 | tf_op jit(solution)/shard_map/ppermute | solution.py:24
  61.6 25.0 %collective-permute-start.11 = (bf16[128,2048]{1,0:T(8,128)(2,1)S(1)}, bf16[128,2048]{1,0:T(8,128)(2,1)S(1)}, u32[]{:S(2)}, u32[]{:S(2)}) collective-permute-start(bf16[128,2048]{1,0:T(8,128)(2,1)S(1)} %join_columns.31.refs_1_), channel_id=1, source_target_pairs={{0,3},{1,2},{2,1},{3,0},{4,7},{5,6},{6,5},{7,4},{8,11},{9,10},{10,... | collective-permute-start | bytes 1572872 | tf_op jit(solution)/shard_map/ppermute | solution.py:24
  61.7 35.2 %collective-permute-start.14 = (bf16[128,2048]{1,0:T(8,128)(2,1)S(1)}, bf16[128,2048]{1,0:T(8,128)(2,1)S(1)}, u32[]{:S(2)}, u32[]{:S(2)}) collective-permute-start(bf16[128,2048]{1,0:T(8,128)(2,1)S(1)} %join_columns.32.refs_0_), channel_id=1, source_target_pairs={{0,1},{1,0},{2,3},{3,2},{4,5},{5,4},{6,7},{7,6},{8,9},{9,8},{10,11... | collective-permute-start | bytes 1572872 | tf_op jit(solution)/shard_map/ppermute | solution.py:24
  62.8 53.8 %collective-permute-start.7 = (bf16[128,2048]{1,0:T(8,128)(2,1)S(1)}, bf16[128,2048]{1,0:T(8,128)(2,1)S(1)}, u32[]{:S(2)}, u32[]{:S(2)}) collective-permute-start(bf16[128,2048]{1,0:T(8,128)(2,1)S(1)} %join_columns.33.refs_1_), channel_id=1, source_target_pairs={{0,5},{1,4},{2,7},{3,6},{4,1},{5,0},{6,3},{7,2},{8,13},{9,12},{10,... | collective-permute-start | bytes 1572872 | tf_op jit(solution)/shard_map/ppermute | solution.py:24
  69.2 47.4 %collective-permute-start.9 = (bf16[128,2048]{1,0:T(8,128)(2,1)S(1)}, bf16[128,2048]{1,0:T(8,128)(2,1)S(1)}, u32[]{:S(2)}, u32[]{:S(2)}) collective-permute-start(bf16[128,2048]{1,0:T(8,128)(2,1)S(1)} %join_columns.34.refs_2_), channel_id=1, source_target_pairs={{0,6},{1,7},{2,4},{3,5},{4,2},{5,3},{6,0},{7,1},{8,14},{9,15},{10,... | collective-permute-start | bytes 1572872 | tf_op jit(solution)/shard_map/ppermute | solution.py:24
  86.6 1.1 copy-start.6
  86.6 23.1 %collective-permute-start.13 = (bf16[128,4096]{1,0:T(8,128)(2,1)S(1)}, bf16[128,4096]{1,0:T(8,128)(2,1)S(1)}, u32[]{:S(2)}, u32[]{:S(2)}) collective-permute-start(bf16[128,4096]{1,0:T(8,128)(2,1)S(1)} %join_columns.35.refs_4_.refs_0_.refs_2_), channel_id=1, source_target_pairs={{0,16},{8,24},{16,0},{24,8},{1,17},{9,25},{17,1},{25,9},{2,18},{10... | collective-permute-start | bytes 3145736 | tf_op jit(solution)/shard_map/ppermute | solution.py:24
  87.6 22.1 %collective-permute-start.15 = (bf16[128,12288]{1,0:T(8,128)(2,1)S(1)}, bf16[128,12288]{1,0:T(8,128)(2,1)S(1)}, u32[]{:S(2)}, u32[]{:S(2)}) collective-permute-start(bf16[128,12288]{1,0:T(8,128)(2,1)S(1)} %join_columns.36.refs_1_), channel_id=1, source_target_pairs={{0,8},{8,0},{16,24},{24,16},{1,9},{9,1},{17,25},{25,17},{2,10},{10... | collective-permute-start | bytes 9437192 | tf_op jit(solution)/shard_map/ppermute | solution.py:24
  96.9 18.9 %collective-permute-start.12 = (bf16[128,2048]{1,0:T(8,128)(2,1)S(1)}, bf16[128,2048]{1,0:T(8,128)(2,1)S(1)}, u32[]{:S(2)}, u32[]{:S(2)}) collective-permute-start(bf16[128,2048]{1,0:T(8,128)(2,1)S(1)} %join_columns.37.refs_0_), channel_id=1, source_target_pairs={{0,2},{1,3},{2,0},{3,1},{4,6},{5,7},{6,4},{7,5},{8,10},{9,11},{10,... | collective-permute-start | bytes 1572872 | tf_op jit(solution)/shard_map/ppermute | solution.py:24
  109.8 9.4 %collective-permute-start.16 = (bf16[128,8192]{1,0:T(8,128)(2,1)S(1)}, bf16[128,8192]{1,0:T(8,128)(2,1)S(1)}, u32[]{:S(2)}, u32[]{:S(2)}) collective-permute-start(bf16[128,8192]{1,0:T(8,128)(2,1)S(1)} %join_columns.38.refs_2_), channel_id=1, source_target_pairs={{0,8},{8,0},{16,24},{24,16},{1,9},{9,1},{17,25},{25,17},{2,10},{10... | collective-permute-start | bytes 6291464 | tf_op jit(solution)/shard_map/ppermute | solution.py:24
  115.9 36.4 %collective-permute-start.20 = (bf16[128,4096]{1,0:T(8,128)(2,1)S(1)}, bf16[128,4096]{1,0:T(8,128)(2,1)S(1)}, u32[]{:S(2)}, u32[]{:S(2)}) collective-permute-start(bf16[128,4096]{1,0:T(8,128)(2,1)S(1)} %join_columns.39.refs_0_), channel_id=1, source_target_pairs={{0,1},{1,0},{2,3},{3,2},{4,5},{5,4},{6,7},{7,6},{8,9},{9,8},{10,11... | collective-permute-start | bytes 3145736 | tf_op jit(solution)/shard_map/ppermute | solution.py:24
  116.8 2.5 %copy-start.1 = (bf16[128,4096]{1,0:T(8,128)(2,1)S(1)}, bf16[128,4096]{1,0:T(8,128)(2,1)}, u32[]{:S(2)}) copy-start(bf16[128,4096]{1,0:T(8,128)(2,1)} %copy-done) | copy-start | bytes 3145732
  116.8 2.4 %copy-start.3 = (bf16[128,2048]{1,0:T(8,128)(2,1)S(1)}, bf16[128,2048]{1,0:T(8,128)(2,1)}, u32[]{:S(2)}) copy-start(bf16[128,2048]{1,0:T(8,128)(2,1)} %copy-done.2) | copy-start | bytes 1572868
  116.8 2.4 %copy-start.5 = (bf16[128,2048]{1,0:T(8,128)(2,1)S(1)}, bf16[128,2048]{1,0:T(8,128)(2,1)}, u32[]{:S(2)}) copy-start(bf16[128,2048]{1,0:T(8,128)(2,1)} %copy-done.4) | copy-start | bytes 1572868
  116.8 2.4 %copy-start.7 = (bf16[128,4096]{1,0:T(8,128)(2,1)S(1)}, bf16[128,4096]{1,0:T(8,128)(2,1)}, u32[]{:S(2)}) copy-start(bf16[128,4096]{1,0:T(8,128)(2,1)} %copy-done.6) | copy-start | bytes 3145732
  116.8 2.4 %copy-start.9 = (bf16[128,4096]{1,0:T(8,128)(2,1)S(1)}, bf16[128,4096]{1,0:T(8,128)(2,1)}, u32[]{:S(2)}) copy-start(bf16[128,4096]{1,0:T(8,128)(2,1)} %copy-done.8) | copy-start | bytes 3145732
  116.8 2.5 %copy-start.11 = (bf16[128,4096]{1,0:T(8,128)(2,1)S(1)}, bf16[128,4096]{1,0:T(8,128)(2,1)}, u32[]{:S(2)}) copy-start(bf16[128,4096]{1,0:T(8,128)(2,1)} %copy-done.10) | copy-start | bytes 3145732
  116.8 24.9 %collective-permute-start.19 = (bf16[128,4096]{1,0:T(8,128)(2,1)S(1)}, bf16[128,4096]{1,0:T(8,128)(2,1)S(1)}, u32[]{:S(2)}, u32[]{:S(2)}) collective-permute-start(bf16[128,4096]{1,0:T(8,128)(2,1)S(1)} %join_columns.41.refs_0_), channel_id=1, source_target_pairs={{0,16},{8,24},{16,0},{24,8},{1,17},{9,25},{17,1},{25,9},{2,18},{10... | collective-permute-start | bytes 3145736 | tf_op jit(solution)/shard_map/ppermute | solution.py:24
  117.9 14.5 %collective-permute-start.17 = (bf16[128,1024]{1,0:T(8,128)(2,1)S(1)}, bf16[128,1024]{1,0:T(8,128)(2,1)S(1)}, u32[]{:S(2)}, u32[]{:S(2)}) collective-permute-start(bf16[128,1024]{1,0:T(8,128)(2,1)S(1)} %join_columns.40.refs_2_), channel_id=1, source_target_pairs={{0,7},{1,6},{2,5},{3,4},{4,3},{5,2},{6,1},{7,0},{8,15},{9,14},{10,... | collective-permute-start | bytes 786440 | tf_op jit(solution)/shard_map/ppermute | solution.py:24
  132.5 19.9 %collective-permute-start.18 = (bf16[128,1024]{1,0:T(8,128)(2,1)S(1)}, bf16[128,1024]{1,0:T(8,128)(2,1)S(1)}, u32[]{:S(2)}, u32[]{:S(2)}) collective-permute-start(bf16[128,1024]{1,0:T(8,128)(2,1)S(1)} %join_columns.42.refs_1_), channel_id=1, source_target_pairs={{0,7},{1,6},{2,5},{3,4},{4,3},{5,2},{6,1},{7,0},{8,15},{9,14},{10,... | collective-permute-start | bytes 786440 | tf_op jit(solution)/shard_map/ppermute | solution.py:24
  141.7 10.6 %collective-permute-start.21 = (bf16[128,1024]{1,0:T(8,128)(2,1)S(1)}, bf16[128,1024]{1,0:T(8,128)(2,1)S(1)}, u32[]{:S(2)}, u32[]{:S(2)}) collective-permute-start(bf16[128,1024]{1,0:T(8,128)(2,1)S(1)} %join_columns.43.refs_2_.refs_0_.refs_1_), channel_id=1, source_target_pairs={{0,16},{8,24},{16,0},{24,8},{1,17},{9,25},{17,1},{25,9},{2,18},{10... | collective-permute-start | bytes 786440 | tf_op jit(solution)/shard_map/ppermute | solution.py:24
  142.9 9.5 %collective-permute-start.22 = (bf16[128,8192]{1,0:T(8,128)(2,1)S(1)}, bf16[128,8192]{1,0:T(8,128)(2,1)S(1)}, u32[]{:S(2)}, u32[]{:S(2)}) collective-permute-start(bf16[128,8192]{1,0:T(8,128)(2,1)S(1)} %join_columns.44.refs_0_), channel_id=1, source_target_pairs={{0,8},{8,0},{16,24},{24,16},{1,9},{9,1},{17,25},{25,17},{2,10},{10... | collective-permute-start | bytes 6291464 | tf_op jit(solution)/shard_map/ppermute | solution.py:24
  152.4 8.8 %collective-permute-start.24 = (bf16[128,2048]{1,0:T(8,128)(2,1)S(1)}, bf16[128,2048]{1,0:T(8,128)(2,1)S(1)}, u32[]{:S(2)}, u32[]{:S(2)}) collective-permute-start(bf16[128,2048]{1,0:T(8,128)(2,1)S(1)} %join_columns.46.refs_2_), channel_id=1, source_target_pairs={{0,8},{8,0},{16,24},{24,16},{1,9},{9,1},{17,25},{25,17},{2,10},{10... | collective-permute-start | bytes 1572872 | tf_op jit(solution)/shard_map/ppermute | solution.py:24
  152.5 8.7 %collective-permute-start.23 = (bf16[128,1024]{1,0:T(8,128)(2,1)S(1)}, bf16[128,1024]{1,0:T(8,128)(2,1)S(1)}, u32[]{:S(2)}, u32[]{:S(2)}) collective-permute-start(bf16[128,1024]{1,0:T(8,128)(2,1)S(1)} %join_columns.45.refs_2_.refs_0_.refs_1_), channel_id=1, source_target_pairs={{0,16},{8,24},{16,0},{24,8},{1,17},{9,25},{17,1},{25,9},{2,18},{10... | collective-permute-start | bytes 786440 | tf_op jit(solution)/shard_map/ppermute | solution.py:24
  161.2 5.8 %collective-permute-start.25 = (bf16[128,2048]{1,0:T(8,128)(2,1)S(1)}, bf16[128,2048]{1,0:T(8,128)(2,1)S(1)}, u32[]{:S(2)}, u32[]{:S(2)}) collective-permute-start(bf16[128,2048]{1,0:T(8,128)(2,1)S(1)} %join_columns.47), channel_id=1, source_target_pairs={{0,8},{8,0},{16,24},{24,16},{1,9},{9,1},{17,25},{25,17},{2,10},{10... | collective-permute-start | bytes 1572872 | tf_op jit(solution)/shard_map/ppermute | solution.py:24

commit v11 on v10

--- a/solution.py
+++ b/solution.py
@@ -10,7 +10,7 @@
 
 epsilon = 1e-06
 lanes = 128
-first_part = 0.5
+first_part = 0.625
 dear = 24 * 10**10
 dear_per_byte = 2 * 10**5
 ANY = pl.BlockSpec(memory_space=pl.ANY)
@@ -301,7 +301,7 @@
 
     masked = mask(valid, user, cotangent, user_count)
     by_slot = [masked[0]] + [exchange(masked[s], "user", s) for s in range(1, user_count)]
-    outgoing = pack(tok, hidden, list(range(tok_count)), own_width, [masked[0]])
+    outgoing = pack(tok, hidden, list(range(tok_count)), own_width, [])
     ready += [(0, i, outgoing[0], start) for i, (start, _) in enumerate(pieces)]
 
     far = list(range(half + 1, tok_count))
@@ -406,6 +406,15 @@
                 cots[d] = cots_at(array, own_width)
         near_before.clear()
         arrivals = finish_relays(step)
+        bit = half // 2
+        while bit:
+            sources = [d for d in sorted(cots) if bit in bits_below(d) and d + bit not in relayed]
+            if sources and flying < 3:
+                relayed.update(d + bit for d in sources)
+                parts = [part for d in sources for part in cot_parts(d)]
+                relay_before.append((step + (2 if step >= last_pair else 1), bit, sources, send("tok", bit, parts)[1]))
+                flying += 1
+            bit //= 2
         if cross_before is not None:
             crossed.append(cross_before)
         earlier = [cross_before[2]] if cross_before is not None else []
@@ -432,10 +441,7 @@
                 flying += 1
         before = [core_before[1]] if core_before else []
         finish_core()
-        relays_wait = any(
-            d and d + bit not in relayed for d in cots for bit in bits_below(d)
-        )
-        if crossed and (flying < 5 - relays_wait or step > last_pair):
+        if crossed and (flying < 5 or step >= last_pair):
             parts = []
             for blocks, own, other in crossed:
                 total = sum(pieces[i][1] for _, i, _, _ in blocks)
@@ -443,21 +449,16 @@
             core_before = (list(crossed), send("user", core, parts, before)[1])
             crossed.clear()
             flying += 1
-        bit = half // 2
-        while bit:
-            sources = [d for d in sorted(cots) if bit in bits_below(d) and d + bit not in relayed]
-            if sources and flying < 5:
-                relayed.update(d + bit for d in sources)
-                parts = [part for d in sources for part in cot_parts(d)]
-                relay_before.append((step + (2 if step >= last_pair else 1), bit, sources, send("tok", bit, parts)[1]))
-                flying += 1
-            bit //= 2
         if step < len(far_steps):
             tick[:] = [hold(tick[0], arrivals, max(sizes))]
             sizes[:] = [0]
         if step == last_pair + 1:
             add_products(0)
+        elif step == last_pair + 2:
             add_products(1)
+        elif step == len(far_steps):
+            finish_core()
+            add_products(0)
     finish_core()
     add_products(0)
     add_products(1)

time: 187 us -> 187 us (level)
  waiting for transfers between devices: 110 us -> 99.8 us
  blocking collectives: 9.44 us -> 13.8 us
  starting transfers between devices: 31.8 us -> 35.4 us
    ppermute x26, waiting for transfers between devices: 110 us -> 99.8 us  [exchange(): return lax.ppermute(block, axis, [(i, i ^ distance) for i in range(size)])]
    all_to_all x1, blocking collectives: 9.44 us -> 13.8 us  [body(): lax.all_to_all(gradients[1][1], ('user', 'tok'), split_axis=0, concat_axi...]
    ppermute x26, starting transfers between devices: 31.8 us -> 35.4 us  [exchange(): return lax.ppermute(block, axis, [(i, i ^ distance) for i in range(size)])]
    unnamed x28 -> x32, local copies, waits for them, and re-layouts: 3.69 us -> 5.15 us
  transfers between devices with their start and end apart: 26 -> 26, of which waited for: 9 -> 8; matrix products, arithmetic and copies ran while one was open for 0% -> 0% of each run, Pallas kernels for 11% -> 12%
where the time goes in v11:
time: 187 us; the launch traced here: 186 us
  waiting for transfers between devices  99.8 us (53%)
  starting transfers between devices  35.4 us (19%)
  Pallas kernels  31.1 us (17%)
  blocking collectives  13.8 us (7%)
  local copies, waits for them, and re-layouts  5.15 us (3%)
    ppermute x26, waiting for transfers between devices, exchange(): return lax.ppermute(block, axis, [(i, i ^ distance) for i in range(size)])  99.8 us
    ppermute x26, starting transfers between devices, exchange(): return lax.ppermute(block, axis, [(i, i ^ distance) for i in range(size)])  35.4 us
    pallas_call x4, Pallas kernels, product(): pl.pallas_call(functools.partial(product_kernel, left_places, right_place...  24.5 us
    all_to_all x1, blocking collectives, body(): lax.all_to_all(gradients[1][1], ('user', 'tok'), split_axis=0, concat_axi...  13.8 us
    unnamed x32, local copies, waits for them, and re-layouts  5.15 us
    pallas_call x1, Pallas kernels, combine(): pl.pallas_call(functools.partial(combine_kernel, user_count, clip_bound,...  4.81 us
  transfers between devices with their start and end apart: 26, of which 8 were waited for; matrix products, arithmetic and copies ran while one was open for 0% of the time, Pallas kernels for 12%

profile of v11, /device:TPU:0, one launch (start us, length us, event | category | flops | bytes accessed | tf_op | source)
XLA Modules:
  0.0 186.4 jit_solution(1863133545720545948)
XLA Ops:
  0.7 1.0 copy-done.15
  1.7 0.5 collective-permute-start
  2.3 2.6 %collective-permute-start.1 = (bf16[128,512]{1,0:T(8,128)(2,1)S(1)}, bf16[128,512]{1,0:T(8,128)(2,1)S(1)}, u32[]{:S(2)}, u32[]{:S(2)}) collective-permute-start(bf16[128,512]{1,0:T(8,128)(2,1)S(1)} %get-tuple-element.26), channel_id=1, source_target_pairs={{0,16},{8,24},{16,0},{24,8},{1,17},{9,25},{17,1},{25,9},{2,18},{10... | collective-permute-start | bytes 393224 | tf_op jit(solution)/shard_map/ppermute | solution.py:24
  4.8 0.1 collective-permute-start.2
  4.9 2.2 %copy-done.14 = bf16[1,128,16384]{2,1,0:T(8,128)(2,1)S(1)} copy-done((bf16[1,128,16384]{2,1,0:T(8,128)(2,1)S(1)}, bf16[1,128,16384]{2,1,0:T(8,128)(2,1)}, u32[]{:S(2)}) %copy-start.14) | copy-done | bytes 4194328
  7.1 0.4 pack_columns.1
  7.5 2.9 %collective-permute-start.6 = (bf16[128,2048]{1,0:T(8,128)(2,1)S(1)}, bf16[128,2048]{1,0:T(8,128)(2,1)S(1)}, u32[]{:S(2)}, u32[]{:S(2)}) collective-permute-start(bf16[128,2048]{1,0:T(8,128)(2,1)S(1)} %join_columns.24.refs_1_), channel_id=1, source_target_pairs={{0,4},{1,5},{2,6},{3,7},{4,0},{5,1},{6,2},{7,3},{8,12},{9,13},{10,... | collective-permute-start | bytes 1572872 | tf_op jit(solution)/shard_map/ppermute | solution.py:24
  10.4 1.6 collective-permute-start.5
  12.0 0.0 collective-permute-done.1.refs_2_
  12.0 0.0 collective-permute-done.2.refs_3_
  12.1 0.1 join_columns.28.refs_2_
  12.2 1.6 collective-permute-start.3
  13.8 0.1 join_columns.29.refs_0_
  13.9 1.6 collective-permute-start.4
  15.5 2.1 %collective-permute-start.8 = (bf16[128,2048]{1,0:T(8,128)(2,1)S(1)}, bf16[128,2048]{1,0:T(8,128)(2,1)S(1)}, u32[]{:S(2)}, u32[]{:S(2)}) collective-permute-start(bf16[128,2048]{1,0:T(8,128)(2,1)S(1)} %join_columns.27.refs_2_), channel_id=1, source_target_pairs={{0,4},{1,5},{2,6},{3,7},{4,0},{5,1},{6,2},{7,3},{8,12},{9,13},{10,... | collective-permute-start | bytes 1572872 | tf_op jit(solution)/shard_map/ppermute | solution.py:24
  17.6 42.2 %collective-permute-done.4.refs_0_.refs_1_.refs_10_ = bf16[128,4096]{1,0:T(8,128)(2,1)S(1)} collective-permute-done((bf16[128,4096]{1,0:T(8,128)(2,1)S(1)}, bf16[128,4096]{1,0:T(8,128)(2,1)S(1)}, u32[]{:S(2)}, u32[]{:S(2)}) %collective-permute-start.4) | collective-permute-done | bytes 1048608 | tf_op jit(solution)/shard_map/ppermute | solution.py:24
  59.9 0.6 collective-permute-start.14
  60.5 0.1 join_columns.31.refs_1_.refs_2_
  60.6 0.0 copy-start
  60.6 1.6 collective-permute-start.11
  62.2 0.6 collective-permute-start.10
  62.8 0.0 collective-permute-done.6.refs_2_.refs_0_
  62.8 6.4 %collective-permute-start.7 = (bf16[128,2048]{1,0:T(8,128)(2,1)S(1)}, bf16[128,2048]{1,0:T(8,128)(2,1)S(1)}, u32[]{:S(2)}, u32[]{:S(2)}) collective-permute-start(bf16[128,2048]{1,0:T(8,128)(2,1)S(1)} %join_columns.33.refs_1_), channel_id=1, source_target_pairs={{0,5},{1,4},{2,7},{3,6},{4,1},{5,0},{6,3},{7,2},{8,13},{9,12},{10,... | collective-permute-start | bytes 1572872 | tf_op jit(solution)/shard_map/ppermute | solution.py:24
  69.2 0.0 collective-permute-done.8.refs_2_.refs_0_.refs_12_
  69.2 0.1 collective-permute-start.9
  69.4 17.5 %collective-permute-done.10.refs_1_ = bf16[128,2048]{1,0:T(8,128)(2,1)S(1)} collective-permute-done((bf16[128,2048]{1,0:T(8,128)(2,1)S(1)}, bf16[128,2048]{1,0:T(8,128)(2,1)S(1)}, u32[]{:S(2)}, u32[]{:S(2)}) %collective-permute-start.10) | collective-permute-done | bytes 524320 | tf_op jit(solution)/shard_map/ppermute | solution.py:24
  86.9 0.1 join_columns.36.refs_4_.refs_0_.refs_2_
  87.0 0.4 collective-permute-start.12
  87.4 0.2 join_columns.37.refs_0_
  87.6 0.4 copy-done.6
  88.0 6.8 %collective-permute-done.14.refs_1_.refs_11_ = bf16[128,2048]{1,0:T(8,128)(2,1)S(1)} collective-permute-done((bf16[128,2048]{1,0:T(8,128)(2,1)S(1)}, bf16[128,2048]{1,0:T(8,128)(2,1)S(1)}, u32[]{:S(2)}, u32[]{:S(2)}) %collective-permute-start.14) | collective-permute-done | bytes 524320 | tf_op jit(solution)/shard_map/ppermute | solution.py:24
  94.8 15.3 %collective-permute-done.13.refs_1_.refs_7_ = bf16[128,2048]{1,0:T(8,128)(2,1)S(1)} collective-permute-done((bf16[128,2048]{1,0:T(8,128)(2,1)S(1)}, bf16[128,2048]{1,0:T(8,128)(2,1)S(1)}, u32[]{:S(2)}, u32[]{:S(2)}) %collective-permute-start.13) | collective-permute-done | bytes 524320 | tf_op jit(solution)/shard_map/ppermute | solution.py:24
  110.2 0.1 join_columns.38.refs_2_
  110.3 1.4 collective-permute-start.20
  111.6 0.1 join_columns.39.refs_0_
  111.8 0.1 collective-permute-start.16
  111.9 5.9 %collective-permute-start.17 = (bf16[128,1280]{1,0:T(8,128)(2,1)S(1)}, bf16[128,1280]{1,0:T(8,128)(2,1)S(1)}, u32[]{:S(2)}, u32[]{:S(2)}) collective-permute-start(bf16[128,1280]{1,0:T(8,128)(2,1)S(1)} %join_columns.40.refs_2_), channel_id=1, source_target_pairs={{0,7},{1,6},{2,5},{3,4},{4,3},{5,2},{6,1},{7,0},{8,15},{9,14},{10,... | collective-permute-start | bytes 983048 | tf_op jit(solution)/shard_map/ppermute | solution.py:24
  117.8 0.1 join_columns.41.refs_0_
  117.9 0.0 copy-start.1
  117.9 1.1 collective-permute-start.19
  119.0 0.1 copy-done.1
  119.1 0.1 copy-done.3
  119.2 0.2 copy-done.5
  119.4 0.3 copy-done.7
  119.7 0.3 copy-done.9
  120.0 0.3 copy-done.11
  120.4 0.1 copy-done.13
  120.5 8.2 %product_and_squares.4.refs_2_.refs_8_ = f32[4,1280,512]{2,1,0:T(8,128)S(1)} custom-call(bf16[128,2048]{1,0:T(8,128)(2,1)S(1)} %copy-done.3, bf16[128,4096]{1,0:T(8,128)(2,1)S(1)} %copy-done.1, bf16[128,4096]{1,0:T(8,128)(2,1)S(1)} %join_columns.36.refs_4_.refs_0_.refs_2_, bf16[128,12288]{1,0:T(8,128)(2,1)S(1)} %collective-permute-done.15.refs_3_, ...), custom_call_target="tpu_custom_call" | custom-call | flops 3355443200 | bytes 9175040 | tf_op jit(solution)/shard_map/product_and_squares/pallas_call | solution.py:194
  128.7 2.1 %collective-permute-start.18 = (bf16[128,768]{1,0:T(8,128)(2,1)S(1)}, bf16[128,768]{1,0:T(8,128)(2,1)S(1)}, u32[]{:S(2)}, u32[]{:S(2)}) collective-permute-start(bf16[128,768]{1,0:T(8,128)(2,1)S(1)} %join_columns.42.refs_1_), channel_id=1, source_target_pairs={{0,7},{1,6},{2,5},{3,4},{4,3},{5,2},{6,1},{7,0},{8,15},{9,14},{10,... | collective-permute-start | bytes 589832 | tf_op jit(solution)/shard_map/ppermute | solution.py:24
  130.8 12.4 %collective-permute-done.19.refs_2_.refs_1_.refs_4_ = bf16[128,4096]{1,0:T(8,128)(2,1)S(1)} collective-permute-done((bf16[128,4096]{1,0:T(8,128)(2,1)S(1)}, bf16[128,4096]{1,0:T(8,128)(2,1)S(1)}, u32[]{:S(2)}, u32[]{:S(2)}) %collective-permute-start.19) | collective-permute-done | bytes 1048608 | tf_op jit(solution)/shard_map/ppermute | solution.py:24
  143.3 1.1 collective-permute-start.21
  144.3 0.1 join_columns.44.refs_0_
  144.5 0.1 collective-permute-start.22
  144.6 5.0 %product_and_squares.5.refs_2_.refs_8_ = f32[4,768,512]{2,1,0:T(8,128)S(1)} custom-call(bf16[128,2048]{1,0:T(8,128)(2,1)S(1)} %copy-done.3, bf16[128,4096]{1,0:T(8,128)(2,1)S(1)} %copy-done.1, bf16[128,4096]{1,0:T(8,128)(2,1)S(1)} %join_columns.36.refs_4_.refs_0_.refs_2_, bf16[128,12288]{1,0:T(8,128)(2,1)S(1)} %collective-permute-done.15.refs_3_, ...), custom_call_target="tpu_custom_call" | custom-call | flops 2013265920 | bytes 6553600 | tf_op jit(solution)/shard_map/product_and_squares/pallas_call | solution.py:194
  149.6 2.7 %collective-permute-done.21.refs_3_.refs_1_.refs_5_ = bf16[128,1280]{1,0:T(8,128)(2,1)S(1)} collective-permute-done((bf16[128,1280]{1,0:T(8,128)(2,1)S(1)}, bf16[128,1280]{1,0:T(8,128)(2,1)S(1)}, u32[]{:S(2)}, u32[]{:S(2)}) %collective-permute-start.21) | collective-permute-done | bytes 327712 | tf_op jit(solution)/shard_map/ppermute | solution.py:24
  152.4 0.1 collective-permute-start.24
  152.5 1.1 collective-permute-start.23
  153.6 1.0 collective-permute-done.24.refs_3_
  154.6 7.0 %product_and_squares.6 = (f32[4,1280,512]{2,1,0:T(8,128)S(1)}, f32[1,8,128]{2,1,0:T(8,128)S(1)}) custom-call(bf16[128,4096]{1,0:T(8,128)(2,1)S(1)} %join_columns.41.refs_0_, bf16[128,1280]{1,0:T(8,128)(2,1)S(1)} %join_columns.43.refs_2_.refs_0_.refs_1_, ...), custom_call_target="tpu_custom_call", output_to_operand_aliasing={{0}: (8, {})} | custom-call | flops 2013265920 | bytes 5505024 | tf_op jit(solution)/shard_map/product_and_squares/pallas_call | solution.py:194
  161.7 0.2 collective-permute-start.25
  161.9 1.6 collective-permute-done.25.refs_3_
  163.5 4.3 %product_and_squares.7 = (f32[4,768,512]{2,1,0:T(8,128)S(1)}, f32[32,8,128]{2,1,0:T(8,128)S(1)}) custom-call(bf16[128,4096]{1,0:T(8,128)(2,1)S(1)} %join_columns.41.refs_0_, bf16[128,768]{1,0:T(8,128)(2,1)S(1)} %join_columns.45.refs_2_.refs_0_.refs_1_, ...), custom_call_target="tpu_custom_call", output_to_operand_aliasing={{0}: (8, {})} | custom-call | flops 1207959552 | bytes 3932160 | tf_op jit(solution)/shard_map/product_and_squares/pallas_call | solution.py:194
  167.7 13.8 %all_to_all.5.sums_ref = f32[32,8,128]{2,1,0:T(8,128)S(1)} all-to-all(f32[32,8,128]{2,1,0:T(8,128)S(1)} %get-tuple-element.35), channel_id=1, replica_groups=mesh['user'=4,'tok'=8] {'user','tok'}, dimensions={0} | all-to-all | bytes 262144 | tf_op jit(solution)/shard_map/all_to_all | solution.py:465
  181.6 4.8 %weighted_sum.1 = f32[2048,512]{1,0:T(8,128)} custom-call(s32[1]{0:T(128)} %bitcast.user_ref, f32[32,8,128]{2,1,0:T(8,128)S(1)} %all_to_all.5.sums_ref, f32[4,1280,512]{2,1,0:T(8,128)S(1)} %get-tuple-element.33.refs_3_.refs_0_, f32[4,768,512]{2,1,0:T(8,128)S(1)} %get-tuple-element.36.refs_1_), custom_call_target="tpu_custom_call" | custom-call | tf_op jit(solution)/shard_map/weighted_sum/pallas_call | solution.py:251
  (58 shorter events, 0.6 us)
Async XLA Ops:
  0.7 1.0 copy-start.15
  1.7 10.3 %collective-permute-start = (bf16[128,512]{1,0:T(8,128)(2,1)S(1)}, bf16[128,512]{1,0:T(8,128)(2,1)S(1)}, u32[]{:S(2)}, u32[]{:S(2)}) collective-permute-start(bf16[128,512]{1,0:T(8,128)(2,1)S(1)} %get-tuple-element.25), channel_id=1, source_target_pairs={{0,8},{8,0},{16,24},{24,16},{1,9},{9,1},{17,25},{25,17},{2,10},{10... | collective-permute-start | bytes 393224 | tf_op jit(solution)/shard_map/ppermute | solution.py:24
  2.3 9.7 %collective-permute-start.1 = (bf16[128,512]{1,0:T(8,128)(2,1)S(1)}, bf16[128,512]{1,0:T(8,128)(2,1)S(1)}, u32[]{:S(2)}, u32[]{:S(2)}) collective-permute-start(bf16[128,512]{1,0:T(8,128)(2,1)S(1)} %get-tuple-element.26), channel_id=1, source_target_pairs={{0,16},{8,24},{16,0},{24,8},{1,17},{9,25},{17,1},{25,9},{2,18},{10... | collective-permute-start | bytes 393224 | tf_op jit(solution)/shard_map/ppermute | solution.py:24
  4.8 7.2 %collective-permute-start.2 = (bf16[128,512]{1,0:T(8,128)(2,1)S(1)}, bf16[128,512]{1,0:T(8,128)(2,1)S(1)}, u32[]{:S(2)}, u32[]{:S(2)}) collective-permute-start(bf16[128,512]{1,0:T(8,128)(2,1)S(1)} %get-tuple-element.27), channel_id=1, source_target_pairs={{0,24},{8,16},{16,8},{24,0},{1,25},{9,17},{17,9},{25,1},{2,26},{10... | collective-permute-start | bytes 393224 | tf_op jit(solution)/shard_map/ppermute | solution.py:24
  4.9 2.2 %copy-start.14 = (bf16[1,128,16384]{2,1,0:T(8,128)(2,1)S(1)}, bf16[1,128,16384]{2,1,0:T(8,128)(2,1)}, u32[]{:S(2)}) copy-start(bf16[1,128,16384]{2,1,0:T(8,128)(2,1)} %hidden_ref.1) | copy-start | bytes 12582916
  7.5 55.3 %collective-permute-start.6 = (bf16[128,2048]{1,0:T(8,128)(2,1)S(1)}, bf16[128,2048]{1,0:T(8,128)(2,1)S(1)}, u32[]{:S(2)}, u32[]{:S(2)}) collective-permute-start(bf16[128,2048]{1,0:T(8,128)(2,1)S(1)} %join_columns.24.refs_1_), channel_id=1, source_target_pairs={{0,4},{1,5},{2,6},{3,7},{4,0},{5,1},{6,2},{7,3},{8,12},{9,13},{10,... | collective-permute-start | bytes 1572872 | tf_op jit(solution)/shard_map/ppermute | solution.py:24
  10.4 76.9 %copy-start.2 = (bf16[128,2048]{1,0:T(8,128)(2,1)}, bf16[128,2048]{1,0:T(8,128)(2,1)S(1)}, u32[]{:S(2)}) copy-start(bf16[128,2048]{1,0:T(8,128)(2,1)S(1)} %join_columns.25.refs_4_.refs_1_.refs_0_) | copy-start | bytes 1572868
  10.4 50.0 %collective-permute-start.5 = (bf16[128,2048]{1,0:T(8,128)(2,1)S(1)}, bf16[128,2048]{1,0:T(8,128)(2,1)S(1)}, u32[]{:S(2)}, u32[]{:S(2)}) collective-permute-start(bf16[128,2048]{1,0:T(8,128)(2,1)S(1)} %join_columns.25.refs_4_.refs_1_.refs_0_), channel_id=1, source_target_pairs={{0,16},{8,24},{16,0},{24,8},{1,17},{9,25},{17,1},{25,9},{2,18},{10... | collective-permute-start | bytes 1572872 | tf_op jit(solution)/shard_map/ppermute | solution.py:24
  12.1 3.5 %copy-start.4 = (bf16[128,2048]{1,0:T(8,128)(2,1)}, bf16[128,2048]{1,0:T(8,128)(2,1)S(1)}, u32[]{:S(2)}) copy-start(bf16[128,2048]{1,0:T(8,128)(2,1)S(1)} %join_columns.26.refs_0_.refs_1_.refs_8_) | copy-start | bytes 1572868
  12.2 48.3 %collective-permute-start.3 = (bf16[128,4096]{1,0:T(8,128)(2,1)S(1)}, bf16[128,4096]{1,0:T(8,128)(2,1)S(1)}, u32[]{:S(2)}, u32[]{:S(2)}) collective-permute-start(bf16[128,4096]{1,0:T(8,128)(2,1)S(1)} %join_columns.28.refs_2_), channel_id=1, source_target_pairs={{0,1},{1,0},{2,3},{3,2},{4,5},{5,4},{6,7},{7,6},{8,9},{9,8},{10,11... | collective-permute-start | bytes 3145736 | tf_op jit(solution)/shard_map/ppermute | solution.py:24
  13.9 45.9 %collective-permute-start.4 = (bf16[128,4096]{1,0:T(8,128)(2,1)S(1)}, bf16[128,4096]{1,0:T(8,128)(2,1)S(1)}, u32[]{:S(2)}, u32[]{:S(2)}) collective-permute-start(bf16[128,4096]{1,0:T(8,128)(2,1)S(1)} %join_columns.29.refs_0_), channel_id=1, source_target_pairs={{0,2},{1,3},{2,0},{3,1},{4,6},{5,7},{6,4},{7,5},{8,10},{9,11},{10,... | collective-permute-start | bytes 3145736 | tf_op jit(solution)/shard_map/ppermute | solution.py:24
  15.5 53.7 %collective-permute-start.8 = (bf16[128,2048]{1,0:T(8,128)(2,1)S(1)}, bf16[128,2048]{1,0:T(8,128)(2,1)S(1)}, u32[]{:S(2)}, u32[]{:S(2)}) collective-permute-start(bf16[128,2048]{1,0:T(8,128)(2,1)S(1)} %join_columns.27.refs_2_), channel_id=1, source_target_pairs={{0,4},{1,5},{2,6},{3,7},{4,0},{5,1},{6,2},{7,3},{8,12},{9,13},{10,... | collective-permute-start | bytes 1572872 | tf_op jit(solution)/shard_map/ppermute | solution.py:24
  59.8 2.9 %copy-start.8 = (bf16[128,4096]{1,0:T(8,128)(2,1)}, bf16[128,4096]{1,0:T(8,128)(2,1)S(1)}, u32[]{:S(2)}) copy-start(bf16[128,4096]{1,0:T(8,128)(2,1)S(1)} %collective-permute-done.4.refs_0_.refs_1_.refs_10_) | copy-start | bytes 3145732
  59.9 35.0 %collective-permute-start.14 = (bf16[128,2048]{1,0:T(8,128)(2,1)S(1)}, bf16[128,2048]{1,0:T(8,128)(2,1)S(1)}, u32[]{:S(2)}, u32[]{:S(2)}) collective-permute-start(bf16[128,2048]{1,0:T(8,128)(2,1)S(1)} %join_columns.30.refs_2_), channel_id=1, source_target_pairs={{0,1},{1,0},{2,3},{3,2},{4,5},{5,4},{6,7},{7,6},{8,9},{9,8},{10,11... | collective-permute-start | bytes 1572872 | tf_op jit(solution)/shard_map/ppermute | solution.py:24
  60.5 26.9 %copy-start.12 = (bf16[128,2048]{1,0:T(8,128)(2,1)}, bf16[128,2048]{1,0:T(8,128)(2,1)S(1)}, u32[]{:S(2)}) copy-start(bf16[128,2048]{1,0:T(8,128)(2,1)S(1)} %collective-permute-done.5.refs_3_.refs_1_.refs_5_) | copy-start | bytes 1572868
  60.5 2.3 %copy-start.10 = (bf16[128,4096]{1,0:T(8,128)(2,1)}, bf16[128,4096]{1,0:T(8,128)(2,1)S(1)}, u32[]{:S(2)}) copy-start(bf16[128,4096]{1,0:T(8,128)(2,1)S(1)} %collective-permute-done.3.refs_0_.refs_9_) | copy-start | bytes 3145732
  60.6 26.8 %copy-start = (bf16[128,4096]{1,0:T(8,128)(2,1)}, bf16[128,4096]{1,0:T(8,128)(2,1)S(1)}, u32[]{:S(2)}) copy-start(bf16[128,4096]{1,0:T(8,128)(2,1)S(1)} %join_columns.31.refs_1_.refs_2_) | copy-start | bytes 3145732
  60.6 26.3 %collective-permute-start.11 = (bf16[128,4096]{1,0:T(8,128)(2,1)S(1)}, bf16[128,4096]{1,0:T(8,128)(2,1)S(1)}, u32[]{:S(2)}, u32[]{:S(2)}) collective-permute-start(bf16[128,4096]{1,0:T(8,128)(2,1)S(1)} %join_columns.31.refs_1_.refs_2_), channel_id=1, source_target_pairs={{0,16},{8,24},{16,0},{24,8},{1,17},{9,25},{17,1},{25,9},{2,18},{10... | collective-permute-start | bytes 3145736 | tf_op jit(solution)/shard_map/ppermute | solution.py:24
  62.2 24.7 %collective-permute-start.10 = (bf16[128,2048]{1,0:T(8,128)(2,1)S(1)}, bf16[128,2048]{1,0:T(8,128)(2,1)S(1)}, u32[]{:S(2)}, u32[]{:S(2)}) collective-permute-start(bf16[128,2048]{1,0:T(8,128)(2,1)S(1)} %join_columns.32.refs_0_), channel_id=1, source_target_pairs={{0,3},{1,2},{2,1},{3,0},{4,7},{5,6},{6,5},{7,4},{8,11},{9,10},{10,... | collective-permute-start | bytes 1572872 | tf_op jit(solution)/shard_map/ppermute | solution.py:24
  62.8 49.1 %collective-permute-start.7 = (bf16[128,2048]{1,0:T(8,128)(2,1)S(1)}, bf16[128,2048]{1,0:T(8,128)(2,1)S(1)}, u32[]{:S(2)}, u32[]{:S(2)}) collective-permute-start(bf16[128,2048]{1,0:T(8,128)(2,1)S(1)} %join_columns.33.refs_1_), channel_id=1, source_target_pairs={{0,5},{1,4},{2,7},{3,6},{4,1},{5,0},{6,3},{7,2},{8,13},{9,12},{10,... | collective-permute-start | bytes 1572872 | tf_op jit(solution)/shard_map/ppermute | solution.py:24
  69.2 48.5 %collective-permute-start.9 = (bf16[128,2048]{1,0:T(8,128)(2,1)S(1)}, bf16[128,2048]{1,0:T(8,128)(2,1)S(1)}, u32[]{:S(2)}, u32[]{:S(2)}) collective-permute-start(bf16[128,2048]{1,0:T(8,128)(2,1)S(1)} %join_columns.34.refs_1_), channel_id=1, source_target_pairs={{0,6},{1,7},{2,4},{3,5},{4,2},{5,3},{6,0},{7,1},{8,14},{9,15},{10,... | collective-permute-start | bytes 1572872 | tf_op jit(solution)/shard_map/ppermute | solution.py:24
  86.9 23.3 %collective-permute-start.13 = (bf16[128,2048]{1,0:T(8,128)(2,1)S(1)}, bf16[128,2048]{1,0:T(8,128)(2,1)S(1)}, u32[]{:S(2)}, u32[]{:S(2)}) collective-permute-start(bf16[128,2048]{1,0:T(8,128)(2,1)S(1)} %join_columns.35.refs_2_), channel_id=1, source_target_pairs={{0,2},{1,3},{2,0},{3,1},{4,6},{5,7},{6,4},{7,5},{8,10},{9,11},{10,... | collective-permute-start | bytes 1572872 | tf_op jit(solution)/shard_map/ppermute | solution.py:24
  86.9 1.1 copy-start.6
  87.0 24.6 %collective-permute-start.12 = (bf16[128,4096]{1,0:T(8,128)(2,1)S(1)}, bf16[128,4096]{1,0:T(8,128)(2,1)S(1)}, u32[]{:S(2)}, u32[]{:S(2)}) collective-permute-start(bf16[128,4096]{1,0:T(8,128)(2,1)S(1)} %join_columns.36.refs_4_.refs_0_.refs_2_), channel_id=1, source_target_pairs={{0,16},{8,24},{16,0},{24,8},{1,17},{9,25},{17,1},{25,9},{2,18},{10... | collective-permute-start | bytes 3145736 | tf_op jit(solution)/shard_map/ppermute | solution.py:24
  94.8 16.8 %collective-permute-start.15 = (bf16[128,12288]{1,0:T(8,128)(2,1)S(1)}, bf16[128,12288]{1,0:T(8,128)(2,1)S(1)}, u32[]{:S(2)}, u32[]{:S(2)}) collective-permute-start(bf16[128,12288]{1,0:T(8,128)(2,1)S(1)} %join_columns.37.refs_0_), channel_id=1, source_target_pairs={{0,8},{8,0},{16,24},{24,16},{1,9},{9,1},{17,25},{25,17},{2,10},{10... | collective-permute-start | bytes 9437192 | tf_op jit(solution)/shard_map/ppermute | solution.py:24
  110.3 34.3 %collective-permute-start.20 = (bf16[128,4096]{1,0:T(8,128)(2,1)S(1)}, bf16[128,4096]{1,0:T(8,128)(2,1)S(1)}, u32[]{:S(2)}, u32[]{:S(2)}) collective-permute-start(bf16[128,4096]{1,0:T(8,128)(2,1)S(1)} %join_columns.38.refs_2_), channel_id=1, source_target_pairs={{0,1},{1,0},{2,3},{3,2},{4,5},{5,4},{6,7},{7,6},{8,9},{9,8},{10,11... | collective-permute-start | bytes 3145736 | tf_op jit(solution)/shard_map/ppermute | solution.py:24
  111.8 7.2 %collective-permute-start.16 = (bf16[128,8192]{1,0:T(8,128)(2,1)S(1)}, bf16[128,8192]{1,0:T(8,128)(2,1)S(1)}, u32[]{:S(2)}, u32[]{:S(2)}) collective-permute-start(bf16[128,8192]{1,0:T(8,128)(2,1)S(1)} %join_columns.39.refs_0_), channel_id=1, source_target_pairs={{0,8},{8,0},{16,24},{24,16},{1,9},{9,1},{17,25},{25,17},{2,10},{10... | collective-permute-start | bytes 6291464 | tf_op jit(solution)/shard_map/ppermute | solution.py:24
  111.9 16.8 %collective-permute-start.17 = (bf16[128,1280]{1,0:T(8,128)(2,1)S(1)}, bf16[128,1280]{1,0:T(8,128)(2,1)S(1)}, u32[]{:S(2)}, u32[]{:S(2)}) collective-permute-start(bf16[128,1280]{1,0:T(8,128)(2,1)S(1)} %join_columns.40.refs_2_), channel_id=1, source_target_pairs={{0,7},{1,6},{2,5},{3,4},{4,3},{5,2},{6,1},{7,0},{8,15},{9,14},{10,... | collective-permute-start | bytes 983048 | tf_op jit(solution)/shard_map/ppermute | solution.py:24
  117.9 1.2 copy-start.1
  117.9 1.3 copy-start.3
  117.9 1.5 copy-start.5
  117.9 1.8 copy-start.7
  117.9 2.1 %copy-start.9 = (bf16[128,4096]{1,0:T(8,128)(2,1)S(1)}, bf16[128,4096]{1,0:T(8,128)(2,1)}, u32[]{:S(2)}) copy-start(bf16[128,4096]{1,0:T(8,128)(2,1)} %copy-done.8) | copy-start | bytes 3145732
  117.9 2.5 %copy-start.11 = (bf16[128,4096]{1,0:T(8,128)(2,1)S(1)}, bf16[128,4096]{1,0:T(8,128)(2,1)}, u32[]{:S(2)}) copy-start(bf16[128,4096]{1,0:T(8,128)(2,1)} %copy-done.10) | copy-start | bytes 3145732
  117.9 2.6 %copy-start.13 = (bf16[128,2048]{1,0:T(8,128)(2,1)S(1)}, bf16[128,2048]{1,0:T(8,128)(2,1)}, u32[]{:S(2)}) copy-start(bf16[128,2048]{1,0:T(8,128)(2,1)} %copy-done.12) | copy-start | bytes 1572868
  117.9 25.3 %collective-permute-start.19 = (bf16[128,4096]{1,0:T(8,128)(2,1)S(1)}, bf16[128,4096]{1,0:T(8,128)(2,1)S(1)}, u32[]{:S(2)}, u32[]{:S(2)}) collective-permute-start(bf16[128,4096]{1,0:T(8,128)(2,1)S(1)} %join_columns.41.refs_0_), channel_id=1, source_target_pairs={{0,16},{8,24},{16,0},{24,8},{1,17},{9,25},{17,1},{25,9},{2,18},{10... | collective-permute-start | bytes 3145736 | tf_op jit(solution)/shard_map/ppermute | solution.py:24
  128.7 20.9 %collective-permute-start.18 = (bf16[128,768]{1,0:T(8,128)(2,1)S(1)}, bf16[128,768]{1,0:T(8,128)(2,1)S(1)}, u32[]{:S(2)}, u32[]{:S(2)}) collective-permute-start(bf16[128,768]{1,0:T(8,128)(2,1)S(1)} %join_columns.42.refs_1_), channel_id=1, source_target_pairs={{0,7},{1,6},{2,5},{3,4},{4,3},{5,2},{6,1},{7,0},{8,15},{9,14},{10,... | collective-permute-start | bytes 589832 | tf_op jit(solution)/shard_map/ppermute | solution.py:24
  143.3 9.1 %collective-permute-start.21 = (bf16[128,1280]{1,0:T(8,128)(2,1)S(1)}, bf16[128,1280]{1,0:T(8,128)(2,1)S(1)}, u32[]{:S(2)}, u32[]{:S(2)}) collective-permute-start(bf16[128,1280]{1,0:T(8,128)(2,1)S(1)} %join_columns.43.refs_2_.refs_0_.refs_1_), channel_id=1, source_target_pairs={{0,16},{8,24},{16,0},{24,8},{1,17},{9,25},{17,1},{25,9},{2,18},{10... | collective-permute-start | bytes 983048 | tf_op jit(solution)/shard_map/ppermute | solution.py:24
  144.5 7.9 %collective-permute-start.22 = (bf16[128,8192]{1,0:T(8,128)(2,1)S(1)}, bf16[128,8192]{1,0:T(8,128)(2,1)S(1)}, u32[]{:S(2)}, u32[]{:S(2)}) collective-permute-start(bf16[128,8192]{1,0:T(8,128)(2,1)S(1)} %join_columns.44.refs_0_), channel_id=1, source_target_pairs={{0,8},{8,0},{16,24},{24,16},{1,9},{9,1},{17,25},{25,17},{2,10},{10... | collective-permute-start | bytes 6291464 | tf_op jit(solution)/shard_map/ppermute | solution.py:24
  152.4 2.2 %collective-permute-start.24 = (bf16[128,2560]{1,0:T(8,128)(2,1)S(1)}, bf16[128,2560]{1,0:T(8,128)(2,1)S(1)}, u32[]{:S(2)}, u32[]{:S(2)}) collective-permute-start(bf16[128,2560]{1,0:T(8,128)(2,1)S(1)} %join_columns.46.refs_2_), channel_id=1, source_target_pairs={{0,8},{8,0},{16,24},{24,16},{1,9},{9,1},{17,25},{25,17},{2,10},{10... | collective-permute-start | bytes 1966088 | tf_op jit(solution)/shard_map/ppermute | solution.py:24
  152.5 9.1 %collective-permute-start.23 = (bf16[128,768]{1,0:T(8,128)(2,1)S(1)}, bf16[128,768]{1,0:T(8,128)(2,1)S(1)}, u32[]{:S(2)}, u32[]{:S(2)}) collective-permute-start(bf16[128,768]{1,0:T(8,128)(2,1)S(1)} %join_columns.45.refs_2_.refs_0_.refs_1_), channel_id=1, source_target_pairs={{0,16},{8,24},{16,0},{24,8},{1,17},{9,25},{17,1},{25,9},{2,18},{10... | collective-permute-start | bytes 589832 | tf_op jit(solution)/shard_map/ppermute | solution.py:24
  161.7 1.8 collective-permute-start.25

commit v12 on v11

--- a/solution.py
+++ b/solution.py
@@ -304,18 +304,22 @@
     outgoing = pack(tok, hidden, list(range(tok_count)), own_width, [])
     ready += [(0, i, outgoing[0], start) for i, (start, _) in enumerate(pieces)]
 
-    far = list(range(half + 1, tok_count))
     far_steps = [[(half, None), ("cots", None)], [None, None]]
-    while len(far) > 1:
-        far_steps += [[(far.pop(0), None), (far.pop(0), None)], [None, None]]
-    far_steps += [[(far[0], 0), ("wait", None)], [(far[0], 1), None]]
-    last_pair = len(far_steps) - 3
+    far = [(d, None) for d in range(half + 1, tok_count - 1)] + [(tok_count - 1, 0), (tok_count - 1, 1)]
+    for at, block in enumerate(far):
+        far_steps.append([block, None] if at % 2 == 0 else [None, block])
+    far_steps += [[("wait", None), None], [None, ("wait", None)]]
     near = list(range(1, half))
     near_steps = [near[:2]] + [[d] for d in near[2:]]
     relayed = set()
 
+    def rides(d):
+        return d & (d - 1) == 0 and d < half // 2
+
     def bits_below(d):
-        return [1 << i for i in range(((d & -d) or 1).bit_length() - 1)]
+        if d == 0:
+            return [half // 2]
+        return [1 << i for i in range((d & -d).bit_length() - 1)]
 
 
     lanes_before = [None, None]
@@ -373,11 +377,9 @@
         gradients[i] = out
         tick.append(out[0])
 
-    for step in range(len(far_steps) + 2):
+    for step in range(len(far_steps) + 1):
         flying = 0
-        now = far_steps[step] if step < len(far_steps) else [None, ("wait", None)]
-        if step == len(far_steps):
-            now = [("wait", None), None]
+        now = far_steps[step] if step < len(far_steps) else [None, None]
         for lane in (0, 1):
             if lane == 1 and now[1] == ("cots", None):
                 continue
@@ -402,17 +404,17 @@
             flying += lanes_before[lane] is not None
         for d, array in near_before:
             ready += [(d, i, array, first) for i, (first, _) in enumerate(pieces)]
-            if d & (d - 1) == 0:
+            if rides(d):
                 cots[d] = cots_at(array, own_width)
         near_before.clear()
         arrivals = finish_relays(step)
         bit = half // 2
         while bit:
             sources = [d for d in sorted(cots) if bit in bits_below(d) and d + bit not in relayed]
-            if sources and flying < 3:
+            if sources and flying < 4 and step > 0:
                 relayed.update(d + bit for d in sources)
                 parts = [part for d in sources for part in cot_parts(d)]
-                relay_before.append((step + (2 if step >= last_pair else 1), bit, sources, send("tok", bit, parts)[1]))
+                relay_before.append((step + 2, bit, sources, send("tok", bit, parts)[1]))
                 flying += 1
             bit //= 2
         if cross_before is not None:
@@ -435,13 +437,13 @@
         if step < len(near_steps):
             for d in near_steps[step]:
                 parts = [(outgoing[d], 0, own_width)]
-                if d & (d - 1) == 0:
+                if rides(d):
                     parts += cot_parts(0)
                 near_before.append((d, send("tok", d, parts)[1]))
                 flying += 1
         before = [core_before[1]] if core_before else []
         finish_core()
-        if crossed and (flying < 5 or step >= last_pair):
+        if crossed and (flying < 5 or step >= len(far_steps) - 3):
             parts = []
             for blocks, own, other in crossed:
                 total = sum(pieces[i][1] for _, i, _, _ in blocks)
@@ -452,11 +454,11 @@
         if step < len(far_steps):
             tick[:] = [hold(tick[0], arrivals, max(sizes))]
             sizes[:] = [0]
-        if step == last_pair + 1:
+        if step == len(far_steps) - 3:
             add_products(0)
-        elif step == last_pair + 2:
+        elif step == len(far_steps) - 2:
             add_products(1)
-        elif step == len(far_steps):
+        elif step == len(far_steps) - 1:
             finish_core()
             add_products(0)
     finish_core()

time: 187 us -> 197 us (1.053)
  starting transfers between devices: 35.4 us -> 45.1 us
  waiting for transfers between devices: 99.8 us -> 102 us
    ppermute x26 -> x29, starting transfers between devices: 35.4 us -> 45.1 us  [exchange(): return lax.ppermute(block, axis, [(i, i ^ distance) for i in range(size)])]
    ppermute x26 -> x29, waiting for transfers between devices: 99.8 us -> 102 us  [exchange(): return lax.ppermute(block, axis, [(i, i ^ distance) for i in range(size)])]
    unnamed x32 -> x24, local copies, waits for them, and re-layouts: 5.15 us -> 3.27 us
  transfers between devices with their start and end apart: 26 -> 29, of which waited for: 8 -> 9; matrix products, arithmetic and copies ran while one was open for 0% -> 0% of each run, Pallas kernels for 12% -> 11%
where the time goes in v12:
time: 197 us; the launch traced here: 196 us
  waiting for transfers between devices  102 us (52%)
  starting transfers between devices  45.1 us (23%)
  Pallas kernels  30.3 us (15%)
  blocking collectives  14.8 us (8%)
  local copies, waits for them, and re-layouts  3.27 us (2%)
    ppermute x29, waiting for transfers between devices, exchange(): return lax.ppermute(block, axis, [(i, i ^ distance) for i in range(size)])  102 us
    ppermute x29, starting transfers between devices, exchange(): return lax.ppermute(block, axis, [(i, i ^ distance) for i in range(size)])  45.1 us
    pallas_call x4, Pallas kernels, product(): pl.pallas_call(functools.partial(product_kernel, left_places, right_place...  23.7 us
    all_to_all x1, blocking collectives, body(): lax.all_to_all(gradients[1][1], ('user', 'tok'), split_axis=0, concat_axi...  14.8 us
    pallas_call x1, Pallas kernels, combine(): pl.pallas_call(functools.partial(combine_kernel, user_count, clip_bound,...  4.81 us
  transfers between devices with their start and end apart: 29, of which 9 were waited for; matrix products, arithmetic and copies ran while one was open for 0% of the time, Pallas kernels for 11%

profile of v12, /device:TPU:0, one launch (start us, length us, event | category | flops | bytes accessed | tf_op | source)
XLA Modules:
  0.0 196.5 jit_solution(284433302624556362)
XLA Ops:
  0.7 1.0 copy-done.11
  1.7 0.5 collective-permute-start.1
  2.3 2.6 %collective-permute-start.2 = (bf16[128,512]{1,0:T(8,128)(2,1)S(1)}, bf16[128,512]{1,0:T(8,128)(2,1)S(1)}, u32[]{:S(2)}, u32[]{:S(2)}) collective-permute-start(bf16[128,512]{1,0:T(8,128)(2,1)S(1)} %get-tuple-element.27), channel_id=1, source_target_pairs={{0,16},{8,24},{16,0},{24,8},{1,17},{9,25},{17,1},{25,9},{2,18},{10... | collective-permute-start | bytes 393224 | tf_op jit(solution)/shard_map/ppermute | solution.py:24
  4.8 0.1 collective-permute-start.3
  4.9 2.2 %copy-done.10 = bf16[1,128,16384]{2,1,0:T(8,128)(2,1)S(1)} copy-done((bf16[1,128,16384]{2,1,0:T(8,128)(2,1)S(1)}, bf16[1,128,16384]{2,1,0:T(8,128)(2,1)}, u32[]{:S(2)}) %copy-start.10) | copy-done | bytes 4194328
  7.1 0.4 pack_columns.1
  7.5 2.9 %collective-permute-start.7 = (bf16[128,2048]{1,0:T(8,128)(2,1)S(1)}, bf16[128,2048]{1,0:T(8,128)(2,1)S(1)}, u32[]{:S(2)}, u32[]{:S(2)}) collective-permute-start(bf16[128,2048]{1,0:T(8,128)(2,1)S(1)} %join_columns.27.refs_1_), channel_id=1, source_target_pairs={{0,4},{1,5},{2,6},{3,7},{4,0},{5,1},{6,2},{7,3},{8,12},{9,13},{10,... | collective-permute-start | bytes 1572872 | tf_op jit(solution)/shard_map/ppermute | solution.py:24
  10.4 1.6 collective-permute-start
  12.0 0.0 collective-permute-done.2.refs_2_
  12.0 0.0 collective-permute-done.3.refs_3_
  12.1 0.1 join_columns.31.refs_1_
  12.2 1.6 collective-permute-start.4
  13.8 1.6 collective-permute-start.5
  15.5 2.1 %collective-permute-start.9 = (bf16[128,2048]{1,0:T(8,128)(2,1)S(1)}, bf16[128,2048]{1,0:T(8,128)(2,1)S(1)}, u32[]{:S(2)}, u32[]{:S(2)}) collective-permute-start(bf16[128,2048]{1,0:T(8,128)(2,1)S(1)} %join_columns.30.refs_2_), channel_id=1, source_target_pairs={{0,4},{1,5},{2,6},{3,7},{4,0},{5,1},{6,2},{7,3},{8,12},{9,13},{10,... | collective-permute-start | bytes 1572872 | tf_op jit(solution)/shard_map/ppermute | solution.py:24
  17.6 6.8 %collective-permute-done.refs_3_.refs_1_.refs_5_.refs_7_ = bf16[128,2048]{1,0:T(8,128)(2,1)S(1)} collective-permute-done((bf16[128,2048]{1,0:T(8,128)(2,1)S(1)}, bf16[128,2048]{1,0:T(8,128)(2,1)S(1)}, u32[]{:S(2)}, u32[]{:S(2)}) %collective-permute-start) | collective-permute-done | bytes 524320 | tf_op jit(solution)/shard_map/ppermute | solution.py:24
  24.4 1.6 collective-permute-start.14
  26.0 14.0 %collective-permute-done.5.refs_1_ = bf16[128,2048]{1,0:T(8,128)(2,1)S(1)} collective-permute-done((bf16[128,2048]{1,0:T(8,128)(2,1)S(1)}, bf16[128,2048]{1,0:T(8,128)(2,1)S(1)}, u32[]{:S(2)}, u32[]{:S(2)}) %collective-permute-start.5) | collective-permute-done | bytes 524320 | tf_op jit(solution)/shard_map/ppermute | solution.py:24
  40.0 0.1 join_columns.34.refs_1_.refs_2_
  40.1 0.0 copy-start
  40.1 1.0 collective-permute-start.6
  41.1 0.3 collective-permute-start.8
  41.4 0.0 collective-permute-done.7.refs_2_.refs_0_
  41.4 4.9 %collective-permute-start.12 = (bf16[128,2048]{1,0:T(8,128)(2,1)S(1)}, bf16[128,2048]{1,0:T(8,128)(2,1)S(1)}, u32[]{:S(2)}, u32[]{:S(2)}) collective-permute-start(bf16[128,2048]{1,0:T(8,128)(2,1)S(1)} %join_columns.36.refs_2_), channel_id=1, source_target_pairs={{0,5},{1,4},{2,7},{3,6},{4,1},{5,0},{6,3},{7,2},{8,13},{9,12},{10,... | collective-permute-start | bytes 1572872 | tf_op jit(solution)/shard_map/ppermute | solution.py:24
  46.4 35.9 %collective-permute-done.8.refs_1_ = bf16[128,2048]{1,0:T(8,128)(2,1)S(1)} collective-permute-done((bf16[128,2048]{1,0:T(8,128)(2,1)S(1)}, bf16[128,2048]{1,0:T(8,128)(2,1)S(1)}, u32[]{:S(2)}, u32[]{:S(2)}) %collective-permute-start.8) | collective-permute-done | bytes 524320 | tf_op jit(solution)/shard_map/ppermute | solution.py:24
  82.2 0.1 join_columns.37.refs_4_.refs_0_.refs_2_
  82.3 1.6 collective-permute-start.13
  83.9 0.2 join_columns.38.refs_0_
  84.1 0.1 collective-permute-start.15
  84.2 5.4 %collective-permute-start.10 = (bf16[128,2048]{1,0:T(8,128)(2,1)S(1)}, bf16[128,2048]{1,0:T(8,128)(2,1)S(1)}, u32[]{:S(2)}, u32[]{:S(2)}) collective-permute-start(bf16[128,2048]{1,0:T(8,128)(2,1)S(1)} %join_columns.39.refs_1_), channel_id=1, source_target_pairs={{0,6},{1,7},{2,4},{3,5},{4,2},{5,3},{6,0},{7,1},{8,14},{9,15},{10,... | collective-permute-start | bytes 1572872 | tf_op jit(solution)/shard_map/ppermute | solution.py:24
  89.7 0.0 collective-permute-done.14.refs_0_.refs_1_.refs_10_.refs_13_
  89.7 0.1 collective-permute-start.11
  89.8 0.1 join_columns.41.refs_2_
  89.9 16.4 %collective-permute-done.13.refs_1_.refs_7_.refs_9_ = bf16[128,4096]{1,0:T(8,128)(2,1)S(1)} collective-permute-done((bf16[128,4096]{1,0:T(8,128)(2,1)S(1)}, bf16[128,4096]{1,0:T(8,128)(2,1)S(1)}, u32[]{:S(2)}, u32[]{:S(2)}) %collective-permute-start.13) | collective-permute-done | bytes 1048608 | tf_op jit(solution)/shard_map/ppermute | solution.py:24
  106.3 1.5 collective-permute-start.20
  107.9 0.0 collective-permute-done.15.refs_3_.refs_4_
  107.9 0.1 join_columns.42.refs_0_
  108.0 0.0 collective-permute-done.12.refs_2_.refs_0_
  108.1 1.8 collective-permute-start.16
  109.9 6.0 %collective-permute-start.19 = (bf16[128,1280]{1,0:T(8,128)(2,1)S(1)}, bf16[128,1280]{1,0:T(8,128)(2,1)S(1)}, u32[]{:S(2)}, u32[]{:S(2)}) collective-permute-start(bf16[128,1280]{1,0:T(8,128)(2,1)S(1)} %join_columns.43.refs_1_), channel_id=1, source_target_pairs={{0,7},{1,6},{2,5},{3,4},{4,3},{5,2},{6,1},{7,0},{8,15},{9,14},{10,... | collective-permute-start | bytes 983048 | tf_op jit(solution)/shard_map/ppermute | solution.py:24
  116.0 0.0 collective-permute-done.10.refs_2_.refs_0_
  116.0 0.0 collective-permute-start.21
  116.0 0.0 collective-permute-done.11.refs_0_.refs_1_.refs_10_.refs_6_
  116.0 0.3 collective-permute-start.17
  116.3 3.8 %collective-permute-done.16.refs_2_.refs_1_.refs_10_.refs_6_ = bf16[128,2048]{1,0:T(8,128)(2,1)S(1)} collective-permute-done((bf16[128,2048]{1,0:T(8,128)(2,1)S(1)}, bf16[128,2048]{1,0:T(8,128)(2,1)S(1)}, u32[]{:S(2)}, u32[]{:S(2)}) %collective-permute-start.16) | collective-permute-done | bytes 524320 | tf_op jit(solution)/shard_map/ppermute | solution.py:24
  120.2 1.8 collective-permute-start.18
  122.0 0.1 join_columns.48.refs_0_
  122.1 0.0 copy-start.1
  122.1 18.5 %collective-permute-done.20.refs_2_.refs_11_.refs_14_.refs_9_ = bf16[128,4096]{1,0:T(8,128)(2,1)S(1)} collective-permute-done((bf16[128,4096]{1,0:T(8,128)(2,1)S(1)}, bf16[128,4096]{1,0:T(8,128)(2,1)S(1)}, u32[]{:S(2)}, u32[]{:S(2)}) %collective-permute-start.20) | collective-permute-done | bytes 1048608 | tf_op jit(solution)/shard_map/ppermute | solution.py:24
  140.6 1.6 collective-permute-start.26
  142.3 8.2 %product_and_squares.4.refs_2_.refs_12_ = f32[4,1280,512]{2,1,0:T(8,128)S(1)} custom-call(bf16[128,2048]{1,0:T(8,128)(2,1)S(1)} %copy-done.3, bf16[128,4096]{1,0:T(8,128)(2,1)S(1)} %copy-done.1, bf16[128,4096]{1,0:T(8,128)(2,1)S(1)} %join_columns.37.refs_4_.refs_0_.refs_2_, bf16[128,12288]{1,0:T(8,128)(2,1)S(1)} %collective-permute-done.15.refs_3_.refs_4_, ...), custom_call_target="tpu_custom_call" | custom-call | flops 3355443200 | bytes 9175040 | tf_op jit(solution)/shard_map/product_and_squares/pallas_call | solution.py:194
  150.5 2.0 %collective-permute-start.23 = (bf16[128,1280]{1,0:T(8,128)(2,1)S(1)}, bf16[128,1280]{1,0:T(8,128)(2,1)S(1)}, u32[]{:S(2)}, u32[]{:S(2)}) collective-permute-start(bf16[128,1280]{1,0:T(8,128)(2,1)S(1)} %join_columns.49.refs_2_.refs_0_), channel_id=1, source_target_pairs={{0,16},{8,24},{16,0},{24,8},{1,17},{9,25},{17,1},{25,9},{2,18},{10... | collective-permute-start | bytes 983048 | tf_op jit(solution)/shard_map/ppermute | solution.py:24
  152.6 0.1 join_columns.50.refs_0_
  152.6 0.1 collective-permute-start.24
  152.7 5.1 %product_and_squares.5.refs_2_.refs_8_ = f32[4,768,512]{2,1,0:T(8,128)S(1)} custom-call(bf16[128,2048]{1,0:T(8,128)(2,1)S(1)} %copy-done.3, bf16[128,4096]{1,0:T(8,128)(2,1)S(1)} %copy-done.1, bf16[128,4096]{1,0:T(8,128)(2,1)S(1)} %join_columns.37.refs_4_.refs_0_.refs_2_, bf16[128,2048]{1,0:T(8,128)(2,1)S(1)} %join_columns.44.refs_0_.refs_3_, ...), custom_call_target="tpu_custom_call" | custom-call | flops 2415919104 | bytes 7864320 | tf_op jit(solution)/shard_map/product_and_squares/pallas_call | solution.py:194
  157.8 2.8 %collective-permute-done.23.refs_3_.refs_1_.refs_8_ = bf16[128,1280]{1,0:T(8,128)(2,1)S(1)} collective-permute-done((bf16[128,1280]{1,0:T(8,128)(2,1)S(1)}, bf16[128,1280]{1,0:T(8,128)(2,1)S(1)}, u32[]{:S(2)}, u32[]{:S(2)}) %collective-permute-start.23) | collective-permute-done | bytes 327712 | tf_op jit(solution)/shard_map/ppermute | solution.py:24
  160.6 1.8 collective-permute-start.25
  162.5 0.1 collective-permute-start.27
  162.6 2.1 %collective-permute-done.27.refs_5_ = bf16[128,2560]{1,0:T(8,128)(2,1)S(1)} collective-permute-done((bf16[128,2560]{1,0:T(8,128)(2,1)S(1)}, bf16[128,2560]{1,0:T(8,128)(2,1)S(1)}, u32[]{:S(2)}, u32[]{:S(2)}) %collective-permute-start.27) | collective-permute-done | bytes 655392 | tf_op jit(solution)/shard_map/ppermute | solution.py:24
  164.6 7.0 %product_and_squares.6 = (f32[4,1280,512]{2,1,0:T(8,128)S(1)}, f32[1,8,128]{2,1,0:T(8,128)S(1)}) custom-call(bf16[128,2048]{1,0:T(8,128)(2,1)S(1)} %join_columns.44.refs_0_.refs_3_, bf16[128,2048]{1,0:T(8,128)(2,1)S(1)} %join_columns.47.refs_2_.refs_0_.refs_1_, bf16[128,1280]{1,0:T(8,128)(2,1)S(1)} %join_columns.49.refs_2_.refs_0_, ...), custom_call_target="tpu_custom_call", output_to_operand_aliasing={{0}: (12, {})} | custom-call | flops 2013265920 | bytes 5505024 | tf_op jit(solution)/shard_map/product_and_squares/pallas_call | solution.py:194
  171.7 0.2 collective-permute-start.28
  171.9 1.6 collective-permute-done.28.refs_3_
  173.5 3.4 %product_and_squares.7 = (f32[4,768,512]{2,1,0:T(8,128)S(1)}, f32[32,8,128]{2,1,0:T(8,128)S(1)}) custom-call(bf16[128,2048]{1,0:T(8,128)(2,1)S(1)} %join_columns.47.refs_2_.refs_0_.refs_1_, bf16[128,768]{1,0:T(8,128)(2,1)S(1)} %join_columns.51.refs_2_.refs_0_.refs_1_, ...), custom_call_target="tpu_custom_call", output_to_operand_aliasing={{0}: (8, {})} | custom-call | flops 805306368 | bytes 2621440 | tf_op jit(solution)/shard_map/product_and_squares/pallas_call | solution.py:194
  176.9 14.8 %all_to_all.5.sums_ref = f32[32,8,128]{2,1,0:T(8,128)S(1)} all-to-all(f32[32,8,128]{2,1,0:T(8,128)S(1)} %get-tuple-element.35), channel_id=1, replica_groups=mesh['user'=4,'tok'=8] {'user','tok'}, dimensions={0} | all-to-all | bytes 262144 | tf_op jit(solution)/shard_map/all_to_all | solution.py:467
  191.7 4.8 %weighted_sum.1 = f32[2048,512]{1,0:T(8,128)} custom-call(s32[1]{0:T(128)} %bitcast.user_ref, f32[32,8,128]{2,1,0:T(8,128)S(1)} %all_to_all.5.sums_ref, f32[4,1280,512]{2,1,0:T(8,128)S(1)} %get-tuple-element.33.refs_3_.refs_0_, f32[4,768,512]{2,1,0:T(8,128)S(1)} %get-tuple-element.36.refs_1_), custom_call_target="tpu_custom_call" | custom-call | tf_op jit(solution)/shard_map/weighted_sum/pallas_call | solution.py:251
  (61 shorter events, 0.8 us)
Async XLA Ops:
  0.7 1.0 copy-start.11
  1.7 10.3 %collective-permute-start.1 = (bf16[128,512]{1,0:T(8,128)(2,1)S(1)}, bf16[128,512]{1,0:T(8,128)(2,1)S(1)}, u32[]{:S(2)}, u32[]{:S(2)}) collective-permute-start(bf16[128,512]{1,0:T(8,128)(2,1)S(1)} %get-tuple-element.26), channel_id=1, source_target_pairs={{0,8},{8,0},{16,24},{24,16},{1,9},{9,1},{17,25},{25,17},{2,10},{10... | collective-permute-start | bytes 393224 | tf_op jit(solution)/shard_map/ppermute | solution.py:24
  2.3 9.7 %collective-permute-start.2 = (bf16[128,512]{1,0:T(8,128)(2,1)S(1)}, bf16[128,512]{1,0:T(8,128)(2,1)S(1)}, u32[]{:S(2)}, u32[]{:S(2)}) collective-permute-start(bf16[128,512]{1,0:T(8,128)(2,1)S(1)} %get-tuple-element.27), channel_id=1, source_target_pairs={{0,16},{8,24},{16,0},{24,8},{1,17},{9,25},{17,1},{25,9},{2,18},{10... | collective-permute-start | bytes 393224 | tf_op jit(solution)/shard_map/ppermute | solution.py:24
  4.8 7.2 %collective-permute-start.3 = (bf16[128,512]{1,0:T(8,128)(2,1)S(1)}, bf16[128,512]{1,0:T(8,128)(2,1)S(1)}, u32[]{:S(2)}, u32[]{:S(2)}) collective-permute-start(bf16[128,512]{1,0:T(8,128)(2,1)S(1)} %get-tuple-element.28), channel_id=1, source_target_pairs={{0,24},{8,16},{16,8},{24,0},{1,25},{9,17},{17,9},{25,1},{2,26},{10... | collective-permute-start | bytes 393224 | tf_op jit(solution)/shard_map/ppermute | solution.py:24
  4.9 2.2 %copy-start.10 = (bf16[1,128,16384]{2,1,0:T(8,128)(2,1)S(1)}, bf16[1,128,16384]{2,1,0:T(8,128)(2,1)}, u32[]{:S(2)}) copy-start(bf16[1,128,16384]{2,1,0:T(8,128)(2,1)} %hidden_ref.1) | copy-start | bytes 12582916
  7.5 33.9 %collective-permute-start.7 = (bf16[128,2048]{1,0:T(8,128)(2,1)S(1)}, bf16[128,2048]{1,0:T(8,128)(2,1)S(1)}, u32[]{:S(2)}, u32[]{:S(2)}) collective-permute-start(bf16[128,2048]{1,0:T(8,128)(2,1)S(1)} %join_columns.27.refs_1_), channel_id=1, source_target_pairs={{0,4},{1,5},{2,6},{3,7},{4,0},{5,1},{6,2},{7,3},{8,12},{9,13},{10,... | collective-permute-start | bytes 1572872 | tf_op jit(solution)/shard_map/ppermute | solution.py:24
  10.4 73.4 %copy-start.2 = (bf16[128,2048]{1,0:T(8,128)(2,1)}, bf16[128,2048]{1,0:T(8,128)(2,1)S(1)}, u32[]{:S(2)}) copy-start(bf16[128,2048]{1,0:T(8,128)(2,1)S(1)} %join_columns.28.refs_4_.refs_1_.refs_0_) | copy-start | bytes 1572868
  10.4 14.0 %collective-permute-start = (bf16[128,2048]{1,0:T(8,128)(2,1)S(1)}, bf16[128,2048]{1,0:T(8,128)(2,1)S(1)}, u32[]{:S(2)}, u32[]{:S(2)}) collective-permute-start(bf16[128,2048]{1,0:T(8,128)(2,1)S(1)} %join_columns.28.refs_4_.refs_1_.refs_0_), channel_id=1, source_target_pairs={{0,16},{8,24},{16,0},{24,8},{1,17},{9,25},{17,1},{25,9},{2,18},{10... | collective-permute-start | bytes 1572872 | tf_op jit(solution)/shard_map/ppermute | solution.py:24
  12.1 5.5 %copy-start.4 = (bf16[128,2048]{1,0:T(8,128)(2,1)}, bf16[128,2048]{1,0:T(8,128)(2,1)S(1)}, u32[]{:S(2)}) copy-start(bf16[128,2048]{1,0:T(8,128)(2,1)S(1)} %join_columns.29.refs_0_.refs_1_.refs_8_.refs_11_) | copy-start | bytes 1572868
  12.2 27.8 %collective-permute-start.4 = (bf16[128,4096]{1,0:T(8,128)(2,1)S(1)}, bf16[128,4096]{1,0:T(8,128)(2,1)S(1)}, u32[]{:S(2)}, u32[]{:S(2)}) collective-permute-start(bf16[128,4096]{1,0:T(8,128)(2,1)S(1)} %join_columns.31.refs_1_), channel_id=1, source_target_pairs={{0,1},{1,0},{2,3},{3,2},{4,5},{5,4},{6,7},{7,6},{8,9},{9,8},{10,11... | collective-permute-start | bytes 3145736 | tf_op jit(solution)/shard_map/ppermute | solution.py:24
  13.8 26.2 %collective-permute-start.5 = (bf16[128,2048]{1,0:T(8,128)(2,1)S(1)}, bf16[128,2048]{1,0:T(8,128)(2,1)S(1)}, u32[]{:S(2)}, u32[]{:S(2)}) collective-permute-start(bf16[128,2048]{1,0:T(8,128)(2,1)S(1)} %join_columns.32.refs_0_), channel_id=1, source_target_pairs={{0,2},{1,3},{2,0},{3,1},{4,6},{5,7},{6,4},{7,5},{8,10},{9,11},{10,... | collective-permute-start | bytes 1572872 | tf_op jit(solution)/shard_map/ppermute | solution.py:24
  15.5 68.7 %collective-permute-start.9 = (bf16[128,2048]{1,0:T(8,128)(2,1)S(1)}, bf16[128,2048]{1,0:T(8,128)(2,1)S(1)}, u32[]{:S(2)}, u32[]{:S(2)}) collective-permute-start(bf16[128,2048]{1,0:T(8,128)(2,1)S(1)} %join_columns.30.refs_2_), channel_id=1, source_target_pairs={{0,4},{1,5},{2,6},{3,7},{4,0},{5,1},{6,2},{7,3},{8,12},{9,13},{10,... | collective-permute-start | bytes 1572872 | tf_op jit(solution)/shard_map/ppermute | solution.py:24
  24.4 65.3 %collective-permute-start.14 = (bf16[128,2048]{1,0:T(8,128)(2,1)S(1)}, bf16[128,2048]{1,0:T(8,128)(2,1)S(1)}, u32[]{:S(2)}, u32[]{:S(2)}) collective-permute-start(bf16[128,2048]{1,0:T(8,128)(2,1)S(1)} %join_columns.33.refs_2_), channel_id=1, source_target_pairs={{0,2},{1,3},{2,0},{3,1},{4,6},{5,7},{6,4},{7,5},{8,10},{9,11},{10,... | collective-permute-start | bytes 1572872 | tf_op jit(solution)/shard_map/ppermute | solution.py:24
  40.0 1.4 copy-start.8
  40.1 43.8 %copy-start = (bf16[128,4096]{1,0:T(8,128)(2,1)}, bf16[128,4096]{1,0:T(8,128)(2,1)S(1)}, u32[]{:S(2)}) copy-start(bf16[128,4096]{1,0:T(8,128)(2,1)S(1)} %join_columns.34.refs_1_.refs_2_) | copy-start | bytes 3145732
  40.1 42.2 %collective-permute-start.6 = (bf16[128,4096]{1,0:T(8,128)(2,1)S(1)}, bf16[128,4096]{1,0:T(8,128)(2,1)S(1)}, u32[]{:S(2)}, u32[]{:S(2)}) collective-permute-start(bf16[128,4096]{1,0:T(8,128)(2,1)S(1)} %join_columns.34.refs_1_.refs_2_), channel_id=1, source_target_pairs={{0,16},{8,24},{16,0},{24,8},{1,17},{9,25},{17,1},{25,9},{2,18},{10... | collective-permute-start | bytes 3145736 | tf_op jit(solution)/shard_map/ppermute | solution.py:24
  41.1 41.1 %collective-permute-start.8 = (bf16[128,2048]{1,0:T(8,128)(2,1)S(1)}, bf16[128,2048]{1,0:T(8,128)(2,1)S(1)}, u32[]{:S(2)}, u32[]{:S(2)}) collective-permute-start(bf16[128,2048]{1,0:T(8,128)(2,1)S(1)} %join_columns.35.refs_0_), channel_id=1, source_target_pairs={{0,3},{1,2},{2,1},{3,0},{4,7},{5,6},{6,5},{7,4},{8,11},{9,10},{10,... | collective-permute-start | bytes 1572872 | tf_op jit(solution)/shard_map/ppermute | solution.py:24
  41.4 66.6 %collective-permute-start.12 = (bf16[128,2048]{1,0:T(8,128)(2,1)S(1)}, bf16[128,2048]{1,0:T(8,128)(2,1)S(1)}, u32[]{:S(2)}, u32[]{:S(2)}) collective-permute-start(bf16[128,2048]{1,0:T(8,128)(2,1)S(1)} %join_columns.36.refs_2_), channel_id=1, source_target_pairs={{0,5},{1,4},{2,7},{3,6},{4,1},{5,0},{6,3},{7,2},{8,13},{9,12},{10,... | collective-permute-start | bytes 1572872 | tf_op jit(solution)/shard_map/ppermute | solution.py:24
  82.2 1.9 copy-start.6
  82.3 24.0 %collective-permute-start.13 = (bf16[128,4096]{1,0:T(8,128)(2,1)S(1)}, bf16[128,4096]{1,0:T(8,128)(2,1)S(1)}, u32[]{:S(2)}, u32[]{:S(2)}) collective-permute-start(bf16[128,4096]{1,0:T(8,128)(2,1)S(1)} %join_columns.37.refs_4_.refs_0_.refs_2_), channel_id=1, source_target_pairs={{0,16},{8,24},{16,0},{24,8},{1,17},{9,25},{17,1},{25,9},{2,18},{10... | collective-permute-start | bytes 3145736 | tf_op jit(solution)/shard_map/ppermute | solution.py:24
  84.1 23.8 %collective-permute-start.15 = (bf16[128,12288]{1,0:T(8,128)(2,1)S(1)}, bf16[128,12288]{1,0:T(8,128)(2,1)S(1)}, u32[]{:S(2)}, u32[]{:S(2)}) collective-permute-start(bf16[128,12288]{1,0:T(8,128)(2,1)S(1)} %join_columns.38.refs_0_), channel_id=1, source_target_pairs={{0,8},{8,0},{16,24},{24,16},{1,9},{9,1},{17,25},{25,17},{2,10},{10... | collective-permute-start | bytes 9437192 | tf_op jit(solution)/shard_map/ppermute | solution.py:24
  84.2 31.7 %collective-permute-start.10 = (bf16[128,2048]{1,0:T(8,128)(2,1)S(1)}, bf16[128,2048]{1,0:T(8,128)(2,1)S(1)}, u32[]{:S(2)}, u32[]{:S(2)}) collective-permute-start(bf16[128,2048]{1,0:T(8,128)(2,1)S(1)} %join_columns.39.refs_1_), channel_id=1, source_target_pairs={{0,6},{1,7},{2,4},{3,5},{4,2},{5,3},{6,0},{7,1},{8,14},{9,15},{10,... | collective-permute-start | bytes 1572872 | tf_op jit(solution)/shard_map/ppermute | solution.py:24
  89.7 26.3 %collective-permute-start.11 = (bf16[128,2048]{1,0:T(8,128)(2,1)S(1)}, bf16[128,2048]{1,0:T(8,128)(2,1)S(1)}, u32[]{:S(2)}, u32[]{:S(2)}) collective-permute-start(bf16[128,2048]{1,0:T(8,128)(2,1)S(1)} %join_columns.40.refs_2_), channel_id=1, source_target_pairs={{0,2},{1,3},{2,0},{3,1},{4,6},{5,7},{6,4},{7,5},{8,10},{9,11},{10,... | collective-permute-start | bytes 1572872 | tf_op jit(solution)/shard_map/ppermute | solution.py:24
  106.3 34.3 %collective-permute-start.20 = (bf16[128,4096]{1,0:T(8,128)(2,1)S(1)}, bf16[128,4096]{1,0:T(8,128)(2,1)S(1)}, u32[]{:S(2)}, u32[]{:S(2)}) collective-permute-start(bf16[128,4096]{1,0:T(8,128)(2,1)S(1)} %join_columns.41.refs_2_), channel_id=1, source_target_pairs={{0,1},{1,0},{2,3},{3,2},{4,5},{5,4},{6,7},{7,6},{8,9},{9,8},{10,11... | collective-permute-start | bytes 3145736 | tf_op jit(solution)/shard_map/ppermute | solution.py:24
  108.1 12.1 %collective-permute-start.16 = (bf16[128,2048]{1,0:T(8,128)(2,1)S(1)}, bf16[128,2048]{1,0:T(8,128)(2,1)S(1)}, u32[]{:S(2)}, u32[]{:S(2)}) collective-permute-start(bf16[128,2048]{1,0:T(8,128)(2,1)S(1)} %join_columns.44.refs_0_.refs_3_), channel_id=1, source_target_pairs={{0,16},{8,24},{16,0},{24,8},{1,17},{9,25},{17,1},{25,9},{2,18},{10... | collective-permute-start | bytes 1572872 | tf_op jit(solution)/shard_map/ppermute | solution.py:24
  109.9 40.6 %collective-permute-start.19 = (bf16[128,1280]{1,0:T(8,128)(2,1)S(1)}, bf16[128,1280]{1,0:T(8,128)(2,1)S(1)}, u32[]{:S(2)}, u32[]{:S(2)}) collective-permute-start(bf16[128,1280]{1,0:T(8,128)(2,1)S(1)} %join_columns.43.refs_1_), channel_id=1, source_target_pairs={{0,7},{1,6},{2,5},{3,4},{4,3},{5,2},{6,1},{7,0},{8,15},{9,14},{10,... | collective-permute-start | bytes 983048 | tf_op jit(solution)/shard_map/ppermute | solution.py:24
  116.0 24.7 %collective-permute-start.21 = (bf16[128,8192]{1,0:T(8,128)(2,1)S(1)}, bf16[128,8192]{1,0:T(8,128)(2,1)S(1)}, u32[]{:S(2)}, u32[]{:S(2)}) collective-permute-start(bf16[128,8192]{1,0:T(8,128)(2,1)S(1)} %join_columns.42.refs_0_), channel_id=1, source_target_pairs={{0,8},{8,0},{16,24},{24,16},{1,9},{9,1},{17,25},{25,17},{2,10},{10... | collective-permute-start | bytes 6291464 | tf_op jit(solution)/shard_map/ppermute | solution.py:24
  116.0 41.8 %collective-permute-start.17 = (bf16[128,768]{1,0:T(8,128)(2,1)S(1)}, bf16[128,768]{1,0:T(8,128)(2,1)S(1)}, u32[]{:S(2)}, u32[]{:S(2)}) collective-permute-start(bf16[128,768]{1,0:T(8,128)(2,1)S(1)} %join_columns.45.refs_1_), channel_id=1, source_target_pairs={{0,7},{1,6},{2,5},{3,4},{4,3},{5,2},{6,1},{7,0},{8,15},{9,14},{10,... | collective-permute-start | bytes 589832 | tf_op jit(solution)/shard_map/ppermute | solution.py:24
  120.2 30.3 %collective-permute-start.18 = (bf16[128,2048]{1,0:T(8,128)(2,1)S(1)}, bf16[128,2048]{1,0:T(8,128)(2,1)S(1)}, u32[]{:S(2)}, u32[]{:S(2)}) collective-permute-start(bf16[128,2048]{1,0:T(8,128)(2,1)S(1)} %join_columns.47.refs_2_.refs_0_.refs_1_), channel_id=1, source_target_pairs={{0,16},{8,24},{16,0},{24,8},{1,17},{9,25},{17,1},{25,9},{2,18},{10... | collective-permute-start | bytes 1572872 | tf_op jit(solution)/shard_map/ppermute | solution.py:24
  122.1 20.2 %copy-start.1 = (bf16[128,4096]{1,0:T(8,128)(2,1)S(1)}, bf16[128,4096]{1,0:T(8,128)(2,1)}, u32[]{:S(2)}) copy-start(bf16[128,4096]{1,0:T(8,128)(2,1)} %copy-done) | copy-start | bytes 3145732
  122.1 20.2 %copy-start.3 = (bf16[128,2048]{1,0:T(8,128)(2,1)S(1)}, bf16[128,2048]{1,0:T(8,128)(2,1)}, u32[]{:S(2)}) copy-start(bf16[128,2048]{1,0:T(8,128)(2,1)} %copy-done.2) | copy-start | bytes 1572868
  122.1 20.2 %copy-start.5 = (bf16[128,2048]{1,0:T(8,128)(2,1)S(1)}, bf16[128,2048]{1,0:T(8,128)(2,1)}, u32[]{:S(2)}) copy-start(bf16[128,2048]{1,0:T(8,128)(2,1)} %copy-done.4) | copy-start | bytes 1572868
  122.1 20.2 %copy-start.7 = (bf16[128,4096]{1,0:T(8,128)(2,1)S(1)}, bf16[128,4096]{1,0:T(8,128)(2,1)}, u32[]{:S(2)}) copy-start(bf16[128,4096]{1,0:T(8,128)(2,1)} %copy-done.6) | copy-start | bytes 3145732
  122.1 20.2 %copy-start.9 = (bf16[128,4096]{1,0:T(8,128)(2,1)S(1)}, bf16[128,4096]{1,0:T(8,128)(2,1)}, u32[]{:S(2)}) copy-start(bf16[128,4096]{1,0:T(8,128)(2,1)} %copy-done.8) | copy-start | bytes 3145732
  140.6 12.0 %collective-permute-start.22 = (bf16[128,4096]{1,0:T(8,128)(2,1)S(1)}, bf16[128,4096]{1,0:T(8,128)(2,1)S(1)}, u32[]{:S(2)}, u32[]{:S(2)}) collective-permute-start(bf16[128,4096]{1,0:T(8,128)(2,1)S(1)} %join_columns.48.refs_0_), channel_id=1, source_target_pairs={{0,8},{8,0},{16,24},{24,16},{1,9},{9,1},{17,25},{25,17},{2,10},{10... | collective-permute-start | bytes 3145736 | tf_op jit(solution)/shard_map/ppermute | solution.py:24
  140.6 21.9 %collective-permute-start.26 = (bf16[128,2048]{1,0:T(8,128)(2,1)S(1)}, bf16[128,2048]{1,0:T(8,128)(2,1)S(1)}, u32[]{:S(2)}, u32[]{:S(2)}) collective-permute-start(bf16[128,2048]{1,0:T(8,128)(2,1)S(1)} %join_columns.46.refs_1_), channel_id=1, source_target_pairs={{0,1},{1,0},{2,3},{3,2},{4,5},{5,4},{6,7},{7,6},{8,9},{9,8},{10,11... | collective-permute-start | bytes 1572872 | tf_op jit(solution)/shard_map/ppermute | solution.py:24
  150.5 10.0 %collective-permute-start.23 = (bf16[128,1280]{1,0:T(8,128)(2,1)S(1)}, bf16[128,1280]{1,0:T(8,128)(2,1)S(1)}, u32[]{:S(2)}, u32[]{:S(2)}) collective-permute-start(bf16[128,1280]{1,0:T(8,128)(2,1)S(1)} %join_columns.49.refs_2_.refs_0_), channel_id=1, source_target_pairs={{0,16},{8,24},{16,0},{24,8},{1,17},{9,25},{17,1},{25,9},{2,18},{10... | collective-permute-start | bytes 983048 | tf_op jit(solution)/shard_map/ppermute | solution.py:24
  152.6 9.8 %collective-permute-start.24 = (bf16[128,4096]{1,0:T(8,128)(2,1)S(1)}, bf16[128,4096]{1,0:T(8,128)(2,1)S(1)}, u32[]{:S(2)}, u32[]{:S(2)}) collective-permute-start(bf16[128,4096]{1,0:T(8,128)(2,1)S(1)} %join_columns.50.refs_0_), channel_id=1, source_target_pairs={{0,8},{8,0},{16,24},{24,16},{1,9},{9,1},{17,25},{25,17},{2,10},{10... | collective-permute-start | bytes 3145736 | tf_op jit(solution)/shard_map/ppermute | solution.py:24
  160.6 11.0 %collective-permute-start.25 = (bf16[128,768]{1,0:T(8,128)(2,1)S(1)}, bf16[128,768]{1,0:T(8,128)(2,1)S(1)}, u32[]{:S(2)}, u32[]{:S(2)}) collective-permute-start(bf16[128,768]{1,0:T(8,128)(2,1)S(1)} %join_columns.51.refs_2_.refs_0_.refs_1_), channel_id=1, source_target_pairs={{0,16},{8,24},{16,0},{24,8},{1,17},{9,25},{17,1},{25,9},{2,18},{10... | collective-permute-start | bytes 589832 | tf_op jit(solution)/shard_map/ppermute | solution.py:24
  162.5 2.2 %collective-permute-start.27 = (bf16[128,2560]{1,0:T(8,128)(2,1)S(1)}, bf16[128,2560]{1,0:T(8,128)(2,1)S(1)}, u32[]{:S(2)}, u32[]{:S(2)}) collective-permute-start(bf16[128,2560]{1,0:T(8,128)(2,1)S(1)} %join_columns.52.refs_0_), channel_id=1, source_target_pairs={{0,8},{8,0},{16,24},{24,16},{1,9},{9,1},{17,25},{25,17},{2,10},{10... | collective-permute-start | bytes 1966088 | tf_op jit(solution)/shard_map/ppermute | solution.py:24
  171.7 1.8 collective-permute-start.28

commit v13 on v12

--- a/solution.py
+++ b/solution.py
@@ -310,7 +310,7 @@
         far_steps.append([block, None] if at % 2 == 0 else [None, block])
     far_steps += [[("wait", None), None], [None, ("wait", None)]]
     near = list(range(1, half))
-    near_steps = [near[:2]] + [[d] for d in near[2:]]
+    near_steps = [near[:2], [], [], []] + [[d] for d in near[2:]]
     relayed = set()
 
     def rides(d):
@@ -408,19 +408,19 @@
                 cots[d] = cots_at(array, own_width)
         near_before.clear()
         arrivals = finish_relays(step)
+        if cross_before is not None:
+            crossed.append(cross_before)
+        earlier = [cross_before[2]] if cross_before is not None else []
+        cross_before = None
         bit = half // 2
         while bit:
             sources = [d for d in sorted(cots) if bit in bits_below(d) and d + bit not in relayed]
             if sources and flying < 4 and step > 0:
                 relayed.update(d + bit for d in sources)
                 parts = [part for d in sources for part in cot_parts(d)]
-                relay_before.append((step + 2, bit, sources, send("tok", bit, parts)[1]))
+                relay_before.append((step + 1, bit, sources, send("tok", bit, parts, earlier)[1]))
                 flying += 1
             bit //= 2
-        if cross_before is not None:
-            crossed.append(cross_before)
-        earlier = [cross_before[2]] if cross_before is not None else []
-        cross_before = None
         if ready:
             blocks = []
             while ready and sum(pieces[i][1] for _, i, _, _ in blocks) < 2 * own_width:

time: 197 us -> 193 us (0.980)
  blocking collectives: 14.8 us -> 10.4 us
  waiting for transfers between devices: 102 us -> 104 us
    all_to_all x1, blocking collectives: 14.8 us -> 10.4 us  [body(): lax.all_to_all(gradients[1][1], ('user', 'tok'), split_axis=0, concat_axi...]
    ppermute x29 -> x31, waiting for transfers between devices: 102 us -> 104 us  [exchange(): return lax.ppermute(block, axis, [(i, i ^ distance) for i in range(size)])]
    ppermute x29 -> x31, starting transfers between devices: 45.1 us -> 44 us  [exchange(): return lax.ppermute(block, axis, [(i, i ^ distance) for i in range(size)])]
    unnamed x24 -> x32, local copies, waits for them, and re-layouts: 3.27 us -> 4.06 us
  transfers between devices with their start and end apart: 29 -> 31, of which waited for: 9 -> 13; matrix products, arithmetic and copies ran while one was open for 0% -> 0% of each run, Pallas kernels for 11% -> 11%
where the time goes in v13:
time: 193 us
  waiting for transfers between devices  104 us (54%)
  starting transfers between devices  44 us (23%)
  Pallas kernels  30 us (16%)
  blocking collectives  10.4 us (5%)
  local copies, waits for them, and re-layouts  4.06 us (2%)
    ppermute x31, waiting for transfers between devices, exchange(): return lax.ppermute(block, axis, [(i, i ^ distance) for i in range(size)])  104 us
    ppermute x31, starting transfers between devices, exchange(): return lax.ppermute(block, axis, [(i, i ^ distance) for i in range(size)])  44 us
    pallas_call x4, Pallas kernels, product(): pl.pallas_call(functools.partial(product_kernel, left_places, right_place...  23.3 us
    all_to_all x1, blocking collectives, body(): lax.all_to_all(gradients[1][1], ('user', 'tok'), split_axis=0, concat_axi...  10.4 us
    pallas_call x1, Pallas kernels, combine(): pl.pallas_call(functools.partial(combine_kernel, user_count, clip_bound,...  4.82 us
    unnamed x32, local copies, waits for them, and re-layouts  4.06 us
  transfers between devices with their start and end apart: 31, of which 13 were waited for; matrix products, arithmetic and copies ran while one was open for 0% of the time, Pallas kernels for 11%

profile of v13, /device:TPU:0, one launch (start us, length us, event | category | flops | bytes accessed | tf_op | source)
XLA Modules:
  0.0 193.2 jit_solution(13229276079654526492)
XLA Ops:
  0.7 1.0 copy-done.15
  1.7 0.5 collective-permute-start
  2.3 2.6 %collective-permute-start.1 = (bf16[128,512]{1,0:T(8,128)(2,1)S(1)}, bf16[128,512]{1,0:T(8,128)(2,1)S(1)}, u32[]{:S(2)}, u32[]{:S(2)}) collective-permute-start(bf16[128,512]{1,0:T(8,128)(2,1)S(1)} %get-tuple-element.25), channel_id=1, source_target_pairs={{0,16},{8,24},{16,0},{24,8},{1,17},{9,25},{17,1},{25,9},{2,18},{10... | collective-permute-start | bytes 393224 | tf_op jit(solution)/shard_map/ppermute | solution.py:24
  4.8 0.1 collective-permute-start.2
  4.9 2.2 %copy-done.12 = bf16[1,128,16384]{2,1,0:T(8,128)(2,1)S(1)} copy-done((bf16[1,128,16384]{2,1,0:T(8,128)(2,1)S(1)}, bf16[1,128,16384]{2,1,0:T(8,128)(2,1)}, u32[]{:S(2)}) %copy-start.12) | copy-done | bytes 4194328
  7.1 0.4 pack_columns.1
  7.5 2.9 %collective-permute-start.7 = (bf16[128,2048]{1,0:T(8,128)(2,1)S(1)}, bf16[128,2048]{1,0:T(8,128)(2,1)S(1)}, u32[]{:S(2)}, u32[]{:S(2)}) collective-permute-start(bf16[128,2048]{1,0:T(8,128)(2,1)S(1)} %join_columns.29.refs_1_), channel_id=1, source_target_pairs={{0,4},{1,5},{2,6},{3,7},{4,0},{5,1},{6,2},{7,3},{8,12},{9,13},{10,... | collective-permute-start | bytes 1572872 | tf_op jit(solution)/shard_map/ppermute | solution.py:24
  10.4 1.6 collective-permute-start.5
  12.0 0.0 collective-permute-done.1.refs_2_
  12.1 0.1 join_columns.33.refs_1_
  12.2 1.6 collective-permute-start.3
  13.8 1.6 collective-permute-start.4
  15.5 2.1 %collective-permute-start.10 = (bf16[128,2048]{1,0:T(8,128)(2,1)S(1)}, bf16[128,2048]{1,0:T(8,128)(2,1)S(1)}, u32[]{:S(2)}, u32[]{:S(2)}) collective-permute-start(bf16[128,2048]{1,0:T(8,128)(2,1)S(1)} %join_columns.32.refs_2_), channel_id=1, source_target_pairs={{0,4},{1,5},{2,6},{3,7},{4,0},{5,1},{6,2},{7,3},{8,12},{9,13},{10,... | collective-permute-start | bytes 1572872 | tf_op jit(solution)/shard_map/ppermute | solution.py:24
  17.6 6.8 %collective-permute-done.5.refs_2_.refs_3_.refs_1_.refs_6_.refs_8_ = bf16[128,2048]{1,0:T(8,128)(2,1)S(1)} collective-permute-done((bf16[128,2048]{1,0:T(8,128)(2,1)S(1)}, bf16[128,2048]{1,0:T(8,128)(2,1)S(1)}, u32[]{:S(2)}, u32[]{:S(2)}) %collective-permute-start.5) | collective-permute-done | bytes 524320 | tf_op jit(solution)/shard_map/ppermute | solution.py:24
  24.5 1.6 collective-permute-start.8
  26.1 13.9 %collective-permute-done.4.refs_1_ = bf16[128,2048]{1,0:T(8,128)(2,1)S(1)} collective-permute-done((bf16[128,2048]{1,0:T(8,128)(2,1)S(1)}, bf16[128,2048]{1,0:T(8,128)(2,1)S(1)}, u32[]{:S(2)}, u32[]{:S(2)}) %collective-permute-start.4) | collective-permute-done | bytes 524320 | tf_op jit(solution)/shard_map/ppermute | solution.py:24
  40.0 0.1 join_columns.36.refs_2_.refs_0_.refs_1_
  40.1 0.0 copy-start
  40.1 1.0 collective-permute-start.6
  41.1 0.1 join_columns.37.refs_0_
  41.2 0.1 collective-permute-start.9
  41.3 1.9 %collective-permute-start.12 = (bf16[128,2048]{1,0:T(8,128)(2,1)S(1)}, bf16[128,2048]{1,0:T(8,128)(2,1)S(1)}, u32[]{:S(2)}, u32[]{:S(2)}) collective-permute-start(bf16[128,2048]{1,0:T(8,128)(2,1)S(1)} %join_columns.38.refs_1_), channel_id=1, source_target_pairs={{0,5},{1,4},{2,7},{3,6},{4,1},{5,0},{6,3},{7,2},{8,13},{9,12},{10,... | collective-permute-start | bytes 1572872 | tf_op jit(solution)/shard_map/ppermute | solution.py:24
  43.3 17.7 %collective-permute-done.8.refs_0_.refs_1_.refs_11_.refs_14_ = bf16[128,2048]{1,0:T(8,128)(2,1)S(1)} collective-permute-done((bf16[128,2048]{1,0:T(8,128)(2,1)S(1)}, bf16[128,2048]{1,0:T(8,128)(2,1)S(1)}, u32[]{:S(2)}, u32[]{:S(2)}) %collective-permute-start.8) | collective-permute-done | bytes 524320 | tf_op jit(solution)/shard_map/ppermute | solution.py:24
  60.9 1.6 collective-permute-done.6.refs_2_.refs_1_.refs_7_.refs_9_
  62.6 0.6 collective-permute-start.16
  63.2 1.8 collective-permute-start.13
  65.1 0.1 join_columns.41.refs_0_
  65.2 0.1 collective-permute-start.15
  65.3 5.2 %collective-permute-start.11 = (bf16[128,2048]{1,0:T(8,128)(2,1)S(1)}, bf16[128,2048]{1,0:T(8,128)(2,1)S(1)}, u32[]{:S(2)}, u32[]{:S(2)}) collective-permute-start(bf16[128,2048]{1,0:T(8,128)(2,1)S(1)} %join_columns.42.refs_1_), channel_id=1, source_target_pairs={{0,6},{1,7},{2,4},{3,5},{4,2},{5,3},{6,0},{7,1},{8,14},{9,15},{10,... | collective-permute-start | bytes 1572872 | tf_op jit(solution)/shard_map/ppermute | solution.py:24
  70.5 3.6 %collective-permute-done.13.refs_2_.refs_1_.refs_8_.refs_10_ = bf16[128,2048]{1,0:T(8,128)(2,1)S(1)} collective-permute-done((bf16[128,2048]{1,0:T(8,128)(2,1)S(1)}, bf16[128,2048]{1,0:T(8,128)(2,1)S(1)}, u32[]{:S(2)}, u32[]{:S(2)}) %collective-permute-start.13) | collective-permute-done | bytes 524320 | tf_op jit(solution)/shard_map/ppermute | solution.py:24
  74.2 2.9 %collective-permute-start.14 = (bf16[128,2048]{1,0:T(8,128)(2,1)S(1)}, bf16[128,2048]{1,0:T(8,128)(2,1)S(1)}, u32[]{:S(2)}, u32[]{:S(2)}) collective-permute-start(bf16[128,2048]{1,0:T(8,128)(2,1)S(1)} %join_columns.43.refs_1_), channel_id=1, source_target_pairs={{0,2},{1,3},{2,0},{3,1},{4,6},{5,7},{6,4},{7,5},{8,10},{9,11},{10,... | collective-permute-start | bytes 1572872 | tf_op jit(solution)/shard_map/ppermute | solution.py:24
  77.1 0.4 collective-permute-start.18
  77.5 0.1 join_columns.45.refs_0_
  77.6 0.8 copy-done.13
  78.4 13.7 %collective-permute-done.12.refs_2_.refs_0_ = bf16[128,2048]{1,0:T(8,128)(2,1)S(1)} collective-permute-done((bf16[128,2048]{1,0:T(8,128)(2,1)S(1)}, bf16[128,2048]{1,0:T(8,128)(2,1)S(1)}, u32[]{:S(2)}, u32[]{:S(2)}) %collective-permute-start.12) | collective-permute-done | bytes 524320 | tf_op jit(solution)/shard_map/ppermute | solution.py:24
  92.1 3.0 %collective-permute-start.22 = (bf16[128,1280]{1,0:T(8,128)(2,1)S(1)}, bf16[128,1280]{1,0:T(8,128)(2,1)S(1)}, u32[]{:S(2)}, u32[]{:S(2)}) collective-permute-start(bf16[128,1280]{1,0:T(8,128)(2,1)S(1)} %join_columns.46.refs_1_), channel_id=1, source_target_pairs={{0,7},{1,6},{2,5},{3,4},{4,3},{5,2},{6,1},{7,0},{8,15},{9,14},{10,... | collective-permute-start | bytes 983048 | tf_op jit(solution)/shard_map/ppermute | solution.py:24
  95.1 13.5 %collective-permute-done.14.refs_0_.refs_1_.refs_11_.refs_7_ = bf16[128,2048]{1,0:T(8,128)(2,1)S(1)} collective-permute-done((bf16[128,2048]{1,0:T(8,128)(2,1)S(1)}, bf16[128,2048]{1,0:T(8,128)(2,1)S(1)}, u32[]{:S(2)}, u32[]{:S(2)}) %collective-permute-start.14) | collective-permute-done | bytes 524320 | tf_op jit(solution)/shard_map/ppermute | solution.py:24
  108.7 1.6 collective-permute-start.23
  110.4 1.6 collective-permute-start.19
  112.0 0.1 collective-permute-start.17
  112.1 0.1 collective-permute-start.24
  112.2 14.2 %collective-permute-done.17.refs_1_ = bf16[128,2048]{1,0:T(8,128)(2,1)S(1)} collective-permute-done((bf16[128,2048]{1,0:T(8,128)(2,1)S(1)}, bf16[128,2048]{1,0:T(8,128)(2,1)S(1)}, u32[]{:S(2)}, u32[]{:S(2)}) %collective-permute-start.17) | collective-permute-done | bytes 524320 | tf_op jit(solution)/shard_map/ppermute | solution.py:24
  126.3 3.4 %collective-permute-start.20 = (bf16[128,768]{1,0:T(8,128)(2,1)S(1)}, bf16[128,768]{1,0:T(8,128)(2,1)S(1)}, u32[]{:S(2)}, u32[]{:S(2)}) collective-permute-start(bf16[128,768]{1,0:T(8,128)(2,1)S(1)} %join_columns.50.refs_2_), channel_id=1, source_target_pairs={{0,7},{1,6},{2,5},{3,4},{4,3},{5,2},{6,1},{7,0},{8,15},{9,14},{10,... | collective-permute-start | bytes 589832 | tf_op jit(solution)/shard_map/ppermute | solution.py:24
  129.8 0.1 join_columns.51.refs_2_.refs_0_
  129.8 1.9 %collective-permute-start.21 = (bf16[128,4096]{1,0:T(8,128)(2,1)S(1)}, bf16[128,4096]{1,0:T(8,128)(2,1)S(1)}, u32[]{:S(2)}, u32[]{:S(2)}) collective-permute-start(bf16[128,4096]{1,0:T(8,128)(2,1)S(1)} %join_columns.51.refs_2_.refs_0_), channel_id=1, source_target_pairs={{0,16},{8,24},{16,0},{24,8},{1,17},{9,25},{17,1},{25,9},{2,18},{10... | collective-permute-start | bytes 3145736 | tf_op jit(solution)/shard_map/ppermute | solution.py:24
  131.8 0.1 join_columns.52.refs_0_
  131.8 0.0 copy-start.1
  131.9 6.1 %collective-permute-done.23.refs_1_.refs_12_.refs_8_ = bf16[128,2048]{1,0:T(8,128)(2,1)S(1)} collective-permute-done((bf16[128,2048]{1,0:T(8,128)(2,1)S(1)}, bf16[128,2048]{1,0:T(8,128)(2,1)S(1)}, u32[]{:S(2)}, u32[]{:S(2)}) %collective-permute-start.23) | collective-permute-done | bytes 524320 | tf_op jit(solution)/shard_map/ppermute | solution.py:24
  138.1 6.8 %product_and_squares.4.refs_2_.refs_13_ = f32[4,1280,512]{2,1,0:T(8,128)S(1)} custom-call(bf16[128,2048]{1,0:T(8,128)(2,1)S(1)} %copy-done.7, bf16[128,4096]{1,0:T(8,128)(2,1)S(1)} %copy-done.1, bf16[128,2048]{1,0:T(8,128)(2,1)S(1)} %join_columns.40.refs_2_.refs_0_, bf16[128,4096]{1,0:T(8,128)(2,1)S(1)} %collective-permute-done.9.refs_3_.refs_4_, ...), custom_call_target="tpu_custom_call" | custom-call | flops 2684354560 | bytes 7340032 | tf_op jit(solution)/shard_map/product_and_squares/pallas_call | solution.py:194
  144.9 8.5 %collective-permute-done.21.refs_3_.refs_1_.refs_6_.refs_4_ = bf16[128,4096]{1,0:T(8,128)(2,1)S(1)} collective-permute-done((bf16[128,4096]{1,0:T(8,128)(2,1)S(1)}, bf16[128,4096]{1,0:T(8,128)(2,1)S(1)}, u32[]{:S(2)}, u32[]{:S(2)}) %collective-permute-start.21) | collective-permute-done | bytes 1048608 | tf_op jit(solution)/shard_map/ppermute | solution.py:24
  153.4 1.7 collective-permute-start.26
  155.1 0.1 join_columns.54.refs_0_
  155.2 0.1 collective-permute-start.27
  155.3 5.0 %product_and_squares.5.refs_2_.refs_9_ = f32[4,768,512]{2,1,0:T(8,128)S(1)} custom-call(bf16[128,2048]{1,0:T(8,128)(2,1)S(1)} %copy-done.7, bf16[128,4096]{1,0:T(8,128)(2,1)S(1)} %copy-done.1, bf16[128,2048]{1,0:T(8,128)(2,1)S(1)} %join_columns.40.refs_2_.refs_0_, bf16[128,2048]{1,0:T(8,128)(2,1)S(1)} %join_columns.48.refs_1_.refs_0_.refs_3_, ...), custom_call_target="tpu_custom_call" | custom-call | flops 2013265920 | bytes 6553600 | tf_op jit(solution)/shard_map/product_and_squares/pallas_call | solution.py:194
  160.3 0.2 collective-permute-done.26.refs_3_.refs_1_.refs_8_
  160.5 1.7 collective-permute-start.28
  162.3 0.1 collective-permute-start.29
  162.4 2.1 %collective-permute-done.29.refs_5_ = bf16[128,2560]{1,0:T(8,128)(2,1)S(1)} collective-permute-done((bf16[128,2560]{1,0:T(8,128)(2,1)S(1)}, bf16[128,2560]{1,0:T(8,128)(2,1)S(1)}, u32[]{:S(2)}, u32[]{:S(2)}) %collective-permute-start.29) | collective-permute-done | bytes 655392 | tf_op jit(solution)/shard_map/ppermute | solution.py:24
  164.5 7.3 %product_and_squares.6 = (f32[4,1280,512]{2,1,0:T(8,128)S(1)}, f32[1,8,128]{2,1,0:T(8,128)S(1)}) custom-call(bf16[128,4096]{1,0:T(8,128)(2,1)S(1)} %join_columns.51.refs_2_.refs_0_, bf16[128,2048]{1,0:T(8,128)(2,1)S(1)} %join_columns.48.refs_1_.refs_0_.refs_3_, bf16[128,1280]{1,0:T(8,128)(2,1)S(1)} %join_columns.53.refs_2_.refs_0_, ...), custom_call_target="tpu_custom_call", output_to_operand_aliasing={{0}: (13, {})} | custom-call | flops 2684354560 | bytes 7340032 | tf_op jit(solution)/shard_map/product_and_squares/pallas_call | solution.py:194
  171.8 0.2 collective-permute-start.30
  172.0 1.6 collective-permute-done.30.refs_3_
  173.6 4.3 %product_and_squares.7 = (f32[4,768,512]{2,1,0:T(8,128)S(1)}, f32[32,8,128]{2,1,0:T(8,128)S(1)}) custom-call(bf16[128,4096]{1,0:T(8,128)(2,1)S(1)} %join_columns.51.refs_2_.refs_0_, bf16[128,768]{1,0:T(8,128)(2,1)S(1)} %join_columns.55.refs_2_.refs_0_.refs_1_, ...), custom_call_target="tpu_custom_call", output_to_operand_aliasing={{0}: (9, {})} | custom-call | flops 1207959552 | bytes 3932160 | tf_op jit(solution)/shard_map/product_and_squares/pallas_call | solution.py:194
  178.0 10.4 %all_to_all.5.sums_ref = f32[32,8,128]{2,1,0:T(8,128)S(1)} all-to-all(f32[32,8,128]{2,1,0:T(8,128)S(1)} %get-tuple-element.35), channel_id=1, replica_groups=mesh['user'=4,'tok'=8] {'user','tok'}, dimensions={0} | all-to-all | bytes 262144 | tf_op jit(solution)/shard_map/all_to_all | solution.py:467
  188.4 4.8 %weighted_sum.1 = f32[2048,512]{1,0:T(8,128)} custom-call(s32[1]{0:T(128)} %bitcast.user_ref, f32[32,8,128]{2,1,0:T(8,128)S(1)} %all_to_all.5.sums_ref, f32[4,1280,512]{2,1,0:T(8,128)S(1)} %get-tuple-element.33.refs_3_.refs_0_, f32[4,768,512]{2,1,0:T(8,128)S(1)} %get-tuple-element.36.refs_1_), custom_call_target="tpu_custom_call" | custom-call | tf_op jit(solution)/shard_map/weighted_sum/pallas_call | solution.py:251
  (75 shorter events, 0.9 us)
Async XLA Ops:
  0.7 1.0 copy-start.15
  1.7 10.3 %collective-permute-start = (bf16[128,512]{1,0:T(8,128)(2,1)S(1)}, bf16[128,512]{1,0:T(8,128)(2,1)S(1)}, u32[]{:S(2)}, u32[]{:S(2)}) collective-permute-start(bf16[128,512]{1,0:T(8,128)(2,1)S(1)} %get-tuple-element.24), channel_id=1, source_target_pairs={{0,8},{8,0},{16,24},{24,16},{1,9},{9,1},{17,25},{25,17},{2,10},{10... | collective-permute-start | bytes 393224 | tf_op jit(solution)/shard_map/ppermute | solution.py:24
  2.3 9.7 %collective-permute-start.1 = (bf16[128,512]{1,0:T(8,128)(2,1)S(1)}, bf16[128,512]{1,0:T(8,128)(2,1)S(1)}, u32[]{:S(2)}, u32[]{:S(2)}) collective-permute-start(bf16[128,512]{1,0:T(8,128)(2,1)S(1)} %get-tuple-element.25), channel_id=1, source_target_pairs={{0,16},{8,24},{16,0},{24,8},{1,17},{9,25},{17,1},{25,9},{2,18},{10... | collective-permute-start | bytes 393224 | tf_op jit(solution)/shard_map/ppermute | solution.py:24
  4.8 7.2 %collective-permute-start.2 = (bf16[128,512]{1,0:T(8,128)(2,1)S(1)}, bf16[128,512]{1,0:T(8,128)(2,1)S(1)}, u32[]{:S(2)}, u32[]{:S(2)}) collective-permute-start(bf16[128,512]{1,0:T(8,128)(2,1)S(1)} %get-tuple-element.26), channel_id=1, source_target_pairs={{0,24},{8,16},{16,8},{24,0},{1,25},{9,17},{17,9},{25,1},{2,26},{10... | collective-permute-start | bytes 393224 | tf_op jit(solution)/shard_map/ppermute | solution.py:24
  4.9 2.2 %copy-start.12 = (bf16[1,128,16384]{2,1,0:T(8,128)(2,1)S(1)}, bf16[1,128,16384]{2,1,0:T(8,128)(2,1)}, u32[]{:S(2)}) copy-start(bf16[1,128,16384]{2,1,0:T(8,128)(2,1)} %hidden_ref.1) | copy-start | bytes 12582916
  7.5 33.8 %collective-permute-start.7 = (bf16[128,2048]{1,0:T(8,128)(2,1)S(1)}, bf16[128,2048]{1,0:T(8,128)(2,1)S(1)}, u32[]{:S(2)}, u32[]{:S(2)}) collective-permute-start(bf16[128,2048]{1,0:T(8,128)(2,1)S(1)} %join_columns.29.refs_1_), channel_id=1, source_target_pairs={{0,4},{1,5},{2,6},{3,7},{4,0},{5,1},{6,2},{7,3},{8,12},{9,13},{10,... | collective-permute-start | bytes 1572872 | tf_op jit(solution)/shard_map/ppermute | solution.py:24
  10.4 30.6 %copy-start.6 = (bf16[128,2048]{1,0:T(8,128)(2,1)}, bf16[128,2048]{1,0:T(8,128)(2,1)S(1)}, u32[]{:S(2)}) copy-start(bf16[128,2048]{1,0:T(8,128)(2,1)S(1)} %join_columns.30.refs_4_.refs_1_.refs_0_) | copy-start | bytes 1572868
  10.4 14.0 %collective-permute-start.5 = (bf16[128,2048]{1,0:T(8,128)(2,1)S(1)}, bf16[128,2048]{1,0:T(8,128)(2,1)S(1)}, u32[]{:S(2)}, u32[]{:S(2)}) collective-permute-start(bf16[128,2048]{1,0:T(8,128)(2,1)S(1)} %join_columns.30.refs_4_.refs_1_.refs_0_), channel_id=1, source_target_pairs={{0,16},{8,24},{16,0},{24,8},{1,17},{9,25},{17,1},{25,9},{2,18},{10... | collective-permute-start | bytes 1572872 | tf_op jit(solution)/shard_map/ppermute | solution.py:24
  12.1 12.3 %copy-start.4 = (bf16[128,2048]{1,0:T(8,128)(2,1)}, bf16[128,2048]{1,0:T(8,128)(2,1)S(1)}, u32[]{:S(2)}) copy-start(bf16[128,2048]{1,0:T(8,128)(2,1)S(1)} %join_columns.31.refs_0_.refs_1_.refs_9_.refs_12_) | copy-start | bytes 1572868
  12.2 27.8 %collective-permute-start.3 = (bf16[128,4096]{1,0:T(8,128)(2,1)S(1)}, bf16[128,4096]{1,0:T(8,128)(2,1)S(1)}, u32[]{:S(2)}, u32[]{:S(2)}) collective-permute-start(bf16[128,4096]{1,0:T(8,128)(2,1)S(1)} %join_columns.33.refs_1_), channel_id=1, source_target_pairs={{0,1},{1,0},{2,3},{3,2},{4,5},{5,4},{6,7},{7,6},{8,9},{9,8},{10,11... | collective-permute-start | bytes 3145736 | tf_op jit(solution)/shard_map/ppermute | solution.py:24
  13.8 26.2 %collective-permute-start.4 = (bf16[128,2048]{1,0:T(8,128)(2,1)S(1)}, bf16[128,2048]{1,0:T(8,128)(2,1)S(1)}, u32[]{:S(2)}, u32[]{:S(2)}) collective-permute-start(bf16[128,2048]{1,0:T(8,128)(2,1)S(1)} %join_columns.34.refs_0_), channel_id=1, source_target_pairs={{0,2},{1,3},{2,0},{3,1},{4,6},{5,7},{6,4},{7,5},{8,10},{9,11},{10,... | collective-permute-start | bytes 1572872 | tf_op jit(solution)/shard_map/ppermute | solution.py:24
  15.5 49.8 %collective-permute-start.10 = (bf16[128,2048]{1,0:T(8,128)(2,1)S(1)}, bf16[128,2048]{1,0:T(8,128)(2,1)S(1)}, u32[]{:S(2)}, u32[]{:S(2)}) collective-permute-start(bf16[128,2048]{1,0:T(8,128)(2,1)S(1)} %join_columns.32.refs_2_), channel_id=1, source_target_pairs={{0,4},{1,5},{2,6},{3,7},{4,0},{5,1},{6,2},{7,3},{8,12},{9,13},{10,... | collective-permute-start | bytes 1572872 | tf_op jit(solution)/shard_map/ppermute | solution.py:24
  24.4 16.7 %copy-start.8 = (bf16[128,2048]{1,0:T(8,128)(2,1)}, bf16[128,2048]{1,0:T(8,128)(2,1)S(1)}, u32[]{:S(2)}) copy-start(bf16[128,2048]{1,0:T(8,128)(2,1)S(1)} %collective-permute-done.5.refs_2_.refs_3_.refs_1_.refs_6_.refs_8_) | copy-start | bytes 1572868
  24.5 36.5 %collective-permute-start.8 = (bf16[128,2048]{1,0:T(8,128)(2,1)S(1)}, bf16[128,2048]{1,0:T(8,128)(2,1)S(1)}, u32[]{:S(2)}, u32[]{:S(2)}) collective-permute-start(bf16[128,2048]{1,0:T(8,128)(2,1)S(1)} %join_columns.35.refs_2_), channel_id=1, source_target_pairs={{0,2},{1,3},{2,0},{3,1},{4,6},{5,7},{6,4},{7,5},{8,10},{9,11},{10,... | collective-permute-start | bytes 1572872 | tf_op jit(solution)/shard_map/ppermute | solution.py:24
  40.0 1.3 copy-start.10
  40.1 25.0 %copy-start = (bf16[128,4096]{1,0:T(8,128)(2,1)}, bf16[128,4096]{1,0:T(8,128)(2,1)S(1)}, u32[]{:S(2)}) copy-start(bf16[128,4096]{1,0:T(8,128)(2,1)S(1)} %join_columns.36.refs_2_.refs_0_.refs_1_) | copy-start | bytes 3145732
  40.1 22.5 %collective-permute-start.6 = (bf16[128,4096]{1,0:T(8,128)(2,1)S(1)}, bf16[128,4096]{1,0:T(8,128)(2,1)S(1)}, u32[]{:S(2)}, u32[]{:S(2)}) collective-permute-start(bf16[128,4096]{1,0:T(8,128)(2,1)S(1)} %join_columns.36.refs_2_.refs_0_.refs_1_), channel_id=1, source_target_pairs={{0,16},{8,24},{16,0},{24,8},{1,17},{9,25},{17,1},{25,9},{2,18},{10... | collective-permute-start | bytes 3145736 | tf_op jit(solution)/shard_map/ppermute | solution.py:24
  41.2 23.9 %collective-permute-start.9 = (bf16[128,4096]{1,0:T(8,128)(2,1)S(1)}, bf16[128,4096]{1,0:T(8,128)(2,1)S(1)}, u32[]{:S(2)}, u32[]{:S(2)}) collective-permute-start(bf16[128,4096]{1,0:T(8,128)(2,1)S(1)} %join_columns.37.refs_0_), channel_id=1, source_target_pairs={{0,8},{8,0},{16,24},{24,16},{1,9},{9,1},{17,25},{25,17},{2,10},{10... | collective-permute-start | bytes 3145736 | tf_op jit(solution)/shard_map/ppermute | solution.py:24
  41.3 50.7 %collective-permute-start.12 = (bf16[128,2048]{1,0:T(8,128)(2,1)S(1)}, bf16[128,2048]{1,0:T(8,128)(2,1)S(1)}, u32[]{:S(2)}, u32[]{:S(2)}) collective-permute-start(bf16[128,2048]{1,0:T(8,128)(2,1)S(1)} %join_columns.38.refs_1_), channel_id=1, source_target_pairs={{0,5},{1,4},{2,7},{3,6},{4,1},{5,0},{6,3},{7,2},{8,13},{9,12},{10,... | collective-permute-start | bytes 1572872 | tf_op jit(solution)/shard_map/ppermute | solution.py:24
  62.6 2.6 %copy-start.2 = (bf16[128,4096]{1,0:T(8,128)(2,1)}, bf16[128,4096]{1,0:T(8,128)(2,1)S(1)}, u32[]{:S(2)}) copy-start(bf16[128,4096]{1,0:T(8,128)(2,1)S(1)} %collective-permute-done.6.refs_2_.refs_1_.refs_7_.refs_9_) | copy-start | bytes 3145732
  62.6 14.9 %collective-permute-start.16 = (bf16[128,2048]{1,0:T(8,128)(2,1)S(1)}, bf16[128,2048]{1,0:T(8,128)(2,1)S(1)}, u32[]{:S(2)}, u32[]{:S(2)}) collective-permute-start(bf16[128,2048]{1,0:T(8,128)(2,1)S(1)} %join_columns.39.refs_1_), channel_id=1, source_target_pairs={{0,1},{1,0},{2,3},{3,2},{4,5},{5,4},{6,7},{7,6},{8,9},{9,8},{10,11... | collective-permute-start | bytes 1572872 | tf_op jit(solution)/shard_map/ppermute | solution.py:24
  63.2 10.9 %collective-permute-start.13 = (bf16[128,2048]{1,0:T(8,128)(2,1)S(1)}, bf16[128,2048]{1,0:T(8,128)(2,1)S(1)}, u32[]{:S(2)}, u32[]{:S(2)}) collective-permute-start(bf16[128,2048]{1,0:T(8,128)(2,1)S(1)} %join_columns.40.refs_2_.refs_0_), channel_id=1, source_target_pairs={{0,16},{8,24},{16,0},{24,8},{1,17},{9,25},{17,1},{25,9},{2,18},{10... | collective-permute-start | bytes 1572872 | tf_op jit(solution)/shard_map/ppermute | solution.py:24
  65.2 11.9 %collective-permute-start.15 = (bf16[128,8192]{1,0:T(8,128)(2,1)S(1)}, bf16[128,8192]{1,0:T(8,128)(2,1)S(1)}, u32[]{:S(2)}, u32[]{:S(2)}) collective-permute-start(bf16[128,8192]{1,0:T(8,128)(2,1)S(1)} %join_columns.41.refs_0_), channel_id=1, source_target_pairs={{0,8},{8,0},{16,24},{24,16},{1,9},{9,1},{17,25},{25,17},{2,10},{10... | collective-permute-start | bytes 6291464 | tf_op jit(solution)/shard_map/ppermute | solution.py:24
  65.3 46.7 %collective-permute-start.11 = (bf16[128,2048]{1,0:T(8,128)(2,1)S(1)}, bf16[128,2048]{1,0:T(8,128)(2,1)S(1)}, u32[]{:S(2)}, u32[]{:S(2)}) collective-permute-start(bf16[128,2048]{1,0:T(8,128)(2,1)S(1)} %join_columns.42.refs_1_), channel_id=1, source_target_pairs={{0,6},{1,7},{2,4},{3,5},{4,2},{5,3},{6,0},{7,1},{8,14},{9,15},{10,... | collective-permute-start | bytes 1572872 | tf_op jit(solution)/shard_map/ppermute | solution.py:24
  74.2 34.5 %collective-permute-start.14 = (bf16[128,2048]{1,0:T(8,128)(2,1)S(1)}, bf16[128,2048]{1,0:T(8,128)(2,1)S(1)}, u32[]{:S(2)}, u32[]{:S(2)}) collective-permute-start(bf16[128,2048]{1,0:T(8,128)(2,1)S(1)} %join_columns.43.refs_1_), channel_id=1, source_target_pairs={{0,2},{1,3},{2,0},{3,1},{4,6},{5,7},{6,4},{7,5},{8,10},{9,11},{10,... | collective-permute-start | bytes 1572872 | tf_op jit(solution)/shard_map/ppermute | solution.py:24
  77.1 34.8 %collective-permute-start.18 = (bf16[128,2048]{1,0:T(8,128)(2,1)S(1)}, bf16[128,2048]{1,0:T(8,128)(2,1)S(1)}, u32[]{:S(2)}, u32[]{:S(2)}) collective-permute-start(bf16[128,2048]{1,0:T(8,128)(2,1)S(1)} %join_columns.44.refs_2_), channel_id=1, source_target_pairs={{0,1},{1,0},{2,3},{3,2},{4,5},{5,4},{6,7},{7,6},{8,9},{9,8},{10,11... | collective-permute-start | bytes 1572872 | tf_op jit(solution)/shard_map/ppermute | solution.py:24
  77.6 0.8 copy-start.13
  92.1 52.8 %collective-permute-start.22 = (bf16[128,1280]{1,0:T(8,128)(2,1)S(1)}, bf16[128,1280]{1,0:T(8,128)(2,1)S(1)}, u32[]{:S(2)}, u32[]{:S(2)}) collective-permute-start(bf16[128,1280]{1,0:T(8,128)(2,1)S(1)} %join_columns.46.refs_1_), channel_id=1, source_target_pairs={{0,7},{1,6},{2,5},{3,4},{4,3},{5,2},{6,1},{7,0},{8,15},{9,14},{10,... | collective-permute-start | bytes 983048 | tf_op jit(solution)/shard_map/ppermute | solution.py:24
  108.7 29.4 %collective-permute-start.23 = (bf16[128,2048]{1,0:T(8,128)(2,1)S(1)}, bf16[128,2048]{1,0:T(8,128)(2,1)S(1)}, u32[]{:S(2)}, u32[]{:S(2)}) collective-permute-start(bf16[128,2048]{1,0:T(8,128)(2,1)S(1)} %join_columns.47.refs_1_), channel_id=1, source_target_pairs={{0,1},{1,0},{2,3},{3,2},{4,5},{5,4},{6,7},{7,6},{8,9},{9,8},{10,11... | collective-permute-start | bytes 1572872 | tf_op jit(solution)/shard_map/ppermute | solution.py:24
  110.4 19.4 %collective-permute-start.19 = (bf16[128,2048]{1,0:T(8,128)(2,1)S(1)}, bf16[128,2048]{1,0:T(8,128)(2,1)S(1)}, u32[]{:S(2)}, u32[]{:S(2)}) collective-permute-start(bf16[128,2048]{1,0:T(8,128)(2,1)S(1)} %join_columns.48.refs_1_.refs_0_.refs_3_), channel_id=1, source_target_pairs={{0,16},{8,24},{16,0},{24,8},{1,17},{9,25},{17,1},{25,9},{2,18},{10... | collective-permute-start | bytes 1572872 | tf_op jit(solution)/shard_map/ppermute | solution.py:24
  112.0 14.4 %collective-permute-start.17 = (bf16[128,2048]{1,0:T(8,128)(2,1)S(1)}, bf16[128,2048]{1,0:T(8,128)(2,1)S(1)}, u32[]{:S(2)}, u32[]{:S(2)}) collective-permute-start(bf16[128,2048]{1,0:T(8,128)(2,1)S(1)} %join_columns.49.refs_0_), channel_id=1, source_target_pairs={{0,3},{1,2},{2,1},{3,0},{4,7},{5,6},{6,5},{7,4},{8,11},{9,10},{10,... | collective-permute-start | bytes 1572872 | tf_op jit(solution)/shard_map/ppermute | solution.py:24
  112.1 26.0 %collective-permute-start.24 = (bf16[128,4096]{1,0:T(8,128)(2,1)S(1)}, bf16[128,4096]{1,0:T(8,128)(2,1)S(1)}, u32[]{:S(2)}, u32[]{:S(2)}) collective-permute-start(bf16[128,4096]{1,0:T(8,128)(2,1)S(1)} %join_columns.45.refs_0_), channel_id=1, source_target_pairs={{0,8},{8,0},{16,24},{24,16},{1,9},{9,1},{17,25},{25,17},{2,10},{10... | collective-permute-start | bytes 3145736 | tf_op jit(solution)/shard_map/ppermute | solution.py:24
  126.3 34.0 %collective-permute-start.20 = (bf16[128,768]{1,0:T(8,128)(2,1)S(1)}, bf16[128,768]{1,0:T(8,128)(2,1)S(1)}, u32[]{:S(2)}, u32[]{:S(2)}) collective-permute-start(bf16[128,768]{1,0:T(8,128)(2,1)S(1)} %join_columns.50.refs_2_), channel_id=1, source_target_pairs={{0,7},{1,6},{2,5},{3,4},{4,3},{5,2},{6,1},{7,0},{8,15},{9,14},{10,... | collective-permute-start | bytes 589832 | tf_op jit(solution)/shard_map/ppermute | solution.py:24
  129.8 23.5 %collective-permute-start.21 = (bf16[128,4096]{1,0:T(8,128)(2,1)S(1)}, bf16[128,4096]{1,0:T(8,128)(2,1)S(1)}, u32[]{:S(2)}, u32[]{:S(2)}) collective-permute-start(bf16[128,4096]{1,0:T(8,128)(2,1)S(1)} %join_columns.51.refs_2_.refs_0_), channel_id=1, source_target_pairs={{0,16},{8,24},{16,0},{24,8},{1,17},{9,25},{17,1},{25,9},{2,18},{10... | collective-permute-start | bytes 3145736 | tf_op jit(solution)/shard_map/ppermute | solution.py:24
  131.8 6.2 %copy-start.1 = (bf16[128,4096]{1,0:T(8,128)(2,1)S(1)}, bf16[128,4096]{1,0:T(8,128)(2,1)}, u32[]{:S(2)}) copy-start(bf16[128,4096]{1,0:T(8,128)(2,1)} %copy-done) | copy-start | bytes 3145732
  131.9 6.2 %copy-start.3 = (bf16[128,4096]{1,0:T(8,128)(2,1)S(1)}, bf16[128,4096]{1,0:T(8,128)(2,1)}, u32[]{:S(2)}) copy-start(bf16[128,4096]{1,0:T(8,128)(2,1)} %copy-done.2) | copy-start | bytes 3145732
  131.9 6.2 %copy-start.5 = (bf16[128,2048]{1,0:T(8,128)(2,1)S(1)}, bf16[128,2048]{1,0:T(8,128)(2,1)}, u32[]{:S(2)}) copy-start(bf16[128,2048]{1,0:T(8,128)(2,1)} %copy-done.4) | copy-start | bytes 1572868
  131.9 6.2 %copy-start.7 = (bf16[128,2048]{1,0:T(8,128)(2,1)S(1)}, bf16[128,2048]{1,0:T(8,128)(2,1)}, u32[]{:S(2)}) copy-start(bf16[128,2048]{1,0:T(8,128)(2,1)} %copy-done.6) | copy-start | bytes 1572868
  131.9 6.2 %copy-start.9 = (bf16[128,2048]{1,0:T(8,128)(2,1)S(1)}, bf16[128,2048]{1,0:T(8,128)(2,1)}, u32[]{:S(2)}) copy-start(bf16[128,2048]{1,0:T(8,128)(2,1)} %copy-done.8) | copy-start | bytes 1572868
  131.9 6.2 %copy-start.11 = (bf16[128,4096]{1,0:T(8,128)(2,1)S(1)}, bf16[128,4096]{1,0:T(8,128)(2,1)}, u32[]{:S(2)}) copy-start(bf16[128,4096]{1,0:T(8,128)(2,1)} %copy-done.10) | copy-start | bytes 3145732
  138.0 17.1 %collective-permute-start.25 = (bf16[128,4096]{1,0:T(8,128)(2,1)S(1)}, bf16[128,4096]{1,0:T(8,128)(2,1)S(1)}, u32[]{:S(2)}, u32[]{:S(2)}) collective-permute-start(bf16[128,4096]{1,0:T(8,128)(2,1)S(1)} %join_columns.52.refs_0_), channel_id=1, source_target_pairs={{0,8},{8,0},{16,24},{24,16},{1,9},{9,1},{17,25},{25,17},{2,10},{10... | collective-permute-start | bytes 3145736 | tf_op jit(solution)/shard_map/ppermute | solution.py:24
  153.4 7.1 %collective-permute-start.26 = (bf16[128,1280]{1,0:T(8,128)(2,1)S(1)}, bf16[128,1280]{1,0:T(8,128)(2,1)S(1)}, u32[]{:S(2)}, u32[]{:S(2)}) collective-permute-start(bf16[128,1280]{1,0:T(8,128)(2,1)S(1)} %join_columns.53.refs_2_.refs_0_), channel_id=1, source_target_pairs={{0,16},{8,24},{16,0},{24,8},{1,17},{9,25},{17,1},{25,9},{2,18},{10... | collective-permute-start | bytes 983048 | tf_op jit(solution)/shard_map/ppermute | solution.py:24
  155.2 7.0 %collective-permute-start.27 = (bf16[128,8192]{1,0:T(8,128)(2,1)S(1)}, bf16[128,8192]{1,0:T(8,128)(2,1)S(1)}, u32[]{:S(2)}, u32[]{:S(2)}) collective-permute-start(bf16[128,8192]{1,0:T(8,128)(2,1)S(1)} %join_columns.54.refs_0_), channel_id=1, source_target_pairs={{0,8},{8,0},{16,24},{24,16},{1,9},{9,1},{17,25},{25,17},{2,10},{10... | collective-permute-start | bytes 6291464 | tf_op jit(solution)/shard_map/ppermute | solution.py:24
  160.5 11.3 %collective-permute-start.28 = (bf16[128,768]{1,0:T(8,128)(2,1)S(1)}, bf16[128,768]{1,0:T(8,128)(2,1)S(1)}, u32[]{:S(2)}, u32[]{:S(2)}) collective-permute-start(bf16[128,768]{1,0:T(8,128)(2,1)S(1)} %join_columns.55.refs_2_.refs_0_.refs_1_), channel_id=1, source_target_pairs={{0,16},{8,24},{16,0},{24,8},{1,17},{9,25},{17,1},{25,9},{2,18},{10... | collective-permute-start | bytes 589832 | tf_op jit(solution)/shard_map/ppermute | solution.py:24
  162.3 2.2 %copy-start.14 = (bf16[128,2048]{1,0:T(8,128)(2,1)S(1)}, bf16[128,2048]{1,0:T(8,128)(2,1)}, u32[]{:S(2)}) copy-start(bf16[128,2048]{1,0:T(8,128)(2,1)} %copy-done.13) | copy-start | bytes 1572868
  162.3 2.2 %collective-permute-start.29 = (bf16[128,2560]{1,0:T(8,128)(2,1)S(1)}, bf16[128,2560]{1,0:T(8,128)(2,1)S(1)}, u32[]{:S(2)}, u32[]{:S(2)}) collective-permute-start(bf16[128,2560]{1,0:T(8,128)(2,1)S(1)} %join_columns.56.refs_0_), channel_id=1, source_target_pairs={{0,8},{8,0},{16,24},{24,16},{1,9},{9,1},{17,25},{25,17},{2,10},{10... | collective-permute-start | bytes 1966088 | tf_op jit(solution)/shard_map/ppermute | solution.py:24
  171.8 1.8 collective-permute-start.30

commit v14 on v13

--- a/solution.py
+++ b/solution.py
@@ -310,7 +310,7 @@
         far_steps.append([block, None] if at % 2 == 0 else [None, block])
     far_steps += [[("wait", None), None], [None, ("wait", None)]]
     near = list(range(1, half))
-    near_steps = [near[:2], [], [], []] + [[d] for d in near[2:]]
+    near_steps = [near[:2], []] + [[d] for d in near[2:]]
     relayed = set()
 
     def rides(d):
@@ -402,33 +402,41 @@
                     array = send("tok", d, [(outgoing[d], first, width)], after)[1]
                     lanes_before[lane] = (now[lane], array)
             flying += lanes_before[lane] is not None
-        for d, array in near_before:
+        for entry in list(near_before):
+            due, d, array = entry
+            if due > step:
+                flying += 1
+                continue
+            near_before.remove(entry)
             ready += [(d, i, array, first) for i, (first, _) in enumerate(pieces)]
             if rides(d):
                 cots[d] = cots_at(array, own_width)
-        near_before.clear()
         arrivals = finish_relays(step)
         if cross_before is not None:
             crossed.append(cross_before)
         earlier = [cross_before[2]] if cross_before is not None else []
+        earlier += [core_before[1]] if core_before is not None else []
         cross_before = None
-        bit = half // 2
-        while bit:
-            sources = [d for d in sorted(cots) if bit in bits_below(d) and d + bit not in relayed]
-            if sources and flying < 4 and step > 0:
-                relayed.update(d + bit for d in sources)
-                parts = [part for d in sources for part in cot_parts(d)]
-                relay_before.append((step + 1, bit, sources, send("tok", bit, parts, earlier)[1]))
-                flying += 1
-            bit //= 2
         if ready:
             blocks = []
             while ready and sum(pieces[i][1] for _, i, _, _ in blocks) < 2 * own_width:
                 blocks.append(ready.pop(0))
             parts = [(array, first, pieces[i][1]) for _, i, array, first in blocks]
             own, other = send("user", across, parts, earlier)
+            earlier = []
             cross_before = (blocks, own, other)
             flying += 1
+        bit, sent = half // 2, False
+        while bit:
+            sources = [d for d in sorted(cots) if bit in bits_below(d) and d + bit not in relayed]
+            if sources and flying < 5 and step > 0 and not sent:
+                relayed.update(d + bit for d in sources)
+                parts = [part for d in sources for part in cot_parts(d)]
+                relay_before.append((step + (1 if step < 4 else 2), bit, sources, send("tok", bit, parts, earlier)[1]))
+                earlier = []
+                flying += 1
+                sent = True
+            bit //= 2
         if step == 0:
             cots[0] = [(block, 0) for block in by_slot]
             cots[0] = cots_at(join(cot_parts(0), tick), 0)
@@ -439,7 +447,7 @@
                 parts = [(outgoing[d], 0, own_width)]
                 if rides(d):
                     parts += cot_parts(0)
-                near_before.append((d, send("tok", d, parts)[1]))
+                near_before.append((step + (2 if step else 1), d, send("tok", d, parts)[1]))
                 flying += 1
         before = [core_before[1]] if core_before else []
         finish_core()
@@ -452,7 +460,7 @@
             crossed.clear()
             flying += 1
         if step < len(far_steps):
-            tick[:] = [hold(tick[0], arrivals, max(sizes))]
+            tick[:] = [hold(tick[0], arrivals + earlier, max(sizes))]
             sizes[:] = [0]
         if step == len(far_steps) - 3:
             add_products(0)

time: 193 us -> 187 us (0.969)
  starting transfers between devices: 44 us -> 39.9 us
  waiting for transfers between devices: 104 us -> 100 us
  blocking collectives: 10.4 us -> 13.6 us
    ppermute x31 -> x29, starting transfers between devices: 44 us -> 39.9 us  [exchange(): return lax.ppermute(block, axis, [(i, i ^ distance) for i in range(size)])]
    ppermute x31 -> x29, waiting for transfers between devices: 104 us -> 100 us  [exchange(): return lax.ppermute(block, axis, [(i, i ^ distance) for i in range(size)])]
    all_to_all x1, blocking collectives: 10.4 us -> 13.6 us  [body(): lax.all_to_all(gradients[1][1], ('user', 'tok'), split_axis=0, concat_axi...]
    unnamed x32 -> x24, local copies, waits for them, and re-layouts: 4.06 us -> 3.26 us
  transfers between devices with their start and end apart: 31 -> 29, of which waited for: 13 -> 11; matrix products, arithmetic and copies ran while one was open for 0% -> 0% of each run, Pallas kernels for 11% -> 11%
where the time goes in v14:
time: 187 us
  waiting for transfers between devices  100 us (53%)
  starting transfers between devices  39.9 us (21%)
  Pallas kernels  29.2 us (16%)
  blocking collectives  13.6 us (7%)
  local copies, waits for them, and re-layouts  3.26 us (2%)
    ppermute x29, waiting for transfers between devices, exchange(): return lax.ppermute(block, axis, [(i, i ^ distance) for i in range(size)])  100 us
    ppermute x29, starting transfers between devices, exchange(): return lax.ppermute(block, axis, [(i, i ^ distance) for i in range(size)])  39.9 us
    pallas_call x4, Pallas kernels, product(): pl.pallas_call(functools.partial(product_kernel, left_places, right_place...  22.6 us
    all_to_all x1, blocking collectives, body(): lax.all_to_all(gradients[1][1], ('user', 'tok'), split_axis=0, concat_axi...  13.6 us
    pallas_call x1, Pallas kernels, combine(): pl.pallas_call(functools.partial(combine_kernel, user_count, clip_bound,...  4.81 us
  transfers between devices with their start and end apart: 29, of which 11 were waited for; matrix products, arithmetic and copies ran while one was open for 0% of the time, Pallas kernels for 11%

profile of v14, /device:TPU:0, one launch (start us, length us, event | category | flops | bytes accessed | tf_op | source)
XLA Modules:
  0.0 187.2 jit_solution(2679892576959107298)
XLA Ops:
  0.7 1.0 copy-done.11
  1.7 0.5 collective-permute-start
  2.3 2.6 %collective-permute-start.1 = (bf16[128,512]{1,0:T(8,128)(2,1)S(1)}, bf16[128,512]{1,0:T(8,128)(2,1)S(1)}, u32[]{:S(2)}, u32[]{:S(2)}) collective-permute-start(bf16[128,512]{1,0:T(8,128)(2,1)S(1)} %get-tuple-element.25), channel_id=1, source_target_pairs={{0,16},{8,24},{16,0},{24,8},{1,17},{9,25},{17,1},{25,9},{2,18},{10... | collective-permute-start | bytes 393224 | tf_op jit(solution)/shard_map/ppermute | solution.py:24
  4.8 0.1 collective-permute-start.2
  4.9 2.2 %copy-done.10 = bf16[1,128,16384]{2,1,0:T(8,128)(2,1)S(1)} copy-done((bf16[1,128,16384]{2,1,0:T(8,128)(2,1)S(1)}, bf16[1,128,16384]{2,1,0:T(8,128)(2,1)}, u32[]{:S(2)}) %copy-start.10) | copy-done | bytes 4194328
  7.1 0.4 pack_columns.1
  7.5 2.9 %collective-permute-start.7 = (bf16[128,2048]{1,0:T(8,128)(2,1)S(1)}, bf16[128,2048]{1,0:T(8,128)(2,1)S(1)}, u32[]{:S(2)}, u32[]{:S(2)}) collective-permute-start(bf16[128,2048]{1,0:T(8,128)(2,1)S(1)} %join_columns.27.refs_1_), channel_id=1, source_target_pairs={{0,4},{1,5},{2,6},{3,7},{4,0},{5,1},{6,2},{7,3},{8,12},{9,13},{10,... | collective-permute-start | bytes 1572872 | tf_op jit(solution)/shard_map/ppermute | solution.py:24
  10.4 1.6 collective-permute-start.5
  12.0 0.0 collective-permute-done.1.refs_2_
  12.0 0.0 collective-permute-done.2.refs_3_
  12.1 0.1 join_columns.31.refs_1_
  12.2 1.6 collective-permute-start.3
  13.8 1.6 collective-permute-start.4
  15.5 2.1 %collective-permute-start.10 = (bf16[128,2048]{1,0:T(8,128)(2,1)S(1)}, bf16[128,2048]{1,0:T(8,128)(2,1)S(1)}, u32[]{:S(2)}, u32[]{:S(2)}) collective-permute-start(bf16[128,2048]{1,0:T(8,128)(2,1)S(1)} %join_columns.30.refs_2_), channel_id=1, source_target_pairs={{0,4},{1,5},{2,6},{3,7},{4,0},{5,1},{6,2},{7,3},{8,12},{9,13},{10,... | collective-permute-start | bytes 1572872 | tf_op jit(solution)/shard_map/ppermute | solution.py:24
  17.6 6.8 %collective-permute-done.5.refs_3_.refs_1_.refs_5_.refs_7_ = bf16[128,2048]{1,0:T(8,128)(2,1)S(1)} collective-permute-done((bf16[128,2048]{1,0:T(8,128)(2,1)S(1)}, bf16[128,2048]{1,0:T(8,128)(2,1)S(1)}, u32[]{:S(2)}, u32[]{:S(2)}) %collective-permute-start.5) | collective-permute-done | bytes 524320 | tf_op jit(solution)/shard_map/ppermute | solution.py:24
  24.4 14.1 %collective-permute-done.4.refs_1_ = bf16[128,2048]{1,0:T(8,128)(2,1)S(1)} collective-permute-done((bf16[128,2048]{1,0:T(8,128)(2,1)S(1)}, bf16[128,2048]{1,0:T(8,128)(2,1)S(1)}, u32[]{:S(2)}, u32[]{:S(2)}) %collective-permute-start.4) | collective-permute-done | bytes 524320 | tf_op jit(solution)/shard_map/ppermute | solution.py:24
  38.5 0.0 collective-permute-done.3.refs_0_.refs_9_.refs_12_
  38.5 0.1 join_columns.33.refs_1_.refs_0_
  38.6 1.6 collective-permute-start.8
  40.2 0.2 collective-permute-start.6
  40.4 0.1 join_columns.35.refs_0_
  40.5 0.1 collective-permute-start.9
  40.6 4.7 %collective-permute-start.14 = (bf16[128,2048]{1,0:T(8,128)(2,1)S(1)}, bf16[128,2048]{1,0:T(8,128)(2,1)S(1)}, u32[]{:S(2)}, u32[]{:S(2)}) collective-permute-start(bf16[128,2048]{1,0:T(8,128)(2,1)S(1)} %join_columns.36.refs_1_), channel_id=1, source_target_pairs={{0,5},{1,4},{2,7},{3,6},{4,1},{5,0},{6,3},{7,2},{8,13},{9,12},{10,... | collective-permute-start | bytes 1572872 | tf_op jit(solution)/shard_map/ppermute | solution.py:24
  45.3 0.0 collective-permute-done.9.refs_3_.refs_4_
  45.3 17.3 %collective-permute-done.8.refs_2_.refs_1_.refs_6_.refs_8_ = bf16[128,4096]{1,0:T(8,128)(2,1)S(1)} collective-permute-done((bf16[128,4096]{1,0:T(8,128)(2,1)S(1)}, bf16[128,4096]{1,0:T(8,128)(2,1)S(1)}, u32[]{:S(2)}, u32[]{:S(2)}) %collective-permute-start.8) | collective-permute-done | bytes 1048608 | tf_op jit(solution)/shard_map/ppermute | solution.py:24
  62.7 1.8 collective-permute-start.12
  64.5 0.6 collective-permute-start.16
  65.1 1.6 collective-permute-start.15
  66.8 4.2 %collective-permute-start.11 = (bf16[128,2048]{1,0:T(8,128)(2,1)S(1)}, bf16[128,2048]{1,0:T(8,128)(2,1)S(1)}, u32[]{:S(2)}, u32[]{:S(2)}) collective-permute-start(bf16[128,2048]{1,0:T(8,128)(2,1)S(1)} %join_columns.40.refs_1_), channel_id=1, source_target_pairs={{0,6},{1,7},{2,4},{3,5},{4,2},{5,3},{6,0},{7,1},{8,14},{9,15},{10,... | collective-permute-start | bytes 1572872 | tf_op jit(solution)/shard_map/ppermute | solution.py:24
  70.9 3.9 %collective-permute-done.12.refs_2_.refs_3_.refs_7_.refs_10_ = bf16[128,2048]{1,0:T(8,128)(2,1)S(1)} collective-permute-done((bf16[128,2048]{1,0:T(8,128)(2,1)S(1)}, bf16[128,2048]{1,0:T(8,128)(2,1)S(1)}, u32[]{:S(2)}, u32[]{:S(2)}) %collective-permute-start.12) | collective-permute-done | bytes 524320 | tf_op jit(solution)/shard_map/ppermute | solution.py:24
  74.8 0.9 collective-permute-start.13
  75.8 0.2 join_columns.42.refs_0_
  76.0 17.1 %collective-permute-done.16.refs_1_.refs_14_.refs_9_ = bf16[128,2048]{1,0:T(8,128)(2,1)S(1)} collective-permute-done((bf16[128,2048]{1,0:T(8,128)(2,1)S(1)}, bf16[128,2048]{1,0:T(8,128)(2,1)S(1)}, u32[]{:S(2)}, u32[]{:S(2)}) %collective-permute-start.16) | collective-permute-done | bytes 524320 | tf_op jit(solution)/shard_map/ppermute | solution.py:24
  93.1 0.4 collective-permute-start.21
  93.5 8.7 %collective-permute-done.15.refs_1_ = bf16[128,2048]{1,0:T(8,128)(2,1)S(1)} collective-permute-done((bf16[128,2048]{1,0:T(8,128)(2,1)S(1)}, bf16[128,2048]{1,0:T(8,128)(2,1)S(1)}, u32[]{:S(2)}, u32[]{:S(2)}) %collective-permute-start.15) | collective-permute-done | bytes 524320 | tf_op jit(solution)/shard_map/ppermute | solution.py:24
  102.3 0.0 collective-permute-done.17.refs_3_.refs_4_.refs_5_
  102.3 0.1 join_columns.44.refs_2_.refs_0_
  102.4 0.3 collective-permute-start.18
  102.7 14.6 %collective-permute-done.13.refs_1_.refs_11_.refs_6_ = bf16[128,2048]{1,0:T(8,128)(2,1)S(1)} collective-permute-done((bf16[128,2048]{1,0:T(8,128)(2,1)S(1)}, bf16[128,2048]{1,0:T(8,128)(2,1)S(1)}, u32[]{:S(2)}, u32[]{:S(2)}) %collective-permute-start.13) | collective-permute-done | bytes 524320 | tf_op jit(solution)/shard_map/ppermute | solution.py:24
  117.3 0.1 join_columns.45.refs_0_
  117.4 0.0 copy-start.5
  117.4 0.6 collective-permute-start.23
  118.0 0.0 collective-permute-done.11.refs_2_.refs_0_
  118.1 7.1 %collective-permute-start.19 = (bf16[128,768]{1,0:T(8,128)(2,1)S(1)}, bf16[128,768]{1,0:T(8,128)(2,1)S(1)}, u32[]{:S(2)}, u32[]{:S(2)}) collective-permute-start(bf16[128,768]{1,0:T(8,128)(2,1)S(1)} %join_columns.46.refs_1_), channel_id=1, source_target_pairs={{0,7},{1,6},{2,5},{3,4},{4,3},{5,2},{6,1},{7,0},{8,15},{9,14},{10,... | collective-permute-start | bytes 589832 | tf_op jit(solution)/shard_map/ppermute | solution.py:24
  125.2 6.8 %product_and_squares.4.refs_2_.refs_12_ = f32[4,1280,512]{2,1,0:T(8,128)S(1)} custom-call(bf16[128,2048]{1,0:T(8,128)(2,1)S(1)} %copy-done.1, bf16[128,4096]{1,0:T(8,128)(2,1)S(1)} %join_columns.33.refs_1_.refs_0_, bf16[128,2048]{1,0:T(8,128)(2,1)S(1)} %join_columns.37.refs_1_.refs_2_.refs_3_, bf16[128,4096]{1,0:T(8,128)(2,1)S(1)} %copy-done.5, ...), custom_call_target="tpu_custom_call" | custom-call | flops 2684354560 | bytes 7340032 | tf_op jit(solution)/shard_map/product_and_squares/pallas_call | solution.py:194
  132.0 1.2 collective-permute-start.20
  133.3 0.1 join_columns.48.refs_0_
  133.4 0.1 collective-permute-start.22
  133.5 0.0 collective-permute-done.21.refs_0_
  133.5 11.9 %collective-permute-done.20.refs_3_.refs_1_.refs_7_.refs_4_ = bf16[128,2048]{1,0:T(8,128)(2,1)S(1)} collective-permute-done((bf16[128,2048]{1,0:T(8,128)(2,1)S(1)}, bf16[128,2048]{1,0:T(8,128)(2,1)S(1)}, u32[]{:S(2)}, u32[]{:S(2)}) %collective-permute-start.20) | collective-permute-done | bytes 524320 | tf_op jit(solution)/shard_map/ppermute | solution.py:24
  145.4 0.8 collective-permute-start.24
  146.2 0.1 join_columns.50.refs_0_
  146.3 0.1 collective-permute-start.25
  146.4 5.1 %product_and_squares.5.refs_2_.refs_8_ = f32[4,768,512]{2,1,0:T(8,128)S(1)} custom-call(bf16[128,2048]{1,0:T(8,128)(2,1)S(1)} %copy-done.1, bf16[128,4096]{1,0:T(8,128)(2,1)S(1)} %join_columns.33.refs_1_.refs_0_, bf16[128,4096]{1,0:T(8,128)(2,1)S(1)} %join_columns.44.refs_2_.refs_0_, bf16[128,2048]{1,0:T(8,128)(2,1)S(1)} %join_columns.37.refs_1_.refs_2_.refs_3_, ...), custom_call_target="tpu_custom_call" | custom-call | flops 2415919104 | bytes 7864320 | tf_op jit(solution)/shard_map/product_and_squares/pallas_call | solution.py:194
  151.5 2.1 %collective-permute-done.24.refs_3_.refs_1_.refs_8_ = bf16[128,1280]{1,0:T(8,128)(2,1)S(1)} collective-permute-done((bf16[128,1280]{1,0:T(8,128)(2,1)S(1)}, bf16[128,1280]{1,0:T(8,128)(2,1)S(1)}, u32[]{:S(2)}, u32[]{:S(2)}) %collective-permute-start.24) | collective-permute-done | bytes 327712 | tf_op jit(solution)/shard_map/ppermute | solution.py:24
  153.7 0.4 collective-permute-start.26
  154.1 0.1 collective-permute-start.27
  154.2 2.1 %collective-permute-done.27.refs_5_ = bf16[128,2560]{1,0:T(8,128)(2,1)S(1)} collective-permute-done((bf16[128,2560]{1,0:T(8,128)(2,1)S(1)}, bf16[128,2560]{1,0:T(8,128)(2,1)S(1)}, u32[]{:S(2)}, u32[]{:S(2)}) %collective-permute-start.27) | collective-permute-done | bytes 655392 | tf_op jit(solution)/shard_map/ppermute | solution.py:24
  156.3 7.2 %product_and_squares.6 = (f32[4,1280,512]{2,1,0:T(8,128)S(1)}, f32[1,8,128]{2,1,0:T(8,128)S(1)}) custom-call(bf16[128,4096]{1,0:T(8,128)(2,1)S(1)} %join_columns.44.refs_2_.refs_0_, bf16[128,2048]{1,0:T(8,128)(2,1)S(1)} %join_columns.47.refs_2_.refs_0_.refs_1_, bf16[128,1280]{1,0:T(8,128)(2,1)S(1)} %join_columns.49.refs_2_.refs_0_, ...), custom_call_target="tpu_custom_call", output_to_operand_aliasing={{0}: (12, {})} | custom-call | flops 2684354560 | bytes 7340032 | tf_op jit(solution)/shard_map/product_and_squares/pallas_call | solution.py:194
  163.5 0.2 collective-permute-start.28
  163.7 1.6 collective-permute-done.28.refs_3_
  165.3 3.4 %product_and_squares.7 = (f32[4,768,512]{2,1,0:T(8,128)S(1)}, f32[32,8,128]{2,1,0:T(8,128)S(1)}) custom-call(bf16[128,2048]{1,0:T(8,128)(2,1)S(1)} %join_columns.47.refs_2_.refs_0_.refs_1_, bf16[128,768]{1,0:T(8,128)(2,1)S(1)} %join_columns.51.refs_2_.refs_0_.refs_1_, ...), custom_call_target="tpu_custom_call", output_to_operand_aliasing={{0}: (8, {})} | custom-call | flops 805306368 | bytes 2621440 | tf_op jit(solution)/shard_map/product_and_squares/pallas_call | solution.py:194
  168.8 13.6 %all_to_all.5.sums_ref = f32[32,8,128]{2,1,0:T(8,128)S(1)} all-to-all(f32[32,8,128]{2,1,0:T(8,128)S(1)} %get-tuple-element.35), channel_id=1, replica_groups=mesh['user'=4,'tok'=8] {'user','tok'}, dimensions={0} | all-to-all | bytes 262144 | tf_op jit(solution)/shard_map/all_to_all | solution.py:475
  182.4 4.8 %weighted_sum.1 = f32[2048,512]{1,0:T(8,128)} custom-call(s32[1]{0:T(128)} %bitcast.user_ref, f32[32,8,128]{2,1,0:T(8,128)S(1)} %all_to_all.5.sums_ref, f32[4,1280,512]{2,1,0:T(8,128)S(1)} %get-tuple-element.33.refs_3_.refs_0_, f32[4,768,512]{2,1,0:T(8,128)S(1)} %get-tuple-element.36.refs_1_), custom_call_target="tpu_custom_call" | custom-call | tf_op jit(solution)/shard_map/weighted_sum/pallas_call | solution.py:251
  (61 shorter events, 0.8 us)
Async XLA Ops:
  0.7 1.0 copy-start.11
  1.7 10.3 %collective-permute-start = (bf16[128,512]{1,0:T(8,128)(2,1)S(1)}, bf16[128,512]{1,0:T(8,128)(2,1)S(1)}, u32[]{:S(2)}, u32[]{:S(2)}) collective-permute-start(bf16[128,512]{1,0:T(8,128)(2,1)S(1)} %get-tuple-element.24), channel_id=1, source_target_pairs={{0,8},{8,0},{16,24},{24,16},{1,9},{9,1},{17,25},{25,17},{2,10},{10... | collective-permute-start | bytes 393224 | tf_op jit(solution)/shard_map/ppermute | solution.py:24
  2.3 9.7 %collective-permute-start.1 = (bf16[128,512]{1,0:T(8,128)(2,1)S(1)}, bf16[128,512]{1,0:T(8,128)(2,1)S(1)}, u32[]{:S(2)}, u32[]{:S(2)}) collective-permute-start(bf16[128,512]{1,0:T(8,128)(2,1)S(1)} %get-tuple-element.25), channel_id=1, source_target_pairs={{0,16},{8,24},{16,0},{24,8},{1,17},{9,25},{17,1},{25,9},{2,18},{10... | collective-permute-start | bytes 393224 | tf_op jit(solution)/shard_map/ppermute | solution.py:24
  4.8 7.2 %collective-permute-start.2 = (bf16[128,512]{1,0:T(8,128)(2,1)S(1)}, bf16[128,512]{1,0:T(8,128)(2,1)S(1)}, u32[]{:S(2)}, u32[]{:S(2)}) collective-permute-start(bf16[128,512]{1,0:T(8,128)(2,1)S(1)} %get-tuple-element.26), channel_id=1, source_target_pairs={{0,24},{8,16},{16,8},{24,0},{1,25},{9,17},{17,9},{25,1},{2,26},{10... | collective-permute-start | bytes 393224 | tf_op jit(solution)/shard_map/ppermute | solution.py:24
  4.9 2.2 %copy-start.10 = (bf16[1,128,16384]{2,1,0:T(8,128)(2,1)S(1)}, bf16[1,128,16384]{2,1,0:T(8,128)(2,1)}, u32[]{:S(2)}) copy-start(bf16[1,128,16384]{2,1,0:T(8,128)(2,1)} %hidden_ref.1) | copy-start | bytes 12582916
  7.5 33.1 %collective-permute-start.7 = (bf16[128,2048]{1,0:T(8,128)(2,1)S(1)}, bf16[128,2048]{1,0:T(8,128)(2,1)S(1)}, u32[]{:S(2)}, u32[]{:S(2)}) collective-permute-start(bf16[128,2048]{1,0:T(8,128)(2,1)S(1)} %join_columns.27.refs_1_), channel_id=1, source_target_pairs={{0,4},{1,5},{2,6},{3,7},{4,0},{5,1},{6,2},{7,3},{8,12},{9,13},{10,... | collective-permute-start | bytes 1572872 | tf_op jit(solution)/shard_map/ppermute | solution.py:24
  10.4 30.0 %copy-start = (bf16[128,2048]{1,0:T(8,128)(2,1)}, bf16[128,2048]{1,0:T(8,128)(2,1)S(1)}, u32[]{:S(2)}) copy-start(bf16[128,2048]{1,0:T(8,128)(2,1)S(1)} %join_columns.28.refs_4_.refs_1_.refs_0_) | copy-start | bytes 1572868
  10.4 14.0 %collective-permute-start.5 = (bf16[128,2048]{1,0:T(8,128)(2,1)S(1)}, bf16[128,2048]{1,0:T(8,128)(2,1)S(1)}, u32[]{:S(2)}, u32[]{:S(2)}) collective-permute-start(bf16[128,2048]{1,0:T(8,128)(2,1)S(1)} %join_columns.28.refs_4_.refs_1_.refs_0_), channel_id=1, source_target_pairs={{0,16},{8,24},{16,0},{24,8},{1,17},{9,25},{17,1},{25,9},{2,18},{10... | collective-permute-start | bytes 1572872 | tf_op jit(solution)/shard_map/ppermute | solution.py:24
  12.1 26.5 %copy-start.2 = (bf16[128,2048]{1,0:T(8,128)(2,1)}, bf16[128,2048]{1,0:T(8,128)(2,1)S(1)}, u32[]{:S(2)}) copy-start(bf16[128,2048]{1,0:T(8,128)(2,1)S(1)} %join_columns.29.refs_0_.refs_1_.refs_8_.refs_11_) | copy-start | bytes 1572868
  12.2 26.3 %collective-permute-start.3 = (bf16[128,4096]{1,0:T(8,128)(2,1)S(1)}, bf16[128,4096]{1,0:T(8,128)(2,1)S(1)}, u32[]{:S(2)}, u32[]{:S(2)}) collective-permute-start(bf16[128,4096]{1,0:T(8,128)(2,1)S(1)} %join_columns.31.refs_1_), channel_id=1, source_target_pairs={{0,1},{1,0},{2,3},{3,2},{4,5},{5,4},{6,7},{7,6},{8,9},{9,8},{10,11... | collective-permute-start | bytes 3145736 | tf_op jit(solution)/shard_map/ppermute | solution.py:24
  13.8 24.6 %collective-permute-start.4 = (bf16[128,2048]{1,0:T(8,128)(2,1)S(1)}, bf16[128,2048]{1,0:T(8,128)(2,1)S(1)}, u32[]{:S(2)}, u32[]{:S(2)}) collective-permute-start(bf16[128,2048]{1,0:T(8,128)(2,1)S(1)} %join_columns.32.refs_0_), channel_id=1, source_target_pairs={{0,2},{1,3},{2,0},{3,1},{4,6},{5,7},{6,4},{7,5},{8,10},{9,11},{10,... | collective-permute-start | bytes 1572872 | tf_op jit(solution)/shard_map/ppermute | solution.py:24
  15.5 51.2 %collective-permute-start.10 = (bf16[128,2048]{1,0:T(8,128)(2,1)S(1)}, bf16[128,2048]{1,0:T(8,128)(2,1)S(1)}, u32[]{:S(2)}, u32[]{:S(2)}) collective-permute-start(bf16[128,2048]{1,0:T(8,128)(2,1)S(1)} %join_columns.30.refs_2_), channel_id=1, source_target_pairs={{0,4},{1,5},{2,6},{3,7},{4,0},{5,1},{6,2},{7,3},{8,12},{9,13},{10,... | collective-permute-start | bytes 1572872 | tf_op jit(solution)/shard_map/ppermute | solution.py:24
  24.4 16.1 %copy-start.8 = (bf16[128,2048]{1,0:T(8,128)(2,1)}, bf16[128,2048]{1,0:T(8,128)(2,1)S(1)}, u32[]{:S(2)}) copy-start(bf16[128,2048]{1,0:T(8,128)(2,1)S(1)} %collective-permute-done.5.refs_3_.refs_1_.refs_5_.refs_7_) | copy-start | bytes 1572868
  38.5 2.1 %copy-start.6 = (bf16[128,4096]{1,0:T(8,128)(2,1)}, bf16[128,4096]{1,0:T(8,128)(2,1)S(1)}, u32[]{:S(2)}) copy-start(bf16[128,4096]{1,0:T(8,128)(2,1)S(1)} %collective-permute-done.3.refs_0_.refs_9_.refs_12_) | copy-start | bytes 3145732
  38.6 24.0 %collective-permute-start.8 = (bf16[128,4096]{1,0:T(8,128)(2,1)S(1)}, bf16[128,4096]{1,0:T(8,128)(2,1)S(1)}, u32[]{:S(2)}, u32[]{:S(2)}) collective-permute-start(bf16[128,4096]{1,0:T(8,128)(2,1)S(1)} %join_columns.33.refs_1_.refs_0_), channel_id=1, source_target_pairs={{0,16},{8,24},{16,0},{24,8},{1,17},{9,25},{17,1},{25,9},{2,18},{10... | collective-permute-start | bytes 3145736 | tf_op jit(solution)/shard_map/ppermute | solution.py:24
  40.2 24.3 %collective-permute-start.6 = (bf16[128,2048]{1,0:T(8,128)(2,1)S(1)}, bf16[128,2048]{1,0:T(8,128)(2,1)S(1)}, u32[]{:S(2)}, u32[]{:S(2)}) collective-permute-start(bf16[128,2048]{1,0:T(8,128)(2,1)S(1)} %join_columns.34.refs_2_), channel_id=1, source_target_pairs={{0,2},{1,3},{2,0},{3,1},{4,6},{5,7},{6,4},{7,5},{8,10},{9,11},{10,... | collective-permute-start | bytes 1572872 | tf_op jit(solution)/shard_map/ppermute | solution.py:24
  40.5 4.9 %collective-permute-start.9 = (bf16[128,4096]{1,0:T(8,128)(2,1)S(1)}, bf16[128,4096]{1,0:T(8,128)(2,1)S(1)}, u32[]{:S(2)}, u32[]{:S(2)}) collective-permute-start(bf16[128,4096]{1,0:T(8,128)(2,1)S(1)} %join_columns.35.refs_0_), channel_id=1, source_target_pairs={{0,8},{8,0},{16,24},{24,16},{1,9},{9,1},{17,25},{25,17},{2,10},{10... | collective-permute-start | bytes 3145736 | tf_op jit(solution)/shard_map/ppermute | solution.py:24
  40.6 52.4 %collective-permute-start.14 = (bf16[128,2048]{1,0:T(8,128)(2,1)S(1)}, bf16[128,2048]{1,0:T(8,128)(2,1)S(1)}, u32[]{:S(2)}, u32[]{:S(2)}) collective-permute-start(bf16[128,2048]{1,0:T(8,128)(2,1)S(1)} %join_columns.36.refs_1_), channel_id=1, source_target_pairs={{0,5},{1,4},{2,7},{3,6},{4,1},{5,0},{6,3},{7,2},{8,13},{9,12},{10,... | collective-permute-start | bytes 1572872 | tf_op jit(solution)/shard_map/ppermute | solution.py:24
  45.3 21.4 %copy-start.4 = (bf16[128,4096]{1,0:T(8,128)(2,1)}, bf16[128,4096]{1,0:T(8,128)(2,1)S(1)}, u32[]{:S(2)}) copy-start(bf16[128,4096]{1,0:T(8,128)(2,1)S(1)} %collective-permute-done.9.refs_3_.refs_4_) | copy-start | bytes 3145732
  62.7 12.1 %collective-permute-start.12 = (bf16[128,2048]{1,0:T(8,128)(2,1)S(1)}, bf16[128,2048]{1,0:T(8,128)(2,1)S(1)}, u32[]{:S(2)}, u32[]{:S(2)}) collective-permute-start(bf16[128,2048]{1,0:T(8,128)(2,1)S(1)} %join_columns.37.refs_1_.refs_2_.refs_3_), channel_id=1, source_target_pairs={{0,16},{8,24},{16,0},{24,8},{1,17},{9,25},{17,1},{25,9},{2,18},{10... | collective-permute-start | bytes 1572872 | tf_op jit(solution)/shard_map/ppermute | solution.py:24
  64.5 28.5 %collective-permute-start.16 = (bf16[128,2048]{1,0:T(8,128)(2,1)S(1)}, bf16[128,2048]{1,0:T(8,128)(2,1)S(1)}, u32[]{:S(2)}, u32[]{:S(2)}) collective-permute-start(bf16[128,2048]{1,0:T(8,128)(2,1)S(1)} %join_columns.38.refs_1_), channel_id=1, source_target_pairs={{0,1},{1,0},{2,3},{3,2},{4,5},{5,4},{6,7},{7,6},{8,9},{9,8},{10,11... | collective-permute-start | bytes 1572872 | tf_op jit(solution)/shard_map/ppermute | solution.py:24
  65.1 37.1 %collective-permute-start.15 = (bf16[128,2048]{1,0:T(8,128)(2,1)S(1)}, bf16[128,2048]{1,0:T(8,128)(2,1)S(1)}, u32[]{:S(2)}, u32[]{:S(2)}) collective-permute-start(bf16[128,2048]{1,0:T(8,128)(2,1)S(1)} %join_columns.39.refs_0_), channel_id=1, source_target_pairs={{0,3},{1,2},{2,1},{3,0},{4,7},{5,6},{6,5},{7,4},{8,11},{9,10},{10,... | collective-permute-start | bytes 1572872 | tf_op jit(solution)/shard_map/ppermute | solution.py:24
  66.8 51.3 %collective-permute-start.11 = (bf16[128,2048]{1,0:T(8,128)(2,1)S(1)}, bf16[128,2048]{1,0:T(8,128)(2,1)S(1)}, u32[]{:S(2)}, u32[]{:S(2)}) collective-permute-start(bf16[128,2048]{1,0:T(8,128)(2,1)S(1)} %join_columns.40.refs_1_), channel_id=1, source_target_pairs={{0,6},{1,7},{2,4},{3,5},{4,2},{5,3},{6,0},{7,1},{8,14},{9,15},{10,... | collective-permute-start | bytes 1572872 | tf_op jit(solution)/shard_map/ppermute | solution.py:24
  74.8 42.4 %collective-permute-start.13 = (bf16[128,2048]{1,0:T(8,128)(2,1)S(1)}, bf16[128,2048]{1,0:T(8,128)(2,1)S(1)}, u32[]{:S(2)}, u32[]{:S(2)}) collective-permute-start(bf16[128,2048]{1,0:T(8,128)(2,1)S(1)} %join_columns.41.refs_4_), channel_id=1, source_target_pairs={{0,2},{1,3},{2,0},{3,1},{4,6},{5,7},{6,4},{7,5},{8,10},{9,11},{10,... | collective-permute-start | bytes 1572872 | tf_op jit(solution)/shard_map/ppermute | solution.py:24
  93.0 9.2 %collective-permute-start.17 = (bf16[128,12288]{1,0:T(8,128)(2,1)S(1)}, bf16[128,12288]{1,0:T(8,128)(2,1)S(1)}, u32[]{:S(2)}, u32[]{:S(2)}) collective-permute-start(bf16[128,12288]{1,0:T(8,128)(2,1)S(1)} %join_columns.42.refs_0_), channel_id=1, source_target_pairs={{0,8},{8,0},{16,24},{24,16},{1,9},{9,1},{17,25},{25,17},{2,10},{10... | collective-permute-start | bytes 9437192 | tf_op jit(solution)/shard_map/ppermute | solution.py:24
  93.1 40.4 %collective-permute-start.21 = (bf16[128,1280]{1,0:T(8,128)(2,1)S(1)}, bf16[128,1280]{1,0:T(8,128)(2,1)S(1)}, u32[]{:S(2)}, u32[]{:S(2)}) collective-permute-start(bf16[128,1280]{1,0:T(8,128)(2,1)S(1)} %join_columns.43.refs_2_), channel_id=1, source_target_pairs={{0,7},{1,6},{2,5},{3,4},{4,3},{5,2},{6,1},{7,0},{8,15},{9,14},{10,... | collective-permute-start | bytes 983048 | tf_op jit(solution)/shard_map/ppermute | solution.py:24
  102.4 29.6 %collective-permute-start.18 = (bf16[128,4096]{1,0:T(8,128)(2,1)S(1)}, bf16[128,4096]{1,0:T(8,128)(2,1)S(1)}, u32[]{:S(2)}, u32[]{:S(2)}) collective-permute-start(bf16[128,4096]{1,0:T(8,128)(2,1)S(1)} %join_columns.44.refs_2_.refs_0_), channel_id=1, source_target_pairs={{0,16},{8,24},{16,0},{24,8},{1,17},{9,25},{17,1},{25,9},{2,18},{10... | collective-permute-start | bytes 3145736 | tf_op jit(solution)/shard_map/ppermute | solution.py:24
  117.4 7.8 %copy-start.1 = (bf16[128,2048]{1,0:T(8,128)(2,1)S(1)}, bf16[128,2048]{1,0:T(8,128)(2,1)}, u32[]{:S(2)}) copy-start(bf16[128,2048]{1,0:T(8,128)(2,1)} %copy-done) | copy-start | bytes 1572868
  117.4 7.8 %copy-start.3 = (bf16[128,2048]{1,0:T(8,128)(2,1)S(1)}, bf16[128,2048]{1,0:T(8,128)(2,1)}, u32[]{:S(2)}) copy-start(bf16[128,2048]{1,0:T(8,128)(2,1)} %copy-done.2) | copy-start | bytes 1572868
  117.4 7.8 %copy-start.5 = (bf16[128,4096]{1,0:T(8,128)(2,1)S(1)}, bf16[128,4096]{1,0:T(8,128)(2,1)}, u32[]{:S(2)}) copy-start(bf16[128,4096]{1,0:T(8,128)(2,1)} %copy-done.4) | copy-start | bytes 3145732
  117.4 7.8 %copy-start.7 = (bf16[128,4096]{1,0:T(8,128)(2,1)S(1)}, bf16[128,4096]{1,0:T(8,128)(2,1)}, u32[]{:S(2)}) copy-start(bf16[128,4096]{1,0:T(8,128)(2,1)} %copy-done.6) | copy-start | bytes 3145732
  117.4 7.8 %copy-start.9 = (bf16[128,2048]{1,0:T(8,128)(2,1)S(1)}, bf16[128,2048]{1,0:T(8,128)(2,1)}, u32[]{:S(2)}) copy-start(bf16[128,2048]{1,0:T(8,128)(2,1)} %copy-done.8) | copy-start | bytes 1572868
  117.4 29.0 %collective-permute-start.23 = (bf16[128,4096]{1,0:T(8,128)(2,1)S(1)}, bf16[128,4096]{1,0:T(8,128)(2,1)S(1)}, u32[]{:S(2)}, u32[]{:S(2)}) collective-permute-start(bf16[128,4096]{1,0:T(8,128)(2,1)S(1)} %join_columns.45.refs_0_), channel_id=1, source_target_pairs={{0,1},{1,0},{2,3},{3,2},{4,5},{5,4},{6,7},{7,6},{8,9},{9,8},{10,11... | collective-permute-start | bytes 3145736 | tf_op jit(solution)/shard_map/ppermute | solution.py:24
  118.1 33.5 %collective-permute-start.19 = (bf16[128,768]{1,0:T(8,128)(2,1)S(1)}, bf16[128,768]{1,0:T(8,128)(2,1)S(1)}, u32[]{:S(2)}, u32[]{:S(2)}) collective-permute-start(bf16[128,768]{1,0:T(8,128)(2,1)S(1)} %join_columns.46.refs_1_), channel_id=1, source_target_pairs={{0,7},{1,6},{2,5},{3,4},{4,3},{5,2},{6,1},{7,0},{8,15},{9,14},{10,... | collective-permute-start | bytes 589832 | tf_op jit(solution)/shard_map/ppermute | solution.py:24
  132.0 13.4 %collective-permute-start.20 = (bf16[128,2048]{1,0:T(8,128)(2,1)S(1)}, bf16[128,2048]{1,0:T(8,128)(2,1)S(1)}, u32[]{:S(2)}, u32[]{:S(2)}) collective-permute-start(bf16[128,2048]{1,0:T(8,128)(2,1)S(1)} %join_columns.47.refs_2_.refs_0_.refs_1_), channel_id=1, source_target_pairs={{0,16},{8,24},{16,0},{24,8},{1,17},{9,25},{17,1},{25,9},{2,18},{10... | collective-permute-start | bytes 1572872 | tf_op jit(solution)/shard_map/ppermute | solution.py:24
  133.4 12.0 %collective-permute-start.22 = (bf16[128,8192]{1,0:T(8,128)(2,1)S(1)}, bf16[128,8192]{1,0:T(8,128)(2,1)S(1)}, u32[]{:S(2)}, u32[]{:S(2)}) collective-permute-start(bf16[128,8192]{1,0:T(8,128)(2,1)S(1)} %join_columns.48.refs_0_), channel_id=1, source_target_pairs={{0,8},{8,0},{16,24},{24,16},{1,9},{9,1},{17,25},{25,17},{2,10},{10... | collective-permute-start | bytes 6291464 | tf_op jit(solution)/shard_map/ppermute | solution.py:24
  145.4 8.2 %collective-permute-start.24 = (bf16[128,1280]{1,0:T(8,128)(2,1)S(1)}, bf16[128,1280]{1,0:T(8,128)(2,1)S(1)}, u32[]{:S(2)}, u32[]{:S(2)}) collective-permute-start(bf16[128,1280]{1,0:T(8,128)(2,1)S(1)} %join_columns.49.refs_2_.refs_0_), channel_id=1, source_target_pairs={{0,16},{8,24},{16,0},{24,8},{1,17},{9,25},{17,1},{25,9},{2,18},{10... | collective-permute-start | bytes 983048 | tf_op jit(solution)/shard_map/ppermute | solution.py:24
  146.3 7.3 %collective-permute-start.25 = (bf16[128,4096]{1,0:T(8,128)(2,1)S(1)}, bf16[128,4096]{1,0:T(8,128)(2,1)S(1)}, u32[]{:S(2)}, u32[]{:S(2)}) collective-permute-start(bf16[128,4096]{1,0:T(8,128)(2,1)S(1)} %join_columns.50.refs_0_), channel_id=1, source_target_pairs={{0,8},{8,0},{16,24},{24,16},{1,9},{9,1},{17,25},{25,17},{2,10},{10... | collective-permute-start | bytes 3145736 | tf_op jit(solution)/shard_map/ppermute | solution.py:24
  153.7 9.8 %collective-permute-start.26 = (bf16[128,768]{1,0:T(8,128)(2,1)S(1)}, bf16[128,768]{1,0:T(8,128)(2,1)S(1)}, u32[]{:S(2)}, u32[]{:S(2)}) collective-permute-start(bf16[128,768]{1,0:T(8,128)(2,1)S(1)} %join_columns.51.refs_2_.refs_0_.refs_1_), channel_id=1, source_target_pairs={{0,16},{8,24},{16,0},{24,8},{1,17},{9,25},{17,1},{25,9},{2,18},{10... | collective-permute-start | bytes 589832 | tf_op jit(solution)/shard_map/ppermute | solution.py:24
  154.1 2.2 %collective-permute-start.27 = (bf16[128,2560]{1,0:T(8,128)(2,1)S(1)}, bf16[128,2560]{1,0:T(8,128)(2,1)S(1)}, u32[]{:S(2)}, u32[]{:S(2)}) collective-permute-start(bf16[128,2560]{1,0:T(8,128)(2,1)S(1)} %join_columns.52.refs_0_), channel_id=1, source_target_pairs={{0,8},{8,0},{16,24},{24,16},{1,9},{9,1},{17,25},{25,17},{2,10},{10... | collective-permute-start | bytes 1966088 | tf_op jit(solution)/shard_map/ppermute | solution.py:24
  163.5 1.8 collective-permute-start.28

commit v15 on v14

--- a/solution.py
+++ b/solution.py
@@ -167,7 +167,7 @@
         outs[1][...] = jnp.broadcast_to(rows[None], outs[1].shape)
 
 
-def product(lefts, rights, width, columns, held=None, sums=None, copies=0):
+def product(lefts, rights, width, columns, held=None, sums=None, copies=0, after=()):
     operands, at = [], {}
 
     def place(part):
@@ -181,6 +181,9 @@
     left_places = [[place(part) for part in slot] for slot in lefts]
     right_places = [[place(part) for part in slot] for slot in rights]
     tokens = sources * lefts[0][0][0].shape[0]
+    blocks = len(operands)
+    operands += [array for array in after if id(array) not in at and array is not held]
+    waits = len(operands) - blocks
     aliases = {}
     if held is not None:
         aliases = {len(operands): 0}
@@ -196,7 +199,7 @@
             product_kernel, left_places, right_places, tile, held is not None, sums is not None, copies
         ),
         out_shape=out_shape,
-        in_specs=[VMEM] * len(operands),
+        in_specs=[VMEM] * blocks + [ANY] * waits + [VMEM] * (len(operands) - blocks - waits),
         out_specs=[VMEM] * len(out_shape),
         input_output_aliases=aliases,
         compiler_params=pltpu.CompilerParams(vmem_limit_bytes=8 * 2**20),
@@ -373,6 +376,7 @@
             held=gradients[i][0] if gradients[i] else None,
             sums=gradients[0][1] if full and i == 1 else None,
             copies=0 if not full else tok_count * user_count if i == 1 else 1,
+            after=tick[:1] if not full else [],
         )
         gradients[i] = out
         tick.append(out[0])
@@ -429,10 +433,10 @@
         bit, sent = half // 2, False
         while bit:
             sources = [d for d in sorted(cots) if bit in bits_below(d) and d + bit not in relayed]
-            if sources and flying < 5 and step > 0 and not sent:
+            if sources and step > 0 and (step > 5 or (flying < 5 and not sent)):
                 relayed.update(d + bit for d in sources)
                 parts = [part for d in sources for part in cot_parts(d)]
-                relay_before.append((step + (1 if step < 4 else 2), bit, sources, send("tok", bit, parts, earlier)[1]))
+                relay_before.append((step + (1 if step < 3 else 2), bit, sources, send("tok", bit, parts, earlier)[1]))
                 earlier = []
                 flying += 1
                 sent = True
@@ -447,7 +451,7 @@
                 parts = [(outgoing[d], 0, own_width)]
                 if rides(d):
                     parts += cot_parts(0)
-                near_before.append((step + (2 if step else 1), d, send("tok", d, parts)[1]))
+                near_before.append((step + (3 if step else 1), d, send("tok", d, parts)[1]))
                 flying += 1
         before = [core_before[1]] if core_before else []
         finish_core()

time: 187 us -> 178 us (0.952)
  waiting for transfers between devices: 100 us -> 86.9 us
  starting transfers between devices: 39.9 us -> 43.6 us
  blocking collectives: 13.6 us -> 9.9 us
  local copies, waits for them, and re-layouts: 3.26 us -> 6.07 us
    ppermute x29 -> x30, waiting for transfers between devices: 100 us -> 86.9 us  [exchange(): return lax.ppermute(block, axis, [(i, i ^ distance) for i in range(size)])]
    ppermute x29 -> x30, starting transfers between devices: 39.9 us -> 43.6 us  [exchange(): return lax.ppermute(block, axis, [(i, i ^ distance) for i in range(size)])]
    all_to_all x1, blocking collectives: 13.6 us -> 9.9 us  [body(): lax.all_to_all(gradients[1][1], ('user', 'tok'), split_axis=0, concat_axi...]
    unnamed x24 -> x32, local copies, waits for them, and re-layouts: 3.26 us -> 6.07 us
  transfers between devices with their start and end apart: 29 -> 30, of which waited for: 11 -> 12; matrix products, arithmetic and copies ran while one was open for 0% -> 0% of each run, Pallas kernels for 11% -> 12%
where the time goes in v15:
time: 178 us
  waiting for transfers between devices  86.9 us (49%)
  starting transfers between devices  43.6 us (24%)
  Pallas kernels  30.1 us (17%)
  blocking collectives  9.9 us (6%)
  local copies, waits for them, and re-layouts  6.07 us (3%)
    ppermute x30, waiting for transfers between devices, exchange(): return lax.ppermute(block, axis, [(i, i ^ distance) for i in range(size)])  86.9 us
    ppermute x30, starting transfers between devices, exchange(): return lax.ppermute(block, axis, [(i, i ^ distance) for i in range(size)])  43.6 us
    pallas_call x4, Pallas kernels, product(): pl.pallas_call(functools.partial(product_kernel, left_places, right_place...  23.4 us
    all_to_all x1, blocking collectives, body(): lax.all_to_all(gradients[1][1], ('user', 'tok'), split_axis=0, concat_axi...  9.9 us
    unnamed x32, local copies, waits for them, and re-layouts  6.07 us
    pallas_call x1, Pallas kernels, combine(): pl.pallas_call(functools.partial(combine_kernel, user_count, clip_bound,...  4.82 us
  transfers between devices with their start and end apart: 30, of which 12 were waited for; matrix products, arithmetic and copies ran while one was open for 0% of the time, Pallas kernels for 12%

profile of v15, /device:TPU:0, one launch (start us, length us, event | category | flops | bytes accessed | tf_op | source)
XLA Modules:
  0.0 177.7 jit_solution(1453554946660899963)
XLA Ops:
  0.7 1.0 copy-done.15
  1.7 0.5 collective-permute-start
  2.3 2.6 %collective-permute-start.1 = (bf16[128,512]{1,0:T(8,128)(2,1)S(1)}, bf16[128,512]{1,0:T(8,128)(2,1)S(1)}, u32[]{:S(2)}, u32[]{:S(2)}) collective-permute-start(bf16[128,512]{1,0:T(8,128)(2,1)S(1)} %get-tuple-element.25), channel_id=1, source_target_pairs={{0,16},{8,24},{16,0},{24,8},{1,17},{9,25},{17,1},{25,9},{2,18},{10... | collective-permute-start | bytes 393224 | tf_op jit(solution)/shard_map/ppermute | solution.py:24
  4.8 0.1 collective-permute-start.2
  4.9 2.2 %copy-done.12 = bf16[1,128,16384]{2,1,0:T(8,128)(2,1)S(1)} copy-done((bf16[1,128,16384]{2,1,0:T(8,128)(2,1)S(1)}, bf16[1,128,16384]{2,1,0:T(8,128)(2,1)}, u32[]{:S(2)}) %copy-start.12) | copy-done | bytes 4194328
  7.1 0.4 pack_columns.1
  7.5 2.9 %collective-permute-start.7 = (bf16[128,2048]{1,0:T(8,128)(2,1)S(1)}, bf16[128,2048]{1,0:T(8,128)(2,1)S(1)}, u32[]{:S(2)}, u32[]{:S(2)}) collective-permute-start(bf16[128,2048]{1,0:T(8,128)(2,1)S(1)} %join_columns.28.refs_1_), channel_id=1, source_target_pairs={{0,4},{1,5},{2,6},{3,7},{4,0},{5,1},{6,2},{7,3},{8,12},{9,13},{10,... | collective-permute-start | bytes 1572872 | tf_op jit(solution)/shard_map/ppermute | solution.py:24
  10.4 1.6 collective-permute-start.5
  12.1 0.1 join_columns.32.refs_1_
  12.2 1.6 collective-permute-start.3
  13.8 1.6 collective-permute-start.4
  15.5 2.1 %collective-permute-start.10 = (bf16[128,2048]{1,0:T(8,128)(2,1)S(1)}, bf16[128,2048]{1,0:T(8,128)(2,1)S(1)}, u32[]{:S(2)}, u32[]{:S(2)}) collective-permute-start(bf16[128,2048]{1,0:T(8,128)(2,1)S(1)} %join_columns.31.refs_2_), channel_id=1, source_target_pairs={{0,4},{1,5},{2,6},{3,7},{4,0},{5,1},{6,2},{7,3},{8,12},{9,13},{10,... | collective-permute-start | bytes 1572872 | tf_op jit(solution)/shard_map/ppermute | solution.py:24
  17.6 6.8 %collective-permute-done.5.refs_3_.refs_1_.refs_5_.refs_7_ = bf16[128,2048]{1,0:T(8,128)(2,1)S(1)} collective-permute-done((bf16[128,2048]{1,0:T(8,128)(2,1)S(1)}, bf16[128,2048]{1,0:T(8,128)(2,1)S(1)}, u32[]{:S(2)}, u32[]{:S(2)}) %collective-permute-start.5) | collective-permute-done | bytes 524320 | tf_op jit(solution)/shard_map/ppermute | solution.py:24
  24.4 14.1 %collective-permute-done.4.refs_1_ = bf16[128,2048]{1,0:T(8,128)(2,1)S(1)} collective-permute-done((bf16[128,2048]{1,0:T(8,128)(2,1)S(1)}, bf16[128,2048]{1,0:T(8,128)(2,1)S(1)}, u32[]{:S(2)}, u32[]{:S(2)}) %collective-permute-start.4) | collective-permute-done | bytes 524320 | tf_op jit(solution)/shard_map/ppermute | solution.py:24
  38.5 0.1 join_columns.34.refs_1_.refs_0_
  38.6 1.6 collective-permute-start.8
  40.2 0.2 collective-permute-start.6
  40.4 0.1 join_columns.36.refs_0_
  40.5 0.1 collective-permute-start.9
  40.6 4.7 %collective-permute-start.13 = (bf16[128,2048]{1,0:T(8,128)(2,1)S(1)}, bf16[128,2048]{1,0:T(8,128)(2,1)S(1)}, u32[]{:S(2)}, u32[]{:S(2)}) collective-permute-start(bf16[128,2048]{1,0:T(8,128)(2,1)S(1)} %join_columns.37.refs_1_), channel_id=1, source_target_pairs={{0,5},{1,4},{2,7},{3,6},{4,1},{5,0},{6,3},{7,2},{8,13},{9,12},{10,... | collective-permute-start | bytes 1572872 | tf_op jit(solution)/shard_map/ppermute | solution.py:24
  45.3 17.3 %collective-permute-done.8.refs_2_.refs_1_.refs_6_.refs_8_ = bf16[128,4096]{1,0:T(8,128)(2,1)S(1)} collective-permute-done((bf16[128,4096]{1,0:T(8,128)(2,1)S(1)}, bf16[128,4096]{1,0:T(8,128)(2,1)S(1)}, u32[]{:S(2)}, u32[]{:S(2)}) %collective-permute-start.8) | collective-permute-done | bytes 1048608 | tf_op jit(solution)/shard_map/ppermute | solution.py:24
  62.7 1.8 %collective-permute-start.14 = (bf16[128,2048]{1,0:T(8,128)(2,1)S(1)}, bf16[128,2048]{1,0:T(8,128)(2,1)S(1)}, u32[]{:S(2)}, u32[]{:S(2)}) collective-permute-start(bf16[128,2048]{1,0:T(8,128)(2,1)S(1)} %join_columns.38.refs_1_.refs_2_), channel_id=1, source_target_pairs={{0,16},{8,24},{16,0},{24,8},{1,17},{9,25},{17,1},{25,9},{2,18},{10... | collective-permute-start | bytes 1572872 | tf_op jit(solution)/shard_map/ppermute | solution.py:24
  64.5 0.6 collective-permute-start.15
  65.1 1.6 collective-permute-start.12
  66.8 4.2 %collective-permute-start.11 = (bf16[128,2048]{1,0:T(8,128)(2,1)S(1)}, bf16[128,2048]{1,0:T(8,128)(2,1)S(1)}, u32[]{:S(2)}, u32[]{:S(2)}) collective-permute-start(bf16[128,2048]{1,0:T(8,128)(2,1)S(1)} %join_columns.41.refs_1_), channel_id=1, source_target_pairs={{0,6},{1,7},{2,4},{3,5},{4,2},{5,3},{6,0},{7,1},{8,14},{9,15},{10,... | collective-permute-start | bytes 1572872 | tf_op jit(solution)/shard_map/ppermute | solution.py:24
  70.9 3.9 %collective-permute-done.14.refs_2_.refs_3_.refs_7_.refs_9_ = bf16[128,2048]{1,0:T(8,128)(2,1)S(1)} collective-permute-done((bf16[128,2048]{1,0:T(8,128)(2,1)S(1)}, bf16[128,2048]{1,0:T(8,128)(2,1)S(1)}, u32[]{:S(2)}, u32[]{:S(2)}) %collective-permute-start.14) | collective-permute-done | bytes 524320 | tf_op jit(solution)/shard_map/ppermute | solution.py:24
  74.8 0.9 collective-permute-start.21
  75.8 0.2 join_columns.43.refs_0_
  76.0 17.1 %collective-permute-done.15.refs_1_.refs_9_.refs_6_ = bf16[128,2048]{1,0:T(8,128)(2,1)S(1)} collective-permute-done((bf16[128,2048]{1,0:T(8,128)(2,1)S(1)}, bf16[128,2048]{1,0:T(8,128)(2,1)S(1)}, u32[]{:S(2)}, u32[]{:S(2)}) %collective-permute-start.15) | collective-permute-done | bytes 524320 | tf_op jit(solution)/shard_map/ppermute | solution.py:24
  93.1 0.8 copy-done.13
  93.9 0.4 collective-permute-start.20
  94.3 4.4 %collective-permute-done.16.refs_2_.refs_4_.refs_5_ = bf16[128,12288]{1,0:T(8,128)(2,1)S(1)} collective-permute-done((bf16[128,12288]{1,0:T(8,128)(2,1)S(1)}, bf16[128,12288]{1,0:T(8,128)(2,1)S(1)}, u32[]{:S(2)}, u32[]{:S(2)}) %collective-permute-start.16) | collective-permute-done | bytes 3145760 | tf_op jit(solution)/shard_map/ppermute | solution.py:24
  98.7 1.1 collective-permute-start.17
  99.9 0.1 collective-permute-start.23
  100.0 2.3 %collective-permute-done.12.refs_1_ = bf16[128,2048]{1,0:T(8,128)(2,1)S(1)} collective-permute-done((bf16[128,2048]{1,0:T(8,128)(2,1)S(1)}, bf16[128,2048]{1,0:T(8,128)(2,1)S(1)}, u32[]{:S(2)}, u32[]{:S(2)}) %collective-permute-start.12) | collective-permute-done | bytes 524320 | tf_op jit(solution)/shard_map/ppermute | solution.py:24
  102.3 4.6 %collective-permute-start.18 = (bf16[128,768]{1,0:T(8,128)(2,1)S(1)}, bf16[128,768]{1,0:T(8,128)(2,1)S(1)}, u32[]{:S(2)}, u32[]{:S(2)}) collective-permute-start(bf16[128,768]{1,0:T(8,128)(2,1)S(1)} %join_columns.47.refs_2_), channel_id=1, source_target_pairs={{0,7},{1,6},{2,5},{3,4},{4,3},{5,2},{6,1},{7,0},{8,15},{9,14},{10,... | collective-permute-start | bytes 589832 | tf_op jit(solution)/shard_map/ppermute | solution.py:24
  106.9 5.9 %collective-permute-done.17.refs_3_.refs_1_.refs_10_.refs_7_ = bf16[128,2048]{1,0:T(8,128)(2,1)S(1)} collective-permute-done((bf16[128,2048]{1,0:T(8,128)(2,1)S(1)}, bf16[128,2048]{1,0:T(8,128)(2,1)S(1)}, u32[]{:S(2)}, u32[]{:S(2)}) %collective-permute-start.17) | collective-permute-done | bytes 524320 | tf_op jit(solution)/shard_map/ppermute | solution.py:24
  112.8 0.1 join_columns.48.refs_1_.refs_0_
  112.9 4.2 %collective-permute-start.19 = (bf16[128,4096]{1,0:T(8,128)(2,1)S(1)}, bf16[128,4096]{1,0:T(8,128)(2,1)S(1)}, u32[]{:S(2)}, u32[]{:S(2)}) collective-permute-start(bf16[128,4096]{1,0:T(8,128)(2,1)S(1)} %join_columns.48.refs_1_.refs_0_), channel_id=1, source_target_pairs={{0,16},{8,24},{16,0},{24,8},{1,17},{9,25},{17,1},{25,9},{2,18},{10... | collective-permute-start | bytes 3145736 | tf_op jit(solution)/shard_map/ppermute | solution.py:24
  117.0 4.4 %collective-permute-done.21.refs_0_.refs_1_.refs_11_.refs_7_ = bf16[128,2048]{1,0:T(8,128)(2,1)S(1)} collective-permute-done((bf16[128,2048]{1,0:T(8,128)(2,1)S(1)}, bf16[128,2048]{1,0:T(8,128)(2,1)S(1)}, u32[]{:S(2)}, u32[]{:S(2)}) %collective-permute-start.21) | collective-permute-done | bytes 524320 | tf_op jit(solution)/shard_map/ppermute | solution.py:24
  121.5 0.1 join_columns.50.refs_0_
  121.7 0.1 collective-permute-start.22
  121.8 0.9 copy-done.1
  122.6 0.2 copy-done.3
  122.8 0.3 copy-done.5
  123.2 0.3 copy-done.7
  123.5 0.1 copy-done.9
  123.6 0.2 copy-done.11
  123.8 6.8 %product_and_squares.4.refs_2_.refs_13_ = f32[4,1280,512]{2,1,0:T(8,128)S(1)} custom-call(bf16[128,2048]{1,0:T(8,128)(2,1)S(1)} %copy-done.1, bf16[128,4096]{1,0:T(8,128)(2,1)S(1)} %join_columns.34.refs_1_.refs_0_, bf16[128,2048]{1,0:T(8,128)(2,1)S(1)} %join_columns.38.refs_1_.refs_2_, bf16[128,4096]{1,0:T(8,128)(2,1)S(1)} %copy-done.5, ...), custom_call_target="tpu_custom_call" | custom-call | flops 2684354560 | bytes 7340032 | tf_op jit(solution)/shard_map/product_and_squares/pallas_call | solution.py:197
  130.6 0.6 collective-permute-start.27
  131.2 7.1 %collective-permute-done.19.refs_3_.refs_1_.refs_6_.refs_4_ = bf16[128,4096]{1,0:T(8,128)(2,1)S(1)} collective-permute-done((bf16[128,4096]{1,0:T(8,128)(2,1)S(1)}, bf16[128,4096]{1,0:T(8,128)(2,1)S(1)}, u32[]{:S(2)}, u32[]{:S(2)}) %collective-permute-start.19) | collective-permute-done | bytes 1048608 | tf_op jit(solution)/shard_map/ppermute | solution.py:24
  138.3 1.8 %collective-permute-start.24 = (bf16[128,1280]{1,0:T(8,128)(2,1)S(1)}, bf16[128,1280]{1,0:T(8,128)(2,1)S(1)}, u32[]{:S(2)}, u32[]{:S(2)}) collective-permute-start(bf16[128,1280]{1,0:T(8,128)(2,1)S(1)} %join_columns.51.refs_2_.refs_0_), channel_id=1, source_target_pairs={{0,16},{8,24},{16,0},{24,8},{1,17},{9,25},{17,1},{25,9},{2,18},{10... | collective-permute-start | bytes 983048 | tf_op jit(solution)/shard_map/ppermute | solution.py:24
  140.1 0.1 join_columns.52.refs_0_
  140.3 0.1 collective-permute-start.25
  140.4 5.0 %product_and_squares.5.refs_2_.refs_9_ = f32[4,768,512]{2,1,0:T(8,128)S(1)} custom-call(bf16[128,2048]{1,0:T(8,128)(2,1)S(1)} %copy-done.1, bf16[128,4096]{1,0:T(8,128)(2,1)S(1)} %join_columns.34.refs_1_.refs_0_, bf16[128,2048]{1,0:T(8,128)(2,1)S(1)} %join_columns.38.refs_1_.refs_2_, bf16[128,2048]{1,0:T(8,128)(2,1)S(1)} %join_columns.45.refs_1_.refs_0_.refs_3_, ...), custom_call_target="tpu_custom_call" | custom-call | flops 2013265920 | bytes 6553600 | tf_op jit(solution)/shard_map/product_and_squares/pallas_call | solution.py:197
  145.4 1.8 %collective-permute-start.26 = (bf16[128,768]{1,0:T(8,128)(2,1)S(1)}, bf16[128,768]{1,0:T(8,128)(2,1)S(1)}, u32[]{:S(2)}, u32[]{:S(2)}) collective-permute-start(bf16[128,768]{1,0:T(8,128)(2,1)S(1)} %join_columns.53.refs_2_.refs_0_.refs_1_), channel_id=1, source_target_pairs={{0,16},{8,24},{16,0},{24,8},{1,17},{9,25},{17,1},{25,9},{2,18},{10... | collective-permute-start | bytes 589832 | tf_op jit(solution)/shard_map/ppermute | solution.py:24
  147.3 0.1 collective-permute-start.28
  147.4 2.1 %collective-permute-done.28.refs_5_ = bf16[128,2560]{1,0:T(8,128)(2,1)S(1)} collective-permute-done((bf16[128,2560]{1,0:T(8,128)(2,1)S(1)}, bf16[128,2560]{1,0:T(8,128)(2,1)S(1)}, u32[]{:S(2)}, u32[]{:S(2)}) %collective-permute-start.28) | collective-permute-done | bytes 655392 | tf_op jit(solution)/shard_map/ppermute | solution.py:24
  149.5 7.3 %product_and_squares.6 = (f32[4,1280,512]{2,1,0:T(8,128)S(1)}, f32[1,8,128]{2,1,0:T(8,128)S(1)}) custom-call(bf16[128,4096]{1,0:T(8,128)(2,1)S(1)} %join_columns.48.refs_1_.refs_0_, bf16[128,2048]{1,0:T(8,128)(2,1)S(1)} %join_columns.45.refs_1_.refs_0_.refs_3_, bf16[128,1280]{1,0:T(8,128)(2,1)S(1)} %join_columns.51.refs_2_.refs_0_, ...), custom_call_target="tpu_custom_call", output_to_operand_aliasing={{0}: (13, {})} | custom-call | flops 2684354560 | bytes 7340032 | tf_op jit(solution)/shard_map/product_and_squares/pallas_call | solution.py:197
  156.9 0.2 collective-permute-start.29
  157.1 1.6 collective-permute-done.29.refs_3_
  158.7 4.3 %product_and_squares.7 = (f32[4,768,512]{2,1,0:T(8,128)S(1)}, f32[32,8,128]{2,1,0:T(8,128)S(1)}) custom-call(bf16[128,4096]{1,0:T(8,128)(2,1)S(1)} %join_columns.48.refs_1_.refs_0_, bf16[128,768]{1,0:T(8,128)(2,1)S(1)} %join_columns.53.refs_2_.refs_0_.refs_1_, ...), custom_call_target="tpu_custom_call", output_to_operand_aliasing={{0}: (9, {})} | custom-call | flops 1207959552 | bytes 3932160 | tf_op jit(solution)/shard_map/product_and_squares/pallas_call | solution.py:197
  163.0 9.9 %all_to_all.5.sums_ref = f32[32,8,128]{2,1,0:T(8,128)S(1)} all-to-all(f32[32,8,128]{2,1,0:T(8,128)S(1)} %get-tuple-element.35), channel_id=1, replica_groups=mesh['user'=4,'tok'=8] {'user','tok'}, dimensions={0} | all-to-all | bytes 262144 | tf_op jit(solution)/shard_map/all_to_all | solution.py:479
  172.9 4.8 %weighted_sum.1 = f32[2048,512]{1,0:T(8,128)} custom-call(s32[1]{0:T(128)} %bitcast.user_ref, f32[32,8,128]{2,1,0:T(8,128)S(1)} %all_to_all.5.sums_ref, f32[4,1280,512]{2,1,0:T(8,128)S(1)} %get-tuple-element.33.refs_3_.refs_0_, f32[4,768,512]{2,1,0:T(8,128)S(1)} %get-tuple-element.36.refs_1_), custom_call_target="tpu_custom_call" | custom-call | tf_op jit(solution)/shard_map/weighted_sum/pallas_call | solution.py:254
  (72 shorter events, 0.9 us)
Async XLA Ops:
  0.7 1.0 copy-start.15
  1.7 10.3 %collective-permute-start = (bf16[128,512]{1,0:T(8,128)(2,1)S(1)}, bf16[128,512]{1,0:T(8,128)(2,1)S(1)}, u32[]{:S(2)}, u32[]{:S(2)}) collective-permute-start(bf16[128,512]{1,0:T(8,128)(2,1)S(1)} %get-tuple-element.24), channel_id=1, source_target_pairs={{0,8},{8,0},{16,24},{24,16},{1,9},{9,1},{17,25},{25,17},{2,10},{10... | collective-permute-start | bytes 393224 | tf_op jit(solution)/shard_map/ppermute | solution.py:24
  2.3 9.7 %collective-permute-start.1 = (bf16[128,512]{1,0:T(8,128)(2,1)S(1)}, bf16[128,512]{1,0:T(8,128)(2,1)S(1)}, u32[]{:S(2)}, u32[]{:S(2)}) collective-permute-start(bf16[128,512]{1,0:T(8,128)(2,1)S(1)} %get-tuple-element.25), channel_id=1, source_target_pairs={{0,16},{8,24},{16,0},{24,8},{1,17},{9,25},{17,1},{25,9},{2,18},{10... | collective-permute-start | bytes 393224 | tf_op jit(solution)/shard_map/ppermute | solution.py:24
  4.8 7.2 %collective-permute-start.2 = (bf16[128,512]{1,0:T(8,128)(2,1)S(1)}, bf16[128,512]{1,0:T(8,128)(2,1)S(1)}, u32[]{:S(2)}, u32[]{:S(2)}) collective-permute-start(bf16[128,512]{1,0:T(8,128)(2,1)S(1)} %get-tuple-element.26), channel_id=1, source_target_pairs={{0,24},{8,16},{16,8},{24,0},{1,25},{9,17},{17,9},{25,1},{2,26},{10... | collective-permute-start | bytes 393224 | tf_op jit(solution)/shard_map/ppermute | solution.py:24
  4.9 2.2 %copy-start.12 = (bf16[1,128,16384]{2,1,0:T(8,128)(2,1)S(1)}, bf16[1,128,16384]{2,1,0:T(8,128)(2,1)}, u32[]{:S(2)}) copy-start(bf16[1,128,16384]{2,1,0:T(8,128)(2,1)} %hidden_ref.1) | copy-start | bytes 12582916
  7.5 33.1 %collective-permute-start.7 = (bf16[128,2048]{1,0:T(8,128)(2,1)S(1)}, bf16[128,2048]{1,0:T(8,128)(2,1)S(1)}, u32[]{:S(2)}, u32[]{:S(2)}) collective-permute-start(bf16[128,2048]{1,0:T(8,128)(2,1)S(1)} %join_columns.28.refs_1_), channel_id=1, source_target_pairs={{0,4},{1,5},{2,6},{3,7},{4,0},{5,1},{6,2},{7,3},{8,12},{9,13},{10,... | collective-permute-start | bytes 1572872 | tf_op jit(solution)/shard_map/ppermute | solution.py:24
  10.4 30.0 %copy-start = (bf16[128,2048]{1,0:T(8,128)(2,1)}, bf16[128,2048]{1,0:T(8,128)(2,1)S(1)}, u32[]{:S(2)}) copy-start(bf16[128,2048]{1,0:T(8,128)(2,1)S(1)} %join_columns.29.refs_4_.refs_1_.refs_0_) | copy-start | bytes 1572868
  10.4 14.0 %collective-permute-start.5 = (bf16[128,2048]{1,0:T(8,128)(2,1)S(1)}, bf16[128,2048]{1,0:T(8,128)(2,1)S(1)}, u32[]{:S(2)}, u32[]{:S(2)}) collective-permute-start(bf16[128,2048]{1,0:T(8,128)(2,1)S(1)} %join_columns.29.refs_4_.refs_1_.refs_0_), channel_id=1, source_target_pairs={{0,16},{8,24},{16,0},{24,8},{1,17},{9,25},{17,1},{25,9},{2,18},{10... | collective-permute-start | bytes 1572872 | tf_op jit(solution)/shard_map/ppermute | solution.py:24
  12.1 26.5 %copy-start.2 = (bf16[128,2048]{1,0:T(8,128)(2,1)}, bf16[128,2048]{1,0:T(8,128)(2,1)S(1)}, u32[]{:S(2)}) copy-start(bf16[128,2048]{1,0:T(8,128)(2,1)S(1)} %join_columns.30.refs_0_.refs_1_.refs_8_.refs_11_) | copy-start | bytes 1572868
  12.2 26.3 %collective-permute-start.3 = (bf16[128,4096]{1,0:T(8,128)(2,1)S(1)}, bf16[128,4096]{1,0:T(8,128)(2,1)S(1)}, u32[]{:S(2)}, u32[]{:S(2)}) collective-permute-start(bf16[128,4096]{1,0:T(8,128)(2,1)S(1)} %join_columns.32.refs_1_), channel_id=1, source_target_pairs={{0,1},{1,0},{2,3},{3,2},{4,5},{5,4},{6,7},{7,6},{8,9},{9,8},{10,11... | collective-permute-start | bytes 3145736 | tf_op jit(solution)/shard_map/ppermute | solution.py:24
  13.8 24.6 %collective-permute-start.4 = (bf16[128,2048]{1,0:T(8,128)(2,1)S(1)}, bf16[128,2048]{1,0:T(8,128)(2,1)S(1)}, u32[]{:S(2)}, u32[]{:S(2)}) collective-permute-start(bf16[128,2048]{1,0:T(8,128)(2,1)S(1)} %join_columns.33.refs_0_), channel_id=1, source_target_pairs={{0,2},{1,3},{2,0},{3,1},{4,6},{5,7},{6,4},{7,5},{8,10},{9,11},{10,... | collective-permute-start | bytes 1572872 | tf_op jit(solution)/shard_map/ppermute | solution.py:24
  15.5 51.2 %collective-permute-start.10 = (bf16[128,2048]{1,0:T(8,128)(2,1)S(1)}, bf16[128,2048]{1,0:T(8,128)(2,1)S(1)}, u32[]{:S(2)}, u32[]{:S(2)}) collective-permute-start(bf16[128,2048]{1,0:T(8,128)(2,1)S(1)} %join_columns.31.refs_2_), channel_id=1, source_target_pairs={{0,4},{1,5},{2,6},{3,7},{4,0},{5,1},{6,2},{7,3},{8,12},{9,13},{10,... | collective-permute-start | bytes 1572872 | tf_op jit(solution)/shard_map/ppermute | solution.py:24
  24.4 16.2 %copy-start.8 = (bf16[128,2048]{1,0:T(8,128)(2,1)}, bf16[128,2048]{1,0:T(8,128)(2,1)S(1)}, u32[]{:S(2)}) copy-start(bf16[128,2048]{1,0:T(8,128)(2,1)S(1)} %collective-permute-done.5.refs_3_.refs_1_.refs_5_.refs_7_) | copy-start | bytes 1572868
  38.5 1.9 %copy-start.6 = (bf16[128,4096]{1,0:T(8,128)(2,1)}, bf16[128,4096]{1,0:T(8,128)(2,1)S(1)}, u32[]{:S(2)}) copy-start(bf16[128,4096]{1,0:T(8,128)(2,1)S(1)} %collective-permute-done.3.refs_0_.refs_9_.refs_12_) | copy-start | bytes 3145732
  38.6 24.0 %collective-permute-start.8 = (bf16[128,4096]{1,0:T(8,128)(2,1)S(1)}, bf16[128,4096]{1,0:T(8,128)(2,1)S(1)}, u32[]{:S(2)}, u32[]{:S(2)}) collective-permute-start(bf16[128,4096]{1,0:T(8,128)(2,1)S(1)} %join_columns.34.refs_1_.refs_0_), channel_id=1, source_target_pairs={{0,16},{8,24},{16,0},{24,8},{1,17},{9,25},{17,1},{25,9},{2,18},{10... | collective-permute-start | bytes 3145736 | tf_op jit(solution)/shard_map/ppermute | solution.py:24
  40.2 24.3 %collective-permute-start.6 = (bf16[128,2048]{1,0:T(8,128)(2,1)S(1)}, bf16[128,2048]{1,0:T(8,128)(2,1)S(1)}, u32[]{:S(2)}, u32[]{:S(2)}) collective-permute-start(bf16[128,2048]{1,0:T(8,128)(2,1)S(1)} %join_columns.35.refs_2_), channel_id=1, source_target_pairs={{0,2},{1,3},{2,0},{3,1},{4,6},{5,7},{6,4},{7,5},{8,10},{9,11},{10,... | collective-permute-start | bytes 1572872 | tf_op jit(solution)/shard_map/ppermute | solution.py:24
  40.5 4.8 %collective-permute-start.9 = (bf16[128,4096]{1,0:T(8,128)(2,1)S(1)}, bf16[128,4096]{1,0:T(8,128)(2,1)S(1)}, u32[]{:S(2)}, u32[]{:S(2)}) collective-permute-start(bf16[128,4096]{1,0:T(8,128)(2,1)S(1)} %join_columns.36.refs_0_), channel_id=1, source_target_pairs={{0,8},{8,0},{16,24},{24,16},{1,9},{9,1},{17,25},{25,17},{2,10},{10... | collective-permute-start | bytes 3145736 | tf_op jit(solution)/shard_map/ppermute | solution.py:24
  40.6 53.2 %collective-permute-start.13 = (bf16[128,2048]{1,0:T(8,128)(2,1)S(1)}, bf16[128,2048]{1,0:T(8,128)(2,1)S(1)}, u32[]{:S(2)}, u32[]{:S(2)}) collective-permute-start(bf16[128,2048]{1,0:T(8,128)(2,1)S(1)} %join_columns.37.refs_1_), channel_id=1, source_target_pairs={{0,5},{1,4},{2,7},{3,6},{4,1},{5,0},{6,3},{7,2},{8,13},{9,12},{10,... | collective-permute-start | bytes 1572872 | tf_op jit(solution)/shard_map/ppermute | solution.py:24
  45.3 21.4 %copy-start.4 = (bf16[128,4096]{1,0:T(8,128)(2,1)}, bf16[128,4096]{1,0:T(8,128)(2,1)S(1)}, u32[]{:S(2)}) copy-start(bf16[128,4096]{1,0:T(8,128)(2,1)S(1)} %collective-permute-done.9.refs_3_.refs_4_) | copy-start | bytes 3145732
  62.7 12.1 %collective-permute-start.14 = (bf16[128,2048]{1,0:T(8,128)(2,1)S(1)}, bf16[128,2048]{1,0:T(8,128)(2,1)S(1)}, u32[]{:S(2)}, u32[]{:S(2)}) collective-permute-start(bf16[128,2048]{1,0:T(8,128)(2,1)S(1)} %join_columns.38.refs_1_.refs_2_), channel_id=1, source_target_pairs={{0,16},{8,24},{16,0},{24,8},{1,17},{9,25},{17,1},{25,9},{2,18},{10... | collective-permute-start | bytes 1572872 | tf_op jit(solution)/shard_map/ppermute | solution.py:24
  64.5 2.2 %copy-start.10 = (bf16[128,2048]{1,0:T(8,128)(2,1)}, bf16[128,2048]{1,0:T(8,128)(2,1)S(1)}, u32[]{:S(2)}) copy-start(bf16[128,2048]{1,0:T(8,128)(2,1)S(1)} %collective-permute-done.6.refs_0_.refs_1_.refs_10_.refs_13_) | copy-start | bytes 1572868
  64.5 28.5 %collective-permute-start.15 = (bf16[128,2048]{1,0:T(8,128)(2,1)S(1)}, bf16[128,2048]{1,0:T(8,128)(2,1)S(1)}, u32[]{:S(2)}, u32[]{:S(2)}) collective-permute-start(bf16[128,2048]{1,0:T(8,128)(2,1)S(1)} %join_columns.39.refs_1_), channel_id=1, source_target_pairs={{0,1},{1,0},{2,3},{3,2},{4,5},{5,4},{6,7},{7,6},{8,9},{9,8},{10,11... | collective-permute-start | bytes 1572872 | tf_op jit(solution)/shard_map/ppermute | solution.py:24
  65.1 37.1 %collective-permute-start.12 = (bf16[128,2048]{1,0:T(8,128)(2,1)S(1)}, bf16[128,2048]{1,0:T(8,128)(2,1)S(1)}, u32[]{:S(2)}, u32[]{:S(2)}) collective-permute-start(bf16[128,2048]{1,0:T(8,128)(2,1)S(1)} %join_columns.40.refs_0_), channel_id=1, source_target_pairs={{0,3},{1,2},{2,1},{3,0},{4,7},{5,6},{6,5},{7,4},{8,11},{9,10},{10,... | collective-permute-start | bytes 1572872 | tf_op jit(solution)/shard_map/ppermute | solution.py:24
  66.8 33.1 %collective-permute-start.11 = (bf16[128,2048]{1,0:T(8,128)(2,1)S(1)}, bf16[128,2048]{1,0:T(8,128)(2,1)S(1)}, u32[]{:S(2)}, u32[]{:S(2)}) collective-permute-start(bf16[128,2048]{1,0:T(8,128)(2,1)S(1)} %join_columns.41.refs_1_), channel_id=1, source_target_pairs={{0,6},{1,7},{2,4},{3,5},{4,2},{5,3},{6,0},{7,1},{8,14},{9,15},{10,... | collective-permute-start | bytes 1572872 | tf_op jit(solution)/shard_map/ppermute | solution.py:24
  74.8 46.6 %collective-permute-start.21 = (bf16[128,2048]{1,0:T(8,128)(2,1)S(1)}, bf16[128,2048]{1,0:T(8,128)(2,1)S(1)}, u32[]{:S(2)}, u32[]{:S(2)}) collective-permute-start(bf16[128,2048]{1,0:T(8,128)(2,1)S(1)} %join_columns.42.refs_4_), channel_id=1, source_target_pairs={{0,2},{1,3},{2,0},{3,1},{4,6},{5,7},{6,4},{7,5},{8,10},{9,11},{10,... | collective-permute-start | bytes 1572872 | tf_op jit(solution)/shard_map/ppermute | solution.py:24
  93.0 0.8 copy-start.13
  93.0 5.7 %collective-permute-start.16 = (bf16[128,12288]{1,0:T(8,128)(2,1)S(1)}, bf16[128,12288]{1,0:T(8,128)(2,1)S(1)}, u32[]{:S(2)}, u32[]{:S(2)}) collective-permute-start(bf16[128,12288]{1,0:T(8,128)(2,1)S(1)} %join_columns.43.refs_0_), channel_id=1, source_target_pairs={{0,8},{8,0},{16,24},{24,16},{1,9},{9,1},{17,25},{25,17},{2,10},{10... | collective-permute-start | bytes 9437192 | tf_op jit(solution)/shard_map/ppermute | solution.py:24
  93.9 36.7 %collective-permute-start.20 = (bf16[128,1280]{1,0:T(8,128)(2,1)S(1)}, bf16[128,1280]{1,0:T(8,128)(2,1)S(1)}, u32[]{:S(2)}, u32[]{:S(2)}) collective-permute-start(bf16[128,1280]{1,0:T(8,128)(2,1)S(1)} %join_columns.44.refs_1_), channel_id=1, source_target_pairs={{0,7},{1,6},{2,5},{3,4},{4,3},{5,2},{6,1},{7,0},{8,15},{9,14},{10,... | collective-permute-start | bytes 983048 | tf_op jit(solution)/shard_map/ppermute | solution.py:24
  98.7 14.0 %collective-permute-start.17 = (bf16[128,2048]{1,0:T(8,128)(2,1)S(1)}, bf16[128,2048]{1,0:T(8,128)(2,1)S(1)}, u32[]{:S(2)}, u32[]{:S(2)}) collective-permute-start(bf16[128,2048]{1,0:T(8,128)(2,1)S(1)} %join_columns.45.refs_1_.refs_0_.refs_3_), channel_id=1, source_target_pairs={{0,16},{8,24},{16,0},{24,8},{1,17},{9,25},{17,1},{25,9},{2,18},{10... | collective-permute-start | bytes 1572872 | tf_op jit(solution)/shard_map/ppermute | solution.py:24
  99.9 40.4 %collective-permute-start.23 = (bf16[128,2048]{1,0:T(8,128)(2,1)S(1)}, bf16[128,2048]{1,0:T(8,128)(2,1)S(1)}, u32[]{:S(2)}, u32[]{:S(2)}) collective-permute-start(bf16[128,2048]{1,0:T(8,128)(2,1)S(1)} %join_columns.46.refs_0_), channel_id=1, source_target_pairs={{0,1},{1,0},{2,3},{3,2},{4,5},{5,4},{6,7},{7,6},{8,9},{9,8},{10,11... | collective-permute-start | bytes 1572872 | tf_op jit(solution)/shard_map/ppermute | solution.py:24
  102.3 43.1 %collective-permute-start.18 = (bf16[128,768]{1,0:T(8,128)(2,1)S(1)}, bf16[128,768]{1,0:T(8,128)(2,1)S(1)}, u32[]{:S(2)}, u32[]{:S(2)}) collective-permute-start(bf16[128,768]{1,0:T(8,128)(2,1)S(1)} %join_columns.47.refs_2_), channel_id=1, source_target_pairs={{0,7},{1,6},{2,5},{3,4},{4,3},{5,2},{6,1},{7,0},{8,15},{9,14},{10,... | collective-permute-start | bytes 589832 | tf_op jit(solution)/shard_map/ppermute | solution.py:24
  112.9 25.4 %collective-permute-start.19 = (bf16[128,4096]{1,0:T(8,128)(2,1)S(1)}, bf16[128,4096]{1,0:T(8,128)(2,1)S(1)}, u32[]{:S(2)}, u32[]{:S(2)}) collective-permute-start(bf16[128,4096]{1,0:T(8,128)(2,1)S(1)} %join_columns.48.refs_1_.refs_0_), channel_id=1, source_target_pairs={{0,16},{8,24},{16,0},{24,8},{1,17},{9,25},{17,1},{25,9},{2,18},{10... | collective-permute-start | bytes 3145736 | tf_op jit(solution)/shard_map/ppermute | solution.py:24
  121.6 1.0 copy-start.1
  121.6 1.2 copy-start.3
  121.6 1.5 copy-start.5
  121.6 1.8 %copy-start.7 = (bf16[128,4096]{1,0:T(8,128)(2,1)S(1)}, bf16[128,4096]{1,0:T(8,128)(2,1)}, u32[]{:S(2)}) copy-start(bf16[128,4096]{1,0:T(8,128)(2,1)} %copy-done.6) | copy-start | bytes 3145732
  121.6 2.0 %copy-start.9 = (bf16[128,2048]{1,0:T(8,128)(2,1)S(1)}, bf16[128,2048]{1,0:T(8,128)(2,1)}, u32[]{:S(2)}) copy-start(bf16[128,2048]{1,0:T(8,128)(2,1)} %copy-done.8) | copy-start | bytes 1572868
  121.7 2.1 %copy-start.11 = (bf16[128,2048]{1,0:T(8,128)(2,1)S(1)}, bf16[128,2048]{1,0:T(8,128)(2,1)}, u32[]{:S(2)}) copy-start(bf16[128,2048]{1,0:T(8,128)(2,1)} %copy-done.10) | copy-start | bytes 1572868
  121.7 9.5 %collective-permute-start.22 = (bf16[128,4096]{1,0:T(8,128)(2,1)S(1)}, bf16[128,4096]{1,0:T(8,128)(2,1)S(1)}, u32[]{:S(2)}, u32[]{:S(2)}) collective-permute-start(bf16[128,4096]{1,0:T(8,128)(2,1)S(1)} %join_columns.50.refs_0_), channel_id=1, source_target_pairs={{0,8},{8,0},{16,24},{24,16},{1,9},{9,1},{17,25},{25,17},{2,10},{10... | collective-permute-start | bytes 3145736 | tf_op jit(solution)/shard_map/ppermute | solution.py:24
  130.6 16.9 %collective-permute-start.27 = (bf16[128,2048]{1,0:T(8,128)(2,1)S(1)}, bf16[128,2048]{1,0:T(8,128)(2,1)S(1)}, u32[]{:S(2)}, u32[]{:S(2)}) collective-permute-start(bf16[128,2048]{1,0:T(8,128)(2,1)S(1)} %join_columns.49.refs_2_), channel_id=1, source_target_pairs={{0,1},{1,0},{2,3},{3,2},{4,5},{5,4},{6,7},{7,6},{8,9},{9,8},{10,11... | collective-permute-start | bytes 1572872 | tf_op jit(solution)/shard_map/ppermute | solution.py:24
  138.3 7.1 %collective-permute-start.24 = (bf16[128,1280]{1,0:T(8,128)(2,1)S(1)}, bf16[128,1280]{1,0:T(8,128)(2,1)S(1)}, u32[]{:S(2)}, u32[]{:S(2)}) collective-permute-start(bf16[128,1280]{1,0:T(8,128)(2,1)S(1)} %join_columns.51.refs_2_.refs_0_), channel_id=1, source_target_pairs={{0,16},{8,24},{16,0},{24,8},{1,17},{9,25},{17,1},{25,9},{2,18},{10... | collective-permute-start | bytes 983048 | tf_op jit(solution)/shard_map/ppermute | solution.py:24
  140.3 5.2 %collective-permute-start.25 = (bf16[128,8192]{1,0:T(8,128)(2,1)S(1)}, bf16[128,8192]{1,0:T(8,128)(2,1)S(1)}, u32[]{:S(2)}, u32[]{:S(2)}) collective-permute-start(bf16[128,8192]{1,0:T(8,128)(2,1)S(1)} %join_columns.52.refs_0_), channel_id=1, source_target_pairs={{0,8},{8,0},{16,24},{24,16},{1,9},{9,1},{17,25},{25,17},{2,10},{10... | collective-permute-start | bytes 6291464 | tf_op jit(solution)/shard_map/ppermute | solution.py:24
  145.4 11.4 %collective-permute-start.26 = (bf16[128,768]{1,0:T(8,128)(2,1)S(1)}, bf16[128,768]{1,0:T(8,128)(2,1)S(1)}, u32[]{:S(2)}, u32[]{:S(2)}) collective-permute-start(bf16[128,768]{1,0:T(8,128)(2,1)S(1)} %join_columns.53.refs_2_.refs_0_.refs_1_), channel_id=1, source_target_pairs={{0,16},{8,24},{16,0},{24,8},{1,17},{9,25},{17,1},{25,9},{2,18},{10... | collective-permute-start | bytes 589832 | tf_op jit(solution)/shard_map/ppermute | solution.py:24
  147.3 2.2 %copy-start.14 = (bf16[128,2048]{1,0:T(8,128)(2,1)S(1)}, bf16[128,2048]{1,0:T(8,128)(2,1)}, u32[]{:S(2)}) copy-start(bf16[128,2048]{1,0:T(8,128)(2,1)} %copy-done.13) | copy-start | bytes 1572868
  147.3 2.2 %collective-permute-start.28 = (bf16[128,2560]{1,0:T(8,128)(2,1)S(1)}, bf16[128,2560]{1,0:T(8,128)(2,1)S(1)}, u32[]{:S(2)}, u32[]{:S(2)}) collective-permute-start(bf16[128,2560]{1,0:T(8,128)(2,1)S(1)} %join_columns.54.refs_0_), channel_id=1, source_target_pairs={{0,8},{8,0},{16,24},{24,16},{1,9},{9,1},{17,25},{25,17},{2,10},{10... | collective-permute-start | bytes 1966088 | tf_op jit(solution)/shard_map/ppermute | solution.py:24
  156.9 1.8 %collective-permute-start.29 = (bf16[128,1536]{1,0:T(8,128)(2,1)S(1)}, bf16[128,1536]{1,0:T(8,128)(2,1)S(1)}, u32[]{:S(2)}, u32[]{:S(2)}) collective-permute-start(bf16[128,1536]{1,0:T(8,128)(2,1)S(1)} %join_columns.55), channel_id=1, source_target_pairs={{0,8},{8,0},{16,24},{24,16},{1,9},{9,1},{17,25},{25,17},{2,10},{10... | collective-permute-start | bytes 1179656 | tf_op jit(solution)/shard_map/ppermute | solution.py:24

commit v16 on v15

--- a/solution.py
+++ b/solution.py
@@ -313,7 +313,7 @@
         far_steps.append([block, None] if at % 2 == 0 else [None, block])
     far_steps += [[("wait", None), None], [None, ("wait", None)]]
     near = list(range(1, half))
-    near_steps = [near[:2], []] + [[d] for d in near[2:]]
+    near_steps = [near[:2], [], []] + [[d] for d in near[2:]]
     relayed = set()
 
     def rides(d):
@@ -420,6 +420,8 @@
             crossed.append(cross_before)
         earlier = [cross_before[2]] if cross_before is not None else []
         earlier += [core_before[1]] if core_before is not None else []
+        if step == 3:
+            earlier, arrivals = earlier + arrivals, []
         cross_before = None
         if ready:
             blocks = []
@@ -451,7 +453,7 @@
                 parts = [(outgoing[d], 0, own_width)]
                 if rides(d):
                     parts += cot_parts(0)
-                near_before.append((step + (3 if step else 1), d, send("tok", d, parts)[1]))
+                near_before.append((step + (2 if step else 1), d, send("tok", d, parts)[1]))
                 flying += 1
         before = [core_before[1]] if core_before else []
         finish_core()

time: 178 us -> 190 us (1.067)
  waiting for transfers between devices: 86.9 us -> 96.9 us
  starting transfers between devices: 43.6 us -> 46 us
    ppermute x30 -> x31, waiting for transfers between devices: 86.9 us -> 96.9 us  [exchange(): return lax.ppermute(block, axis, [(i, i ^ distance) for i in range(size)])]
    ppermute x30 -> x31, starting transfers between devices: 43.6 us -> 46 us  [exchange(): return lax.ppermute(block, axis, [(i, i ^ distance) for i in range(size)])]
  transfers between devices with their start and end apart: 30 -> 31, of which waited for: 12 -> 10; matrix products, arithmetic and copies ran while one was open for 0% -> 0% of each run, Pallas kernels for 12% -> 11%
where the time goes in v16:
time: 190 us; the launch traced here: 189 us
  waiting for transfers between devices  96.9 us (51%)
  starting transfers between devices  46 us (24%)
  Pallas kernels  30.1 us (16%)
  blocking collectives  9.44 us (5%)
  local copies, waits for them, and re-layouts  5.73 us (3%)
    ppermute x31, waiting for transfers between devices, exchange(): return lax.ppermute(block, axis, [(i, i ^ distance) for i in range(size)])  96.9 us
    ppermute x31, starting transfers between devices, exchange(): return lax.ppermute(block, axis, [(i, i ^ distance) for i in range(size)])  46 us
    pallas_call x4, Pallas kernels, product(): pl.pallas_call(functools.partial(product_kernel, left_places, right_place...  23.4 us
    all_to_all x1, blocking collectives, body(): lax.all_to_all(gradients[1][1], ('user', 'tok'), split_axis=0, concat_axi...  9.44 us
    unnamed x32, local copies, waits for them, and re-layouts  5.73 us
    pallas_call x1, Pallas kernels, combine(): pl.pallas_call(functools.partial(combine_kernel, user_count, clip_bound,...  4.82 us
  transfers between devices with their start and end apart: 31, of which 10 were waited for; matrix products, arithmetic and copies ran while one was open for 0% of the time, Pallas kernels for 11%

profile of v16, /device:TPU:0, one launch (start us, length us, event | category | flops | bytes accessed | tf_op | source)
XLA Modules:
  0.0 189.3 jit_solution(8257574915062389981)
XLA Ops:
  0.7 1.0 copy-done.15
  1.7 0.5 collective-permute-start
  2.3 2.6 %collective-permute-start.1 = (bf16[128,512]{1,0:T(8,128)(2,1)S(1)}, bf16[128,512]{1,0:T(8,128)(2,1)S(1)}, u32[]{:S(2)}, u32[]{:S(2)}) collective-permute-start(bf16[128,512]{1,0:T(8,128)(2,1)S(1)} %get-tuple-element.25), channel_id=1, source_target_pairs={{0,16},{8,24},{16,0},{24,8},{1,17},{9,25},{17,1},{25,9},{2,18},{10... | collective-permute-start | bytes 393224 | tf_op jit(solution)/shard_map/ppermute | solution.py:24
  4.8 0.1 collective-permute-start.2
  4.9 2.2 %copy-done.14 = bf16[1,128,16384]{2,1,0:T(8,128)(2,1)S(1)} copy-done((bf16[1,128,16384]{2,1,0:T(8,128)(2,1)S(1)}, bf16[1,128,16384]{2,1,0:T(8,128)(2,1)}, u32[]{:S(2)}) %copy-start.14) | copy-done | bytes 4194328
  7.1 0.4 pack_columns.1
  7.5 2.9 %collective-permute-start.8 = (bf16[128,2048]{1,0:T(8,128)(2,1)S(1)}, bf16[128,2048]{1,0:T(8,128)(2,1)S(1)}, u32[]{:S(2)}, u32[]{:S(2)}) collective-permute-start(bf16[128,2048]{1,0:T(8,128)(2,1)S(1)} %join_columns.29.refs_1_), channel_id=1, source_target_pairs={{0,4},{1,5},{2,6},{3,7},{4,0},{5,1},{6,2},{7,3},{8,12},{9,13},{10,... | collective-permute-start | bytes 1572872 | tf_op jit(solution)/shard_map/ppermute | solution.py:24
  10.4 1.6 collective-permute-start.5
  12.1 0.1 join_columns.33.refs_1_
  12.2 1.6 collective-permute-start.3
  13.8 1.6 collective-permute-start.4
  15.5 2.1 %collective-permute-start.10 = (bf16[128,2048]{1,0:T(8,128)(2,1)S(1)}, bf16[128,2048]{1,0:T(8,128)(2,1)S(1)}, u32[]{:S(2)}, u32[]{:S(2)}) collective-permute-start(bf16[128,2048]{1,0:T(8,128)(2,1)S(1)} %join_columns.32.refs_2_), channel_id=1, source_target_pairs={{0,4},{1,5},{2,6},{3,7},{4,0},{5,1},{6,2},{7,3},{8,12},{9,13},{10,... | collective-permute-start | bytes 1572872 | tf_op jit(solution)/shard_map/ppermute | solution.py:24
  17.6 6.8 %collective-permute-done.5.refs_3_.refs_1_.refs_6_.refs_8_ = bf16[128,2048]{1,0:T(8,128)(2,1)S(1)} collective-permute-done((bf16[128,2048]{1,0:T(8,128)(2,1)S(1)}, bf16[128,2048]{1,0:T(8,128)(2,1)S(1)}, u32[]{:S(2)}, u32[]{:S(2)}) %collective-permute-start.5) | collective-permute-done | bytes 524320 | tf_op jit(solution)/shard_map/ppermute | solution.py:24
  24.4 14.1 %collective-permute-done.4.refs_1_ = bf16[128,2048]{1,0:T(8,128)(2,1)S(1)} collective-permute-done((bf16[128,2048]{1,0:T(8,128)(2,1)S(1)}, bf16[128,2048]{1,0:T(8,128)(2,1)S(1)}, u32[]{:S(2)}, u32[]{:S(2)}) %collective-permute-start.4) | collective-permute-done | bytes 524320 | tf_op jit(solution)/shard_map/ppermute | solution.py:24
  38.5 0.1 join_columns.35.refs_1_.refs_0_
  38.6 1.6 collective-permute-start.6
  40.2 0.2 collective-permute-start.7
  40.4 0.1 join_columns.37.refs_0_
  40.5 0.1 collective-permute-start.9
  40.6 4.7 %collective-permute-start.16 = (bf16[128,2048]{1,0:T(8,128)(2,1)S(1)}, bf16[128,2048]{1,0:T(8,128)(2,1)S(1)}, u32[]{:S(2)}, u32[]{:S(2)}) collective-permute-start(bf16[128,2048]{1,0:T(8,128)(2,1)S(1)} %join_columns.38.refs_1_), channel_id=1, source_target_pairs={{0,5},{1,4},{2,7},{3,6},{4,1},{5,0},{6,3},{7,2},{8,13},{9,12},{10,... | collective-permute-start | bytes 1572872 | tf_op jit(solution)/shard_map/ppermute | solution.py:24
  45.3 17.3 %collective-permute-done.6.refs_2_.refs_1_.refs_7_.refs_9_ = bf16[128,4096]{1,0:T(8,128)(2,1)S(1)} collective-permute-done((bf16[128,4096]{1,0:T(8,128)(2,1)S(1)}, bf16[128,4096]{1,0:T(8,128)(2,1)S(1)}, u32[]{:S(2)}, u32[]{:S(2)}) %collective-permute-start.6) | collective-permute-done | bytes 1048608 | tf_op jit(solution)/shard_map/ppermute | solution.py:24
  62.7 1.8 collective-permute-start.12
  64.5 0.6 collective-permute-start.14
  65.1 0.1 join_columns.41.refs_0_
  65.3 0.1 collective-permute-start.13
  65.4 5.2 %collective-permute-start.11 = (bf16[128,2048]{1,0:T(8,128)(2,1)S(1)}, bf16[128,2048]{1,0:T(8,128)(2,1)S(1)}, u32[]{:S(2)}, u32[]{:S(2)}) collective-permute-start(bf16[128,2048]{1,0:T(8,128)(2,1)S(1)} %join_columns.42.refs_1_), channel_id=1, source_target_pairs={{0,6},{1,7},{2,4},{3,5},{4,2},{5,3},{6,0},{7,1},{8,14},{9,15},{10,... | collective-permute-start | bytes 1572872 | tf_op jit(solution)/shard_map/ppermute | solution.py:24
  70.6 8.8 %collective-permute-done.14.refs_4_.refs_9_.refs_6_ = bf16[128,2048]{1,0:T(8,128)(2,1)S(1)} collective-permute-done((bf16[128,2048]{1,0:T(8,128)(2,1)S(1)}, bf16[128,2048]{1,0:T(8,128)(2,1)S(1)}, u32[]{:S(2)}, u32[]{:S(2)}) %collective-permute-start.14) | collective-permute-done | bytes 524320 | tf_op jit(solution)/shard_map/ppermute | solution.py:24
  79.4 2.5 %collective-permute-start.22 = (bf16[128,2048]{1,0:T(8,128)(2,1)S(1)}, bf16[128,2048]{1,0:T(8,128)(2,1)S(1)}, u32[]{:S(2)}, u32[]{:S(2)}) collective-permute-start(bf16[128,2048]{1,0:T(8,128)(2,1)S(1)} %join_columns.43.refs_1_), channel_id=1, source_target_pairs={{0,2},{1,3},{2,0},{3,1},{4,6},{5,7},{6,4},{7,5},{8,10},{9,11},{10,... | collective-permute-start | bytes 1572872 | tf_op jit(solution)/shard_map/ppermute | solution.py:24
  81.9 0.1 collective-permute-start.15
  82.0 0.1 join_columns.45.refs_0_
  82.1 0.1 collective-permute-start.17
  82.2 9.8 %collective-permute-done.16.refs_2_.refs_0_ = bf16[128,2048]{1,0:T(8,128)(2,1)S(1)} collective-permute-done((bf16[128,2048]{1,0:T(8,128)(2,1)S(1)}, bf16[128,2048]{1,0:T(8,128)(2,1)S(1)}, u32[]{:S(2)}, u32[]{:S(2)}) %collective-permute-start.16) | collective-permute-done | bytes 524320 | tf_op jit(solution)/shard_map/ppermute | solution.py:24
  92.0 3.0 %collective-permute-start.21 = (bf16[128,1280]{1,0:T(8,128)(2,1)S(1)}, bf16[128,1280]{1,0:T(8,128)(2,1)S(1)}, u32[]{:S(2)}, u32[]{:S(2)}) collective-permute-start(bf16[128,1280]{1,0:T(8,128)(2,1)S(1)} %join_columns.46.refs_1_), channel_id=1, source_target_pairs={{0,7},{1,6},{2,5},{3,4},{4,3},{5,2},{6,1},{7,0},{8,15},{9,14},{10,... | collective-permute-start | bytes 983048 | tf_op jit(solution)/shard_map/ppermute | solution.py:24
  95.1 1.6 collective-permute-start.18
  96.7 1.6 collective-permute-start.24
  98.3 22.7 %collective-permute-done.15.refs_1_ = bf16[128,2048]{1,0:T(8,128)(2,1)S(1)} collective-permute-done((bf16[128,2048]{1,0:T(8,128)(2,1)S(1)}, bf16[128,2048]{1,0:T(8,128)(2,1)S(1)}, u32[]{:S(2)}, u32[]{:S(2)}) %collective-permute-start.15) | collective-permute-done | bytes 524320 | tf_op jit(solution)/shard_map/ppermute | solution.py:24
  121.0 3.4 %collective-permute-start.19 = (bf16[128,768]{1,0:T(8,128)(2,1)S(1)}, bf16[128,768]{1,0:T(8,128)(2,1)S(1)}, u32[]{:S(2)}, u32[]{:S(2)}) collective-permute-start(bf16[128,768]{1,0:T(8,128)(2,1)S(1)} %join_columns.49.refs_2_), channel_id=1, source_target_pairs={{0,7},{1,6},{2,5},{3,4},{4,3},{5,2},{6,1},{7,0},{8,15},{9,14},{10,... | collective-permute-start | bytes 589832 | tf_op jit(solution)/shard_map/ppermute | solution.py:24
  124.5 1.6 collective-permute-start.20
  126.1 0.1 join_columns.52.refs_0_
  126.2 0.1 collective-permute-start.23
  126.3 1.1 copy-done.1
  127.4 0.1 copy-done.3
  127.5 0.2 copy-done.5
  127.7 0.3 copy-done.7
  128.0 0.3 copy-done.9
  128.4 0.3 copy-done.11
  128.7 0.1 copy-done.13
  128.8 6.8 %product_and_squares.4.refs_2_.refs_13_ = f32[4,1280,512]{2,1,0:T(8,128)S(1)} custom-call(bf16[128,2048]{1,0:T(8,128)(2,1)S(1)} %copy-done.3, bf16[128,4096]{1,0:T(8,128)(2,1)S(1)} %copy-done.1, bf16[128,2048]{1,0:T(8,128)(2,1)S(1)} %join_columns.39.refs_1_.refs_0_.refs_2_, bf16[128,4096]{1,0:T(8,128)(2,1)S(1)} %copy-done.9, ...), custom_call_target="tpu_custom_call" | custom-call | flops 2684354560 | bytes 7340032 | tf_op jit(solution)/shard_map/product_and_squares/pallas_call | solution.py:197
  135.6 1.6 collective-permute-start.28
  137.2 12.1 %collective-permute-done.20.refs_3_.refs_1_.refs_6_.refs_4_ = bf16[128,4096]{1,0:T(8,128)(2,1)S(1)} collective-permute-done((bf16[128,4096]{1,0:T(8,128)(2,1)S(1)}, bf16[128,4096]{1,0:T(8,128)(2,1)S(1)}, u32[]{:S(2)}, u32[]{:S(2)}) %collective-permute-start.20) | collective-permute-done | bytes 1048608 | tf_op jit(solution)/shard_map/ppermute | solution.py:24
  149.3 1.6 collective-permute-start.25
  150.9 0.1 join_columns.54.refs_0_
  151.0 0.1 collective-permute-start.26
  151.1 5.0 %product_and_squares.5.refs_2_.refs_9_ = f32[4,768,512]{2,1,0:T(8,128)S(1)} custom-call(bf16[128,2048]{1,0:T(8,128)(2,1)S(1)} %copy-done.3, bf16[128,4096]{1,0:T(8,128)(2,1)S(1)} %copy-done.1, bf16[128,2048]{1,0:T(8,128)(2,1)S(1)} %join_columns.39.refs_1_.refs_0_.refs_2_, bf16[128,2048]{1,0:T(8,128)(2,1)S(1)} %join_columns.47.refs_1_.refs_0_.refs_3_, ...), custom_call_target="tpu_custom_call" | custom-call | flops 2013265920 | bytes 6553600 | tf_op jit(solution)/shard_map/product_and_squares/pallas_call | solution.py:197
  156.1 1.6 collective-permute-done.25.refs_3_.refs_1_.refs_8_
  157.8 1.6 collective-permute-start.27
  159.4 0.1 collective-permute-start.29
  159.5 2.1 %collective-permute-done.29.refs_5_ = bf16[128,2560]{1,0:T(8,128)(2,1)S(1)} collective-permute-done((bf16[128,2560]{1,0:T(8,128)(2,1)S(1)}, bf16[128,2560]{1,0:T(8,128)(2,1)S(1)}, u32[]{:S(2)}, u32[]{:S(2)}) %collective-permute-start.29) | collective-permute-done | bytes 655392 | tf_op jit(solution)/shard_map/ppermute | solution.py:24
  161.6 7.3 %product_and_squares.6 = (f32[4,1280,512]{2,1,0:T(8,128)S(1)}, f32[1,8,128]{2,1,0:T(8,128)S(1)}) custom-call(bf16[128,4096]{1,0:T(8,128)(2,1)S(1)} %join_columns.50.refs_1_.refs_0_, bf16[128,2048]{1,0:T(8,128)(2,1)S(1)} %join_columns.47.refs_1_.refs_0_.refs_3_, bf16[128,1280]{1,0:T(8,128)(2,1)S(1)} %join_columns.53.refs_2_.refs_0_, ...), custom_call_target="tpu_custom_call", output_to_operand_aliasing={{0}: (13, {})} | custom-call | flops 2684354560 | bytes 7340032 | tf_op jit(solution)/shard_map/product_and_squares/pallas_call | solution.py:197
  168.9 0.2 collective-permute-start.30
  169.1 1.6 collective-permute-done.30.refs_3_
  170.7 4.3 %product_and_squares.7 = (f32[4,768,512]{2,1,0:T(8,128)S(1)}, f32[32,8,128]{2,1,0:T(8,128)S(1)}) custom-call(bf16[128,4096]{1,0:T(8,128)(2,1)S(1)} %join_columns.50.refs_1_.refs_0_, bf16[128,768]{1,0:T(8,128)(2,1)S(1)} %join_columns.55.refs_2_.refs_0_.refs_1_, ...), custom_call_target="tpu_custom_call", output_to_operand_aliasing={{0}: (9, {})} | custom-call | flops 1207959552 | bytes 3932160 | tf_op jit(solution)/shard_map/product_and_squares/pallas_call | solution.py:197
  175.0 9.4 %all_to_all.5.sums_ref = f32[32,8,128]{2,1,0:T(8,128)S(1)} all-to-all(f32[32,8,128]{2,1,0:T(8,128)S(1)} %get-tuple-element.35), channel_id=1, replica_groups=mesh['user'=4,'tok'=8] {'user','tok'}, dimensions={0} | all-to-all | bytes 262144 | tf_op jit(solution)/shard_map/all_to_all | solution.py:481
  184.5 4.8 %weighted_sum.1 = f32[2048,512]{1,0:T(8,128)} custom-call(s32[1]{0:T(128)} %bitcast.user_ref, f32[32,8,128]{2,1,0:T(8,128)S(1)} %all_to_all.5.sums_ref, f32[4,1280,512]{2,1,0:T(8,128)S(1)} %get-tuple-element.33.refs_3_.refs_0_, f32[4,768,512]{2,1,0:T(8,128)S(1)} %get-tuple-element.36.refs_1_), custom_call_target="tpu_custom_call" | custom-call | tf_op jit(solution)/shard_map/weighted_sum/pallas_call | solution.py:254
  (75 shorter events, 0.9 us)
Async XLA Ops:
  0.7 1.0 copy-start.15
  1.7 10.3 %collective-permute-start = (bf16[128,512]{1,0:T(8,128)(2,1)S(1)}, bf16[128,512]{1,0:T(8,128)(2,1)S(1)}, u32[]{:S(2)}, u32[]{:S(2)}) collective-permute-start(bf16[128,512]{1,0:T(8,128)(2,1)S(1)} %get-tuple-element.24), channel_id=1, source_target_pairs={{0,8},{8,0},{16,24},{24,16},{1,9},{9,1},{17,25},{25,17},{2,10},{10... | collective-permute-start | bytes 393224 | tf_op jit(solution)/shard_map/ppermute | solution.py:24
  2.3 9.7 %collective-permute-start.1 = (bf16[128,512]{1,0:T(8,128)(2,1)S(1)}, bf16[128,512]{1,0:T(8,128)(2,1)S(1)}, u32[]{:S(2)}, u32[]{:S(2)}) collective-permute-start(bf16[128,512]{1,0:T(8,128)(2,1)S(1)} %get-tuple-element.25), channel_id=1, source_target_pairs={{0,16},{8,24},{16,0},{24,8},{1,17},{9,25},{17,1},{25,9},{2,18},{10... | collective-permute-start | bytes 393224 | tf_op jit(solution)/shard_map/ppermute | solution.py:24
  4.8 7.2 %collective-permute-start.2 = (bf16[128,512]{1,0:T(8,128)(2,1)S(1)}, bf16[128,512]{1,0:T(8,128)(2,1)S(1)}, u32[]{:S(2)}, u32[]{:S(2)}) collective-permute-start(bf16[128,512]{1,0:T(8,128)(2,1)S(1)} %get-tuple-element.26), channel_id=1, source_target_pairs={{0,24},{8,16},{16,8},{24,0},{1,25},{9,17},{17,9},{25,1},{2,26},{10... | collective-permute-start | bytes 393224 | tf_op jit(solution)/shard_map/ppermute | solution.py:24
  4.9 2.2 %copy-start.14 = (bf16[1,128,16384]{2,1,0:T(8,128)(2,1)S(1)}, bf16[1,128,16384]{2,1,0:T(8,128)(2,1)}, u32[]{:S(2)}) copy-start(bf16[1,128,16384]{2,1,0:T(8,128)(2,1)} %hidden_ref.1) | copy-start | bytes 12582916
  7.5 33.1 %collective-permute-start.8 = (bf16[128,2048]{1,0:T(8,128)(2,1)S(1)}, bf16[128,2048]{1,0:T(8,128)(2,1)S(1)}, u32[]{:S(2)}, u32[]{:S(2)}) collective-permute-start(bf16[128,2048]{1,0:T(8,128)(2,1)S(1)} %join_columns.29.refs_1_), channel_id=1, source_target_pairs={{0,4},{1,5},{2,6},{3,7},{4,0},{5,1},{6,2},{7,3},{8,12},{9,13},{10,... | collective-permute-start | bytes 1572872 | tf_op jit(solution)/shard_map/ppermute | solution.py:24
  10.4 30.0 %copy-start.2 = (bf16[128,2048]{1,0:T(8,128)(2,1)}, bf16[128,2048]{1,0:T(8,128)(2,1)S(1)}, u32[]{:S(2)}) copy-start(bf16[128,2048]{1,0:T(8,128)(2,1)S(1)} %join_columns.30.refs_4_.refs_1_.refs_0_) | copy-start | bytes 1572868
  10.4 14.0 %collective-permute-start.5 = (bf16[128,2048]{1,0:T(8,128)(2,1)S(1)}, bf16[128,2048]{1,0:T(8,128)(2,1)S(1)}, u32[]{:S(2)}, u32[]{:S(2)}) collective-permute-start(bf16[128,2048]{1,0:T(8,128)(2,1)S(1)} %join_columns.30.refs_4_.refs_1_.refs_0_), channel_id=1, source_target_pairs={{0,16},{8,24},{16,0},{24,8},{1,17},{9,25},{17,1},{25,9},{2,18},{10... | collective-permute-start | bytes 1572872 | tf_op jit(solution)/shard_map/ppermute | solution.py:24
  12.1 26.5 %copy-start.4 = (bf16[128,2048]{1,0:T(8,128)(2,1)}, bf16[128,2048]{1,0:T(8,128)(2,1)S(1)}, u32[]{:S(2)}) copy-start(bf16[128,2048]{1,0:T(8,128)(2,1)S(1)} %join_columns.31.refs_0_.refs_1_.refs_9_.refs_12_) | copy-start | bytes 1572868
  12.2 26.3 %collective-permute-start.3 = (bf16[128,4096]{1,0:T(8,128)(2,1)S(1)}, bf16[128,4096]{1,0:T(8,128)(2,1)S(1)}, u32[]{:S(2)}, u32[]{:S(2)}) collective-permute-start(bf16[128,4096]{1,0:T(8,128)(2,1)S(1)} %join_columns.33.refs_1_), channel_id=1, source_target_pairs={{0,1},{1,0},{2,3},{3,2},{4,5},{5,4},{6,7},{7,6},{8,9},{9,8},{10,11... | collective-permute-start | bytes 3145736 | tf_op jit(solution)/shard_map/ppermute | solution.py:24
  13.8 24.6 %collective-permute-start.4 = (bf16[128,2048]{1,0:T(8,128)(2,1)S(1)}, bf16[128,2048]{1,0:T(8,128)(2,1)S(1)}, u32[]{:S(2)}, u32[]{:S(2)}) collective-permute-start(bf16[128,2048]{1,0:T(8,128)(2,1)S(1)} %join_columns.34.refs_0_), channel_id=1, source_target_pairs={{0,2},{1,3},{2,0},{3,1},{4,6},{5,7},{6,4},{7,5},{8,10},{9,11},{10,... | collective-permute-start | bytes 1572872 | tf_op jit(solution)/shard_map/ppermute | solution.py:24
  15.5 49.9 %collective-permute-start.10 = (bf16[128,2048]{1,0:T(8,128)(2,1)S(1)}, bf16[128,2048]{1,0:T(8,128)(2,1)S(1)}, u32[]{:S(2)}, u32[]{:S(2)}) collective-permute-start(bf16[128,2048]{1,0:T(8,128)(2,1)S(1)} %join_columns.32.refs_2_), channel_id=1, source_target_pairs={{0,4},{1,5},{2,6},{3,7},{4,0},{5,1},{6,2},{7,3},{8,12},{9,13},{10,... | collective-permute-start | bytes 1572872 | tf_op jit(solution)/shard_map/ppermute | solution.py:24
  24.4 16.2 %copy-start.12 = (bf16[128,2048]{1,0:T(8,128)(2,1)}, bf16[128,2048]{1,0:T(8,128)(2,1)S(1)}, u32[]{:S(2)}) copy-start(bf16[128,2048]{1,0:T(8,128)(2,1)S(1)} %collective-permute-done.5.refs_3_.refs_1_.refs_6_.refs_8_) | copy-start | bytes 1572868
  38.5 2.1 %copy-start.10 = (bf16[128,4096]{1,0:T(8,128)(2,1)}, bf16[128,4096]{1,0:T(8,128)(2,1)S(1)}, u32[]{:S(2)}) copy-start(bf16[128,4096]{1,0:T(8,128)(2,1)S(1)} %collective-permute-done.3.refs_0_.refs_10_.refs_13_) | copy-start | bytes 3145732
  38.6 26.6 %copy-start = (bf16[128,4096]{1,0:T(8,128)(2,1)}, bf16[128,4096]{1,0:T(8,128)(2,1)S(1)}, u32[]{:S(2)}) copy-start(bf16[128,4096]{1,0:T(8,128)(2,1)S(1)} %join_columns.35.refs_1_.refs_0_) | copy-start | bytes 3145732
  38.6 24.0 %collective-permute-start.6 = (bf16[128,4096]{1,0:T(8,128)(2,1)S(1)}, bf16[128,4096]{1,0:T(8,128)(2,1)S(1)}, u32[]{:S(2)}, u32[]{:S(2)}) collective-permute-start(bf16[128,4096]{1,0:T(8,128)(2,1)S(1)} %join_columns.35.refs_1_.refs_0_), channel_id=1, source_target_pairs={{0,16},{8,24},{16,0},{24,8},{1,17},{9,25},{17,1},{25,9},{2,18},{10... | collective-permute-start | bytes 3145736 | tf_op jit(solution)/shard_map/ppermute | solution.py:24
  40.2 24.3 %collective-permute-start.7 = (bf16[128,2048]{1,0:T(8,128)(2,1)S(1)}, bf16[128,2048]{1,0:T(8,128)(2,1)S(1)}, u32[]{:S(2)}, u32[]{:S(2)}) collective-permute-start(bf16[128,2048]{1,0:T(8,128)(2,1)S(1)} %join_columns.36.refs_2_), channel_id=1, source_target_pairs={{0,2},{1,3},{2,0},{3,1},{4,6},{5,7},{6,4},{7,5},{8,10},{9,11},{10,... | collective-permute-start | bytes 1572872 | tf_op jit(solution)/shard_map/ppermute | solution.py:24
  40.5 4.9 %collective-permute-start.9 = (bf16[128,4096]{1,0:T(8,128)(2,1)S(1)}, bf16[128,4096]{1,0:T(8,128)(2,1)S(1)}, u32[]{:S(2)}, u32[]{:S(2)}) collective-permute-start(bf16[128,4096]{1,0:T(8,128)(2,1)S(1)} %join_columns.37.refs_0_), channel_id=1, source_target_pairs={{0,8},{8,0},{16,24},{24,16},{1,9},{9,1},{17,25},{25,17},{2,10},{10... | collective-permute-start | bytes 3145736 | tf_op jit(solution)/shard_map/ppermute | solution.py:24
  40.6 51.4 %collective-permute-start.16 = (bf16[128,2048]{1,0:T(8,128)(2,1)S(1)}, bf16[128,2048]{1,0:T(8,128)(2,1)S(1)}, u32[]{:S(2)}, u32[]{:S(2)}) collective-permute-start(bf16[128,2048]{1,0:T(8,128)(2,1)S(1)} %join_columns.38.refs_1_), channel_id=1, source_target_pairs={{0,5},{1,4},{2,7},{3,6},{4,1},{5,0},{6,3},{7,2},{8,13},{9,12},{10,... | collective-permute-start | bytes 1572872 | tf_op jit(solution)/shard_map/ppermute | solution.py:24
  45.3 19.9 %copy-start.8 = (bf16[128,4096]{1,0:T(8,128)(2,1)}, bf16[128,4096]{1,0:T(8,128)(2,1)S(1)}, u32[]{:S(2)}) copy-start(bf16[128,4096]{1,0:T(8,128)(2,1)S(1)} %collective-permute-done.9.refs_3_.refs_4_) | copy-start | bytes 3145732
  62.6 2.6 %copy-start.6 = (bf16[128,4096]{1,0:T(8,128)(2,1)}, bf16[128,4096]{1,0:T(8,128)(2,1)S(1)}, u32[]{:S(2)}) copy-start(bf16[128,4096]{1,0:T(8,128)(2,1)S(1)} %collective-permute-done.6.refs_2_.refs_1_.refs_7_.refs_9_) | copy-start | bytes 3145732
  62.7 16.7 %collective-permute-start.12 = (bf16[128,2048]{1,0:T(8,128)(2,1)S(1)}, bf16[128,2048]{1,0:T(8,128)(2,1)S(1)}, u32[]{:S(2)}, u32[]{:S(2)}) collective-permute-start(bf16[128,2048]{1,0:T(8,128)(2,1)S(1)} %join_columns.39.refs_1_.refs_0_.refs_2_), channel_id=1, source_target_pairs={{0,16},{8,24},{16,0},{24,8},{1,17},{9,25},{17,1},{25,9},{2,18},{10... | collective-permute-start | bytes 1572872 | tf_op jit(solution)/shard_map/ppermute | solution.py:24
  64.5 14.8 %collective-permute-start.14 = (bf16[128,2048]{1,0:T(8,128)(2,1)S(1)}, bf16[128,2048]{1,0:T(8,128)(2,1)S(1)}, u32[]{:S(2)}, u32[]{:S(2)}) collective-permute-start(bf16[128,2048]{1,0:T(8,128)(2,1)S(1)} %join_columns.40.refs_2_), channel_id=1, source_target_pairs={{0,1},{1,0},{2,3},{3,2},{4,5},{5,4},{6,7},{7,6},{8,9},{9,8},{10,11... | collective-permute-start | bytes 1572872 | tf_op jit(solution)/shard_map/ppermute | solution.py:24
  65.3 14.1 %collective-permute-start.13 = (bf16[128,8192]{1,0:T(8,128)(2,1)S(1)}, bf16[128,8192]{1,0:T(8,128)(2,1)S(1)}, u32[]{:S(2)}, u32[]{:S(2)}) collective-permute-start(bf16[128,8192]{1,0:T(8,128)(2,1)S(1)} %join_columns.41.refs_0_), channel_id=1, source_target_pairs={{0,8},{8,0},{16,24},{24,16},{1,9},{9,1},{17,25},{25,17},{2,10},{10... | collective-permute-start | bytes 6291464 | tf_op jit(solution)/shard_map/ppermute | solution.py:24
  65.4 31.3 %collective-permute-start.11 = (bf16[128,2048]{1,0:T(8,128)(2,1)S(1)}, bf16[128,2048]{1,0:T(8,128)(2,1)S(1)}, u32[]{:S(2)}, u32[]{:S(2)}) collective-permute-start(bf16[128,2048]{1,0:T(8,128)(2,1)S(1)} %join_columns.42.refs_1_), channel_id=1, source_target_pairs={{0,6},{1,7},{2,4},{3,5},{4,2},{5,3},{6,0},{7,1},{8,14},{9,15},{10,... | collective-permute-start | bytes 1572872 | tf_op jit(solution)/shard_map/ppermute | solution.py:24
  79.4 46.6 %collective-permute-start.22 = (bf16[128,2048]{1,0:T(8,128)(2,1)S(1)}, bf16[128,2048]{1,0:T(8,128)(2,1)S(1)}, u32[]{:S(2)}, u32[]{:S(2)}) collective-permute-start(bf16[128,2048]{1,0:T(8,128)(2,1)S(1)} %join_columns.43.refs_1_), channel_id=1, source_target_pairs={{0,2},{1,3},{2,0},{3,1},{4,6},{5,7},{6,4},{7,5},{8,10},{9,11},{10,... | collective-permute-start | bytes 1572872 | tf_op jit(solution)/shard_map/ppermute | solution.py:24
  81.9 39.0 %collective-permute-start.15 = (bf16[128,2048]{1,0:T(8,128)(2,1)S(1)}, bf16[128,2048]{1,0:T(8,128)(2,1)S(1)}, u32[]{:S(2)}, u32[]{:S(2)}) collective-permute-start(bf16[128,2048]{1,0:T(8,128)(2,1)S(1)} %join_columns.44.refs_2_), channel_id=1, source_target_pairs={{0,3},{1,2},{2,1},{3,0},{4,7},{5,6},{6,5},{7,4},{8,11},{9,10},{10,... | collective-permute-start | bytes 1572872 | tf_op jit(solution)/shard_map/ppermute | solution.py:24
  82.1 12.9 %collective-permute-start.17 = (bf16[128,4096]{1,0:T(8,128)(2,1)S(1)}, bf16[128,4096]{1,0:T(8,128)(2,1)S(1)}, u32[]{:S(2)}, u32[]{:S(2)}) collective-permute-start(bf16[128,4096]{1,0:T(8,128)(2,1)S(1)} %join_columns.45.refs_0_), channel_id=1, source_target_pairs={{0,8},{8,0},{16,24},{24,16},{1,9},{9,1},{17,25},{25,17},{2,10},{10... | collective-permute-start | bytes 3145736 | tf_op jit(solution)/shard_map/ppermute | solution.py:24
  92.0 43.6 %collective-permute-start.21 = (bf16[128,1280]{1,0:T(8,128)(2,1)S(1)}, bf16[128,1280]{1,0:T(8,128)(2,1)S(1)}, u32[]{:S(2)}, u32[]{:S(2)}) collective-permute-start(bf16[128,1280]{1,0:T(8,128)(2,1)S(1)} %join_columns.46.refs_1_), channel_id=1, source_target_pairs={{0,7},{1,6},{2,5},{3,4},{4,3},{5,2},{6,1},{7,0},{8,15},{9,14},{10,... | collective-permute-start | bytes 983048 | tf_op jit(solution)/shard_map/ppermute | solution.py:24
  95.1 29.4 %collective-permute-start.18 = (bf16[128,2048]{1,0:T(8,128)(2,1)S(1)}, bf16[128,2048]{1,0:T(8,128)(2,1)S(1)}, u32[]{:S(2)}, u32[]{:S(2)}) collective-permute-start(bf16[128,2048]{1,0:T(8,128)(2,1)S(1)} %join_columns.47.refs_1_.refs_0_.refs_3_), channel_id=1, source_target_pairs={{0,16},{8,24},{16,0},{24,8},{1,17},{9,25},{17,1},{25,9},{2,18},{10... | collective-permute-start | bytes 1572872 | tf_op jit(solution)/shard_map/ppermute | solution.py:24
  96.7 54.4 %collective-permute-start.24 = (bf16[128,2048]{1,0:T(8,128)(2,1)S(1)}, bf16[128,2048]{1,0:T(8,128)(2,1)S(1)}, u32[]{:S(2)}, u32[]{:S(2)}) collective-permute-start(bf16[128,2048]{1,0:T(8,128)(2,1)S(1)} %join_columns.48.refs_0_), channel_id=1, source_target_pairs={{0,1},{1,0},{2,3},{3,2},{4,5},{5,4},{6,7},{7,6},{8,9},{9,8},{10,11... | collective-permute-start | bytes 1572872 | tf_op jit(solution)/shard_map/ppermute | solution.py:24
  121.0 35.1 %collective-permute-start.19 = (bf16[128,768]{1,0:T(8,128)(2,1)S(1)}, bf16[128,768]{1,0:T(8,128)(2,1)S(1)}, u32[]{:S(2)}, u32[]{:S(2)}) collective-permute-start(bf16[128,768]{1,0:T(8,128)(2,1)S(1)} %join_columns.49.refs_2_), channel_id=1, source_target_pairs={{0,7},{1,6},{2,5},{3,4},{4,3},{5,2},{6,1},{7,0},{8,15},{9,14},{10,... | collective-permute-start | bytes 589832 | tf_op jit(solution)/shard_map/ppermute | solution.py:24
  124.5 24.8 %collective-permute-start.20 = (bf16[128,4096]{1,0:T(8,128)(2,1)S(1)}, bf16[128,4096]{1,0:T(8,128)(2,1)S(1)}, u32[]{:S(2)}, u32[]{:S(2)}) collective-permute-start(bf16[128,4096]{1,0:T(8,128)(2,1)S(1)} %join_columns.50.refs_1_.refs_0_), channel_id=1, source_target_pairs={{0,16},{8,24},{16,0},{24,8},{1,17},{9,25},{17,1},{25,9},{2,18},{10... | collective-permute-start | bytes 3145736 | tf_op jit(solution)/shard_map/ppermute | solution.py:24
  126.2 1.2 copy-start.1
  126.2 1.3 copy-start.3
  126.2 1.5 copy-start.5
  126.2 1.8 copy-start.7
  126.2 2.1 %copy-start.9 = (bf16[128,4096]{1,0:T(8,128)(2,1)S(1)}, bf16[128,4096]{1,0:T(8,128)(2,1)}, u32[]{:S(2)}) copy-start(bf16[128,4096]{1,0:T(8,128)(2,1)} %copy-done.8) | copy-start | bytes 3145732
  126.2 2.5 %copy-start.11 = (bf16[128,4096]{1,0:T(8,128)(2,1)S(1)}, bf16[128,4096]{1,0:T(8,128)(2,1)}, u32[]{:S(2)}) copy-start(bf16[128,4096]{1,0:T(8,128)(2,1)} %copy-done.10) | copy-start | bytes 3145732
  126.2 2.6 %copy-start.13 = (bf16[128,2048]{1,0:T(8,128)(2,1)S(1)}, bf16[128,2048]{1,0:T(8,128)(2,1)}, u32[]{:S(2)}) copy-start(bf16[128,2048]{1,0:T(8,128)(2,1)} %copy-done.12) | copy-start | bytes 1572868
  126.2 11.0 %collective-permute-start.23 = (bf16[128,4096]{1,0:T(8,128)(2,1)S(1)}, bf16[128,4096]{1,0:T(8,128)(2,1)S(1)}, u32[]{:S(2)}, u32[]{:S(2)}) collective-permute-start(bf16[128,4096]{1,0:T(8,128)(2,1)S(1)} %join_columns.52.refs_0_), channel_id=1, source_target_pairs={{0,8},{8,0},{16,24},{24,16},{1,9},{9,1},{17,25},{25,17},{2,10},{10... | collective-permute-start | bytes 3145736 | tf_op jit(solution)/shard_map/ppermute | solution.py:24
  135.6 23.9 %collective-permute-start.28 = (bf16[128,2048]{1,0:T(8,128)(2,1)S(1)}, bf16[128,2048]{1,0:T(8,128)(2,1)S(1)}, u32[]{:S(2)}, u32[]{:S(2)}) collective-permute-start(bf16[128,2048]{1,0:T(8,128)(2,1)S(1)} %join_columns.51.refs_2_), channel_id=1, source_target_pairs={{0,1},{1,0},{2,3},{3,2},{4,5},{5,4},{6,7},{7,6},{8,9},{9,8},{10,11... | collective-permute-start | bytes 1572872 | tf_op jit(solution)/shard_map/ppermute | solution.py:24
  149.3 8.5 %collective-permute-start.25 = (bf16[128,1280]{1,0:T(8,128)(2,1)S(1)}, bf16[128,1280]{1,0:T(8,128)(2,1)S(1)}, u32[]{:S(2)}, u32[]{:S(2)}) collective-permute-start(bf16[128,1280]{1,0:T(8,128)(2,1)S(1)} %join_columns.53.refs_2_.refs_0_), channel_id=1, source_target_pairs={{0,16},{8,24},{16,0},{24,8},{1,17},{9,25},{17,1},{25,9},{2,18},{10... | collective-permute-start | bytes 983048 | tf_op jit(solution)/shard_map/ppermute | solution.py:24
  151.0 6.8 %collective-permute-start.26 = (bf16[128,8192]{1,0:T(8,128)(2,1)S(1)}, bf16[128,8192]{1,0:T(8,128)(2,1)S(1)}, u32[]{:S(2)}, u32[]{:S(2)}) collective-permute-start(bf16[128,8192]{1,0:T(8,128)(2,1)S(1)} %join_columns.54.refs_0_), channel_id=1, source_target_pairs={{0,8},{8,0},{16,24},{24,16},{1,9},{9,1},{17,25},{25,17},{2,10},{10... | collective-permute-start | bytes 6291464 | tf_op jit(solution)/shard_map/ppermute | solution.py:24
  157.8 11.1 %collective-permute-start.27 = (bf16[128,768]{1,0:T(8,128)(2,1)S(1)}, bf16[128,768]{1,0:T(8,128)(2,1)S(1)}, u32[]{:S(2)}, u32[]{:S(2)}) collective-permute-start(bf16[128,768]{1,0:T(8,128)(2,1)S(1)} %join_columns.55.refs_2_.refs_0_.refs_1_), channel_id=1, source_target_pairs={{0,16},{8,24},{16,0},{24,8},{1,17},{9,25},{17,1},{25,9},{2,18},{10... | collective-permute-start | bytes 589832 | tf_op jit(solution)/shard_map/ppermute | solution.py:24
  159.4 2.2 %collective-permute-start.29 = (bf16[128,2560]{1,0:T(8,128)(2,1)S(1)}, bf16[128,2560]{1,0:T(8,128)(2,1)S(1)}, u32[]{:S(2)}, u32[]{:S(2)}) collective-permute-start(bf16[128,2560]{1,0:T(8,128)(2,1)S(1)} %join_columns.56.refs_0_), channel_id=1, source_target_pairs={{0,8},{8,0},{16,24},{24,16},{1,9},{9,1},{17,25},{25,17},{2,10},{10... | collective-permute-start | bytes 1966088 | tf_op jit(solution)/shard_map/ppermute | solution.py:24
  168.9 1.8 collective-permute-start.30

commit v17 on v15

--- a/solution.py
+++ b/solution.py
@@ -468,7 +468,6 @@
             sizes[:] = [0]
         if step == len(far_steps) - 3:
             add_products(0)
-        elif step == len(far_steps) - 2:
             add_products(1)
         elif step == len(far_steps) - 1:
             finish_core()

time: 178 us -> 182 us (1.022)
  blocking collectives: 9.9 us -> 13.9 us
    all_to_all x1, blocking collectives: 9.9 us -> 13.9 us  [body(): lax.all_to_all(gradients[1][1], ('user', 'tok'), split_axis=0, concat_axi...]
    unnamed x32 -> x28, local copies, waits for them, and re-layouts: 6.07 us -> 5.91 us
  transfers between devices with their start and end apart: 30 -> 30, of which waited for: 12 -> 13; matrix products, arithmetic and copies ran while one was open for 0% -> 0% of each run, Pallas kernels for 12% -> 11%
where the time goes in v17:
time: 182 us
  waiting for transfers between devices  88 us (48%)
  starting transfers between devices  43.7 us (24%)
  Pallas kernels  29.3 us (16%)
  blocking collectives  13.9 us (8%)
  local copies, waits for them, and re-layouts  5.91 us (3%)
    ppermute x30, waiting for transfers between devices, exchange(): return lax.ppermute(block, axis, [(i, i ^ distance) for i in range(size)])  88 us
    ppermute x30, starting transfers between devices, exchange(): return lax.ppermute(block, axis, [(i, i ^ distance) for i in range(size)])  43.7 us
    pallas_call x4, Pallas kernels, product(): pl.pallas_call(functools.partial(product_kernel, left_places, right_place...  22.6 us
    all_to_all x1, blocking collectives, body(): lax.all_to_all(gradients[1][1], ('user', 'tok'), split_axis=0, concat_axi...  13.9 us
    unnamed x28, local copies, waits for them, and re-layouts  5.91 us
    pallas_call x1, Pallas kernels, combine(): pl.pallas_call(functools.partial(combine_kernel, user_count, clip_bound,...  4.82 us
  transfers between devices with their start and end apart: 30, of which 13 were waited for; matrix products, arithmetic and copies ran while one was open for 0% of the time, Pallas kernels for 11%

profile of v17, /device:TPU:0, one launch (start us, length us, event | category | flops | bytes accessed | tf_op | source)
XLA Modules:
  0.0 181.8 jit_solution(6794236011107719089)
XLA Ops:
  0.7 1.0 copy-done.13
  1.7 0.5 collective-permute-start
  2.3 2.6 %collective-permute-start.1 = (bf16[128,512]{1,0:T(8,128)(2,1)S(1)}, bf16[128,512]{1,0:T(8,128)(2,1)S(1)}, u32[]{:S(2)}, u32[]{:S(2)}) collective-permute-start(bf16[128,512]{1,0:T(8,128)(2,1)S(1)} %get-tuple-element.25), channel_id=1, source_target_pairs={{0,16},{8,24},{16,0},{24,8},{1,17},{9,25},{17,1},{25,9},{2,18},{10... | collective-permute-start | bytes 393224 | tf_op jit(solution)/shard_map/ppermute | solution.py:24
  4.8 0.1 collective-permute-start.2
  4.9 2.2 %copy-done.10 = bf16[1,128,16384]{2,1,0:T(8,128)(2,1)S(1)} copy-done((bf16[1,128,16384]{2,1,0:T(8,128)(2,1)S(1)}, bf16[1,128,16384]{2,1,0:T(8,128)(2,1)}, u32[]{:S(2)}) %copy-start.10) | copy-done | bytes 4194328
  7.1 0.4 pack_columns.1
  7.5 2.9 %collective-permute-start.7 = (bf16[128,2048]{1,0:T(8,128)(2,1)S(1)}, bf16[128,2048]{1,0:T(8,128)(2,1)S(1)}, u32[]{:S(2)}, u32[]{:S(2)}) collective-permute-start(bf16[128,2048]{1,0:T(8,128)(2,1)S(1)} %join_columns.28.refs_1_), channel_id=1, source_target_pairs={{0,4},{1,5},{2,6},{3,7},{4,0},{5,1},{6,2},{7,3},{8,12},{9,13},{10,... | collective-permute-start | bytes 1572872 | tf_op jit(solution)/shard_map/ppermute | solution.py:24
  10.4 1.6 collective-permute-start.5
  12.1 0.1 join_columns.32.refs_1_
  12.2 1.6 collective-permute-start.3
  13.8 1.6 collective-permute-start.4
  15.5 2.1 %collective-permute-start.10 = (bf16[128,2048]{1,0:T(8,128)(2,1)S(1)}, bf16[128,2048]{1,0:T(8,128)(2,1)S(1)}, u32[]{:S(2)}, u32[]{:S(2)}) collective-permute-start(bf16[128,2048]{1,0:T(8,128)(2,1)S(1)} %join_columns.31.refs_2_), channel_id=1, source_target_pairs={{0,4},{1,5},{2,6},{3,7},{4,0},{5,1},{6,2},{7,3},{8,12},{9,13},{10,... | collective-permute-start | bytes 1572872 | tf_op jit(solution)/shard_map/ppermute | solution.py:24
  17.6 6.8 %collective-permute-done.5.refs_3_.refs_1_.refs_5_ = bf16[128,2048]{1,0:T(8,128)(2,1)S(1)} collective-permute-done((bf16[128,2048]{1,0:T(8,128)(2,1)S(1)}, bf16[128,2048]{1,0:T(8,128)(2,1)S(1)}, u32[]{:S(2)}, u32[]{:S(2)}) %collective-permute-start.5) | collective-permute-done | bytes 524320 | tf_op jit(solution)/shard_map/ppermute | solution.py:24
  24.4 14.1 %collective-permute-done.4.refs_1_ = bf16[128,2048]{1,0:T(8,128)(2,1)S(1)} collective-permute-done((bf16[128,2048]{1,0:T(8,128)(2,1)S(1)}, bf16[128,2048]{1,0:T(8,128)(2,1)S(1)}, u32[]{:S(2)}, u32[]{:S(2)}) %collective-permute-start.4) | collective-permute-done | bytes 524320 | tf_op jit(solution)/shard_map/ppermute | solution.py:24
  38.5 0.1 join_columns.34.refs_1_.refs_0_
  38.6 1.6 collective-permute-start.8
  40.2 0.2 collective-permute-start.6
  40.4 0.1 join_columns.36.refs_0_
  40.5 0.1 collective-permute-start.9
  40.6 4.7 %collective-permute-start.13 = (bf16[128,2048]{1,0:T(8,128)(2,1)S(1)}, bf16[128,2048]{1,0:T(8,128)(2,1)S(1)}, u32[]{:S(2)}, u32[]{:S(2)}) collective-permute-start(bf16[128,2048]{1,0:T(8,128)(2,1)S(1)} %join_columns.37.refs_1_), channel_id=1, source_target_pairs={{0,5},{1,4},{2,7},{3,6},{4,1},{5,0},{6,3},{7,2},{8,13},{9,12},{10,... | collective-permute-start | bytes 1572872 | tf_op jit(solution)/shard_map/ppermute | solution.py:24
  45.3 17.3 %collective-permute-done.8.refs_2_.refs_1_.refs_6_ = bf16[128,4096]{1,0:T(8,128)(2,1)S(1)} collective-permute-done((bf16[128,4096]{1,0:T(8,128)(2,1)S(1)}, bf16[128,4096]{1,0:T(8,128)(2,1)S(1)}, u32[]{:S(2)}, u32[]{:S(2)}) %collective-permute-start.8) | collective-permute-done | bytes 1048608 | tf_op jit(solution)/shard_map/ppermute | solution.py:24
  62.7 1.8 collective-permute-start.14
  64.5 0.6 collective-permute-start.15
  65.1 1.6 collective-permute-start.12
  66.8 4.2 %collective-permute-start.11 = (bf16[128,2048]{1,0:T(8,128)(2,1)S(1)}, bf16[128,2048]{1,0:T(8,128)(2,1)S(1)}, u32[]{:S(2)}, u32[]{:S(2)}) collective-permute-start(bf16[128,2048]{1,0:T(8,128)(2,1)S(1)} %join_columns.41.refs_1_), channel_id=1, source_target_pairs={{0,6},{1,7},{2,4},{3,5},{4,2},{5,3},{6,0},{7,1},{8,14},{9,15},{10,... | collective-permute-start | bytes 1572872 | tf_op jit(solution)/shard_map/ppermute | solution.py:24
  70.9 3.9 %collective-permute-done.14.refs_2_.refs_3_.refs_7_ = bf16[128,2048]{1,0:T(8,128)(2,1)S(1)} collective-permute-done((bf16[128,2048]{1,0:T(8,128)(2,1)S(1)}, bf16[128,2048]{1,0:T(8,128)(2,1)S(1)}, u32[]{:S(2)}, u32[]{:S(2)}) %collective-permute-start.14) | collective-permute-done | bytes 524320 | tf_op jit(solution)/shard_map/ppermute | solution.py:24
  74.8 0.9 collective-permute-start.21
  75.8 0.2 join_columns.43.refs_0_
  76.0 17.1 %collective-permute-done.15.refs_1_.refs_9_ = bf16[128,2048]{1,0:T(8,128)(2,1)S(1)} collective-permute-done((bf16[128,2048]{1,0:T(8,128)(2,1)S(1)}, bf16[128,2048]{1,0:T(8,128)(2,1)S(1)}, u32[]{:S(2)}, u32[]{:S(2)}) %collective-permute-start.15) | collective-permute-done | bytes 524320 | tf_op jit(solution)/shard_map/ppermute | solution.py:24
  93.1 0.8 copy-done.11
  93.9 0.4 collective-permute-start.20
  94.3 4.4 %collective-permute-done.16.refs_2_.refs_4_ = bf16[128,12288]{1,0:T(8,128)(2,1)S(1)} collective-permute-done((bf16[128,12288]{1,0:T(8,128)(2,1)S(1)}, bf16[128,12288]{1,0:T(8,128)(2,1)S(1)}, u32[]{:S(2)}, u32[]{:S(2)}) %collective-permute-start.16) | collective-permute-done | bytes 3145760 | tf_op jit(solution)/shard_map/ppermute | solution.py:24
  98.7 1.1 collective-permute-start.17
  99.9 0.1 collective-permute-start.23
  100.0 2.3 %collective-permute-done.12.refs_1_ = bf16[128,2048]{1,0:T(8,128)(2,1)S(1)} collective-permute-done((bf16[128,2048]{1,0:T(8,128)(2,1)S(1)}, bf16[128,2048]{1,0:T(8,128)(2,1)S(1)}, u32[]{:S(2)}, u32[]{:S(2)}) %collective-permute-start.12) | collective-permute-done | bytes 524320 | tf_op jit(solution)/shard_map/ppermute | solution.py:24
  102.3 4.6 %collective-permute-start.18 = (bf16[128,768]{1,0:T(8,128)(2,1)S(1)}, bf16[128,768]{1,0:T(8,128)(2,1)S(1)}, u32[]{:S(2)}, u32[]{:S(2)}) collective-permute-start(bf16[128,768]{1,0:T(8,128)(2,1)S(1)} %join_columns.47.refs_2_), channel_id=1, source_target_pairs={{0,7},{1,6},{2,5},{3,4},{4,3},{5,2},{6,1},{7,0},{8,15},{9,14},{10,... | collective-permute-start | bytes 589832 | tf_op jit(solution)/shard_map/ppermute | solution.py:24
  106.9 5.9 %collective-permute-done.17.refs_3_.refs_1_.refs_7_ = bf16[128,2048]{1,0:T(8,128)(2,1)S(1)} collective-permute-done((bf16[128,2048]{1,0:T(8,128)(2,1)S(1)}, bf16[128,2048]{1,0:T(8,128)(2,1)S(1)}, u32[]{:S(2)}, u32[]{:S(2)}) %collective-permute-start.17) | collective-permute-done | bytes 524320 | tf_op jit(solution)/shard_map/ppermute | solution.py:24
  112.8 0.1 join_columns.48.refs_1_.refs_0_
  112.8 4.2 %collective-permute-start.19 = (bf16[128,4096]{1,0:T(8,128)(2,1)S(1)}, bf16[128,4096]{1,0:T(8,128)(2,1)S(1)}, u32[]{:S(2)}, u32[]{:S(2)}) collective-permute-start(bf16[128,4096]{1,0:T(8,128)(2,1)S(1)} %join_columns.48.refs_1_.refs_0_), channel_id=1, source_target_pairs={{0,16},{8,24},{16,0},{24,8},{1,17},{9,25},{17,1},{25,9},{2,18},{10... | collective-permute-start | bytes 3145736 | tf_op jit(solution)/shard_map/ppermute | solution.py:24
  117.0 4.4 %collective-permute-done.21.refs_0_.refs_1_.refs_11_ = bf16[128,2048]{1,0:T(8,128)(2,1)S(1)} collective-permute-done((bf16[128,2048]{1,0:T(8,128)(2,1)S(1)}, bf16[128,2048]{1,0:T(8,128)(2,1)S(1)}, u32[]{:S(2)}, u32[]{:S(2)}) %collective-permute-start.21) | collective-permute-done | bytes 524320 | tf_op jit(solution)/shard_map/ppermute | solution.py:24
  121.5 0.1 join_columns.50.refs_0_
  121.7 0.1 collective-permute-start.22
  121.7 0.9 copy-done.1
  122.6 0.2 copy-done.3
  122.8 0.3 copy-done.5
  123.2 0.3 copy-done.7
  123.5 0.1 copy-done.9
  123.6 4.1 %product_and_squares.5.refs_3_.refs_13_ = f32[4,768,512]{2,1,0:T(8,128)S(1)} custom-call(bf16[128,2048]{1,0:T(8,128)(2,1)S(1)} %copy-done.1, bf16[128,4096]{1,0:T(8,128)(2,1)S(1)} %join_columns.34.refs_1_.refs_0_, bf16[128,2048]{1,0:T(8,128)(2,1)S(1)} %join_columns.38.refs_1_.refs_2_, bf16[128,4096]{1,0:T(8,128)(2,1)S(1)} %copy-done.5, ...), custom_call_target="tpu_custom_call" | custom-call | flops 1610612736 | bytes 5242880 | tf_op jit(solution)/shard_map/product_and_squares/pallas_call | solution.py:197
  127.7 6.8 %product_and_squares.4.refs_2_.refs_13_ = f32[4,1280,512]{2,1,0:T(8,128)S(1)} custom-call(bf16[128,2048]{1,0:T(8,128)(2,1)S(1)} %copy-done.1, bf16[128,4096]{1,0:T(8,128)(2,1)S(1)} %join_columns.34.refs_1_.refs_0_, bf16[128,2048]{1,0:T(8,128)(2,1)S(1)} %join_columns.38.refs_1_.refs_2_, bf16[128,4096]{1,0:T(8,128)(2,1)S(1)} %copy-done.5, ...), custom_call_target="tpu_custom_call" | custom-call | flops 2684354560 | bytes 7340032 | tf_op jit(solution)/shard_map/product_and_squares/pallas_call | solution.py:197
  134.5 0.6 collective-permute-start.27
  135.1 3.1 %collective-permute-done.19.refs_4_.refs_1_.refs_6_ = bf16[128,4096]{1,0:T(8,128)(2,1)S(1)} collective-permute-done((bf16[128,4096]{1,0:T(8,128)(2,1)S(1)}, bf16[128,4096]{1,0:T(8,128)(2,1)S(1)}, u32[]{:S(2)}, u32[]{:S(2)}) %collective-permute-start.19) | collective-permute-done | bytes 1048608 | tf_op jit(solution)/shard_map/ppermute | solution.py:24
  138.3 1.8 %collective-permute-start.24 = (bf16[128,1280]{1,0:T(8,128)(2,1)S(1)}, bf16[128,1280]{1,0:T(8,128)(2,1)S(1)}, u32[]{:S(2)}, u32[]{:S(2)}) collective-permute-start(bf16[128,1280]{1,0:T(8,128)(2,1)S(1)} %join_columns.51.refs_2_.refs_0_), channel_id=1, source_target_pairs={{0,16},{8,24},{16,0},{24,8},{1,17},{9,25},{17,1},{25,9},{2,18},{10... | collective-permute-start | bytes 983048 | tf_op jit(solution)/shard_map/ppermute | solution.py:24
  140.1 0.1 join_columns.52.refs_0_
  140.3 0.1 collective-permute-start.25
  140.4 5.0 %collective-permute-done.24.refs_2_.refs_1_.refs_8_ = bf16[128,1280]{1,0:T(8,128)(2,1)S(1)} collective-permute-done((bf16[128,1280]{1,0:T(8,128)(2,1)S(1)}, bf16[128,1280]{1,0:T(8,128)(2,1)S(1)}, u32[]{:S(2)}, u32[]{:S(2)}) %collective-permute-start.24) | collective-permute-done | bytes 327712 | tf_op jit(solution)/shard_map/ppermute | solution.py:24
  145.4 1.8 %collective-permute-start.26 = (bf16[128,768]{1,0:T(8,128)(2,1)S(1)}, bf16[128,768]{1,0:T(8,128)(2,1)S(1)}, u32[]{:S(2)}, u32[]{:S(2)}) collective-permute-start(bf16[128,768]{1,0:T(8,128)(2,1)S(1)} %join_columns.53.refs_2_.refs_0_), channel_id=1, source_target_pairs={{0,16},{8,24},{16,0},{24,8},{1,17},{9,25},{17,1},{25,9},{2,18},{10... | collective-permute-start | bytes 589832 | tf_op jit(solution)/shard_map/ppermute | solution.py:24
  147.3 0.1 collective-permute-start.28
  147.4 2.1 %collective-permute-done.28.refs_5_ = bf16[128,2560]{1,0:T(8,128)(2,1)S(1)} collective-permute-done((bf16[128,2560]{1,0:T(8,128)(2,1)S(1)}, bf16[128,2560]{1,0:T(8,128)(2,1)S(1)}, u32[]{:S(2)}, u32[]{:S(2)}) %collective-permute-start.28) | collective-permute-done | bytes 655392 | tf_op jit(solution)/shard_map/ppermute | solution.py:24
  149.5 7.3 %product_and_squares.6 = (f32[4,1280,512]{2,1,0:T(8,128)S(1)}, f32[1,8,128]{2,1,0:T(8,128)S(1)}) custom-call(bf16[128,4096]{1,0:T(8,128)(2,1)S(1)} %join_columns.48.refs_1_.refs_0_, bf16[128,2048]{1,0:T(8,128)(2,1)S(1)} %join_columns.45.refs_1_.refs_0_, bf16[128,1280]{1,0:T(8,128)(2,1)S(1)} %join_columns.51.refs_2_.refs_0_, ...), custom_call_target="tpu_custom_call", output_to_operand_aliasing={{0}: (13, {})} | custom-call | flops 2684354560 | bytes 7340032 | tf_op jit(solution)/shard_map/product_and_squares/pallas_call | solution.py:197
  156.8 0.2 collective-permute-start.29
  157.1 1.6 collective-permute-done.29.refs_5_
  158.6 4.5 %product_and_squares.7 = (f32[4,768,512]{2,1,0:T(8,128)S(1)}, f32[32,8,128]{2,1,0:T(8,128)S(1)}) custom-call(bf16[128,4096]{1,0:T(8,128)(2,1)S(1)} %join_columns.48.refs_1_.refs_0_, bf16[128,2048]{1,0:T(8,128)(2,1)S(1)} %join_columns.45.refs_1_.refs_0_, bf16[128,768]{1,0:T(8,128)(2,1)S(1)} %join_columns.53.refs_2_.refs_0_, ...), custom_call_target="tpu_custom_call", output_to_operand_aliasing={{0}: (13, {})} | custom-call | flops 1610612736 | bytes 5242880 | tf_op jit(solution)/shard_map/product_and_squares/pallas_call | solution.py:197
  163.1 13.9 %all_to_all.5.sums_ref = f32[32,8,128]{2,1,0:T(8,128)S(1)} all-to-all(f32[32,8,128]{2,1,0:T(8,128)S(1)} %get-tuple-element.35), channel_id=1, replica_groups=mesh['user'=4,'tok'=8] {'user','tok'}, dimensions={0} | all-to-all | bytes 262144 | tf_op jit(solution)/shard_map/all_to_all | solution.py:478
  177.0 4.8 %weighted_sum.1 = f32[2048,512]{1,0:T(8,128)} custom-call(s32[1]{0:T(128)} %bitcast.user_ref, f32[32,8,128]{2,1,0:T(8,128)S(1)} %all_to_all.5.sums_ref, f32[4,1280,512]{2,1,0:T(8,128)S(1)} %get-tuple-element.33.refs_3_.refs_0_, f32[4,768,512]{2,1,0:T(8,128)S(1)} %get-tuple-element.36.refs_1_), custom_call_target="tpu_custom_call" | custom-call | tf_op jit(solution)/shard_map/weighted_sum/pallas_call | solution.py:254
  (68 shorter events, 0.9 us)
Async XLA Ops:
  0.7 1.0 copy-start.13
  1.7 10.3 %collective-permute-start = (bf16[128,512]{1,0:T(8,128)(2,1)S(1)}, bf16[128,512]{1,0:T(8,128)(2,1)S(1)}, u32[]{:S(2)}, u32[]{:S(2)}) collective-permute-start(bf16[128,512]{1,0:T(8,128)(2,1)S(1)} %get-tuple-element.24), channel_id=1, source_target_pairs={{0,8},{8,0},{16,24},{24,16},{1,9},{9,1},{17,25},{25,17},{2,10},{10... | collective-permute-start | bytes 393224 | tf_op jit(solution)/shard_map/ppermute | solution.py:24
  2.3 9.7 %collective-permute-start.1 = (bf16[128,512]{1,0:T(8,128)(2,1)S(1)}, bf16[128,512]{1,0:T(8,128)(2,1)S(1)}, u32[]{:S(2)}, u32[]{:S(2)}) collective-permute-start(bf16[128,512]{1,0:T(8,128)(2,1)S(1)} %get-tuple-element.25), channel_id=1, source_target_pairs={{0,16},{8,24},{16,0},{24,8},{1,17},{9,25},{17,1},{25,9},{2,18},{10... | collective-permute-start | bytes 393224 | tf_op jit(solution)/shard_map/ppermute | solution.py:24
  4.8 7.2 %collective-permute-start.2 = (bf16[128,512]{1,0:T(8,128)(2,1)S(1)}, bf16[128,512]{1,0:T(8,128)(2,1)S(1)}, u32[]{:S(2)}, u32[]{:S(2)}) collective-permute-start(bf16[128,512]{1,0:T(8,128)(2,1)S(1)} %get-tuple-element.26), channel_id=1, source_target_pairs={{0,24},{8,16},{16,8},{24,0},{1,25},{9,17},{17,9},{25,1},{2,26},{10... | collective-permute-start | bytes 393224 | tf_op jit(solution)/shard_map/ppermute | solution.py:24
  4.9 2.2 %copy-start.10 = (bf16[1,128,16384]{2,1,0:T(8,128)(2,1)S(1)}, bf16[1,128,16384]{2,1,0:T(8,128)(2,1)}, u32[]{:S(2)}) copy-start(bf16[1,128,16384]{2,1,0:T(8,128)(2,1)} %hidden_ref.1) | copy-start | bytes 12582916
  7.5 33.1 %collective-permute-start.7 = (bf16[128,2048]{1,0:T(8,128)(2,1)S(1)}, bf16[128,2048]{1,0:T(8,128)(2,1)S(1)}, u32[]{:S(2)}, u32[]{:S(2)}) collective-permute-start(bf16[128,2048]{1,0:T(8,128)(2,1)S(1)} %join_columns.28.refs_1_), channel_id=1, source_target_pairs={{0,4},{1,5},{2,6},{3,7},{4,0},{5,1},{6,2},{7,3},{8,12},{9,13},{10,... | collective-permute-start | bytes 1572872 | tf_op jit(solution)/shard_map/ppermute | solution.py:24
  10.4 30.0 %copy-start = (bf16[128,2048]{1,0:T(8,128)(2,1)}, bf16[128,2048]{1,0:T(8,128)(2,1)S(1)}, u32[]{:S(2)}) copy-start(bf16[128,2048]{1,0:T(8,128)(2,1)S(1)} %join_columns.29.refs_4_.refs_1_.refs_0_) | copy-start | bytes 1572868
  10.4 14.0 %collective-permute-start.5 = (bf16[128,2048]{1,0:T(8,128)(2,1)S(1)}, bf16[128,2048]{1,0:T(8,128)(2,1)S(1)}, u32[]{:S(2)}, u32[]{:S(2)}) collective-permute-start(bf16[128,2048]{1,0:T(8,128)(2,1)S(1)} %join_columns.29.refs_4_.refs_1_.refs_0_), channel_id=1, source_target_pairs={{0,16},{8,24},{16,0},{24,8},{1,17},{9,25},{17,1},{25,9},{2,18},{10... | collective-permute-start | bytes 1572872 | tf_op jit(solution)/shard_map/ppermute | solution.py:24
  12.1 26.5 %copy-start.2 = (bf16[128,2048]{1,0:T(8,128)(2,1)}, bf16[128,2048]{1,0:T(8,128)(2,1)S(1)}, u32[]{:S(2)}) copy-start(bf16[128,2048]{1,0:T(8,128)(2,1)S(1)} %join_columns.30.refs_0_.refs_1_.refs_8_) | copy-start | bytes 1572868
  12.2 26.3 %collective-permute-start.3 = (bf16[128,4096]{1,0:T(8,128)(2,1)S(1)}, bf16[128,4096]{1,0:T(8,128)(2,1)S(1)}, u32[]{:S(2)}, u32[]{:S(2)}) collective-permute-start(bf16[128,4096]{1,0:T(8,128)(2,1)S(1)} %join_columns.32.refs_1_), channel_id=1, source_target_pairs={{0,1},{1,0},{2,3},{3,2},{4,5},{5,4},{6,7},{7,6},{8,9},{9,8},{10,11... | collective-permute-start | bytes 3145736 | tf_op jit(solution)/shard_map/ppermute | solution.py:24
  13.8 24.6 %collective-permute-start.4 = (bf16[128,2048]{1,0:T(8,128)(2,1)S(1)}, bf16[128,2048]{1,0:T(8,128)(2,1)S(1)}, u32[]{:S(2)}, u32[]{:S(2)}) collective-permute-start(bf16[128,2048]{1,0:T(8,128)(2,1)S(1)} %join_columns.33.refs_0_), channel_id=1, source_target_pairs={{0,2},{1,3},{2,0},{3,1},{4,6},{5,7},{6,4},{7,5},{8,10},{9,11},{10,... | collective-permute-start | bytes 1572872 | tf_op jit(solution)/shard_map/ppermute | solution.py:24
  15.5 51.2 %collective-permute-start.10 = (bf16[128,2048]{1,0:T(8,128)(2,1)S(1)}, bf16[128,2048]{1,0:T(8,128)(2,1)S(1)}, u32[]{:S(2)}, u32[]{:S(2)}) collective-permute-start(bf16[128,2048]{1,0:T(8,128)(2,1)S(1)} %join_columns.31.refs_2_), channel_id=1, source_target_pairs={{0,4},{1,5},{2,6},{3,7},{4,0},{5,1},{6,2},{7,3},{8,12},{9,13},{10,... | collective-permute-start | bytes 1572872 | tf_op jit(solution)/shard_map/ppermute | solution.py:24
  24.4 16.2 %copy-start.8 = (bf16[128,2048]{1,0:T(8,128)(2,1)}, bf16[128,2048]{1,0:T(8,128)(2,1)S(1)}, u32[]{:S(2)}) copy-start(bf16[128,2048]{1,0:T(8,128)(2,1)S(1)} %collective-permute-done.5.refs_3_.refs_1_.refs_5_) | copy-start | bytes 1572868
  38.5 1.9 %copy-start.6 = (bf16[128,4096]{1,0:T(8,128)(2,1)}, bf16[128,4096]{1,0:T(8,128)(2,1)S(1)}, u32[]{:S(2)}) copy-start(bf16[128,4096]{1,0:T(8,128)(2,1)S(1)} %collective-permute-done.3.refs_0_.refs_9_) | copy-start | bytes 3145732
  38.6 24.0 %collective-permute-start.8 = (bf16[128,4096]{1,0:T(8,128)(2,1)S(1)}, bf16[128,4096]{1,0:T(8,128)(2,1)S(1)}, u32[]{:S(2)}, u32[]{:S(2)}) collective-permute-start(bf16[128,4096]{1,0:T(8,128)(2,1)S(1)} %join_columns.34.refs_1_.refs_0_), channel_id=1, source_target_pairs={{0,16},{8,24},{16,0},{24,8},{1,17},{9,25},{17,1},{25,9},{2,18},{10... | collective-permute-start | bytes 3145736 | tf_op jit(solution)/shard_map/ppermute | solution.py:24
  40.2 24.3 %collective-permute-start.6 = (bf16[128,2048]{1,0:T(8,128)(2,1)S(1)}, bf16[128,2048]{1,0:T(8,128)(2,1)S(1)}, u32[]{:S(2)}, u32[]{:S(2)}) collective-permute-start(bf16[128,2048]{1,0:T(8,128)(2,1)S(1)} %join_columns.35.refs_2_), channel_id=1, source_target_pairs={{0,2},{1,3},{2,0},{3,1},{4,6},{5,7},{6,4},{7,5},{8,10},{9,11},{10,... | collective-permute-start | bytes 1572872 | tf_op jit(solution)/shard_map/ppermute | solution.py:24
  40.5 4.8 %collective-permute-start.9 = (bf16[128,4096]{1,0:T(8,128)(2,1)S(1)}, bf16[128,4096]{1,0:T(8,128)(2,1)S(1)}, u32[]{:S(2)}, u32[]{:S(2)}) collective-permute-start(bf16[128,4096]{1,0:T(8,128)(2,1)S(1)} %join_columns.36.refs_0_), channel_id=1, source_target_pairs={{0,8},{8,0},{16,24},{24,16},{1,9},{9,1},{17,25},{25,17},{2,10},{10... | collective-permute-start | bytes 3145736 | tf_op jit(solution)/shard_map/ppermute | solution.py:24
  40.6 53.2 %collective-permute-start.13 = (bf16[128,2048]{1,0:T(8,128)(2,1)S(1)}, bf16[128,2048]{1,0:T(8,128)(2,1)S(1)}, u32[]{:S(2)}, u32[]{:S(2)}) collective-permute-start(bf16[128,2048]{1,0:T(8,128)(2,1)S(1)} %join_columns.37.refs_1_), channel_id=1, source_target_pairs={{0,5},{1,4},{2,7},{3,6},{4,1},{5,0},{6,3},{7,2},{8,13},{9,12},{10,... | collective-permute-start | bytes 1572872 | tf_op jit(solution)/shard_map/ppermute | solution.py:24
  45.3 21.4 %copy-start.4 = (bf16[128,4096]{1,0:T(8,128)(2,1)}, bf16[128,4096]{1,0:T(8,128)(2,1)S(1)}, u32[]{:S(2)}) copy-start(bf16[128,4096]{1,0:T(8,128)(2,1)S(1)} %collective-permute-done.9.refs_3_) | copy-start | bytes 3145732
  62.7 12.1 %collective-permute-start.14 = (bf16[128,2048]{1,0:T(8,128)(2,1)S(1)}, bf16[128,2048]{1,0:T(8,128)(2,1)S(1)}, u32[]{:S(2)}, u32[]{:S(2)}) collective-permute-start(bf16[128,2048]{1,0:T(8,128)(2,1)S(1)} %join_columns.38.refs_1_.refs_2_), channel_id=1, source_target_pairs={{0,16},{8,24},{16,0},{24,8},{1,17},{9,25},{17,1},{25,9},{2,18},{10... | collective-permute-start | bytes 1572872 | tf_op jit(solution)/shard_map/ppermute | solution.py:24
  64.5 28.5 %collective-permute-start.15 = (bf16[128,2048]{1,0:T(8,128)(2,1)S(1)}, bf16[128,2048]{1,0:T(8,128)(2,1)S(1)}, u32[]{:S(2)}, u32[]{:S(2)}) collective-permute-start(bf16[128,2048]{1,0:T(8,128)(2,1)S(1)} %join_columns.39.refs_1_), channel_id=1, source_target_pairs={{0,1},{1,0},{2,3},{3,2},{4,5},{5,4},{6,7},{7,6},{8,9},{9,8},{10,11... | collective-permute-start | bytes 1572872 | tf_op jit(solution)/shard_map/ppermute | solution.py:24
  65.1 37.1 %collective-permute-start.12 = (bf16[128,2048]{1,0:T(8,128)(2,1)S(1)}, bf16[128,2048]{1,0:T(8,128)(2,1)S(1)}, u32[]{:S(2)}, u32[]{:S(2)}) collective-permute-start(bf16[128,2048]{1,0:T(8,128)(2,1)S(1)} %join_columns.40.refs_0_), channel_id=1, source_target_pairs={{0,3},{1,2},{2,1},{3,0},{4,7},{5,6},{6,5},{7,4},{8,11},{9,10},{10,... | collective-permute-start | bytes 1572872 | tf_op jit(solution)/shard_map/ppermute | solution.py:24
  66.8 33.2 %collective-permute-start.11 = (bf16[128,2048]{1,0:T(8,128)(2,1)S(1)}, bf16[128,2048]{1,0:T(8,128)(2,1)S(1)}, u32[]{:S(2)}, u32[]{:S(2)}) collective-permute-start(bf16[128,2048]{1,0:T(8,128)(2,1)S(1)} %join_columns.41.refs_1_), channel_id=1, source_target_pairs={{0,6},{1,7},{2,4},{3,5},{4,2},{5,3},{6,0},{7,1},{8,14},{9,15},{10,... | collective-permute-start | bytes 1572872 | tf_op jit(solution)/shard_map/ppermute | solution.py:24
  74.8 46.6 %collective-permute-start.21 = (bf16[128,2048]{1,0:T(8,128)(2,1)S(1)}, bf16[128,2048]{1,0:T(8,128)(2,1)S(1)}, u32[]{:S(2)}, u32[]{:S(2)}) collective-permute-start(bf16[128,2048]{1,0:T(8,128)(2,1)S(1)} %join_columns.42.refs_4_), channel_id=1, source_target_pairs={{0,2},{1,3},{2,0},{3,1},{4,6},{5,7},{6,4},{7,5},{8,10},{9,11},{10,... | collective-permute-start | bytes 1572872 | tf_op jit(solution)/shard_map/ppermute | solution.py:24
  93.0 0.8 copy-start.11
  93.0 5.7 %collective-permute-start.16 = (bf16[128,12288]{1,0:T(8,128)(2,1)S(1)}, bf16[128,12288]{1,0:T(8,128)(2,1)S(1)}, u32[]{:S(2)}, u32[]{:S(2)}) collective-permute-start(bf16[128,12288]{1,0:T(8,128)(2,1)S(1)} %join_columns.43.refs_0_), channel_id=1, source_target_pairs={{0,8},{8,0},{16,24},{24,16},{1,9},{9,1},{17,25},{25,17},{2,10},{10... | collective-permute-start | bytes 9437192 | tf_op jit(solution)/shard_map/ppermute | solution.py:24
  93.9 40.6 %collective-permute-start.20 = (bf16[128,1280]{1,0:T(8,128)(2,1)S(1)}, bf16[128,1280]{1,0:T(8,128)(2,1)S(1)}, u32[]{:S(2)}, u32[]{:S(2)}) collective-permute-start(bf16[128,1280]{1,0:T(8,128)(2,1)S(1)} %join_columns.44.refs_1_), channel_id=1, source_target_pairs={{0,7},{1,6},{2,5},{3,4},{4,3},{5,2},{6,1},{7,0},{8,15},{9,14},{10,... | collective-permute-start | bytes 983048 | tf_op jit(solution)/shard_map/ppermute | solution.py:24
  98.7 14.0 %collective-permute-start.17 = (bf16[128,2048]{1,0:T(8,128)(2,1)S(1)}, bf16[128,2048]{1,0:T(8,128)(2,1)S(1)}, u32[]{:S(2)}, u32[]{:S(2)}) collective-permute-start(bf16[128,2048]{1,0:T(8,128)(2,1)S(1)} %join_columns.45.refs_1_.refs_0_), channel_id=1, source_target_pairs={{0,16},{8,24},{16,0},{24,8},{1,17},{9,25},{17,1},{25,9},{2,18},{10... | collective-permute-start | bytes 1572872 | tf_op jit(solution)/shard_map/ppermute | solution.py:24
  99.9 40.4 %collective-permute-start.23 = (bf16[128,2048]{1,0:T(8,128)(2,1)S(1)}, bf16[128,2048]{1,0:T(8,128)(2,1)S(1)}, u32[]{:S(2)}, u32[]{:S(2)}) collective-permute-start(bf16[128,2048]{1,0:T(8,128)(2,1)S(1)} %join_columns.46.refs_0_), channel_id=1, source_target_pairs={{0,1},{1,0},{2,3},{3,2},{4,5},{5,4},{6,7},{7,6},{8,9},{9,8},{10,11... | collective-permute-start | bytes 1572872 | tf_op jit(solution)/shard_map/ppermute | solution.py:24
  102.3 38.1 %collective-permute-start.18 = (bf16[128,768]{1,0:T(8,128)(2,1)S(1)}, bf16[128,768]{1,0:T(8,128)(2,1)S(1)}, u32[]{:S(2)}, u32[]{:S(2)}) collective-permute-start(bf16[128,768]{1,0:T(8,128)(2,1)S(1)} %join_columns.47.refs_2_), channel_id=1, source_target_pairs={{0,7},{1,6},{2,5},{3,4},{4,3},{5,2},{6,1},{7,0},{8,15},{9,14},{10,... | collective-permute-start | bytes 589832 | tf_op jit(solution)/shard_map/ppermute | solution.py:24
  112.8 25.4 %collective-permute-start.19 = (bf16[128,4096]{1,0:T(8,128)(2,1)S(1)}, bf16[128,4096]{1,0:T(8,128)(2,1)S(1)}, u32[]{:S(2)}, u32[]{:S(2)}) collective-permute-start(bf16[128,4096]{1,0:T(8,128)(2,1)S(1)} %join_columns.48.refs_1_.refs_0_), channel_id=1, source_target_pairs={{0,16},{8,24},{16,0},{24,8},{1,17},{9,25},{17,1},{25,9},{2,18},{10... | collective-permute-start | bytes 3145736 | tf_op jit(solution)/shard_map/ppermute | solution.py:24
  121.6 1.0 copy-start.1
  121.6 1.2 copy-start.3
  121.6 1.5 copy-start.5
  121.6 1.8 %copy-start.7 = (bf16[128,4096]{1,0:T(8,128)(2,1)S(1)}, bf16[128,4096]{1,0:T(8,128)(2,1)}, u32[]{:S(2)}) copy-start(bf16[128,4096]{1,0:T(8,128)(2,1)} %copy-done.6) | copy-start | bytes 3145732
  121.6 2.0 %copy-start.9 = (bf16[128,2048]{1,0:T(8,128)(2,1)S(1)}, bf16[128,2048]{1,0:T(8,128)(2,1)}, u32[]{:S(2)}) copy-start(bf16[128,2048]{1,0:T(8,128)(2,1)} %copy-done.8) | copy-start | bytes 1572868
  121.7 13.5 %collective-permute-start.22 = (bf16[128,4096]{1,0:T(8,128)(2,1)S(1)}, bf16[128,4096]{1,0:T(8,128)(2,1)S(1)}, u32[]{:S(2)}, u32[]{:S(2)}) collective-permute-start(bf16[128,4096]{1,0:T(8,128)(2,1)S(1)} %join_columns.50.refs_0_), channel_id=1, source_target_pairs={{0,8},{8,0},{16,24},{24,16},{1,9},{9,1},{17,25},{25,17},{2,10},{10... | collective-permute-start | bytes 3145736 | tf_op jit(solution)/shard_map/ppermute | solution.py:24
  134.5 12.9 %collective-permute-start.27 = (bf16[128,2048]{1,0:T(8,128)(2,1)S(1)}, bf16[128,2048]{1,0:T(8,128)(2,1)S(1)}, u32[]{:S(2)}, u32[]{:S(2)}) collective-permute-start(bf16[128,2048]{1,0:T(8,128)(2,1)S(1)} %join_columns.49.refs_2_), channel_id=1, source_target_pairs={{0,1},{1,0},{2,3},{3,2},{4,5},{5,4},{6,7},{7,6},{8,9},{9,8},{10,11... | collective-permute-start | bytes 1572872 | tf_op jit(solution)/shard_map/ppermute | solution.py:24
  138.3 7.1 %collective-permute-start.24 = (bf16[128,1280]{1,0:T(8,128)(2,1)S(1)}, bf16[128,1280]{1,0:T(8,128)(2,1)S(1)}, u32[]{:S(2)}, u32[]{:S(2)}) collective-permute-start(bf16[128,1280]{1,0:T(8,128)(2,1)S(1)} %join_columns.51.refs_2_.refs_0_), channel_id=1, source_target_pairs={{0,16},{8,24},{16,0},{24,8},{1,17},{9,25},{17,1},{25,9},{2,18},{10... | collective-permute-start | bytes 983048 | tf_op jit(solution)/shard_map/ppermute | solution.py:24
  140.3 5.2 %collective-permute-start.25 = (bf16[128,8192]{1,0:T(8,128)(2,1)S(1)}, bf16[128,8192]{1,0:T(8,128)(2,1)S(1)}, u32[]{:S(2)}, u32[]{:S(2)}) collective-permute-start(bf16[128,8192]{1,0:T(8,128)(2,1)S(1)} %join_columns.52.refs_0_), channel_id=1, source_target_pairs={{0,8},{8,0},{16,24},{24,16},{1,9},{9,1},{17,25},{25,17},{2,10},{10... | collective-permute-start | bytes 6291464 | tf_op jit(solution)/shard_map/ppermute | solution.py:24
  145.4 11.4 %collective-permute-start.26 = (bf16[128,768]{1,0:T(8,128)(2,1)S(1)}, bf16[128,768]{1,0:T(8,128)(2,1)S(1)}, u32[]{:S(2)}, u32[]{:S(2)}) collective-permute-start(bf16[128,768]{1,0:T(8,128)(2,1)S(1)} %join_columns.53.refs_2_.refs_0_), channel_id=1, source_target_pairs={{0,16},{8,24},{16,0},{24,8},{1,17},{9,25},{17,1},{25,9},{2,18},{10... | collective-permute-start | bytes 589832 | tf_op jit(solution)/shard_map/ppermute | solution.py:24
  147.3 2.2 %copy-start.12 = (bf16[128,2048]{1,0:T(8,128)(2,1)S(1)}, bf16[128,2048]{1,0:T(8,128)(2,1)}, u32[]{:S(2)}) copy-start(bf16[128,2048]{1,0:T(8,128)(2,1)} %copy-done.11) | copy-start | bytes 1572868
  147.3 2.2 %collective-permute-start.28 = (bf16[128,2560]{1,0:T(8,128)(2,1)S(1)}, bf16[128,2560]{1,0:T(8,128)(2,1)S(1)}, u32[]{:S(2)}, u32[]{:S(2)}) collective-permute-start(bf16[128,2560]{1,0:T(8,128)(2,1)S(1)} %join_columns.54.refs_0_), channel_id=1, source_target_pairs={{0,8},{8,0},{16,24},{24,16},{1,9},{9,1},{17,25},{25,17},{2,10},{10... | collective-permute-start | bytes 1966088 | tf_op jit(solution)/shard_map/ppermute | solution.py:24
  156.8 1.8 collective-permute-start.29

commit v18 on v15

--- a/solution.py
+++ b/solution.py
@@ -10,7 +10,7 @@
 
 epsilon = 1e-06
 lanes = 128
-first_part = 0.625
+first_part = 0.5
 dear = 24 * 10**10
 dear_per_byte = 2 * 10**5
 ANY = pl.BlockSpec(memory_space=pl.ANY)

time: 178 us -> 177 us (level)
  starting transfers between devices: 43.6 us -> 41.5 us
  waiting for transfers between devices: 86.9 us -> 88.7 us
    ppermute x30, starting transfers between devices: 43.6 us -> 41.5 us  [exchange(): return lax.ppermute(block, axis, [(i, i ^ distance) for i in range(size)])]
  transfers between devices with their start and end apart: 30 -> 30, of which waited for: 12 -> 13; matrix products, arithmetic and copies ran while one was open for 0% -> 0% of each run, Pallas kernels for 12% -> 11%
where the time goes in v18:
time: 177 us
  waiting for transfers between devices  88.7 us (50%)
  starting transfers between devices  41.5 us (23%)
  Pallas kernels  30.3 us (17%)
  blocking collectives  9.44 us (5%)
  local copies, waits for them, and re-layouts  6.07 us (3%)
    ppermute x30, waiting for transfers between devices, exchange(): return lax.ppermute(block, axis, [(i, i ^ distance) for i in range(size)])  88.7 us
    ppermute x30, starting transfers between devices, exchange(): return lax.ppermute(block, axis, [(i, i ^ distance) for i in range(size)])  41.5 us
    pallas_call x4, Pallas kernels, product(): pl.pallas_call(functools.partial(product_kernel, left_places, right_place...  23.7 us
    all_to_all x1, blocking collectives, body(): lax.all_to_all(gradients[1][1], ('user', 'tok'), split_axis=0, concat_axi...  9.44 us
    unnamed x32, local copies, waits for them, and re-layouts  6.07 us
    pallas_call x1, Pallas kernels, combine(): pl.pallas_call(functools.partial(combine_kernel, user_count, clip_bound,...  4.82 us
  transfers between devices with their start and end apart: 30, of which 13 were waited for; matrix products, arithmetic and copies ran while one was open for 0% of the time, Pallas kernels for 11%

profile of v18, /device:TPU:0, one launch (start us, length us, event | category | flops | bytes accessed | tf_op | source)
XLA Modules:
  0.0 177.2 jit_solution(4197818989379636248)
XLA Ops:
  0.7 1.0 copy-done.15
  1.7 0.5 collective-permute-start
  2.3 2.6 %collective-permute-start.1 = (bf16[128,512]{1,0:T(8,128)(2,1)S(1)}, bf16[128,512]{1,0:T(8,128)(2,1)S(1)}, u32[]{:S(2)}, u32[]{:S(2)}) collective-permute-start(bf16[128,512]{1,0:T(8,128)(2,1)S(1)} %get-tuple-element.25), channel_id=1, source_target_pairs={{0,16},{8,24},{16,0},{24,8},{1,17},{9,25},{17,1},{25,9},{2,18},{10... | collective-permute-start | bytes 393224 | tf_op jit(solution)/shard_map/ppermute | solution.py:24
  4.8 0.1 collective-permute-start.2
  4.9 2.2 %copy-done.12 = bf16[1,128,16384]{2,1,0:T(8,128)(2,1)S(1)} copy-done((bf16[1,128,16384]{2,1,0:T(8,128)(2,1)S(1)}, bf16[1,128,16384]{2,1,0:T(8,128)(2,1)}, u32[]{:S(2)}) %copy-start.12) | copy-done | bytes 4194328
  7.1 0.4 pack_columns.1
  7.5 2.9 %collective-permute-start.7 = (bf16[128,2048]{1,0:T(8,128)(2,1)S(1)}, bf16[128,2048]{1,0:T(8,128)(2,1)S(1)}, u32[]{:S(2)}, u32[]{:S(2)}) collective-permute-start(bf16[128,2048]{1,0:T(8,128)(2,1)S(1)} %join_columns.28.refs_1_), channel_id=1, source_target_pairs={{0,4},{1,5},{2,6},{3,7},{4,0},{5,1},{6,2},{7,3},{8,12},{9,13},{10,... | collective-permute-start | bytes 1572872 | tf_op jit(solution)/shard_map/ppermute | solution.py:24
  10.5 1.6 collective-permute-start.5
  12.1 0.1 join_columns.32.refs_1_
  12.2 1.6 collective-permute-start.3
  13.8 1.6 collective-permute-start.4
  15.5 2.1 %collective-permute-start.10 = (bf16[128,2048]{1,0:T(8,128)(2,1)S(1)}, bf16[128,2048]{1,0:T(8,128)(2,1)S(1)}, u32[]{:S(2)}, u32[]{:S(2)}) collective-permute-start(bf16[128,2048]{1,0:T(8,128)(2,1)S(1)} %join_columns.31.refs_2_), channel_id=1, source_target_pairs={{0,4},{1,5},{2,6},{3,7},{4,0},{5,1},{6,2},{7,3},{8,12},{9,13},{10,... | collective-permute-start | bytes 1572872 | tf_op jit(solution)/shard_map/ppermute | solution.py:24
  17.6 6.8 %collective-permute-done.5.refs_3_.refs_1_.refs_5_.refs_7_ = bf16[128,2048]{1,0:T(8,128)(2,1)S(1)} collective-permute-done((bf16[128,2048]{1,0:T(8,128)(2,1)S(1)}, bf16[128,2048]{1,0:T(8,128)(2,1)S(1)}, u32[]{:S(2)}, u32[]{:S(2)}) %collective-permute-start.5) | collective-permute-done | bytes 524320 | tf_op jit(solution)/shard_map/ppermute | solution.py:24
  24.4 14.1 %collective-permute-done.4.refs_1_ = bf16[128,2048]{1,0:T(8,128)(2,1)S(1)} collective-permute-done((bf16[128,2048]{1,0:T(8,128)(2,1)S(1)}, bf16[128,2048]{1,0:T(8,128)(2,1)S(1)}, u32[]{:S(2)}, u32[]{:S(2)}) %collective-permute-start.4) | collective-permute-done | bytes 524320 | tf_op jit(solution)/shard_map/ppermute | solution.py:24
  38.5 0.1 join_columns.34.refs_1_.refs_0_
  38.6 1.6 collective-permute-start.8
  40.2 0.2 collective-permute-start.6
  40.4 0.1 join_columns.36.refs_0_
  40.5 0.1 collective-permute-start.9
  40.6 4.7 %collective-permute-start.13 = (bf16[128,2048]{1,0:T(8,128)(2,1)S(1)}, bf16[128,2048]{1,0:T(8,128)(2,1)S(1)}, u32[]{:S(2)}, u32[]{:S(2)}) collective-permute-start(bf16[128,2048]{1,0:T(8,128)(2,1)S(1)} %join_columns.37.refs_1_), channel_id=1, source_target_pairs={{0,5},{1,4},{2,7},{3,6},{4,1},{5,0},{6,3},{7,2},{8,13},{9,12},{10,... | collective-permute-start | bytes 1572872 | tf_op jit(solution)/shard_map/ppermute | solution.py:24
  45.3 17.3 %collective-permute-done.8.refs_2_.refs_1_.refs_6_.refs_8_ = bf16[128,4096]{1,0:T(8,128)(2,1)S(1)} collective-permute-done((bf16[128,4096]{1,0:T(8,128)(2,1)S(1)}, bf16[128,4096]{1,0:T(8,128)(2,1)S(1)}, u32[]{:S(2)}, u32[]{:S(2)}) %collective-permute-start.8) | collective-permute-done | bytes 1048608 | tf_op jit(solution)/shard_map/ppermute | solution.py:24
  62.7 1.8 %collective-permute-start.14 = (bf16[128,2048]{1,0:T(8,128)(2,1)S(1)}, bf16[128,2048]{1,0:T(8,128)(2,1)S(1)}, u32[]{:S(2)}, u32[]{:S(2)}) collective-permute-start(bf16[128,2048]{1,0:T(8,128)(2,1)S(1)} %join_columns.38.refs_1_.refs_2_), channel_id=1, source_target_pairs={{0,16},{8,24},{16,0},{24,8},{1,17},{9,25},{17,1},{25,9},{2,18},{10... | collective-permute-start | bytes 1572872 | tf_op jit(solution)/shard_map/ppermute | solution.py:24
  64.5 0.6 collective-permute-start.15
  65.1 1.6 collective-permute-start.12
  66.8 4.2 %collective-permute-start.11 = (bf16[128,2048]{1,0:T(8,128)(2,1)S(1)}, bf16[128,2048]{1,0:T(8,128)(2,1)S(1)}, u32[]{:S(2)}, u32[]{:S(2)}) collective-permute-start(bf16[128,2048]{1,0:T(8,128)(2,1)S(1)} %join_columns.41.refs_1_), channel_id=1, source_target_pairs={{0,6},{1,7},{2,4},{3,5},{4,2},{5,3},{6,0},{7,1},{8,14},{9,15},{10,... | collective-permute-start | bytes 1572872 | tf_op jit(solution)/shard_map/ppermute | solution.py:24
  70.9 3.9 %collective-permute-done.14.refs_2_.refs_3_.refs_7_.refs_9_ = bf16[128,2048]{1,0:T(8,128)(2,1)S(1)} collective-permute-done((bf16[128,2048]{1,0:T(8,128)(2,1)S(1)}, bf16[128,2048]{1,0:T(8,128)(2,1)S(1)}, u32[]{:S(2)}, u32[]{:S(2)}) %collective-permute-start.14) | collective-permute-done | bytes 524320 | tf_op jit(solution)/shard_map/ppermute | solution.py:24
  74.8 0.9 collective-permute-start.21
  75.8 0.2 join_columns.43.refs_0_
  76.0 17.1 %collective-permute-done.15.refs_1_.refs_9_.refs_6_ = bf16[128,2048]{1,0:T(8,128)(2,1)S(1)} collective-permute-done((bf16[128,2048]{1,0:T(8,128)(2,1)S(1)}, bf16[128,2048]{1,0:T(8,128)(2,1)S(1)}, u32[]{:S(2)}, u32[]{:S(2)}) %collective-permute-start.15) | collective-permute-done | bytes 524320 | tf_op jit(solution)/shard_map/ppermute | solution.py:24
  93.1 0.8 copy-done.13
  93.9 0.4 collective-permute-start.20
  94.3 4.4 %collective-permute-done.16.refs_2_.refs_4_.refs_5_ = bf16[128,12288]{1,0:T(8,128)(2,1)S(1)} collective-permute-done((bf16[128,12288]{1,0:T(8,128)(2,1)S(1)}, bf16[128,12288]{1,0:T(8,128)(2,1)S(1)}, u32[]{:S(2)}, u32[]{:S(2)}) %collective-permute-start.16) | collective-permute-done | bytes 3145760 | tf_op jit(solution)/shard_map/ppermute | solution.py:24
  98.8 1.1 collective-permute-start.17
  99.9 0.1 collective-permute-start.23
  100.0 2.3 %collective-permute-done.12.refs_1_ = bf16[128,2048]{1,0:T(8,128)(2,1)S(1)} collective-permute-done((bf16[128,2048]{1,0:T(8,128)(2,1)S(1)}, bf16[128,2048]{1,0:T(8,128)(2,1)S(1)}, u32[]{:S(2)}, u32[]{:S(2)}) %collective-permute-start.12) | collective-permute-done | bytes 524320 | tf_op jit(solution)/shard_map/ppermute | solution.py:24
  102.3 4.6 %collective-permute-start.18 = (bf16[128,1024]{1,0:T(8,128)(2,1)S(1)}, bf16[128,1024]{1,0:T(8,128)(2,1)S(1)}, u32[]{:S(2)}, u32[]{:S(2)}) collective-permute-start(bf16[128,1024]{1,0:T(8,128)(2,1)S(1)} %join_columns.47.refs_2_), channel_id=1, source_target_pairs={{0,7},{1,6},{2,5},{3,4},{4,3},{5,2},{6,1},{7,0},{8,15},{9,14},{10,... | collective-permute-start | bytes 786440 | tf_op jit(solution)/shard_map/ppermute | solution.py:24
  106.9 5.9 %collective-permute-done.17.refs_3_.refs_1_.refs_10_.refs_7_ = bf16[128,2048]{1,0:T(8,128)(2,1)S(1)} collective-permute-done((bf16[128,2048]{1,0:T(8,128)(2,1)S(1)}, bf16[128,2048]{1,0:T(8,128)(2,1)S(1)}, u32[]{:S(2)}, u32[]{:S(2)}) %collective-permute-start.17) | collective-permute-done | bytes 524320 | tf_op jit(solution)/shard_map/ppermute | solution.py:24
  112.9 3.5 %collective-permute-start.19 = (bf16[128,4096]{1,0:T(8,128)(2,1)S(1)}, bf16[128,4096]{1,0:T(8,128)(2,1)S(1)}, u32[]{:S(2)}, u32[]{:S(2)}) collective-permute-start(bf16[128,4096]{1,0:T(8,128)(2,1)S(1)} %join_columns.48.refs_1_.refs_0_), channel_id=1, source_target_pairs={{0,16},{8,24},{16,0},{24,8},{1,17},{9,25},{17,1},{25,9},{2,18},{10... | collective-permute-start | bytes 3145736 | tf_op jit(solution)/shard_map/ppermute | solution.py:24
  116.3 5.1 %collective-permute-done.21.refs_0_.refs_1_.refs_11_.refs_7_ = bf16[128,2048]{1,0:T(8,128)(2,1)S(1)} collective-permute-done((bf16[128,2048]{1,0:T(8,128)(2,1)S(1)}, bf16[128,2048]{1,0:T(8,128)(2,1)S(1)}, u32[]{:S(2)}, u32[]{:S(2)}) %collective-permute-start.21) | collective-permute-done | bytes 524320 | tf_op jit(solution)/shard_map/ppermute | solution.py:24
  121.5 0.1 join_columns.50.refs_0_
  121.7 0.1 collective-permute-start.22
  121.8 0.9 copy-done.1
  122.6 0.2 copy-done.3
  122.8 0.3 copy-done.5
  123.2 0.3 copy-done.7
  123.5 0.1 copy-done.9
  123.6 0.2 copy-done.11
  123.8 5.4 %product_and_squares.4.refs_2_.refs_13_ = f32[4,1024,512]{2,1,0:T(8,128)S(1)} custom-call(bf16[128,2048]{1,0:T(8,128)(2,1)S(1)} %copy-done.1, bf16[128,4096]{1,0:T(8,128)(2,1)S(1)} %join_columns.34.refs_1_.refs_0_, bf16[128,2048]{1,0:T(8,128)(2,1)S(1)} %join_columns.38.refs_1_.refs_2_, bf16[128,4096]{1,0:T(8,128)(2,1)S(1)} %copy-done.5, ...), custom_call_target="tpu_custom_call" | custom-call | flops 2147483648 | bytes 6291456 | tf_op jit(solution)/shard_map/product_and_squares/pallas_call | solution.py:197
  129.2 0.6 collective-permute-start.27
  129.8 7.7 %collective-permute-done.19.refs_3_.refs_1_.refs_6_.refs_4_ = bf16[128,4096]{1,0:T(8,128)(2,1)S(1)} collective-permute-done((bf16[128,4096]{1,0:T(8,128)(2,1)S(1)}, bf16[128,4096]{1,0:T(8,128)(2,1)S(1)}, u32[]{:S(2)}, u32[]{:S(2)}) %collective-permute-start.19) | collective-permute-done | bytes 1048608 | tf_op jit(solution)/shard_map/ppermute | solution.py:24
  137.6 1.8 %collective-permute-start.24 = (bf16[128,1024]{1,0:T(8,128)(2,1)S(1)}, bf16[128,1024]{1,0:T(8,128)(2,1)S(1)}, u32[]{:S(2)}, u32[]{:S(2)}) collective-permute-start(bf16[128,1024]{1,0:T(8,128)(2,1)S(1)} %join_columns.51.refs_2_.refs_0_), channel_id=1, source_target_pairs={{0,16},{8,24},{16,0},{24,8},{1,17},{9,25},{17,1},{25,9},{2,18},{10... | collective-permute-start | bytes 786440 | tf_op jit(solution)/shard_map/ppermute | solution.py:24
  139.4 0.1 join_columns.52.refs_0_
  139.6 0.1 collective-permute-start.25
  139.7 6.6 %product_and_squares.5.refs_2_.refs_9_ = f32[4,1024,512]{2,1,0:T(8,128)S(1)} custom-call(bf16[128,2048]{1,0:T(8,128)(2,1)S(1)} %copy-done.1, bf16[128,4096]{1,0:T(8,128)(2,1)S(1)} %join_columns.34.refs_1_.refs_0_, bf16[128,2048]{1,0:T(8,128)(2,1)S(1)} %join_columns.38.refs_1_.refs_2_, bf16[128,2048]{1,0:T(8,128)(2,1)S(1)} %join_columns.45.refs_1_.refs_0_.refs_3_, ...), custom_call_target="tpu_custom_call" | custom-call | flops 2684354560 | bytes 7864320 | tf_op jit(solution)/shard_map/product_and_squares/pallas_call | solution.py:197
  146.4 0.3 collective-permute-start.26
  146.7 0.3 collective-permute-start.28
  147.0 1.7 collective-permute-done.28.refs_5_
  148.7 5.9 %product_and_squares.6 = (f32[4,1024,512]{2,1,0:T(8,128)S(1)}, f32[1,8,128]{2,1,0:T(8,128)S(1)}) custom-call(bf16[128,4096]{1,0:T(8,128)(2,1)S(1)} %join_columns.48.refs_1_.refs_0_, bf16[128,2048]{1,0:T(8,128)(2,1)S(1)} %join_columns.45.refs_1_.refs_0_.refs_3_, bf16[128,1024]{1,0:T(8,128)(2,1)S(1)} %join_columns.51.refs_2_.refs_0_, ...), custom_call_target="tpu_custom_call", output_to_operand_aliasing={{0}: (13, {})} | custom-call | flops 2147483648 | bytes 6291456 | tf_op jit(solution)/shard_map/product_and_squares/pallas_call | solution.py:197
  154.6 0.5 collective-permute-done.26.refs_1_.refs_5_
  155.2 0.1 collective-permute-start.29
  155.2 1.9 %collective-permute-done.29.refs_3_ = bf16[128,2048]{1,0:T(8,128)(2,1)S(1)} collective-permute-done((bf16[128,2048]{1,0:T(8,128)(2,1)S(1)}, bf16[128,2048]{1,0:T(8,128)(2,1)S(1)}, u32[]{:S(2)}, u32[]{:S(2)}) %collective-permute-start.29) | collective-permute-done | bytes 524320 | tf_op jit(solution)/shard_map/ppermute | solution.py:24
  157.1 5.8 %product_and_squares.7 = (f32[4,1024,512]{2,1,0:T(8,128)S(1)}, f32[32,8,128]{2,1,0:T(8,128)S(1)}) custom-call(bf16[128,4096]{1,0:T(8,128)(2,1)S(1)} %join_columns.48.refs_1_.refs_0_, bf16[128,1024]{1,0:T(8,128)(2,1)S(1)} %join_columns.53.refs_2_.refs_0_.refs_1_, ...), custom_call_target="tpu_custom_call", output_to_operand_aliasing={{0}: (9, {})} | custom-call | flops 1610612736 | bytes 4718592 | tf_op jit(solution)/shard_map/product_and_squares/pallas_call | solution.py:197
  162.9 9.4 %all_to_all.5.sums_ref = f32[32,8,128]{2,1,0:T(8,128)S(1)} all-to-all(f32[32,8,128]{2,1,0:T(8,128)S(1)} %get-tuple-element.35), channel_id=1, replica_groups=mesh['user'=4,'tok'=8] {'user','tok'}, dimensions={0} | all-to-all | bytes 262144 | tf_op jit(solution)/shard_map/all_to_all | solution.py:479
  172.3 4.8 %weighted_sum.1 = f32[2048,512]{1,0:T(8,128)} custom-call(s32[1]{0:T(128)} %bitcast.user_ref, f32[32,8,128]{2,1,0:T(8,128)S(1)} %all_to_all.5.sums_ref, f32[4,1024,512]{2,1,0:T(8,128)S(1)} %get-tuple-element.33.refs_3_.refs_0_, f32[4,1024,512]{2,1,0:T(8,128)S(1)} %get-tuple-element.36.refs_1_), custom_call_target="tpu_custom_call" | custom-call | tf_op jit(solution)/shard_map/weighted_sum/pallas_call | solution.py:254
  (72 shorter events, 0.9 us)
Async XLA Ops:
  0.7 1.0 copy-start.15
  1.7 10.3 %collective-permute-start = (bf16[128,512]{1,0:T(8,128)(2,1)S(1)}, bf16[128,512]{1,0:T(8,128)(2,1)S(1)}, u32[]{:S(2)}, u32[]{:S(2)}) collective-permute-start(bf16[128,512]{1,0:T(8,128)(2,1)S(1)} %get-tuple-element.24), channel_id=1, source_target_pairs={{0,8},{8,0},{16,24},{24,16},{1,9},{9,1},{17,25},{25,17},{2,10},{10... | collective-permute-start | bytes 393224 | tf_op jit(solution)/shard_map/ppermute | solution.py:24
  2.3 9.7 %collective-permute-start.1 = (bf16[128,512]{1,0:T(8,128)(2,1)S(1)}, bf16[128,512]{1,0:T(8,128)(2,1)S(1)}, u32[]{:S(2)}, u32[]{:S(2)}) collective-permute-start(bf16[128,512]{1,0:T(8,128)(2,1)S(1)} %get-tuple-element.25), channel_id=1, source_target_pairs={{0,16},{8,24},{16,0},{24,8},{1,17},{9,25},{17,1},{25,9},{2,18},{10... | collective-permute-start | bytes 393224 | tf_op jit(solution)/shard_map/ppermute | solution.py:24
  4.8 7.2 %collective-permute-start.2 = (bf16[128,512]{1,0:T(8,128)(2,1)S(1)}, bf16[128,512]{1,0:T(8,128)(2,1)S(1)}, u32[]{:S(2)}, u32[]{:S(2)}) collective-permute-start(bf16[128,512]{1,0:T(8,128)(2,1)S(1)} %get-tuple-element.26), channel_id=1, source_target_pairs={{0,24},{8,16},{16,8},{24,0},{1,25},{9,17},{17,9},{25,1},{2,26},{10... | collective-permute-start | bytes 393224 | tf_op jit(solution)/shard_map/ppermute | solution.py:24
  4.9 2.2 %copy-start.12 = (bf16[1,128,16384]{2,1,0:T(8,128)(2,1)S(1)}, bf16[1,128,16384]{2,1,0:T(8,128)(2,1)}, u32[]{:S(2)}) copy-start(bf16[1,128,16384]{2,1,0:T(8,128)(2,1)} %hidden_ref.1) | copy-start | bytes 12582916
  7.5 33.1 %collective-permute-start.7 = (bf16[128,2048]{1,0:T(8,128)(2,1)S(1)}, bf16[128,2048]{1,0:T(8,128)(2,1)S(1)}, u32[]{:S(2)}, u32[]{:S(2)}) collective-permute-start(bf16[128,2048]{1,0:T(8,128)(2,1)S(1)} %join_columns.28.refs_1_), channel_id=1, source_target_pairs={{0,4},{1,5},{2,6},{3,7},{4,0},{5,1},{6,2},{7,3},{8,12},{9,13},{10,... | collective-permute-start | bytes 1572872 | tf_op jit(solution)/shard_map/ppermute | solution.py:24
  10.4 30.0 %copy-start = (bf16[128,2048]{1,0:T(8,128)(2,1)}, bf16[128,2048]{1,0:T(8,128)(2,1)S(1)}, u32[]{:S(2)}) copy-start(bf16[128,2048]{1,0:T(8,128)(2,1)S(1)} %join_columns.29.refs_4_.refs_1_.refs_0_) | copy-start | bytes 1572868
  10.5 14.0 %collective-permute-start.5 = (bf16[128,2048]{1,0:T(8,128)(2,1)S(1)}, bf16[128,2048]{1,0:T(8,128)(2,1)S(1)}, u32[]{:S(2)}, u32[]{:S(2)}) collective-permute-start(bf16[128,2048]{1,0:T(8,128)(2,1)S(1)} %join_columns.29.refs_4_.refs_1_.refs_0_), channel_id=1, source_target_pairs={{0,16},{8,24},{16,0},{24,8},{1,17},{9,25},{17,1},{25,9},{2,18},{10... | collective-permute-start | bytes 1572872 | tf_op jit(solution)/shard_map/ppermute | solution.py:24
  12.1 26.5 %copy-start.2 = (bf16[128,2048]{1,0:T(8,128)(2,1)}, bf16[128,2048]{1,0:T(8,128)(2,1)S(1)}, u32[]{:S(2)}) copy-start(bf16[128,2048]{1,0:T(8,128)(2,1)S(1)} %join_columns.30.refs_0_.refs_1_.refs_8_.refs_11_) | copy-start | bytes 1572868
  12.2 26.3 %collective-permute-start.3 = (bf16[128,4096]{1,0:T(8,128)(2,1)S(1)}, bf16[128,4096]{1,0:T(8,128)(2,1)S(1)}, u32[]{:S(2)}, u32[]{:S(2)}) collective-permute-start(bf16[128,4096]{1,0:T(8,128)(2,1)S(1)} %join_columns.32.refs_1_), channel_id=1, source_target_pairs={{0,1},{1,0},{2,3},{3,2},{4,5},{5,4},{6,7},{7,6},{8,9},{9,8},{10,11... | collective-permute-start | bytes 3145736 | tf_op jit(solution)/shard_map/ppermute | solution.py:24
  13.8 24.6 %collective-permute-start.4 = (bf16[128,2048]{1,0:T(8,128)(2,1)S(1)}, bf16[128,2048]{1,0:T(8,128)(2,1)S(1)}, u32[]{:S(2)}, u32[]{:S(2)}) collective-permute-start(bf16[128,2048]{1,0:T(8,128)(2,1)S(1)} %join_columns.33.refs_0_), channel_id=1, source_target_pairs={{0,2},{1,3},{2,0},{3,1},{4,6},{5,7},{6,4},{7,5},{8,10},{9,11},{10,... | collective-permute-start | bytes 1572872 | tf_op jit(solution)/shard_map/ppermute | solution.py:24
  15.5 51.2 %collective-permute-start.10 = (bf16[128,2048]{1,0:T(8,128)(2,1)S(1)}, bf16[128,2048]{1,0:T(8,128)(2,1)S(1)}, u32[]{:S(2)}, u32[]{:S(2)}) collective-permute-start(bf16[128,2048]{1,0:T(8,128)(2,1)S(1)} %join_columns.31.refs_2_), channel_id=1, source_target_pairs={{0,4},{1,5},{2,6},{3,7},{4,0},{5,1},{6,2},{7,3},{8,12},{9,13},{10,... | collective-permute-start | bytes 1572872 | tf_op jit(solution)/shard_map/ppermute | solution.py:24
  24.4 16.1 %copy-start.8 = (bf16[128,2048]{1,0:T(8,128)(2,1)}, bf16[128,2048]{1,0:T(8,128)(2,1)S(1)}, u32[]{:S(2)}) copy-start(bf16[128,2048]{1,0:T(8,128)(2,1)S(1)} %collective-permute-done.5.refs_3_.refs_1_.refs_5_.refs_7_) | copy-start | bytes 1572868
  38.5 2.1 %copy-start.6 = (bf16[128,4096]{1,0:T(8,128)(2,1)}, bf16[128,4096]{1,0:T(8,128)(2,1)S(1)}, u32[]{:S(2)}) copy-start(bf16[128,4096]{1,0:T(8,128)(2,1)S(1)} %collective-permute-done.3.refs_0_.refs_9_.refs_12_) | copy-start | bytes 3145732
  38.6 24.0 %collective-permute-start.8 = (bf16[128,4096]{1,0:T(8,128)(2,1)S(1)}, bf16[128,4096]{1,0:T(8,128)(2,1)S(1)}, u32[]{:S(2)}, u32[]{:S(2)}) collective-permute-start(bf16[128,4096]{1,0:T(8,128)(2,1)S(1)} %join_columns.34.refs_1_.refs_0_), channel_id=1, source_target_pairs={{0,16},{8,24},{16,0},{24,8},{1,17},{9,25},{17,1},{25,9},{2,18},{10... | collective-permute-start | bytes 3145736 | tf_op jit(solution)/shard_map/ppermute | solution.py:24
  40.2 24.3 %collective-permute-start.6 = (bf16[128,2048]{1,0:T(8,128)(2,1)S(1)}, bf16[128,2048]{1,0:T(8,128)(2,1)S(1)}, u32[]{:S(2)}, u32[]{:S(2)}) collective-permute-start(bf16[128,2048]{1,0:T(8,128)(2,1)S(1)} %join_columns.35.refs_2_), channel_id=1, source_target_pairs={{0,2},{1,3},{2,0},{3,1},{4,6},{5,7},{6,4},{7,5},{8,10},{9,11},{10,... | collective-permute-start | bytes 1572872 | tf_op jit(solution)/shard_map/ppermute | solution.py:24
  40.5 4.9 %collective-permute-start.9 = (bf16[128,4096]{1,0:T(8,128)(2,1)S(1)}, bf16[128,4096]{1,0:T(8,128)(2,1)S(1)}, u32[]{:S(2)}, u32[]{:S(2)}) collective-permute-start(bf16[128,4096]{1,0:T(8,128)(2,1)S(1)} %join_columns.36.refs_0_), channel_id=1, source_target_pairs={{0,8},{8,0},{16,24},{24,16},{1,9},{9,1},{17,25},{25,17},{2,10},{10... | collective-permute-start | bytes 3145736 | tf_op jit(solution)/shard_map/ppermute | solution.py:24
  40.6 53.2 %collective-permute-start.13 = (bf16[128,2048]{1,0:T(8,128)(2,1)S(1)}, bf16[128,2048]{1,0:T(8,128)(2,1)S(1)}, u32[]{:S(2)}, u32[]{:S(2)}) collective-permute-start(bf16[128,2048]{1,0:T(8,128)(2,1)S(1)} %join_columns.37.refs_1_), channel_id=1, source_target_pairs={{0,5},{1,4},{2,7},{3,6},{4,1},{5,0},{6,3},{7,2},{8,13},{9,12},{10,... | collective-permute-start | bytes 1572872 | tf_op jit(solution)/shard_map/ppermute | solution.py:24
  45.3 21.4 %copy-start.4 = (bf16[128,4096]{1,0:T(8,128)(2,1)}, bf16[128,4096]{1,0:T(8,128)(2,1)S(1)}, u32[]{:S(2)}) copy-start(bf16[128,4096]{1,0:T(8,128)(2,1)S(1)} %collective-permute-done.9.refs_3_.refs_4_) | copy-start | bytes 3145732
  62.7 12.1 %collective-permute-start.14 = (bf16[128,2048]{1,0:T(8,128)(2,1)S(1)}, bf16[128,2048]{1,0:T(8,128)(2,1)S(1)}, u32[]{:S(2)}, u32[]{:S(2)}) collective-permute-start(bf16[128,2048]{1,0:T(8,128)(2,1)S(1)} %join_columns.38.refs_1_.refs_2_), channel_id=1, source_target_pairs={{0,16},{8,24},{16,0},{24,8},{1,17},{9,25},{17,1},{25,9},{2,18},{10... | collective-permute-start | bytes 1572872 | tf_op jit(solution)/shard_map/ppermute | solution.py:24
  64.5 2.2 %copy-start.10 = (bf16[128,2048]{1,0:T(8,128)(2,1)}, bf16[128,2048]{1,0:T(8,128)(2,1)S(1)}, u32[]{:S(2)}) copy-start(bf16[128,2048]{1,0:T(8,128)(2,1)S(1)} %collective-permute-done.6.refs_0_.refs_1_.refs_10_.refs_13_) | copy-start | bytes 1572868
  64.5 28.5 %collective-permute-start.15 = (bf16[128,2048]{1,0:T(8,128)(2,1)S(1)}, bf16[128,2048]{1,0:T(8,128)(2,1)S(1)}, u32[]{:S(2)}, u32[]{:S(2)}) collective-permute-start(bf16[128,2048]{1,0:T(8,128)(2,1)S(1)} %join_columns.39.refs_1_), channel_id=1, source_target_pairs={{0,1},{1,0},{2,3},{3,2},{4,5},{5,4},{6,7},{7,6},{8,9},{9,8},{10,11... | collective-permute-start | bytes 1572872 | tf_op jit(solution)/shard_map/ppermute | solution.py:24
  65.1 37.1 %collective-permute-start.12 = (bf16[128,2048]{1,0:T(8,128)(2,1)S(1)}, bf16[128,2048]{1,0:T(8,128)(2,1)S(1)}, u32[]{:S(2)}, u32[]{:S(2)}) collective-permute-start(bf16[128,2048]{1,0:T(8,128)(2,1)S(1)} %join_columns.40.refs_0_), channel_id=1, source_target_pairs={{0,3},{1,2},{2,1},{3,0},{4,7},{5,6},{6,5},{7,4},{8,11},{9,10},{10,... | collective-permute-start | bytes 1572872 | tf_op jit(solution)/shard_map/ppermute | solution.py:24
  66.8 33.1 %collective-permute-start.11 = (bf16[128,2048]{1,0:T(8,128)(2,1)S(1)}, bf16[128,2048]{1,0:T(8,128)(2,1)S(1)}, u32[]{:S(2)}, u32[]{:S(2)}) collective-permute-start(bf16[128,2048]{1,0:T(8,128)(2,1)S(1)} %join_columns.41.refs_1_), channel_id=1, source_target_pairs={{0,6},{1,7},{2,4},{3,5},{4,2},{5,3},{6,0},{7,1},{8,14},{9,15},{10,... | collective-permute-start | bytes 1572872 | tf_op jit(solution)/shard_map/ppermute | solution.py:24
  74.8 46.6 %collective-permute-start.21 = (bf16[128,2048]{1,0:T(8,128)(2,1)S(1)}, bf16[128,2048]{1,0:T(8,128)(2,1)S(1)}, u32[]{:S(2)}, u32[]{:S(2)}) collective-permute-start(bf16[128,2048]{1,0:T(8,128)(2,1)S(1)} %join_columns.42.refs_4_), channel_id=1, source_target_pairs={{0,2},{1,3},{2,0},{3,1},{4,6},{5,7},{6,4},{7,5},{8,10},{9,11},{10,... | collective-permute-start | bytes 1572872 | tf_op jit(solution)/shard_map/ppermute | solution.py:24
  93.1 0.8 copy-start.13
  93.1 5.7 %collective-permute-start.16 = (bf16[128,12288]{1,0:T(8,128)(2,1)S(1)}, bf16[128,12288]{1,0:T(8,128)(2,1)S(1)}, u32[]{:S(2)}, u32[]{:S(2)}) collective-permute-start(bf16[128,12288]{1,0:T(8,128)(2,1)S(1)} %join_columns.43.refs_0_), channel_id=1, source_target_pairs={{0,8},{8,0},{16,24},{24,16},{1,9},{9,1},{17,25},{25,17},{2,10},{10... | collective-permute-start | bytes 9437192 | tf_op jit(solution)/shard_map/ppermute | solution.py:24
  93.9 35.3 %collective-permute-start.20 = (bf16[128,1024]{1,0:T(8,128)(2,1)S(1)}, bf16[128,1024]{1,0:T(8,128)(2,1)S(1)}, u32[]{:S(2)}, u32[]{:S(2)}) collective-permute-start(bf16[128,1024]{1,0:T(8,128)(2,1)S(1)} %join_columns.44.refs_1_), channel_id=1, source_target_pairs={{0,7},{1,6},{2,5},{3,4},{4,3},{5,2},{6,1},{7,0},{8,15},{9,14},{10,... | collective-permute-start | bytes 786440 | tf_op jit(solution)/shard_map/ppermute | solution.py:24
  98.8 14.0 %collective-permute-start.17 = (bf16[128,2048]{1,0:T(8,128)(2,1)S(1)}, bf16[128,2048]{1,0:T(8,128)(2,1)S(1)}, u32[]{:S(2)}, u32[]{:S(2)}) collective-permute-start(bf16[128,2048]{1,0:T(8,128)(2,1)S(1)} %join_columns.45.refs_1_.refs_0_.refs_3_), channel_id=1, source_target_pairs={{0,16},{8,24},{16,0},{24,8},{1,17},{9,25},{17,1},{25,9},{2,18},{10... | collective-permute-start | bytes 1572872 | tf_op jit(solution)/shard_map/ppermute | solution.py:24
  99.9 39.7 %collective-permute-start.23 = (bf16[128,2048]{1,0:T(8,128)(2,1)S(1)}, bf16[128,2048]{1,0:T(8,128)(2,1)S(1)}, u32[]{:S(2)}, u32[]{:S(2)}) collective-permute-start(bf16[128,2048]{1,0:T(8,128)(2,1)S(1)} %join_columns.46.refs_0_), channel_id=1, source_target_pairs={{0,1},{1,0},{2,3},{3,2},{4,5},{5,4},{6,7},{7,6},{8,9},{9,8},{10,11... | collective-permute-start | bytes 1572872 | tf_op jit(solution)/shard_map/ppermute | solution.py:24
  102.3 44.0 %collective-permute-start.18 = (bf16[128,1024]{1,0:T(8,128)(2,1)S(1)}, bf16[128,1024]{1,0:T(8,128)(2,1)S(1)}, u32[]{:S(2)}, u32[]{:S(2)}) collective-permute-start(bf16[128,1024]{1,0:T(8,128)(2,1)S(1)} %join_columns.47.refs_2_), channel_id=1, source_target_pairs={{0,7},{1,6},{2,5},{3,4},{4,3},{5,2},{6,1},{7,0},{8,15},{9,14},{10,... | collective-permute-start | bytes 786440 | tf_op jit(solution)/shard_map/ppermute | solution.py:24
  112.9 24.7 %collective-permute-start.19 = (bf16[128,4096]{1,0:T(8,128)(2,1)S(1)}, bf16[128,4096]{1,0:T(8,128)(2,1)S(1)}, u32[]{:S(2)}, u32[]{:S(2)}) collective-permute-start(bf16[128,4096]{1,0:T(8,128)(2,1)S(1)} %join_columns.48.refs_1_.refs_0_), channel_id=1, source_target_pairs={{0,16},{8,24},{16,0},{24,8},{1,17},{9,25},{17,1},{25,9},{2,18},{10... | collective-permute-start | bytes 3145736 | tf_op jit(solution)/shard_map/ppermute | solution.py:24
  121.6 1.0 copy-start.1
  121.6 1.2 copy-start.3
  121.6 1.5 copy-start.5
  121.6 1.8 %copy-start.7 = (bf16[128,4096]{1,0:T(8,128)(2,1)S(1)}, bf16[128,4096]{1,0:T(8,128)(2,1)}, u32[]{:S(2)}) copy-start(bf16[128,4096]{1,0:T(8,128)(2,1)} %copy-done.6) | copy-start | bytes 3145732
  121.6 2.0 %copy-start.9 = (bf16[128,2048]{1,0:T(8,128)(2,1)S(1)}, bf16[128,2048]{1,0:T(8,128)(2,1)}, u32[]{:S(2)}) copy-start(bf16[128,2048]{1,0:T(8,128)(2,1)} %copy-done.8) | copy-start | bytes 1572868
  121.7 2.1 %copy-start.11 = (bf16[128,2048]{1,0:T(8,128)(2,1)S(1)}, bf16[128,2048]{1,0:T(8,128)(2,1)}, u32[]{:S(2)}) copy-start(bf16[128,2048]{1,0:T(8,128)(2,1)} %copy-done.10) | copy-start | bytes 1572868
  121.7 8.2 %collective-permute-start.22 = (bf16[128,4096]{1,0:T(8,128)(2,1)S(1)}, bf16[128,4096]{1,0:T(8,128)(2,1)S(1)}, u32[]{:S(2)}, u32[]{:S(2)}) collective-permute-start(bf16[128,4096]{1,0:T(8,128)(2,1)S(1)} %join_columns.50.refs_0_), channel_id=1, source_target_pairs={{0,8},{8,0},{16,24},{24,16},{1,9},{9,1},{17,25},{25,17},{2,10},{10... | collective-permute-start | bytes 3145736 | tf_op jit(solution)/shard_map/ppermute | solution.py:24
  129.2 17.8 %collective-permute-start.27 = (bf16[128,2048]{1,0:T(8,128)(2,1)S(1)}, bf16[128,2048]{1,0:T(8,128)(2,1)S(1)}, u32[]{:S(2)}, u32[]{:S(2)}) collective-permute-start(bf16[128,2048]{1,0:T(8,128)(2,1)S(1)} %join_columns.49.refs_2_), channel_id=1, source_target_pairs={{0,1},{1,0},{2,3},{3,2},{4,5},{5,4},{6,7},{7,6},{8,9},{9,8},{10,11... | collective-permute-start | bytes 1572872 | tf_op jit(solution)/shard_map/ppermute | solution.py:24
  137.6 8.7 %collective-permute-start.24 = (bf16[128,1024]{1,0:T(8,128)(2,1)S(1)}, bf16[128,1024]{1,0:T(8,128)(2,1)S(1)}, u32[]{:S(2)}, u32[]{:S(2)}) collective-permute-start(bf16[128,1024]{1,0:T(8,128)(2,1)S(1)} %join_columns.51.refs_2_.refs_0_), channel_id=1, source_target_pairs={{0,16},{8,24},{16,0},{24,8},{1,17},{9,25},{17,1},{25,9},{2,18},{10... | collective-permute-start | bytes 786440 | tf_op jit(solution)/shard_map/ppermute | solution.py:24
  139.6 6.8 %collective-permute-start.25 = (bf16[128,8192]{1,0:T(8,128)(2,1)S(1)}, bf16[128,8192]{1,0:T(8,128)(2,1)S(1)}, u32[]{:S(2)}, u32[]{:S(2)}) collective-permute-start(bf16[128,8192]{1,0:T(8,128)(2,1)S(1)} %join_columns.52.refs_0_), channel_id=1, source_target_pairs={{0,8},{8,0},{16,24},{24,16},{1,9},{9,1},{17,25},{25,17},{2,10},{10... | collective-permute-start | bytes 6291464 | tf_op jit(solution)/shard_map/ppermute | solution.py:24
  146.4 8.8 %collective-permute-start.26 = (bf16[128,1024]{1,0:T(8,128)(2,1)S(1)}, bf16[128,1024]{1,0:T(8,128)(2,1)S(1)}, u32[]{:S(2)}, u32[]{:S(2)}) collective-permute-start(bf16[128,1024]{1,0:T(8,128)(2,1)S(1)} %join_columns.53.refs_2_.refs_0_.refs_1_), channel_id=1, source_target_pairs={{0,16},{8,24},{16,0},{24,8},{1,17},{9,25},{17,1},{25,9},{2,18},{10... | collective-permute-start | bytes 786440 | tf_op jit(solution)/shard_map/ppermute | solution.py:24
  146.7 2.0 %copy-start.14 = (bf16[128,2048]{1,0:T(8,128)(2,1)S(1)}, bf16[128,2048]{1,0:T(8,128)(2,1)}, u32[]{:S(2)}) copy-start(bf16[128,2048]{1,0:T(8,128)(2,1)} %copy-done.13) | copy-start | bytes 1572868
  146.7 2.0 %collective-permute-start.28 = (bf16[128,2048]{1,0:T(8,128)(2,1)S(1)}, bf16[128,2048]{1,0:T(8,128)(2,1)S(1)}, u32[]{:S(2)}, u32[]{:S(2)}) collective-permute-start(bf16[128,2048]{1,0:T(8,128)(2,1)S(1)} %join_columns.54.refs_0_), channel_id=1, source_target_pairs={{0,8},{8,0},{16,24},{24,16},{1,9},{9,1},{17,25},{25,17},{2,10},{10... | collective-permute-start | bytes 1572872 | tf_op jit(solution)/shard_map/ppermute | solution.py:24
  155.2 2.0 %collective-permute-start.29 = (bf16[128,2048]{1,0:T(8,128)(2,1)S(1)}, bf16[128,2048]{1,0:T(8,128)(2,1)S(1)}, u32[]{:S(2)}, u32[]{:S(2)}) collective-permute-start(bf16[128,2048]{1,0:T(8,128)(2,1)S(1)} %join_columns.55), channel_id=1, source_target_pairs={{0,8},{8,0},{16,24},{24,16},{1,9},{9,1},{17,25},{25,17},{2,10},{10... | collective-permute-start | bytes 1572872 | tf_op jit(solution)/shard_map/ppermute | solution.py:24

commit v19 on v18

--- a/solution.py
+++ b/solution.py
@@ -250,7 +250,7 @@
     heights = [gradient.shape[1] for gradient in gradients]
     starts = [sum(heights[:i]) for i in range(len(heights))]
     rows = sum(heights)
-    tile = math.gcd(256, *heights)
+    tile = math.gcd(512, *heights)
     return pl.pallas_call(
         functools.partial(combine_kernel, user_count, clip_bound, scaling, starts),
         grid=(rows // tile,),

time: 177 us -> 176 us (level)
  no operation moved by 1% of the time
where the time goes in v19:
time: 176 us
  waiting for transfers between devices  88.7 us (50%)
  starting transfers between devices  41.5 us (24%)
  Pallas kernels  29.4 us (17%)
  blocking collectives  9.44 us (5%)
  local copies, waits for them, and re-layouts  6.07 us (3%)
    ppermute x30, waiting for transfers between devices, exchange(): return lax.ppermute(block, axis, [(i, i ^ distance) for i in range(size)])  88.7 us
    ppermute x30, starting transfers between devices, exchange(): return lax.ppermute(block, axis, [(i, i ^ distance) for i in range(size)])  41.5 us
    pallas_call x4, Pallas kernels, product(): pl.pallas_call(functools.partial(product_kernel, left_places, right_place...  23.7 us
    all_to_all x1, blocking collectives, body(): lax.all_to_all(gradients[1][1], ('user', 'tok'), split_axis=0, concat_axi...  9.44 us
    unnamed x32, local copies, waits for them, and re-layouts  6.07 us
    pallas_call x1, Pallas kernels, combine(): pl.pallas_call(functools.partial(combine_kernel, user_count, clip_bound,...  3.88 us
  transfers between devices with their start and end apart: 30, of which 13 were waited for; matrix products, arithmetic and copies ran while one was open for 0% of the time, Pallas kernels for 11%

profile of v19, /device:TPU:0, one launch (start us, length us, event | category | flops | bytes accessed | tf_op | source)
XLA Modules:
  0.0 176.2 jit_solution(7646881354133031884)
XLA Ops:
  0.7 1.0 copy-done.15
  1.7 0.5 collective-permute-start
  2.3 2.6 %collective-permute-start.1 = (bf16[128,512]{1,0:T(8,128)(2,1)S(1)}, bf16[128,512]{1,0:T(8,128)(2,1)S(1)}, u32[]{:S(2)}, u32[]{:S(2)}) collective-permute-start(bf16[128,512]{1,0:T(8,128)(2,1)S(1)} %get-tuple-element.25), channel_id=1, source_target_pairs={{0,16},{8,24},{16,0},{24,8},{1,17},{9,25},{17,1},{25,9},{2,18},{10... | collective-permute-start | bytes 393224 | tf_op jit(solution)/shard_map/ppermute | solution.py:24
  4.8 0.1 collective-permute-start.2
  4.9 2.2 %copy-done.12 = bf16[1,128,16384]{2,1,0:T(8,128)(2,1)S(1)} copy-done((bf16[1,128,16384]{2,1,0:T(8,128)(2,1)S(1)}, bf16[1,128,16384]{2,1,0:T(8,128)(2,1)}, u32[]{:S(2)}) %copy-start.12) | copy-done | bytes 4194328
  7.1 0.4 pack_columns.1
  7.5 2.9 %collective-permute-start.7 = (bf16[128,2048]{1,0:T(8,128)(2,1)S(1)}, bf16[128,2048]{1,0:T(8,128)(2,1)S(1)}, u32[]{:S(2)}, u32[]{:S(2)}) collective-permute-start(bf16[128,2048]{1,0:T(8,128)(2,1)S(1)} %join_columns.28.refs_1_), channel_id=1, source_target_pairs={{0,4},{1,5},{2,6},{3,7},{4,0},{5,1},{6,2},{7,3},{8,12},{9,13},{10,... | collective-permute-start | bytes 1572872 | tf_op jit(solution)/shard_map/ppermute | solution.py:24
  10.5 1.6 collective-permute-start.5
  12.1 0.1 join_columns.32.refs_1_
  12.2 1.6 collective-permute-start.3
  13.8 1.6 collective-permute-start.4
  15.5 2.1 %collective-permute-start.10 = (bf16[128,2048]{1,0:T(8,128)(2,1)S(1)}, bf16[128,2048]{1,0:T(8,128)(2,1)S(1)}, u32[]{:S(2)}, u32[]{:S(2)}) collective-permute-start(bf16[128,2048]{1,0:T(8,128)(2,1)S(1)} %join_columns.31.refs_2_), channel_id=1, source_target_pairs={{0,4},{1,5},{2,6},{3,7},{4,0},{5,1},{6,2},{7,3},{8,12},{9,13},{10,... | collective-permute-start | bytes 1572872 | tf_op jit(solution)/shard_map/ppermute | solution.py:24
  17.6 6.8 %collective-permute-done.5.refs_3_.refs_1_.refs_5_.refs_7_ = bf16[128,2048]{1,0:T(8,128)(2,1)S(1)} collective-permute-done((bf16[128,2048]{1,0:T(8,128)(2,1)S(1)}, bf16[128,2048]{1,0:T(8,128)(2,1)S(1)}, u32[]{:S(2)}, u32[]{:S(2)}) %collective-permute-start.5) | collective-permute-done | bytes 524320 | tf_op jit(solution)/shard_map/ppermute | solution.py:24
  24.4 14.1 %collective-permute-done.4.refs_1_ = bf16[128,2048]{1,0:T(8,128)(2,1)S(1)} collective-permute-done((bf16[128,2048]{1,0:T(8,128)(2,1)S(1)}, bf16[128,2048]{1,0:T(8,128)(2,1)S(1)}, u32[]{:S(2)}, u32[]{:S(2)}) %collective-permute-start.4) | collective-permute-done | bytes 524320 | tf_op jit(solution)/shard_map/ppermute | solution.py:24
  38.5 0.1 join_columns.34.refs_1_.refs_0_
  38.6 1.6 collective-permute-start.8
  40.2 0.2 collective-permute-start.6
  40.4 0.1 join_columns.36.refs_0_
  40.5 0.1 collective-permute-start.9
  40.6 4.7 %collective-permute-start.13 = (bf16[128,2048]{1,0:T(8,128)(2,1)S(1)}, bf16[128,2048]{1,0:T(8,128)(2,1)S(1)}, u32[]{:S(2)}, u32[]{:S(2)}) collective-permute-start(bf16[128,2048]{1,0:T(8,128)(2,1)S(1)} %join_columns.37.refs_1_), channel_id=1, source_target_pairs={{0,5},{1,4},{2,7},{3,6},{4,1},{5,0},{6,3},{7,2},{8,13},{9,12},{10,... | collective-permute-start | bytes 1572872 | tf_op jit(solution)/shard_map/ppermute | solution.py:24
  45.3 17.3 %collective-permute-done.8.refs_2_.refs_1_.refs_6_.refs_8_ = bf16[128,4096]{1,0:T(8,128)(2,1)S(1)} collective-permute-done((bf16[128,4096]{1,0:T(8,128)(2,1)S(1)}, bf16[128,4096]{1,0:T(8,128)(2,1)S(1)}, u32[]{:S(2)}, u32[]{:S(2)}) %collective-permute-start.8) | collective-permute-done | bytes 1048608 | tf_op jit(solution)/shard_map/ppermute | solution.py:24
  62.7 1.8 %collective-permute-start.14 = (bf16[128,2048]{1,0:T(8,128)(2,1)S(1)}, bf16[128,2048]{1,0:T(8,128)(2,1)S(1)}, u32[]{:S(2)}, u32[]{:S(2)}) collective-permute-start(bf16[128,2048]{1,0:T(8,128)(2,1)S(1)} %join_columns.38.refs_1_.refs_2_), channel_id=1, source_target_pairs={{0,16},{8,24},{16,0},{24,8},{1,17},{9,25},{17,1},{25,9},{2,18},{10... | collective-permute-start | bytes 1572872 | tf_op jit(solution)/shard_map/ppermute | solution.py:24
  64.5 0.6 collective-permute-start.15
  65.1 1.6 collective-permute-start.12
  66.8 4.2 %collective-permute-start.11 = (bf16[128,2048]{1,0:T(8,128)(2,1)S(1)}, bf16[128,2048]{1,0:T(8,128)(2,1)S(1)}, u32[]{:S(2)}, u32[]{:S(2)}) collective-permute-start(bf16[128,2048]{1,0:T(8,128)(2,1)S(1)} %join_columns.41.refs_1_), channel_id=1, source_target_pairs={{0,6},{1,7},{2,4},{3,5},{4,2},{5,3},{6,0},{7,1},{8,14},{9,15},{10,... | collective-permute-start | bytes 1572872 | tf_op jit(solution)/shard_map/ppermute | solution.py:24
  70.9 3.9 %collective-permute-done.14.refs_2_.refs_3_.refs_7_.refs_9_ = bf16[128,2048]{1,0:T(8,128)(2,1)S(1)} collective-permute-done((bf16[128,2048]{1,0:T(8,128)(2,1)S(1)}, bf16[128,2048]{1,0:T(8,128)(2,1)S(1)}, u32[]{:S(2)}, u32[]{:S(2)}) %collective-permute-start.14) | collective-permute-done | bytes 524320 | tf_op jit(solution)/shard_map/ppermute | solution.py:24
  74.8 0.9 collective-permute-start.21
  75.8 0.2 join_columns.43.refs_0_
  76.0 17.1 %collective-permute-done.15.refs_1_.refs_9_.refs_6_ = bf16[128,2048]{1,0:T(8,128)(2,1)S(1)} collective-permute-done((bf16[128,2048]{1,0:T(8,128)(2,1)S(1)}, bf16[128,2048]{1,0:T(8,128)(2,1)S(1)}, u32[]{:S(2)}, u32[]{:S(2)}) %collective-permute-start.15) | collective-permute-done | bytes 524320 | tf_op jit(solution)/shard_map/ppermute | solution.py:24
  93.1 0.8 copy-done.13
  93.9 0.4 collective-permute-start.20
  94.3 4.4 %collective-permute-done.16.refs_2_.refs_4_.refs_5_ = bf16[128,12288]{1,0:T(8,128)(2,1)S(1)} collective-permute-done((bf16[128,12288]{1,0:T(8,128)(2,1)S(1)}, bf16[128,12288]{1,0:T(8,128)(2,1)S(1)}, u32[]{:S(2)}, u32[]{:S(2)}) %collective-permute-start.16) | collective-permute-done | bytes 3145760 | tf_op jit(solution)/shard_map/ppermute | solution.py:24
  98.8 1.1 collective-permute-start.17
  99.9 0.1 collective-permute-start.23
  100.0 2.3 %collective-permute-done.12.refs_1_ = bf16[128,2048]{1,0:T(8,128)(2,1)S(1)} collective-permute-done((bf16[128,2048]{1,0:T(8,128)(2,1)S(1)}, bf16[128,2048]{1,0:T(8,128)(2,1)S(1)}, u32[]{:S(2)}, u32[]{:S(2)}) %collective-permute-start.12) | collective-permute-done | bytes 524320 | tf_op jit(solution)/shard_map/ppermute | solution.py:24
  102.3 4.6 %collective-permute-start.18 = (bf16[128,1024]{1,0:T(8,128)(2,1)S(1)}, bf16[128,1024]{1,0:T(8,128)(2,1)S(1)}, u32[]{:S(2)}, u32[]{:S(2)}) collective-permute-start(bf16[128,1024]{1,0:T(8,128)(2,1)S(1)} %join_columns.47.refs_2_), channel_id=1, source_target_pairs={{0,7},{1,6},{2,5},{3,4},{4,3},{5,2},{6,1},{7,0},{8,15},{9,14},{10,... | collective-permute-start | bytes 786440 | tf_op jit(solution)/shard_map/ppermute | solution.py:24
  106.9 5.9 %collective-permute-done.17.refs_3_.refs_1_.refs_10_.refs_7_ = bf16[128,2048]{1,0:T(8,128)(2,1)S(1)} collective-permute-done((bf16[128,2048]{1,0:T(8,128)(2,1)S(1)}, bf16[128,2048]{1,0:T(8,128)(2,1)S(1)}, u32[]{:S(2)}, u32[]{:S(2)}) %collective-permute-start.17) | collective-permute-done | bytes 524320 | tf_op jit(solution)/shard_map/ppermute | solution.py:24
  112.9 3.5 %collective-permute-start.19 = (bf16[128,4096]{1,0:T(8,128)(2,1)S(1)}, bf16[128,4096]{1,0:T(8,128)(2,1)S(1)}, u32[]{:S(2)}, u32[]{:S(2)}) collective-permute-start(bf16[128,4096]{1,0:T(8,128)(2,1)S(1)} %join_columns.48.refs_1_.refs_0_), channel_id=1, source_target_pairs={{0,16},{8,24},{16,0},{24,8},{1,17},{9,25},{17,1},{25,9},{2,18},{10... | collective-permute-start | bytes 3145736 | tf_op jit(solution)/shard_map/ppermute | solution.py:24
  116.3 5.1 %collective-permute-done.21.refs_0_.refs_1_.refs_11_.refs_7_ = bf16[128,2048]{1,0:T(8,128)(2,1)S(1)} collective-permute-done((bf16[128,2048]{1,0:T(8,128)(2,1)S(1)}, bf16[128,2048]{1,0:T(8,128)(2,1)S(1)}, u32[]{:S(2)}, u32[]{:S(2)}) %collective-permute-start.21) | collective-permute-done | bytes 524320 | tf_op jit(solution)/shard_map/ppermute | solution.py:24
  121.5 0.1 join_columns.50.refs_0_
  121.7 0.1 collective-permute-start.22
  121.8 0.9 copy-done.1
  122.6 0.2 copy-done.3
  122.8 0.3 copy-done.5
  123.2 0.3 copy-done.7
  123.5 0.1 copy-done.9
  123.6 0.2 copy-done.11
  123.8 5.4 %product_and_squares.4.refs_2_.refs_13_ = f32[4,1024,512]{2,1,0:T(8,128)S(1)} custom-call(bf16[128,2048]{1,0:T(8,128)(2,1)S(1)} %copy-done.1, bf16[128,4096]{1,0:T(8,128)(2,1)S(1)} %join_columns.34.refs_1_.refs_0_, bf16[128,2048]{1,0:T(8,128)(2,1)S(1)} %join_columns.38.refs_1_.refs_2_, bf16[128,4096]{1,0:T(8,128)(2,1)S(1)} %copy-done.5, ...), custom_call_target="tpu_custom_call" | custom-call | flops 2147483648 | bytes 6291456 | tf_op jit(solution)/shard_map/product_and_squares/pallas_call | solution.py:197
  129.2 0.6 collective-permute-start.27
  129.8 7.7 %collective-permute-done.19.refs_3_.refs_1_.refs_6_.refs_4_ = bf16[128,4096]{1,0:T(8,128)(2,1)S(1)} collective-permute-done((bf16[128,4096]{1,0:T(8,128)(2,1)S(1)}, bf16[128,4096]{1,0:T(8,128)(2,1)S(1)}, u32[]{:S(2)}, u32[]{:S(2)}) %collective-permute-start.19) | collective-permute-done | bytes 1048608 | tf_op jit(solution)/shard_map/ppermute | solution.py:24
  137.6 1.8 %collective-permute-start.24 = (bf16[128,1024]{1,0:T(8,128)(2,1)S(1)}, bf16[128,1024]{1,0:T(8,128)(2,1)S(1)}, u32[]{:S(2)}, u32[]{:S(2)}) collective-permute-start(bf16[128,1024]{1,0:T(8,128)(2,1)S(1)} %join_columns.51.refs_2_.refs_0_), channel_id=1, source_target_pairs={{0,16},{8,24},{16,0},{24,8},{1,17},{9,25},{17,1},{25,9},{2,18},{10... | collective-permute-start | bytes 786440 | tf_op jit(solution)/shard_map/ppermute | solution.py:24
  139.4 0.1 join_columns.52.refs_0_
  139.6 0.1 collective-permute-start.25
  139.7 6.6 %product_and_squares.5.refs_2_.refs_9_ = f32[4,1024,512]{2,1,0:T(8,128)S(1)} custom-call(bf16[128,2048]{1,0:T(8,128)(2,1)S(1)} %copy-done.1, bf16[128,4096]{1,0:T(8,128)(2,1)S(1)} %join_columns.34.refs_1_.refs_0_, bf16[128,2048]{1,0:T(8,128)(2,1)S(1)} %join_columns.38.refs_1_.refs_2_, bf16[128,2048]{1,0:T(8,128)(2,1)S(1)} %join_columns.45.refs_1_.refs_0_.refs_3_, ...), custom_call_target="tpu_custom_call" | custom-call | flops 2684354560 | bytes 7864320 | tf_op jit(solution)/shard_map/product_and_squares/pallas_call | solution.py:197
  146.4 0.3 collective-permute-start.26
  146.7 0.3 collective-permute-start.28
  147.0 1.7 collective-permute-done.28.refs_5_
  148.7 5.9 %product_and_squares.6 = (f32[4,1024,512]{2,1,0:T(8,128)S(1)}, f32[1,8,128]{2,1,0:T(8,128)S(1)}) custom-call(bf16[128,4096]{1,0:T(8,128)(2,1)S(1)} %join_columns.48.refs_1_.refs_0_, bf16[128,2048]{1,0:T(8,128)(2,1)S(1)} %join_columns.45.refs_1_.refs_0_.refs_3_, bf16[128,1024]{1,0:T(8,128)(2,1)S(1)} %join_columns.51.refs_2_.refs_0_, ...), custom_call_target="tpu_custom_call", output_to_operand_aliasing={{0}: (13, {})} | custom-call | flops 2147483648 | bytes 6291456 | tf_op jit(solution)/shard_map/product_and_squares/pallas_call | solution.py:197
  154.6 0.5 collective-permute-done.26.refs_1_.refs_5_
  155.2 0.1 collective-permute-start.29
  155.2 1.9 %collective-permute-done.29.refs_3_ = bf16[128,2048]{1,0:T(8,128)(2,1)S(1)} collective-permute-done((bf16[128,2048]{1,0:T(8,128)(2,1)S(1)}, bf16[128,2048]{1,0:T(8,128)(2,1)S(1)}, u32[]{:S(2)}, u32[]{:S(2)}) %collective-permute-start.29) | collective-permute-done | bytes 524320 | tf_op jit(solution)/shard_map/ppermute | solution.py:24
  157.1 5.8 %product_and_squares.7 = (f32[4,1024,512]{2,1,0:T(8,128)S(1)}, f32[32,8,128]{2,1,0:T(8,128)S(1)}) custom-call(bf16[128,4096]{1,0:T(8,128)(2,1)S(1)} %join_columns.48.refs_1_.refs_0_, bf16[128,1024]{1,0:T(8,128)(2,1)S(1)} %join_columns.53.refs_2_.refs_0_.refs_1_, ...), custom_call_target="tpu_custom_call", output_to_operand_aliasing={{0}: (9, {})} | custom-call | flops 1610612736 | bytes 4718592 | tf_op jit(solution)/shard_map/product_and_squares/pallas_call | solution.py:197
  162.9 9.4 %all_to_all.5.sums_ref = f32[32,8,128]{2,1,0:T(8,128)S(1)} all-to-all(f32[32,8,128]{2,1,0:T(8,128)S(1)} %get-tuple-element.35), channel_id=1, replica_groups=mesh['user'=4,'tok'=8] {'user','tok'}, dimensions={0} | all-to-all | bytes 262144 | tf_op jit(solution)/shard_map/all_to_all | solution.py:479
  172.3 3.9 %weighted_sum.1 = f32[2048,512]{1,0:T(8,128)} custom-call(s32[1]{0:T(128)} %bitcast.user_ref, f32[32,8,128]{2,1,0:T(8,128)S(1)} %all_to_all.5.sums_ref, f32[4,1024,512]{2,1,0:T(8,128)S(1)} %get-tuple-element.33.refs_3_.refs_0_, f32[4,1024,512]{2,1,0:T(8,128)S(1)} %get-tuple-element.36.refs_1_), custom_call_target="tpu_custom_call" | custom-call | tf_op jit(solution)/shard_map/weighted_sum/pallas_call | solution.py:254
  (72 shorter events, 0.9 us)
Async XLA Ops:
  0.7 1.0 copy-start.15
  1.7 10.3 %collective-permute-start = (bf16[128,512]{1,0:T(8,128)(2,1)S(1)}, bf16[128,512]{1,0:T(8,128)(2,1)S(1)}, u32[]{:S(2)}, u32[]{:S(2)}) collective-permute-start(bf16[128,512]{1,0:T(8,128)(2,1)S(1)} %get-tuple-element.24), channel_id=1, source_target_pairs={{0,8},{8,0},{16,24},{24,16},{1,9},{9,1},{17,25},{25,17},{2,10},{10... | collective-permute-start | bytes 393224 | tf_op jit(solution)/shard_map/ppermute | solution.py:24
  2.3 9.7 %collective-permute-start.1 = (bf16[128,512]{1,0:T(8,128)(2,1)S(1)}, bf16[128,512]{1,0:T(8,128)(2,1)S(1)}, u32[]{:S(2)}, u32[]{:S(2)}) collective-permute-start(bf16[128,512]{1,0:T(8,128)(2,1)S(1)} %get-tuple-element.25), channel_id=1, source_target_pairs={{0,16},{8,24},{16,0},{24,8},{1,17},{9,25},{17,1},{25,9},{2,18},{10... | collective-permute-start | bytes 393224 | tf_op jit(solution)/shard_map/ppermute | solution.py:24
  4.8 7.2 %collective-permute-start.2 = (bf16[128,512]{1,0:T(8,128)(2,1)S(1)}, bf16[128,512]{1,0:T(8,128)(2,1)S(1)}, u32[]{:S(2)}, u32[]{:S(2)}) collective-permute-start(bf16[128,512]{1,0:T(8,128)(2,1)S(1)} %get-tuple-element.26), channel_id=1, source_target_pairs={{0,24},{8,16},{16,8},{24,0},{1,25},{9,17},{17,9},{25,1},{2,26},{10... | collective-permute-start | bytes 393224 | tf_op jit(solution)/shard_map/ppermute | solution.py:24
  4.9 2.2 %copy-start.12 = (bf16[1,128,16384]{2,1,0:T(8,128)(2,1)S(1)}, bf16[1,128,16384]{2,1,0:T(8,128)(2,1)}, u32[]{:S(2)}) copy-start(bf16[1,128,16384]{2,1,0:T(8,128)(2,1)} %hidden_ref.1) | copy-start | bytes 12582916
  7.5 33.1 %collective-permute-start.7 = (bf16[128,2048]{1,0:T(8,128)(2,1)S(1)}, bf16[128,2048]{1,0:T(8,128)(2,1)S(1)}, u32[]{:S(2)}, u32[]{:S(2)}) collective-permute-start(bf16[128,2048]{1,0:T(8,128)(2,1)S(1)} %join_columns.28.refs_1_), channel_id=1, source_target_pairs={{0,4},{1,5},{2,6},{3,7},{4,0},{5,1},{6,2},{7,3},{8,12},{9,13},{10,... | collective-permute-start | bytes 1572872 | tf_op jit(solution)/shard_map/ppermute | solution.py:24
  10.4 30.0 %copy-start = (bf16[128,2048]{1,0:T(8,128)(2,1)}, bf16[128,2048]{1,0:T(8,128)(2,1)S(1)}, u32[]{:S(2)}) copy-start(bf16[128,2048]{1,0:T(8,128)(2,1)S(1)} %join_columns.29.refs_4_.refs_1_.refs_0_) | copy-start | bytes 1572868
  10.5 14.0 %collective-permute-start.5 = (bf16[128,2048]{1,0:T(8,128)(2,1)S(1)}, bf16[128,2048]{1,0:T(8,128)(2,1)S(1)}, u32[]{:S(2)}, u32[]{:S(2)}) collective-permute-start(bf16[128,2048]{1,0:T(8,128)(2,1)S(1)} %join_columns.29.refs_4_.refs_1_.refs_0_), channel_id=1, source_target_pairs={{0,16},{8,24},{16,0},{24,8},{1,17},{9,25},{17,1},{25,9},{2,18},{10... | collective-permute-start | bytes 1572872 | tf_op jit(solution)/shard_map/ppermute | solution.py:24
  12.1 26.5 %copy-start.2 = (bf16[128,2048]{1,0:T(8,128)(2,1)}, bf16[128,2048]{1,0:T(8,128)(2,1)S(1)}, u32[]{:S(2)}) copy-start(bf16[128,2048]{1,0:T(8,128)(2,1)S(1)} %join_columns.30.refs_0_.refs_1_.refs_8_.refs_11_) | copy-start | bytes 1572868
  12.2 26.3 %collective-permute-start.3 = (bf16[128,4096]{1,0:T(8,128)(2,1)S(1)}, bf16[128,4096]{1,0:T(8,128)(2,1)S(1)}, u32[]{:S(2)}, u32[]{:S(2)}) collective-permute-start(bf16[128,4096]{1,0:T(8,128)(2,1)S(1)} %join_columns.32.refs_1_), channel_id=1, source_target_pairs={{0,1},{1,0},{2,3},{3,2},{4,5},{5,4},{6,7},{7,6},{8,9},{9,8},{10,11... | collective-permute-start | bytes 3145736 | tf_op jit(solution)/shard_map/ppermute | solution.py:24
  13.8 24.6 %collective-permute-start.4 = (bf16[128,2048]{1,0:T(8,128)(2,1)S(1)}, bf16[128,2048]{1,0:T(8,128)(2,1)S(1)}, u32[]{:S(2)}, u32[]{:S(2)}) collective-permute-start(bf16[128,2048]{1,0:T(8,128)(2,1)S(1)} %join_columns.33.refs_0_), channel_id=1, source_target_pairs={{0,2},{1,3},{2,0},{3,1},{4,6},{5,7},{6,4},{7,5},{8,10},{9,11},{10,... | collective-permute-start | bytes 1572872 | tf_op jit(solution)/shard_map/ppermute | solution.py:24
  15.5 51.2 %collective-permute-start.10 = (bf16[128,2048]{1,0:T(8,128)(2,1)S(1)}, bf16[128,2048]{1,0:T(8,128)(2,1)S(1)}, u32[]{:S(2)}, u32[]{:S(2)}) collective-permute-start(bf16[128,2048]{1,0:T(8,128)(2,1)S(1)} %join_columns.31.refs_2_), channel_id=1, source_target_pairs={{0,4},{1,5},{2,6},{3,7},{4,0},{5,1},{6,2},{7,3},{8,12},{9,13},{10,... | collective-permute-start | bytes 1572872 | tf_op jit(solution)/shard_map/ppermute | solution.py:24
  24.4 16.1 %copy-start.8 = (bf16[128,2048]{1,0:T(8,128)(2,1)}, bf16[128,2048]{1,0:T(8,128)(2,1)S(1)}, u32[]{:S(2)}) copy-start(bf16[128,2048]{1,0:T(8,128)(2,1)S(1)} %collective-permute-done.5.refs_3_.refs_1_.refs_5_.refs_7_) | copy-start | bytes 1572868
  38.5 2.1 %copy-start.6 = (bf16[128,4096]{1,0:T(8,128)(2,1)}, bf16[128,4096]{1,0:T(8,128)(2,1)S(1)}, u32[]{:S(2)}) copy-start(bf16[128,4096]{1,0:T(8,128)(2,1)S(1)} %collective-permute-done.3.refs_0_.refs_9_.refs_12_) | copy-start | bytes 3145732
  38.6 24.0 %collective-permute-start.8 = (bf16[128,4096]{1,0:T(8,128)(2,1)S(1)}, bf16[128,4096]{1,0:T(8,128)(2,1)S(1)}, u32[]{:S(2)}, u32[]{:S(2)}) collective-permute-start(bf16[128,4096]{1,0:T(8,128)(2,1)S(1)} %join_columns.34.refs_1_.refs_0_), channel_id=1, source_target_pairs={{0,16},{8,24},{16,0},{24,8},{1,17},{9,25},{17,1},{25,9},{2,18},{10... | collective-permute-start | bytes 3145736 | tf_op jit(solution)/shard_map/ppermute | solution.py:24
  40.2 24.3 %collective-permute-start.6 = (bf16[128,2048]{1,0:T(8,128)(2,1)S(1)}, bf16[128,2048]{1,0:T(8,128)(2,1)S(1)}, u32[]{:S(2)}, u32[]{:S(2)}) collective-permute-start(bf16[128,2048]{1,0:T(8,128)(2,1)S(1)} %join_columns.35.refs_2_), channel_id=1, source_target_pairs={{0,2},{1,3},{2,0},{3,1},{4,6},{5,7},{6,4},{7,5},{8,10},{9,11},{10,... | collective-permute-start | bytes 1572872 | tf_op jit(solution)/shard_map/ppermute | solution.py:24
  40.5 4.9 %collective-permute-start.9 = (bf16[128,4096]{1,0:T(8,128)(2,1)S(1)}, bf16[128,4096]{1,0:T(8,128)(2,1)S(1)}, u32[]{:S(2)}, u32[]{:S(2)}) collective-permute-start(bf16[128,4096]{1,0:T(8,128)(2,1)S(1)} %join_columns.36.refs_0_), channel_id=1, source_target_pairs={{0,8},{8,0},{16,24},{24,16},{1,9},{9,1},{17,25},{25,17},{2,10},{10... | collective-permute-start | bytes 3145736 | tf_op jit(solution)/shard_map/ppermute | solution.py:24
  40.6 53.2 %collective-permute-start.13 = (bf16[128,2048]{1,0:T(8,128)(2,1)S(1)}, bf16[128,2048]{1,0:T(8,128)(2,1)S(1)}, u32[]{:S(2)}, u32[]{:S(2)}) collective-permute-start(bf16[128,2048]{1,0:T(8,128)(2,1)S(1)} %join_columns.37.refs_1_), channel_id=1, source_target_pairs={{0,5},{1,4},{2,7},{3,6},{4,1},{5,0},{6,3},{7,2},{8,13},{9,12},{10,... | collective-permute-start | bytes 1572872 | tf_op jit(solution)/shard_map/ppermute | solution.py:24
  45.3 21.4 %copy-start.4 = (bf16[128,4096]{1,0:T(8,128)(2,1)}, bf16[128,4096]{1,0:T(8,128)(2,1)S(1)}, u32[]{:S(2)}) copy-start(bf16[128,4096]{1,0:T(8,128)(2,1)S(1)} %collective-permute-done.9.refs_3_.refs_4_) | copy-start | bytes 3145732
  62.7 12.1 %collective-permute-start.14 = (bf16[128,2048]{1,0:T(8,128)(2,1)S(1)}, bf16[128,2048]{1,0:T(8,128)(2,1)S(1)}, u32[]{:S(2)}, u32[]{:S(2)}) collective-permute-start(bf16[128,2048]{1,0:T(8,128)(2,1)S(1)} %join_columns.38.refs_1_.refs_2_), channel_id=1, source_target_pairs={{0,16},{8,24},{16,0},{24,8},{1,17},{9,25},{17,1},{25,9},{2,18},{10... | collective-permute-start | bytes 1572872 | tf_op jit(solution)/shard_map/ppermute | solution.py:24
  64.5 2.2 %copy-start.10 = (bf16[128,2048]{1,0:T(8,128)(2,1)}, bf16[128,2048]{1,0:T(8,128)(2,1)S(1)}, u32[]{:S(2)}) copy-start(bf16[128,2048]{1,0:T(8,128)(2,1)S(1)} %collective-permute-done.6.refs_0_.refs_1_.refs_10_.refs_13_) | copy-start | bytes 1572868
  64.5 28.5 %collective-permute-start.15 = (bf16[128,2048]{1,0:T(8,128)(2,1)S(1)}, bf16[128,2048]{1,0:T(8,128)(2,1)S(1)}, u32[]{:S(2)}, u32[]{:S(2)}) collective-permute-start(bf16[128,2048]{1,0:T(8,128)(2,1)S(1)} %join_columns.39.refs_1_), channel_id=1, source_target_pairs={{0,1},{1,0},{2,3},{3,2},{4,5},{5,4},{6,7},{7,6},{8,9},{9,8},{10,11... | collective-permute-start | bytes 1572872 | tf_op jit(solution)/shard_map/ppermute | solution.py:24
  65.1 37.1 %collective-permute-start.12 = (bf16[128,2048]{1,0:T(8,128)(2,1)S(1)}, bf16[128,2048]{1,0:T(8,128)(2,1)S(1)}, u32[]{:S(2)}, u32[]{:S(2)}) collective-permute-start(bf16[128,2048]{1,0:T(8,128)(2,1)S(1)} %join_columns.40.refs_0_), channel_id=1, source_target_pairs={{0,3},{1,2},{2,1},{3,0},{4,7},{5,6},{6,5},{7,4},{8,11},{9,10},{10,... | collective-permute-start | bytes 1572872 | tf_op jit(solution)/shard_map/ppermute | solution.py:24
  66.8 33.1 %collective-permute-start.11 = (bf16[128,2048]{1,0:T(8,128)(2,1)S(1)}, bf16[128,2048]{1,0:T(8,128)(2,1)S(1)}, u32[]{:S(2)}, u32[]{:S(2)}) collective-permute-start(bf16[128,2048]{1,0:T(8,128)(2,1)S(1)} %join_columns.41.refs_1_), channel_id=1, source_target_pairs={{0,6},{1,7},{2,4},{3,5},{4,2},{5,3},{6,0},{7,1},{8,14},{9,15},{10,... | collective-permute-start | bytes 1572872 | tf_op jit(solution)/shard_map/ppermute | solution.py:24
  74.8 46.6 %collective-permute-start.21 = (bf16[128,2048]{1,0:T(8,128)(2,1)S(1)}, bf16[128,2048]{1,0:T(8,128)(2,1)S(1)}, u32[]{:S(2)}, u32[]{:S(2)}) collective-permute-start(bf16[128,2048]{1,0:T(8,128)(2,1)S(1)} %join_columns.42.refs_4_), channel_id=1, source_target_pairs={{0,2},{1,3},{2,0},{3,1},{4,6},{5,7},{6,4},{7,5},{8,10},{9,11},{10,... | collective-permute-start | bytes 1572872 | tf_op jit(solution)/shard_map/ppermute | solution.py:24
  93.1 0.8 copy-start.13
  93.1 5.7 %collective-permute-start.16 = (bf16[128,12288]{1,0:T(8,128)(2,1)S(1)}, bf16[128,12288]{1,0:T(8,128)(2,1)S(1)}, u32[]{:S(2)}, u32[]{:S(2)}) collective-permute-start(bf16[128,12288]{1,0:T(8,128)(2,1)S(1)} %join_columns.43.refs_0_), channel_id=1, source_target_pairs={{0,8},{8,0},{16,24},{24,16},{1,9},{9,1},{17,25},{25,17},{2,10},{10... | collective-permute-start | bytes 9437192 | tf_op jit(solution)/shard_map/ppermute | solution.py:24
  93.9 35.3 %collective-permute-start.20 = (bf16[128,1024]{1,0:T(8,128)(2,1)S(1)}, bf16[128,1024]{1,0:T(8,128)(2,1)S(1)}, u32[]{:S(2)}, u32[]{:S(2)}) collective-permute-start(bf16[128,1024]{1,0:T(8,128)(2,1)S(1)} %join_columns.44.refs_1_), channel_id=1, source_target_pairs={{0,7},{1,6},{2,5},{3,4},{4,3},{5,2},{6,1},{7,0},{8,15},{9,14},{10,... | collective-permute-start | bytes 786440 | tf_op jit(solution)/shard_map/ppermute | solution.py:24
  98.8 14.0 %collective-permute-start.17 = (bf16[128,2048]{1,0:T(8,128)(2,1)S(1)}, bf16[128,2048]{1,0:T(8,128)(2,1)S(1)}, u32[]{:S(2)}, u32[]{:S(2)}) collective-permute-start(bf16[128,2048]{1,0:T(8,128)(2,1)S(1)} %join_columns.45.refs_1_.refs_0_.refs_3_), channel_id=1, source_target_pairs={{0,16},{8,24},{16,0},{24,8},{1,17},{9,25},{17,1},{25,9},{2,18},{10... | collective-permute-start | bytes 1572872 | tf_op jit(solution)/shard_map/ppermute | solution.py:24
  99.9 39.7 %collective-permute-start.23 = (bf16[128,2048]{1,0:T(8,128)(2,1)S(1)}, bf16[128,2048]{1,0:T(8,128)(2,1)S(1)}, u32[]{:S(2)}, u32[]{:S(2)}) collective-permute-start(bf16[128,2048]{1,0:T(8,128)(2,1)S(1)} %join_columns.46.refs_0_), channel_id=1, source_target_pairs={{0,1},{1,0},{2,3},{3,2},{4,5},{5,4},{6,7},{7,6},{8,9},{9,8},{10,11... | collective-permute-start | bytes 1572872 | tf_op jit(solution)/shard_map/ppermute | solution.py:24
  102.3 44.0 %collective-permute-start.18 = (bf16[128,1024]{1,0:T(8,128)(2,1)S(1)}, bf16[128,1024]{1,0:T(8,128)(2,1)S(1)}, u32[]{:S(2)}, u32[]{:S(2)}) collective-permute-start(bf16[128,1024]{1,0:T(8,128)(2,1)S(1)} %join_columns.47.refs_2_), channel_id=1, source_target_pairs={{0,7},{1,6},{2,5},{3,4},{4,3},{5,2},{6,1},{7,0},{8,15},{9,14},{10,... | collective-permute-start | bytes 786440 | tf_op jit(solution)/shard_map/ppermute | solution.py:24
  112.9 24.7 %collective-permute-start.19 = (bf16[128,4096]{1,0:T(8,128)(2,1)S(1)}, bf16[128,4096]{1,0:T(8,128)(2,1)S(1)}, u32[]{:S(2)}, u32[]{:S(2)}) collective-permute-start(bf16[128,4096]{1,0:T(8,128)(2,1)S(1)} %join_columns.48.refs_1_.refs_0_), channel_id=1, source_target_pairs={{0,16},{8,24},{16,0},{24,8},{1,17},{9,25},{17,1},{25,9},{2,18},{10... | collective-permute-start | bytes 3145736 | tf_op jit(solution)/shard_map/ppermute | solution.py:24
  121.6 1.0 copy-start.1
  121.6 1.2 copy-start.3
  121.6 1.5 copy-start.5
  121.6 1.8 %copy-start.7 = (bf16[128,4096]{1,0:T(8,128)(2,1)S(1)}, bf16[128,4096]{1,0:T(8,128)(2,1)}, u32[]{:S(2)}) copy-start(bf16[128,4096]{1,0:T(8,128)(2,1)} %copy-done.6) | copy-start | bytes 3145732
  121.6 2.0 %copy-start.9 = (bf16[128,2048]{1,0:T(8,128)(2,1)S(1)}, bf16[128,2048]{1,0:T(8,128)(2,1)}, u32[]{:S(2)}) copy-start(bf16[128,2048]{1,0:T(8,128)(2,1)} %copy-done.8) | copy-start | bytes 1572868
  121.7 2.1 %copy-start.11 = (bf16[128,2048]{1,0:T(8,128)(2,1)S(1)}, bf16[128,2048]{1,0:T(8,128)(2,1)}, u32[]{:S(2)}) copy-start(bf16[128,2048]{1,0:T(8,128)(2,1)} %copy-done.10) | copy-start | bytes 1572868
  121.7 8.2 %collective-permute-start.22 = (bf16[128,4096]{1,0:T(8,128)(2,1)S(1)}, bf16[128,4096]{1,0:T(8,128)(2,1)S(1)}, u32[]{:S(2)}, u32[]{:S(2)}) collective-permute-start(bf16[128,4096]{1,0:T(8,128)(2,1)S(1)} %join_columns.50.refs_0_), channel_id=1, source_target_pairs={{0,8},{8,0},{16,24},{24,16},{1,9},{9,1},{17,25},{25,17},{2,10},{10... | collective-permute-start | bytes 3145736 | tf_op jit(solution)/shard_map/ppermute | solution.py:24
  129.2 17.8 %collective-permute-start.27 = (bf16[128,2048]{1,0:T(8,128)(2,1)S(1)}, bf16[128,2048]{1,0:T(8,128)(2,1)S(1)}, u32[]{:S(2)}, u32[]{:S(2)}) collective-permute-start(bf16[128,2048]{1,0:T(8,128)(2,1)S(1)} %join_columns.49.refs_2_), channel_id=1, source_target_pairs={{0,1},{1,0},{2,3},{3,2},{4,5},{5,4},{6,7},{7,6},{8,9},{9,8},{10,11... | collective-permute-start | bytes 1572872 | tf_op jit(solution)/shard_map/ppermute | solution.py:24
  137.6 8.7 %collective-permute-start.24 = (bf16[128,1024]{1,0:T(8,128)(2,1)S(1)}, bf16[128,1024]{1,0:T(8,128)(2,1)S(1)}, u32[]{:S(2)}, u32[]{:S(2)}) collective-permute-start(bf16[128,1024]{1,0:T(8,128)(2,1)S(1)} %join_columns.51.refs_2_.refs_0_), channel_id=1, source_target_pairs={{0,16},{8,24},{16,0},{24,8},{1,17},{9,25},{17,1},{25,9},{2,18},{10... | collective-permute-start | bytes 786440 | tf_op jit(solution)/shard_map/ppermute | solution.py:24
  139.6 6.8 %collective-permute-start.25 = (bf16[128,8192]{1,0:T(8,128)(2,1)S(1)}, bf16[128,8192]{1,0:T(8,128)(2,1)S(1)}, u32[]{:S(2)}, u32[]{:S(2)}) collective-permute-start(bf16[128,8192]{1,0:T(8,128)(2,1)S(1)} %join_columns.52.refs_0_), channel_id=1, source_target_pairs={{0,8},{8,0},{16,24},{24,16},{1,9},{9,1},{17,25},{25,17},{2,10},{10... | collective-permute-start | bytes 6291464 | tf_op jit(solution)/shard_map/ppermute | solution.py:24
  146.4 8.8 %collective-permute-start.26 = (bf16[128,1024]{1,0:T(8,128)(2,1)S(1)}, bf16[128,1024]{1,0:T(8,128)(2,1)S(1)}, u32[]{:S(2)}, u32[]{:S(2)}) collective-permute-start(bf16[128,1024]{1,0:T(8,128)(2,1)S(1)} %join_columns.53.refs_2_.refs_0_.refs_1_), channel_id=1, source_target_pairs={{0,16},{8,24},{16,0},{24,8},{1,17},{9,25},{17,1},{25,9},{2,18},{10... | collective-permute-start | bytes 786440 | tf_op jit(solution)/shard_map/ppermute | solution.py:24
  146.7 2.0 %copy-start.14 = (bf16[128,2048]{1,0:T(8,128)(2,1)S(1)}, bf16[128,2048]{1,0:T(8,128)(2,1)}, u32[]{:S(2)}) copy-start(bf16[128,2048]{1,0:T(8,128)(2,1)} %copy-done.13) | copy-start | bytes 1572868
  146.7 2.0 %collective-permute-start.28 = (bf16[128,2048]{1,0:T(8,128)(2,1)S(1)}, bf16[128,2048]{1,0:T(8,128)(2,1)S(1)}, u32[]{:S(2)}, u32[]{:S(2)}) collective-permute-start(bf16[128,2048]{1,0:T(8,128)(2,1)S(1)} %join_columns.54.refs_0_), channel_id=1, source_target_pairs={{0,8},{8,0},{16,24},{24,16},{1,9},{9,1},{17,25},{25,17},{2,10},{10... | collective-permute-start | bytes 1572872 | tf_op jit(solution)/shard_map/ppermute | solution.py:24
  155.2 2.0 %collective-permute-start.29 = (bf16[128,2048]{1,0:T(8,128)(2,1)S(1)}, bf16[128,2048]{1,0:T(8,128)(2,1)S(1)}, u32[]{:S(2)}, u32[]{:S(2)}) collective-permute-start(bf16[128,2048]{1,0:T(8,128)(2,1)S(1)} %join_columns.55), channel_id=1, source_target_pairs={{0,8},{8,0},{16,24},{24,16},{1,9},{9,1},{17,25},{25,17},{2,10},{10... | collective-permute-start | bytes 1572872 | tf_op jit(solution)/shard_map/ppermute | solution.py:24
